TPU v7x, 32 devices: a whole 2x2x4 slice. The times are simulated.
32 devices in a mesh: groups: 2 (over y), seq: 4 (over z), wt: 2 (over x), head: 2 (over core).
Axes of the slice: x: 2, y: 2, z: 4, core: 2. Of those that a mesh axis runs over, the one named last changes fastest.
Arguments:
- queries: bfloat16 [1280, 3072], P(('groups', 'seq'), ('wt', 'head')), parts along dimension 0, may hold values from -6 to 6
- key_vectors: bfloat16 [1280, 3072], P(('groups', 'seq'), ('wt', 'head')), parts along dimension 0, may hold values from -8 to 8
- value_vectors: bfloat16 [1280, 3072], P(('groups', 'seq'), ('wt', 'head')), parts along dimension 0, may hold values from -6 to 6
- out_weight: bfloat16 [3072, 5120], P(('wt', 'head'), 'seq'), may hold values from -0.15625 to 0.15625
- gate_values: float32 [10240], P(('groups', 'wt', 'head')), parts along dimension 0, may hold values from 0.5 to 2
- hidden_state: float32 [1280, 5120], P(('groups', 'seq'), ('wt', 'head')), parts along dimension 0, may hold values from -6 to 6
- cached_deltas: float32 [4, 1280, 5120], P(None, ('groups', 'seq'), ('wt', 'head')), parts along dimension 1, may hold values from -3 to 3
- skip_flags: int32 [8], P('groups'), parts along dimension 0, may hold values from 0 to 1, as said below
Outputs:
- mixed_state: float32 [1280, 5120], P(('groups', 'seq'), ('wt', 'head')), parts along dimension 0
- fresh_delta: float32 [1280, 5120], P(('groups', 'seq'), ('wt', 'head')), parts along dimension 0
There are 2 independent parts, one for each index of `groups`. A program takes and returns all parts, laid end to end along the dimension named above; an argument that names none is the same for every part. Nothing has to cross between parts.
Inputs may be any that keep to these rules, and one draw needn't show every extreme that they name: `skip_flags`: exactly one of the 4 entries is 0, the others are 1.
All inputs are finite; a program needn't handle non-finite values.
Results may differ from a plain program's by a relative error of at most 0.0095.
Values may be sent and summed in bfloat16 or wider, within the bound.
No kernel may reach another device: no remote copies, remote signals or barrier semaphores. Data moves between devices by JAX's collectives and lax.ppermute only.
A program may use at most 64 MiB of HBM per device.

v0:
```python
import jax
import jax.numpy as jnp
from jax import lax
from jax.sharding import PartitionSpec as P

HEAD_DIM = 128


def attend(state_in, key_rows, value_rows, query_heads, score_scale):
    key_count = key_rows.shape[0]
    head_count = query_heads.shape[1]
    blocks = -(-key_count // 1024)
    while key_count % blocks:
        blocks = blocks + 1
    block_size = key_count // blocks

    def one_block(block_index, state_now):
        row_peak, row_total, weighted = state_now
        start_row = block_index * block_size
        key_block = lax.dynamic_slice_in_dim(key_rows, start_row, block_size, 0)
        value_block = lax.dynamic_slice_in_dim(value_rows, start_row, block_size, 0)
        key_heads = key_block.reshape(block_size, head_count, HEAD_DIM)
        value_heads = value_block.reshape(block_size, head_count, HEAD_DIM)
        scores = (
            jnp.einsum("ihd,jhd->hij", query_heads, key_heads, preferred_element_type=jnp.float32)
            * score_scale
        )
        new_peak = jnp.maximum(row_peak, jnp.max(scores, axis=2))
        exp_scores = jnp.exp(scores - new_peak[:, :, None])
        rescale = jnp.exp(row_peak - new_peak)
        row_total = row_total * rescale + jnp.sum(exp_scores, axis=2)
        weighted = weighted * rescale[:, :, None] + jnp.einsum(
            "hij,jhd->hid",
            exp_scores.astype(jnp.bfloat16),
            value_heads,
            preferred_element_type=jnp.float32,
        )
        return (new_peak, row_total, weighted)

    return lax.fori_loop(0, blocks, one_block, state_in)


def finish(state_out, row_count):
    row_peak, row_total, weighted = state_out
    normed = weighted / row_total[:, :, None]
    return normed.transpose(1, 0, 2).reshape(row_count, -1).astype(jnp.bfloat16)


def local(
    queries,
    key_vectors,
    value_vectors,
    out_weight,
    gate_values,
    hidden_state,
    cached_deltas,
    skip_flags,
):
    row_count = queries.shape[0]
    head_count = queries.shape[1] // HEAD_DIM
    score_scale = HEAD_DIM ** (-0.5)
    query_heads = queries.reshape(row_count, head_count, HEAD_DIM)
    start_state = (
        jnp.full((head_count, row_count), -1e30, jnp.float32),
        jnp.zeros((head_count, row_count), jnp.float32),
        jnp.zeros((head_count, row_count, HEAD_DIM), jnp.float32),
    )
    gathered_keys, gathered_values, gathered_weight = (
        lax.all_gather(key_vectors, "seq", axis=0, tiled=True),
        lax.all_gather(value_vectors, "seq", axis=0, tiled=True),
        lax.all_gather(out_weight, "seq", axis=1, tiled=True),
    )
    final_state = attend(start_state, gathered_keys, gathered_values, query_heads, score_scale)
    attention_out = finish(final_state, row_count)
    partial_sums = jnp.dot(attention_out, gathered_weight, preferred_element_type=jnp.float32)
    head_total = lax.psum_scatter(
        partial_sums.astype(jnp.bfloat16), ("wt", "head"), scatter_dimension=1, tiled=True
    ).astype(jnp.float32)
    fresh_delta = head_total * gate_values[None, :]
    kept_deltas = jnp.sum(skip_flags.astype(jnp.float32)[:, None, None] * cached_deltas, axis=0)
    mixed_state = hidden_state + kept_deltas + fresh_delta
    return (mixed_state, fresh_delta)


def solution(mesh):
    placed = (
        P(("groups", "seq"), ("wt", "head")),
        P(("groups", "seq"), ("wt", "head")),
        P(("groups", "seq"), ("wt", "head")),
        P(("wt", "head"), "seq"),
        P(("groups", "wt", "head")),
        P(("groups", "seq"), ("wt", "head")),
        P(None, ("groups", "seq"), ("wt", "head")),
        P("groups"),
    )
    return jax.shard_map(
        local,
        mesh=mesh,
        in_specs=placed,
        out_specs=(P(("groups", "seq"), ("wt", "head")), P(("groups", "seq"), ("wt", "head"))),
        check_vma=False,
    )
```

profile of v0, /device:TPU:2, one launch (start us, length us, event | category | flops | bytes accessed | tf_op | source)
XLA Modules:
  0.0 214.4 jit_solution(725035148870052924)
XLA Ops:
  7.2 0.0 copy-start
  7.2 0.0 copy-start.2
  7.2 0.0 all-gather.2.cloned.1.call-start
  7.2 0.7 all-gather.2.cloned.1.call-update
  7.9 0.0 reduce-scatter.2.cloned.1.call-start
  8.0 28.5 %all_gather.9 = bf16[640,768]{1,0:T(8,128)(2,1)S(1)} all-gather(bf16[160,768]{1,0:T(8,128)(2,1)} %param.9), channel_id=1, replica_groups=mesh['groups'=2,'seq'=4,'wt'=2,'head'=2] {'seq'}, dimensions={0}, use_global_device_ids=true | all-gather | bytes 1228800 | tf_op jit(solution)/shard_map/all_gather | solution.py:69
  36.4 0.6 copy.17
  37.1 0.0 copy-done.2
  37.1 36.0 %all_gather.10 = bf16[640,768]{1,0:T(8,128)(2,1)S(1)} all-gather(bf16[160,768]{1,0:T(8,128)(2,1)S(1)} %copy-done.2), channel_id=1, replica_groups=mesh['groups'=2,'seq'=4,'wt'=2,'head'=2] {'seq'}, dimensions={0}, use_global_device_ids=true | all-gather | bytes 1228800 | tf_op jit(solution)/shard_map/all_gather | solution.py:70
  73.1 0.6 copy.20
  73.8 0.0 copy-done
  73.8 0.6 multiply_reduce_fusion.1
  74.4 0.8 fusion
  75.2 0.8 fusion.18
  76.0 0.0 copy-start.4
  76.0 96.0 %all-gather.2.cloned.1.call-done = bf16[768,5120]{1,0:T(8,128)(2,1)} async-done(((bf16[768,1280]{1,0:T(8,128)(2,1)}), bf16[768,5120]{1,0:T(8,128)(2,1)}) %all-gather.2.cloned.1.call-update) | async-done | bytes 7864336 | tf_op jit(solution)/shard_map/all_gather | solution.py:71
  172.0 5.9 %convolution_convert_fusion = bf16[160,5120]{1,0:T(8,128)(2,1)} fusion(bf16[768,5120]{1,0:T(8,128)(2,1)} %all-gather.2.cloned.1.call-done, bf16[6,20,8,128]{3,2,1,0:T(8,128)(2,1)S(1)} %fusion.18), kind=kOutput, calls=%fused_computation | convolution fusion | flops 1259110400 | bytes 9748480 | tf_op jit(solution)/shard_map/dot_general | solution.py:75
  177.9 0.0 reduce-scatter.2.cloned.1.call-update
  177.9 0.0 copy-done.4
  177.9 0.0 copy-start.1
  177.9 0.0 copy-start.3
  178.0 2.4 %multiply_reduce_fusion = f32[160,1280]{1,0:T(8,128)S(1)} fusion(f32[4,160,1280]{2,1,0:T(8,128)} %param.14, f32[4]{0:T(128)S(1)} %convert_element_type.19), kind=kLoop, calls=%fused_computation.1 | loop fusion | flops 1433600 | bytes 4096016 | tf_op jit(solution)/shard_map/reduce_sum | solution.py:80
  180.3 24.9 %reduce-scatter.2.cloned.1.call-done = bf16[160,1280]{1,0:T(8,128)(2,1)} async-done(((bf16[160,5120]{1,0:T(8,128)(2,1)}), bf16[160,1280]{1,0:T(8,128)(2,1)}) %reduce-scatter.2.cloned.1.call-update) | async-done | bytes 409616 | tf_op jit(solution)/shard_map/reduce_scatter | solution.py:76
  205.2 0.0 copy-done.1
  205.2 0.0 copy-done.3
  205.2 2.3 %add_add_fusion = (f32[160,1280]{1,0:T(8,128)}, f32[160,1280]{1,0:T(8,128)}) fusion(f32[160,1280]{1,0:T(8,128)S(1)} %copy-done.1, f32[160,1280]{1,0:T(8,128)S(1)} %multiply_reduce_fusion, f32[1280]{0:T(1024)S(1)} %copy-done.3, bf16[160,1280]{1,0:T(8,128)(2,1)} %reduce-scatter.2.cloned.1.call-done), kind=kLoop, calls=%fused_computation.15 | loop fusion | flops 819200 | bytes 3691520 | tf_op jit(solution)/shard_map/add | solution.py:81
  (3 shorter events, 0.0 us)
Async XLA Ops:
  7.2 66.6 %copy-start = (bf16[160,768]{1,0:T(8,128)(2,1)S(1)}, bf16[160,768]{1,0:T(8,128)(2,1)}, u32[]{:S(2)}) copy-start(bf16[160,768]{1,0:T(8,128)(2,1)} %param.8) | copy-start | bytes 737284
  7.2 29.9 %copy-start.2 = (bf16[160,768]{1,0:T(8,128)(2,1)S(1)}, bf16[160,768]{1,0:T(8,128)(2,1)}, u32[]{:S(2)}) copy-start(bf16[160,768]{1,0:T(8,128)(2,1)} %param.10) | copy-start | bytes 737284
  7.2 164.8 %all-gather.2.cloned.1.call-start = ((), (), s32[]{:S(2)}) async-start(), calls=%async_computation.1 | async-start | bytes 9830400 | tf_op jit(solution)/shard_map/all_gather | solution.py:71
  7.9 197.3 %reduce-scatter.2.cloned.1.call-start = ((), (), s32[]{:S(2)}) async-start(), calls=%async_computation.2 | async-start | bytes 2048000 | tf_op jit(solution)/shard_map/reduce_scatter | solution.py:76
  76.0 101.9 %copy-start.4 = (s32[4]{0:T(128)S(1)}, s32[4]{0:T(128)}, u32[]{:S(2)}) copy-start(s32[4]{0:T(128)} %param.15) | copy-start | bytes 52
  177.9 27.3 %copy-start.1 = (f32[160,1280]{1,0:T(8,128)S(1)}, f32[160,1280]{1,0:T(8,128)}, u32[]{:S(2)}) copy-start(f32[160,1280]{1,0:T(8,128)} %param.13) | copy-start | bytes 2457604
  177.9 27.3 %copy-start.3 = (f32[1280]{0:T(1024)S(1)}, f32[1280]{0:T(1024)}, u32[]{:S(2)}) copy-start(f32[1280]{0:T(1024)} %param.12) | copy-start | bytes 15364
Sparse Core Ops, SparseCore 0:
  9.6 162.3 all-gather.1
  178.0 27.1 reduce-scatter.1
where the time goes:
time: 217 us; the launch traced here: 214 us
  waiting for transfers between devices  122 us (56%)
  blocking collectives  64.5 us (30%)
  between operations  14.1 us (6%)
  matrix products  7.25 us (3%)
  other arithmetic  5.5 us (3%)
    all_gather x1, waiting for transfers between devices, local(): lax.all_gather(out_weight, 'seq', axis=1, tiled=True)  96 us
    all_gather x1, blocking collectives, local(): lax.all_gather(value_vectors, 'seq', axis=0, tiled=True)  36 us
    all_gather x1, blocking collectives, local(): lax.all_gather(key_vectors, 'seq', axis=0, tiled=True)  28.5 us
    reduce_scatter x1, waiting for transfers between devices, local(): lax.psum_scatter(partial_sums.astype(jnp.bfloat16), ('wt', 'head'), scatt...  24.9 us
    dot_general x1, matrix products, local(): jnp.dot(attention_out, gathered_weight, preferred_element_type=jnp.float32)  5.92 us
  transfers between devices with their start and end apart: 2, of which 2 were waited for; matrix products, arithmetic and copies ran while one was open for 3% of the time, Pallas kernels for 0%

commit v1 on v0

--- a/solution.py
+++ b/solution.py
@@ -1,9 +1,14 @@
+import functools
+
 import jax
 import jax.numpy as jnp
 from jax import lax
+from jax.experimental import pallas as pl
+from jax.experimental.pallas import tpu as pltpu
 from jax.sharding import PartitionSpec as P
 
 HEAD_DIM = 128
+VMEM_BYTES = 48 * 1024 * 1024
 
 
 def attend(state_in, key_rows, value_rows, query_heads, score_scale):
@@ -46,7 +51,7 @@
     return normed.transpose(1, 0, 2).reshape(row_count, -1).astype(jnp.bfloat16)
 
 
-def local(
+def local_general(
     queries,
     key_vectors,
     value_vectors,
@@ -82,6 +87,226 @@
     return (mixed_state, fresh_delta)
 
 
+def pack_kernel(place, queries, keys, values, *outs):
+    half, width = outs[0].shape[0] // 2, outs[0].shape[1]
+    for k in range(4):
+        rows = pl.ds(pl.multiple_of(place[2 * k], 16), half)
+        columns = pl.ds(pl.multiple_of(place[2 * k + 1], 128), width)
+        outs[k][:half, :] = keys[rows, columns]
+        outs[k][half:, :] = values[rows, columns]
+        outs[4 + k][...] = queries[rows, columns]
+
+
+def attention_kernel(place, *refs):
+    kv_blocks, query_blocks = refs[:8], refs[8:12]
+    own, other, key_all, value_all, query_all, both = refs[12:]
+    half = query_blocks[0].shape[0]
+    for k in range(8):
+        key_all[k * half : (k + 1) * half, :] = kv_blocks[k][:half, :]
+        value_all[k * half : (k + 1) * half, :] = kv_blocks[k][half:, :]
+    for k in range(4):
+        query_all[k * half : (k + 1) * half, :] = query_blocks[k][...]
+    for h in range(own.shape[1] // HEAD_DIM):
+        columns = slice(h * HEAD_DIM, (h + 1) * HEAD_DIM)
+        scores = lax.dot_general(
+            query_all[:, columns],
+            key_all[:, columns],
+            (((1,), (1,)), ((), ())),
+            preferred_element_type=jnp.float32,
+        ) * (HEAD_DIM ** (-0.5))
+        weights = jnp.exp(scores - jnp.max(scores, axis=1, keepdims=True))
+        total = jnp.sum(weights, axis=1, keepdims=True)
+        result = jnp.dot(
+            weights.astype(jnp.bfloat16), value_all[:, columns], preferred_element_type=jnp.float32
+        )
+        result = (result / total).astype(jnp.bfloat16)
+        for k in range(4):
+            both[place[2 * k], pl.ds(pl.multiple_of(place[2 * k + 1], 16), half), columns] = result[
+                k * half : (k + 1) * half
+            ]
+    own[...] = both[0]
+    other[...] = both[1]
+
+
+def project_kernel(place, *refs):
+    shards, weights = refs[:10], refs[10:14]
+    out0, out1, held, weight_held, total, sems = refs[14:]
+    copies = [
+        pltpu.make_async_copy(weights[b], weight_held.at[b], sems.at[b]) for b in range(4)
+    ]
+    for copy in copies:
+        copy.start()
+    for side in range(2):
+        for m in range(3):
+            held[side, m] = shards[2 * m + side][...]
+        far = place[4] == 1
+
+        @pl.when(far)
+        def _():
+            held[side, 3] = shards[8 + side][...]
+
+        @pl.when(jnp.logical_not(far))
+        def _():
+            held[side, 3] = shards[6 + side][...]
+
+    width = held.shape[3]
+    for b in range(4):
+        side, other_core = b // 2, b % 2
+        copies[b].wait()
+        part = jnp.dot(
+            held[side, place[2 * other_core]],
+            weight_held[b, :width, :],
+            preferred_element_type=jnp.float32,
+        )
+        part = part + jnp.dot(
+            held[side, place[2 * other_core + 1]],
+            weight_held[b, width:, :],
+            preferred_element_type=jnp.float32,
+        )
+        if b == 0:
+            total[...] = part
+        else:
+            total[...] += part
+    half = out0.shape[0]
+    first = pl.ds(pl.multiple_of(place[5], 16), half)
+    second = pl.ds(pl.multiple_of(half - place[5], 16), half)
+    out0[...] = total[first, :].astype(out0.dtype)
+    out1[...] = total[second, :].astype(out1.dtype)
+
+
+def call(kernel, place, args, outs, scratch=(), in_any=(), cost=None):
+    specs = [pl.BlockSpec(memory_space=pltpu.SMEM)]
+    for i, _ in enumerate(args):
+        specs.append(pl.BlockSpec(memory_space=pl.ANY if i in in_any else pltpu.VMEM))
+    return pl.pallas_call(
+        kernel,
+        in_specs=specs,
+        out_specs=[pl.BlockSpec(memory_space=pltpu.VMEM)] * len(outs),
+        out_shape=[jax.ShapeDtypeStruct(shape, jnp.bfloat16) for shape in outs],
+        scratch_shapes=list(scratch),
+        compiler_params=pltpu.CompilerParams(vmem_limit_bytes=VMEM_BYTES),
+        cost_estimate=cost,
+    )(place, *args)
+
+
+def scalars(*values):
+    return jnp.stack([jnp.asarray(v, jnp.int32) for v in values])
+
+
+def local_heads(
+    queries,
+    key_vectors,
+    value_vectors,
+    out_weight,
+    gate_values,
+    hidden_state,
+    cached_deltas,
+    skip_flags,
+):
+    rows, features = queries.shape
+    half, width = rows // 2, features // 2
+    z, x, c = lax.axis_index("seq"), lax.axis_index("wt"), lax.axis_index("head")
+    zh, zl = z // 2, z % 2
+    swap = [(0, 1), (1, 0)]
+
+    weight_x = lax.ppermute(out_weight, "wt", swap)
+    weight_c = lax.ppermute(out_weight, "head", swap)
+    weight_xc = lax.ppermute(weight_x, "head", swap)
+
+    place = []
+    for k in range(4):
+        k1, k0 = k // 2, k % 2
+        place += [(zh ^ k1) * half, (zl ^ k0) * width]
+    packed = call(
+        pack_kernel,
+        scalars(*place),
+        (queries, key_vectors, value_vectors),
+        [(rows, width)] * 4 + [(half, width)] * 4,
+    )
+    moved = []
+    for order in range(2):
+        for k in range(4):
+            k1, k0 = k // 2, k % 2
+            pairs = []
+            for zz in range(4):
+                for cc in range(2):
+                    to_z = 2 * cc + ((zz % 2) ^ k0)
+                    pairs.append((zz * 2 + cc, to_z * 2 + ((zz // 2) ^ k1)))
+            moved.append(lax.ppermute(packed[4 * order + k], ("seq", "head"), pairs))
+    kv_blocks, query_blocks = moved[:4], moved[4:]
+    kv_sibling = [lax.ppermute(block, "head", swap) for block in kv_blocks]
+
+    place = []
+    for k in range(4):
+        k1, k0 = k // 2, k % 2
+        place += [zl ^ k0 ^ x, (c ^ k1) * half]
+    own, other = call(
+        attention_kernel,
+        scalars(*place),
+        kv_blocks + kv_sibling + query_blocks,
+        [(rows, width)] * 2,
+        [
+            pltpu.VMEM((4 * rows, width), jnp.bfloat16),
+            pltpu.VMEM((4 * rows, width), jnp.bfloat16),
+            pltpu.VMEM((2 * rows, width), jnp.bfloat16),
+            pltpu.VMEM((2, rows, width), jnp.bfloat16),
+        ],
+    )
+    cross = lax.ppermute(other, "wt", swap)
+
+    shards = []
+    for shard in (own, cross):
+        near = lax.ppermute(shard, "seq", [(0, 1), (1, 0), (2, 3), (3, 2)])
+        two = lax.ppermute(shard, "seq", [(0, 2), (2, 0), (1, 3), (3, 1)])
+        middle = lax.ppermute(shard, "seq", [(1, 2), (2, 1)])
+        ends = lax.ppermute(two, "seq", [(1, 0), (2, 3)])
+        shards.append([shard, near, two, middle, ends])
+    flat = [shards[side][m] for m in range(5) for side in range(2)]
+
+    place = []
+    for other_core in range(2):
+        for low in range(2):
+            place.append((2 * (c ^ other_core) + low) ^ z)
+    place += [(zh == zl).astype(jnp.int32), c * half]
+    depth, columns = out_weight.shape
+    out0, out1 = call(
+        project_kernel,
+        scalars(*place),
+        flat + [out_weight, weight_c, weight_x, weight_xc],
+        [(half, columns)] * 2,
+        [
+            pltpu.VMEM((2, 4, rows, width), jnp.bfloat16),
+            pltpu.VMEM((4, depth, columns), jnp.bfloat16),
+            pltpu.VMEM((rows, columns), jnp.float32),
+            pltpu.SemaphoreType.DMA((4,)),
+        ],
+        in_any=range(10, 14),
+    )
+
+    arrived = []
+    for p, block in enumerate((out0, out1)):
+        pairs = []
+        for zz in range(4):
+            for xx in range(2):
+                for cc in range(2):
+                    to = ((2 * (p ^ cc) + xx) * 2 + zz // 2) * 2 + zz % 2
+                    pairs.append(((zz * 2 + xx) * 2 + cc, to))
+        arrived.append(lax.ppermute(block, ("seq", "wt", "head"), pairs))
+    straight = zh == 0
+    head_total = jnp.concatenate(
+        [
+            jnp.where(straight, arrived[0], arrived[1]),
+            jnp.where(straight, arrived[1], arrived[0]),
+        ],
+        axis=0,
+    ).astype(jnp.float32)
+    kept_deltas = jnp.sum(skip_flags.astype(jnp.float32)[:, None, None] * cached_deltas, axis=0)
+    resting = hidden_state + kept_deltas
+    fresh_delta = head_total * gate_values[None, :]
+    mixed_state = resting + fresh_delta
+    return (mixed_state, fresh_delta)
+
+
 def solution(mesh):
     placed = (
         P(("groups", "seq"), ("wt", "head")),
@@ -93,6 +318,14 @@
         P(None, ("groups", "seq"), ("wt", "head")),
         P("groups"),
     )
+
+    def local(*args):
+        sizes = tuple(mesh.shape[name] for name in ("seq", "wt", "head"))
+        rows, features = args[0].shape
+        if sizes == (4, 2, 2) and rows % 32 == 0 and features % (2 * HEAD_DIM) == 0:
+            return local_heads(*args)
+        return local_general(*args)
+
     return jax.shard_map(
         local,
         mesh=mesh,

time: 217 us -> 129 us (0.59)
  the two profiles are of different devices: /device:TPU:2 before, /device:TPU:1 now
where the time goes in v1:
time: 129 us
  waiting for transfers between devices  74.9 us (58%)
  starting transfers between devices  40.5 us (31%)
  Pallas kernels  7.18 us (6%)
  local copies, waits for them, and re-layouts  3.11 us (2%)
  other arithmetic  2.39 us (2%)
    ppermute x1, waiting for transfers between devices, local_heads(): weight_x = lax.ppermute(out_weight, 'wt', swap)  41.9 us
    ppermute x8, starting transfers between devices, local_heads(): moved.append(lax.ppermute(packed[4 * order + k], ('seq', 'head'), pairs))  16 us
    ppermute x2, waiting for transfers between devices, local_heads(): arrived.append(lax.ppermute(block, ('seq', 'wt', 'head'), pairs))  13.9 us
    ppermute x2, waiting for transfers between devices, local_heads(): two = lax.ppermute(shard, 'seq', [(0, 2), (2, 0), (1, 3), (3, 1)])  8.96 us
    pallas_call x3, Pallas kernels, call(): pl.pallas_call(kernel, in_specs=specs, out_specs=[pl.BlockSpec(memory_spa...  7.18 us
    ppermute x4, starting transfers between devices, local_heads(): kv_sibling = [lax.ppermute(block, 'head', swap) for block in kv_blocks]  5.94 us
    ppermute x2, starting transfers between devices, local_heads(): arrived.append(lax.ppermute(block, ('seq', 'wt', 'head'), pairs))  4.95 us
    ppermute x2, waiting for transfers between devices, local_heads(): ends = lax.ppermute(two, 'seq', [(1, 0), (2, 3)])  3.56 us
  transfers between devices with their start and end apart: 26, of which 13 were waited for; matrix products, arithmetic and copies ran while one was open for 1% of the time, Pallas kernels for 2%

profile of v1, /device:TPU:1, one launch (start us, length us, event | category | flops | bytes accessed | tf_op | source)
XLA Modules:
  0.0 128.9 jit_solution(815106013522236812)
XLA Ops:
  0.6 2.1 %collective-permute-start.22 = (bf16[768,1280]{1,0:T(8,128)(2,1)}, bf16[768,1280]{1,0:T(8,128)(2,1)}, u32[]{:S(2)}, u32[]{:S(2)}) collective-permute-start(bf16[768,1280]{1,0:T(8,128)(2,1)} %refs_10_.1), channel_id=1, source_target_pairs={{0,2},{2,0},{1,3},{3,1},{4,6},{6,4},{5,7},{7,5},{8,10},{10,8},{9,1... | collective-permute-start | bytes 5898248 | tf_op jit(solution)/shard_map/ppermute | solution.py:212
  2.7 1.0 collective-permute-start.21
  3.7 41.9 %collective-permute-done.22.refs_12_ = bf16[768,1280]{1,0:T(8,128)(2,1)} collective-permute-done((bf16[768,1280]{1,0:T(8,128)(2,1)}, bf16[768,1280]{1,0:T(8,128)(2,1)}, u32[]{:S(2)}, u32[]{:S(2)}) %collective-permute-start.22) | collective-permute-done | bytes 1966112 | tf_op jit(solution)/shard_map/ppermute | solution.py:212
  45.6 1.2 collective-permute-start.23
  46.8 0.1 stack.76.place
  46.9 0.9 copy-done.1
  47.9 0.9 copy-done.2
  48.8 0.9 copy-done.3
  49.8 0.6 shard_map.95
  50.4 2.6 %collective-permute-start.10 = (bf16[80,384]{1,0:T(8,128)(2,1)S(1)}, bf16[80,384]{1,0:T(8,128)(2,1)S(1)}, u32[]{:S(2)}, u32[]{:S(2)}) collective-permute-start(bf16[80,384]{1,0:T(8,128)(2,1)S(1)} %get-tuple-element.20), channel_id=1, source_target_pairs={{0,1},{1,9},{4,5},{5,13},{8,0},{9,8},{12,4},{13,12},{2,3},{3,11},{... | collective-permute-start | bytes 184328 | tf_op jit(solution)/shard_map/ppermute | solution.py:235
  53.0 1.1 collective-permute-start.11
  54.1 1.9 %collective-permute-start.8 = (bf16[80,384]{1,0:T(8,128)(2,1)S(1)}, bf16[80,384]{1,0:T(8,128)(2,1)S(1)}, u32[]{:S(2)}, u32[]{:S(2)}) collective-permute-start(bf16[80,384]{1,0:T(8,128)(2,1)S(1)} %get-tuple-element.18), channel_id=1, source_target_pairs={{0,0},{1,8},{4,4},{5,12},{8,1},{9,9},{12,5},{13,13},{2,2},{3,10},{... | collective-permute-start | bytes 184328 | tf_op jit(solution)/shard_map/ppermute | solution.py:235
  56.0 4.5 %collective-permute-start = (bf16[160,384]{1,0:T(8,128)(2,1)S(1)}, bf16[160,384]{1,0:T(8,128)(2,1)S(1)}, u32[]{:S(2)}, u32[]{:S(2)}) collective-permute-start(bf16[160,384]{1,0:T(8,128)(2,1)S(1)} %get-tuple-element.14), channel_id=1, source_target_pairs={{0,0},{1,8},{4,4},{5,12},{8,1},{9,9},{12,5},{13,13},{2,2},{3,10},{... | collective-permute-start | bytes 368648 | tf_op jit(solution)/shard_map/ppermute | solution.py:235
  60.6 0.4 collective-permute-start.1
  61.0 0.1 collective-permute-done.8.refs_8_
  61.1 3.1 %collective-permute-start.9 = (bf16[80,384]{1,0:T(8,128)(2,1)S(1)}, bf16[80,384]{1,0:T(8,128)(2,1)S(1)}, u32[]{:S(2)}, u32[]{:S(2)}) collective-permute-start(bf16[80,384]{1,0:T(8,128)(2,1)S(1)} %get-tuple-element.19), channel_id=1, source_target_pairs={{0,4},{1,12},{4,0},{5,8},{8,5},{9,13},{12,1},{13,9},{2,6},{3,14},{... | collective-permute-start | bytes 184328 | tf_op jit(solution)/shard_map/ppermute | solution.py:235
  64.2 3.3 %collective-permute-done.9.refs_9_ = bf16[80,384]{1,0:T(8,128)(2,1)S(1)} collective-permute-done((bf16[80,384]{1,0:T(8,128)(2,1)S(1)}, bf16[80,384]{1,0:T(8,128)(2,1)S(1)}, u32[]{:S(2)}, u32[]{:S(2)}) %collective-permute-start.9) | collective-permute-done | bytes 61472 | tf_op jit(solution)/shard_map/ppermute | solution.py:235
  67.5 2.3 %collective-permute-start.3 = (bf16[160,384]{1,0:T(8,128)(2,1)S(1)}, bf16[160,384]{1,0:T(8,128)(2,1)S(1)}, u32[]{:S(2)}, u32[]{:S(2)}) collective-permute-start(bf16[160,384]{1,0:T(8,128)(2,1)S(1)} %get-tuple-element.17), channel_id=1, source_target_pairs={{0,5},{1,13},{4,1},{5,9},{8,4},{9,12},{12,0},{13,8},{2,7},{3,15},{... | collective-permute-start | bytes 368648 | tf_op jit(solution)/shard_map/ppermute | solution.py:235
  69.9 5.4 %collective-permute-start.5 = (bf16[160,384]{1,0:T(8,128)(2,1)S(1)}, bf16[160,384]{1,0:T(8,128)(2,1)S(1)}, u32[]{:S(2)}, u32[]{:S(2)}) collective-permute-start(bf16[160,384]{1,0:T(8,128)(2,1)S(1)} %collective-permute-done.1.refs_1_), channel_id=1, source_target_pairs={{0,1},{1,0},{2,3},{3,2},{4,5},{5,4},{6,7},{7,6},{8,9},{9,8},{10,11... | collective-permute-start | bytes 368648 | tf_op jit(solution)/shard_map/ppermute | solution.py:237
  75.3 0.4 collective-permute-start.6
  75.7 0.2 collective-permute-start.7
  75.8 0.1 stack.71.place
  75.9 0.4 collective-permute-done.5.refs_5_
  76.3 0.4 collective-permute-done.6.refs_6_
  76.6 0.4 collective-permute-done.7.refs_7_
  77.0 2.3 %shard_map.96 = (bf16[160,384]{1,0:T(8,128)(2,1)S(1)}, bf16[160,384]{1,0:T(8,128)(2,1)S(1)}) custom-call(s32[8]{0:T(128)S(1)} %stack.71.place, bf16[160,384]{1,0:T(8,128)(2,1)S(1)} %collective-permute-done.refs_0_, bf16[160,384]{1,0:T(8,128)(2,1)S(1)} %collective-permute-done.1.refs_1_, bf16[160,384]{1,0:T(8,128)(2,1)S(1)} %collective-permute-done.2.refs_2_, ...), custom_call_target="tpu_custom_call" | custom-call | tf_op jit(solution)/shard_map/pallas_call | solution.py:181
  79.3 1.3 collective-permute-start.12
  80.6 0.6 collective-permute-start.15
  81.2 0.9 collective-permute-start.13
  82.1 2.0 %collective-permute-done.12.refs_1_ = bf16[160,384]{1,0:T(8,128)(2,1)S(1)} collective-permute-done((bf16[160,384]{1,0:T(8,128)(2,1)S(1)}, bf16[160,384]{1,0:T(8,128)(2,1)S(1)}, u32[]{:S(2)}, u32[]{:S(2)}) %collective-permute-start.12) | collective-permute-done | bytes 122912 | tf_op jit(solution)/shard_map/ppermute | solution.py:255
  84.1 0.7 collective-permute-start.17
  84.8 3.4 %collective-permute-done.15.refs_4_ = bf16[160,384]{1,0:T(8,128)(2,1)S(1)} collective-permute-done((bf16[160,384]{1,0:T(8,128)(2,1)S(1)}, bf16[160,384]{1,0:T(8,128)(2,1)S(1)}, u32[]{:S(2)}, u32[]{:S(2)}) %collective-permute-start.15) | collective-permute-done | bytes 122912 | tf_op jit(solution)/shard_map/ppermute | solution.py:260
  88.1 0.7 collective-permute-start.16
  88.8 1.9 %collective-permute-start.14 = (bf16[160,384]{1,0:T(8,128)(2,1)S(1)}, bf16[160,384]{1,0:T(8,128)(2,1)S(1)}, u32[]{:S(2)}, u32[]{:S(2)}) collective-permute-start(bf16[160,384]{1,0:T(8,128)(2,1)S(1)} %collective-permute-done.12.refs_1_), channel_id=1, source_target_pairs={{0,4},{4,0},{8,12},{12,8},{1,5},{5,1},{9,13},{13,9},{2,6},{6,2},{1... | collective-permute-start | bytes 368648 | tf_op jit(solution)/shard_map/ppermute | solution.py:259
  90.7 0.7 collective-permute-start.18
  91.4 5.6 %collective-permute-done.16.refs_5_ = bf16[160,384]{1,0:T(8,128)(2,1)S(1)} collective-permute-done((bf16[160,384]{1,0:T(8,128)(2,1)S(1)}, bf16[160,384]{1,0:T(8,128)(2,1)S(1)}, u32[]{:S(2)}, u32[]{:S(2)}) %collective-permute-start.16) | collective-permute-done | bytes 122912 | tf_op jit(solution)/shard_map/ppermute | solution.py:260
  97.0 1.3 collective-permute-start.19
  98.3 1.3 %collective-permute-start.20 = (bf16[160,384]{1,0:T(8,128)(2,1)S(1)}, bf16[160,384]{1,0:T(8,128)(2,1)S(1)}, u32[]{:S(2)}, u32[]{:S(2)}) collective-permute-start(bf16[160,384]{1,0:T(8,128)(2,1)S(1)} %collective-permute-done.16.refs_5_), channel_id=1, source_target_pairs={{4,0},{8,12},{5,1},{9,13},{6,2},{10,14},{7,3},{11,15},{20,16},{24,... | collective-permute-start | bytes 368648 | tf_op jit(solution)/shard_map/ppermute | solution.py:262
  99.6 0.7 convert_element_type.7
  100.3 0.1 stack.67.place
  100.4 2.2 %collective-permute-done.19.refs_8_ = bf16[160,384]{1,0:T(8,128)(2,1)S(1)} collective-permute-done((bf16[160,384]{1,0:T(8,128)(2,1)S(1)}, bf16[160,384]{1,0:T(8,128)(2,1)S(1)}, u32[]{:S(2)}, u32[]{:S(2)}) %collective-permute-start.19) | collective-permute-done | bytes 122912 | tf_op jit(solution)/shard_map/ppermute | solution.py:262
  102.6 1.3 %collective-permute-done.20.refs_9_ = bf16[160,384]{1,0:T(8,128)(2,1)S(1)} collective-permute-done((bf16[160,384]{1,0:T(8,128)(2,1)S(1)}, bf16[160,384]{1,0:T(8,128)(2,1)S(1)}, u32[]{:S(2)}, u32[]{:S(2)}) %collective-permute-start.20) | collective-permute-done | bytes 122912 | tf_op jit(solution)/shard_map/ppermute | solution.py:262
  103.9 4.3 %shard_map.97 = (bf16[80,1280]{1,0:T(8,128)(2,1)S(1)}, bf16[80,1280]{1,0:T(8,128)(2,1)S(1)}) custom-call(s32[6]{0:T(128)S(1)} %stack.67.place, bf16[160,384]{1,0:T(8,128)(2,1)S(1)} %get-tuple-element.22.refs_0_, bf16[160,384]{1,0:T(8,128)(2,1)S(1)} %collective-permute-done.12.refs_1_, bf16[160,384]{1,0:T(8,128)(2,1)S(1)} %collective-permute-done.13.refs_2_, ...), custom_call_target="tpu_custom_call" | custom-call | tf_op jit(solution)/shard_map/pallas_call | solution.py:181
  108.3 4.9 %collective-permute-start.24 = (bf16[80,1280]{1,0:T(8,128)(2,1)S(1)}, bf16[80,1280]{1,0:T(8,128)(2,1)S(1)}, u32[]{:S(2)}, u32[]{:S(2)}) collective-permute-start(bf16[80,1280]{1,0:T(8,128)(2,1)S(1)} %get-tuple-element.24), channel_id=1, source_target_pairs={{0,0},{1,8},{2,4},{3,12},{4,1},{5,9},{6,5},{7,13},{8,2},{9,10},{10... | collective-permute-start | bytes 614408 | tf_op jit(solution)/shard_map/ppermute | solution.py:294
  113.2 0.3 multiply_reduce_fusion
  113.6 12.5 %collective-permute-done.24 = bf16[80,1280]{1,0:T(8,128)(2,1)S(1)} collective-permute-done((bf16[80,1280]{1,0:T(8,128)(2,1)S(1)}, bf16[80,1280]{1,0:T(8,128)(2,1)S(1)}, u32[]{:S(2)}, u32[]{:S(2)}) %collective-permute-start.24) | collective-permute-done | bytes 204832 | tf_op jit(solution)/shard_map/ppermute | solution.py:294
  126.1 1.4 %collective-permute-done.25 = bf16[80,1280]{1,0:T(8,128)(2,1)S(1)} collective-permute-done((bf16[80,1280]{1,0:T(8,128)(2,1)S(1)}, bf16[80,1280]{1,0:T(8,128)(2,1)S(1)}, u32[]{:S(2)}, u32[]{:S(2)}) %collective-permute-start.25) | collective-permute-done | bytes 204832 | tf_op jit(solution)/shard_map/ppermute | solution.py:294
  127.5 1.4 %add_add_fusion = (f32[160,1280]{1,0:T(8,128)}, f32[160,1280]{1,0:T(8,128)}) fusion(f32[160,1280]{1,0:T(8,128)S(1)} %copy-done.5, f32[160,1280]{1,0:T(8,128)S(1)} %multiply_reduce_fusion, f32[1280]{0:T(1024)S(1)} %copy-done.6, bf16[80,1280]{1,0:T(8,128)(2,1)S(1)} %get-tuple-element.29, bf16[80,1280]{1,0:T(8,128)(2,1)S(1)} %get-tuple-element.28), kind=kLoop, calls=%fused_computation.2 | loop fusion | flops 1433600 | bytes 3691520 | tf_op jit(solution)/shard_map/add | solution.py:306
  (28 shorter events, 0.2 us)
Async XLA Ops:
  0.6 103.3 %copy-start = (bf16[768,1280]{1,0:T(8,128)(2,1)S(1)}, bf16[768,1280]{1,0:T(8,128)(2,1)}, u32[]{:S(2)}) copy-start(bf16[768,1280]{1,0:T(8,128)(2,1)} %refs_10_.1) | copy-start | bytes 5898244
  0.6 45.0 %collective-permute-start.22 = (bf16[768,1280]{1,0:T(8,128)(2,1)}, bf16[768,1280]{1,0:T(8,128)(2,1)}, u32[]{:S(2)}, u32[]{:S(2)}) collective-permute-start(bf16[768,1280]{1,0:T(8,128)(2,1)} %refs_10_.1), channel_id=1, source_target_pairs={{0,2},{2,0},{1,3},{3,1},{4,6},{6,4},{5,7},{7,5},{8,10},{10,8},{9,1... | collective-permute-start | bytes 5898248 | tf_op jit(solution)/shard_map/ppermute | solution.py:212
  2.7 101.2 %collective-permute-start.21 = (bf16[768,1280]{1,0:T(8,128)(2,1)}, bf16[768,1280]{1,0:T(8,128)(2,1)}, u32[]{:S(2)}, u32[]{:S(2)}) collective-permute-start(bf16[768,1280]{1,0:T(8,128)(2,1)} %refs_10_.1), channel_id=1, source_target_pairs={{0,1},{1,0},{2,3},{3,2},{4,5},{5,4},{6,7},{7,6},{8,9},{9,8},{10,11... | collective-permute-start | bytes 5898248 | tf_op jit(solution)/shard_map/ppermute | solution.py:213
  45.6 58.3 %collective-permute-start.23 = (bf16[768,1280]{1,0:T(8,128)(2,1)}, bf16[768,1280]{1,0:T(8,128)(2,1)}, u32[]{:S(2)}, u32[]{:S(2)}) collective-permute-start(bf16[768,1280]{1,0:T(8,128)(2,1)} %collective-permute-done.22.refs_12_), channel_id=1, source_target_pairs={{0,1},{1,0},{2,3},{3,2},{4,5},{5,4},{6,7},{7,6},{8,9},{9,8},{10,11... | collective-permute-start | bytes 5898248 | tf_op jit(solution)/shard_map/ppermute | solution.py:214
  46.9 0.9 copy-start.1
  47.9 0.9 copy-start.2
  48.8 0.9 copy-start.3
  50.4 5.6 %collective-permute-start.10 = (bf16[80,384]{1,0:T(8,128)(2,1)S(1)}, bf16[80,384]{1,0:T(8,128)(2,1)S(1)}, u32[]{:S(2)}, u32[]{:S(2)}) collective-permute-start(bf16[80,384]{1,0:T(8,128)(2,1)S(1)} %get-tuple-element.20), channel_id=1, source_target_pairs={{0,1},{1,9},{4,5},{5,13},{8,0},{9,8},{12,4},{13,12},{2,3},{3,11},{... | collective-permute-start | bytes 184328 | tf_op jit(solution)/shard_map/ppermute | solution.py:235
  53.0 7.6 %collective-permute-start.11 = (bf16[80,384]{1,0:T(8,128)(2,1)S(1)}, bf16[80,384]{1,0:T(8,128)(2,1)S(1)}, u32[]{:S(2)}, u32[]{:S(2)}) collective-permute-start(bf16[80,384]{1,0:T(8,128)(2,1)S(1)} %get-tuple-element.21), channel_id=1, source_target_pairs={{0,5},{1,13},{4,1},{5,9},{8,4},{9,12},{12,0},{13,8},{2,7},{3,15},{... | collective-permute-start | bytes 184328 | tf_op jit(solution)/shard_map/ppermute | solution.py:235
  54.1 7.0 %collective-permute-start.8 = (bf16[80,384]{1,0:T(8,128)(2,1)S(1)}, bf16[80,384]{1,0:T(8,128)(2,1)S(1)}, u32[]{:S(2)}, u32[]{:S(2)}) collective-permute-start(bf16[80,384]{1,0:T(8,128)(2,1)S(1)} %get-tuple-element.18), channel_id=1, source_target_pairs={{0,0},{1,8},{4,4},{5,12},{8,1},{9,9},{12,5},{13,13},{2,2},{3,10},{... | collective-permute-start | bytes 184328 | tf_op jit(solution)/shard_map/ppermute | solution.py:235
  56.0 11.5 %collective-permute-start = (bf16[160,384]{1,0:T(8,128)(2,1)S(1)}, bf16[160,384]{1,0:T(8,128)(2,1)S(1)}, u32[]{:S(2)}, u32[]{:S(2)}) collective-permute-start(bf16[160,384]{1,0:T(8,128)(2,1)S(1)} %get-tuple-element.14), channel_id=1, source_target_pairs={{0,0},{1,8},{4,4},{5,12},{8,1},{9,9},{12,5},{13,13},{2,2},{3,10},{... | collective-permute-start | bytes 368648 | tf_op jit(solution)/shard_map/ppermute | solution.py:235
  60.6 9.3 %collective-permute-start.1 = (bf16[160,384]{1,0:T(8,128)(2,1)S(1)}, bf16[160,384]{1,0:T(8,128)(2,1)S(1)}, u32[]{:S(2)}, u32[]{:S(2)}) collective-permute-start(bf16[160,384]{1,0:T(8,128)(2,1)S(1)} %get-tuple-element.15), channel_id=1, source_target_pairs={{0,4},{1,12},{4,0},{5,8},{8,5},{9,13},{12,1},{13,9},{2,6},{3,14},{... | collective-permute-start | bytes 368648 | tf_op jit(solution)/shard_map/ppermute | solution.py:235
  61.1 6.4 %collective-permute-start.9 = (bf16[80,384]{1,0:T(8,128)(2,1)S(1)}, bf16[80,384]{1,0:T(8,128)(2,1)S(1)}, u32[]{:S(2)}, u32[]{:S(2)}) collective-permute-start(bf16[80,384]{1,0:T(8,128)(2,1)S(1)} %get-tuple-element.19), channel_id=1, source_target_pairs={{0,4},{1,12},{4,0},{5,8},{8,5},{9,13},{12,1},{13,9},{2,6},{3,14},{... | collective-permute-start | bytes 184328 | tf_op jit(solution)/shard_map/ppermute | solution.py:235
  67.5 2.4 %collective-permute-start.2 = (bf16[160,384]{1,0:T(8,128)(2,1)S(1)}, bf16[160,384]{1,0:T(8,128)(2,1)S(1)}, u32[]{:S(2)}, u32[]{:S(2)}) collective-permute-start(bf16[160,384]{1,0:T(8,128)(2,1)S(1)} %get-tuple-element.16), channel_id=1, source_target_pairs={{0,1},{1,9},{4,5},{5,13},{8,0},{9,8},{12,4},{13,12},{2,3},{3,11},{... | collective-permute-start | bytes 368648 | tf_op jit(solution)/shard_map/ppermute | solution.py:235
  67.5 7.8 %collective-permute-start.3 = (bf16[160,384]{1,0:T(8,128)(2,1)S(1)}, bf16[160,384]{1,0:T(8,128)(2,1)S(1)}, u32[]{:S(2)}, u32[]{:S(2)}) collective-permute-start(bf16[160,384]{1,0:T(8,128)(2,1)S(1)} %get-tuple-element.17), channel_id=1, source_target_pairs={{0,5},{1,13},{4,1},{5,9},{8,4},{9,12},{12,0},{13,8},{2,7},{3,15},{... | collective-permute-start | bytes 368648 | tf_op jit(solution)/shard_map/ppermute | solution.py:235
  69.9 5.8 %collective-permute-start.4 = (bf16[160,384]{1,0:T(8,128)(2,1)S(1)}, bf16[160,384]{1,0:T(8,128)(2,1)S(1)}, u32[]{:S(2)}, u32[]{:S(2)}) collective-permute-start(bf16[160,384]{1,0:T(8,128)(2,1)S(1)} %collective-permute-done.refs_0_), channel_id=1, source_target_pairs={{0,1},{1,0},{2,3},{3,2},{4,5},{5,4},{6,7},{7,6},{8,9},{9,8},{10,11... | collective-permute-start | bytes 368648 | tf_op jit(solution)/shard_map/ppermute | solution.py:237
  69.9 6.4 %collective-permute-start.5 = (bf16[160,384]{1,0:T(8,128)(2,1)S(1)}, bf16[160,384]{1,0:T(8,128)(2,1)S(1)}, u32[]{:S(2)}, u32[]{:S(2)}) collective-permute-start(bf16[160,384]{1,0:T(8,128)(2,1)S(1)} %collective-permute-done.1.refs_1_), channel_id=1, source_target_pairs={{0,1},{1,0},{2,3},{3,2},{4,5},{5,4},{6,7},{7,6},{8,9},{9,8},{10,11... | collective-permute-start | bytes 368648 | tf_op jit(solution)/shard_map/ppermute | solution.py:237
  75.3 1.3 %collective-permute-start.6 = (bf16[160,384]{1,0:T(8,128)(2,1)S(1)}, bf16[160,384]{1,0:T(8,128)(2,1)S(1)}, u32[]{:S(2)}, u32[]{:S(2)}) collective-permute-start(bf16[160,384]{1,0:T(8,128)(2,1)S(1)} %collective-permute-done.2.refs_2_), channel_id=1, source_target_pairs={{0,1},{1,0},{2,3},{3,2},{4,5},{5,4},{6,7},{7,6},{8,9},{9,8},{10,11... | collective-permute-start | bytes 368648 | tf_op jit(solution)/shard_map/ppermute | solution.py:237
  75.7 1.3 %collective-permute-start.7 = (bf16[160,384]{1,0:T(8,128)(2,1)S(1)}, bf16[160,384]{1,0:T(8,128)(2,1)S(1)}, u32[]{:S(2)}, u32[]{:S(2)}) collective-permute-start(bf16[160,384]{1,0:T(8,128)(2,1)S(1)} %collective-permute-done.3.refs_3_), channel_id=1, source_target_pairs={{0,1},{1,0},{2,3},{3,2},{4,5},{5,4},{6,7},{7,6},{8,9},{9,8},{10,11... | collective-permute-start | bytes 368648 | tf_op jit(solution)/shard_map/ppermute | solution.py:237
  79.3 4.8 %collective-permute-start.12 = (bf16[160,384]{1,0:T(8,128)(2,1)S(1)}, bf16[160,384]{1,0:T(8,128)(2,1)S(1)}, u32[]{:S(2)}, u32[]{:S(2)}) collective-permute-start(bf16[160,384]{1,0:T(8,128)(2,1)S(1)} %get-tuple-element.23), channel_id=1, source_target_pairs={{0,2},{2,0},{1,3},{3,1},{4,6},{6,4},{5,7},{7,5},{8,10},{10,8},{9,1... | collective-permute-start | bytes 368648 | tf_op jit(solution)/shard_map/ppermute | solution.py:255
  80.6 7.6 %collective-permute-start.15 = (bf16[160,384]{1,0:T(8,128)(2,1)S(1)}, bf16[160,384]{1,0:T(8,128)(2,1)S(1)}, u32[]{:S(2)}, u32[]{:S(2)}) collective-permute-start(bf16[160,384]{1,0:T(8,128)(2,1)S(1)} %get-tuple-element.22.refs_0_), channel_id=1, source_target_pairs={{0,8},{8,0},{4,12},{12,4},{1,9},{9,1},{5,13},{13,5},{2,10},{10,2},... | collective-permute-start | bytes 368648 | tf_op jit(solution)/shard_map/ppermute | solution.py:260
  81.2 7.7 %collective-permute-start.13 = (bf16[160,384]{1,0:T(8,128)(2,1)S(1)}, bf16[160,384]{1,0:T(8,128)(2,1)S(1)}, u32[]{:S(2)}, u32[]{:S(2)}) collective-permute-start(bf16[160,384]{1,0:T(8,128)(2,1)S(1)} %get-tuple-element.22.refs_0_), channel_id=1, source_target_pairs={{0,4},{4,0},{8,12},{12,8},{1,5},{5,1},{9,13},{13,9},{2,6},{6,2},{1... | collective-permute-start | bytes 368648 | tf_op jit(solution)/shard_map/ppermute | solution.py:259
  84.1 6.6 %collective-permute-start.17 = (bf16[160,384]{1,0:T(8,128)(2,1)S(1)}, bf16[160,384]{1,0:T(8,128)(2,1)S(1)}, u32[]{:S(2)}, u32[]{:S(2)}) collective-permute-start(bf16[160,384]{1,0:T(8,128)(2,1)S(1)} %get-tuple-element.22.refs_0_), channel_id=1, source_target_pairs={{4,8},{8,4},{5,9},{9,5},{6,10},{10,6},{7,11},{11,7},{20,24},{24,20... | collective-permute-start | bytes 368648 | tf_op jit(solution)/shard_map/ppermute | solution.py:261
  88.1 8.9 %collective-permute-start.16 = (bf16[160,384]{1,0:T(8,128)(2,1)S(1)}, bf16[160,384]{1,0:T(8,128)(2,1)S(1)}, u32[]{:S(2)}, u32[]{:S(2)}) collective-permute-start(bf16[160,384]{1,0:T(8,128)(2,1)S(1)} %collective-permute-done.12.refs_1_), channel_id=1, source_target_pairs={{0,8},{8,0},{4,12},{12,4},{1,9},{9,1},{5,13},{13,5},{2,10},{10,2},... | collective-permute-start | bytes 368648 | tf_op jit(solution)/shard_map/ppermute | solution.py:260
  88.8 9.4 %collective-permute-start.14 = (bf16[160,384]{1,0:T(8,128)(2,1)S(1)}, bf16[160,384]{1,0:T(8,128)(2,1)S(1)}, u32[]{:S(2)}, u32[]{:S(2)}) collective-permute-start(bf16[160,384]{1,0:T(8,128)(2,1)S(1)} %collective-permute-done.12.refs_1_), channel_id=1, source_target_pairs={{0,4},{4,0},{8,12},{12,8},{1,5},{5,1},{9,13},{13,9},{2,6},{6,2},{1... | collective-permute-start | bytes 368648 | tf_op jit(solution)/shard_map/ppermute | solution.py:259
  90.7 9.6 %collective-permute-start.18 = (bf16[160,384]{1,0:T(8,128)(2,1)S(1)}, bf16[160,384]{1,0:T(8,128)(2,1)S(1)}, u32[]{:S(2)}, u32[]{:S(2)}) collective-permute-start(bf16[160,384]{1,0:T(8,128)(2,1)S(1)} %collective-permute-done.12.refs_1_), channel_id=1, source_target_pairs={{4,8},{8,4},{5,9},{9,5},{6,10},{10,6},{7,11},{11,7},{20,24},{24,20... | collective-permute-start | bytes 368648 | tf_op jit(solution)/shard_map/ppermute | solution.py:261
  97.0 5.6 %collective-permute-start.19 = (bf16[160,384]{1,0:T(8,128)(2,1)S(1)}, bf16[160,384]{1,0:T(8,128)(2,1)S(1)}, u32[]{:S(2)}, u32[]{:S(2)}) collective-permute-start(bf16[160,384]{1,0:T(8,128)(2,1)S(1)} %collective-permute-done.15.refs_4_), channel_id=1, source_target_pairs={{4,0},{8,12},{5,1},{9,13},{6,2},{10,14},{7,3},{11,15},{20,16},{24,... | collective-permute-start | bytes 368648 | tf_op jit(solution)/shard_map/ppermute | solution.py:262
  98.3 5.6 %collective-permute-start.20 = (bf16[160,384]{1,0:T(8,128)(2,1)S(1)}, bf16[160,384]{1,0:T(8,128)(2,1)S(1)}, u32[]{:S(2)}, u32[]{:S(2)}) collective-permute-start(bf16[160,384]{1,0:T(8,128)(2,1)S(1)} %collective-permute-done.16.refs_5_), channel_id=1, source_target_pairs={{4,0},{8,12},{5,1},{9,13},{6,2},{10,14},{7,3},{11,15},{20,16},{24,... | collective-permute-start | bytes 368648 | tf_op jit(solution)/shard_map/ppermute | solution.py:262
  100.4 12.9 %copy-start.4 = (f32[4,160,1280]{2,1,0:T(8,128)S(1)}, f32[4,160,1280]{2,1,0:T(8,128)}, u32[]{:S(2)}) copy-start(f32[4,160,1280]{2,1,0:T(8,128)} %param.14) | copy-start | bytes 9830404
  108.2 19.3 %copy-start.5 = (f32[160,1280]{1,0:T(8,128)S(1)}, f32[160,1280]{1,0:T(8,128)}, u32[]{:S(2)}) copy-start(f32[160,1280]{1,0:T(8,128)} %param.13) | copy-start | bytes 2457604
  108.2 19.3 %copy-start.6 = (f32[1280]{0:T(1024)S(1)}, f32[1280]{0:T(1024)}, u32[]{:S(2)}) copy-start(f32[1280]{0:T(1024)} %param.12) | copy-start | bytes 15364
  108.3 17.8 %collective-permute-start.24 = (bf16[80,1280]{1,0:T(8,128)(2,1)S(1)}, bf16[80,1280]{1,0:T(8,128)(2,1)S(1)}, u32[]{:S(2)}, u32[]{:S(2)}) collective-permute-start(bf16[80,1280]{1,0:T(8,128)(2,1)S(1)} %get-tuple-element.24), channel_id=1, source_target_pairs={{0,0},{1,8},{2,4},{3,12},{4,1},{5,9},{6,5},{7,13},{8,2},{9,10},{10... | collective-permute-start | bytes 614408 | tf_op jit(solution)/shard_map/ppermute | solution.py:294
  113.2 14.3 %collective-permute-start.25 = (bf16[80,1280]{1,0:T(8,128)(2,1)S(1)}, bf16[80,1280]{1,0:T(8,128)(2,1)S(1)}, u32[]{:S(2)}, u32[]{:S(2)}) collective-permute-start(bf16[80,1280]{1,0:T(8,128)(2,1)S(1)} %get-tuple-element.25), channel_id=1, source_target_pairs={{0,8},{1,0},{2,12},{3,4},{4,9},{5,1},{6,13},{7,5},{8,10},{9,2},{10... | collective-permute-start | bytes 614408 | tf_op jit(solution)/shard_map/ppermute | solution.py:294

commit v2 on v1

--- a/solution.py
+++ b/solution.py
@@ -8,7 +8,7 @@
 from jax.sharding import PartitionSpec as P
 
 HEAD_DIM = 128
-VMEM_BYTES = 48 * 1024 * 1024
+VMEM_BYTES = 16 * 1024 * 1024
 
 
 def attend(state_in, key_rows, value_rows, query_heads, score_scale):
@@ -87,25 +87,46 @@
     return (mixed_state, fresh_delta)
 
 
-def pack_kernel(place, queries, keys, values, *outs):
-    half, width = outs[0].shape[0] // 2, outs[0].shape[1]
+def pack_kernel(place, queries, keys, values, *refs):
+    outs, sems = refs[:4], refs[4]
+    half, width = outs[0].shape[0] // 3, outs[0].shape[1]
+    copies = []
     for k in range(4):
         rows = pl.ds(pl.multiple_of(place[2 * k], 16), half)
         columns = pl.ds(pl.multiple_of(place[2 * k + 1], 128), width)
-        outs[k][:half, :] = keys[rows, columns]
-        outs[k][half:, :] = values[rows, columns]
-        outs[4 + k][...] = queries[rows, columns]
+        for i, source in enumerate((keys, values, queries)):
+            copies.append(
+                pltpu.make_async_copy(
+                    source.at[rows, columns],
+                    outs[k].at[pl.ds(i * half, half), :],
+                    sems.at[3 * k + i],
+                )
+            )
+    for copy in copies:
+        copy.start()
+    for copy in copies:
+        copy.wait()
+
+
+def join_kernel(place, *refs):
+    blocks, joined = refs[:-1], refs[-1]
+    rows = joined.shape[0] // len(blocks)
+    for k, block in enumerate(blocks):
+        joined[k * rows : (k + 1) * rows, :] = block[:rows, :]
 
 
 def attention_kernel(place, *refs):
-    kv_blocks, query_blocks = refs[:8], refs[8:12]
-    own, other, key_all, value_all, query_all, both = refs[12:]
-    half = query_blocks[0].shape[0]
-    for k in range(8):
-        key_all[k * half : (k + 1) * half, :] = kv_blocks[k][:half, :]
-        value_all[k * half : (k + 1) * half, :] = kv_blocks[k][half:, :]
-    for k in range(4):
-        query_all[k * half : (k + 1) * half, :] = query_blocks[k][...]
+    blocks, sibling = refs[:4], refs[4]
+    own, other, key_all, value_all, query_all, both = refs[5:]
+    half = blocks[0].shape[0] // 3
+    for k in range(4):
+        key_all[k * half : (k + 1) * half, :] = blocks[k][:half, :]
+        value_all[k * half : (k + 1) * half, :] = blocks[k][half : 2 * half, :]
+        query_all[k * half : (k + 1) * half, :] = blocks[k][2 * half :, :]
+        key_all[(4 + k) * half : (5 + k) * half, :] = sibling[2 * k * half : (2 * k + 1) * half, :]
+        value_all[(4 + k) * half : (5 + k) * half, :] = sibling[
+            (2 * k + 1) * half : (2 * k + 2) * half, :
+        ]
     for h in range(own.shape[1] // HEAD_DIM):
         columns = slice(h * HEAD_DIM, (h + 1) * HEAD_DIM)
         scores = lax.dot_general(
@@ -128,64 +149,62 @@
     other[...] = both[1]
 
 
-def project_kernel(place, *refs):
-    shards, weights = refs[:10], refs[10:14]
-    out0, out1, held, weight_held, total, sems = refs[14:]
-    copies = [
-        pltpu.make_async_copy(weights[b], weight_held.at[b], sems.at[b]) for b in range(4)
-    ]
-    for copy in copies:
-        copy.start()
-    for side in range(2):
-        for m in range(3):
-            held[side, m] = shards[2 * m + side][...]
-        far = place[4] == 1
-
-        @pl.when(far)
+def add_term(total, left, pick, row, first, second):
+    rows = pl.ds(pl.multiple_of(row, 128), left.shape[1])
+    for value, weight in enumerate((first, second)):
+
+        @pl.when(pick == value)
         def _():
-            held[side, 3] = shards[8 + side][...]
-
-        @pl.when(jnp.logical_not(far))
-        def _():
-            held[side, 3] = shards[6 + side][...]
-
-    width = held.shape[3]
-    for b in range(4):
-        side, other_core = b // 2, b % 2
-        copies[b].wait()
-        part = jnp.dot(
-            held[side, place[2 * other_core]],
-            weight_held[b, :width, :],
-            preferred_element_type=jnp.float32,
-        )
-        part = part + jnp.dot(
-            held[side, place[2 * other_core + 1]],
-            weight_held[b, width:, :],
-            preferred_element_type=jnp.float32,
-        )
-        if b == 0:
-            total[...] = part
-        else:
-            total[...] += part
+            total[...] += jnp.dot(left, weight[rows, :], preferred_element_type=jnp.float32)
+
+
+def early_kernel(place, own, near, two, weight, weight_c, total):
+    width = own.shape[1] // 2
+    total[...] = jnp.zeros_like(total)
+    for m, shard in enumerate((own, near, two)):
+        add_term(total, shard[:, :width], place[2 * m], place[2 * m + 1], weight, weight_c)
+
+
+def late_kernel(place, *refs):
+    total_in, shards, weights = refs[0], refs[1:6], refs[6:12]
+    out0, out1, held, left, total = refs[12:]
+    far = jnp.where(place[5] == 1, shards[4][...], shards[3][...])
+    width = far.shape[1] // 2
+    for m in range(3):
+        held[m] = shards[m][:, width:]
+    held[3] = far[:, width:]
+    total[...] = total_in[...]
+    add_term(total, far[:, :width], place[6], place[7], weights[0], weights[1])
+    for b in range(2):
+        for low in range(2):
+            left[b, :, low * width : (low + 1) * width] = held[place[2 * b + low]]
+        row = 0
+        for block in weights[2 + 2 * b : 4 + 2 * b]:
+            total[...] += jnp.dot(
+                left[b, :, row : row + block.shape[0]],
+                block[...],
+                preferred_element_type=jnp.float32,
+            )
+            row += block.shape[0]
     half = out0.shape[0]
-    first = pl.ds(pl.multiple_of(place[5], 16), half)
-    second = pl.ds(pl.multiple_of(half - place[5], 16), half)
+    first = pl.ds(pl.multiple_of(place[4], 16), half)
+    second = pl.ds(pl.multiple_of(half - place[4], 16), half)
     out0[...] = total[first, :].astype(out0.dtype)
     out1[...] = total[second, :].astype(out1.dtype)
 
 
-def call(kernel, place, args, outs, scratch=(), in_any=(), cost=None):
+def call(kernel, place, args, outs, scratch=(), in_any=(), vmem=VMEM_BYTES, dtype=jnp.bfloat16, flops=0):
     specs = [pl.BlockSpec(memory_space=pltpu.SMEM)]
     for i, _ in enumerate(args):
-        specs.append(pl.BlockSpec(memory_space=pl.ANY if i in in_any else pltpu.VMEM))
+        specs.append(pl.BlockSpec(memory_space=pltpu.HBM if i in in_any else pltpu.VMEM))
     return pl.pallas_call(
         kernel,
         in_specs=specs,
         out_specs=[pl.BlockSpec(memory_space=pltpu.VMEM)] * len(outs),
-        out_shape=[jax.ShapeDtypeStruct(shape, jnp.bfloat16) for shape in outs],
+        out_shape=[jax.ShapeDtypeStruct(shape, dtype) for shape in outs],
         scratch_shapes=list(scratch),
-        compiler_params=pltpu.CompilerParams(vmem_limit_bytes=VMEM_BYTES),
-        cost_estimate=cost,
+        compiler_params=pltpu.CompilerParams(vmem_limit_bytes=vmem),
+        cost_estimate=pl.CostEstimate(flops=flops, bytes_accessed=0, transcendentals=0),
     )(place, *args)
 
 
@@ -209,9 +228,10 @@
     zh, zl = z // 2, z % 2
     swap = [(0, 1), (1, 0)]
 
-    weight_x = lax.ppermute(out_weight, "wt", swap)
-    weight_c = lax.ppermute(out_weight, "head", swap)
-    weight_xc = lax.ppermute(weight_x, "head", swap)
+    depth, columns = out_weight.shape
+    cut = depth * 2 // 3 // HEAD_DIM * HEAD_DIM
+    weight_x0 = lax.ppermute(out_weight[:cut], "wt", swap)
+    weight_x1 = lax.ppermute(out_weight[cut:], "wt", swap)
 
     place = []
     for k in range(4):
@@ -221,20 +241,22 @@
         pack_kernel,
         scalars(*place),
         (queries, key_vectors, value_vectors),
-        [(rows, width)] * 4 + [(half, width)] * 4,
+        [(3 * half, width)] * 4,
+        [pltpu.SemaphoreType.DMA((12,))],
+        in_any=range(3),
+        vmem=60 * 1024 * 1024,
     )
     moved = []
-    for order in range(2):
-        for k in range(4):
-            k1, k0 = k // 2, k % 2
-            pairs = []
-            for zz in range(4):
-                for cc in range(2):
-                    to_z = 2 * cc + ((zz % 2) ^ k0)
-                    pairs.append((zz * 2 + cc, to_z * 2 + ((zz // 2) ^ k1)))
-            moved.append(lax.ppermute(packed[4 * order + k], ("seq", "head"), pairs))
-    kv_blocks, query_blocks = moved[:4], moved[4:]
-    kv_sibling = [lax.ppermute(block, "head", swap) for block in kv_blocks]
+    for k in range(4):
+        k1, k0 = k // 2, k % 2
+        pairs = []
+        for zz in range(4):
+            for cc in range(2):
+                to_z = 2 * cc + ((zz % 2) ^ k0)
+                pairs.append((zz * 2 + cc, to_z * 2 + ((zz // 2) ^ k1)))
+        moved.append(lax.ppermute(packed[k], ("seq", "head"), pairs))
+    (joined,) = call(join_kernel, scalars(0), moved, [(4 * rows, width)])
+    sibling = lax.ppermute(joined, "head", swap)
 
     place = []
     for k in range(4):
@@ -243,7 +265,7 @@
     own, other = call(
         attention_kernel,
         scalars(*place),
-        kv_blocks + kv_sibling + query_blocks,
+        moved + [sibling],
         [(rows, width)] * 2,
         [
             pltpu.VMEM((4 * rows, width), jnp.bfloat16),
@@ -251,36 +273,47 @@
             pltpu.VMEM((2 * rows, width), jnp.bfloat16),
             pltpu.VMEM((2, rows, width), jnp.bfloat16),
         ],
+        flops=4 * (2 * rows) * (4 * rows) * width,
     )
     cross = lax.ppermute(other, "wt", swap)
 
-    shards = []
-    for shard in (own, cross):
-        near = lax.ppermute(shard, "seq", [(0, 1), (1, 0), (2, 3), (3, 2)])
-        two = lax.ppermute(shard, "seq", [(0, 2), (2, 0), (1, 3), (3, 1)])
-        middle = lax.ppermute(shard, "seq", [(1, 2), (2, 1)])
-        ends = lax.ppermute(two, "seq", [(1, 0), (2, 3)])
-        shards.append([shard, near, two, middle, ends])
-    flat = [shards[side][m] for m in range(5) for side in range(2)]
-
+    shard = jnp.concatenate([own, cross], axis=1)
+    near = lax.ppermute(shard, "seq", [(0, 1), (1, 0), (2, 3), (3, 2)])
+    two = lax.ppermute(shard, "seq", [(0, 2), (2, 0), (1, 3), (3, 1)])
+    late_c, _ = lax.optimization_barrier((out_weight, cross))
+    weight_c = lax.ppermute(late_c, "head", swap)
+    late_shard, late_two, _ = lax.optimization_barrier((shard, two, near))
+    middle = lax.ppermute(late_shard, "seq", [(1, 2), (2, 1)])
+    ends = lax.ppermute(late_two, "seq", [(1, 0), (2, 3)])
     place = []
-    for other_core in range(2):
-        for low in range(2):
-            place.append((2 * (c ^ other_core) + low) ^ z)
-    place += [(zh == zl).astype(jnp.int32), c * half]
-    depth, columns = out_weight.shape
+    for m in range(4):
+        place += [(zh ^ (m // 2)) ^ c, (zl ^ (m % 2)) * width]
+    (early,) = call(
+        early_kernel,
+        scalars(*place[:6]),
+        (shard, near, two, out_weight, weight_c),
+        [(rows, columns)],
+        dtype=jnp.float32,
+        flops=6 * rows * width * columns,
+    )
+    late_x0, _ = lax.optimization_barrier((weight_x0, cross))
+    late_x1, _, _ = lax.optimization_barrier((weight_x1, middle, ends))
+    weight_xc0 = lax.ppermute(late_x0, "head", swap)
+    weight_xc1 = lax.ppermute(late_x1, "head", swap)
+    late_place = [(2 * (c ^ b) + low) ^ z for b in range(2) for low in range(2)]
+    late_place += [c * half, (zh == zl).astype(jnp.int32)] + place[6:]
     out0, out1 = call(
-        project_kernel,
-        scalars(*place),
-        flat + [out_weight, weight_c, weight_x, weight_xc],
+        late_kernel,
+        scalars(*late_place),
+        [early, shard, near, two, middle, ends, out_weight, weight_c]
+        + [weight_x0, weight_x1, weight_xc0, weight_xc1],
         [(half, columns)] * 2,
         [
-            pltpu.VMEM((2, 4, rows, width), jnp.bfloat16),
-            pltpu.VMEM((4, depth, columns), jnp.bfloat16),
+            pltpu.VMEM((4, rows, width), jnp.bfloat16),
+            pltpu.VMEM((2, rows, 2 * width), jnp.bfloat16),
             pltpu.VMEM((rows, columns), jnp.float32),
-            pltpu.SemaphoreType.DMA((4,)),
         ],
-        in_any=range(10, 14),
+        flops=10 * rows * width * columns,
     )
 
     arrived = []

time: 129 us -> 106 us (0.82)
  waiting for transfers between devices: 74.9 us -> 46.3 us
  starting transfers between devices: 40.5 us -> 31.7 us
  local copies, waits for them, and re-layouts: 3.11 us -> 11.6 us
  Pallas kernels: 7.18 us -> 13 us
    ppermute x19 -> x12, waiting for transfers between devices: 50 us -> 10.5 us  [the longest x4 4.51 us: local_heads(): moved.append(lax.ppermute(packed[k], ('seq', 'head'), pairs))]
    ppermute x2 -> x1, waiting for transfers between devices: 0.01 us -> 10.4 us  [local_heads(): near = lax.ppermute(shard, 'seq', [(0, 1), (1, 0), (2, 3), (3, 2)])]
    ppermute x1, waiting for transfers between devices: 1.98 us -> 12.1 us  [local_heads(): cross = lax.ppermute(other, 'wt', swap)]
    ppermute x2 -> x1, waiting for transfers between devices: 8.96 us -> 0.01 us  [local_heads(): two = lax.ppermute(shard, 'seq', [(0, 2), (2, 0), (1, 3), (3, 1)])]
    ppermute x19 -> x12, starting transfers between devices: 30.1 us -> 22.1 us  [the longest x4 9.33 us: local_heads(): moved.append(lax.ppermute(packed[k], ('seq', 'head'), pairs))]
    pallas_call x3 -> x5, Pallas kernels: 7.18 us -> 13 us  [call(): pl.pallas_call(kernel, in_specs=specs, out_specs=[pl.BlockSpec(memory_spa...]
    unnamed x14 -> x39, local copies, waits for them, and re-layouts: 2.85 us -> 8.15 us
    slice x0 -> x2, local copies, waits for them, and re-layouts: none -> 2.54 us  [the longest x1 2.49 us: local_heads(): weight_x0 = lax.ppermute(out_weight[:cut], 'wt', swap)]
  transfers between devices with their start and end apart: 26 -> 17, of which waited for: 13 -> 9; matrix products, arithmetic and copies ran while one was open for 1% -> 3% of each run, Pallas kernels for 2% -> 6%
where the time goes in v2:
time: 106 us; the launch traced here: 105 us
  waiting for transfers between devices  46.3 us (44%)
  starting transfers between devices  31.7 us (30%)
  Pallas kernels  13 us (12%)
  local copies, waits for them, and re-layouts  11.6 us (11%)
  other arithmetic  1.67 us (2%)
    ppermute x2, waiting for transfers between devices, local_heads(): arrived.append(lax.ppermute(block, ('seq', 'wt', 'head'), pairs))  13.2 us
    pallas_call x5, Pallas kernels, call(): pl.pallas_call(kernel, in_specs=specs, out_specs=[pl.BlockSpec(memory_spa...  13 us
    ppermute x1, waiting for transfers between devices, local_heads(): cross = lax.ppermute(other, 'wt', swap)  12.1 us
    ppermute x1, waiting for transfers between devices, local_heads(): near = lax.ppermute(shard, 'seq', [(0, 1), (1, 0), (2, 3), (3, 2)])  10.4 us
    ppermute x4, starting transfers between devices, local_heads(): moved.append(lax.ppermute(packed[k], ('seq', 'head'), pairs))  9.33 us
    unnamed x39, local copies, waits for them, and re-layouts  8.15 us
    ppermute x2, starting transfers between devices, local_heads(): arrived.append(lax.ppermute(block, ('seq', 'wt', 'head'), pairs))  6.21 us
    ppermute x4, waiting for transfers between devices, local_heads(): moved.append(lax.ppermute(packed[k], ('seq', 'head'), pairs))  4.51 us
  transfers between devices with their start and end apart: 17, of which 9 were waited for; matrix products, arithmetic and copies ran while one was open for 3% of the time, Pallas kernels for 6%

profile of v2, /device:TPU:1, one launch (start us, length us, event | category | flops | bytes accessed | tf_op | source)
XLA Modules:
  0.0 105.1 jit_solution(16042119484872412572)
XLA Ops:
  0.7 0.6 stack.94.place
  1.3 2.8 %shard_map.95 = (bf16[240,384]{1,0:T(8,128)(2,1)}, bf16[240,384]{1,0:T(8,128)(2,1)}, bf16[240,384]{1,0:T(8,128)(2,1)}, bf16[240,384]{1,0:T(8,128)(2,1)}) custom-call(s32[8]{0:T(128)} %stack.94.place, bf16[160,768]{1,0:T(8,128)(2,1)} %queries.1, bf16[160,768]{1,0:T(8,128)(2,1)} %keys.1, bf16[160,768]{1,0:T(8,128)(2,1)} %values.1), custom_call_target="tpu_custom_call" | custom-call | tf_op jit(solution)/shard_map/pallas_call | solution.py:200
  4.0 5.6 %collective-permute-start = (bf16[240,384]{1,0:T(8,128)(2,1)}, bf16[240,384]{1,0:T(8,128)(2,1)S(1)}, u32[]{:S(2)}, u32[]{:S(2)}) collective-permute-start(bf16[240,384]{1,0:T(8,128)(2,1)} %get-tuple-element.15), channel_id=1, source_target_pairs={{0,0},{1,8},{4,4},{5,12},{8,1},{9,9},{12,5},{13,13},{2,2},{3,10},{... | collective-permute-start | bytes 552968 | tf_op jit(solution)/shard_map/ppermute | solution.py:257
  9.6 1.1 %collective-permute-start.1 = (bf16[240,384]{1,0:T(8,128)(2,1)}, bf16[240,384]{1,0:T(8,128)(2,1)S(1)}, u32[]{:S(2)}, u32[]{:S(2)}) collective-permute-start(bf16[240,384]{1,0:T(8,128)(2,1)} %get-tuple-element.16), channel_id=1, source_target_pairs={{0,4},{1,12},{4,0},{5,8},{8,5},{9,13},{12,1},{13,9},{2,6},{3,14},{... | collective-permute-start | bytes 552968 | tf_op jit(solution)/shard_map/ppermute | solution.py:257
  10.7 2.6 %collective-permute-start.3 = (bf16[240,384]{1,0:T(8,128)(2,1)}, bf16[240,384]{1,0:T(8,128)(2,1)S(1)}, u32[]{:S(2)}, u32[]{:S(2)}) collective-permute-start(bf16[240,384]{1,0:T(8,128)(2,1)} %get-tuple-element.18), channel_id=1, source_target_pairs={{0,5},{1,13},{4,1},{5,9},{8,4},{9,12},{12,0},{13,8},{2,7},{3,15},{... | collective-permute-start | bytes 552968 | tf_op jit(solution)/shard_map/ppermute | solution.py:257
  13.4 2.5 %slice.6 = bf16[512,1280]{1,0:T(8,128)(2,1)} slice(bf16[768,1280]{1,0:T(8,128)(2,1)} %refs_6_.1), slice={[0:512], [0:1280]} | slice | bytes 2621440 | tf_op jit(solution)/shard_map/slice | solution.py:233
  15.9 1.2 %collective-permute-start.11 = (bf16[512,1280]{1,0:T(8,128)(2,1)}, bf16[512,1280]{1,0:T(8,128)(2,1)S(1)}, u32[]{:S(2)}, u32[]{:S(2)}) collective-permute-start(bf16[512,1280]{1,0:T(8,128)(2,1)} %slice.6), channel_id=1, source_target_pairs={{0,2},{2,0},{1,3},{3,1},{4,6},{6,4},{5,7},{7,5},{8,10},{10,8},{9,1... | collective-permute-start | bytes 3932168 | tf_op jit(solution)/shard_map/ppermute | solution.py:233
  17.1 1.9 %collective-permute-done.1.refs_1_ = bf16[240,384]{1,0:T(8,128)(2,1)S(1)} collective-permute-done((bf16[240,384]{1,0:T(8,128)(2,1)}, bf16[240,384]{1,0:T(8,128)(2,1)S(1)}, u32[]{:S(2)}, u32[]{:S(2)}) %collective-permute-start.1) | collective-permute-done | bytes 184352 | tf_op jit(solution)/shard_map/ppermute | solution.py:257
  19.0 0.6 collective-permute-done.2.refs_2_
  19.6 2.0 %collective-permute-done.3.refs_3_ = bf16[240,384]{1,0:T(8,128)(2,1)S(1)} collective-permute-done((bf16[240,384]{1,0:T(8,128)(2,1)}, bf16[240,384]{1,0:T(8,128)(2,1)S(1)}, u32[]{:S(2)}, u32[]{:S(2)}) %collective-permute-start.3) | collective-permute-done | bytes 184352 | tf_op jit(solution)/shard_map/ppermute | solution.py:257
  21.6 0.8 shard_map.96
  22.4 0.7 copy-done.5
  23.1 4.1 %collective-permute-start.4 = (bf16[640,384]{1,0:T(8,128)(2,1)}, bf16[640,384]{1,0:T(8,128)(2,1)}, u32[]{:S(2)}, u32[]{:S(2)}) collective-permute-start(bf16[640,384]{1,0:T(8,128)(2,1)} %shard_map.96), channel_id=1, source_target_pairs={{0,1},{1,0},{2,3},{3,2},{4,5},{5,4},{6,7},{7,6},{8,9},{9,8},{10,11... | collective-permute-start | bytes 1474568 | tf_op jit(solution)/shard_map/ppermute | solution.py:259
  27.3 0.1 stack.91.place
  27.3 1.7 %collective-permute-done.4.refs_4_ = bf16[640,384]{1,0:T(8,128)(2,1)} collective-permute-done((bf16[640,384]{1,0:T(8,128)(2,1)}, bf16[640,384]{1,0:T(8,128)(2,1)}, u32[]{:S(2)}, u32[]{:S(2)}) %collective-permute-start.4) | collective-permute-done | bytes 491552 | tf_op jit(solution)/shard_map/ppermute | solution.py:259
  29.1 0.9 copy-done.6
  30.0 0.9 copy-done.8
  30.9 0.9 copy-done.10
  31.9 2.8 %shard_map.97 = (bf16[160,384]{1,0:T(8,128)(2,1)S(1)}, bf16[160,384]{1,0:T(8,128)(2,1)S(1)}) custom-call(s32[8]{0:T(128)S(1)} %stack.91.place, bf16[240,384]{1,0:T(8,128)(2,1)S(1)} %collective-permute-done.refs_0_, bf16[240,384]{1,0:T(8,128)(2,1)S(1)} %copy-done.6, bf16[240,384]{1,0:T(8,128)(2,1)S(1)} %copy-done.8, bf16[240,384]{1,0:T(8,128)(2,1)S(1)} %copy-done.10, ...), custom_call_target="tpu_custom_call" | custom-call | flops 314572800 | tf_op jit(solution)/shard_map/pallas_call | solution.py:200
  34.6 1.3 %collective-permute-start.5 = (bf16[160,384]{1,0:T(8,128)(2,1)S(1)}, bf16[160,384]{1,0:T(8,128)(2,1)S(1)}, u32[]{:S(2)}, u32[]{:S(2)}) collective-permute-start(bf16[160,384]{1,0:T(8,128)(2,1)S(1)} %get-tuple-element.20), channel_id=1, source_target_pairs={{0,2},{2,0},{1,3},{3,1},{4,6},{6,4},{5,7},{7,5},{8,10},{10,8},{9,1... | collective-permute-start | bytes 368648 | tf_op jit(solution)/shard_map/ppermute | solution.py:278
  35.9 12.1 %collective-permute-done.5 = bf16[160,384]{1,0:T(8,128)(2,1)S(1)} collective-permute-done((bf16[160,384]{1,0:T(8,128)(2,1)S(1)}, bf16[160,384]{1,0:T(8,128)(2,1)S(1)}, u32[]{:S(2)}, u32[]{:S(2)}) %collective-permute-start.5) | collective-permute-done | bytes 122912 | tf_op jit(solution)/shard_map/ppermute | solution.py:278
  48.1 1.3 %collective-permute-start.12 = (bf16[256,1280]{1,0:T(8,128)(2,1)S(1)}, bf16[256,1280]{1,0:T(8,128)(2,1)}, u32[]{:S(2)}, u32[]{:S(2)}) collective-permute-start(bf16[256,1280]{1,0:T(8,128)(2,1)S(1)} %slice.7), channel_id=1, source_target_pairs={{0,2},{2,0},{1,3},{3,1},{4,6},{6,4},{5,7},{7,5},{8,10},{10,8},{9,1... | collective-permute-start | bytes 1966088 | tf_op jit(solution)/shard_map/ppermute | solution.py:234
  49.3 0.8 collective-permute-start.13
  50.2 0.9 collective-permute-start.6
  51.1 1.2 %collective-permute-start.7 = (bf16[160,768]{1,0:T(8,128)(2,1)S(1)}, bf16[160,768]{1,0:T(8,128)(2,1)S(1)}, u32[]{:S(2)}, u32[]{:S(2)}) collective-permute-start(bf16[160,768]{1,0:T(8,128)(2,1)S(1)} %constant_dynamic-update-slice_fusion.own.refs_1_), channel_id=1, source_target_pairs={{0,8},{8,0},{4,12},{12,4},{1,9},{9,1},{5,13},{13,5},{2,10},{10,2},... | collective-permute-start | bytes 737288 | tf_op jit(solution)/shard_map/ppermute | solution.py:282
  52.3 10.4 %collective-permute-done.6.near.refs_2_ = bf16[160,768]{1,0:T(8,128)(2,1)S(1)} collective-permute-done((bf16[160,768]{1,0:T(8,128)(2,1)S(1)}, bf16[160,768]{1,0:T(8,128)(2,1)S(1)}, u32[]{:S(2)}, u32[]{:S(2)}) %collective-permute-start.6) | collective-permute-done | bytes 245792 | tf_op jit(solution)/shard_map/ppermute | solution.py:281
  62.8 0.7 copy-done.1
  63.5 1.3 %collective-permute-start.10 = (bf16[160,768]{1,0:T(8,128)(2,1)S(1)}, bf16[160,768]{1,0:T(8,128)(2,1)S(1)}, u32[]{:S(2)}, u32[]{:S(2)}) collective-permute-start(bf16[160,768]{1,0:T(8,128)(2,1)S(1)} %collective-permute-done.7.two.refs_3_), channel_id=1, source_target_pairs={{4,0},{8,12},{5,1},{9,13},{6,2},{10,14},{7,3},{11,15},{20,16},{24,... | collective-permute-start | bytes 737288 | tf_op jit(solution)/shard_map/ppermute | solution.py:287
  64.7 0.0 copy-start.3
  64.8 0.7 copy-done.3
  65.4 0.7 collective-permute-start.9
  66.1 4.3 %collective-permute-done.10.refs_5_ = bf16[160,768]{1,0:T(8,128)(2,1)S(1)} collective-permute-done((bf16[160,768]{1,0:T(8,128)(2,1)S(1)}, bf16[160,768]{1,0:T(8,128)(2,1)S(1)}, u32[]{:S(2)}, u32[]{:S(2)}) %collective-permute-start.10) | collective-permute-done | bytes 245792 | tf_op jit(solution)/shard_map/ppermute | solution.py:287
  70.4 0.7 copy-done.11
  71.1 0.7 copy-done.13
  71.8 3.4 %collective-permute-start.14 = (bf16[256,1280]{1,0:T(8,128)(2,1)}, bf16[256,1280]{1,0:T(8,128)(2,1)}, u32[]{:S(2)}, u32[]{:S(2)}) collective-permute-start(bf16[256,1280]{1,0:T(8,128)(2,1)} %collective-permute-done.12.refs_9_), channel_id=1, source_target_pairs={{0,1},{1,0},{2,3},{3,2},{4,5},{5,4},{6,7},{7,6},{8,9},{9,8},{10,11... | collective-permute-start | bytes 1966088 | tf_op jit(solution)/shard_map/ppermute | solution.py:302
  75.2 0.1 stack.87.place
  75.3 0.1 stack.84.place
  75.4 0.9 copy-done.2
  76.3 0.9 copy-done.4
  77.3 2.8 %shard_map.98.refs_0_ = f32[160,1280]{1,0:T(8,128)S(1)} custom-call(s32[6]{0:T(128)S(1)} %stack.87.place, bf16[160,768]{1,0:T(8,128)(2,1)S(1)} %constant_dynamic-update-slice_fusion.own.refs_1_, bf16[160,768]{1,0:T(8,128)(2,1)S(1)} %copy-done.2, bf16[160,768]{1,0:T(8,128)(2,1)S(1)} %copy-done.4, bf16[768,1280]{1,0:T(8,128)(2,1)S(1)} %copy-done, ...), custom_call_target="tpu_custom_call" | custom-call | flops 471859200 | tf_op jit(solution)/shard_map/pallas_call | solution.py:200
  80.1 0.0 copy-start.15
  80.2 3.8 %shard_map.99 = (bf16[80,1280]{1,0:T(8,128)(2,1)S(1)}, bf16[80,1280]{1,0:T(8,128)(2,1)S(1)}) custom-call(s32[8]{0:T(128)S(1)} %stack.84.place, f32[160,1280]{1,0:T(8,128)S(1)} %shard_map.98.refs_0_, bf16[160,768]{1,0:T(8,128)(2,1)S(1)} %constant_dynamic-update-slice_fusion.own.refs_1_, bf16[160,768]{1,0:T(8,128)(2,1)S(1)} %copy-done.2, ...), custom_call_target="tpu_custom_call" | custom-call | flops 786432000 | tf_op jit(solution)/shard_map/pallas_call | solution.py:200
  83.9 6.1 %collective-permute-start.15 = (bf16[80,1280]{1,0:T(8,128)(2,1)S(1)}, bf16[80,1280]{1,0:T(8,128)(2,1)S(1)}, u32[]{:S(2)}, u32[]{:S(2)}) collective-permute-start(bf16[80,1280]{1,0:T(8,128)(2,1)S(1)} %get-tuple-element.26), channel_id=1, source_target_pairs={{0,0},{1,8},{2,4},{3,12},{4,1},{5,9},{6,5},{7,13},{8,2},{9,10},{10... | collective-permute-start | bytes 614408 | tf_op jit(solution)/shard_map/ppermute | solution.py:327
  90.1 0.1 collective-permute-start.16
  90.2 0.3 multiply_reduce_fusion
  90.5 13.1 %collective-permute-done.15 = bf16[80,1280]{1,0:T(8,128)(2,1)S(1)} collective-permute-done((bf16[80,1280]{1,0:T(8,128)(2,1)S(1)}, bf16[80,1280]{1,0:T(8,128)(2,1)S(1)}, u32[]{:S(2)}, u32[]{:S(2)}) %collective-permute-start.15) | collective-permute-done | bytes 204832 | tf_op jit(solution)/shard_map/ppermute | solution.py:327
  103.7 0.1 collective-permute-done.16
  103.8 1.3 %add_add_fusion = (f32[160,1280]{1,0:T(8,128)}, f32[160,1280]{1,0:T(8,128)}) fusion(f32[160,1280]{1,0:T(8,128)S(1)} %copy-done.16, f32[160,1280]{1,0:T(8,128)S(1)} %multiply_reduce_fusion, f32[1280]{0:T(1024)S(1)} %copy-done.17, bf16[80,1280]{1,0:T(8,128)(2,1)S(1)} %get-tuple-element.31, bf16[80,1280]{1,0:T(8,128)(2,1)S(1)} %get-tuple-element.30), kind=kLoop, calls=%fused_computation.2 | loop fusion | flops 1433600 | bytes 3691520 | tf_op jit(solution)/shard_map/add | solution.py:339
  (41 shorter events, 0.2 us)
Async XLA Ops:
  4.0 13.1 %collective-permute-start = (bf16[240,384]{1,0:T(8,128)(2,1)}, bf16[240,384]{1,0:T(8,128)(2,1)S(1)}, u32[]{:S(2)}, u32[]{:S(2)}) collective-permute-start(bf16[240,384]{1,0:T(8,128)(2,1)} %get-tuple-element.15), channel_id=1, source_target_pairs={{0,0},{1,8},{4,4},{5,12},{8,1},{9,9},{12,5},{13,13},{2,2},{3,10},{... | collective-permute-start | bytes 552968 | tf_op jit(solution)/shard_map/ppermute | solution.py:257
  9.6 9.4 %collective-permute-start.1 = (bf16[240,384]{1,0:T(8,128)(2,1)}, bf16[240,384]{1,0:T(8,128)(2,1)S(1)}, u32[]{:S(2)}, u32[]{:S(2)}) collective-permute-start(bf16[240,384]{1,0:T(8,128)(2,1)} %get-tuple-element.16), channel_id=1, source_target_pairs={{0,4},{1,12},{4,0},{5,8},{8,5},{9,13},{12,1},{13,9},{2,6},{3,14},{... | collective-permute-start | bytes 552968 | tf_op jit(solution)/shard_map/ppermute | solution.py:257
  10.7 8.9 %collective-permute-start.2 = (bf16[240,384]{1,0:T(8,128)(2,1)}, bf16[240,384]{1,0:T(8,128)(2,1)S(1)}, u32[]{:S(2)}, u32[]{:S(2)}) collective-permute-start(bf16[240,384]{1,0:T(8,128)(2,1)} %get-tuple-element.17), channel_id=1, source_target_pairs={{0,1},{1,9},{4,5},{5,13},{8,0},{9,8},{12,4},{13,12},{2,3},{3,11},{... | collective-permute-start | bytes 552968 | tf_op jit(solution)/shard_map/ppermute | solution.py:257
  10.7 37.3 %copy-start = (bf16[768,1280]{1,0:T(8,128)(2,1)S(1)}, bf16[768,1280]{1,0:T(8,128)(2,1)}, u32[]{:S(2)}) copy-start(bf16[768,1280]{1,0:T(8,128)(2,1)} %refs_6_.1) | copy-start | bytes 5898244
  10.7 10.9 %collective-permute-start.3 = (bf16[240,384]{1,0:T(8,128)(2,1)}, bf16[240,384]{1,0:T(8,128)(2,1)S(1)}, u32[]{:S(2)}, u32[]{:S(2)}) collective-permute-start(bf16[240,384]{1,0:T(8,128)(2,1)} %get-tuple-element.18), channel_id=1, source_target_pairs={{0,5},{1,13},{4,1},{5,9},{8,4},{9,12},{12,0},{13,8},{2,7},{3,15},{... | collective-permute-start | bytes 552968 | tf_op jit(solution)/shard_map/ppermute | solution.py:257
  15.9 59.3 %copy-start.18 = (s32[4]{0:T(128)S(1)}, s32[4]{0:T(128)}, u32[]{:S(2)}) copy-start(s32[4]{0:T(128)} %param.15) | copy-start | bytes 52
  15.9 33.5 %collective-permute-start.11 = (bf16[512,1280]{1,0:T(8,128)(2,1)}, bf16[512,1280]{1,0:T(8,128)(2,1)S(1)}, u32[]{:S(2)}, u32[]{:S(2)}) collective-permute-start(bf16[512,1280]{1,0:T(8,128)(2,1)} %slice.6), channel_id=1, source_target_pairs={{0,2},{2,0},{1,3},{3,1},{4,6},{6,4},{5,7},{7,5},{8,10},{10,8},{9,1... | collective-permute-start | bytes 3932168 | tf_op jit(solution)/shard_map/ppermute | solution.py:233
  19.6 2.8 %copy-start.7 = (bf16[240,384]{1,0:T(8,128)(2,1)}, bf16[240,384]{1,0:T(8,128)(2,1)S(1)}, u32[]{:S(2)}) copy-start(bf16[240,384]{1,0:T(8,128)(2,1)S(1)} %collective-permute-done.2.refs_2_) | copy-start | bytes 552964
  21.6 0.8 copy-start.9
  22.4 0.7 copy-start.5
  23.1 6.0 %collective-permute-start.4 = (bf16[640,384]{1,0:T(8,128)(2,1)}, bf16[640,384]{1,0:T(8,128)(2,1)}, u32[]{:S(2)}, u32[]{:S(2)}) collective-permute-start(bf16[640,384]{1,0:T(8,128)(2,1)} %shard_map.96), channel_id=1, source_target_pairs={{0,1},{1,0},{2,3},{3,2},{4,5},{5,4},{6,7},{7,6},{8,9},{9,8},{10,11... | collective-permute-start | bytes 1474568 | tf_op jit(solution)/shard_map/ppermute | solution.py:259
  29.1 0.9 copy-start.6
  30.0 0.9 copy-start.8
  30.9 0.9 copy-start.10
  34.6 13.4 %collective-permute-start.5 = (bf16[160,384]{1,0:T(8,128)(2,1)S(1)}, bf16[160,384]{1,0:T(8,128)(2,1)S(1)}, u32[]{:S(2)}, u32[]{:S(2)}) collective-permute-start(bf16[160,384]{1,0:T(8,128)(2,1)S(1)} %get-tuple-element.20), channel_id=1, source_target_pairs={{0,2},{2,0},{1,3},{3,1},{4,6},{6,4},{5,7},{7,5},{8,10},{10,8},{9,1... | collective-permute-start | bytes 368648 | tf_op jit(solution)/shard_map/ppermute | solution.py:278
  48.0 27.3 %collective-permute-start.8 = (bf16[768,1280]{1,0:T(8,128)(2,1)S(1)}, bf16[768,1280]{1,0:T(8,128)(2,1)}, u32[]{:S(2)}, u32[]{:S(2)}) collective-permute-start(bf16[768,1280]{1,0:T(8,128)(2,1)S(1)} %copy-done), channel_id=1, source_target_pairs={{0,1},{1,0},{2,3},{3,2},{4,5},{5,4},{6,7},{7,6},{8,9},{9,8},{10,11... | collective-permute-start | bytes 5898248 | tf_op jit(solution)/shard_map/ppermute | solution.py:284
  48.1 18.0 %collective-permute-start.12 = (bf16[256,1280]{1,0:T(8,128)(2,1)S(1)}, bf16[256,1280]{1,0:T(8,128)(2,1)}, u32[]{:S(2)}, u32[]{:S(2)}) collective-permute-start(bf16[256,1280]{1,0:T(8,128)(2,1)S(1)} %slice.7), channel_id=1, source_target_pairs={{0,2},{2,0},{1,3},{3,1},{4,6},{6,4},{5,7},{7,5},{8,10},{10,8},{9,1... | collective-permute-start | bytes 1966088 | tf_op jit(solution)/shard_map/ppermute | solution.py:234
  49.3 30.8 %collective-permute-start.13 = (bf16[512,1280]{1,0:T(8,128)(2,1)S(1)}, bf16[512,1280]{1,0:T(8,128)(2,1)}, u32[]{:S(2)}, u32[]{:S(2)}) collective-permute-start(bf16[512,1280]{1,0:T(8,128)(2,1)S(1)} %collective-permute-done.11.refs_8_), channel_id=1, source_target_pairs={{0,1},{1,0},{2,3},{3,2},{4,5},{5,4},{6,7},{7,6},{8,9},{9,8},{10,11... | collective-permute-start | bytes 3932168 | tf_op jit(solution)/shard_map/ppermute | solution.py:301
  50.2 12.6 %collective-permute-start.6 = (bf16[160,768]{1,0:T(8,128)(2,1)S(1)}, bf16[160,768]{1,0:T(8,128)(2,1)S(1)}, u32[]{:S(2)}, u32[]{:S(2)}) collective-permute-start(bf16[160,768]{1,0:T(8,128)(2,1)S(1)} %constant_dynamic-update-slice_fusion.own.refs_1_), channel_id=1, source_target_pairs={{0,4},{4,0},{8,12},{12,8},{1,5},{5,1},{9,13},{13,9},{2,6},{6,2},{1... | collective-permute-start | bytes 737288 | tf_op jit(solution)/shard_map/ppermute | solution.py:281
  51.1 12.3 %collective-permute-start.7 = (bf16[160,768]{1,0:T(8,128)(2,1)S(1)}, bf16[160,768]{1,0:T(8,128)(2,1)S(1)}, u32[]{:S(2)}, u32[]{:S(2)}) collective-permute-start(bf16[160,768]{1,0:T(8,128)(2,1)S(1)} %constant_dynamic-update-slice_fusion.own.refs_1_), channel_id=1, source_target_pairs={{0,8},{8,0},{4,12},{12,4},{1,9},{9,1},{5,13},{13,5},{2,10},{10,2},... | collective-permute-start | bytes 737288 | tf_op jit(solution)/shard_map/ppermute | solution.py:282
  62.8 0.7 copy-start.1
  63.5 6.9 %collective-permute-start.10 = (bf16[160,768]{1,0:T(8,128)(2,1)S(1)}, bf16[160,768]{1,0:T(8,128)(2,1)S(1)}, u32[]{:S(2)}, u32[]{:S(2)}) collective-permute-start(bf16[160,768]{1,0:T(8,128)(2,1)S(1)} %collective-permute-done.7.two.refs_3_), channel_id=1, source_target_pairs={{4,0},{8,12},{5,1},{9,13},{6,2},{10,14},{7,3},{11,15},{20,16},{24,... | collective-permute-start | bytes 737288 | tf_op jit(solution)/shard_map/ppermute | solution.py:287
  64.7 0.7 copy-start.3
  65.4 5.7 %collective-permute-start.9 = (bf16[160,768]{1,0:T(8,128)(2,1)S(1)}, bf16[160,768]{1,0:T(8,128)(2,1)S(1)}, u32[]{:S(2)}, u32[]{:S(2)}) collective-permute-start(bf16[160,768]{1,0:T(8,128)(2,1)S(1)} %constant_dynamic-update-slice_fusion.own.refs_1_), channel_id=1, source_target_pairs={{4,8},{8,4},{5,9},{9,5},{6,10},{10,6},{7,11},{11,7},{20,24},{24,20... | collective-permute-start | bytes 737288 | tf_op jit(solution)/shard_map/ppermute | solution.py:286
  70.4 0.7 copy-start.11
  71.1 0.7 copy-start.13
  71.8 8.3 %collective-permute-start.14 = (bf16[256,1280]{1,0:T(8,128)(2,1)}, bf16[256,1280]{1,0:T(8,128)(2,1)}, u32[]{:S(2)}, u32[]{:S(2)}) collective-permute-start(bf16[256,1280]{1,0:T(8,128)(2,1)} %collective-permute-done.12.refs_9_), channel_id=1, source_target_pairs={{0,1},{1,0},{2,3},{3,2},{4,5},{5,4},{6,7},{7,6},{8,9},{9,8},{10,11... | collective-permute-start | bytes 1966088 | tf_op jit(solution)/shard_map/ppermute | solution.py:302
  75.4 0.9 copy-start.2
  76.3 0.9 copy-start.4
  77.3 2.9 %copy-start.12 = (bf16[160,768]{1,0:T(8,128)(2,1)S(1)}, bf16[160,768]{1,0:T(8,128)(2,1)}, u32[]{:S(2)}) copy-start(bf16[160,768]{1,0:T(8,128)(2,1)} %copy-done.11) | copy-start | bytes 737284
  77.3 2.9 %copy-start.14 = (bf16[160,768]{1,0:T(8,128)(2,1)S(1)}, bf16[160,768]{1,0:T(8,128)(2,1)}, u32[]{:S(2)}) copy-start(bf16[160,768]{1,0:T(8,128)(2,1)} %copy-done.13) | copy-start | bytes 737284
  80.1 10.1 %copy-start.15 = (f32[4,160,1280]{2,1,0:T(8,128)S(1)}, f32[4,160,1280]{2,1,0:T(8,128)}, u32[]{:S(2)}) copy-start(f32[4,160,1280]{2,1,0:T(8,128)} %param.14) | copy-start | bytes 9830404
  83.9 19.7 %collective-permute-start.15 = (bf16[80,1280]{1,0:T(8,128)(2,1)S(1)}, bf16[80,1280]{1,0:T(8,128)(2,1)S(1)}, u32[]{:S(2)}, u32[]{:S(2)}) collective-permute-start(bf16[80,1280]{1,0:T(8,128)(2,1)S(1)} %get-tuple-element.26), channel_id=1, source_target_pairs={{0,0},{1,8},{2,4},{3,12},{4,1},{5,9},{6,5},{7,13},{8,2},{9,10},{10... | collective-permute-start | bytes 614408 | tf_op jit(solution)/shard_map/ppermute | solution.py:327
  90.1 13.7 %copy-start.16 = (f32[160,1280]{1,0:T(8,128)S(1)}, f32[160,1280]{1,0:T(8,128)}, u32[]{:S(2)}) copy-start(f32[160,1280]{1,0:T(8,128)} %param.13) | copy-start | bytes 2457604
  90.1 13.7 %copy-start.17 = (f32[1280]{0:T(1024)S(1)}, f32[1280]{0:T(1024)}, u32[]{:S(2)}) copy-start(f32[1280]{0:T(1024)} %param.12) | copy-start | bytes 15364
  90.1 13.6 %collective-permute-start.16 = (bf16[80,1280]{1,0:T(8,128)(2,1)S(1)}, bf16[80,1280]{1,0:T(8,128)(2,1)S(1)}, u32[]{:S(2)}, u32[]{:S(2)}) collective-permute-start(bf16[80,1280]{1,0:T(8,128)(2,1)S(1)} %get-tuple-element.27), channel_id=1, source_target_pairs={{0,8},{1,0},{2,12},{3,4},{4,9},{5,1},{6,13},{7,5},{8,10},{9,2},{10... | collective-permute-start | bytes 614408 | tf_op jit(solution)/shard_map/ppermute | solution.py:327

commit v3 on v0

--- a/solution.py
+++ b/solution.py
@@ -1,9 +1,14 @@
+import functools
+
 import jax
 import jax.numpy as jnp
 from jax import lax
+from jax.experimental import pallas as pl
+from jax.experimental.pallas import tpu as pltpu
 from jax.sharding import PartitionSpec as P
 
 HEAD_DIM = 128
+VMEM_BYTES = 48 * 1024 * 1024
 
 
 def attend(state_in, key_rows, value_rows, query_heads, score_scale):
@@ -46,7 +51,7 @@
     return normed.transpose(1, 0, 2).reshape(row_count, -1).astype(jnp.bfloat16)
 
 
-def local(
+def local_general(
     queries,
     key_vectors,
     value_vectors,
@@ -82,6 +87,254 @@
     return (mixed_state, fresh_delta)
 
 
+def bits():
+    z = lax.axis_index("seq")
+    return lax.div(z, 2), lax.rem(z, 2)
+
+
+def flip(bit, value):
+    return 1 - bit if value else bit
+
+
+def run(copies):
+    for copy in copies:
+        copy.start()
+    for copy in copies:
+        copy.wait()
+
+
+def pack_kernel(queries, keys, values, *refs):
+    outs, sems = refs[:4], refs[4]
+    half, width = outs[0].shape[0] // 3, outs[0].shape[1]
+    zh, zl = bits()
+    copies = []
+    for k in range(4):
+        rows = pl.ds(pl.multiple_of(flip(zh, k // 2) * half, 16), half)
+        columns = pl.ds(pl.multiple_of(flip(zl, k % 2) * width, 128), width)
+        for i, source in enumerate((keys, values, queries)):
+            copies.append(
+                pltpu.make_async_copy(
+                    source.at[rows, columns],
+                    outs[k].at[pl.ds(i * half, half), :],
+                    sems.at[3 * k + i],
+                )
+            )
+    run(copies)
+
+
+def join_kernel(*refs):
+    blocks, joined, sems = refs[:4], refs[4], refs[5]
+    rows = joined.shape[0] // 4
+    run(
+        [
+            pltpu.make_async_copy(
+                block.at[pl.ds(0, rows), :], joined.at[pl.ds(k * rows, rows), :], sems.at[k]
+            )
+            for k, block in enumerate(blocks)
+        ]
+    )
+
+
+def attention_kernel(*refs):
+    blocks, sibling, out = refs[:4], refs[4], refs[5]
+    key_all, value_all, query_all, sems = refs[6:]
+    half = blocks[0].shape[0] // 3
+    _, zl = bits()
+    core = lax.axis_index("head")
+
+    def rows(k):
+        return pl.ds(k * half, half)
+
+    copies = []
+    for k in range(4):
+        source = 2 * flip(core, k // 2) + flip(zl, k % 2)
+        at = pl.ds(pl.multiple_of(source * half, 16), half)
+        parts = (
+            (blocks[k].at[rows(0), :], key_all.at[rows(k), :]),
+            (blocks[k].at[rows(1), :], value_all.at[rows(k), :]),
+            (blocks[k].at[rows(2), :], query_all.at[at, :]),
+            (sibling.at[rows(2 * k), :], key_all.at[rows(4 + k), :]),
+            (sibling.at[rows(2 * k + 1), :], value_all.at[rows(4 + k), :]),
+        )
+        for i, (start, end) in enumerate(parts):
+            copies.append(pltpu.make_async_copy(start, end, sems.at[5 * k + i]))
+    run(copies)
+    for h in range(out.shape[1] // HEAD_DIM):
+        columns = slice(h * HEAD_DIM, (h + 1) * HEAD_DIM)
+        scores = lax.dot_general(
+            query_all[:, columns],
+            key_all[:, columns],
+            (((1,), (1,)), ((), ())),
+            preferred_element_type=jnp.float32,
+        ) * (HEAD_DIM ** (-0.5))
+        weights = jnp.exp(scores - jnp.max(scores, axis=1, keepdims=True))
+        total = jnp.sum(weights, axis=1, keepdims=True)
+        result = jnp.dot(
+            weights.astype(jnp.bfloat16), value_all[:, columns], preferred_element_type=jnp.float32
+        )
+        out[:, columns] = (result / total).astype(out.dtype)
+
+
+def project_kernel(gathered, weight, weight_c, *refs):
+    keeps, sends = refs[0:2], refs[2:4]
+    left, rights, total, sems = refs[4:]
+    rows, depth = left.shape[1], weight.shape[0]
+    core, x = lax.axis_index("head"), lax.axis_index("wt")
+    copies = [
+        pltpu.make_async_copy(weight, rights.at[core], sems.at[0]),
+        pltpu.make_async_copy(weight_c, rights.at[1 - core], sems.at[1]),
+    ]
+    for m in range(4):
+        copies.append(
+            pltpu.make_async_copy(gathered.at[pl.ds(m * rows, rows), :], left.at[m], sems.at[2 + m])
+        )
+    run(copies)
+    block = rows // 4
+    count = sends[0].shape[1]
+    for h in range(2):
+        columns = slice(h * count, (h + 1) * count)
+        for m in range(4):
+            term = jnp.dot(
+                left[m],
+                rights[m // 2, (m % 2) * depth // 2 : (m % 2 + 1) * depth // 2, columns],
+                preferred_element_type=jnp.float32,
+            )
+            if m == 0:
+                total[...] = term
+            else:
+                total[...] += term
+        for high in range(2):
+            kept = pl.ds(pl.multiple_of((2 * high + x) * block, 16), block)
+            sent = pl.ds(pl.multiple_of((2 * high + 1 - x) * block, 16), block)
+            at = slice(high * block, (high + 1) * block)
+            keeps[h][at, :] = total[kept, :]
+            sends[h][at, :] = total[sent, :].astype(sends[h].dtype)
+
+
+def add_kernel(keep, arrived, out0, out1):
+    half = out0.shape[0]
+    core = lax.axis_index("head")
+    first = pl.ds(pl.multiple_of(core * half, 16), half)
+    second = pl.ds(pl.multiple_of((1 - core) * half, 16), half)
+    for out, at in ((out0, first), (out1, second)):
+        out[...] = (keep[at, :] + arrived[at, :].astype(jnp.float32)).astype(out.dtype)
+
+
+def call(kernel, args, outs, scratch=(), far_in=True, far_out=False, flops=0, vmem=VMEM_BYTES):
+    place = {True: pl.ANY, False: pltpu.VMEM}
+    return pl.pallas_call(
+        kernel,
+        in_specs=[pl.BlockSpec(memory_space=place[far_in])] * len(args),
+        out_specs=[pl.BlockSpec(memory_space=place[far_out])] * len(outs),
+        out_shape=[jax.ShapeDtypeStruct(shape, dtype) for shape, dtype in outs],
+        scratch_shapes=list(scratch),
+        compiler_params=pltpu.CompilerParams(vmem_limit_bytes=vmem),
+        cost_estimate=pl.CostEstimate(flops=flops, bytes_accessed=0, transcendentals=0),
+    )(*args)
+
+
+def local_heads(
+    queries,
+    key_vectors,
+    value_vectors,
+    out_weight,
+    gate_values,
+    hidden_state,
+    cached_deltas,
+    skip_flags,
+):
+    rows, features = queries.shape
+    half, width = rows // 2, features // 2
+    depth, columns = out_weight.shape
+    count = columns // 2
+    zh = lax.axis_index("seq") // 2
+    swap = [(0, 1), (1, 0)]
+    bf16 = jnp.bfloat16
+
+    weight_c = lax.ppermute(out_weight, "head", swap)
+
+    packed = call(
+        pack_kernel,
+        (queries, key_vectors, value_vectors),
+        [((3 * half, width), bf16)] * 4,
+        [pltpu.SemaphoreType.DMA((12,))],
+        far_out=True,
+        vmem=60 * 1024 * 1024,
+    )
+    moved = []
+    for k in range(4):
+        k1, k0 = k // 2, k % 2
+        pairs = []
+        for zz in range(4):
+            for cc in range(2):
+                to_z = 2 * cc + ((zz % 2) ^ k0)
+                pairs.append((zz * 2 + cc, to_z * 2 + ((zz // 2) ^ k1)))
+        moved.append(lax.ppermute(packed[k], ("seq", "head"), pairs))
+    (joined,) = call(
+        join_kernel,
+        moved,
+        [((4 * rows, width), bf16)],
+        [pltpu.SemaphoreType.DMA((4,))],
+        far_out=True,
+    )
+    sibling = lax.ppermute(joined, "head", swap)
+    (attention_out,) = call(
+        attention_kernel,
+        moved + [sibling],
+        [((2 * rows, width), bf16)],
+        [
+            pltpu.VMEM((4 * rows, width), bf16),
+            pltpu.VMEM((4 * rows, width), bf16),
+            pltpu.VMEM((2 * rows, width), bf16),
+            pltpu.SemaphoreType.DMA((20,)),
+        ],
+        flops=4 * (2 * rows) * (4 * rows) * width,
+    )
+    gathered = lax.all_gather(attention_out, "seq", axis=0, tiled=True)
+
+    outs = call(
+        project_kernel,
+        (gathered, out_weight, weight_c),
+        [((rows, count), jnp.float32)] * 2 + [((rows, count), bf16)] * 2,
+        [
+            pltpu.VMEM((4, 2 * rows, width), bf16),
+            pltpu.VMEM((2, depth, columns), bf16),
+            pltpu.VMEM((2 * rows, count), jnp.float32),
+            pltpu.SemaphoreType.DMA((6,)),
+        ],
+        flops=4 * (2 * rows) * depth * columns,
+    )
+    summed = []
+    for keep, send in zip(outs[:2], outs[2:]):
+        arrived = lax.ppermute(send, "wt", swap)
+        pieces = call(add_kernel, (keep, arrived), [((half, count), bf16)] * 2, far_in=False)
+        owned = []
+        for p, piece in enumerate(pieces):
+            pairs = []
+            for zz in range(4):
+                for xx in range(2):
+                    for cc in range(2):
+                        to = ((2 * (p ^ cc) + xx) * 2 + zz // 2) * 2 + zz % 2
+                        pairs.append(((zz * 2 + xx) * 2 + cc, to))
+            owned.append(lax.ppermute(piece, ("seq", "wt", "head"), pairs))
+        straight = zh == 0
+        summed.append(
+            jnp.concatenate(
+                [
+                    jnp.where(straight, owned[0], owned[1]),
+                    jnp.where(straight, owned[1], owned[0]),
+                ],
+                axis=0,
+            )
+        )
+    head_total = jnp.concatenate(summed, axis=1).astype(jnp.float32)
+    kept_deltas = jnp.sum(skip_flags.astype(jnp.float32)[:, None, None] * cached_deltas, axis=0)
+    resting = hidden_state + kept_deltas
+    fresh_delta = head_total * gate_values[None, :]
+    mixed_state = resting + fresh_delta
+    return (mixed_state, fresh_delta)
+
+
 def solution(mesh):
     placed = (
         P(("groups", "seq"), ("wt", "head")),
@@ -93,6 +346,14 @@
         P(None, ("groups", "seq"), ("wt", "head")),
         P("groups"),
     )
+
+    def local(*args):
+        sizes = tuple(mesh.shape[name] for name in ("seq", "wt", "head"))
+        rows, features = args[0].shape
+        if sizes == (4, 2, 2) and rows % 32 == 0 and features % (2 * HEAD_DIM) == 0 and args[3].shape[1] % 256 == 0:
+            return local_heads(*args)
+        return local_general(*args)
+
     return jax.shard_map(
         local,
         mesh=mesh,

time: 217 us -> 106 us (0.49)
  the two profiles are of different devices: /device:TPU:2 before, /device:TPU:1 now
where the time goes in v3:
time: 106 us
  Pallas kernels  32.6 us (31%)
  starting transfers between devices  27 us (25%)
  waiting for transfers between devices  21.9 us (21%)
  blocking collectives  21.2 us (20%)
  other arithmetic  1.65 us (2%)
    pallas_call x6, Pallas kernels, call(): pl.pallas_call(kernel, in_specs=[pl.BlockSpec(memory_space=place[far_in])...  32.6 us
    all_gather x1, blocking collectives, local_heads(): gathered = lax.all_gather(attention_out, 'seq', axis=0, tiled=True)  21.2 us
    ppermute x4, starting transfers between devices, local_heads(): owned.append(lax.ppermute(piece, ('seq', 'wt', 'head'), pairs))  11.9 us
    ppermute x4, starting transfers between devices, local_heads(): moved.append(lax.ppermute(packed[k], ('seq', 'head'), pairs))  9.31 us
    ppermute x4, waiting for transfers between devices, local_heads(): owned.append(lax.ppermute(piece, ('seq', 'wt', 'head'), pairs))  8.59 us
    ppermute x4, waiting for transfers between devices, local_heads(): moved.append(lax.ppermute(packed[k], ('seq', 'head'), pairs))  8.22 us
    ppermute x1, starting transfers between devices, local_heads(): sibling = lax.ppermute(joined, 'head', swap)  4.23 us
    ppermute x2, waiting for transfers between devices, local_heads(): arrived = lax.ppermute(send, 'wt', swap)  3.61 us
  transfers between devices with their start and end apart: 12, of which 8 were waited for; matrix products, arithmetic and copies ran while one was open for 0% of the time, Pallas kernels for 26%

profile of v3, /device:TPU:1, one launch (start us, length us, event | category | flops | bytes accessed | tf_op | source)
XLA Modules:
  0.0 105.9 jit_solution(15589927045442236725)
XLA Ops:
  0.6 0.0 copy-start
  0.6 0.1 collective-permute-start.5
  0.8 23.5 %shard_map.95 = (bf16[240,384]{1,0:T(8,128)(2,1)}, bf16[240,384]{1,0:T(8,128)(2,1)}, bf16[240,384]{1,0:T(8,128)(2,1)}, bf16[240,384]{1,0:T(8,128)(2,1)}) custom-call(bf16[160,768]{1,0:T(8,128)(2,1)} %queries.1, bf16[160,768]{1,0:T(8,128)(2,1)} %keys.1, bf16[160,768]{1,0:T(8,128)(2,1)} %values.1), custom_call_target="tpu_custom_call" | custom-call | tf_op jit(solution)/shard_map/pallas_call | solution.py:225
  24.3 5.6 %collective-permute-start = (bf16[240,384]{1,0:T(8,128)(2,1)}, bf16[240,384]{1,0:T(8,128)(2,1)S(1)}, u32[]{:S(2)}, u32[]{:S(2)}) collective-permute-start(bf16[240,384]{1,0:T(8,128)(2,1)} %get-tuple-element.14), channel_id=1, source_target_pairs={{0,0},{1,8},{4,4},{5,12},{8,1},{9,9},{12,5},{13,13},{2,2},{3,10},{... | collective-permute-start | bytes 552968 | tf_op jit(solution)/shard_map/ppermute | solution.py:272
  29.9 1.5 %collective-permute-start.1 = (bf16[240,384]{1,0:T(8,128)(2,1)}, bf16[240,384]{1,0:T(8,128)(2,1)S(1)}, u32[]{:S(2)}, u32[]{:S(2)}) collective-permute-start(bf16[240,384]{1,0:T(8,128)(2,1)} %get-tuple-element.15), channel_id=1, source_target_pairs={{0,4},{1,12},{4,0},{5,8},{8,5},{9,13},{12,1},{13,9},{2,6},{3,14},{... | collective-permute-start | bytes 552968 | tf_op jit(solution)/shard_map/ppermute | solution.py:272
  31.4 0.0 collective-permute-start.2
  31.4 2.2 %collective-permute-start.3 = (bf16[240,384]{1,0:T(8,128)(2,1)}, bf16[240,384]{1,0:T(8,128)(2,1)S(1)}, u32[]{:S(2)}, u32[]{:S(2)}) collective-permute-start(bf16[240,384]{1,0:T(8,128)(2,1)} %get-tuple-element.17), channel_id=1, source_target_pairs={{0,5},{1,13},{4,1},{5,9},{8,4},{9,12},{12,0},{13,8},{2,7},{3,15},{... | collective-permute-start | bytes 552968 | tf_op jit(solution)/shard_map/ppermute | solution.py:272
  33.6 1.0 collective-permute-done.refs_0_
  34.6 5.3 %collective-permute-done.1.refs_1_ = bf16[240,384]{1,0:T(8,128)(2,1)S(1)} collective-permute-done((bf16[240,384]{1,0:T(8,128)(2,1)}, bf16[240,384]{1,0:T(8,128)(2,1)S(1)}, u32[]{:S(2)}, u32[]{:S(2)}) %collective-permute-start.1) | collective-permute-done | bytes 184352 | tf_op jit(solution)/shard_map/ppermute | solution.py:272
  39.9 0.0 collective-permute-done.2.refs_2_
  39.9 2.0 %collective-permute-done.3.refs_3_ = bf16[240,384]{1,0:T(8,128)(2,1)S(1)} collective-permute-done((bf16[240,384]{1,0:T(8,128)(2,1)}, bf16[240,384]{1,0:T(8,128)(2,1)S(1)}, u32[]{:S(2)}, u32[]{:S(2)}) %collective-permute-start.3) | collective-permute-done | bytes 184352 | tf_op jit(solution)/shard_map/ppermute | solution.py:272
  41.9 0.6 shard_map.96
  42.5 4.2 %collective-permute-start.4 = (bf16[640,384]{1,0:T(8,128)(2,1)S(1)}, bf16[640,384]{1,0:T(8,128)(2,1)S(1)}, u32[]{:S(2)}, u32[]{:S(2)}) collective-permute-start(bf16[640,384]{1,0:T(8,128)(2,1)S(1)} %shard_map.96), channel_id=1, source_target_pairs={{0,1},{1,0},{2,3},{3,2},{4,5},{5,4},{6,7},{7,6},{8,9},{9,8},{10,11... | collective-permute-start | bytes 1474568 | tf_op jit(solution)/shard_map/ppermute | solution.py:280
  46.7 1.5 %collective-permute-done.4.refs_4_ = bf16[640,384]{1,0:T(8,128)(2,1)S(1)} collective-permute-done((bf16[640,384]{1,0:T(8,128)(2,1)S(1)}, bf16[640,384]{1,0:T(8,128)(2,1)S(1)}, u32[]{:S(2)}, u32[]{:S(2)}) %collective-permute-start.4) | collective-permute-done | bytes 491552 | tf_op jit(solution)/shard_map/ppermute | solution.py:280
  48.2 3.4 %shard_map.97 = bf16[320,384]{1,0:T(8,128)(2,1)S(1)} custom-call(bf16[240,384]{1,0:T(8,128)(2,1)S(1)} %collective-permute-done.refs_0_, bf16[240,384]{1,0:T(8,128)(2,1)S(1)} %collective-permute-done.1.refs_1_, bf16[240,384]{1,0:T(8,128)(2,1)S(1)} %collective-permute-done.2.refs_2_, bf16[240,384]{1,0:T(8,128)(2,1)S(1)} %collective-permute-done.3.refs_3_, ...), custom_call_target="tpu_custom_call" | custom-call | flops 314572800 | tf_op jit(solution)/shard_map/pallas_call | solution.py:225
  51.6 0.0 copy-start.6
  51.6 0.0 copy-start.3
  51.7 21.2 %all_gather.3.gathered = bf16[1280,384]{1,0:T(8,128)(2,1)S(1)} all-gather(bf16[320,384]{1,0:T(8,128)(2,1)S(1)} %shard_map.97), channel_id=1, replica_groups=mesh['groups'=2,'seq'=4,'wt'=2,'head'=2] {'seq'}, dimensions={0}, use_global_device_ids=true | all-gather | bytes 1228800 | tf_op jit(solution)/shard_map/all_gather | solution.py:293
  72.8 0.0 collective-permute-done.5.weight_c
  72.8 0.0 copy-done
  72.8 4.9 %shard_map.98 = (f32[160,640]{1,0:T(8,128)S(1)}, f32[160,640]{1,0:T(8,128)S(1)}, bf16[160,640]{1,0:T(8,128)(2,1)S(1)}, bf16[160,640]{1,0:T(8,128)(2,1)}) custom-call(bf16[1280,384]{1,0:T(8,128)(2,1)S(1)} %all_gather.3.gathered, bf16[768,1280]{1,0:T(8,128)(2,1)S(1)} %copy-done, bf16[768,1280]{1,0:T(8,128)(2,1)S(1)} %collective-permute-done.5.weight_c), custom_call_target="tpu_custom_call" | custom-call | flops 1258291200 | tf_op jit(solution)/shard_map/pallas_call | solution.py:225
  77.8 0.0 copy-start.1
  77.8 0.7 copy-done.1
  78.5 0.0 copy-start.4
  78.5 0.0 copy-start.5
  78.5 0.0 copy-start.2
  78.5 1.2 %collective-permute-start.6 = (bf16[160,640]{1,0:T(8,128)(2,1)S(1)}, bf16[160,640]{1,0:T(8,128)(2,1)S(1)}, u32[]{:S(2)}, u32[]{:S(2)}) collective-permute-start(bf16[160,640]{1,0:T(8,128)(2,1)S(1)} %get-tuple-element.19), channel_id=1, source_target_pairs={{0,2},{2,0},{1,3},{3,1},{4,6},{6,4},{5,7},{7,5},{8,10},{10,8},{9,1... | collective-permute-start | bytes 614408 | tf_op jit(solution)/shard_map/ppermute | solution.py:309
  79.8 0.0 copy-done.6
  79.8 0.2 collective-permute-start.9
  80.0 3.6 %collective-permute-done.6.arrived = bf16[160,640]{1,0:T(8,128)(2,1)S(1)} collective-permute-done((bf16[160,640]{1,0:T(8,128)(2,1)S(1)}, bf16[160,640]{1,0:T(8,128)(2,1)S(1)}, u32[]{:S(2)}, u32[]{:S(2)}) %collective-permute-start.6) | collective-permute-done | bytes 204832 | tf_op jit(solution)/shard_map/ppermute | solution.py:309
  83.7 6.8 %collective-permute-start.7 = (bf16[80,640]{1,0:T(8,128)(2,1)S(1)}, bf16[80,640]{1,0:T(8,128)(2,1)S(1)}, u32[]{:S(2)}, u32[]{:S(2)}) collective-permute-start(bf16[80,640]{1,0:T(8,128)(2,1)S(1)} %get-tuple-element.20), channel_id=1, source_target_pairs={{0,0},{1,8},{2,4},{3,12},{4,1},{5,9},{6,5},{7,13},{8,2},{9,10},{10... | collective-permute-start | bytes 307208 | tf_op jit(solution)/shard_map/ppermute | solution.py:319
  90.5 0.1 collective-permute-start.8
  90.6 0.0 copy-done.3
  90.6 0.3 multiply_reduce_fusion
  90.9 0.0 collective-permute-done.9.arrived
  90.9 0.0 copy-done.2
  90.9 0.1 shard_map.100
  91.0 4.9 %collective-permute-start.10 = (bf16[80,640]{1,0:T(8,128)(2,1)S(1)}, bf16[80,640]{1,0:T(8,128)(2,1)S(1)}, u32[]{:S(2)}, u32[]{:S(2)}) collective-permute-start(bf16[80,640]{1,0:T(8,128)(2,1)S(1)} %get-tuple-element.24), channel_id=1, source_target_pairs={{0,0},{1,8},{2,4},{3,12},{4,1},{5,9},{6,5},{7,13},{8,2},{9,10},{10... | collective-permute-start | bytes 307208 | tf_op jit(solution)/shard_map/ppermute | solution.py:319
  95.9 0.1 collective-permute-start.11
  95.9 0.0 collective-permute-done.7
  95.9 2.3 %collective-permute-done.8 = bf16[80,640]{1,0:T(8,128)(2,1)S(1)} collective-permute-done((bf16[80,640]{1,0:T(8,128)(2,1)S(1)}, bf16[80,640]{1,0:T(8,128)(2,1)S(1)}, u32[]{:S(2)}, u32[]{:S(2)}) %collective-permute-start.8) | collective-permute-done | bytes 102432 | tf_op jit(solution)/shard_map/ppermute | solution.py:319
  98.3 5.8 %collective-permute-done.10 = bf16[80,640]{1,0:T(8,128)(2,1)S(1)} collective-permute-done((bf16[80,640]{1,0:T(8,128)(2,1)S(1)}, bf16[80,640]{1,0:T(8,128)(2,1)S(1)}, u32[]{:S(2)}, u32[]{:S(2)}) %collective-permute-start.10) | collective-permute-done | bytes 102432 | tf_op jit(solution)/shard_map/ppermute | solution.py:319
  104.1 0.4 collective-permute-done.11
  104.6 0.0 copy-done.4
  104.6 0.0 copy-done.5
  104.6 1.3 %add_add_fusion = (f32[160,1280]{1,0:T(8,128)}, f32[160,1280]{1,0:T(8,128)}) fusion(f32[160,1280]{1,0:T(8,128)S(1)} %copy-done.4, f32[160,1280]{1,0:T(8,128)S(1)} %multiply_reduce_fusion, f32[1280]{0:T(1024)S(1)} %copy-done.5, bf16[80,640]{1,0:T(8,128)(2,1)S(1)} %get-tuple-element.31, bf16[80,640]{1,0:T(8,128)(2,1)S(1)} %get-tuple-element.30, ...), kind=kLoop, calls=%fused_computation.2 | loop fusion | flops 2252800 | bytes 3691520 | tf_op jit(solution)/shard_map/add | solution.py:334
  (4 shorter events, 0.1 us)
Async XLA Ops:
  0.6 72.2 %copy-start = (bf16[768,1280]{1,0:T(8,128)(2,1)S(1)}, bf16[768,1280]{1,0:T(8,128)(2,1)}, u32[]{:S(2)}) copy-start(bf16[768,1280]{1,0:T(8,128)(2,1)} %weight.1) | copy-start | bytes 5898244
  0.6 72.2 %collective-permute-start.5 = (bf16[768,1280]{1,0:T(8,128)(2,1)}, bf16[768,1280]{1,0:T(8,128)(2,1)S(1)}, u32[]{:S(2)}, u32[]{:S(2)}) collective-permute-start(bf16[768,1280]{1,0:T(8,128)(2,1)} %weight.1), channel_id=1, source_target_pairs={{0,1},{1,0},{2,3},{3,2},{4,5},{5,4},{6,7},{7,6},{8,9},{9,8},{10,11... | collective-permute-start | bytes 5898248 | tf_op jit(solution)/shard_map/ppermute | solution.py:254
  24.3 10.3 %collective-permute-start = (bf16[240,384]{1,0:T(8,128)(2,1)}, bf16[240,384]{1,0:T(8,128)(2,1)S(1)}, u32[]{:S(2)}, u32[]{:S(2)}) collective-permute-start(bf16[240,384]{1,0:T(8,128)(2,1)} %get-tuple-element.14), channel_id=1, source_target_pairs={{0,0},{1,8},{4,4},{5,12},{8,1},{9,9},{12,5},{13,13},{2,2},{3,10},{... | collective-permute-start | bytes 552968 | tf_op jit(solution)/shard_map/ppermute | solution.py:272
  29.9 10.0 %collective-permute-start.1 = (bf16[240,384]{1,0:T(8,128)(2,1)}, bf16[240,384]{1,0:T(8,128)(2,1)S(1)}, u32[]{:S(2)}, u32[]{:S(2)}) collective-permute-start(bf16[240,384]{1,0:T(8,128)(2,1)} %get-tuple-element.15), channel_id=1, source_target_pairs={{0,4},{1,12},{4,0},{5,8},{8,5},{9,13},{12,1},{13,9},{2,6},{3,14},{... | collective-permute-start | bytes 552968 | tf_op jit(solution)/shard_map/ppermute | solution.py:272
  31.4 8.5 %collective-permute-start.2 = (bf16[240,384]{1,0:T(8,128)(2,1)}, bf16[240,384]{1,0:T(8,128)(2,1)S(1)}, u32[]{:S(2)}, u32[]{:S(2)}) collective-permute-start(bf16[240,384]{1,0:T(8,128)(2,1)} %get-tuple-element.16), channel_id=1, source_target_pairs={{0,1},{1,9},{4,5},{5,13},{8,0},{9,8},{12,4},{13,12},{2,3},{3,11},{... | collective-permute-start | bytes 552968 | tf_op jit(solution)/shard_map/ppermute | solution.py:272
  31.4 10.4 %collective-permute-start.3 = (bf16[240,384]{1,0:T(8,128)(2,1)}, bf16[240,384]{1,0:T(8,128)(2,1)S(1)}, u32[]{:S(2)}, u32[]{:S(2)}) collective-permute-start(bf16[240,384]{1,0:T(8,128)(2,1)} %get-tuple-element.17), channel_id=1, source_target_pairs={{0,5},{1,13},{4,1},{5,9},{8,4},{9,12},{12,0},{13,8},{2,7},{3,15},{... | collective-permute-start | bytes 552968 | tf_op jit(solution)/shard_map/ppermute | solution.py:272
  42.5 5.7 %collective-permute-start.4 = (bf16[640,384]{1,0:T(8,128)(2,1)S(1)}, bf16[640,384]{1,0:T(8,128)(2,1)S(1)}, u32[]{:S(2)}, u32[]{:S(2)}) collective-permute-start(bf16[640,384]{1,0:T(8,128)(2,1)S(1)} %shard_map.96), channel_id=1, source_target_pairs={{0,1},{1,0},{2,3},{3,2},{4,5},{5,4},{6,7},{7,6},{8,9},{9,8},{10,11... | collective-permute-start | bytes 1474568 | tf_op jit(solution)/shard_map/ppermute | solution.py:280
  51.6 28.1 %copy-start.6 = (s32[4]{0:T(128)S(1)}, s32[4]{0:T(128)}, u32[]{:S(2)}) copy-start(s32[4]{0:T(128)} %param.15) | copy-start | bytes 52
  51.6 38.9 %copy-start.3 = (f32[4,160,1280]{2,1,0:T(8,128)S(1)}, f32[4,160,1280]{2,1,0:T(8,128)}, u32[]{:S(2)}) copy-start(f32[4,160,1280]{2,1,0:T(8,128)} %param.14) | copy-start | bytes 9830404
  77.8 0.8 copy-start.1
  78.5 26.1 %copy-start.4 = (f32[160,1280]{1,0:T(8,128)S(1)}, f32[160,1280]{1,0:T(8,128)}, u32[]{:S(2)}) copy-start(f32[160,1280]{1,0:T(8,128)} %param.13) | copy-start | bytes 2457604
  78.5 26.1 %copy-start.5 = (f32[1280]{0:T(1024)S(1)}, f32[1280]{0:T(1024)}, u32[]{:S(2)}) copy-start(f32[1280]{0:T(1024)} %param.12) | copy-start | bytes 15364
  78.5 12.4 %copy-start.2 = (f32[160,640]{1,0:T(8,128)S(1)}, f32[160,640]{1,0:T(8,128)}, u32[]{:S(2)}) copy-start(f32[160,640]{1,0:T(8,128)} %copy-done.1) | copy-start | bytes 1228804
  78.5 5.1 %collective-permute-start.6 = (bf16[160,640]{1,0:T(8,128)(2,1)S(1)}, bf16[160,640]{1,0:T(8,128)(2,1)S(1)}, u32[]{:S(2)}, u32[]{:S(2)}) collective-permute-start(bf16[160,640]{1,0:T(8,128)(2,1)S(1)} %get-tuple-element.19), channel_id=1, source_target_pairs={{0,2},{2,0},{1,3},{3,1},{4,6},{6,4},{5,7},{7,5},{8,10},{10,8},{9,1... | collective-permute-start | bytes 614408 | tf_op jit(solution)/shard_map/ppermute | solution.py:309
  79.8 11.1 %collective-permute-start.9 = (bf16[160,640]{1,0:T(8,128)(2,1)}, bf16[160,640]{1,0:T(8,128)(2,1)S(1)}, u32[]{:S(2)}, u32[]{:S(2)}) collective-permute-start(bf16[160,640]{1,0:T(8,128)(2,1)} %get-tuple-element.23), channel_id=1, source_target_pairs={{0,2},{2,0},{1,3},{3,1},{4,6},{6,4},{5,7},{7,5},{8,10},{10,8},{9,1... | collective-permute-start | bytes 614408 | tf_op jit(solution)/shard_map/ppermute | solution.py:309
  83.7 12.3 %collective-permute-start.7 = (bf16[80,640]{1,0:T(8,128)(2,1)S(1)}, bf16[80,640]{1,0:T(8,128)(2,1)S(1)}, u32[]{:S(2)}, u32[]{:S(2)}) collective-permute-start(bf16[80,640]{1,0:T(8,128)(2,1)S(1)} %get-tuple-element.20), channel_id=1, source_target_pairs={{0,0},{1,8},{2,4},{3,12},{4,1},{5,9},{6,5},{7,13},{8,2},{9,10},{10... | collective-permute-start | bytes 307208 | tf_op jit(solution)/shard_map/ppermute | solution.py:319
  90.5 7.8 %collective-permute-start.8 = (bf16[80,640]{1,0:T(8,128)(2,1)S(1)}, bf16[80,640]{1,0:T(8,128)(2,1)S(1)}, u32[]{:S(2)}, u32[]{:S(2)}) collective-permute-start(bf16[80,640]{1,0:T(8,128)(2,1)S(1)} %get-tuple-element.21), channel_id=1, source_target_pairs={{0,8},{1,0},{2,12},{3,4},{4,9},{5,1},{6,13},{7,5},{8,10},{9,2},{10... | collective-permute-start | bytes 307208 | tf_op jit(solution)/shard_map/ppermute | solution.py:319
  91.0 13.2 %collective-permute-start.10 = (bf16[80,640]{1,0:T(8,128)(2,1)S(1)}, bf16[80,640]{1,0:T(8,128)(2,1)S(1)}, u32[]{:S(2)}, u32[]{:S(2)}) collective-permute-start(bf16[80,640]{1,0:T(8,128)(2,1)S(1)} %get-tuple-element.24), channel_id=1, source_target_pairs={{0,0},{1,8},{2,4},{3,12},{4,1},{5,9},{6,5},{7,13},{8,2},{9,10},{10... | collective-permute-start | bytes 307208 | tf_op jit(solution)/shard_map/ppermute | solution.py:319
  95.9 8.7 %collective-permute-start.11 = (bf16[80,640]{1,0:T(8,128)(2,1)S(1)}, bf16[80,640]{1,0:T(8,128)(2,1)S(1)}, u32[]{:S(2)}, u32[]{:S(2)}) collective-permute-start(bf16[80,640]{1,0:T(8,128)(2,1)S(1)} %get-tuple-element.25), channel_id=1, source_target_pairs={{0,8},{1,0},{2,12},{3,4},{4,9},{5,1},{6,13},{7,5},{8,10},{9,2},{10... | collective-permute-start | bytes 307208 | tf_op jit(solution)/shard_map/ppermute | solution.py:319

commit v4 on v0

--- a/solution.py
+++ b/solution.py
@@ -1,9 +1,16 @@
+import functools
+
 import jax
 import jax.numpy as jnp
 from jax import lax
+from jax.experimental import pallas as pl
+from jax.experimental.pallas import tpu as pltpu
 from jax.sharding import PartitionSpec as P
 
 HEAD_DIM = 128
+VMEM_BYTES = 48 * 1024 * 1024
+PACK_BYTES = 59 * 1024 * 1024 + 400 * 1024
+LOG2_E = 1.4426950408889634
 
 
 def attend(state_in, key_rows, value_rows, query_heads, score_scale):
@@ -46,7 +53,7 @@
     return normed.transpose(1, 0, 2).reshape(row_count, -1).astype(jnp.bfloat16)
 
 
-def local(
+def local_general(
     queries,
     key_vectors,
     value_vectors,
@@ -82,6 +89,199 @@
     return (mixed_state, fresh_delta)
 
 
+def bits():
+    z = lax.axis_index("seq")
+    return lax.div(z, 2), lax.rem(z, 2)
+
+
+def flip(bit, value):
+    return 1 - bit if value else bit
+
+
+def pack_kernel(queries, keys, values, *refs):
+    outs, sems = refs[:4], refs[4]
+    rows, width = queries.shape[0], outs[0].shape[1]
+    half = rows // 2
+    zh, zl = bits()
+    copies = []
+    for k in range(4):
+        part = pl.ds(pl.multiple_of(flip(zh, k // 2) * half, 16), half)
+        columns = pl.ds(pl.multiple_of(flip(zl, k % 2) * width, 128), width)
+        moves = [
+            (keys.at[part, columns], outs[k].at[pl.ds(0, half), :]),
+            (values.at[part, columns], outs[k].at[pl.ds(half, half), :]),
+        ]
+        if k < 2:
+            moves.append((queries.at[:, columns], outs[k].at[pl.ds(rows, rows), :]))
+        for start, end in moves:
+            copies.append(pltpu.make_async_copy(start, end, sems.at[len(copies)]))
+    for copy in copies:
+        copy.start()
+    for copy in copies:
+        copy.wait()
+
+
+def join_kernel(*refs):
+    blocks, joined = refs[:4], refs[4]
+    rows = joined.shape[0] // 4
+    for k, block in enumerate(blocks):
+        joined[k * rows : (k + 1) * rows, :] = block[:rows, :]
+
+
+def attention_kernel(*refs):
+    blocks, sibling, out = refs[:4], refs[4], refs[5]
+    key_all, value_all, query_all = refs[6:]
+    rows = query_all.shape[0] // 2
+    half = rows // 2
+    for k in range(4):
+        here, there = slice(k * half, (k + 1) * half), slice((4 + k) * half, (5 + k) * half)
+        key_all[here, :] = blocks[k][:half, :]
+        value_all[here, :] = blocks[k][half:rows, :]
+        key_all[there, :] = sibling[k * rows : k * rows + half, :]
+        value_all[there, :] = sibling[k * rows + half : (k + 1) * rows, :]
+    _, zl = bits()
+    for k in range(2):
+        at = pl.ds(pl.multiple_of(flip(zl, k) * rows, 16), rows)
+        query_all[at, :] = blocks[k][rows:, :]
+    for h in range(out.shape[1] // HEAD_DIM):
+        columns = slice(h * HEAD_DIM, (h + 1) * HEAD_DIM)
+        scores = lax.dot_general(
+            query_all[:, columns],
+            key_all[:, columns],
+            (((1,), (1,)), ((), ())),
+            preferred_element_type=jnp.float32,
+        )
+        peak = jnp.max(scores, axis=1, keepdims=True)
+        weights = jnp.exp2((scores - peak) * (LOG2_E * HEAD_DIM ** (-0.5)))
+        total = jnp.sum(weights, axis=1, keepdims=True)
+        result = jnp.dot(
+            weights.astype(jnp.bfloat16), value_all[:, columns], preferred_element_type=jnp.float32
+        )
+        out[:, columns] = (result / total).astype(out.dtype)
+
+
+def project_kernel(first, gathered, weight, weight_c, keep, send):
+    rows, count = keep.shape
+    core, x = lax.axis_index("head"), lax.axis_index("wt")
+    columns = slice(first, first + count)
+    total = None
+    for other, block in enumerate((weight, weight_c)):
+        start = 2 * flip(core, other) * 2 * rows
+        left = jnp.concatenate(
+            [
+                gathered[pl.ds(pl.multiple_of(start + low * 2 * rows, 16), 2 * rows), :]
+                for low in range(2)
+            ],
+            axis=1,
+        )
+        term = jnp.dot(left, block[:, columns], preferred_element_type=jnp.float32)
+        total = term if total is None else total + term
+    for low in range(2):
+        part = total[low * rows : (low + 1) * rows]
+
+        @pl.when(x == low)
+        def _():
+            keep[...] = part
+
+        @pl.when(x != low)
+        def _():
+            send[...] = part.astype(send.dtype)
+
+
+def add_kernel(keep, arrived, out):
+    out[...] = (keep[...] + arrived[...].astype(jnp.float32)).astype(out.dtype)
+
+
+def call(kernel, args, outs, scratch=(), far_in=False, flops=0, vmem=VMEM_BYTES):
+    place = pl.ANY if far_in else pltpu.VMEM
+    return pl.pallas_call(
+        kernel,
+        in_specs=[pl.BlockSpec(memory_space=place)] * len(args),
+        out_specs=[pl.BlockSpec(memory_space=pltpu.VMEM)] * len(outs),
+        out_shape=[jax.ShapeDtypeStruct(shape, dtype) for shape, dtype in outs],
+        scratch_shapes=list(scratch),
+        compiler_params=pltpu.CompilerParams(vmem_limit_bytes=vmem),
+        cost_estimate=pl.CostEstimate(flops=flops, bytes_accessed=0, transcendentals=0),
+    )(*args)
+
+
+def local_heads(
+    queries,
+    key_vectors,
+    value_vectors,
+    out_weight,
+    gate_values,
+    hidden_state,
+    cached_deltas,
+    skip_flags,
+):
+    rows, features = queries.shape
+    width = features // 2
+    depth, columns = out_weight.shape
+    swap = [(0, 1), (1, 0)]
+    bf16 = jnp.bfloat16
+
+    weight_c = lax.ppermute(out_weight, "head", swap)
+
+    packed = call(
+        pack_kernel,
+        (queries, key_vectors, value_vectors),
+        [((2 * rows, width), bf16)] * 2 + [((rows, width), bf16)] * 2,
+        [pltpu.SemaphoreType.DMA((10,))],
+        far_in=True,
+        vmem=PACK_BYTES,
+    )
+    moved = []
+    for k in range(4):
+        k1, k0 = k // 2, k % 2
+        pairs = []
+        for zz in range(4):
+            for cc in range(2):
+                to_z = 2 * cc + ((zz % 2) ^ k0)
+                pairs.append((zz * 2 + cc, to_z * 2 + ((zz // 2) ^ k1)))
+        moved.append(lax.ppermute(packed[k], ("seq", "head"), pairs))
+    (joined,) = call(join_kernel, moved, [((4 * rows, width), bf16)])
+    sibling = lax.ppermute(joined, "head", swap)
+    (attention_out,) = call(
+        attention_kernel,
+        moved + [sibling],
+        [((2 * rows, width), bf16)],
+        [
+            pltpu.VMEM((4 * rows, width), bf16),
+            pltpu.VMEM((4 * rows, width), bf16),
+            pltpu.VMEM((2 * rows, width), bf16),
+        ],
+        flops=4 * (2 * rows) * (4 * rows) * width,
+    )
+    gathered = lax.all_gather(attention_out, "seq", axis=0, tiled=True)
+
+    pairs = []
+    for zz in range(4):
+        for xx in range(2):
+            for cc in range(2):
+                to = ((2 * cc + xx) * 2 + zz // 2) * 2 + zz % 2
+                pairs.append(((zz * 2 + xx) * 2 + cc, to))
+    cut = columns * 2 // 5 // 256 * 256
+    owned = []
+    for first, count in ((0, cut), (cut, columns - cut)):
+        keep, send = call(
+            functools.partial(project_kernel, first),
+            (gathered, out_weight, weight_c),
+            [((rows, count), jnp.float32), ((rows, count), bf16)],
+            flops=4 * (2 * rows) * depth * count,
+        )
+        gathered, _ = lax.optimization_barrier((gathered, send))
+        arrived = lax.ppermute(send, "wt", swap)
+        (summed,) = call(add_kernel, (keep, arrived), [((rows, count), bf16)])
+        owned.append(lax.ppermute(summed, ("seq", "wt", "head"), pairs))
+    head_total = jnp.concatenate(owned, axis=1).astype(jnp.float32)
+    kept_deltas = jnp.sum(skip_flags.astype(jnp.float32)[:, None, None] * cached_deltas, axis=0)
+    resting = hidden_state + kept_deltas
+    fresh_delta = head_total * gate_values[None, :]
+    mixed_state = resting + fresh_delta
+    return (mixed_state, fresh_delta)
+
+
 def solution(mesh):
     placed = (
         P(("groups", "seq"), ("wt", "head")),
@@ -93,6 +293,14 @@
         P(None, ("groups", "seq"), ("wt", "head")),
         P("groups"),
     )
+
+    def local(*args):
+        sizes = tuple(mesh.shape[name] for name in ("seq", "wt", "head"))
+        rows, features = args[0].shape
+        if sizes == (4, 2, 2) and rows % 32 == 0 and features % (2 * HEAD_DIM) == 0 and args[3].shape[1] % 256 == 0 and args[3].shape[1] >= 640:
+            return local_heads(*args)
+        return local_general(*args)
+
     return jax.shard_map(
         local,
         mesh=mesh,

time: 217 us -> 78.6 us (0.36)
  the two profiles are of different devices: /device:TPU:2 before, /device:TPU:1 now
where the time goes in v4:
time: 78.6 us; the launch traced here: 78.4 us
  starting transfers between devices  27.2 us (35%)
  waiting for transfers between devices  22.6 us (29%)
  blocking collectives  20.5 us (26%)
  Pallas kernels  5.61 us (7%)
  other arithmetic  1.64 us (2%)
  between operations  0.79 us (1%)
    all_gather x1, blocking collectives, local_heads(): gathered = lax.all_gather(attention_out, 'seq', axis=0, tiled=True)  20.5 us
    ppermute x2, starting transfers between devices, local_heads(): owned.append(lax.ppermute(summed, ('seq', 'wt', 'head'), pairs))  11.4 us
    ppermute x4, starting transfers between devices, local_heads(): moved.append(lax.ppermute(packed[k], ('seq', 'head'), pairs))  9.31 us
    ppermute x2, waiting for transfers between devices, local_heads(): owned.append(lax.ppermute(summed, ('seq', 'wt', 'head'), pairs))  8.4 us
    ppermute x4, waiting for transfers between devices, local_heads(): moved.append(lax.ppermute(packed[k], ('seq', 'head'), pairs))  8.25 us
    pallas_call x7, Pallas kernels, call(): pl.pallas_call(kernel, in_specs=[pl.BlockSpec(memory_space=place)] * len(...  5.61 us
    ppermute x1, starting transfers between devices, local_heads(): sibling = lax.ppermute(joined, 'head', swap)  4.77 us
    ppermute x2, waiting for transfers between devices, local_heads(): arrived = lax.ppermute(send, 'wt', swap)  4.5 us
  transfers between devices with their start and end apart: 10, of which 5 were waited for; matrix products, arithmetic and copies ran while one was open for 0% of the time, Pallas kernels for 5%

profile of v4, /device:TPU:1, one launch (start us, length us, event | category | flops | bytes accessed | tf_op | source)
XLA Modules:
  0.0 78.4 jit_solution(15445720098821666392)
XLA Ops:
  0.6 0.0 copy-start
  0.6 0.1 collective-permute-start.5
  0.8 2.2 %shard_map.95 = (bf16[320,384]{1,0:T(8,128)(2,1)}, bf16[320,384]{1,0:T(8,128)(2,1)}, bf16[160,384]{1,0:T(8,128)(2,1)}, bf16[160,384]{1,0:T(8,128)(2,1)}) custom-call(bf16[160,768]{1,0:T(8,128)(2,1)} %queries.1, bf16[160,768]{1,0:T(8,128)(2,1)} %keys.1, bf16[160,768]{1,0:T(8,128)(2,1)} %values.1), custom_call_target="tpu_custom_call" | custom-call | tf_op jit(solution)/shard_map/pallas_call | solution.py:197
  3.0 5.6 %collective-permute-start = (bf16[320,384]{1,0:T(8,128)(2,1)}, bf16[320,384]{1,0:T(8,128)(2,1)S(1)}, u32[]{:S(2)}, u32[]{:S(2)}) collective-permute-start(bf16[320,384]{1,0:T(8,128)(2,1)} %get-tuple-element.11), channel_id=1, source_target_pairs={{0,0},{1,8},{4,4},{5,12},{8,1},{9,9},{12,5},{13,13},{2,2},{3,10},{... | collective-permute-start | bytes 737288 | tf_op jit(solution)/shard_map/ppermute | solution.py:242
  8.5 1.4 %collective-permute-start.1 = (bf16[320,384]{1,0:T(8,128)(2,1)}, bf16[320,384]{1,0:T(8,128)(2,1)S(1)}, u32[]{:S(2)}, u32[]{:S(2)}) collective-permute-start(bf16[320,384]{1,0:T(8,128)(2,1)} %get-tuple-element.12), channel_id=1, source_target_pairs={{0,4},{1,12},{4,0},{5,8},{8,5},{9,13},{12,1},{13,9},{2,6},{3,14},{... | collective-permute-start | bytes 737288 | tf_op jit(solution)/shard_map/ppermute | solution.py:242
  9.9 0.0 collective-permute-start.2
  9.9 2.3 %collective-permute-start.3 = (bf16[160,384]{1,0:T(8,128)(2,1)}, bf16[160,384]{1,0:T(8,128)(2,1)S(1)}, u32[]{:S(2)}, u32[]{:S(2)}) collective-permute-start(bf16[160,384]{1,0:T(8,128)(2,1)} %get-tuple-element.14), channel_id=1, source_target_pairs={{0,5},{1,13},{4,1},{5,9},{8,4},{9,12},{12,0},{13,8},{2,7},{3,15},{... | collective-permute-start | bytes 368648 | tf_op jit(solution)/shard_map/ppermute | solution.py:242
  12.3 6.9 %collective-permute-done.2.refs_2_ = bf16[160,384]{1,0:T(8,128)(2,1)S(1)} collective-permute-done((bf16[160,384]{1,0:T(8,128)(2,1)}, bf16[160,384]{1,0:T(8,128)(2,1)S(1)}, u32[]{:S(2)}, u32[]{:S(2)}) %collective-permute-start.2) | collective-permute-done | bytes 122912 | tf_op jit(solution)/shard_map/ppermute | solution.py:242
  19.2 1.3 %collective-permute-done.3.refs_3_ = bf16[160,384]{1,0:T(8,128)(2,1)S(1)} collective-permute-done((bf16[160,384]{1,0:T(8,128)(2,1)}, bf16[160,384]{1,0:T(8,128)(2,1)S(1)}, u32[]{:S(2)}, u32[]{:S(2)}) %collective-permute-start.3) | collective-permute-done | bytes 122912 | tf_op jit(solution)/shard_map/ppermute | solution.py:242
  20.5 0.0 collective-permute-done.refs_0_
  20.5 0.0 collective-permute-done.1.refs_1_
  20.6 4.8 %collective-permute-start.4 = (bf16[640,384]{1,0:T(8,128)(2,1)S(1)}, bf16[640,384]{1,0:T(8,128)(2,1)S(1)}, u32[]{:S(2)}, u32[]{:S(2)}) collective-permute-start(bf16[640,384]{1,0:T(8,128)(2,1)S(1)} %shard_map.96), channel_id=1, source_target_pairs={{0,1},{1,0},{2,3},{3,2},{4,5},{5,4},{6,7},{7,6},{8,9},{9,8},{10,11... | collective-permute-start | bytes 1474568 | tf_op jit(solution)/shard_map/ppermute | solution.py:244
  25.3 1.5 %collective-permute-done.4.refs_4_ = bf16[640,384]{1,0:T(8,128)(2,1)S(1)} collective-permute-done((bf16[640,384]{1,0:T(8,128)(2,1)S(1)}, bf16[640,384]{1,0:T(8,128)(2,1)S(1)}, u32[]{:S(2)}, u32[]{:S(2)}) %collective-permute-start.4) | collective-permute-done | bytes 491552 | tf_op jit(solution)/shard_map/ppermute | solution.py:244
  26.8 1.6 %shard_map.97 = bf16[320,384]{1,0:T(8,128)(2,1)S(1)} custom-call(bf16[320,384]{1,0:T(8,128)(2,1)S(1)} %collective-permute-done.refs_0_, bf16[320,384]{1,0:T(8,128)(2,1)S(1)} %collective-permute-done.1.refs_1_, bf16[160,384]{1,0:T(8,128)(2,1)S(1)} %collective-permute-done.2.refs_2_, bf16[160,384]{1,0:T(8,128)(2,1)S(1)} %collective-permute-done.3.refs_3_, ...), custom_call_target="tpu_custom_call" | custom-call | flops 314572800 | tf_op jit(solution)/shard_map/pallas_call | solution.py:197
  28.5 20.5 %all_gather.3.gathered = bf16[1280,384]{1,0:T(8,128)(2,1)S(1)} all-gather(bf16[320,384]{1,0:T(8,128)(2,1)S(1)} %shard_map.97), channel_id=1, replica_groups=mesh['groups'=2,'seq'=4,'wt'=2,'head'=2] {'seq'}, dimensions={0}, use_global_device_ids=true | all-gather | bytes 1228800 | tf_op jit(solution)/shard_map/all_gather | solution.py:256
  49.0 0.0 collective-permute-done.5.weight_c
  49.0 0.0 copy-done
  49.0 0.7 shard_map.98
  49.7 0.0 copy-start.4
  49.7 0.0 copy-start.1
  49.7 1.0 %shard_map.100 = (f32[160,768]{1,0:T(8,128)S(1)}, bf16[160,768]{1,0:T(8,128)(2,1)S(1)}) custom-call(bf16[1280,384]{1,0:T(8,128)(2,1)S(1)} %all_gather.3.gathered, bf16[768,1280]{1,0:T(8,128)(2,1)S(1)} %copy-done, bf16[768,1280]{1,0:T(8,128)(2,1)S(1)} %collective-permute-done.5.weight_c), custom_call_target="tpu_custom_call" | custom-call | flops 754974720 | tf_op jit(solution)/shard_map/pallas_call | solution.py:197
  50.7 0.0 copy-start.2
  50.7 0.0 copy-start.3
  50.7 1.3 %collective-permute-start.8 = (bf16[160,768]{1,0:T(8,128)(2,1)S(1)}, bf16[160,768]{1,0:T(8,128)(2,1)S(1)}, u32[]{:S(2)}, u32[]{:S(2)}) collective-permute-start(bf16[160,768]{1,0:T(8,128)(2,1)S(1)} %get-tuple-element.19), channel_id=1, source_target_pairs={{0,2},{2,0},{1,3},{3,1},{4,6},{6,4},{5,7},{7,5},{8,10},{10,8},{9,1... | collective-permute-start | bytes 737288 | tf_op jit(solution)/shard_map/ppermute | solution.py:274
  52.0 0.2 collective-permute-start.6
  52.2 4.5 %collective-permute-done.8.arrived = bf16[160,768]{1,0:T(8,128)(2,1)S(1)} collective-permute-done((bf16[160,768]{1,0:T(8,128)(2,1)S(1)}, bf16[160,768]{1,0:T(8,128)(2,1)S(1)}, u32[]{:S(2)}, u32[]{:S(2)}) %collective-permute-start.8) | collective-permute-done | bytes 245792 | tf_op jit(solution)/shard_map/ppermute | solution.py:274
  56.8 6.8 %collective-permute-start.9 = (bf16[160,768]{1,0:T(8,128)(2,1)S(1)}, bf16[160,768]{1,0:T(8,128)(2,1)S(1)}, u32[]{:S(2)}, u32[]{:S(2)}) collective-permute-start(bf16[160,768]{1,0:T(8,128)(2,1)S(1)} %shard_map.101), channel_id=1, source_target_pairs={{0,0},{1,8},{2,4},{3,12},{4,1},{5,9},{6,5},{7,13},{8,2},{9,10},{10... | collective-permute-start | bytes 737288 | tf_op jit(solution)/shard_map/ppermute | solution.py:276
  63.6 0.0 copy-done.4
  63.6 0.0 collective-permute-done.6.arrived
  63.7 4.6 %collective-permute-start.7 = (bf16[160,512]{1,0:T(8,128)(2,1)S(1)}, bf16[160,512]{1,0:T(8,128)(2,1)S(1)}, u32[]{:S(2)}, u32[]{:S(2)}) collective-permute-start(bf16[160,512]{1,0:T(8,128)(2,1)S(1)} %shard_map.99), channel_id=1, source_target_pairs={{0,0},{1,8},{2,4},{3,12},{4,1},{5,9},{6,5},{7,13},{8,2},{9,10},{10... | collective-permute-start | bytes 491528 | tf_op jit(solution)/shard_map/ppermute | solution.py:276
  68.3 0.0 copy-done.1
  68.3 0.3 multiply_reduce_fusion
  68.6 8.4 %collective-permute-done.7 = bf16[160,512]{1,0:T(8,128)(2,1)S(1)} collective-permute-done((bf16[160,512]{1,0:T(8,128)(2,1)S(1)}, bf16[160,512]{1,0:T(8,128)(2,1)S(1)}, u32[]{:S(2)}, u32[]{:S(2)}) %collective-permute-start.7) | collective-permute-done | bytes 163872 | tf_op jit(solution)/shard_map/ppermute | solution.py:276
  77.0 0.0 collective-permute-done.9
  77.0 0.0 copy-done.2
  77.0 0.0 copy-done.3
  77.0 1.3 %add_add_fusion = (f32[160,1280]{1,0:T(8,128)}, f32[160,1280]{1,0:T(8,128)}) fusion(f32[160,1280]{1,0:T(8,128)S(1)} %copy-done.2, f32[160,1280]{1,0:T(8,128)S(1)} %multiply_reduce_fusion, f32[1280]{0:T(1024)S(1)} %copy-done.3, bf16[160,768]{1,0:T(8,128)(2,1)S(1)} %collective-permute-done.9, bf16[160,512]{1,0:T(8,128)(2,1)S(1)} %collective-permute-done.7), kind=kLoop, calls=%fused_computation.2 | loop fusion | flops 1433600 | bytes 3691520 | tf_op jit(solution)/shard_map/add | solution.py:281
  (4 shorter events, 0.1 us)
Async XLA Ops:
  0.6 48.3 %copy-start = (bf16[768,1280]{1,0:T(8,128)(2,1)S(1)}, bf16[768,1280]{1,0:T(8,128)(2,1)}, u32[]{:S(2)}) copy-start(bf16[768,1280]{1,0:T(8,128)(2,1)} %weight.3) | copy-start | bytes 5898244
  0.6 48.3 %collective-permute-start.5 = (bf16[768,1280]{1,0:T(8,128)(2,1)}, bf16[768,1280]{1,0:T(8,128)(2,1)S(1)}, u32[]{:S(2)}, u32[]{:S(2)}) collective-permute-start(bf16[768,1280]{1,0:T(8,128)(2,1)} %weight.3), channel_id=1, source_target_pairs={{0,1},{1,0},{2,3},{3,2},{4,5},{5,4},{6,7},{7,6},{8,9},{9,8},{10,11... | collective-permute-start | bytes 5898248 | tf_op jit(solution)/shard_map/ppermute | solution.py:224
  3.0 17.6 %collective-permute-start = (bf16[320,384]{1,0:T(8,128)(2,1)}, bf16[320,384]{1,0:T(8,128)(2,1)S(1)}, u32[]{:S(2)}, u32[]{:S(2)}) collective-permute-start(bf16[320,384]{1,0:T(8,128)(2,1)} %get-tuple-element.11), channel_id=1, source_target_pairs={{0,0},{1,8},{4,4},{5,12},{8,1},{9,9},{12,5},{13,13},{2,2},{3,10},{... | collective-permute-start | bytes 737288 | tf_op jit(solution)/shard_map/ppermute | solution.py:242
  8.5 12.0 %collective-permute-start.1 = (bf16[320,384]{1,0:T(8,128)(2,1)}, bf16[320,384]{1,0:T(8,128)(2,1)S(1)}, u32[]{:S(2)}, u32[]{:S(2)}) collective-permute-start(bf16[320,384]{1,0:T(8,128)(2,1)} %get-tuple-element.12), channel_id=1, source_target_pairs={{0,4},{1,12},{4,0},{5,8},{8,5},{9,13},{12,1},{13,9},{2,6},{3,14},{... | collective-permute-start | bytes 737288 | tf_op jit(solution)/shard_map/ppermute | solution.py:242
  9.9 9.3 %collective-permute-start.2 = (bf16[160,384]{1,0:T(8,128)(2,1)}, bf16[160,384]{1,0:T(8,128)(2,1)S(1)}, u32[]{:S(2)}, u32[]{:S(2)}) collective-permute-start(bf16[160,384]{1,0:T(8,128)(2,1)} %get-tuple-element.13), channel_id=1, source_target_pairs={{0,1},{1,9},{4,5},{5,13},{8,0},{9,8},{12,4},{13,12},{2,3},{3,11},{... | collective-permute-start | bytes 368648 | tf_op jit(solution)/shard_map/ppermute | solution.py:242
  9.9 10.6 %collective-permute-start.3 = (bf16[160,384]{1,0:T(8,128)(2,1)}, bf16[160,384]{1,0:T(8,128)(2,1)S(1)}, u32[]{:S(2)}, u32[]{:S(2)}) collective-permute-start(bf16[160,384]{1,0:T(8,128)(2,1)} %get-tuple-element.14), channel_id=1, source_target_pairs={{0,5},{1,13},{4,1},{5,9},{8,4},{9,12},{12,0},{13,8},{2,7},{3,15},{... | collective-permute-start | bytes 368648 | tf_op jit(solution)/shard_map/ppermute | solution.py:242
  20.6 6.3 %collective-permute-start.4 = (bf16[640,384]{1,0:T(8,128)(2,1)S(1)}, bf16[640,384]{1,0:T(8,128)(2,1)S(1)}, u32[]{:S(2)}, u32[]{:S(2)}) collective-permute-start(bf16[640,384]{1,0:T(8,128)(2,1)S(1)} %shard_map.96), channel_id=1, source_target_pairs={{0,1},{1,0},{2,3},{3,2},{4,5},{5,4},{6,7},{7,6},{8,9},{9,8},{10,11... | collective-permute-start | bytes 1474568 | tf_op jit(solution)/shard_map/ppermute | solution.py:244
  49.7 13.9 %copy-start.4 = (s32[4]{0:T(128)S(1)}, s32[4]{0:T(128)}, u32[]{:S(2)}) copy-start(s32[4]{0:T(128)} %param.15) | copy-start | bytes 52
  49.7 18.6 %copy-start.1 = (f32[4,160,1280]{2,1,0:T(8,128)S(1)}, f32[4,160,1280]{2,1,0:T(8,128)}, u32[]{:S(2)}) copy-start(f32[4,160,1280]{2,1,0:T(8,128)} %param.14) | copy-start | bytes 9830404
  50.7 26.3 %copy-start.2 = (f32[160,1280]{1,0:T(8,128)S(1)}, f32[160,1280]{1,0:T(8,128)}, u32[]{:S(2)}) copy-start(f32[160,1280]{1,0:T(8,128)} %param.13) | copy-start | bytes 2457604
  50.7 26.3 %copy-start.3 = (f32[1280]{0:T(1024)S(1)}, f32[1280]{0:T(1024)}, u32[]{:S(2)}) copy-start(f32[1280]{0:T(1024)} %param.12) | copy-start | bytes 15364
  50.7 6.0 %collective-permute-start.8 = (bf16[160,768]{1,0:T(8,128)(2,1)S(1)}, bf16[160,768]{1,0:T(8,128)(2,1)S(1)}, u32[]{:S(2)}, u32[]{:S(2)}) collective-permute-start(bf16[160,768]{1,0:T(8,128)(2,1)S(1)} %get-tuple-element.19), channel_id=1, source_target_pairs={{0,2},{2,0},{1,3},{3,1},{4,6},{6,4},{5,7},{7,5},{8,10},{10,8},{9,1... | collective-permute-start | bytes 737288 | tf_op jit(solution)/shard_map/ppermute | solution.py:274
  52.0 11.6 %collective-permute-start.6 = (bf16[160,512]{1,0:T(8,128)(2,1)S(1)}, bf16[160,512]{1,0:T(8,128)(2,1)S(1)}, u32[]{:S(2)}, u32[]{:S(2)}) collective-permute-start(bf16[160,512]{1,0:T(8,128)(2,1)S(1)} %get-tuple-element.16), channel_id=1, source_target_pairs={{0,2},{2,0},{1,3},{3,1},{4,6},{6,4},{5,7},{7,5},{8,10},{10,8},{9,1... | collective-permute-start | bytes 491528 | tf_op jit(solution)/shard_map/ppermute | solution.py:274
  56.8 20.2 %collective-permute-start.9 = (bf16[160,768]{1,0:T(8,128)(2,1)S(1)}, bf16[160,768]{1,0:T(8,128)(2,1)S(1)}, u32[]{:S(2)}, u32[]{:S(2)}) collective-permute-start(bf16[160,768]{1,0:T(8,128)(2,1)S(1)} %shard_map.101), channel_id=1, source_target_pairs={{0,0},{1,8},{2,4},{3,12},{4,1},{5,9},{6,5},{7,13},{8,2},{9,10},{10... | collective-permute-start | bytes 737288 | tf_op jit(solution)/shard_map/ppermute | solution.py:276
  63.7 13.3 %collective-permute-start.7 = (bf16[160,512]{1,0:T(8,128)(2,1)S(1)}, bf16[160,512]{1,0:T(8,128)(2,1)S(1)}, u32[]{:S(2)}, u32[]{:S(2)}) collective-permute-start(bf16[160,512]{1,0:T(8,128)(2,1)S(1)} %shard_map.99), channel_id=1, source_target_pairs={{0,0},{1,8},{2,4},{3,12},{4,1},{5,9},{6,5},{7,13},{8,2},{9,10},{10... | collective-permute-start | bytes 491528 | tf_op jit(solution)/shard_map/ppermute | solution.py:276

commit v5 on v4

--- a/solution.py
+++ b/solution.py
@@ -1,5 +1,3 @@
-import functools
-
 import jax
 import jax.numpy as jnp
 from jax import lax
@@ -129,9 +127,9 @@
 
 
 def attention_kernel(*refs):
-    blocks, sibling, out = refs[:4], refs[4], refs[5]
-    key_all, value_all, query_all = refs[6:]
-    rows = query_all.shape[0] // 2
+    blocks, sibling = refs[:4], refs[4]
+    sent, kept, key_all, value_all, query_all = refs[5:]
+    rows = sent.shape[0]
     half = rows // 2
     for k in range(4):
         here, there = slice(k * half, (k + 1) * half), slice((4 + k) * half, (5 + k) * half)
@@ -140,10 +138,15 @@
         key_all[there, :] = sibling[k * rows : k * rows + half, :]
         value_all[there, :] = sibling[k * rows + half : (k + 1) * rows, :]
     _, zl = bits()
+    x = lax.axis_index("wt")
     for k in range(2):
-        at = pl.ds(pl.multiple_of(flip(zl, k) * rows, 16), rows)
-        query_all[at, :] = blocks[k][rows:, :]
-    for h in range(out.shape[1] // HEAD_DIM):
+        for part in range(2):
+            at = rows + flip(x, part == 0) * half
+            to = (part * 2 + flip(zl, k)) * half
+            query_all[pl.ds(pl.multiple_of(to, 16), half), :] = blocks[k][
+                pl.ds(pl.multiple_of(at, 16), half), :
+            ]
+    for h in range(sent.shape[1] // HEAD_DIM):
         columns = slice(h * HEAD_DIM, (h + 1) * HEAD_DIM)
         scores = lax.dot_general(
             query_all[:, columns],
@@ -157,39 +160,47 @@
         result = jnp.dot(
             weights.astype(jnp.bfloat16), value_all[:, columns], preferred_element_type=jnp.float32
         )
-        out[:, columns] = (result / total).astype(out.dtype)
-
-
-def project_kernel(first, gathered, weight, weight_c, keep, send):
-    rows, count = keep.shape
-    core, x = lax.axis_index("head"), lax.axis_index("wt")
-    columns = slice(first, first + count)
+        result = (result / total).astype(sent.dtype)
+        sent[:, columns] = result[:rows]
+        kept[:, columns] = result[rows:]
+
+
+def multiply(gathered, weight, weight_c):
+    rows = gathered.shape[0] // 4
+    core = lax.axis_index("head")
     total = None
     for other, block in enumerate((weight, weight_c)):
-        start = 2 * flip(core, other) * 2 * rows
+        start = 2 * flip(core, other) * rows
         left = jnp.concatenate(
             [
-                gathered[pl.ds(pl.multiple_of(start + low * 2 * rows, 16), 2 * rows), :]
+                gathered[pl.ds(pl.multiple_of(start + low * rows, 16), rows), :]
                 for low in range(2)
             ],
             axis=1,
         )
-        term = jnp.dot(left, block[:, columns], preferred_element_type=jnp.float32)
+        term = jnp.dot(left, block[...], preferred_element_type=jnp.float32)
         total = term if total is None else total + term
+    return total
+
+
+def sent_kernel(gathered, weight, weight_c, out):
+    out[...] = multiply(gathered, weight, weight_c).astype(out.dtype)
+
+
+def kept_kernel(gathered, weight, weight_c, arrived, out0, out1):
+    total = multiply(gathered, weight, weight_c) + arrived[...].astype(jnp.float32)
+    half = out0.shape[0]
+    x = lax.axis_index("wt")
     for low in range(2):
-        part = total[low * rows : (low + 1) * rows]
+        part = total[low * half : (low + 1) * half].astype(out0.dtype)
 
         @pl.when(x == low)
         def _():
-            keep[...] = part
+            out0[...] = part
 
         @pl.when(x != low)
         def _():
-            send[...] = part.astype(send.dtype)
-
-
-def add_kernel(keep, arrived, out):
-    out[...] = (keep[...] + arrived[...].astype(jnp.float32)).astype(out.dtype)
+            out1[...] = part
 
 
 def call(kernel, args, outs, scratch=(), far_in=False, flops=0, vmem=VMEM_BYTES):
@@ -221,7 +232,8 @@
     swap = [(0, 1), (1, 0)]
     bf16 = jnp.bfloat16
 
-    weight_c = lax.ppermute(out_weight, "head", swap)
+    half = rows // 2
+    zl = lax.axis_index("seq") % 2
 
     packed = call(
         pack_kernel,
@@ -242,10 +254,12 @@
         moved.append(lax.ppermute(packed[k], ("seq", "head"), pairs))
     (joined,) = call(join_kernel, moved, [((4 * rows, width), bf16)])
     sibling = lax.ppermute(joined, "head", swap)
-    (attention_out,) = call(
+    late_weight, _ = lax.optimization_barrier((out_weight, sibling))
+    weight_c = lax.ppermute(late_weight, "head", swap)
+    sent_rows, kept_rows = call(
         attention_kernel,
         moved + [sibling],
-        [((2 * rows, width), bf16)],
+        [((rows, width), bf16)] * 2,
         [
             pltpu.VMEM((4 * rows, width), bf16),
             pltpu.VMEM((4 * rows, width), bf16),
@@ -253,28 +267,38 @@
         ],
         flops=4 * (2 * rows) * (4 * rows) * width,
     )
-    gathered = lax.all_gather(attention_out, "seq", axis=0, tiled=True)
-
-    pairs = []
-    for zz in range(4):
-        for xx in range(2):
-            for cc in range(2):
-                to = ((2 * cc + xx) * 2 + zz // 2) * 2 + zz % 2
-                pairs.append(((zz * 2 + xx) * 2 + cc, to))
-    cut = columns * 2 // 5 // 256 * 256
+
+    flops = 4 * rows * depth * columns
+    gathered = lax.all_gather(sent_rows, "seq", axis=0, tiled=True)
+    (send,) = call(
+        sent_kernel, (gathered, out_weight, weight_c), [((rows, columns), bf16)], flops=flops
+    )
+    arrived = lax.ppermute(send, "wt", swap)
+    kept_rows, _ = lax.optimization_barrier((kept_rows, send))
+    gathered = lax.all_gather(kept_rows, "seq", axis=0, tiled=True)
+    sums = call(
+        kept_kernel,
+        (gathered, out_weight, weight_c, arrived),
+        [((half, columns), bf16)] * 2,
+        flops=flops,
+    )
+
     owned = []
-    for first, count in ((0, cut), (cut, columns - cut)):
-        keep, send = call(
-            functools.partial(project_kernel, first),
-            (gathered, out_weight, weight_c),
-            [((rows, count), jnp.float32), ((rows, count), bf16)],
-            flops=4 * (2 * rows) * depth * count,
-        )
-        gathered, _ = lax.optimization_barrier((gathered, send))
-        arrived = lax.ppermute(send, "wt", swap)
-        (summed,) = call(add_kernel, (keep, arrived), [((rows, count), bf16)])
-        owned.append(lax.ppermute(summed, ("seq", "wt", "head"), pairs))
-    head_total = jnp.concatenate(owned, axis=1).astype(jnp.float32)
+    for p, part in enumerate(sums):
+        pairs = []
+        for zz in range(4):
+            for xx in range(2):
+                for cc in range(2):
+                    to = ((2 * cc + (p ^ xx)) * 2 + zz // 2) * 2 + zz % 2
+                    pairs.append(((zz * 2 + xx) * 2 + cc, to))
+        owned.append(lax.ppermute(part, ("seq", "wt", "head"), pairs))
+    head_total = jnp.concatenate(
+        [
+            jnp.where(zl == 0, owned[0], owned[1]),
+            jnp.where(zl == 0, owned[1], owned[0]),
+        ],
+        axis=0,
+    ).astype(jnp.float32)
     kept_deltas = jnp.sum(skip_flags.astype(jnp.float32)[:, None, None] * cached_deltas, axis=0)
     resting = hidden_state + kept_deltas
     fresh_delta = head_total * gate_values[None, :]
@@ -297,7 +321,7 @@
     def local(*args):
         sizes = tuple(mesh.shape[name] for name in ("seq", "wt", "head"))
         rows, features = args[0].shape
-        if sizes == (4, 2, 2) and rows % 32 == 0 and features % (2 * HEAD_DIM) == 0 and args[3].shape[1] % 256 == 0 and args[3].shape[1] >= 640:
+        if sizes == (4, 2, 2) and rows % 32 == 0 and features % (2 * HEAD_DIM) == 0:
             return local_heads(*args)
         return local_general(*args)
 

time: 78.6 us -> 80 us (1.018)
  the two profiles are of different devices: /device:TPU:1 before, /device:TPU:2 now
where the time goes in v5:
time: 80 us; the launch traced here: 79.2 us
  blocking collectives  31.3 us (39%)
  waiting for transfers between devices  27 us (34%)
  starting transfers between devices  10 us (12%)
  Pallas kernels  5.56 us (7%)
  local copies, waits for them, and re-layouts  2.87 us (4%)
  other arithmetic  1.63 us (2%)
    all_gather x1, blocking collectives, local_heads(): gathered = lax.all_gather(sent_rows, 'seq', axis=0, tiled=True)  16.5 us
    all_gather x1, blocking collectives, local_heads(): gathered = lax.all_gather(kept_rows, 'seq', axis=0, tiled=True)  14.8 us
    ppermute x4, waiting for transfers between devices, local_heads(): moved.append(lax.ppermute(packed[k], ('seq', 'head'), pairs))  14.8 us
    ppermute x2, waiting for transfers between devices, local_heads(): owned.append(lax.ppermute(part, ('seq', 'wt', 'head'), pairs))  10.4 us
    ppermute x4, starting transfers between devices, local_heads(): moved.append(lax.ppermute(packed[k], ('seq', 'head'), pairs))  6.01 us
    pallas_call x5, Pallas kernels, call(): pl.pallas_call(kernel, in_specs=[pl.BlockSpec(memory_space=place)] * len(...  5.56 us
    ppermute x2, starting transfers between devices, local_heads(): owned.append(lax.ppermute(part, ('seq', 'wt', 'head'), pairs))  3.25 us
    unnamed x14, local copies, waits for them, and re-layouts  2.87 us
  transfers between devices with their start and end apart: 9, of which 4 were waited for; matrix products, arithmetic and copies ran while one was open for 0% of the time, Pallas kernels for 2%

profile of v5, /device:TPU:2, one launch (start us, length us, event | category | flops | bytes accessed | tf_op | source)
XLA Modules:
  0.0 79.2 jit_solution(7351042959678639768)
XLA Ops:
  0.6 0.0 copy-start
  0.6 2.2 %shard_map.95 = (bf16[320,384]{1,0:T(8,128)(2,1)}, bf16[320,384]{1,0:T(8,128)(2,1)}, bf16[160,384]{1,0:T(8,128)(2,1)}, bf16[160,384]{1,0:T(8,128)(2,1)}) custom-call(bf16[160,768]{1,0:T(8,128)(2,1)} %queries.1, bf16[160,768]{1,0:T(8,128)(2,1)} %keys.1, bf16[160,768]{1,0:T(8,128)(2,1)} %values.1), custom_call_target="tpu_custom_call" | custom-call | tf_op jit(solution)/shard_map/pallas_call | solution.py:208
  2.9 1.6 %collective-permute-start = (bf16[320,384]{1,0:T(8,128)(2,1)}, bf16[320,384]{1,0:T(8,128)(2,1)S(1)}, u32[]{:S(2)}, u32[]{:S(2)}) collective-permute-start(bf16[320,384]{1,0:T(8,128)(2,1)} %get-tuple-element.12), channel_id=1, source_target_pairs={{0,0},{1,8},{4,4},{5,12},{8,1},{9,9},{12,5},{13,13},{2,2},{3,10},{... | collective-permute-start | bytes 737288 | tf_op jit(solution)/shard_map/ppermute | solution.py:254
  4.5 1.6 %collective-permute-start.1 = (bf16[320,384]{1,0:T(8,128)(2,1)}, bf16[320,384]{1,0:T(8,128)(2,1)S(1)}, u32[]{:S(2)}, u32[]{:S(2)}) collective-permute-start(bf16[320,384]{1,0:T(8,128)(2,1)} %get-tuple-element.13), channel_id=1, source_target_pairs={{0,4},{1,12},{4,0},{5,8},{8,5},{9,13},{12,1},{13,9},{2,6},{3,14},{... | collective-permute-start | bytes 737288 | tf_op jit(solution)/shard_map/ppermute | solution.py:254
  6.0 2.5 %collective-permute-start.2 = (bf16[160,384]{1,0:T(8,128)(2,1)}, bf16[160,384]{1,0:T(8,128)(2,1)S(1)}, u32[]{:S(2)}, u32[]{:S(2)}) collective-permute-start(bf16[160,384]{1,0:T(8,128)(2,1)} %get-tuple-element.14), channel_id=1, source_target_pairs={{0,1},{1,9},{4,5},{5,13},{8,0},{9,8},{12,4},{13,12},{2,3},{3,11},{... | collective-permute-start | bytes 368648 | tf_op jit(solution)/shard_map/ppermute | solution.py:254
  8.6 0.3 collective-permute-start.3
  8.9 14.8 %collective-permute-done.2.refs_2_ = bf16[160,384]{1,0:T(8,128)(2,1)S(1)} collective-permute-done((bf16[160,384]{1,0:T(8,128)(2,1)}, bf16[160,384]{1,0:T(8,128)(2,1)S(1)}, u32[]{:S(2)}, u32[]{:S(2)}) %collective-permute-start.2) | collective-permute-done | bytes 122912 | tf_op jit(solution)/shard_map/ppermute | solution.py:254
  23.6 0.0 collective-permute-done.3.refs_3_
  23.6 0.0 collective-permute-done.refs_0_
  23.6 0.0 collective-permute-done.1.refs_1_
  23.7 0.0 copy-start.6
  23.7 0.1 collective-permute-start.4
  23.8 1.9 %collective-permute-done.4.refs_4_ = bf16[640,384]{1,0:T(8,128)(2,1)S(1)} collective-permute-done((bf16[640,384]{1,0:T(8,128)(2,1)S(1)}, bf16[640,384]{1,0:T(8,128)(2,1)S(1)}, u32[]{:S(2)}, u32[]{:S(2)}) %collective-permute-start.4) | collective-permute-done | bytes 491552 | tf_op jit(solution)/shard_map/ppermute | solution.py:256
  25.6 0.1 collective-permute-start.5
  25.8 1.6 %shard_map.97 = (bf16[160,384]{1,0:T(8,128)(2,1)S(1)}, bf16[160,384]{1,0:T(8,128)(2,1)S(1)}) custom-call(bf16[320,384]{1,0:T(8,128)(2,1)S(1)} %collective-permute-done.refs_0_, bf16[320,384]{1,0:T(8,128)(2,1)S(1)} %collective-permute-done.1.refs_1_, bf16[160,384]{1,0:T(8,128)(2,1)S(1)} %collective-permute-done.2.refs_2_, ...), custom_call_target="tpu_custom_call" | custom-call | flops 314572800 | tf_op jit(solution)/shard_map/pallas_call | solution.py:208
  27.4 16.5 %all_gather.6.gathered = bf16[640,384]{1,0:T(8,128)(2,1)S(1)} all-gather(bf16[160,384]{1,0:T(8,128)(2,1)S(1)} %get-tuple-element.17), channel_id=1, replica_groups=mesh['groups'=2,'seq'=4,'wt'=2,'head'=2] {'seq'}, dimensions={0}, use_global_device_ids=true | all-gather | bytes 614400 | tf_op jit(solution)/shard_map/all_gather | solution.py:272
  44.0 0.0 collective-permute-done.5.weight_c
  44.0 0.0 copy-done
  44.0 0.8 %shard_map.98 = bf16[160,1280]{1,0:T(8,128)(2,1)S(1)} custom-call(bf16[640,384]{1,0:T(8,128)(2,1)S(1)} %all_gather.6.gathered, bf16[768,1280]{1,0:T(8,128)(2,1)S(1)} %copy-done, bf16[768,1280]{1,0:T(8,128)(2,1)S(1)} %collective-permute-done.5.weight_c), custom_call_target="tpu_custom_call" | custom-call | flops 629145600 | tf_op jit(solution)/shard_map/pallas_call | solution.py:208
  44.8 0.0 copy-start.1
  44.8 1.3 %copy-done.1 = bf16[768,1280]{1,0:T(8,128)(2,1)} copy-done((bf16[768,1280]{1,0:T(8,128)(2,1)}, bf16[768,1280]{1,0:T(8,128)(2,1)S(1)}, u32[]{:S(2)}) %copy-start.1) | copy-done | bytes 1966104
  46.1 0.5 collective-permute-start.6
  46.6 0.0 copy-done.6
  46.6 14.8 %all_gather.7.gathered = bf16[640,384]{1,0:T(8,128)(2,1)S(1)} all-gather(bf16[160,384]{1,0:T(8,128)(2,1)S(1)} %get-tuple-element.19), channel_id=1, replica_groups=mesh['groups'=2,'seq'=4,'wt'=2,'head'=2] {'seq'}, dimensions={0}, use_global_device_ids=true | all-gather | bytes 614400 | tf_op jit(solution)/shard_map/all_gather | solution.py:278
  61.4 0.0 collective-permute-done.6.arrived
  61.4 0.0 copy-start.2
  61.4 1.5 %copy-done.2 = bf16[768,1280]{1,0:T(8,128)(2,1)S(1)} copy-done((bf16[768,1280]{1,0:T(8,128)(2,1)S(1)}, bf16[768,1280]{1,0:T(8,128)(2,1)}, u32[]{:S(2)}) %copy-start.2) | copy-done | bytes 1966104
  63.0 0.0 copy-start.3
  63.0 0.9 %shard_map.99 = (bf16[80,1280]{1,0:T(8,128)(2,1)S(1)}, bf16[80,1280]{1,0:T(8,128)(2,1)S(1)}) custom-call(bf16[640,384]{1,0:T(8,128)(2,1)S(1)} %all_gather.7.gathered, bf16[768,1280]{1,0:T(8,128)(2,1)S(1)} %copy-done, bf16[768,1280]{1,0:T(8,128)(2,1)S(1)} %copy-done.2, bf16[160,1280]{1,0:T(8,128)(2,1)S(1)} %collective-permute-done.6.arrived), custom_call_target="tpu_custom_call" | custom-call | flops 629145600 | tf_op jit(solution)/shard_map/pallas_call | solution.py:208
  63.8 0.0 copy-start.4
  63.9 0.0 copy-start.5
  63.9 3.2 %collective-permute-start.7 = (bf16[80,1280]{1,0:T(8,128)(2,1)S(1)}, bf16[80,1280]{1,0:T(8,128)(2,1)S(1)}, u32[]{:S(2)}, u32[]{:S(2)}) collective-permute-start(bf16[80,1280]{1,0:T(8,128)(2,1)S(1)} %get-tuple-element.20), channel_id=1, source_target_pairs={{0,0},{1,8},{2,4},{3,12},{4,1},{5,9},{6,5},{7,13},{8,2},{9,10},{10... | collective-permute-start | bytes 614408 | tf_op jit(solution)/shard_map/ppermute | solution.py:294
  67.1 0.1 collective-permute-start.8
  67.1 0.0 copy-done.3
  67.1 0.3 multiply_reduce_fusion
  67.4 9.8 %collective-permute-done.7 = bf16[80,1280]{1,0:T(8,128)(2,1)S(1)} collective-permute-done((bf16[80,1280]{1,0:T(8,128)(2,1)S(1)}, bf16[80,1280]{1,0:T(8,128)(2,1)S(1)}, u32[]{:S(2)}, u32[]{:S(2)}) %collective-permute-start.7) | collective-permute-done | bytes 204832 | tf_op jit(solution)/shard_map/ppermute | solution.py:294
  77.2 0.6 collective-permute-done.8
  77.9 0.0 copy-done.4
  77.9 0.0 copy-done.5
  77.9 1.3 %add_add_fusion = (f32[160,1280]{1,0:T(8,128)}, f32[160,1280]{1,0:T(8,128)}) fusion(f32[160,1280]{1,0:T(8,128)S(1)} %copy-done.4, f32[160,1280]{1,0:T(8,128)S(1)} %multiply_reduce_fusion, f32[1280]{0:T(1024)S(1)} %copy-done.5, bf16[80,1280]{1,0:T(8,128)(2,1)S(1)} %get-tuple-element.25, bf16[80,1280]{1,0:T(8,128)(2,1)S(1)} %get-tuple-element.24), kind=kLoop, calls=%fused_computation.2 | loop fusion | flops 1433600 | bytes 3691520 | tf_op jit(solution)/shard_map/add | solution.py:305
  (3 shorter events, 0.1 us)
Async XLA Ops:
  0.6 43.3 %copy-start = (bf16[768,1280]{1,0:T(8,128)(2,1)S(1)}, bf16[768,1280]{1,0:T(8,128)(2,1)}, u32[]{:S(2)}) copy-start(bf16[768,1280]{1,0:T(8,128)(2,1)} %weight.3) | copy-start | bytes 5898244
  2.9 20.8 %collective-permute-start = (bf16[320,384]{1,0:T(8,128)(2,1)}, bf16[320,384]{1,0:T(8,128)(2,1)S(1)}, u32[]{:S(2)}, u32[]{:S(2)}) collective-permute-start(bf16[320,384]{1,0:T(8,128)(2,1)} %get-tuple-element.12), channel_id=1, source_target_pairs={{0,0},{1,8},{4,4},{5,12},{8,1},{9,9},{12,5},{13,13},{2,2},{3,10},{... | collective-permute-start | bytes 737288 | tf_op jit(solution)/shard_map/ppermute | solution.py:254
  4.5 19.2 %collective-permute-start.1 = (bf16[320,384]{1,0:T(8,128)(2,1)}, bf16[320,384]{1,0:T(8,128)(2,1)S(1)}, u32[]{:S(2)}, u32[]{:S(2)}) collective-permute-start(bf16[320,384]{1,0:T(8,128)(2,1)} %get-tuple-element.13), channel_id=1, source_target_pairs={{0,4},{1,12},{4,0},{5,8},{8,5},{9,13},{12,1},{13,9},{2,6},{3,14},{... | collective-permute-start | bytes 737288 | tf_op jit(solution)/shard_map/ppermute | solution.py:254
  6.0 17.6 %collective-permute-start.2 = (bf16[160,384]{1,0:T(8,128)(2,1)}, bf16[160,384]{1,0:T(8,128)(2,1)S(1)}, u32[]{:S(2)}, u32[]{:S(2)}) collective-permute-start(bf16[160,384]{1,0:T(8,128)(2,1)} %get-tuple-element.14), channel_id=1, source_target_pairs={{0,1},{1,9},{4,5},{5,13},{8,0},{9,8},{12,4},{13,12},{2,3},{3,11},{... | collective-permute-start | bytes 368648 | tf_op jit(solution)/shard_map/ppermute | solution.py:254
  8.6 15.1 %collective-permute-start.3 = (bf16[160,384]{1,0:T(8,128)(2,1)}, bf16[160,384]{1,0:T(8,128)(2,1)S(1)}, u32[]{:S(2)}, u32[]{:S(2)}) collective-permute-start(bf16[160,384]{1,0:T(8,128)(2,1)} %get-tuple-element.15), channel_id=1, source_target_pairs={{0,5},{1,13},{4,1},{5,9},{8,4},{9,12},{12,0},{13,8},{2,7},{3,15},{... | collective-permute-start | bytes 368648 | tf_op jit(solution)/shard_map/ppermute | solution.py:254
  23.7 22.9 %copy-start.6 = (s32[4]{0:T(128)S(1)}, s32[4]{0:T(128)}, u32[]{:S(2)}) copy-start(s32[4]{0:T(128)} %param.15) | copy-start | bytes 52
  23.7 1.9 %collective-permute-start.4 = (bf16[640,384]{1,0:T(8,128)(2,1)S(1)}, bf16[640,384]{1,0:T(8,128)(2,1)S(1)}, u32[]{:S(2)}, u32[]{:S(2)}) collective-permute-start(bf16[640,384]{1,0:T(8,128)(2,1)S(1)} %shard_map.96), channel_id=1, source_target_pairs={{0,1},{1,0},{2,3},{3,2},{4,5},{5,4},{6,7},{7,6},{8,9},{9,8},{10,11... | collective-permute-start | bytes 1474568 | tf_op jit(solution)/shard_map/ppermute | solution.py:256
  25.6 18.3 %collective-permute-start.5 = (bf16[768,1280]{1,0:T(8,128)(2,1)}, bf16[768,1280]{1,0:T(8,128)(2,1)S(1)}, u32[]{:S(2)}, u32[]{:S(2)}) collective-permute-start(bf16[768,1280]{1,0:T(8,128)(2,1)} %weight.3), channel_id=1, source_target_pairs={{0,1},{1,0},{2,3},{3,2},{4,5},{5,4},{6,7},{7,6},{8,9},{9,8},{10,11... | collective-permute-start | bytes 5898248 | tf_op jit(solution)/shard_map/ppermute | solution.py:258
  44.8 1.3 %copy-start.1 = (bf16[768,1280]{1,0:T(8,128)(2,1)}, bf16[768,1280]{1,0:T(8,128)(2,1)S(1)}, u32[]{:S(2)}) copy-start(bf16[768,1280]{1,0:T(8,128)(2,1)S(1)} %collective-permute-done.5.weight_c) | copy-start | bytes 5898244
  46.1 15.3 %collective-permute-start.6 = (bf16[160,1280]{1,0:T(8,128)(2,1)S(1)}, bf16[160,1280]{1,0:T(8,128)(2,1)S(1)}, u32[]{:S(2)}, u32[]{:S(2)}) collective-permute-start(bf16[160,1280]{1,0:T(8,128)(2,1)S(1)} %shard_map.98), channel_id=1, source_target_pairs={{0,2},{2,0},{1,3},{3,1},{4,6},{6,4},{5,7},{7,5},{8,10},{10,8},{9,1... | collective-permute-start | bytes 1228808 | tf_op jit(solution)/shard_map/ppermute | solution.py:276
  61.4 1.5 %copy-start.2 = (bf16[768,1280]{1,0:T(8,128)(2,1)S(1)}, bf16[768,1280]{1,0:T(8,128)(2,1)}, u32[]{:S(2)}) copy-start(bf16[768,1280]{1,0:T(8,128)(2,1)} %copy-done.1) | copy-start | bytes 5898244
  63.0 4.2 %copy-start.3 = (f32[4,160,1280]{2,1,0:T(8,128)S(1)}, f32[4,160,1280]{2,1,0:T(8,128)}, u32[]{:S(2)}) copy-start(f32[4,160,1280]{2,1,0:T(8,128)} %param.14) | copy-start | bytes 9830404
  63.8 14.0 %copy-start.4 = (f32[160,1280]{1,0:T(8,128)S(1)}, f32[160,1280]{1,0:T(8,128)}, u32[]{:S(2)}) copy-start(f32[160,1280]{1,0:T(8,128)} %param.13) | copy-start | bytes 2457604
  63.9 14.0 %copy-start.5 = (f32[1280]{0:T(1024)S(1)}, f32[1280]{0:T(1024)}, u32[]{:S(2)}) copy-start(f32[1280]{0:T(1024)} %param.12) | copy-start | bytes 15364
  63.9 13.3 %collective-permute-start.7 = (bf16[80,1280]{1,0:T(8,128)(2,1)S(1)}, bf16[80,1280]{1,0:T(8,128)(2,1)S(1)}, u32[]{:S(2)}, u32[]{:S(2)}) collective-permute-start(bf16[80,1280]{1,0:T(8,128)(2,1)S(1)} %get-tuple-element.20), channel_id=1, source_target_pairs={{0,0},{1,8},{2,4},{3,12},{4,1},{5,9},{6,5},{7,13},{8,2},{9,10},{10... | collective-permute-start | bytes 614408 | tf_op jit(solution)/shard_map/ppermute | solution.py:294
  67.1 10.8 %collective-permute-start.8 = (bf16[80,1280]{1,0:T(8,128)(2,1)S(1)}, bf16[80,1280]{1,0:T(8,128)(2,1)S(1)}, u32[]{:S(2)}, u32[]{:S(2)}) collective-permute-start(bf16[80,1280]{1,0:T(8,128)(2,1)S(1)} %get-tuple-element.21), channel_id=1, source_target_pairs={{0,4},{1,12},{2,0},{3,8},{4,5},{5,13},{6,1},{7,9},{8,6},{9,14},{10... | collective-permute-start | bytes 614408 | tf_op jit(solution)/shard_map/ppermute | solution.py:294

commit v6 on v5

--- a/solution.py
+++ b/solution.py
@@ -1,3 +1,5 @@
+import functools
+
 import jax
 import jax.numpy as jnp
 from jax import lax
@@ -126,10 +128,10 @@
         joined[k * rows : (k + 1) * rows, :] = block[:rows, :]
 
 
-def attention_kernel(*refs):
+def attention_kernel(part, *refs):
     blocks, sibling = refs[:4], refs[4]
-    sent, kept, key_all, value_all, query_all = refs[5:]
-    rows = sent.shape[0]
+    out, key_all, value_all, query_all = refs[5:]
+    rows = out.shape[0]
     half = rows // 2
     for k in range(4):
         here, there = slice(k * half, (k + 1) * half), slice((4 + k) * half, (5 + k) * half)
@@ -138,15 +140,12 @@
         key_all[there, :] = sibling[k * rows : k * rows + half, :]
         value_all[there, :] = sibling[k * rows + half : (k + 1) * rows, :]
     _, zl = bits()
-    x = lax.axis_index("wt")
+    start = rows + flip(lax.axis_index("wt"), part == 0) * half
     for k in range(2):
-        for part in range(2):
-            at = rows + flip(x, part == 0) * half
-            to = (part * 2 + flip(zl, k)) * half
-            query_all[pl.ds(pl.multiple_of(to, 16), half), :] = blocks[k][
-                pl.ds(pl.multiple_of(at, 16), half), :
-            ]
-    for h in range(sent.shape[1] // HEAD_DIM):
+        query_all[pl.ds(pl.multiple_of(flip(zl, k) * half, 16), half), :] = blocks[k][
+            pl.ds(pl.multiple_of(start, 16), half), :
+        ]
+    for h in range(out.shape[1] // HEAD_DIM):
         columns = slice(h * HEAD_DIM, (h + 1) * HEAD_DIM)
         scores = lax.dot_general(
             query_all[:, columns],
@@ -160,35 +159,32 @@
         result = jnp.dot(
             weights.astype(jnp.bfloat16), value_all[:, columns], preferred_element_type=jnp.float32
         )
-        result = (result / total).astype(sent.dtype)
-        sent[:, columns] = result[:rows]
-        kept[:, columns] = result[rows:]
-
-
-def multiply(gathered, weight, weight_c):
-    rows = gathered.shape[0] // 4
+        out[:, columns] = (result / total).astype(out.dtype)
+
+
+def multiply(shards, weight, weight_c, held):
+    zh, zl = bits()
     core = lax.axis_index("head")
+    for m in range(3):
+        held[m] = shards[m][...]
+    held[3] = jnp.where(zh == zl, shards[4][...], shards[3][...])
     total = None
     for other, block in enumerate((weight, weight_c)):
-        start = 2 * flip(core, other) * rows
-        left = jnp.concatenate(
-            [
-                gathered[pl.ds(pl.multiple_of(start + low * rows, 16), rows), :]
-                for low in range(2)
-            ],
-            axis=1,
-        )
+        high = 2 * jnp.where(flip(core, other) == zh, 0, 1)
+        left = jnp.concatenate([held[high + zl], held[high + 1 - zl]], axis=1)
         term = jnp.dot(left, block[...], preferred_element_type=jnp.float32)
         total = term if total is None else total + term
     return total
 
 
-def sent_kernel(gathered, weight, weight_c, out):
-    out[...] = multiply(gathered, weight, weight_c).astype(out.dtype)
-
-
-def kept_kernel(gathered, weight, weight_c, arrived, out0, out1):
-    total = multiply(gathered, weight, weight_c) + arrived[...].astype(jnp.float32)
+def sent_kernel(*refs):
+    shards, (weight, weight_c, out, held) = refs[:5], refs[5:]
+    out[...] = multiply(shards, weight, weight_c, held).astype(out.dtype)
+
+
+def kept_kernel(*refs):
+    shards, (weight, weight_c, arrived, out0, out1, held) = refs[:5], refs[5:]
+    total = multiply(shards, weight, weight_c, held) + arrived[...].astype(jnp.float32)
     half = out0.shape[0]
     x = lax.axis_index("wt")
     for low in range(2):
@@ -201,6 +197,15 @@
         @pl.when(x != low)
         def _():
             out1[...] = part
+
+
+def gather(shard, *ahead):
+    near = lax.ppermute(shard, "seq", [(0, 1), (1, 0), (2, 3), (3, 2)])
+    two = lax.ppermute(shard, "seq", [(0, 2), (2, 0), (1, 3), (3, 1)])
+    late_shard, late_two = lax.optimization_barrier((shard, two, near) + ahead)[:2]
+    middle = lax.ppermute(late_shard, "seq", [(1, 2), (2, 1)])
+    ends = lax.ppermute(late_two, "seq", [(1, 0), (2, 3)])
+    return [shard, near, two, middle, ends]
 
 
 def call(kernel, args, outs, scratch=(), far_in=False, flops=0, vmem=VMEM_BYTES):
@@ -235,6 +240,8 @@
     half = rows // 2
     zl = lax.axis_index("seq") % 2
 
+    weight_c = lax.ppermute(out_weight, "head", swap)
+
     packed = call(
         pack_kernel,
         (queries, key_vectors, value_vectors),
@@ -254,32 +261,35 @@
         moved.append(lax.ppermute(packed[k], ("seq", "head"), pairs))
     (joined,) = call(join_kernel, moved, [((4 * rows, width), bf16)])
     sibling = lax.ppermute(joined, "head", swap)
-    late_weight, _ = lax.optimization_barrier((out_weight, sibling))
-    weight_c = lax.ppermute(late_weight, "head", swap)
-    sent_rows, kept_rows = call(
-        attention_kernel,
-        moved + [sibling],
-        [((rows, width), bf16)] * 2,
-        [
-            pltpu.VMEM((4 * rows, width), bf16),
-            pltpu.VMEM((4 * rows, width), bf16),
-            pltpu.VMEM((2 * rows, width), bf16),
-        ],
-        flops=4 * (2 * rows) * (4 * rows) * width,
-    )
+    parts = []
+    for part in range(2):
+        parts += call(
+            functools.partial(attention_kernel, part),
+            moved + [sibling],
+            [((rows, width), bf16)],
+            [
+                pltpu.VMEM((4 * rows, width), bf16),
+                pltpu.VMEM((4 * rows, width), bf16),
+                pltpu.VMEM((rows, width), bf16),
+            ],
+            flops=4 * rows * (4 * rows) * width,
+        )
 
     flops = 4 * rows * depth * columns
-    gathered = lax.all_gather(sent_rows, "seq", axis=0, tiled=True)
+    held = [pltpu.VMEM((4, rows, width), bf16)]
+    first, _ = lax.optimization_barrier((parts[0], weight_c))
+    shards = gather(first, parts[1])
     (send,) = call(
-        sent_kernel, (gathered, out_weight, weight_c), [((rows, columns), bf16)], flops=flops
+        sent_kernel, shards + [out_weight, weight_c], [((rows, columns), bf16)], held, flops=flops
     )
     arrived = lax.ppermute(send, "wt", swap)
-    kept_rows, _ = lax.optimization_barrier((kept_rows, send))
-    gathered = lax.all_gather(kept_rows, "seq", axis=0, tiled=True)
+    second, _ = lax.optimization_barrier((parts[1], send))
+    shards = gather(second)
     sums = call(
         kept_kernel,
-        (gathered, out_weight, weight_c, arrived),
+        shards + [out_weight, weight_c, arrived],
         [((half, columns), bf16)] * 2,
+        held,
         flops=flops,
     )
 

time: 80 us -> 82.3 us (1.029)
  blocking collectives: 31.3 us -> 0 us
  waiting for transfers between devices: 27 us -> 49.2 us
  starting transfers between devices: 10 us -> 20 us
  Pallas kernels: 5.56 us -> 9.53 us
  local copies, waits for them, and re-layouts: 2.87 us -> 0.03 us
    all_gather x2 -> x0, blocking collectives: 31.3 us -> none  [the longest x1 16.5 us: local_heads(): gathered = lax.all_gather(sent_rows, 'seq', axis=0, tiled=True)]
    ppermute x1 -> x9, waiting for transfers between devices: 0.01 us -> 21.8 us  [the longest x2 13.3 us: gather(): ends = lax.ppermute(late_two, 'seq', [(1, 0), (2, 3)])]
    ppermute x1 -> x9, starting transfers between devices: 0.14 us -> 10.9 us  [the longest x2 4.4 us: gather(): two = lax.ppermute(shard, 'seq', [(0, 2), (2, 0), (1, 3), (3, 1)])]
    pallas_call x5 -> x6, Pallas kernels: 5.56 us -> 9.53 us  [call(): pl.pallas_call(kernel, in_specs=[pl.BlockSpec(memory_space=place)] * len(...]
    unnamed x14 -> x10, local copies, waits for them, and re-layouts: 2.87 us -> 0.03 us
  transfers between devices with their start and end apart: 9 -> 17, of which waited for: 4 -> 10; matrix products, arithmetic and copies ran while one was open for 0% -> 0% of each run, Pallas kernels for 2% -> 6%
where the time goes in v6:
time: 82.3 us; the launch traced here: 81.2 us
  waiting for transfers between devices  49.2 us (60%)
  starting transfers between devices  20 us (24%)
  Pallas kernels  9.53 us (12%)
  other arithmetic  1.64 us (2%)
  between operations  0.87 us (1%)
    ppermute x4, waiting for transfers between devices, local_heads(): moved.append(lax.ppermute(packed[k], ('seq', 'head'), pairs))  15 us
    ppermute x2, waiting for transfers between devices, gather(): ends = lax.ppermute(late_two, 'seq', [(1, 0), (2, 3)])  13.3 us
    ppermute x2, waiting for transfers between devices, local_heads(): owned.append(lax.ppermute(part, ('seq', 'wt', 'head'), pairs))  10.4 us
    pallas_call x6, Pallas kernels, call(): pl.pallas_call(kernel, in_specs=[pl.BlockSpec(memory_space=place)] * len(...  9.53 us
    ppermute x4, starting transfers between devices, local_heads(): moved.append(lax.ppermute(packed[k], ('seq', 'head'), pairs))  6.01 us
    ppermute x2, waiting for transfers between devices, gather(): near = lax.ppermute(shard, 'seq', [(0, 1), (1, 0), (2, 3), (3, 2)])  4.91 us
    ppermute x2, starting transfers between devices, gather(): two = lax.ppermute(shard, 'seq', [(0, 2), (2, 0), (1, 3), (3, 1)])  4.4 us
    ppermute x2, waiting for transfers between devices, gather(): two = lax.ppermute(shard, 'seq', [(0, 2), (2, 0), (1, 3), (3, 1)])  3.58 us
  transfers between devices with their start and end apart: 17, of which 10 were waited for; matrix products, arithmetic and copies ran while one was open for 0% of the time, Pallas kernels for 6%

profile of v6, /device:TPU:2, one launch (start us, length us, event | category | flops | bytes accessed | tf_op | source)
XLA Modules:
  0.0 81.2 jit_solution(18378036788647948407)
XLA Ops:
  0.6 0.0 copy-start
  0.6 0.1 collective-permute-start.5
  0.7 2.2 %shard_map.95 = (bf16[320,384]{1,0:T(8,128)(2,1)}, bf16[320,384]{1,0:T(8,128)(2,1)}, bf16[160,384]{1,0:T(8,128)(2,1)}, bf16[160,384]{1,0:T(8,128)(2,1)}) custom-call(bf16[160,768]{1,0:T(8,128)(2,1)} %queries.1, bf16[160,768]{1,0:T(8,128)(2,1)} %keys.1, bf16[160,768]{1,0:T(8,128)(2,1)} %values.1), custom_call_target="tpu_custom_call" | custom-call | tf_op jit(solution)/shard_map/pallas_call | solution.py:213
  2.9 1.6 %collective-permute-start = (bf16[320,384]{1,0:T(8,128)(2,1)}, bf16[320,384]{1,0:T(8,128)(2,1)S(1)}, u32[]{:S(2)}, u32[]{:S(2)}) collective-permute-start(bf16[320,384]{1,0:T(8,128)(2,1)} %get-tuple-element.14), channel_id=1, source_target_pairs={{0,0},{1,8},{4,4},{5,12},{8,1},{9,9},{12,5},{13,13},{2,2},{3,10},{... | collective-permute-start | bytes 737288 | tf_op jit(solution)/shard_map/ppermute | solution.py:261
  4.5 1.6 %collective-permute-start.1 = (bf16[320,384]{1,0:T(8,128)(2,1)}, bf16[320,384]{1,0:T(8,128)(2,1)S(1)}, u32[]{:S(2)}, u32[]{:S(2)}) collective-permute-start(bf16[320,384]{1,0:T(8,128)(2,1)} %get-tuple-element.15), channel_id=1, source_target_pairs={{0,4},{1,12},{4,0},{5,8},{8,5},{9,13},{12,1},{13,9},{2,6},{3,14},{... | collective-permute-start | bytes 737288 | tf_op jit(solution)/shard_map/ppermute | solution.py:261
  6.1 2.8 %collective-permute-start.2 = (bf16[160,384]{1,0:T(8,128)(2,1)}, bf16[160,384]{1,0:T(8,128)(2,1)S(1)}, u32[]{:S(2)}, u32[]{:S(2)}) collective-permute-start(bf16[160,384]{1,0:T(8,128)(2,1)} %get-tuple-element.16), channel_id=1, source_target_pairs={{0,1},{1,9},{4,5},{5,13},{8,0},{9,8},{12,4},{13,12},{2,3},{3,11},{... | collective-permute-start | bytes 368648 | tf_op jit(solution)/shard_map/ppermute | solution.py:261
  8.9 0.0 collective-permute-start.3
  9.0 15.0 %collective-permute-done.2.refs_2_ = bf16[160,384]{1,0:T(8,128)(2,1)S(1)} collective-permute-done((bf16[160,384]{1,0:T(8,128)(2,1)}, bf16[160,384]{1,0:T(8,128)(2,1)S(1)}, u32[]{:S(2)}, u32[]{:S(2)}) %collective-permute-start.2) | collective-permute-done | bytes 122912 | tf_op jit(solution)/shard_map/ppermute | solution.py:261
  24.0 0.0 collective-permute-done.3.refs_3_
  24.0 0.0 collective-permute-done.refs_0_
  24.0 0.0 collective-permute-done.1.refs_1_
  24.1 0.1 collective-permute-start.4
  24.1 1.9 %collective-permute-done.4.refs_4_ = bf16[640,384]{1,0:T(8,128)(2,1)S(1)} collective-permute-done((bf16[640,384]{1,0:T(8,128)(2,1)S(1)}, bf16[640,384]{1,0:T(8,128)(2,1)S(1)}, u32[]{:S(2)}, u32[]{:S(2)}) %collective-permute-start.4) | collective-permute-done | bytes 491552 | tf_op jit(solution)/shard_map/ppermute | solution.py:263
  26.0 1.2 %shard_map.98.refs_0_ = bf16[160,384]{1,0:T(8,128)(2,1)S(1)} custom-call(bf16[320,384]{1,0:T(8,128)(2,1)S(1)} %collective-permute-done.refs_0_, bf16[320,384]{1,0:T(8,128)(2,1)S(1)} %collective-permute-done.1.refs_1_, bf16[160,384]{1,0:T(8,128)(2,1)S(1)} %collective-permute-done.2.refs_2_, bf16[160,384]{1,0:T(8,128)(2,1)S(1)} %collective-permute-done.3.refs_3_, ...), custom_call_target="tpu_custom_call" | custom-call | flops 157286400 | tf_op jit(solution)/shard_map/pallas_call | solution.py:213
  27.2 0.0 copy-start.4
  27.2 0.0 collective-permute-done.5.refs_6_
  27.2 1.9 %collective-permute-start.6 = (bf16[160,384]{1,0:T(8,128)(2,1)S(1)}, bf16[160,384]{1,0:T(8,128)(2,1)S(1)}, u32[]{:S(2)}, u32[]{:S(2)}) collective-permute-start(bf16[160,384]{1,0:T(8,128)(2,1)S(1)} %shard_map.98.refs_0_), channel_id=1, source_target_pairs={{0,4},{4,0},{8,12},{12,8},{1,5},{5,1},{9,13},{13,9},{2,6},{6,2},{1... | collective-permute-start | bytes 368648 | tf_op jit(solution)/shard_map/ppermute | solution.py:203
  29.1 1.1 %collective-permute-start.7 = (bf16[160,384]{1,0:T(8,128)(2,1)S(1)}, bf16[160,384]{1,0:T(8,128)(2,1)S(1)}, u32[]{:S(2)}, u32[]{:S(2)}) collective-permute-start(bf16[160,384]{1,0:T(8,128)(2,1)S(1)} %shard_map.98.refs_0_), channel_id=1, source_target_pairs={{0,8},{8,0},{4,12},{12,4},{1,9},{9,1},{5,13},{13,5},{2,10},{10,2},... | collective-permute-start | bytes 368648 | tf_op jit(solution)/shard_map/ppermute | solution.py:204
  30.2 1.2 %shard_map.97.refs_0_ = bf16[160,384]{1,0:T(8,128)(2,1)S(1)} custom-call(bf16[320,384]{1,0:T(8,128)(2,1)S(1)} %collective-permute-done.refs_0_, bf16[320,384]{1,0:T(8,128)(2,1)S(1)} %collective-permute-done.1.refs_1_, bf16[160,384]{1,0:T(8,128)(2,1)S(1)} %collective-permute-done.2.refs_2_, bf16[160,384]{1,0:T(8,128)(2,1)S(1)} %collective-permute-done.3.refs_3_, ...), custom_call_target="tpu_custom_call" | custom-call | flops 157286400 | tf_op jit(solution)/shard_map/pallas_call | solution.py:213
  31.4 3.5 %collective-permute-done.6.refs_1_ = bf16[160,384]{1,0:T(8,128)(2,1)S(1)} collective-permute-done((bf16[160,384]{1,0:T(8,128)(2,1)S(1)}, bf16[160,384]{1,0:T(8,128)(2,1)S(1)}, u32[]{:S(2)}, u32[]{:S(2)}) %collective-permute-start.6) | collective-permute-done | bytes 122912 | tf_op jit(solution)/shard_map/ppermute | solution.py:203
  35.0 0.8 collective-permute-done.7.refs_2_
  35.8 0.7 collective-permute-start.8
  36.4 1.3 %collective-permute-start.9 = (bf16[160,384]{1,0:T(8,128)(2,1)S(1)}, bf16[160,384]{1,0:T(8,128)(2,1)S(1)}, u32[]{:S(2)}, u32[]{:S(2)}) collective-permute-start(bf16[160,384]{1,0:T(8,128)(2,1)S(1)} %collective-permute-done.7.refs_2_), channel_id=1, source_target_pairs={{4,0},{8,12},{5,1},{9,13},{6,2},{10,14},{7,3},{11,15},{20,16},{24,... | collective-permute-start | bytes 368648 | tf_op jit(solution)/shard_map/ppermute | solution.py:207
  37.7 0.0 collective-permute-done.8.refs_3_
  37.7 7.0 %collective-permute-done.9.refs_4_ = bf16[160,384]{1,0:T(8,128)(2,1)S(1)} collective-permute-done((bf16[160,384]{1,0:T(8,128)(2,1)S(1)}, bf16[160,384]{1,0:T(8,128)(2,1)S(1)}, u32[]{:S(2)}, u32[]{:S(2)}) %collective-permute-start.9) | collective-permute-done | bytes 122912 | tf_op jit(solution)/shard_map/ppermute | solution.py:207
  44.8 2.4 %shard_map.99 = bf16[160,1280]{1,0:T(8,128)(2,1)S(1)} custom-call(bf16[160,384]{1,0:T(8,128)(2,1)S(1)} %shard_map.98.refs_0_, bf16[160,384]{1,0:T(8,128)(2,1)S(1)} %collective-permute-done.6.refs_1_, bf16[160,384]{1,0:T(8,128)(2,1)S(1)} %collective-permute-done.7.refs_2_, bf16[160,384]{1,0:T(8,128)(2,1)S(1)} %collective-permute-done.8.refs_3_, ...), custom_call_target="tpu_custom_call" | custom-call | flops 629145600 | tf_op jit(solution)/shard_map/pallas_call | solution.py:213
  47.2 0.4 collective-permute-start.14
  47.6 0.6 collective-permute-start.10
  48.1 3.3 %collective-permute-start.11 = (bf16[160,384]{1,0:T(8,128)(2,1)S(1)}, bf16[160,384]{1,0:T(8,128)(2,1)S(1)}, u32[]{:S(2)}, u32[]{:S(2)}) collective-permute-start(bf16[160,384]{1,0:T(8,128)(2,1)S(1)} %shard_map.97.refs_0_), channel_id=1, source_target_pairs={{0,8},{8,0},{4,12},{12,4},{1,9},{9,1},{5,13},{13,5},{2,10},{10,2},... | collective-permute-start | bytes 368648 | tf_op jit(solution)/shard_map/ppermute | solution.py:204
  51.4 1.4 %collective-permute-done.10.refs_1_ = bf16[160,384]{1,0:T(8,128)(2,1)S(1)} collective-permute-done((bf16[160,384]{1,0:T(8,128)(2,1)S(1)}, bf16[160,384]{1,0:T(8,128)(2,1)S(1)}, u32[]{:S(2)}, u32[]{:S(2)}) %collective-permute-start.10) | collective-permute-done | bytes 122912 | tf_op jit(solution)/shard_map/ppermute | solution.py:203
  52.8 2.8 %collective-permute-done.11.refs_2_ = bf16[160,384]{1,0:T(8,128)(2,1)S(1)} collective-permute-done((bf16[160,384]{1,0:T(8,128)(2,1)S(1)}, bf16[160,384]{1,0:T(8,128)(2,1)S(1)}, u32[]{:S(2)}, u32[]{:S(2)}) %collective-permute-start.11) | collective-permute-done | bytes 122912 | tf_op jit(solution)/shard_map/ppermute | solution.py:204
  55.6 0.7 collective-permute-start.12
  56.3 1.3 %collective-permute-start.13 = (bf16[160,384]{1,0:T(8,128)(2,1)S(1)}, bf16[160,384]{1,0:T(8,128)(2,1)S(1)}, u32[]{:S(2)}, u32[]{:S(2)}) collective-permute-start(bf16[160,384]{1,0:T(8,128)(2,1)S(1)} %collective-permute-done.11.refs_2_), channel_id=1, source_target_pairs={{4,0},{8,12},{5,1},{9,13},{6,2},{10,14},{7,3},{11,15},{20,16},{24,... | collective-permute-start | bytes 368648 | tf_op jit(solution)/shard_map/ppermute | solution.py:207
  57.6 0.0 copy-start.1
  57.6 0.0 collective-permute-done.12.refs_3_
  57.6 6.3 %collective-permute-done.13.refs_4_ = bf16[160,384]{1,0:T(8,128)(2,1)S(1)} collective-permute-done((bf16[160,384]{1,0:T(8,128)(2,1)S(1)}, bf16[160,384]{1,0:T(8,128)(2,1)S(1)}, u32[]{:S(2)}, u32[]{:S(2)}) %collective-permute-start.13) | collective-permute-done | bytes 122912 | tf_op jit(solution)/shard_map/ppermute | solution.py:207
  63.9 0.0 collective-permute-done.14.refs_7_
  63.9 2.5 %shard_map.100 = (bf16[80,1280]{1,0:T(8,128)(2,1)S(1)}, bf16[80,1280]{1,0:T(8,128)(2,1)S(1)}) custom-call(bf16[160,384]{1,0:T(8,128)(2,1)S(1)} %shard_map.97.refs_0_, bf16[160,384]{1,0:T(8,128)(2,1)S(1)} %collective-permute-done.10.refs_1_, bf16[160,384]{1,0:T(8,128)(2,1)S(1)} %collective-permute-done.11.refs_2_, ...), custom_call_target="tpu_custom_call" | custom-call | flops 629145600 | tf_op jit(solution)/shard_map/pallas_call | solution.py:213
  66.4 0.0 copy-start.2
  66.4 0.0 copy-start.3
  66.4 2.6 %collective-permute-start.15 = (bf16[80,1280]{1,0:T(8,128)(2,1)S(1)}, bf16[80,1280]{1,0:T(8,128)(2,1)S(1)}, u32[]{:S(2)}, u32[]{:S(2)}) collective-permute-start(bf16[80,1280]{1,0:T(8,128)(2,1)S(1)} %get-tuple-element.24), channel_id=1, source_target_pairs={{0,0},{1,8},{2,4},{3,12},{4,1},{5,9},{6,5},{7,13},{8,2},{9,10},{10... | collective-permute-start | bytes 614408 | tf_op jit(solution)/shard_map/ppermute | solution.py:304
  69.0 0.1 collective-permute-start.16
  69.1 0.3 multiply_reduce_fusion
  69.4 10.1 %collective-permute-done.15 = bf16[80,1280]{1,0:T(8,128)(2,1)S(1)} collective-permute-done((bf16[80,1280]{1,0:T(8,128)(2,1)S(1)}, bf16[80,1280]{1,0:T(8,128)(2,1)S(1)}, u32[]{:S(2)}, u32[]{:S(2)}) %collective-permute-start.15) | collective-permute-done | bytes 204832 | tf_op jit(solution)/shard_map/ppermute | solution.py:304
  79.5 0.4 collective-permute-done.16
  79.9 0.0 copy-done.2
  79.9 0.0 copy-done.3
  79.9 1.3 %add_add_fusion = (f32[160,1280]{1,0:T(8,128)}, f32[160,1280]{1,0:T(8,128)}) fusion(f32[160,1280]{1,0:T(8,128)S(1)} %copy-done.2, f32[160,1280]{1,0:T(8,128)S(1)} %multiply_reduce_fusion, f32[1280]{0:T(1024)S(1)} %copy-done.3, bf16[80,1280]{1,0:T(8,128)(2,1)S(1)} %get-tuple-element.29, bf16[80,1280]{1,0:T(8,128)(2,1)S(1)} %get-tuple-element.28), kind=kLoop, calls=%fused_computation.2 | loop fusion | flops 1433600 | bytes 3691520 | tf_op jit(solution)/shard_map/add | solution.py:315
  (6 shorter events, 0.1 us)
Async XLA Ops:
  0.6 44.1 %copy-start = (bf16[768,1280]{1,0:T(8,128)(2,1)S(1)}, bf16[768,1280]{1,0:T(8,128)(2,1)}, u32[]{:S(2)}) copy-start(bf16[768,1280]{1,0:T(8,128)(2,1)} %refs_5_.3) | copy-start | bytes 5898244
  0.6 26.6 %collective-permute-start.5 = (bf16[768,1280]{1,0:T(8,128)(2,1)}, bf16[768,1280]{1,0:T(8,128)(2,1)}, u32[]{:S(2)}, u32[]{:S(2)}) collective-permute-start(bf16[768,1280]{1,0:T(8,128)(2,1)} %refs_5_.3), channel_id=1, source_target_pairs={{0,1},{1,0},{2,3},{3,2},{4,5},{5,4},{6,7},{7,6},{8,9},{9,8},{10,11... | collective-permute-start | bytes 5898248 | tf_op jit(solution)/shard_map/ppermute | solution.py:243
  2.9 21.1 %collective-permute-start = (bf16[320,384]{1,0:T(8,128)(2,1)}, bf16[320,384]{1,0:T(8,128)(2,1)S(1)}, u32[]{:S(2)}, u32[]{:S(2)}) collective-permute-start(bf16[320,384]{1,0:T(8,128)(2,1)} %get-tuple-element.14), channel_id=1, source_target_pairs={{0,0},{1,8},{4,4},{5,12},{8,1},{9,9},{12,5},{13,13},{2,2},{3,10},{... | collective-permute-start | bytes 737288 | tf_op jit(solution)/shard_map/ppermute | solution.py:261
  4.5 19.5 %collective-permute-start.1 = (bf16[320,384]{1,0:T(8,128)(2,1)}, bf16[320,384]{1,0:T(8,128)(2,1)S(1)}, u32[]{:S(2)}, u32[]{:S(2)}) collective-permute-start(bf16[320,384]{1,0:T(8,128)(2,1)} %get-tuple-element.15), channel_id=1, source_target_pairs={{0,4},{1,12},{4,0},{5,8},{8,5},{9,13},{12,1},{13,9},{2,6},{3,14},{... | collective-permute-start | bytes 737288 | tf_op jit(solution)/shard_map/ppermute | solution.py:261
  6.1 17.9 %collective-permute-start.2 = (bf16[160,384]{1,0:T(8,128)(2,1)}, bf16[160,384]{1,0:T(8,128)(2,1)S(1)}, u32[]{:S(2)}, u32[]{:S(2)}) collective-permute-start(bf16[160,384]{1,0:T(8,128)(2,1)} %get-tuple-element.16), channel_id=1, source_target_pairs={{0,1},{1,9},{4,5},{5,13},{8,0},{9,8},{12,4},{13,12},{2,3},{3,11},{... | collective-permute-start | bytes 368648 | tf_op jit(solution)/shard_map/ppermute | solution.py:261
  8.9 15.1 %collective-permute-start.3 = (bf16[160,384]{1,0:T(8,128)(2,1)}, bf16[160,384]{1,0:T(8,128)(2,1)S(1)}, u32[]{:S(2)}, u32[]{:S(2)}) collective-permute-start(bf16[160,384]{1,0:T(8,128)(2,1)} %get-tuple-element.17), channel_id=1, source_target_pairs={{0,5},{1,13},{4,1},{5,9},{8,4},{9,12},{12,0},{13,8},{2,7},{3,15},{... | collective-permute-start | bytes 368648 | tf_op jit(solution)/shard_map/ppermute | solution.py:261
  24.1 1.9 %collective-permute-start.4 = (bf16[640,384]{1,0:T(8,128)(2,1)S(1)}, bf16[640,384]{1,0:T(8,128)(2,1)S(1)}, u32[]{:S(2)}, u32[]{:S(2)}) collective-permute-start(bf16[640,384]{1,0:T(8,128)(2,1)S(1)} %shard_map.96), channel_id=1, source_target_pairs={{0,1},{1,0},{2,3},{3,2},{4,5},{5,4},{6,7},{7,6},{8,9},{9,8},{10,11... | collective-permute-start | bytes 1474568 | tf_op jit(solution)/shard_map/ppermute | solution.py:263
  27.2 30.4 %copy-start.4 = (s32[4]{0:T(128)S(1)}, s32[4]{0:T(128)}, u32[]{:S(2)}) copy-start(s32[4]{0:T(128)} %param.15) | copy-start | bytes 52
  27.2 7.8 %collective-permute-start.6 = (bf16[160,384]{1,0:T(8,128)(2,1)S(1)}, bf16[160,384]{1,0:T(8,128)(2,1)S(1)}, u32[]{:S(2)}, u32[]{:S(2)}) collective-permute-start(bf16[160,384]{1,0:T(8,128)(2,1)S(1)} %shard_map.98.refs_0_), channel_id=1, source_target_pairs={{0,4},{4,0},{8,12},{12,8},{1,5},{5,1},{9,13},{13,9},{2,6},{6,2},{1... | collective-permute-start | bytes 368648 | tf_op jit(solution)/shard_map/ppermute | solution.py:203
  29.1 6.6 %collective-permute-start.7 = (bf16[160,384]{1,0:T(8,128)(2,1)S(1)}, bf16[160,384]{1,0:T(8,128)(2,1)S(1)}, u32[]{:S(2)}, u32[]{:S(2)}) collective-permute-start(bf16[160,384]{1,0:T(8,128)(2,1)S(1)} %shard_map.98.refs_0_), channel_id=1, source_target_pairs={{0,8},{8,0},{4,12},{12,4},{1,9},{9,1},{5,13},{13,5},{2,10},{10,2},... | collective-permute-start | bytes 368648 | tf_op jit(solution)/shard_map/ppermute | solution.py:204
  35.8 2.0 %collective-permute-start.8 = (bf16[160,384]{1,0:T(8,128)(2,1)S(1)}, bf16[160,384]{1,0:T(8,128)(2,1)S(1)}, u32[]{:S(2)}, u32[]{:S(2)}) collective-permute-start(bf16[160,384]{1,0:T(8,128)(2,1)S(1)} %shard_map.98.refs_0_), channel_id=1, source_target_pairs={{4,8},{8,4},{5,9},{9,5},{6,10},{10,6},{7,11},{11,7},{20,24},{24,20... | collective-permute-start | bytes 368648 | tf_op jit(solution)/shard_map/ppermute | solution.py:206
  36.4 8.3 %collective-permute-start.9 = (bf16[160,384]{1,0:T(8,128)(2,1)S(1)}, bf16[160,384]{1,0:T(8,128)(2,1)S(1)}, u32[]{:S(2)}, u32[]{:S(2)}) collective-permute-start(bf16[160,384]{1,0:T(8,128)(2,1)S(1)} %collective-permute-done.7.refs_2_), channel_id=1, source_target_pairs={{4,0},{8,12},{5,1},{9,13},{6,2},{10,14},{7,3},{11,15},{20,16},{24,... | collective-permute-start | bytes 368648 | tf_op jit(solution)/shard_map/ppermute | solution.py:207
  47.2 16.7 %collective-permute-start.14 = (bf16[160,1280]{1,0:T(8,128)(2,1)S(1)}, bf16[160,1280]{1,0:T(8,128)(2,1)S(1)}, u32[]{:S(2)}, u32[]{:S(2)}) collective-permute-start(bf16[160,1280]{1,0:T(8,128)(2,1)S(1)} %shard_map.99), channel_id=1, source_target_pairs={{0,2},{2,0},{1,3},{3,1},{4,6},{6,4},{5,7},{7,5},{8,10},{10,8},{9,1... | collective-permute-start | bytes 1228808 | tf_op jit(solution)/shard_map/ppermute | solution.py:285
  47.6 5.2 %collective-permute-start.10 = (bf16[160,384]{1,0:T(8,128)(2,1)S(1)}, bf16[160,384]{1,0:T(8,128)(2,1)S(1)}, u32[]{:S(2)}, u32[]{:S(2)}) collective-permute-start(bf16[160,384]{1,0:T(8,128)(2,1)S(1)} %shard_map.97.refs_0_), channel_id=1, source_target_pairs={{0,4},{4,0},{8,12},{12,8},{1,5},{5,1},{9,13},{13,9},{2,6},{6,2},{1... | collective-permute-start | bytes 368648 | tf_op jit(solution)/shard_map/ppermute | solution.py:203
  48.1 7.5 %collective-permute-start.11 = (bf16[160,384]{1,0:T(8,128)(2,1)S(1)}, bf16[160,384]{1,0:T(8,128)(2,1)S(1)}, u32[]{:S(2)}, u32[]{:S(2)}) collective-permute-start(bf16[160,384]{1,0:T(8,128)(2,1)S(1)} %shard_map.97.refs_0_), channel_id=1, source_target_pairs={{0,8},{8,0},{4,12},{12,4},{1,9},{9,1},{5,13},{13,5},{2,10},{10,2},... | collective-permute-start | bytes 368648 | tf_op jit(solution)/shard_map/ppermute | solution.py:204
  55.6 2.0 %collective-permute-start.12 = (bf16[160,384]{1,0:T(8,128)(2,1)S(1)}, bf16[160,384]{1,0:T(8,128)(2,1)S(1)}, u32[]{:S(2)}, u32[]{:S(2)}) collective-permute-start(bf16[160,384]{1,0:T(8,128)(2,1)S(1)} %shard_map.97.refs_0_), channel_id=1, source_target_pairs={{4,8},{8,4},{5,9},{9,5},{6,10},{10,6},{7,11},{11,7},{20,24},{24,20... | collective-permute-start | bytes 368648 | tf_op jit(solution)/shard_map/ppermute | solution.py:206
  56.3 7.6 %collective-permute-start.13 = (bf16[160,384]{1,0:T(8,128)(2,1)S(1)}, bf16[160,384]{1,0:T(8,128)(2,1)S(1)}, u32[]{:S(2)}, u32[]{:S(2)}) collective-permute-start(bf16[160,384]{1,0:T(8,128)(2,1)S(1)} %collective-permute-done.11.refs_2_), channel_id=1, source_target_pairs={{4,0},{8,12},{5,1},{9,13},{6,2},{10,14},{7,3},{11,15},{20,16},{24,... | collective-permute-start | bytes 368648 | tf_op jit(solution)/shard_map/ppermute | solution.py:207
  57.6 11.5 %copy-start.1 = (f32[4,160,1280]{2,1,0:T(8,128)S(1)}, f32[4,160,1280]{2,1,0:T(8,128)}, u32[]{:S(2)}) copy-start(f32[4,160,1280]{2,1,0:T(8,128)} %param.14) | copy-start | bytes 9830404
  66.4 13.5 %copy-start.2 = (f32[160,1280]{1,0:T(8,128)S(1)}, f32[160,1280]{1,0:T(8,128)}, u32[]{:S(2)}) copy-start(f32[160,1280]{1,0:T(8,128)} %param.13) | copy-start | bytes 2457604
  66.4 13.5 %copy-start.3 = (f32[1280]{0:T(1024)S(1)}, f32[1280]{0:T(1024)}, u32[]{:S(2)}) copy-start(f32[1280]{0:T(1024)} %param.12) | copy-start | bytes 15364
  66.4 13.0 %collective-permute-start.15 = (bf16[80,1280]{1,0:T(8,128)(2,1)S(1)}, bf16[80,1280]{1,0:T(8,128)(2,1)S(1)}, u32[]{:S(2)}, u32[]{:S(2)}) collective-permute-start(bf16[80,1280]{1,0:T(8,128)(2,1)S(1)} %get-tuple-element.24), channel_id=1, source_target_pairs={{0,0},{1,8},{2,4},{3,12},{4,1},{5,9},{6,5},{7,13},{8,2},{9,10},{10... | collective-permute-start | bytes 614408 | tf_op jit(solution)/shard_map/ppermute | solution.py:304
  69.0 10.8 %collective-permute-start.16 = (bf16[80,1280]{1,0:T(8,128)(2,1)S(1)}, bf16[80,1280]{1,0:T(8,128)(2,1)S(1)}, u32[]{:S(2)}, u32[]{:S(2)}) collective-permute-start(bf16[80,1280]{1,0:T(8,128)(2,1)S(1)} %get-tuple-element.25), channel_id=1, source_target_pairs={{0,4},{1,12},{2,0},{3,8},{4,5},{5,13},{6,1},{7,9},{8,6},{9,14},{10... | collective-permute-start | bytes 614408 | tf_op jit(solution)/shard_map/ppermute | solution.py:304

commit v7 on v5

--- a/solution.py
+++ b/solution.py
@@ -165,15 +165,18 @@
         kept[:, columns] = result[rows:]
 
 
-def multiply(gathered, weight, weight_c):
-    rows = gathered.shape[0] // 4
+def multiply(shards, weight, weight_c, held):
+    rows = shards[0].shape[0]
+    zh, zl = bits()
     core = lax.axis_index("head")
+    for m, shard in enumerate(shards):
+        held[m * rows : (m + 1) * rows, :] = shard[...]
     total = None
     for other, block in enumerate((weight, weight_c)):
-        start = 2 * flip(core, other) * rows
+        high = 2 * lax.rem(flip(core, other) + zh, 2)
         left = jnp.concatenate(
             [
-                gathered[pl.ds(pl.multiple_of(start + low * rows, 16), rows), :]
+                held[pl.ds(pl.multiple_of((high + flip(zl, low)) * rows, 16), rows), :]
                 for low in range(2)
             ],
             axis=1,
@@ -183,12 +186,14 @@
     return total
 
 
-def sent_kernel(gathered, weight, weight_c, out):
-    out[...] = multiply(gathered, weight, weight_c).astype(out.dtype)
-
-
-def kept_kernel(gathered, weight, weight_c, arrived, out0, out1):
-    total = multiply(gathered, weight, weight_c) + arrived[...].astype(jnp.float32)
+def sent_kernel(*refs):
+    shards, (weight, weight_c, out, held) = refs[:4], refs[4:]
+    out[...] = multiply(shards, weight, weight_c, held).astype(out.dtype)
+
+
+def kept_kernel(*refs):
+    arrived, shards, (weight, weight_c, out0, out1, held) = refs[0], refs[1:5], refs[5:]
+    total = multiply(shards, weight, weight_c, held) + arrived[...].astype(jnp.float32)
     half = out0.shape[0]
     x = lax.axis_index("wt")
     for low in range(2):
@@ -201,6 +206,10 @@
         @pl.when(x != low)
         def _():
             out1[...] = part
+
+
+def along(shard, m):
+    return lax.ppermute(shard, "seq", [(z, z ^ m) for z in range(4)])
 
 
 def call(kernel, args, outs, scratch=(), far_in=False, flops=0, vmem=VMEM_BYTES):
@@ -235,6 +244,8 @@
     half = rows // 2
     zl = lax.axis_index("seq") % 2
 
+    weight_c = lax.ppermute(out_weight, "head", swap)
+
     packed = call(
         pack_kernel,
         (queries, key_vectors, value_vectors),
@@ -254,9 +265,7 @@
         moved.append(lax.ppermute(packed[k], ("seq", "head"), pairs))
     (joined,) = call(join_kernel, moved, [((4 * rows, width), bf16)])
     sibling = lax.ppermute(joined, "head", swap)
-    late_weight, _ = lax.optimization_barrier((out_weight, sibling))
-    weight_c = lax.ppermute(late_weight, "head", swap)
-    sent_rows, kept_rows = call(
+    parts = call(
         attention_kernel,
         moved + [sibling],
         [((rows, width), bf16)] * 2,
@@ -269,17 +278,21 @@
     )
 
     flops = 4 * rows * depth * columns
-    gathered = lax.all_gather(sent_rows, "seq", axis=0, tiled=True)
+    held = [pltpu.VMEM((4 * rows, width), bf16)]
+    first, second, _ = lax.optimization_barrier((parts[0], parts[1], weight_c))
+    shards = [first] + [along(first, m) for m in (1, 2, 3)]
+    near = along(second, 1)
+    shards[3], _ = lax.optimization_barrier((shards[3], near))
     (send,) = call(
-        sent_kernel, (gathered, out_weight, weight_c), [((rows, columns), bf16)], flops=flops
+        sent_kernel, shards + [out_weight, weight_c], [((rows, columns), bf16)], held, flops=flops
     )
     arrived = lax.ppermute(send, "wt", swap)
-    kept_rows, _ = lax.optimization_barrier((kept_rows, send))
-    gathered = lax.all_gather(kept_rows, "seq", axis=0, tiled=True)
+    shards = [parts[1], near] + [along(parts[1], m) for m in (2, 3)]
     sums = call(
         kept_kernel,
-        (gathered, out_weight, weight_c, arrived),
+        [arrived] + shards + [out_weight, weight_c],
         [((half, columns), bf16)] * 2,
+        held,
         flops=flops,
     )
 

time: 80 us -> 77.3 us (0.966)
  blocking collectives: 31.3 us -> 0 us
  waiting for transfers between devices: 27 us -> 45.2 us
  starting transfers between devices: 10 us -> 20.5 us
  Pallas kernels: 5.56 us -> 8.76 us
  local copies, waits for them, and re-layouts: 2.87 us -> 0.03 us
    all_gather x2 -> x0, blocking collectives: 31.3 us -> none  [the longest x1 16.5 us: local_heads(): gathered = lax.all_gather(sent_rows, 'seq', axis=0, tiled=True)]
    ppermute x1 -> x7, waiting for transfers between devices: 0.01 us -> 18 us  [the longest x6 18 us: along(): return lax.ppermute(shard, 'seq', [(z, z ^ m) for z in range(4)])]
    ppermute x1 -> x7, starting transfers between devices: 0.14 us -> 8.37 us  [the longest x6 8.29 us: along(): return lax.ppermute(shard, 'seq', [(z, z ^ m) for z in range(4)])]
    pallas_call x5, Pallas kernels: 5.56 us -> 8.76 us  [call(): pl.pallas_call(kernel, in_specs=[pl.BlockSpec(memory_space=place)] * len(...]
    unnamed x14 -> x10, local copies, waits for them, and re-layouts: 2.87 us -> 0.03 us
    ppermute x2, starting transfers between devices: 3.25 us -> 5.75 us  [local_heads(): owned.append(lax.ppermute(part, ('seq', 'wt', 'head'), pairs))]
  transfers between devices with their start and end apart: 9 -> 15, of which waited for: 4 -> 9; matrix products, arithmetic and copies ran while one was open for 0% -> 0% of each run, Pallas kernels for 2% -> 5%
where the time goes in v7:
time: 77.3 us; the launch traced here: 77 us
  waiting for transfers between devices  45.2 us (58%)
  starting transfers between devices  20.5 us (27%)
  Pallas kernels  8.76 us (11%)
  other arithmetic  1.64 us (2%)
  between operations  0.79 us (1%)
    ppermute x6, waiting for transfers between devices, along(): return lax.ppermute(shard, 'seq', [(z, z ^ m) for z in range(4)])  18 us
    ppermute x4, waiting for transfers between devices, local_heads(): moved.append(lax.ppermute(packed[k], ('seq', 'head'), pairs))  15 us
    ppermute x2, waiting for transfers between devices, local_heads(): owned.append(lax.ppermute(part, ('seq', 'wt', 'head'), pairs))  10.3 us
    pallas_call x5, Pallas kernels, call(): pl.pallas_call(kernel, in_specs=[pl.BlockSpec(memory_space=place)] * len(...  8.76 us
    ppermute x6, starting transfers between devices, along(): return lax.ppermute(shard, 'seq', [(z, z ^ m) for z in range(4)])  8.29 us
    ppermute x4, starting transfers between devices, local_heads(): moved.append(lax.ppermute(packed[k], ('seq', 'head'), pairs))  6.01 us
    ppermute x2, starting transfers between devices, local_heads(): owned.append(lax.ppermute(part, ('seq', 'wt', 'head'), pairs))  5.75 us
    ppermute x1, waiting for transfers between devices, local_heads(): sibling = lax.ppermute(joined, 'head', swap)  1.85 us
  transfers between devices with their start and end apart: 15, of which 9 were waited for; matrix products, arithmetic and copies ran while one was open for 0% of the time, Pallas kernels for 5%

profile of v7, /device:TPU:2, one launch (start us, length us, event | category | flops | bytes accessed | tf_op | source)
XLA Modules:
  0.0 77.0 jit_solution(2650879097065897080)
XLA Ops:
  0.6 0.0 copy-start
  0.6 0.1 collective-permute-start.5
  0.7 2.2 %shard_map.95 = (bf16[320,384]{1,0:T(8,128)(2,1)}, bf16[320,384]{1,0:T(8,128)(2,1)}, bf16[160,384]{1,0:T(8,128)(2,1)}, bf16[160,384]{1,0:T(8,128)(2,1)}) custom-call(bf16[160,768]{1,0:T(8,128)(2,1)} %queries.1, bf16[160,768]{1,0:T(8,128)(2,1)} %keys.1, bf16[160,768]{1,0:T(8,128)(2,1)} %values.1), custom_call_target="tpu_custom_call" | custom-call | tf_op jit(solution)/shard_map/pallas_call | solution.py:217
  2.9 1.6 %collective-permute-start = (bf16[320,384]{1,0:T(8,128)(2,1)}, bf16[320,384]{1,0:T(8,128)(2,1)S(1)}, u32[]{:S(2)}, u32[]{:S(2)}) collective-permute-start(bf16[320,384]{1,0:T(8,128)(2,1)} %get-tuple-element.13), channel_id=1, source_target_pairs={{0,0},{1,8},{4,4},{5,12},{8,1},{9,9},{12,5},{13,13},{2,2},{3,10},{... | collective-permute-start | bytes 737288 | tf_op jit(solution)/shard_map/ppermute | solution.py:265
  4.5 1.6 %collective-permute-start.1 = (bf16[320,384]{1,0:T(8,128)(2,1)}, bf16[320,384]{1,0:T(8,128)(2,1)S(1)}, u32[]{:S(2)}, u32[]{:S(2)}) collective-permute-start(bf16[320,384]{1,0:T(8,128)(2,1)} %get-tuple-element.14), channel_id=1, source_target_pairs={{0,4},{1,12},{4,0},{5,8},{8,5},{9,13},{12,1},{13,9},{2,6},{3,14},{... | collective-permute-start | bytes 737288 | tf_op jit(solution)/shard_map/ppermute | solution.py:265
  6.1 2.8 %collective-permute-start.2 = (bf16[160,384]{1,0:T(8,128)(2,1)}, bf16[160,384]{1,0:T(8,128)(2,1)S(1)}, u32[]{:S(2)}, u32[]{:S(2)}) collective-permute-start(bf16[160,384]{1,0:T(8,128)(2,1)} %get-tuple-element.15), channel_id=1, source_target_pairs={{0,1},{1,9},{4,5},{5,13},{8,0},{9,8},{12,4},{13,12},{2,3},{3,11},{... | collective-permute-start | bytes 368648 | tf_op jit(solution)/shard_map/ppermute | solution.py:265
  8.9 0.0 collective-permute-start.3
  8.9 15.0 %collective-permute-done.2.refs_2_ = bf16[160,384]{1,0:T(8,128)(2,1)S(1)} collective-permute-done((bf16[160,384]{1,0:T(8,128)(2,1)}, bf16[160,384]{1,0:T(8,128)(2,1)S(1)}, u32[]{:S(2)}, u32[]{:S(2)}) %collective-permute-start.2) | collective-permute-done | bytes 122912 | tf_op jit(solution)/shard_map/ppermute | solution.py:265
  24.0 0.0 collective-permute-done.3.refs_3_
  24.0 0.0 collective-permute-done.refs_0_
  24.0 0.0 collective-permute-done.1.refs_1_
  24.1 0.0 copy-start.4
  24.1 0.1 collective-permute-start.4
  24.1 1.9 %collective-permute-done.4.refs_4_ = bf16[640,384]{1,0:T(8,128)(2,1)S(1)} collective-permute-done((bf16[640,384]{1,0:T(8,128)(2,1)S(1)}, bf16[640,384]{1,0:T(8,128)(2,1)S(1)}, u32[]{:S(2)}, u32[]{:S(2)}) %collective-permute-start.4) | collective-permute-done | bytes 491552 | tf_op jit(solution)/shard_map/ppermute | solution.py:267
  26.0 1.6 %shard_map.97 = (bf16[160,384]{1,0:T(8,128)(2,1)S(1)}, bf16[160,384]{1,0:T(8,128)(2,1)S(1)}) custom-call(bf16[320,384]{1,0:T(8,128)(2,1)S(1)} %collective-permute-done.refs_0_, bf16[320,384]{1,0:T(8,128)(2,1)S(1)} %collective-permute-done.1.refs_1_, bf16[160,384]{1,0:T(8,128)(2,1)S(1)} %collective-permute-done.2.refs_2_, ...), custom_call_target="tpu_custom_call" | custom-call | flops 314572800 | tf_op jit(solution)/shard_map/pallas_call | solution.py:217
  27.6 0.0 collective-permute-done.5.refs_5_.refs_6_
  27.6 2.5 %collective-permute-start.8 = (bf16[160,384]{1,0:T(8,128)(2,1)S(1)}, bf16[160,384]{1,0:T(8,128)(2,1)S(1)}, u32[]{:S(2)}, u32[]{:S(2)}) collective-permute-start(bf16[160,384]{1,0:T(8,128)(2,1)S(1)} %get-tuple-element.19.refs_0_), channel_id=1, source_target_pairs={{0,12},{4,8},{8,4},{12,0},{1,13},{5,9},{9,5},{13,1},{2,14},{6,10},... | collective-permute-start | bytes 368648 | tf_op jit(solution)/shard_map/ppermute | solution.py:212
  30.1 1.0 %collective-permute-start.9 = (bf16[160,384]{1,0:T(8,128)(2,1)S(1)}, bf16[160,384]{1,0:T(8,128)(2,1)S(1)}, u32[]{:S(2)}, u32[]{:S(2)}) collective-permute-start(bf16[160,384]{1,0:T(8,128)(2,1)S(1)} %get-tuple-element.20.refs_1_), channel_id=1, source_target_pairs={{0,4},{4,0},{8,12},{12,8},{1,5},{5,1},{9,13},{13,9},{2,6},{6,2},{1... | collective-permute-start | bytes 368648 | tf_op jit(solution)/shard_map/ppermute | solution.py:212
  31.1 1.1 %collective-permute-start.6 = (bf16[160,384]{1,0:T(8,128)(2,1)S(1)}, bf16[160,384]{1,0:T(8,128)(2,1)S(1)}, u32[]{:S(2)}, u32[]{:S(2)}) collective-permute-start(bf16[160,384]{1,0:T(8,128)(2,1)S(1)} %get-tuple-element.19.refs_0_), channel_id=1, source_target_pairs={{0,4},{4,0},{8,12},{12,8},{1,5},{5,1},{9,13},{13,9},{2,6},{6,2},{1... | collective-permute-start | bytes 368648 | tf_op jit(solution)/shard_map/ppermute | solution.py:212
  32.1 0.9 %collective-permute-start.7 = (bf16[160,384]{1,0:T(8,128)(2,1)S(1)}, bf16[160,384]{1,0:T(8,128)(2,1)S(1)}, u32[]{:S(2)}, u32[]{:S(2)}) collective-permute-start(bf16[160,384]{1,0:T(8,128)(2,1)S(1)} %get-tuple-element.19.refs_0_), channel_id=1, source_target_pairs={{0,8},{4,12},{8,0},{12,4},{1,9},{5,13},{9,1},{13,5},{2,10},{6,14},... | collective-permute-start | bytes 368648 | tf_op jit(solution)/shard_map/ppermute | solution.py:212
  33.1 2.7 %collective-permute-done.8.refs_3_ = bf16[160,384]{1,0:T(8,128)(2,1)S(1)} collective-permute-done((bf16[160,384]{1,0:T(8,128)(2,1)S(1)}, bf16[160,384]{1,0:T(8,128)(2,1)S(1)}, u32[]{:S(2)}, u32[]{:S(2)}) %collective-permute-start.8) | collective-permute-done | bytes 122912 | tf_op jit(solution)/shard_map/ppermute | solution.py:212
  35.7 4.6 %collective-permute-done.9.refs_2_ = bf16[160,384]{1,0:T(8,128)(2,1)S(1)} collective-permute-done((bf16[160,384]{1,0:T(8,128)(2,1)S(1)}, bf16[160,384]{1,0:T(8,128)(2,1)S(1)}, u32[]{:S(2)}, u32[]{:S(2)}) %collective-permute-start.9) | collective-permute-done | bytes 122912 | tf_op jit(solution)/shard_map/ppermute | solution.py:212
  40.3 2.6 %collective-permute-done.6.refs_1_ = bf16[160,384]{1,0:T(8,128)(2,1)S(1)} collective-permute-done((bf16[160,384]{1,0:T(8,128)(2,1)S(1)}, bf16[160,384]{1,0:T(8,128)(2,1)S(1)}, u32[]{:S(2)}, u32[]{:S(2)}) %collective-permute-start.6) | collective-permute-done | bytes 122912 | tf_op jit(solution)/shard_map/ppermute | solution.py:212
  42.9 0.0 collective-permute-done.7.refs_2_
  42.9 0.0 copy-done
  42.9 2.4 %shard_map.98 = bf16[160,1280]{1,0:T(8,128)(2,1)S(1)} custom-call(bf16[160,384]{1,0:T(8,128)(2,1)S(1)} %get-tuple-element.19.refs_0_, bf16[160,384]{1,0:T(8,128)(2,1)S(1)} %collective-permute-done.6.refs_1_, bf16[160,384]{1,0:T(8,128)(2,1)S(1)} %collective-permute-done.7.refs_2_, bf16[160,384]{1,0:T(8,128)(2,1)S(1)} %collective-permute-done.8.refs_3_, ...), custom_call_target="tpu_custom_call" | custom-call | flops 629145600 | tf_op jit(solution)/shard_map/pallas_call | solution.py:217
  45.3 0.3 collective-permute-start.10
  45.6 1.9 %collective-permute-start.11 = (bf16[160,384]{1,0:T(8,128)(2,1)S(1)}, bf16[160,384]{1,0:T(8,128)(2,1)S(1)}, u32[]{:S(2)}, u32[]{:S(2)}) collective-permute-start(bf16[160,384]{1,0:T(8,128)(2,1)S(1)} %get-tuple-element.20.refs_1_), channel_id=1, source_target_pairs={{0,8},{4,12},{8,0},{12,4},{1,9},{5,13},{9,1},{13,5},{2,10},{6,14},... | collective-permute-start | bytes 368648 | tf_op jit(solution)/shard_map/ppermute | solution.py:212
  47.6 0.9 %collective-permute-start.12 = (bf16[160,384]{1,0:T(8,128)(2,1)S(1)}, bf16[160,384]{1,0:T(8,128)(2,1)S(1)}, u32[]{:S(2)}, u32[]{:S(2)}) collective-permute-start(bf16[160,384]{1,0:T(8,128)(2,1)S(1)} %get-tuple-element.20.refs_1_), channel_id=1, source_target_pairs={{0,12},{4,8},{8,4},{12,0},{1,13},{5,9},{9,5},{13,1},{2,14},{6,10},... | collective-permute-start | bytes 368648 | tf_op jit(solution)/shard_map/ppermute | solution.py:212
  48.5 0.0 copy-done.4
  48.5 0.0 copy-start.1
  48.5 8.2 %collective-permute-done.11.refs_3_ = bf16[160,384]{1,0:T(8,128)(2,1)S(1)} collective-permute-done((bf16[160,384]{1,0:T(8,128)(2,1)S(1)}, bf16[160,384]{1,0:T(8,128)(2,1)S(1)}, u32[]{:S(2)}, u32[]{:S(2)}) %collective-permute-start.11) | collective-permute-done | bytes 122912 | tf_op jit(solution)/shard_map/ppermute | solution.py:212
  56.7 0.0 collective-permute-done.12.refs_4_
  56.7 0.1 collective-permute-done.10.refs_0_
  56.8 2.5 %shard_map.99 = (bf16[80,1280]{1,0:T(8,128)(2,1)S(1)}, bf16[80,1280]{1,0:T(8,128)(2,1)S(1)}) custom-call(bf16[160,1280]{1,0:T(8,128)(2,1)S(1)} %collective-permute-done.10.refs_0_, bf16[160,384]{1,0:T(8,128)(2,1)S(1)} %get-tuple-element.20.refs_1_, bf16[160,384]{1,0:T(8,128)(2,1)S(1)} %collective-permute-done.9.refs_2_, ...), custom_call_target="tpu_custom_call" | custom-call | flops 629145600 | tf_op jit(solution)/shard_map/pallas_call | solution.py:217
  59.2 0.0 copy-start.2
  59.2 0.0 copy-start.3
  59.3 5.7 %collective-permute-start.13 = (bf16[80,1280]{1,0:T(8,128)(2,1)S(1)}, bf16[80,1280]{1,0:T(8,128)(2,1)S(1)}, u32[]{:S(2)}, u32[]{:S(2)}) collective-permute-start(bf16[80,1280]{1,0:T(8,128)(2,1)S(1)} %get-tuple-element.22), channel_id=1, source_target_pairs={{0,0},{1,8},{2,4},{3,12},{4,1},{5,9},{6,5},{7,13},{8,2},{9,10},{10... | collective-permute-start | bytes 614408 | tf_op jit(solution)/shard_map/ppermute | solution.py:307
  64.9 0.1 collective-permute-start.14
  65.0 0.0 copy-done.1
  65.0 0.3 multiply_reduce_fusion
  65.3 7.8 %collective-permute-done.13 = bf16[80,1280]{1,0:T(8,128)(2,1)S(1)} collective-permute-done((bf16[80,1280]{1,0:T(8,128)(2,1)S(1)}, bf16[80,1280]{1,0:T(8,128)(2,1)S(1)}, u32[]{:S(2)}, u32[]{:S(2)}) %collective-permute-start.13) | collective-permute-done | bytes 204832 | tf_op jit(solution)/shard_map/ppermute | solution.py:307
  73.1 2.5 %collective-permute-done.14 = bf16[80,1280]{1,0:T(8,128)(2,1)S(1)} collective-permute-done((bf16[80,1280]{1,0:T(8,128)(2,1)S(1)}, bf16[80,1280]{1,0:T(8,128)(2,1)S(1)}, u32[]{:S(2)}, u32[]{:S(2)}) %collective-permute-start.14) | collective-permute-done | bytes 204832 | tf_op jit(solution)/shard_map/ppermute | solution.py:307
  75.6 0.0 copy-done.2
  75.6 0.0 copy-done.3
  75.6 1.3 %add_add_fusion = (f32[160,1280]{1,0:T(8,128)}, f32[160,1280]{1,0:T(8,128)}) fusion(f32[160,1280]{1,0:T(8,128)S(1)} %copy-done.2, f32[160,1280]{1,0:T(8,128)S(1)} %multiply_reduce_fusion, f32[1280]{0:T(1024)S(1)} %copy-done.3, bf16[80,1280]{1,0:T(8,128)(2,1)S(1)} %get-tuple-element.27, bf16[80,1280]{1,0:T(8,128)(2,1)S(1)} %get-tuple-element.26), kind=kLoop, calls=%fused_computation.2 | loop fusion | flops 1433600 | bytes 3691520 | tf_op jit(solution)/shard_map/add | solution.py:318
  (3 shorter events, 0.1 us)
Async XLA Ops:
  0.6 42.3 %copy-start = (bf16[768,1280]{1,0:T(8,128)(2,1)S(1)}, bf16[768,1280]{1,0:T(8,128)(2,1)}, u32[]{:S(2)}) copy-start(bf16[768,1280]{1,0:T(8,128)(2,1)} %refs_5_.1) | copy-start | bytes 5898244
  0.6 27.0 %collective-permute-start.5 = (bf16[768,1280]{1,0:T(8,128)(2,1)}, bf16[768,1280]{1,0:T(8,128)(2,1)}, u32[]{:S(2)}, u32[]{:S(2)}) collective-permute-start(bf16[768,1280]{1,0:T(8,128)(2,1)} %refs_5_.1), channel_id=1, source_target_pairs={{0,1},{1,0},{2,3},{3,2},{4,5},{5,4},{6,7},{7,6},{8,9},{9,8},{10,11... | collective-permute-start | bytes 5898248 | tf_op jit(solution)/shard_map/ppermute | solution.py:247
  2.9 21.1 %collective-permute-start = (bf16[320,384]{1,0:T(8,128)(2,1)}, bf16[320,384]{1,0:T(8,128)(2,1)S(1)}, u32[]{:S(2)}, u32[]{:S(2)}) collective-permute-start(bf16[320,384]{1,0:T(8,128)(2,1)} %get-tuple-element.13), channel_id=1, source_target_pairs={{0,0},{1,8},{4,4},{5,12},{8,1},{9,9},{12,5},{13,13},{2,2},{3,10},{... | collective-permute-start | bytes 737288 | tf_op jit(solution)/shard_map/ppermute | solution.py:265
  4.5 19.5 %collective-permute-start.1 = (bf16[320,384]{1,0:T(8,128)(2,1)}, bf16[320,384]{1,0:T(8,128)(2,1)S(1)}, u32[]{:S(2)}, u32[]{:S(2)}) collective-permute-start(bf16[320,384]{1,0:T(8,128)(2,1)} %get-tuple-element.14), channel_id=1, source_target_pairs={{0,4},{1,12},{4,0},{5,8},{8,5},{9,13},{12,1},{13,9},{2,6},{3,14},{... | collective-permute-start | bytes 737288 | tf_op jit(solution)/shard_map/ppermute | solution.py:265
  6.1 17.9 %collective-permute-start.2 = (bf16[160,384]{1,0:T(8,128)(2,1)}, bf16[160,384]{1,0:T(8,128)(2,1)S(1)}, u32[]{:S(2)}, u32[]{:S(2)}) collective-permute-start(bf16[160,384]{1,0:T(8,128)(2,1)} %get-tuple-element.15), channel_id=1, source_target_pairs={{0,1},{1,9},{4,5},{5,13},{8,0},{9,8},{12,4},{13,12},{2,3},{3,11},{... | collective-permute-start | bytes 368648 | tf_op jit(solution)/shard_map/ppermute | solution.py:265
  8.9 15.1 %collective-permute-start.3 = (bf16[160,384]{1,0:T(8,128)(2,1)}, bf16[160,384]{1,0:T(8,128)(2,1)S(1)}, u32[]{:S(2)}, u32[]{:S(2)}) collective-permute-start(bf16[160,384]{1,0:T(8,128)(2,1)} %get-tuple-element.16), channel_id=1, source_target_pairs={{0,5},{1,13},{4,1},{5,9},{8,4},{9,12},{12,0},{13,8},{2,7},{3,15},{... | collective-permute-start | bytes 368648 | tf_op jit(solution)/shard_map/ppermute | solution.py:265
  24.1 24.4 %copy-start.4 = (s32[4]{0:T(128)S(1)}, s32[4]{0:T(128)}, u32[]{:S(2)}) copy-start(s32[4]{0:T(128)} %param.15) | copy-start | bytes 52
  24.1 1.9 %collective-permute-start.4 = (bf16[640,384]{1,0:T(8,128)(2,1)S(1)}, bf16[640,384]{1,0:T(8,128)(2,1)S(1)}, u32[]{:S(2)}, u32[]{:S(2)}) collective-permute-start(bf16[640,384]{1,0:T(8,128)(2,1)S(1)} %shard_map.96), channel_id=1, source_target_pairs={{0,1},{1,0},{2,3},{3,2},{4,5},{5,4},{6,7},{7,6},{8,9},{9,8},{10,11... | collective-permute-start | bytes 1474568 | tf_op jit(solution)/shard_map/ppermute | solution.py:267
  27.6 8.1 %collective-permute-start.8 = (bf16[160,384]{1,0:T(8,128)(2,1)S(1)}, bf16[160,384]{1,0:T(8,128)(2,1)S(1)}, u32[]{:S(2)}, u32[]{:S(2)}) collective-permute-start(bf16[160,384]{1,0:T(8,128)(2,1)S(1)} %get-tuple-element.19.refs_0_), channel_id=1, source_target_pairs={{0,12},{4,8},{8,4},{12,0},{1,13},{5,9},{9,5},{13,1},{2,14},{6,10},... | collective-permute-start | bytes 368648 | tf_op jit(solution)/shard_map/ppermute | solution.py:212
  30.1 10.2 %collective-permute-start.9 = (bf16[160,384]{1,0:T(8,128)(2,1)S(1)}, bf16[160,384]{1,0:T(8,128)(2,1)S(1)}, u32[]{:S(2)}, u32[]{:S(2)}) collective-permute-start(bf16[160,384]{1,0:T(8,128)(2,1)S(1)} %get-tuple-element.20.refs_1_), channel_id=1, source_target_pairs={{0,4},{4,0},{8,12},{12,8},{1,5},{5,1},{9,13},{13,9},{2,6},{6,2},{1... | collective-permute-start | bytes 368648 | tf_op jit(solution)/shard_map/ppermute | solution.py:212
  31.1 11.8 %collective-permute-start.6 = (bf16[160,384]{1,0:T(8,128)(2,1)S(1)}, bf16[160,384]{1,0:T(8,128)(2,1)S(1)}, u32[]{:S(2)}, u32[]{:S(2)}) collective-permute-start(bf16[160,384]{1,0:T(8,128)(2,1)S(1)} %get-tuple-element.19.refs_0_), channel_id=1, source_target_pairs={{0,4},{4,0},{8,12},{12,8},{1,5},{5,1},{9,13},{13,9},{2,6},{6,2},{1... | collective-permute-start | bytes 368648 | tf_op jit(solution)/shard_map/ppermute | solution.py:212
  32.1 10.7 %collective-permute-start.7 = (bf16[160,384]{1,0:T(8,128)(2,1)S(1)}, bf16[160,384]{1,0:T(8,128)(2,1)S(1)}, u32[]{:S(2)}, u32[]{:S(2)}) collective-permute-start(bf16[160,384]{1,0:T(8,128)(2,1)S(1)} %get-tuple-element.19.refs_0_), channel_id=1, source_target_pairs={{0,8},{4,12},{8,0},{12,4},{1,9},{5,13},{9,1},{13,5},{2,10},{6,14},... | collective-permute-start | bytes 368648 | tf_op jit(solution)/shard_map/ppermute | solution.py:212
  45.3 11.4 %collective-permute-start.10 = (bf16[160,1280]{1,0:T(8,128)(2,1)S(1)}, bf16[160,1280]{1,0:T(8,128)(2,1)S(1)}, u32[]{:S(2)}, u32[]{:S(2)}) collective-permute-start(bf16[160,1280]{1,0:T(8,128)(2,1)S(1)} %shard_map.98), channel_id=1, source_target_pairs={{0,2},{2,0},{1,3},{3,1},{4,6},{6,4},{5,7},{7,5},{8,10},{10,8},{9,1... | collective-permute-start | bytes 1228808 | tf_op jit(solution)/shard_map/ppermute | solution.py:289
  45.6 11.0 %collective-permute-start.11 = (bf16[160,384]{1,0:T(8,128)(2,1)S(1)}, bf16[160,384]{1,0:T(8,128)(2,1)S(1)}, u32[]{:S(2)}, u32[]{:S(2)}) collective-permute-start(bf16[160,384]{1,0:T(8,128)(2,1)S(1)} %get-tuple-element.20.refs_1_), channel_id=1, source_target_pairs={{0,8},{4,12},{8,0},{12,4},{1,9},{5,13},{9,1},{13,5},{2,10},{6,14},... | collective-permute-start | bytes 368648 | tf_op jit(solution)/shard_map/ppermute | solution.py:212
  47.6 9.1 %collective-permute-start.12 = (bf16[160,384]{1,0:T(8,128)(2,1)S(1)}, bf16[160,384]{1,0:T(8,128)(2,1)S(1)}, u32[]{:S(2)}, u32[]{:S(2)}) collective-permute-start(bf16[160,384]{1,0:T(8,128)(2,1)S(1)} %get-tuple-element.20.refs_1_), channel_id=1, source_target_pairs={{0,12},{4,8},{8,4},{12,0},{1,13},{5,9},{9,5},{13,1},{2,14},{6,10},... | collective-permute-start | bytes 368648 | tf_op jit(solution)/shard_map/ppermute | solution.py:212
  48.5 16.5 %copy-start.1 = (f32[4,160,1280]{2,1,0:T(8,128)S(1)}, f32[4,160,1280]{2,1,0:T(8,128)}, u32[]{:S(2)}) copy-start(f32[4,160,1280]{2,1,0:T(8,128)} %param.14) | copy-start | bytes 9830404
  59.2 16.4 %copy-start.2 = (f32[160,1280]{1,0:T(8,128)S(1)}, f32[160,1280]{1,0:T(8,128)}, u32[]{:S(2)}) copy-start(f32[160,1280]{1,0:T(8,128)} %param.13) | copy-start | bytes 2457604
  59.2 16.4 %copy-start.3 = (f32[1280]{0:T(1024)S(1)}, f32[1280]{0:T(1024)}, u32[]{:S(2)}) copy-start(f32[1280]{0:T(1024)} %param.12) | copy-start | bytes 15364
  59.3 13.8 %collective-permute-start.13 = (bf16[80,1280]{1,0:T(8,128)(2,1)S(1)}, bf16[80,1280]{1,0:T(8,128)(2,1)S(1)}, u32[]{:S(2)}, u32[]{:S(2)}) collective-permute-start(bf16[80,1280]{1,0:T(8,128)(2,1)S(1)} %get-tuple-element.22), channel_id=1, source_target_pairs={{0,0},{1,8},{2,4},{3,12},{4,1},{5,9},{6,5},{7,13},{8,2},{9,10},{10... | collective-permute-start | bytes 614408 | tf_op jit(solution)/shard_map/ppermute | solution.py:307
  64.9 10.6 %collective-permute-start.14 = (bf16[80,1280]{1,0:T(8,128)(2,1)S(1)}, bf16[80,1280]{1,0:T(8,128)(2,1)S(1)}, u32[]{:S(2)}, u32[]{:S(2)}) collective-permute-start(bf16[80,1280]{1,0:T(8,128)(2,1)S(1)} %get-tuple-element.23), channel_id=1, source_target_pairs={{0,4},{1,12},{2,0},{3,8},{4,5},{5,13},{6,1},{7,9},{8,6},{9,14},{10... | collective-permute-start | bytes 614408 | tf_op jit(solution)/shard_map/ppermute | solution.py:307

commit v8 on v7

--- a/solution.py
+++ b/solution.py
@@ -192,12 +192,16 @@
 
 
 def kept_kernel(*refs):
-    arrived, shards, (weight, weight_c, out0, out1, held) = refs[0], refs[1:5], refs[5:]
-    total = multiply(shards, weight, weight_c, held) + arrived[...].astype(jnp.float32)
+    shards, (weight, weight_c, out, held) = refs[:4], refs[4:]
+    out[...] = multiply(shards, weight, weight_c, held)
+
+
+def add_kernel(kept, arrived, out0, out1):
     half = out0.shape[0]
     x = lax.axis_index("wt")
     for low in range(2):
-        part = total[low * half : (low + 1) * half].astype(out0.dtype)
+        at = slice(low * half, (low + 1) * half)
+        part = (kept[at, :] + arrived[at, :].astype(jnp.float32)).astype(out0.dtype)
 
         @pl.when(x == low)
         def _():
@@ -244,8 +248,6 @@
     half = rows // 2
     zl = lax.axis_index("seq") % 2
 
-    weight_c = lax.ppermute(out_weight, "head", swap)
-
     packed = call(
         pack_kernel,
         (queries, key_vectors, value_vectors),
@@ -254,6 +256,8 @@
         far_in=True,
         vmem=PACK_BYTES,
     )
+    late_weight, _ = lax.optimization_barrier((out_weight, packed[0]))
+    weight_c = lax.ppermute(late_weight, "head", swap)
     moved = []
     for k in range(4):
         k1, k0 = k // 2, k % 2
@@ -288,13 +292,14 @@
     )
     arrived = lax.ppermute(send, "wt", swap)
     shards = [parts[1], near] + [along(parts[1], m) for m in (2, 3)]
-    sums = call(
+    (kept,) = call(
         kept_kernel,
-        [arrived] + shards + [out_weight, weight_c],
-        [((half, columns), bf16)] * 2,
+        shards + [out_weight, weight_c],
+        [((rows, columns), jnp.float32)],
         held,
-        flops=flops,
-    )
+        flops=8 * flops,
+    )
+    sums = call(add_kernel, (kept, arrived), [((half, columns), bf16)] * 2)
 
     owned = []
     for p, part in enumerate(sums):

time: 77.3 us -> 74.1 us (0.959)
  Pallas kernels: 8.76 us -> 5.81 us
  local copies, waits for them, and re-layouts: 0.03 us -> 2.86 us
  starting transfers between devices: 20.5 us -> 18 us
  waiting for transfers between devices: 45.2 us -> 43.6 us
    ppermute x6, waiting for transfers between devices: 18 us -> 10.3 us  [along(): return lax.ppermute(shard, 'seq', [(z, z ^ m) for z in range(4)])]
    ppermute x1, waiting for transfers between devices: 0.08 us -> 5.24 us  [local_heads(): arrived = lax.ppermute(send, 'wt', swap)]
    ppermute x2, starting transfers between devices: 5.75 us -> 1.98 us  [local_heads(): owned.append(lax.ppermute(part, ('seq', 'wt', 'head'), pairs))]
    pallas_call x5 -> x6, Pallas kernels: 8.76 us -> 5.81 us  [call(): pl.pallas_call(kernel, in_specs=[pl.BlockSpec(memory_space=place)] * len(...]
    unnamed x10 -> x14, local copies, waits for them, and re-layouts: 0.03 us -> 2.86 us
    ppermute x6, starting transfers between devices: 8.29 us -> 9.49 us  [along(): return lax.ppermute(shard, 'seq', [(z, z ^ m) for z in range(4)])]
    ppermute x2, waiting for transfers between devices: 10.3 us -> 11.2 us  [local_heads(): owned.append(lax.ppermute(part, ('seq', 'wt', 'head'), pairs))]
  transfers between devices with their start and end apart: 15 -> 15, of which waited for: 9 -> 8; matrix products, arithmetic and copies ran while one was open for 0% -> 1% of each run, Pallas kernels for 5% -> 5%
where the time goes in v8:
time: 74.1 us; the launch traced here: 73.4 us
  waiting for transfers between devices  43.6 us (59%)
  starting transfers between devices  18 us (24%)
  Pallas kernels  5.81 us (8%)
  local copies, waits for them, and re-layouts  2.86 us (4%)
  other arithmetic  2.35 us (3%)
  between operations  0.8 us (1%)
    ppermute x4, waiting for transfers between devices, local_heads(): moved.append(lax.ppermute(packed[k], ('seq', 'head'), pairs))  15.1 us
    ppermute x2, waiting for transfers between devices, local_heads(): owned.append(lax.ppermute(part, ('seq', 'wt', 'head'), pairs))  11.2 us
    ppermute x6, waiting for transfers between devices, along(): return lax.ppermute(shard, 'seq', [(z, z ^ m) for z in range(4)])  10.3 us
    ppermute x6, starting transfers between devices, along(): return lax.ppermute(shard, 'seq', [(z, z ^ m) for z in range(4)])  9.49 us
    ppermute x4, starting transfers between devices, local_heads(): moved.append(lax.ppermute(packed[k], ('seq', 'head'), pairs))  6.12 us
    pallas_call x6, Pallas kernels, call(): pl.pallas_call(kernel, in_specs=[pl.BlockSpec(memory_space=place)] * len(...  5.81 us
    ppermute x1, waiting for transfers between devices, local_heads(): arrived = lax.ppermute(send, 'wt', swap)  5.24 us
    unnamed x14, local copies, waits for them, and re-layouts  2.86 us
  transfers between devices with their start and end apart: 15, of which 8 were waited for; matrix products, arithmetic and copies ran while one was open for 1% of the time, Pallas kernels for 5%

profile of v8, /device:TPU:2, one launch (start us, length us, event | category | flops | bytes accessed | tf_op | source)
XLA Modules:
  0.0 73.4 jit_solution(5284858023080538798)
XLA Ops:
  0.6 0.0 copy-start
  0.6 2.2 %shard_map.95 = (bf16[320,384]{1,0:T(8,128)(2,1)}, bf16[320,384]{1,0:T(8,128)(2,1)}, bf16[160,384]{1,0:T(8,128)(2,1)}, bf16[160,384]{1,0:T(8,128)(2,1)}) custom-call(bf16[160,768]{1,0:T(8,128)(2,1)} %queries.1, bf16[160,768]{1,0:T(8,128)(2,1)} %keys.1, bf16[160,768]{1,0:T(8,128)(2,1)} %values.1), custom_call_target="tpu_custom_call" | custom-call | tf_op jit(solution)/shard_map/pallas_call | solution.py:221
  2.9 0.1 collective-permute-start.5
  3.0 1.6 %collective-permute-start = (bf16[320,384]{1,0:T(8,128)(2,1)}, bf16[320,384]{1,0:T(8,128)(2,1)S(1)}, u32[]{:S(2)}, u32[]{:S(2)}) collective-permute-start(bf16[320,384]{1,0:T(8,128)(2,1)} %get-tuple-element.14), channel_id=1, source_target_pairs={{0,0},{1,8},{4,4},{5,12},{8,1},{9,9},{12,5},{13,13},{2,2},{3,10},{... | collective-permute-start | bytes 737288 | tf_op jit(solution)/shard_map/ppermute | solution.py:269
  4.6 1.6 %collective-permute-start.1 = (bf16[320,384]{1,0:T(8,128)(2,1)}, bf16[320,384]{1,0:T(8,128)(2,1)S(1)}, u32[]{:S(2)}, u32[]{:S(2)}) collective-permute-start(bf16[320,384]{1,0:T(8,128)(2,1)} %get-tuple-element.15), channel_id=1, source_target_pairs={{0,4},{1,12},{4,0},{5,8},{8,5},{9,13},{12,1},{13,9},{2,6},{3,14},{... | collective-permute-start | bytes 737288 | tf_op jit(solution)/shard_map/ppermute | solution.py:269
  6.1 2.9 %collective-permute-start.2 = (bf16[160,384]{1,0:T(8,128)(2,1)}, bf16[160,384]{1,0:T(8,128)(2,1)S(1)}, u32[]{:S(2)}, u32[]{:S(2)}) collective-permute-start(bf16[160,384]{1,0:T(8,128)(2,1)} %get-tuple-element.16), channel_id=1, source_target_pairs={{0,1},{1,9},{4,5},{5,13},{8,0},{9,8},{12,4},{13,12},{2,3},{3,11},{... | collective-permute-start | bytes 368648 | tf_op jit(solution)/shard_map/ppermute | solution.py:269
  9.1 0.0 collective-permute-start.3
  9.1 15.1 %collective-permute-done.2.refs_2_ = bf16[160,384]{1,0:T(8,128)(2,1)S(1)} collective-permute-done((bf16[160,384]{1,0:T(8,128)(2,1)}, bf16[160,384]{1,0:T(8,128)(2,1)S(1)}, u32[]{:S(2)}, u32[]{:S(2)}) %collective-permute-start.2) | collective-permute-done | bytes 122912 | tf_op jit(solution)/shard_map/ppermute | solution.py:269
  24.1 0.0 collective-permute-done.3.refs_3_
  24.1 0.0 collective-permute-done.refs_0_
  24.1 0.0 collective-permute-done.1.refs_1_
  24.2 0.1 collective-permute-start.4
  24.3 1.9 %collective-permute-done.4.refs_4_ = bf16[640,384]{1,0:T(8,128)(2,1)S(1)} collective-permute-done((bf16[640,384]{1,0:T(8,128)(2,1)S(1)}, bf16[640,384]{1,0:T(8,128)(2,1)S(1)}, u32[]{:S(2)}, u32[]{:S(2)}) %collective-permute-start.4) | collective-permute-done | bytes 491552 | tf_op jit(solution)/shard_map/ppermute | solution.py:271
  26.1 1.6 %shard_map.97 = (bf16[160,384]{1,0:T(8,128)(2,1)S(1)}, bf16[160,384]{1,0:T(8,128)(2,1)S(1)}) custom-call(bf16[320,384]{1,0:T(8,128)(2,1)S(1)} %collective-permute-done.refs_0_, bf16[320,384]{1,0:T(8,128)(2,1)S(1)} %collective-permute-done.1.refs_1_, bf16[160,384]{1,0:T(8,128)(2,1)S(1)} %collective-permute-done.2.refs_2_, ...), custom_call_target="tpu_custom_call" | custom-call | flops 314572800 | tf_op jit(solution)/shard_map/pallas_call | solution.py:221
  27.8 0.0 collective-permute-done.5.refs_5_
  27.8 0.0 copy-start.1
  27.8 1.3 %copy-done.1 = bf16[768,1280]{1,0:T(8,128)(2,1)} copy-done((bf16[768,1280]{1,0:T(8,128)(2,1)}, bf16[768,1280]{1,0:T(8,128)(2,1)S(1)}, u32[]{:S(2)}) %copy-start.1) | copy-done | bytes 1966104
  29.1 2.3 %collective-permute-start.11 = (bf16[160,384]{1,0:T(8,128)(2,1)S(1)}, bf16[160,384]{1,0:T(8,128)(2,1)S(1)}, u32[]{:S(2)}, u32[]{:S(2)}) collective-permute-start(bf16[160,384]{1,0:T(8,128)(2,1)S(1)} %get-tuple-element.22.refs_0_), channel_id=1, source_target_pairs={{0,12},{4,8},{8,4},{12,0},{1,13},{5,9},{9,5},{13,1},{2,14},{6,10},... | collective-permute-start | bytes 368648 | tf_op jit(solution)/shard_map/ppermute | solution.py:216
  31.4 1.0 %collective-permute-start.6 = (bf16[160,384]{1,0:T(8,128)(2,1)S(1)}, bf16[160,384]{1,0:T(8,128)(2,1)S(1)}, u32[]{:S(2)}, u32[]{:S(2)}) collective-permute-start(bf16[160,384]{1,0:T(8,128)(2,1)S(1)} %get-tuple-element.21.refs_0_), channel_id=1, source_target_pairs={{0,4},{4,0},{8,12},{12,8},{1,5},{5,1},{9,13},{13,9},{2,6},{6,2},{1... | collective-permute-start | bytes 368648 | tf_op jit(solution)/shard_map/ppermute | solution.py:216
  32.3 1.1 %collective-permute-start.10 = (bf16[160,384]{1,0:T(8,128)(2,1)S(1)}, bf16[160,384]{1,0:T(8,128)(2,1)S(1)}, u32[]{:S(2)}, u32[]{:S(2)}) collective-permute-start(bf16[160,384]{1,0:T(8,128)(2,1)S(1)} %get-tuple-element.22.refs_0_), channel_id=1, source_target_pairs={{0,8},{4,12},{8,0},{12,4},{1,9},{5,13},{9,1},{13,5},{2,10},{6,14},... | collective-permute-start | bytes 368648 | tf_op jit(solution)/shard_map/ppermute | solution.py:216
  33.5 1.0 %collective-permute-start.9 = (bf16[160,384]{1,0:T(8,128)(2,1)S(1)}, bf16[160,384]{1,0:T(8,128)(2,1)S(1)}, u32[]{:S(2)}, u32[]{:S(2)}) collective-permute-start(bf16[160,384]{1,0:T(8,128)(2,1)S(1)} %get-tuple-element.22.refs_0_), channel_id=1, source_target_pairs={{0,4},{4,0},{8,12},{12,8},{1,5},{5,1},{9,13},{13,9},{2,6},{6,2},{1... | collective-permute-start | bytes 368648 | tf_op jit(solution)/shard_map/ppermute | solution.py:216
  34.4 1.9 %collective-permute-start.7 = (bf16[160,384]{1,0:T(8,128)(2,1)S(1)}, bf16[160,384]{1,0:T(8,128)(2,1)S(1)}, u32[]{:S(2)}, u32[]{:S(2)}) collective-permute-start(bf16[160,384]{1,0:T(8,128)(2,1)S(1)} %get-tuple-element.21.refs_0_), channel_id=1, source_target_pairs={{0,8},{4,12},{8,0},{12,4},{1,9},{5,13},{9,1},{13,5},{2,10},{6,14},... | collective-permute-start | bytes 368648 | tf_op jit(solution)/shard_map/ppermute | solution.py:216
  36.3 0.8 %collective-permute-done.11.refs_3_ = bf16[160,384]{1,0:T(8,128)(2,1)S(1)} collective-permute-done((bf16[160,384]{1,0:T(8,128)(2,1)S(1)}, bf16[160,384]{1,0:T(8,128)(2,1)S(1)}, u32[]{:S(2)}, u32[]{:S(2)}) %collective-permute-start.11) | collective-permute-done | bytes 122912 | tf_op jit(solution)/shard_map/ppermute | solution.py:216
  37.1 2.3 %collective-permute-start.8 = (bf16[160,384]{1,0:T(8,128)(2,1)S(1)}, bf16[160,384]{1,0:T(8,128)(2,1)S(1)}, u32[]{:S(2)}, u32[]{:S(2)}) collective-permute-start(bf16[160,384]{1,0:T(8,128)(2,1)S(1)} %get-tuple-element.21.refs_0_), channel_id=1, source_target_pairs={{0,12},{4,8},{8,4},{12,0},{1,13},{5,9},{9,5},{13,1},{2,14},{6,10},... | collective-permute-start | bytes 368648 | tf_op jit(solution)/shard_map/ppermute | solution.py:216
  39.4 0.7 convert_element_type.6
  40.0 0.0 collective-permute-done.6.refs_1_
  40.0 5.1 %collective-permute-done.10.refs_2_ = bf16[160,384]{1,0:T(8,128)(2,1)S(1)} collective-permute-done((bf16[160,384]{1,0:T(8,128)(2,1)S(1)}, bf16[160,384]{1,0:T(8,128)(2,1)S(1)}, u32[]{:S(2)}, u32[]{:S(2)}) %collective-permute-start.10) | collective-permute-done | bytes 122912 | tf_op jit(solution)/shard_map/ppermute | solution.py:216
  45.1 0.0 collective-permute-done.9.refs_1_
  45.1 0.0 copy-done
  45.1 1.5 %copy-done.2 = bf16[768,1280]{1,0:T(8,128)(2,1)S(1)} copy-done((bf16[768,1280]{1,0:T(8,128)(2,1)S(1)}, bf16[768,1280]{1,0:T(8,128)(2,1)}, u32[]{:S(2)}) %copy-start.2) | copy-done | bytes 1966104
  46.6 0.9 %shard_map.99 = bf16[160,1280]{1,0:T(8,128)(2,1)S(1)} custom-call(bf16[160,384]{1,0:T(8,128)(2,1)S(1)} %get-tuple-element.22.refs_0_, bf16[160,384]{1,0:T(8,128)(2,1)S(1)} %collective-permute-done.9.refs_1_, bf16[160,384]{1,0:T(8,128)(2,1)S(1)} %collective-permute-done.10.refs_2_, bf16[160,384]{1,0:T(8,128)(2,1)S(1)} %collective-permute-done.11.refs_3_, ...), custom_call_target="tpu_custom_call" | custom-call | flops 629145600 | tf_op jit(solution)/shard_map/pallas_call | solution.py:221
  47.5 0.2 collective-permute-start.12
  47.7 4.4 %collective-permute-done.7.refs_2_ = bf16[160,384]{1,0:T(8,128)(2,1)S(1)} collective-permute-done((bf16[160,384]{1,0:T(8,128)(2,1)S(1)}, bf16[160,384]{1,0:T(8,128)(2,1)S(1)}, u32[]{:S(2)}, u32[]{:S(2)}) %collective-permute-start.7) | collective-permute-done | bytes 122912 | tf_op jit(solution)/shard_map/ppermute | solution.py:216
  52.2 0.0 collective-permute-done.8.refs_3_
  52.2 0.0 copy-done.3
  52.2 0.9 %shard_map.98.kept = f32[160,1280]{1,0:T(8,128)S(1)} custom-call(bf16[160,384]{1,0:T(8,128)(2,1)S(1)} %get-tuple-element.21.refs_0_, bf16[160,384]{1,0:T(8,128)(2,1)S(1)} %collective-permute-done.6.refs_1_, bf16[160,384]{1,0:T(8,128)(2,1)S(1)} %collective-permute-done.7.refs_2_, bf16[160,384]{1,0:T(8,128)(2,1)S(1)} %collective-permute-done.8.refs_3_, ...), custom_call_target="tpu_custom_call" | custom-call | flops 5033164800 | tf_op jit(solution)/shard_map/pallas_call | solution.py:221
  53.1 0.0 copy-start.5
  53.1 0.0 copy-start.6
  53.1 5.2 %collective-permute-done.12.arrived = bf16[160,1280]{1,0:T(8,128)(2,1)S(1)} collective-permute-done((bf16[160,1280]{1,0:T(8,128)(2,1)S(1)}, bf16[160,1280]{1,0:T(8,128)(2,1)S(1)}, u32[]{:S(2)}, u32[]{:S(2)}) %collective-permute-start.12) | collective-permute-done | bytes 409632 | tf_op jit(solution)/shard_map/ppermute | solution.py:293
  58.3 0.1 shard_map.100
  58.5 1.9 %collective-permute-start.13 = (bf16[80,1280]{1,0:T(8,128)(2,1)S(1)}, bf16[80,1280]{1,0:T(8,128)(2,1)S(1)}, u32[]{:S(2)}, u32[]{:S(2)}) collective-permute-start(bf16[80,1280]{1,0:T(8,128)(2,1)S(1)} %get-tuple-element.24), channel_id=1, source_target_pairs={{0,0},{1,8},{2,4},{3,12},{4,1},{5,9},{6,5},{7,13},{8,2},{9,10},{10... | collective-permute-start | bytes 614408 | tf_op jit(solution)/shard_map/ppermute | solution.py:312
  60.4 0.1 collective-permute-start.14
  60.5 0.0 copy-done.4
  60.5 0.3 multiply_reduce_fusion
  60.8 10.5 %collective-permute-done.13 = bf16[80,1280]{1,0:T(8,128)(2,1)S(1)} collective-permute-done((bf16[80,1280]{1,0:T(8,128)(2,1)S(1)}, bf16[80,1280]{1,0:T(8,128)(2,1)S(1)}, u32[]{:S(2)}, u32[]{:S(2)}) %collective-permute-start.13) | collective-permute-done | bytes 204832 | tf_op jit(solution)/shard_map/ppermute | solution.py:312
  71.3 0.7 collective-permute-done.14
  72.0 0.0 copy-done.5
  72.0 1.4 %add_add_fusion = (f32[160,1280]{1,0:T(8,128)}, f32[160,1280]{1,0:T(8,128)}) fusion(f32[160,1280]{1,0:T(8,128)S(1)} %copy-done.5, f32[160,1280]{1,0:T(8,128)S(1)} %multiply_reduce_fusion, f32[1280]{0:T(1024)S(1)} %copy-done.6, bf16[80,1280]{1,0:T(8,128)(2,1)S(1)} %get-tuple-element.29, bf16[80,1280]{1,0:T(8,128)(2,1)S(1)} %get-tuple-element.28), kind=kLoop, calls=%fused_computation.2 | loop fusion | flops 1433600 | bytes 3691520 | tf_op jit(solution)/shard_map/add | solution.py:323
  (6 shorter events, 0.1 us)
Async XLA Ops:
  0.6 44.4 %copy-start = (bf16[768,1280]{1,0:T(8,128)(2,1)S(1)}, bf16[768,1280]{1,0:T(8,128)(2,1)}, u32[]{:S(2)}) copy-start(bf16[768,1280]{1,0:T(8,128)(2,1)} %refs_4_.3) | copy-start | bytes 5898244
  2.9 24.9 %collective-permute-start.5 = (bf16[768,1280]{1,0:T(8,128)(2,1)}, bf16[768,1280]{1,0:T(8,128)(2,1)S(1)}, u32[]{:S(2)}, u32[]{:S(2)}) collective-permute-start(bf16[768,1280]{1,0:T(8,128)(2,1)} %refs_4_.3), channel_id=1, source_target_pairs={{0,1},{1,0},{2,3},{3,2},{4,5},{5,4},{6,7},{7,6},{8,9},{9,8},{10,11... | collective-permute-start | bytes 5898248 | tf_op jit(solution)/shard_map/ppermute | solution.py:260
  3.0 21.2 %collective-permute-start = (bf16[320,384]{1,0:T(8,128)(2,1)}, bf16[320,384]{1,0:T(8,128)(2,1)S(1)}, u32[]{:S(2)}, u32[]{:S(2)}) collective-permute-start(bf16[320,384]{1,0:T(8,128)(2,1)} %get-tuple-element.14), channel_id=1, source_target_pairs={{0,0},{1,8},{4,4},{5,12},{8,1},{9,9},{12,5},{13,13},{2,2},{3,10},{... | collective-permute-start | bytes 737288 | tf_op jit(solution)/shard_map/ppermute | solution.py:269
  4.6 19.6 %collective-permute-start.1 = (bf16[320,384]{1,0:T(8,128)(2,1)}, bf16[320,384]{1,0:T(8,128)(2,1)S(1)}, u32[]{:S(2)}, u32[]{:S(2)}) collective-permute-start(bf16[320,384]{1,0:T(8,128)(2,1)} %get-tuple-element.15), channel_id=1, source_target_pairs={{0,4},{1,12},{4,0},{5,8},{8,5},{9,13},{12,1},{13,9},{2,6},{3,14},{... | collective-permute-start | bytes 737288 | tf_op jit(solution)/shard_map/ppermute | solution.py:269
  6.1 18.0 %collective-permute-start.2 = (bf16[160,384]{1,0:T(8,128)(2,1)}, bf16[160,384]{1,0:T(8,128)(2,1)S(1)}, u32[]{:S(2)}, u32[]{:S(2)}) collective-permute-start(bf16[160,384]{1,0:T(8,128)(2,1)} %get-tuple-element.16), channel_id=1, source_target_pairs={{0,1},{1,9},{4,5},{5,13},{8,0},{9,8},{12,4},{13,12},{2,3},{3,11},{... | collective-permute-start | bytes 368648 | tf_op jit(solution)/shard_map/ppermute | solution.py:269
  9.1 15.1 %collective-permute-start.3 = (bf16[160,384]{1,0:T(8,128)(2,1)}, bf16[160,384]{1,0:T(8,128)(2,1)S(1)}, u32[]{:S(2)}, u32[]{:S(2)}) collective-permute-start(bf16[160,384]{1,0:T(8,128)(2,1)} %get-tuple-element.17), channel_id=1, source_target_pairs={{0,5},{1,13},{4,1},{5,9},{8,4},{9,12},{12,0},{13,8},{2,7},{3,15},{... | collective-permute-start | bytes 368648 | tf_op jit(solution)/shard_map/ppermute | solution.py:269
  24.2 1.9 %collective-permute-start.4 = (bf16[640,384]{1,0:T(8,128)(2,1)S(1)}, bf16[640,384]{1,0:T(8,128)(2,1)S(1)}, u32[]{:S(2)}, u32[]{:S(2)}) collective-permute-start(bf16[640,384]{1,0:T(8,128)(2,1)S(1)} %shard_map.96), channel_id=1, source_target_pairs={{0,1},{1,0},{2,3},{3,2},{4,5},{5,4},{6,7},{7,6},{8,9},{9,8},{10,11... | collective-permute-start | bytes 1474568 | tf_op jit(solution)/shard_map/ppermute | solution.py:271
  27.8 1.3 %copy-start.1 = (bf16[768,1280]{1,0:T(8,128)(2,1)}, bf16[768,1280]{1,0:T(8,128)(2,1)S(1)}, u32[]{:S(2)}) copy-start(bf16[768,1280]{1,0:T(8,128)(2,1)S(1)} %collective-permute-done.5.refs_5_) | copy-start | bytes 5898244
  29.1 8.0 %collective-permute-start.11 = (bf16[160,384]{1,0:T(8,128)(2,1)S(1)}, bf16[160,384]{1,0:T(8,128)(2,1)S(1)}, u32[]{:S(2)}, u32[]{:S(2)}) collective-permute-start(bf16[160,384]{1,0:T(8,128)(2,1)S(1)} %get-tuple-element.22.refs_0_), channel_id=1, source_target_pairs={{0,12},{4,8},{8,4},{12,0},{1,13},{5,9},{9,5},{13,1},{2,14},{6,10},... | collective-permute-start | bytes 368648 | tf_op jit(solution)/shard_map/ppermute | solution.py:216
  31.4 8.7 %collective-permute-start.6 = (bf16[160,384]{1,0:T(8,128)(2,1)S(1)}, bf16[160,384]{1,0:T(8,128)(2,1)S(1)}, u32[]{:S(2)}, u32[]{:S(2)}) collective-permute-start(bf16[160,384]{1,0:T(8,128)(2,1)S(1)} %get-tuple-element.21.refs_0_), channel_id=1, source_target_pairs={{0,4},{4,0},{8,12},{12,8},{1,5},{5,1},{9,13},{13,9},{2,6},{6,2},{1... | collective-permute-start | bytes 368648 | tf_op jit(solution)/shard_map/ppermute | solution.py:216
  32.3 12.7 %collective-permute-start.10 = (bf16[160,384]{1,0:T(8,128)(2,1)S(1)}, bf16[160,384]{1,0:T(8,128)(2,1)S(1)}, u32[]{:S(2)}, u32[]{:S(2)}) collective-permute-start(bf16[160,384]{1,0:T(8,128)(2,1)S(1)} %get-tuple-element.22.refs_0_), channel_id=1, source_target_pairs={{0,8},{4,12},{8,0},{12,4},{1,9},{5,13},{9,1},{13,5},{2,10},{6,14},... | collective-permute-start | bytes 368648 | tf_op jit(solution)/shard_map/ppermute | solution.py:216
  33.5 11.6 %collective-permute-start.9 = (bf16[160,384]{1,0:T(8,128)(2,1)S(1)}, bf16[160,384]{1,0:T(8,128)(2,1)S(1)}, u32[]{:S(2)}, u32[]{:S(2)}) collective-permute-start(bf16[160,384]{1,0:T(8,128)(2,1)S(1)} %get-tuple-element.22.refs_0_), channel_id=1, source_target_pairs={{0,4},{4,0},{8,12},{12,8},{1,5},{5,1},{9,13},{13,9},{2,6},{6,2},{1... | collective-permute-start | bytes 368648 | tf_op jit(solution)/shard_map/ppermute | solution.py:216
  34.4 17.7 %collective-permute-start.7 = (bf16[160,384]{1,0:T(8,128)(2,1)S(1)}, bf16[160,384]{1,0:T(8,128)(2,1)S(1)}, u32[]{:S(2)}, u32[]{:S(2)}) collective-permute-start(bf16[160,384]{1,0:T(8,128)(2,1)S(1)} %get-tuple-element.21.refs_0_), channel_id=1, source_target_pairs={{0,8},{4,12},{8,0},{12,4},{1,9},{5,13},{9,1},{13,5},{2,10},{6,14},... | collective-permute-start | bytes 368648 | tf_op jit(solution)/shard_map/ppermute | solution.py:216
  37.1 15.1 %collective-permute-start.8 = (bf16[160,384]{1,0:T(8,128)(2,1)S(1)}, bf16[160,384]{1,0:T(8,128)(2,1)S(1)}, u32[]{:S(2)}, u32[]{:S(2)}) collective-permute-start(bf16[160,384]{1,0:T(8,128)(2,1)S(1)} %get-tuple-element.21.refs_0_), channel_id=1, source_target_pairs={{0,12},{4,8},{8,4},{12,0},{1,13},{5,9},{9,5},{13,1},{2,14},{6,10},... | collective-permute-start | bytes 368648 | tf_op jit(solution)/shard_map/ppermute | solution.py:216
  45.1 1.5 %copy-start.2 = (bf16[768,1280]{1,0:T(8,128)(2,1)S(1)}, bf16[768,1280]{1,0:T(8,128)(2,1)}, u32[]{:S(2)}) copy-start(bf16[768,1280]{1,0:T(8,128)(2,1)} %copy-done.1) | copy-start | bytes 5898244
  46.6 5.5 %copy-start.3 = (bf16[768,1280]{1,0:T(8,128)(2,1)S(1)}, bf16[768,1280]{1,0:T(8,128)(2,1)}, u32[]{:S(2)}) copy-start(bf16[768,1280]{1,0:T(8,128)(2,1)} %copy-done.1) | copy-start | bytes 5898244
  47.5 10.8 %collective-permute-start.12 = (bf16[160,1280]{1,0:T(8,128)(2,1)S(1)}, bf16[160,1280]{1,0:T(8,128)(2,1)S(1)}, u32[]{:S(2)}, u32[]{:S(2)}) collective-permute-start(bf16[160,1280]{1,0:T(8,128)(2,1)S(1)} %shard_map.99), channel_id=1, source_target_pairs={{0,2},{2,0},{1,3},{3,1},{4,6},{6,4},{5,7},{7,5},{8,10},{10,8},{9,1... | collective-permute-start | bytes 1228808 | tf_op jit(solution)/shard_map/ppermute | solution.py:293
  52.2 8.3 %copy-start.4 = (f32[4,160,1280]{2,1,0:T(8,128)S(1)}, f32[4,160,1280]{2,1,0:T(8,128)}, u32[]{:S(2)}) copy-start(f32[4,160,1280]{2,1,0:T(8,128)} %param.14) | copy-start | bytes 9830404
  53.1 18.9 %copy-start.5 = (f32[160,1280]{1,0:T(8,128)S(1)}, f32[160,1280]{1,0:T(8,128)}, u32[]{:S(2)}) copy-start(f32[160,1280]{1,0:T(8,128)} %param.13) | copy-start | bytes 2457604
  53.1 18.9 %copy-start.6 = (f32[1280]{0:T(1024)S(1)}, f32[1280]{0:T(1024)}, u32[]{:S(2)}) copy-start(f32[1280]{0:T(1024)} %param.12) | copy-start | bytes 15364
  58.5 12.8 %collective-permute-start.13 = (bf16[80,1280]{1,0:T(8,128)(2,1)S(1)}, bf16[80,1280]{1,0:T(8,128)(2,1)S(1)}, u32[]{:S(2)}, u32[]{:S(2)}) collective-permute-start(bf16[80,1280]{1,0:T(8,128)(2,1)S(1)} %get-tuple-element.24), channel_id=1, source_target_pairs={{0,0},{1,8},{2,4},{3,12},{4,1},{5,9},{6,5},{7,13},{8,2},{9,10},{10... | collective-permute-start | bytes 614408 | tf_op jit(solution)/shard_map/ppermute | solution.py:312
  60.4 11.6 %collective-permute-start.14 = (bf16[80,1280]{1,0:T(8,128)(2,1)S(1)}, bf16[80,1280]{1,0:T(8,128)(2,1)S(1)}, u32[]{:S(2)}, u32[]{:S(2)}) collective-permute-start(bf16[80,1280]{1,0:T(8,128)(2,1)S(1)} %get-tuple-element.25), channel_id=1, source_target_pairs={{0,4},{1,12},{2,0},{3,8},{4,5},{5,13},{6,1},{7,9},{8,6},{9,14},{10... | collective-permute-start | bytes 614408 | tf_op jit(solution)/shard_map/ppermute | solution.py:312

commit v9 on v8

--- a/solution.py
+++ b/solution.py
@@ -128,8 +128,8 @@
 
 def attention_kernel(*refs):
     blocks, sibling = refs[:4], refs[4]
-    sent, kept, key_all, value_all, query_all = refs[5:]
-    rows = sent.shape[0]
+    outs, key_all, value_all, query_all = refs[5:7], refs[7], refs[8], refs[9]
+    rows = outs[0].shape[0]
     half = rows // 2
     for k in range(4):
         here, there = slice(k * half, (k + 1) * half), slice((4 + k) * half, (5 + k) * half)
@@ -137,16 +137,11 @@
         value_all[here, :] = blocks[k][half:rows, :]
         key_all[there, :] = sibling[k * rows : k * rows + half, :]
         value_all[there, :] = sibling[k * rows + half : (k + 1) * rows, :]
-    _, zl = bits()
     x = lax.axis_index("wt")
     for k in range(2):
-        for part in range(2):
-            at = rows + flip(x, part == 0) * half
-            to = (part * 2 + flip(zl, k)) * half
-            query_all[pl.ds(pl.multiple_of(to, 16), half), :] = blocks[k][
-                pl.ds(pl.multiple_of(at, 16), half), :
-            ]
-    for h in range(sent.shape[1] // HEAD_DIM):
+        at = pl.ds(pl.multiple_of(flip(x, k) * rows, 16), rows)
+        query_all[at, :] = blocks[k][rows:, :]
+    for h in range(outs[0].shape[1] // HEAD_DIM):
         columns = slice(h * HEAD_DIM, (h + 1) * HEAD_DIM)
         scores = lax.dot_general(
             query_all[:, columns],
@@ -160,9 +155,9 @@
         result = jnp.dot(
             weights.astype(jnp.bfloat16), value_all[:, columns], preferred_element_type=jnp.float32
         )
-        result = (result / total).astype(sent.dtype)
-        sent[:, columns] = result[:rows]
-        kept[:, columns] = result[rows:]
+        result = (result / total).astype(outs[0].dtype)
+        for part, out in enumerate(outs):
+            out[:, columns] = result[part * rows : (part + 1) * rows]
 
 
 def multiply(shards, weight, weight_c, held):
@@ -196,31 +191,32 @@
     out[...] = multiply(shards, weight, weight_c, held)
 
 
-def add_kernel(kept, arrived, out0, out1):
-    half = out0.shape[0]
-    x = lax.axis_index("wt")
-    for low in range(2):
-        at = slice(low * half, (low + 1) * half)
-        part = (kept[at, :] + arrived[at, :].astype(jnp.float32)).astype(out0.dtype)
-
-        @pl.when(x == low)
-        def _():
-            out0[...] = part
-
-        @pl.when(x != low)
-        def _():
-            out1[...] = part
+def add_kernel(kept, arrived, out):
+    out[...] = (kept[...] + arrived[...].astype(jnp.float32)).astype(out.dtype)
+
+
+def rest_kernel(flags, hidden, cached, out):
+    total = hidden[...]
+    for layer in range(cached.shape[0]):
+        total = total + flags[layer].astype(jnp.float32) * cached[layer]
+    out[...] = total
+
+
+def final_kernel(owned, gate, resting, mixed, fresh):
+    delta = owned[...].astype(jnp.float32) * gate[...]
+    fresh[...] = delta
+    mixed[...] = resting[...] + delta
 
 
 def along(shard, m):
     return lax.ppermute(shard, "seq", [(z, z ^ m) for z in range(4)])
 
 
-def call(kernel, args, outs, scratch=(), far_in=False, flops=0, vmem=VMEM_BYTES):
-    place = pl.ANY if far_in else pltpu.VMEM
+def call(kernel, args, outs, scratch=(), space=pltpu.VMEM, flops=0, vmem=VMEM_BYTES):
+    spaces = [pltpu.SMEM if arg.dtype == jnp.int32 else space for arg in args]
     return pl.pallas_call(
         kernel,
-        in_specs=[pl.BlockSpec(memory_space=place)] * len(args),
+        in_specs=[pl.BlockSpec(memory_space=place) for place in spaces],
         out_specs=[pl.BlockSpec(memory_space=pltpu.VMEM)] * len(outs),
         out_shape=[jax.ShapeDtypeStruct(shape, dtype) for shape, dtype in outs],
         scratch_shapes=list(scratch),
@@ -245,15 +241,12 @@
     swap = [(0, 1), (1, 0)]
     bf16 = jnp.bfloat16
 
-    half = rows // 2
-    zl = lax.axis_index("seq") % 2
-
     packed = call(
         pack_kernel,
         (queries, key_vectors, value_vectors),
         [((2 * rows, width), bf16)] * 2 + [((rows, width), bf16)] * 2,
         [pltpu.SemaphoreType.DMA((10,))],
-        far_in=True,
+        space=pl.ANY,
         vmem=PACK_BYTES,
     )
     late_weight, _ = lax.optimization_barrier((out_weight, packed[0]))
@@ -269,6 +262,7 @@
         moved.append(lax.ppermute(packed[k], ("seq", "head"), pairs))
     (joined,) = call(join_kernel, moved, [((4 * rows, width), bf16)])
     sibling = lax.ppermute(joined, "head", swap)
+    sibling, _ = lax.optimization_barrier((sibling, weight_c))
     parts = call(
         attention_kernel,
         moved + [sibling],
@@ -283,45 +277,47 @@
 
     flops = 4 * rows * depth * columns
     held = [pltpu.VMEM((4 * rows, width), bf16)]
-    first, second, _ = lax.optimization_barrier((parts[0], parts[1], weight_c))
-    shards = [first] + [along(first, m) for m in (1, 2, 3)]
-    near = along(second, 1)
-    shards[3], _ = lax.optimization_barrier((shards[3], near))
+    gathers = []
+    for kept in range(2):
+        shards = [parts[1 - kept]]
+        for m in range(1, 4):
+            pairs = [(z, z ^ m) for z in range(4)]
+            shards.append(lax.ppermute(parts[(1 - kept) ^ (m % 2)], "seq", pairs))
+        gathers.append(shards)
     (send,) = call(
-        sent_kernel, shards + [out_weight, weight_c], [((rows, columns), bf16)], held, flops=flops
+        sent_kernel,
+        gathers[0] + [out_weight, weight_c],
+        [((rows, columns), bf16)],
+        held,
+        flops=flops,
     )
     arrived = lax.ppermute(send, "wt", swap)
-    shards = [parts[1], near] + [along(parts[1], m) for m in (2, 3)]
     (kept,) = call(
         kept_kernel,
-        shards + [out_weight, weight_c],
+        gathers[1] + [out_weight, weight_c],
         [((rows, columns), jnp.float32)],
         held,
         flops=8 * flops,
     )
-    sums = call(add_kernel, (kept, arrived), [((half, columns), bf16)] * 2)
-
-    owned = []
-    for p, part in enumerate(sums):
-        pairs = []
-        for zz in range(4):
-            for xx in range(2):
-                for cc in range(2):
-                    to = ((2 * cc + (p ^ xx)) * 2 + zz // 2) * 2 + zz % 2
-                    pairs.append(((zz * 2 + xx) * 2 + cc, to))
-        owned.append(lax.ppermute(part, ("seq", "wt", "head"), pairs))
-    head_total = jnp.concatenate(
-        [
-            jnp.where(zl == 0, owned[0], owned[1]),
-            jnp.where(zl == 0, owned[1], owned[0]),
-        ],
-        axis=0,
-    ).astype(jnp.float32)
-    kept_deltas = jnp.sum(skip_flags.astype(jnp.float32)[:, None, None] * cached_deltas, axis=0)
-    resting = hidden_state + kept_deltas
-    fresh_delta = head_total * gate_values[None, :]
-    mixed_state = resting + fresh_delta
-    return (mixed_state, fresh_delta)
+    (summed,) = call(add_kernel, (kept, arrived), [((rows, columns), bf16)])
+
+    pairs = []
+    for zz in range(4):
+        for xx in range(2):
+            for cc in range(2):
+                to = ((2 * cc + (xx ^ (zz % 2))) * 2 + zz // 2) * 2 + zz % 2
+                pairs.append(((zz * 2 + xx) * 2 + cc, to))
+    owned = lax.ppermute(summed, ("seq", "wt", "head"), pairs)
+    (resting,) = call(
+        rest_kernel, (skip_flags, hidden_state, cached_deltas), [((rows, columns), jnp.float32)]
+    )
+    return tuple(
+        call(
+            final_kernel,
+            (owned, gate_values[None, :], resting),
+            [((rows, columns), jnp.float32)] * 2,
+        )
+    )
 
 
 def solution(mesh):

time: 74.1 us -> 70.7 us (0.954)
  local copies, waits for them, and re-layouts: 2.86 us -> 0.03 us
  other arithmetic: 2.35 us -> 0 us
  Pallas kernels: 5.81 us -> 7.74 us
  starting transfers between devices: 18 us -> 19.6 us
  waiting for transfers between devices: 43.6 us -> 42.3 us
    ppermute x1, waiting for transfers between devices: 5.24 us -> 1.92 us  [local_heads(): arrived = lax.ppermute(send, 'wt', swap)]
    unnamed x14 -> x10, local copies, waits for them, and re-layouts: 2.86 us -> 0.03 us
    ppermute x8 -> x7, waiting for transfers between devices: 21.4 us -> 23.5 us  [the longest x6 12.1 us: local_heads(): shards.append(lax.ppermute(parts[1 - kept ^ m % 2], 'seq', pairs))]
    pallas_call x6 -> x8, Pallas kernels: 5.81 us -> 7.74 us  [call(): pl.pallas_call(kernel, in_specs=[pl.BlockSpec(memory_space=place) for pla...]
    add x1 -> x0, other arithmetic: 1.37 us -> none  [local_heads(): mixed_state = resting + fresh_delta]
    ppermute x8 -> x7, starting transfers between devices: 11.5 us -> 12.8 us  [the longest x6 9.46 us: local_heads(): shards.append(lax.ppermute(parts[1 - kept ^ m % 2], 'seq', pairs))]
  transfers between devices with their start and end apart: 15 -> 14, of which waited for: 8 -> 8; matrix products, arithmetic and copies ran while one was open for 1% -> 0% of each run, Pallas kernels for 5% -> 4%
where the time goes in v9:
time: 70.7 us; the launch traced here: 70.5 us
  waiting for transfers between devices  42.3 us (60%)
  starting transfers between devices  19.6 us (28%)
  Pallas kernels  7.74 us (11%)
  between operations  0.79 us (1%)
    ppermute x4, waiting for transfers between devices, local_heads(): moved.append(lax.ppermute(packed[k], ('seq', 'head'), pairs))  15.1 us
    ppermute x6, waiting for transfers between devices, local_heads(): shards.append(lax.ppermute(parts[1 - kept ^ m % 2], 'seq', pairs))  12.1 us
    ppermute x1, waiting for transfers between devices, local_heads(): owned = lax.ppermute(summed, ('seq', 'wt', 'head'), pairs)  11.4 us
    ppermute x6, starting transfers between devices, local_heads(): shards.append(lax.ppermute(parts[1 - kept ^ m % 2], 'seq', pairs))  9.46 us
    pallas_call x8, Pallas kernels, call(): pl.pallas_call(kernel, in_specs=[pl.BlockSpec(memory_space=place) for pla...  7.74 us
    ppermute x4, starting transfers between devices, local_heads(): moved.append(lax.ppermute(packed[k], ('seq', 'head'), pairs))  6.12 us
    ppermute x1, starting transfers between devices, local_heads(): owned = lax.ppermute(summed, ('seq', 'wt', 'head'), pairs)  3.37 us
    ppermute x1, waiting for transfers between devices, local_heads(): arrived = lax.ppermute(send, 'wt', swap)  1.92 us
  transfers between devices with their start and end apart: 14, of which 8 were waited for; matrix products, arithmetic and copies ran while one was open for 0% of the time, Pallas kernels for 4%

profile of v9, /device:TPU:2, one launch (start us, length us, event | category | flops | bytes accessed | tf_op | source)
XLA Modules:
  0.0 70.5 jit_solution(2150826947495087342)
XLA Ops:
  0.6 0.0 copy-start.1
  0.6 2.2 %shard_map.95 = (bf16[320,384]{1,0:T(8,128)(2,1)}, bf16[320,384]{1,0:T(8,128)(2,1)}, bf16[160,384]{1,0:T(8,128)(2,1)}, bf16[160,384]{1,0:T(8,128)(2,1)}) custom-call(bf16[160,768]{1,0:T(8,128)(2,1)} %queries.1, bf16[160,768]{1,0:T(8,128)(2,1)} %keys.1, bf16[160,768]{1,0:T(8,128)(2,1)} %values.1), custom_call_target="tpu_custom_call" | custom-call | tf_op jit(solution)/shard_map/pallas_call | solution.py:217
  2.9 0.1 collective-permute-start.5
  3.0 1.6 %collective-permute-start = (bf16[320,384]{1,0:T(8,128)(2,1)}, bf16[320,384]{1,0:T(8,128)(2,1)S(1)}, u32[]{:S(2)}, u32[]{:S(2)}) collective-permute-start(bf16[320,384]{1,0:T(8,128)(2,1)} %get-tuple-element.10), channel_id=1, source_target_pairs={{0,0},{1,8},{4,4},{5,12},{8,1},{9,9},{12,5},{13,13},{2,2},{3,10},{... | collective-permute-start | bytes 737288 | tf_op jit(solution)/shard_map/ppermute | solution.py:262
  4.6 1.6 %collective-permute-start.1 = (bf16[320,384]{1,0:T(8,128)(2,1)}, bf16[320,384]{1,0:T(8,128)(2,1)S(1)}, u32[]{:S(2)}, u32[]{:S(2)}) collective-permute-start(bf16[320,384]{1,0:T(8,128)(2,1)} %get-tuple-element.11), channel_id=1, source_target_pairs={{0,4},{1,12},{4,0},{5,8},{8,5},{9,13},{12,1},{13,9},{2,6},{3,14},{... | collective-permute-start | bytes 737288 | tf_op jit(solution)/shard_map/ppermute | solution.py:262
  6.2 2.9 %collective-permute-start.2 = (bf16[160,384]{1,0:T(8,128)(2,1)}, bf16[160,384]{1,0:T(8,128)(2,1)S(1)}, u32[]{:S(2)}, u32[]{:S(2)}) collective-permute-start(bf16[160,384]{1,0:T(8,128)(2,1)} %get-tuple-element.12), channel_id=1, source_target_pairs={{0,1},{1,9},{4,5},{5,13},{8,0},{9,8},{12,4},{13,12},{2,3},{3,11},{... | collective-permute-start | bytes 368648 | tf_op jit(solution)/shard_map/ppermute | solution.py:262
  9.1 0.0 collective-permute-start.3
  9.1 15.1 %collective-permute-done.2.refs_2_ = bf16[160,384]{1,0:T(8,128)(2,1)S(1)} collective-permute-done((bf16[160,384]{1,0:T(8,128)(2,1)}, bf16[160,384]{1,0:T(8,128)(2,1)S(1)}, u32[]{:S(2)}, u32[]{:S(2)}) %collective-permute-start.2) | collective-permute-done | bytes 122912 | tf_op jit(solution)/shard_map/ppermute | solution.py:262
  24.2 0.0 collective-permute-done.3.refs_3_
  24.2 0.0 collective-permute-done.refs_0_
  24.2 0.0 collective-permute-done.1.refs_1_
  24.2 0.1 collective-permute-start.4
  24.3 1.9 %collective-permute-done.4.refs_4_ = bf16[640,384]{1,0:T(8,128)(2,1)S(1)} collective-permute-done((bf16[640,384]{1,0:T(8,128)(2,1)S(1)}, bf16[640,384]{1,0:T(8,128)(2,1)S(1)}, u32[]{:S(2)}, u32[]{:S(2)}) %collective-permute-start.4) | collective-permute-done | bytes 491552 | tf_op jit(solution)/shard_map/ppermute | solution.py:264
  26.1 0.0 collective-permute-done.5.refs_5_
  26.2 1.6 %shard_map.97 = (bf16[160,384]{1,0:T(8,128)(2,1)S(1)}, bf16[160,384]{1,0:T(8,128)(2,1)S(1)}) custom-call(bf16[320,384]{1,0:T(8,128)(2,1)S(1)} %collective-permute-done.refs_0_, bf16[320,384]{1,0:T(8,128)(2,1)S(1)} %collective-permute-done.1.refs_1_, bf16[160,384]{1,0:T(8,128)(2,1)S(1)} %collective-permute-done.2.refs_2_, ...), custom_call_target="tpu_custom_call" | custom-call | flops 314572800 | tf_op jit(solution)/shard_map/pallas_call | solution.py:217
  27.8 2.7 %collective-permute-start.10 = (bf16[160,384]{1,0:T(8,128)(2,1)S(1)}, bf16[160,384]{1,0:T(8,128)(2,1)S(1)}, u32[]{:S(2)}, u32[]{:S(2)}) collective-permute-start(bf16[160,384]{1,0:T(8,128)(2,1)S(1)} %get-tuple-element.17.refs_0_), channel_id=1, source_target_pairs={{0,8},{4,12},{8,0},{12,4},{1,9},{5,13},{9,1},{13,5},{2,10},{6,14},... | collective-permute-start | bytes 368648 | tf_op jit(solution)/shard_map/ppermute | solution.py:285
  30.5 1.5 %collective-permute-start.11 = (bf16[160,384]{1,0:T(8,128)(2,1)S(1)}, bf16[160,384]{1,0:T(8,128)(2,1)S(1)}, u32[]{:S(2)}, u32[]{:S(2)}) collective-permute-start(bf16[160,384]{1,0:T(8,128)(2,1)S(1)} %get-tuple-element.16.refs_0_), channel_id=1, source_target_pairs={{0,12},{4,8},{8,4},{12,0},{1,13},{5,9},{9,5},{13,1},{2,14},{6,10},... | collective-permute-start | bytes 368648 | tf_op jit(solution)/shard_map/ppermute | solution.py:285
  32.1 0.0 collective-permute-start.9
  32.1 2.0 %collective-permute-start.6 = (bf16[160,384]{1,0:T(8,128)(2,1)S(1)}, bf16[160,384]{1,0:T(8,128)(2,1)S(1)}, u32[]{:S(2)}, u32[]{:S(2)}) collective-permute-start(bf16[160,384]{1,0:T(8,128)(2,1)S(1)} %get-tuple-element.17.refs_0_), channel_id=1, source_target_pairs={{0,4},{4,0},{8,12},{12,8},{1,5},{5,1},{9,13},{13,9},{2,6},{6,2},{1... | collective-permute-start | bytes 368648 | tf_op jit(solution)/shard_map/ppermute | solution.py:285
  34.1 0.8 %collective-permute-start.7 = (bf16[160,384]{1,0:T(8,128)(2,1)S(1)}, bf16[160,384]{1,0:T(8,128)(2,1)S(1)}, u32[]{:S(2)}, u32[]{:S(2)}) collective-permute-start(bf16[160,384]{1,0:T(8,128)(2,1)S(1)} %get-tuple-element.16.refs_0_), channel_id=1, source_target_pairs={{0,8},{4,12},{8,0},{12,4},{1,9},{5,13},{9,1},{13,5},{2,10},{6,14},... | collective-permute-start | bytes 368648 | tf_op jit(solution)/shard_map/ppermute | solution.py:285
  35.0 5.2 %collective-permute-done.10.refs_2_ = bf16[160,384]{1,0:T(8,128)(2,1)S(1)} collective-permute-done((bf16[160,384]{1,0:T(8,128)(2,1)S(1)}, bf16[160,384]{1,0:T(8,128)(2,1)S(1)}, u32[]{:S(2)}, u32[]{:S(2)}) %collective-permute-start.10) | collective-permute-done | bytes 122912 | tf_op jit(solution)/shard_map/ppermute | solution.py:285
  40.2 2.3 %collective-permute-start.8 = (bf16[160,384]{1,0:T(8,128)(2,1)S(1)}, bf16[160,384]{1,0:T(8,128)(2,1)S(1)}, u32[]{:S(2)}, u32[]{:S(2)}) collective-permute-start(bf16[160,384]{1,0:T(8,128)(2,1)S(1)} %get-tuple-element.17.refs_0_), channel_id=1, source_target_pairs={{0,12},{4,8},{8,4},{12,0},{1,13},{5,9},{9,5},{13,1},{2,14},{6,10},... | collective-permute-start | bytes 368648 | tf_op jit(solution)/shard_map/ppermute | solution.py:285
  42.5 0.0 collective-permute-done.11.refs_3_
  42.5 0.1 collective-permute-done.9.refs_1_
  42.6 0.0 copy-done.1
  42.6 0.9 %shard_map.99 = bf16[160,1280]{1,0:T(8,128)(2,1)S(1)} custom-call(bf16[160,384]{1,0:T(8,128)(2,1)S(1)} %get-tuple-element.17.refs_0_, bf16[160,384]{1,0:T(8,128)(2,1)S(1)} %collective-permute-done.9.refs_1_, bf16[160,384]{1,0:T(8,128)(2,1)S(1)} %collective-permute-done.10.refs_2_, bf16[160,384]{1,0:T(8,128)(2,1)S(1)} %collective-permute-done.11.refs_3_, ...), custom_call_target="tpu_custom_call" | custom-call | flops 629145600 | tf_op jit(solution)/shard_map/pallas_call | solution.py:217
  43.4 0.0 copy-start.4
  43.5 0.0 copy-start.3
  43.5 0.5 collective-permute-start.12
  44.0 0.8 %collective-permute-done.6.refs_1_ = bf16[160,384]{1,0:T(8,128)(2,1)S(1)} collective-permute-done((bf16[160,384]{1,0:T(8,128)(2,1)S(1)}, bf16[160,384]{1,0:T(8,128)(2,1)S(1)}, u32[]{:S(2)}, u32[]{:S(2)}) %collective-permute-start.6) | collective-permute-done | bytes 122912 | tf_op jit(solution)/shard_map/ppermute | solution.py:285
  44.8 5.9 %collective-permute-done.7.refs_2_ = bf16[160,384]{1,0:T(8,128)(2,1)S(1)} collective-permute-done((bf16[160,384]{1,0:T(8,128)(2,1)S(1)}, bf16[160,384]{1,0:T(8,128)(2,1)S(1)}, u32[]{:S(2)}, u32[]{:S(2)}) %collective-permute-start.7) | collective-permute-done | bytes 122912 | tf_op jit(solution)/shard_map/ppermute | solution.py:285
  50.7 0.0 collective-permute-done.8.refs_3_
  50.7 0.0 copy-start
  50.7 0.9 %shard_map.98.kept = f32[160,1280]{1,0:T(8,128)S(1)} custom-call(bf16[160,384]{1,0:T(8,128)(2,1)S(1)} %get-tuple-element.16.refs_0_, bf16[160,384]{1,0:T(8,128)(2,1)S(1)} %collective-permute-done.6.refs_1_, bf16[160,384]{1,0:T(8,128)(2,1)S(1)} %collective-permute-done.7.refs_2_, bf16[160,384]{1,0:T(8,128)(2,1)S(1)} %collective-permute-done.8.refs_3_, ...), custom_call_target="tpu_custom_call" | custom-call | flops 5033164800 | tf_op jit(solution)/shard_map/pallas_call | solution.py:217
  51.6 0.0 copy-start.2
  51.6 1.9 %collective-permute-done.12.arrived = bf16[160,1280]{1,0:T(8,128)(2,1)S(1)} collective-permute-done((bf16[160,1280]{1,0:T(8,128)(2,1)S(1)}, bf16[160,1280]{1,0:T(8,128)(2,1)S(1)}, u32[]{:S(2)}, u32[]{:S(2)}) %collective-permute-start.12) | collective-permute-done | bytes 409632 | tf_op jit(solution)/shard_map/ppermute | solution.py:294
  53.5 0.1 shard_map.100
  53.6 3.4 %collective-permute-start.13 = (bf16[160,1280]{1,0:T(8,128)(2,1)S(1)}, bf16[160,1280]{1,0:T(8,128)(2,1)S(1)}, u32[]{:S(2)}, u32[]{:S(2)}) collective-permute-start(bf16[160,1280]{1,0:T(8,128)(2,1)S(1)} %shard_map.100), channel_id=1, source_target_pairs={{0,0},{1,8},{2,4},{3,12},{4,5},{5,13},{6,1},{7,9},{8,2},{9,10},{10... | collective-permute-start | bytes 1228808 | tf_op jit(solution)/shard_map/ppermute | solution.py:310
  57.0 0.0 copy-done.4
  57.0 0.0 copy-done.3
  57.0 0.0 copy-done
  57.0 0.0 copy-done.2
  57.0 0.8 %shard_map.101.resting = f32[160,1280]{1,0:T(8,128)S(1)} custom-call(s32[4]{0:T(128)S(1)} %copy-done.3, f32[160,1280]{1,0:T(8,128)S(1)} %copy-done.2, f32[4,160,1280]{2,1,0:T(8,128)S(1)} %copy-done), custom_call_target="tpu_custom_call" | custom-call | tf_op jit(solution)/shard_map/pallas_call | solution.py:217
  57.8 11.4 %collective-permute-done.13.owned = bf16[160,1280]{1,0:T(8,128)(2,1)S(1)} collective-permute-done((bf16[160,1280]{1,0:T(8,128)(2,1)S(1)}, bf16[160,1280]{1,0:T(8,128)(2,1)S(1)}, u32[]{:S(2)}, u32[]{:S(2)}) %collective-permute-start.13) | collective-permute-done | bytes 409632 | tf_op jit(solution)/shard_map/ppermute | solution.py:310
  69.2 1.3 %shard_map.102 = (f32[160,1280]{1,0:T(8,128)}, f32[160,1280]{1,0:T(8,128)}) custom-call(bf16[160,1280]{1,0:T(8,128)(2,1)S(1)} %collective-permute-done.13.owned, f32[1,1280]{1,0:T(1,128)S(1)} %broadcast_in_dim.3.gate, f32[160,1280]{1,0:T(8,128)S(1)} %shard_map.101.resting), custom_call_target="tpu_custom_call" | custom-call | tf_op jit(solution)/shard_map/pallas_call | solution.py:217
  (2 shorter events, 0.1 us)
Async XLA Ops:
  0.6 41.9 %copy-start.1 = (bf16[768,1280]{1,0:T(8,128)(2,1)S(1)}, bf16[768,1280]{1,0:T(8,128)(2,1)}, u32[]{:S(2)}) copy-start(bf16[768,1280]{1,0:T(8,128)(2,1)} %refs_4_.3) | copy-start | bytes 5898244
  2.9 23.3 %collective-permute-start.5 = (bf16[768,1280]{1,0:T(8,128)(2,1)}, bf16[768,1280]{1,0:T(8,128)(2,1)S(1)}, u32[]{:S(2)}, u32[]{:S(2)}) collective-permute-start(bf16[768,1280]{1,0:T(8,128)(2,1)} %refs_4_.3), channel_id=1, source_target_pairs={{0,1},{1,0},{2,3},{3,2},{4,5},{5,4},{6,7},{7,6},{8,9},{9,8},{10,11... | collective-permute-start | bytes 5898248 | tf_op jit(solution)/shard_map/ppermute | solution.py:253
  3.0 21.2 %collective-permute-start = (bf16[320,384]{1,0:T(8,128)(2,1)}, bf16[320,384]{1,0:T(8,128)(2,1)S(1)}, u32[]{:S(2)}, u32[]{:S(2)}) collective-permute-start(bf16[320,384]{1,0:T(8,128)(2,1)} %get-tuple-element.10), channel_id=1, source_target_pairs={{0,0},{1,8},{4,4},{5,12},{8,1},{9,9},{12,5},{13,13},{2,2},{3,10},{... | collective-permute-start | bytes 737288 | tf_op jit(solution)/shard_map/ppermute | solution.py:262
  4.6 19.6 %collective-permute-start.1 = (bf16[320,384]{1,0:T(8,128)(2,1)}, bf16[320,384]{1,0:T(8,128)(2,1)S(1)}, u32[]{:S(2)}, u32[]{:S(2)}) collective-permute-start(bf16[320,384]{1,0:T(8,128)(2,1)} %get-tuple-element.11), channel_id=1, source_target_pairs={{0,4},{1,12},{4,0},{5,8},{8,5},{9,13},{12,1},{13,9},{2,6},{3,14},{... | collective-permute-start | bytes 737288 | tf_op jit(solution)/shard_map/ppermute | solution.py:262
  6.2 18.0 %collective-permute-start.2 = (bf16[160,384]{1,0:T(8,128)(2,1)}, bf16[160,384]{1,0:T(8,128)(2,1)S(1)}, u32[]{:S(2)}, u32[]{:S(2)}) collective-permute-start(bf16[160,384]{1,0:T(8,128)(2,1)} %get-tuple-element.12), channel_id=1, source_target_pairs={{0,1},{1,9},{4,5},{5,13},{8,0},{9,8},{12,4},{13,12},{2,3},{3,11},{... | collective-permute-start | bytes 368648 | tf_op jit(solution)/shard_map/ppermute | solution.py:262
  9.1 15.1 %collective-permute-start.3 = (bf16[160,384]{1,0:T(8,128)(2,1)}, bf16[160,384]{1,0:T(8,128)(2,1)S(1)}, u32[]{:S(2)}, u32[]{:S(2)}) collective-permute-start(bf16[160,384]{1,0:T(8,128)(2,1)} %get-tuple-element.13), channel_id=1, source_target_pairs={{0,5},{1,13},{4,1},{5,9},{8,4},{9,12},{12,0},{13,8},{2,7},{3,15},{... | collective-permute-start | bytes 368648 | tf_op jit(solution)/shard_map/ppermute | solution.py:262
  24.2 1.9 %collective-permute-start.4 = (bf16[640,384]{1,0:T(8,128)(2,1)S(1)}, bf16[640,384]{1,0:T(8,128)(2,1)S(1)}, u32[]{:S(2)}, u32[]{:S(2)}) collective-permute-start(bf16[640,384]{1,0:T(8,128)(2,1)S(1)} %shard_map.96), channel_id=1, source_target_pairs={{0,1},{1,0},{2,3},{3,2},{4,5},{5,4},{6,7},{7,6},{8,9},{9,8},{10,11... | collective-permute-start | bytes 1474568 | tf_op jit(solution)/shard_map/ppermute | solution.py:264
  27.8 12.4 %collective-permute-start.10 = (bf16[160,384]{1,0:T(8,128)(2,1)S(1)}, bf16[160,384]{1,0:T(8,128)(2,1)S(1)}, u32[]{:S(2)}, u32[]{:S(2)}) collective-permute-start(bf16[160,384]{1,0:T(8,128)(2,1)S(1)} %get-tuple-element.17.refs_0_), channel_id=1, source_target_pairs={{0,8},{4,12},{8,0},{12,4},{1,9},{5,13},{9,1},{13,5},{2,10},{6,14},... | collective-permute-start | bytes 368648 | tf_op jit(solution)/shard_map/ppermute | solution.py:285
  30.5 11.9 %collective-permute-start.11 = (bf16[160,384]{1,0:T(8,128)(2,1)S(1)}, bf16[160,384]{1,0:T(8,128)(2,1)S(1)}, u32[]{:S(2)}, u32[]{:S(2)}) collective-permute-start(bf16[160,384]{1,0:T(8,128)(2,1)S(1)} %get-tuple-element.16.refs_0_), channel_id=1, source_target_pairs={{0,12},{4,8},{8,4},{12,0},{1,13},{5,9},{9,5},{13,1},{2,14},{6,10},... | collective-permute-start | bytes 368648 | tf_op jit(solution)/shard_map/ppermute | solution.py:285
  32.1 10.5 %collective-permute-start.9 = (bf16[160,384]{1,0:T(8,128)(2,1)S(1)}, bf16[160,384]{1,0:T(8,128)(2,1)S(1)}, u32[]{:S(2)}, u32[]{:S(2)}) collective-permute-start(bf16[160,384]{1,0:T(8,128)(2,1)S(1)} %get-tuple-element.16.refs_0_), channel_id=1, source_target_pairs={{0,4},{4,0},{8,12},{12,8},{1,5},{5,1},{9,13},{13,9},{2,6},{6,2},{1... | collective-permute-start | bytes 368648 | tf_op jit(solution)/shard_map/ppermute | solution.py:285
  32.1 12.7 %collective-permute-start.6 = (bf16[160,384]{1,0:T(8,128)(2,1)S(1)}, bf16[160,384]{1,0:T(8,128)(2,1)S(1)}, u32[]{:S(2)}, u32[]{:S(2)}) collective-permute-start(bf16[160,384]{1,0:T(8,128)(2,1)S(1)} %get-tuple-element.17.refs_0_), channel_id=1, source_target_pairs={{0,4},{4,0},{8,12},{12,8},{1,5},{5,1},{9,13},{13,9},{2,6},{6,2},{1... | collective-permute-start | bytes 368648 | tf_op jit(solution)/shard_map/ppermute | solution.py:285
  34.1 16.6 %collective-permute-start.7 = (bf16[160,384]{1,0:T(8,128)(2,1)S(1)}, bf16[160,384]{1,0:T(8,128)(2,1)S(1)}, u32[]{:S(2)}, u32[]{:S(2)}) collective-permute-start(bf16[160,384]{1,0:T(8,128)(2,1)S(1)} %get-tuple-element.16.refs_0_), channel_id=1, source_target_pairs={{0,8},{4,12},{8,0},{12,4},{1,9},{5,13},{9,1},{13,5},{2,10},{6,14},... | collective-permute-start | bytes 368648 | tf_op jit(solution)/shard_map/ppermute | solution.py:285
  40.2 10.5 %collective-permute-start.8 = (bf16[160,384]{1,0:T(8,128)(2,1)S(1)}, bf16[160,384]{1,0:T(8,128)(2,1)S(1)}, u32[]{:S(2)}, u32[]{:S(2)}) collective-permute-start(bf16[160,384]{1,0:T(8,128)(2,1)S(1)} %get-tuple-element.17.refs_0_), channel_id=1, source_target_pairs={{0,12},{4,8},{8,4},{12,0},{1,13},{5,9},{9,5},{13,1},{2,14},{6,10},... | collective-permute-start | bytes 368648 | tf_op jit(solution)/shard_map/ppermute | solution.py:285
  43.4 13.6 %copy-start.4 = (f32[1280]{0:T(1024)S(1)}, f32[1280]{0:T(1024)}, u32[]{:S(2)}) copy-start(f32[1280]{0:T(1024)} %param.12) | copy-start | bytes 15364
  43.5 13.6 %copy-start.3 = (s32[4]{0:T(128)S(1)}, s32[4]{0:T(128)}, u32[]{:S(2)}) copy-start(s32[4]{0:T(128)} %flags.1) | copy-start | bytes 52
  43.5 10.1 %collective-permute-start.12 = (bf16[160,1280]{1,0:T(8,128)(2,1)S(1)}, bf16[160,1280]{1,0:T(8,128)(2,1)S(1)}, u32[]{:S(2)}, u32[]{:S(2)}) collective-permute-start(bf16[160,1280]{1,0:T(8,128)(2,1)S(1)} %shard_map.99), channel_id=1, source_target_pairs={{0,2},{2,0},{1,3},{3,1},{4,6},{6,4},{5,7},{7,5},{8,10},{10,8},{9,1... | collective-permute-start | bytes 1228808 | tf_op jit(solution)/shard_map/ppermute | solution.py:294
  50.7 6.3 %copy-start = (f32[4,160,1280]{2,1,0:T(8,128)S(1)}, f32[4,160,1280]{2,1,0:T(8,128)}, u32[]{:S(2)}) copy-start(f32[4,160,1280]{2,1,0:T(8,128)} %cached.1) | copy-start | bytes 9830404
  51.6 5.4 %copy-start.2 = (f32[160,1280]{1,0:T(8,128)S(1)}, f32[160,1280]{1,0:T(8,128)}, u32[]{:S(2)}) copy-start(f32[160,1280]{1,0:T(8,128)} %hidden.1) | copy-start | bytes 2457604
  53.6 15.6 %collective-permute-start.13 = (bf16[160,1280]{1,0:T(8,128)(2,1)S(1)}, bf16[160,1280]{1,0:T(8,128)(2,1)S(1)}, u32[]{:S(2)}, u32[]{:S(2)}) collective-permute-start(bf16[160,1280]{1,0:T(8,128)(2,1)S(1)} %shard_map.100), channel_id=1, source_target_pairs={{0,0},{1,8},{2,4},{3,12},{4,5},{5,13},{6,1},{7,9},{8,2},{9,10},{10... | collective-permute-start | bytes 1228808 | tf_op jit(solution)/shard_map/ppermute | solution.py:310

commit v10 on v9

--- a/solution.py
+++ b/solution.py
@@ -97,25 +97,35 @@
 
 
 def pack_kernel(queries, keys, values, *refs):
-    outs, sems = refs[:4], refs[4]
+    outs, stages, read_sems, write_sems = refs[:4], refs[4:8], refs[8], refs[9]
     rows, width = queries.shape[0], outs[0].shape[1]
     half = rows // 2
     zh, zl = bits()
-    copies = []
-    for k in range(4):
+    reads = []
+    for k, stage in enumerate(stages):
         part = pl.ds(pl.multiple_of(flip(zh, k // 2) * half, 16), half)
         columns = pl.ds(pl.multiple_of(flip(zl, k % 2) * width, 128), width)
         moves = [
-            (keys.at[part, columns], outs[k].at[pl.ds(0, half), :]),
-            (values.at[part, columns], outs[k].at[pl.ds(half, half), :]),
+            (keys.at[part, columns], stage.at[pl.ds(0, half), :]),
+            (values.at[part, columns], stage.at[pl.ds(half, half), :]),
         ]
         if k < 2:
-            moves.append((queries.at[:, columns], outs[k].at[pl.ds(rows, rows), :]))
-        for start, end in moves:
-            copies.append(pltpu.make_async_copy(start, end, sems.at[len(copies)]))
-    for copy in copies:
-        copy.start()
-    for copy in copies:
+            moves.append((queries.at[:, columns], stage.at[pl.ds(rows, rows), :]))
+        reads.append(
+            [
+                pltpu.make_async_copy(start, end, read_sems.at[3 * k + i])
+                for i, (start, end) in enumerate(moves)
+            ]
+        )
+        for copy in reads[-1]:
+            copy.start()
+    writes = []
+    for k, stage in enumerate(stages):
+        for copy in reads[k]:
+            copy.wait()
+        writes.append(pltpu.make_async_copy(stage, outs[k], write_sems.at[k]))
+        writes[-1].start()
+    for copy in writes:
         copy.wait()
 
 
@@ -181,14 +191,12 @@
     return total
 
 
-def sent_kernel(*refs):
-    shards, (weight, weight_c, out, held) = refs[:4], refs[4:]
-    out[...] = multiply(shards, weight, weight_c, held).astype(out.dtype)
-
-
-def kept_kernel(*refs):
-    shards, (weight, weight_c, out, held) = refs[:4], refs[4:]
-    out[...] = multiply(shards, weight, weight_c, held)
+def project_kernel(*refs):
+    shards, (weight, weight_c, out0, out1, held) = refs[:4], refs[4:]
+    total = multiply(shards, weight, weight_c, held)
+    count = out0.shape[1]
+    out0[...] = total[:, :count].astype(out0.dtype)
+    out1[...] = total[:, count:].astype(out1.dtype)
 
 
 def add_kernel(kept, arrived, out):
@@ -202,22 +210,30 @@
     out[...] = total
 
 
-def final_kernel(owned, gate, resting, mixed, fresh):
-    delta = owned[...].astype(jnp.float32) * gate[...]
-    fresh[...] = delta
-    mixed[...] = resting[...] + delta
-
-
-def along(shard, m):
-    return lax.ppermute(shard, "seq", [(z, z ^ m) for z in range(4)])
-
-
-def call(kernel, args, outs, scratch=(), space=pltpu.VMEM, flops=0, vmem=VMEM_BYTES):
+def final_kernel(owned0, owned1, gate, resting, mixed, fresh):
+    count = owned0.shape[1]
+    for h, owned in enumerate((owned0, owned1)):
+        columns = slice(h * count, (h + 1) * count)
+        delta = owned[...].astype(jnp.float32) * gate[:, columns]
+        fresh[:, columns] = delta
+        mixed[:, columns] = resting[:, columns] + delta
+
+
+def call(
+    kernel,
+    args,
+    outs,
+    scratch=(),
+    space=pltpu.VMEM,
+    out_space=pltpu.VMEM,
+    flops=0,
+    vmem=VMEM_BYTES,
+):
     spaces = [pltpu.SMEM if arg.dtype == jnp.int32 else space for arg in args]
     return pl.pallas_call(
         kernel,
         in_specs=[pl.BlockSpec(memory_space=place) for place in spaces],
-        out_specs=[pl.BlockSpec(memory_space=pltpu.VMEM)] * len(outs),
+        out_specs=[pl.BlockSpec(memory_space=out_space)] * len(outs),
         out_shape=[jax.ShapeDtypeStruct(shape, dtype) for shape, dtype in outs],
         scratch_shapes=list(scratch),
         compiler_params=pltpu.CompilerParams(vmem_limit_bytes=vmem),
@@ -245,8 +261,11 @@
         pack_kernel,
         (queries, key_vectors, value_vectors),
         [((2 * rows, width), bf16)] * 2 + [((rows, width), bf16)] * 2,
-        [pltpu.SemaphoreType.DMA((10,))],
+        [pltpu.VMEM((2 * rows, width), bf16)] * 2
+        + [pltpu.VMEM((rows, width), bf16)] * 2
+        + [pltpu.SemaphoreType.DMA((12,)), pltpu.SemaphoreType.DMA((4,))],
         space=pl.ANY,
+        out_space=pl.ANY,
         vmem=PACK_BYTES,
     )
     late_weight, _ = lax.optimization_barrier((out_weight, packed[0]))
@@ -284,22 +303,17 @@
             pairs = [(z, z ^ m) for z in range(4)]
             shards.append(lax.ppermute(parts[(1 - kept) ^ (m % 2)], "seq", pairs))
         gathers.append(shards)
-    (send,) = call(
-        sent_kernel,
-        gathers[0] + [out_weight, weight_c],
-        [((rows, columns), bf16)],
-        held,
-        flops=flops,
-    )
-    arrived = lax.ppermute(send, "wt", swap)
-    (kept,) = call(
-        kept_kernel,
-        gathers[1] + [out_weight, weight_c],
-        [((rows, columns), jnp.float32)],
-        held,
-        flops=8 * flops,
-    )
-    (summed,) = call(add_kernel, (kept, arrived), [((rows, columns), bf16)])
+    count = columns // 2
+    sent, kept = (
+        call(
+            project_kernel,
+            shards + [out_weight, weight_c],
+            [((rows, count), dtype)] * 2,
+            held,
+            flops=effort * flops,
+        )
+        for shards, dtype, effort in ((gathers[0], bf16, 1), (gathers[1], jnp.float32, 8))
+    )
 
     pairs = []
     for zz in range(4):
@@ -307,14 +321,18 @@
             for cc in range(2):
                 to = ((2 * cc + (xx ^ (zz % 2))) * 2 + zz // 2) * 2 + zz % 2
                 pairs.append(((zz * 2 + xx) * 2 + cc, to))
-    owned = lax.ppermute(summed, ("seq", "wt", "head"), pairs)
+    owned = []
+    for part, total in zip(sent, kept):
+        arrived = lax.ppermute(part, "wt", swap)
+        (summed,) = call(add_kernel, (total, arrived), [((rows, count), bf16)])
+        owned.append(lax.ppermute(summed, ("seq", "wt", "head"), pairs))
     (resting,) = call(
         rest_kernel, (skip_flags, hidden_state, cached_deltas), [((rows, columns), jnp.float32)]
     )
     return tuple(
         call(
             final_kernel,
-            (owned, gate_values[None, :], resting),
+            (*owned, gate_values[None, :], resting),
             [((rows, columns), jnp.float32)] * 2,
         )
     )
@@ -335,7 +353,7 @@
     def local(*args):
         sizes = tuple(mesh.shape[name] for name in ("seq", "wt", "head"))
         rows, features = args[0].shape
-        if sizes == (4, 2, 2) and rows % 32 == 0 and features % (2 * HEAD_DIM) == 0:
+        if sizes == (4, 2, 2) and rows % 32 == 0 and features % (2 * HEAD_DIM) == 0 and args[3].shape[1] % 256 == 0:
             return local_heads(*args)
         return local_general(*args)
 

time: 70.7 us -> 69.9 us (0.989)
  waiting for transfers between devices: 42.3 us -> 36.1 us
  starting transfers between devices: 19.6 us -> 24.4 us
    ppermute x2 -> x4, starting transfers between devices: 3.9 us -> 8.73 us  [the longest x2 6.63 us: local_heads(): owned.append(lax.ppermute(summed, ('seq', 'wt', 'head'), pairs))]
    ppermute x2 -> x4, waiting for transfers between devices: 13.3 us -> 8.64 us  [the longest x2 8.63 us: local_heads(): owned.append(lax.ppermute(summed, ('seq', 'wt', 'head'), pairs))]
    ppermute x6, waiting for transfers between devices: 12.1 us -> 10.5 us  [local_heads(): shards.append(lax.ppermute(parts[1 - kept ^ m % 2], 'seq', pairs))]
    pallas_call x8 -> x9, Pallas kernels: 7.74 us -> 7.69 us  [call(): pl.pallas_call(kernel, in_specs=[pl.BlockSpec(memory_space=place) for pla...]
  transfers between devices with their start and end apart: 14 -> 16, of which waited for: 8 -> 7; matrix products, arithmetic and copies ran while one was open for 0% -> 0% of each run, Pallas kernels for 4% -> 4%
where the time goes in v10:
time: 69.9 us; the launch traced here: 69 us
  waiting for transfers between devices  36.1 us (52%)
  starting transfers between devices  24.4 us (35%)
  Pallas kernels  7.69 us (11%)
  between operations  0.81 us (1%)
    ppermute x4, waiting for transfers between devices, local_heads(): moved.append(lax.ppermute(packed[k], ('seq', 'head'), pairs))  15.1 us
    ppermute x6, waiting for transfers between devices, local_heads(): shards.append(lax.ppermute(parts[1 - kept ^ m % 2], 'seq', pairs))  10.5 us
    ppermute x6, starting transfers between devices, local_heads(): shards.append(lax.ppermute(parts[1 - kept ^ m % 2], 'seq', pairs))  9.45 us
    ppermute x2, waiting for transfers between devices, local_heads(): owned.append(lax.ppermute(summed, ('seq', 'wt', 'head'), pairs))  8.63 us
    pallas_call x9, Pallas kernels, call(): pl.pallas_call(kernel, in_specs=[pl.BlockSpec(memory_space=place) for pla...  7.69 us
    ppermute x2, starting transfers between devices, local_heads(): owned.append(lax.ppermute(summed, ('seq', 'wt', 'head'), pairs))  6.63 us
    ppermute x4, starting transfers between devices, local_heads(): moved.append(lax.ppermute(packed[k], ('seq', 'head'), pairs))  6.12 us
    ppermute x2, starting transfers between devices, local_heads(): arrived = lax.ppermute(part, 'wt', swap)  2.09 us
  transfers between devices with their start and end apart: 16, of which 7 were waited for; matrix products, arithmetic and copies ran while one was open for 0% of the time, Pallas kernels for 4%

profile of v10, /device:TPU:2, one launch (start us, length us, event | category | flops | bytes accessed | tf_op | source)
XLA Modules:
  0.0 69.0 jit_solution(11040383194457072397)
XLA Ops:
  0.6 0.0 copy-start.1
  0.6 2.1 %shard_map.95 = (bf16[320,384]{1,0:T(8,128)(2,1)}, bf16[320,384]{1,0:T(8,128)(2,1)}, bf16[160,384]{1,0:T(8,128)(2,1)}, bf16[160,384]{1,0:T(8,128)(2,1)}) custom-call(bf16[160,768]{1,0:T(8,128)(2,1)} %queries.1, bf16[160,768]{1,0:T(8,128)(2,1)} %keys.1, bf16[160,768]{1,0:T(8,128)(2,1)} %values.1), custom_call_target="tpu_custom_call" | custom-call | tf_op jit(solution)/shard_map/pallas_call | solution.py:233
  2.8 0.1 collective-permute-start.5
  2.9 1.6 %collective-permute-start = (bf16[320,384]{1,0:T(8,128)(2,1)}, bf16[320,384]{1,0:T(8,128)(2,1)S(1)}, u32[]{:S(2)}, u32[]{:S(2)}) collective-permute-start(bf16[320,384]{1,0:T(8,128)(2,1)} %get-tuple-element.14), channel_id=1, source_target_pairs={{0,0},{1,8},{4,4},{5,12},{8,1},{9,9},{12,5},{13,13},{2,2},{3,10},{... | collective-permute-start | bytes 737288 | tf_op jit(solution)/shard_map/ppermute | solution.py:281
  4.5 1.6 %collective-permute-start.1 = (bf16[320,384]{1,0:T(8,128)(2,1)}, bf16[320,384]{1,0:T(8,128)(2,1)S(1)}, u32[]{:S(2)}, u32[]{:S(2)}) collective-permute-start(bf16[320,384]{1,0:T(8,128)(2,1)} %get-tuple-element.15), channel_id=1, source_target_pairs={{0,4},{1,12},{4,0},{5,8},{8,5},{9,13},{12,1},{13,9},{2,6},{3,14},{... | collective-permute-start | bytes 737288 | tf_op jit(solution)/shard_map/ppermute | solution.py:281
  6.1 2.9 %collective-permute-start.2 = (bf16[160,384]{1,0:T(8,128)(2,1)}, bf16[160,384]{1,0:T(8,128)(2,1)S(1)}, u32[]{:S(2)}, u32[]{:S(2)}) collective-permute-start(bf16[160,384]{1,0:T(8,128)(2,1)} %get-tuple-element.16), channel_id=1, source_target_pairs={{0,1},{1,9},{4,5},{5,13},{8,0},{9,8},{12,4},{13,12},{2,3},{3,11},{... | collective-permute-start | bytes 368648 | tf_op jit(solution)/shard_map/ppermute | solution.py:281
  9.0 0.0 collective-permute-start.3
  9.0 15.1 %collective-permute-done.2.refs_2_ = bf16[160,384]{1,0:T(8,128)(2,1)S(1)} collective-permute-done((bf16[160,384]{1,0:T(8,128)(2,1)}, bf16[160,384]{1,0:T(8,128)(2,1)S(1)}, u32[]{:S(2)}, u32[]{:S(2)}) %collective-permute-start.2) | collective-permute-done | bytes 122912 | tf_op jit(solution)/shard_map/ppermute | solution.py:281
  24.1 0.0 collective-permute-done.3.refs_3_
  24.1 0.0 collective-permute-done.refs_0_
  24.1 0.0 collective-permute-done.1.refs_1_
  24.1 0.1 collective-permute-start.4
  24.2 1.9 %collective-permute-done.4.refs_4_ = bf16[640,384]{1,0:T(8,128)(2,1)S(1)} collective-permute-done((bf16[640,384]{1,0:T(8,128)(2,1)S(1)}, bf16[640,384]{1,0:T(8,128)(2,1)S(1)}, u32[]{:S(2)}, u32[]{:S(2)}) %collective-permute-start.4) | collective-permute-done | bytes 491552 | tf_op jit(solution)/shard_map/ppermute | solution.py:283
  26.0 0.0 collective-permute-done.5.refs_5_
  26.1 1.6 %shard_map.97 = (bf16[160,384]{1,0:T(8,128)(2,1)S(1)}, bf16[160,384]{1,0:T(8,128)(2,1)S(1)}) custom-call(bf16[320,384]{1,0:T(8,128)(2,1)S(1)} %collective-permute-done.refs_0_, bf16[320,384]{1,0:T(8,128)(2,1)S(1)} %collective-permute-done.1.refs_1_, bf16[160,384]{1,0:T(8,128)(2,1)S(1)} %collective-permute-done.2.refs_2_, ...), custom_call_target="tpu_custom_call" | custom-call | flops 314572800 | tf_op jit(solution)/shard_map/pallas_call | solution.py:233
  27.7 2.7 %collective-permute-start.10 = (bf16[160,384]{1,0:T(8,128)(2,1)S(1)}, bf16[160,384]{1,0:T(8,128)(2,1)S(1)}, u32[]{:S(2)}, u32[]{:S(2)}) collective-permute-start(bf16[160,384]{1,0:T(8,128)(2,1)S(1)} %get-tuple-element.21.refs_0_), channel_id=1, source_target_pairs={{0,8},{4,12},{8,0},{12,4},{1,9},{5,13},{9,1},{13,5},{2,10},{6,14},... | collective-permute-start | bytes 368648 | tf_op jit(solution)/shard_map/ppermute | solution.py:304
  30.4 1.5 %collective-permute-start.11 = (bf16[160,384]{1,0:T(8,128)(2,1)S(1)}, bf16[160,384]{1,0:T(8,128)(2,1)S(1)}, u32[]{:S(2)}, u32[]{:S(2)}) collective-permute-start(bf16[160,384]{1,0:T(8,128)(2,1)S(1)} %get-tuple-element.20.refs_0_), channel_id=1, source_target_pairs={{0,12},{4,8},{8,4},{12,0},{1,13},{5,9},{9,5},{13,1},{2,14},{6,10},... | collective-permute-start | bytes 368648 | tf_op jit(solution)/shard_map/ppermute | solution.py:304
  32.0 0.0 collective-permute-start.9
  32.0 2.0 %collective-permute-start.6 = (bf16[160,384]{1,0:T(8,128)(2,1)S(1)}, bf16[160,384]{1,0:T(8,128)(2,1)S(1)}, u32[]{:S(2)}, u32[]{:S(2)}) collective-permute-start(bf16[160,384]{1,0:T(8,128)(2,1)S(1)} %get-tuple-element.21.refs_0_), channel_id=1, source_target_pairs={{0,4},{4,0},{8,12},{12,8},{1,5},{5,1},{9,13},{13,9},{2,6},{6,2},{1... | collective-permute-start | bytes 368648 | tf_op jit(solution)/shard_map/ppermute | solution.py:304
  34.0 0.8 %collective-permute-start.7 = (bf16[160,384]{1,0:T(8,128)(2,1)S(1)}, bf16[160,384]{1,0:T(8,128)(2,1)S(1)}, u32[]{:S(2)}, u32[]{:S(2)}) collective-permute-start(bf16[160,384]{1,0:T(8,128)(2,1)S(1)} %get-tuple-element.20.refs_0_), channel_id=1, source_target_pairs={{0,8},{4,12},{8,0},{12,4},{1,9},{5,13},{9,1},{13,5},{2,10},{6,14},... | collective-permute-start | bytes 368648 | tf_op jit(solution)/shard_map/ppermute | solution.py:304
  34.9 5.2 %collective-permute-done.10.refs_2_ = bf16[160,384]{1,0:T(8,128)(2,1)S(1)} collective-permute-done((bf16[160,384]{1,0:T(8,128)(2,1)S(1)}, bf16[160,384]{1,0:T(8,128)(2,1)S(1)}, u32[]{:S(2)}, u32[]{:S(2)}) %collective-permute-start.10) | collective-permute-done | bytes 122912 | tf_op jit(solution)/shard_map/ppermute | solution.py:304
  40.1 2.3 %collective-permute-start.8 = (bf16[160,384]{1,0:T(8,128)(2,1)S(1)}, bf16[160,384]{1,0:T(8,128)(2,1)S(1)}, u32[]{:S(2)}, u32[]{:S(2)}) collective-permute-start(bf16[160,384]{1,0:T(8,128)(2,1)S(1)} %get-tuple-element.21.refs_0_), channel_id=1, source_target_pairs={{0,12},{4,8},{8,4},{12,0},{1,13},{5,9},{9,5},{13,1},{2,14},{6,10},... | collective-permute-start | bytes 368648 | tf_op jit(solution)/shard_map/ppermute | solution.py:304
  42.4 0.0 collective-permute-done.11.refs_3_
  42.4 0.1 collective-permute-done.9.refs_1_
  42.5 0.0 copy-done.1
  42.5 0.9 %shard_map.99 = (bf16[160,640]{1,0:T(8,128)(2,1)S(1)}, bf16[160,640]{1,0:T(8,128)(2,1)S(1)}) custom-call(bf16[160,384]{1,0:T(8,128)(2,1)S(1)} %get-tuple-element.21.refs_0_, bf16[160,384]{1,0:T(8,128)(2,1)S(1)} %collective-permute-done.9.refs_1_, bf16[160,384]{1,0:T(8,128)(2,1)S(1)} %collective-permute-done.10.refs_2_, ...), custom_call_target="tpu_custom_call" | custom-call | flops 629145600 | tf_op jit(solution)/shard_map/pallas_call | solution.py:233
  43.3 0.5 collective-permute-start.14
  43.9 0.0 copy-start.4
  43.9 0.0 copy-start.3
  43.9 1.6 %collective-permute-start.12 = (bf16[160,640]{1,0:T(8,128)(2,1)S(1)}, bf16[160,640]{1,0:T(8,128)(2,1)S(1)}, u32[]{:S(2)}, u32[]{:S(2)}) collective-permute-start(bf16[160,640]{1,0:T(8,128)(2,1)S(1)} %get-tuple-element.23), channel_id=1, source_target_pairs={{0,2},{2,0},{1,3},{3,1},{4,6},{6,4},{5,7},{7,5},{8,10},{10,8},{9,1... | collective-permute-start | bytes 614408 | tf_op jit(solution)/shard_map/ppermute | solution.py:326
  45.4 0.0 collective-permute-done.6.refs_1_
  45.4 5.2 %collective-permute-done.7.refs_2_ = bf16[160,384]{1,0:T(8,128)(2,1)S(1)} collective-permute-done((bf16[160,384]{1,0:T(8,128)(2,1)S(1)}, bf16[160,384]{1,0:T(8,128)(2,1)S(1)}, u32[]{:S(2)}, u32[]{:S(2)}) %collective-permute-start.7) | collective-permute-done | bytes 122912 | tf_op jit(solution)/shard_map/ppermute | solution.py:304
  50.6 0.0 collective-permute-done.8.refs_3_
  50.6 0.9 %shard_map.98 = (f32[160,640]{1,0:T(8,128)S(1)}, f32[160,640]{1,0:T(8,128)S(1)}) custom-call(bf16[160,384]{1,0:T(8,128)(2,1)S(1)} %get-tuple-element.20.refs_0_, bf16[160,384]{1,0:T(8,128)(2,1)S(1)} %collective-permute-done.6.refs_1_, bf16[160,384]{1,0:T(8,128)(2,1)S(1)} %collective-permute-done.7.refs_2_, ...), custom_call_target="tpu_custom_call" | custom-call | flops 5033164800 | tf_op jit(solution)/shard_map/pallas_call | solution.py:233
  51.5 0.0 copy-start.2
  51.5 0.0 collective-permute-done.14.arrived
  51.5 0.1 shard_map.101
  51.6 4.7 %collective-permute-start.15 = (bf16[160,640]{1,0:T(8,128)(2,1)S(1)}, bf16[160,640]{1,0:T(8,128)(2,1)S(1)}, u32[]{:S(2)}, u32[]{:S(2)}) collective-permute-start(bf16[160,640]{1,0:T(8,128)(2,1)S(1)} %shard_map.101), channel_id=1, source_target_pairs={{0,0},{1,8},{2,4},{3,12},{4,5},{5,13},{6,1},{7,9},{8,2},{9,10},{10... | collective-permute-start | bytes 614408 | tf_op jit(solution)/shard_map/ppermute | solution.py:328
  56.3 0.0 collective-permute-done.12.arrived
  56.4 1.9 %collective-permute-start.13 = (bf16[160,640]{1,0:T(8,128)(2,1)S(1)}, bf16[160,640]{1,0:T(8,128)(2,1)S(1)}, u32[]{:S(2)}, u32[]{:S(2)}) collective-permute-start(bf16[160,640]{1,0:T(8,128)(2,1)S(1)} %shard_map.100), channel_id=1, source_target_pairs={{0,0},{1,8},{2,4},{3,12},{4,5},{5,13},{6,1},{7,9},{8,2},{9,10},{10... | collective-permute-start | bytes 614408 | tf_op jit(solution)/shard_map/ppermute | solution.py:328
  58.3 0.0 copy-done.4
  58.3 0.0 copy-done.3
  58.3 0.0 copy-done
  58.3 0.0 copy-done.2
  58.3 0.8 %shard_map.102.resting = f32[160,1280]{1,0:T(8,128)S(1)} custom-call(s32[4]{0:T(128)S(1)} %copy-done.3, f32[160,1280]{1,0:T(8,128)S(1)} %copy-done.2, f32[4,160,1280]{2,1,0:T(8,128)S(1)} %copy-done), custom_call_target="tpu_custom_call" | custom-call | tf_op jit(solution)/shard_map/pallas_call | solution.py:233
  59.1 4.3 %collective-permute-done.15.owned1 = bf16[160,640]{1,0:T(8,128)(2,1)S(1)} collective-permute-done((bf16[160,640]{1,0:T(8,128)(2,1)S(1)}, bf16[160,640]{1,0:T(8,128)(2,1)S(1)}, u32[]{:S(2)}, u32[]{:S(2)}) %collective-permute-start.15) | collective-permute-done | bytes 204832 | tf_op jit(solution)/shard_map/ppermute | solution.py:328
  63.4 4.4 %collective-permute-done.13.owned0 = bf16[160,640]{1,0:T(8,128)(2,1)S(1)} collective-permute-done((bf16[160,640]{1,0:T(8,128)(2,1)S(1)}, bf16[160,640]{1,0:T(8,128)(2,1)S(1)}, u32[]{:S(2)}, u32[]{:S(2)}) %collective-permute-start.13) | collective-permute-done | bytes 204832 | tf_op jit(solution)/shard_map/ppermute | solution.py:328
  67.7 1.3 %shard_map.103 = (f32[160,1280]{1,0:T(8,128)}, f32[160,1280]{1,0:T(8,128)}) custom-call(bf16[160,640]{1,0:T(8,128)(2,1)S(1)} %collective-permute-done.13.owned0, bf16[160,640]{1,0:T(8,128)(2,1)S(1)} %collective-permute-done.15.owned1, f32[1,1280]{1,0:T(1,128)S(1)} %broadcast_in_dim.3.gate, f32[160,1280]{1,0:T(8,128)S(1)} %shard_map.102.resting), custom_call_target="tpu_custom_call" | custom-call | tf_op jit(solution)/shard_map/pallas_call | solution.py:233
  (4 shorter events, 0.1 us)
Async XLA Ops:
  0.6 41.8 %copy-start.1 = (bf16[768,1280]{1,0:T(8,128)(2,1)S(1)}, bf16[768,1280]{1,0:T(8,128)(2,1)}, u32[]{:S(2)}) copy-start(bf16[768,1280]{1,0:T(8,128)(2,1)} %refs_4_.3) | copy-start | bytes 5898244
  2.8 23.3 %collective-permute-start.5 = (bf16[768,1280]{1,0:T(8,128)(2,1)}, bf16[768,1280]{1,0:T(8,128)(2,1)S(1)}, u32[]{:S(2)}, u32[]{:S(2)}) collective-permute-start(bf16[768,1280]{1,0:T(8,128)(2,1)} %refs_4_.3), channel_id=1, source_target_pairs={{0,1},{1,0},{2,3},{3,2},{4,5},{5,4},{6,7},{7,6},{8,9},{9,8},{10,11... | collective-permute-start | bytes 5898248 | tf_op jit(solution)/shard_map/ppermute | solution.py:272
  2.9 21.2 %collective-permute-start = (bf16[320,384]{1,0:T(8,128)(2,1)}, bf16[320,384]{1,0:T(8,128)(2,1)S(1)}, u32[]{:S(2)}, u32[]{:S(2)}) collective-permute-start(bf16[320,384]{1,0:T(8,128)(2,1)} %get-tuple-element.14), channel_id=1, source_target_pairs={{0,0},{1,8},{4,4},{5,12},{8,1},{9,9},{12,5},{13,13},{2,2},{3,10},{... | collective-permute-start | bytes 737288 | tf_op jit(solution)/shard_map/ppermute | solution.py:281
  4.5 19.6 %collective-permute-start.1 = (bf16[320,384]{1,0:T(8,128)(2,1)}, bf16[320,384]{1,0:T(8,128)(2,1)S(1)}, u32[]{:S(2)}, u32[]{:S(2)}) collective-permute-start(bf16[320,384]{1,0:T(8,128)(2,1)} %get-tuple-element.15), channel_id=1, source_target_pairs={{0,4},{1,12},{4,0},{5,8},{8,5},{9,13},{12,1},{13,9},{2,6},{3,14},{... | collective-permute-start | bytes 737288 | tf_op jit(solution)/shard_map/ppermute | solution.py:281
  6.1 18.0 %collective-permute-start.2 = (bf16[160,384]{1,0:T(8,128)(2,1)}, bf16[160,384]{1,0:T(8,128)(2,1)S(1)}, u32[]{:S(2)}, u32[]{:S(2)}) collective-permute-start(bf16[160,384]{1,0:T(8,128)(2,1)} %get-tuple-element.16), channel_id=1, source_target_pairs={{0,1},{1,9},{4,5},{5,13},{8,0},{9,8},{12,4},{13,12},{2,3},{3,11},{... | collective-permute-start | bytes 368648 | tf_op jit(solution)/shard_map/ppermute | solution.py:281
  9.0 15.1 %collective-permute-start.3 = (bf16[160,384]{1,0:T(8,128)(2,1)}, bf16[160,384]{1,0:T(8,128)(2,1)S(1)}, u32[]{:S(2)}, u32[]{:S(2)}) collective-permute-start(bf16[160,384]{1,0:T(8,128)(2,1)} %get-tuple-element.17), channel_id=1, source_target_pairs={{0,5},{1,13},{4,1},{5,9},{8,4},{9,12},{12,0},{13,8},{2,7},{3,15},{... | collective-permute-start | bytes 368648 | tf_op jit(solution)/shard_map/ppermute | solution.py:281
  24.1 1.9 %collective-permute-start.4 = (bf16[640,384]{1,0:T(8,128)(2,1)S(1)}, bf16[640,384]{1,0:T(8,128)(2,1)S(1)}, u32[]{:S(2)}, u32[]{:S(2)}) collective-permute-start(bf16[640,384]{1,0:T(8,128)(2,1)S(1)} %shard_map.96), channel_id=1, source_target_pairs={{0,1},{1,0},{2,3},{3,2},{4,5},{5,4},{6,7},{7,6},{8,9},{9,8},{10,11... | collective-permute-start | bytes 1474568 | tf_op jit(solution)/shard_map/ppermute | solution.py:283
  27.7 12.4 %collective-permute-start.10 = (bf16[160,384]{1,0:T(8,128)(2,1)S(1)}, bf16[160,384]{1,0:T(8,128)(2,1)S(1)}, u32[]{:S(2)}, u32[]{:S(2)}) collective-permute-start(bf16[160,384]{1,0:T(8,128)(2,1)S(1)} %get-tuple-element.21.refs_0_), channel_id=1, source_target_pairs={{0,8},{4,12},{8,0},{12,4},{1,9},{5,13},{9,1},{13,5},{2,10},{6,14},... | collective-permute-start | bytes 368648 | tf_op jit(solution)/shard_map/ppermute | solution.py:304
  30.4 11.9 %collective-permute-start.11 = (bf16[160,384]{1,0:T(8,128)(2,1)S(1)}, bf16[160,384]{1,0:T(8,128)(2,1)S(1)}, u32[]{:S(2)}, u32[]{:S(2)}) collective-permute-start(bf16[160,384]{1,0:T(8,128)(2,1)S(1)} %get-tuple-element.20.refs_0_), channel_id=1, source_target_pairs={{0,12},{4,8},{8,4},{12,0},{1,13},{5,9},{9,5},{13,1},{2,14},{6,10},... | collective-permute-start | bytes 368648 | tf_op jit(solution)/shard_map/ppermute | solution.py:304
  32.0 10.5 %collective-permute-start.9 = (bf16[160,384]{1,0:T(8,128)(2,1)S(1)}, bf16[160,384]{1,0:T(8,128)(2,1)S(1)}, u32[]{:S(2)}, u32[]{:S(2)}) collective-permute-start(bf16[160,384]{1,0:T(8,128)(2,1)S(1)} %get-tuple-element.20.refs_0_), channel_id=1, source_target_pairs={{0,4},{4,0},{8,12},{12,8},{1,5},{5,1},{9,13},{13,9},{2,6},{6,2},{1... | collective-permute-start | bytes 368648 | tf_op jit(solution)/shard_map/ppermute | solution.py:304
  32.0 13.5 %collective-permute-start.6 = (bf16[160,384]{1,0:T(8,128)(2,1)S(1)}, bf16[160,384]{1,0:T(8,128)(2,1)S(1)}, u32[]{:S(2)}, u32[]{:S(2)}) collective-permute-start(bf16[160,384]{1,0:T(8,128)(2,1)S(1)} %get-tuple-element.21.refs_0_), channel_id=1, source_target_pairs={{0,4},{4,0},{8,12},{12,8},{1,5},{5,1},{9,13},{13,9},{2,6},{6,2},{1... | collective-permute-start | bytes 368648 | tf_op jit(solution)/shard_map/ppermute | solution.py:304
  34.0 16.6 %collective-permute-start.7 = (bf16[160,384]{1,0:T(8,128)(2,1)S(1)}, bf16[160,384]{1,0:T(8,128)(2,1)S(1)}, u32[]{:S(2)}, u32[]{:S(2)}) collective-permute-start(bf16[160,384]{1,0:T(8,128)(2,1)S(1)} %get-tuple-element.20.refs_0_), channel_id=1, source_target_pairs={{0,8},{4,12},{8,0},{12,4},{1,9},{5,13},{9,1},{13,5},{2,10},{6,14},... | collective-permute-start | bytes 368648 | tf_op jit(solution)/shard_map/ppermute | solution.py:304
  40.1 10.5 %collective-permute-start.8 = (bf16[160,384]{1,0:T(8,128)(2,1)S(1)}, bf16[160,384]{1,0:T(8,128)(2,1)S(1)}, u32[]{:S(2)}, u32[]{:S(2)}) collective-permute-start(bf16[160,384]{1,0:T(8,128)(2,1)S(1)} %get-tuple-element.21.refs_0_), channel_id=1, source_target_pairs={{0,12},{4,8},{8,4},{12,0},{1,13},{5,9},{9,5},{13,1},{2,14},{6,10},... | collective-permute-start | bytes 368648 | tf_op jit(solution)/shard_map/ppermute | solution.py:304
  43.3 8.2 %collective-permute-start.14 = (bf16[160,640]{1,0:T(8,128)(2,1)S(1)}, bf16[160,640]{1,0:T(8,128)(2,1)S(1)}, u32[]{:S(2)}, u32[]{:S(2)}) collective-permute-start(bf16[160,640]{1,0:T(8,128)(2,1)S(1)} %get-tuple-element.25), channel_id=1, source_target_pairs={{0,2},{2,0},{1,3},{3,1},{4,6},{6,4},{5,7},{7,5},{8,10},{10,8},{9,1... | collective-permute-start | bytes 614408 | tf_op jit(solution)/shard_map/ppermute | solution.py:326
  43.9 14.4 %copy-start.4 = (f32[1280]{0:T(1024)S(1)}, f32[1280]{0:T(1024)}, u32[]{:S(2)}) copy-start(f32[1280]{0:T(1024)} %param.12) | copy-start | bytes 15364
  43.9 14.4 %copy-start.3 = (s32[4]{0:T(128)S(1)}, s32[4]{0:T(128)}, u32[]{:S(2)}) copy-start(s32[4]{0:T(128)} %flags.1) | copy-start | bytes 52
  43.9 12.4 %collective-permute-start.12 = (bf16[160,640]{1,0:T(8,128)(2,1)S(1)}, bf16[160,640]{1,0:T(8,128)(2,1)S(1)}, u32[]{:S(2)}, u32[]{:S(2)}) collective-permute-start(bf16[160,640]{1,0:T(8,128)(2,1)S(1)} %get-tuple-element.23), channel_id=1, source_target_pairs={{0,2},{2,0},{1,3},{3,1},{4,6},{6,4},{5,7},{7,5},{8,10},{10,8},{9,1... | collective-permute-start | bytes 614408 | tf_op jit(solution)/shard_map/ppermute | solution.py:326
  50.6 7.7 %copy-start = (f32[4,160,1280]{2,1,0:T(8,128)S(1)}, f32[4,160,1280]{2,1,0:T(8,128)}, u32[]{:S(2)}) copy-start(f32[4,160,1280]{2,1,0:T(8,128)} %cached.1) | copy-start | bytes 9830404
  51.5 6.8 %copy-start.2 = (f32[160,1280]{1,0:T(8,128)S(1)}, f32[160,1280]{1,0:T(8,128)}, u32[]{:S(2)}) copy-start(f32[160,1280]{1,0:T(8,128)} %hidden.1) | copy-start | bytes 2457604
  51.6 11.8 %collective-permute-start.15 = (bf16[160,640]{1,0:T(8,128)(2,1)S(1)}, bf16[160,640]{1,0:T(8,128)(2,1)S(1)}, u32[]{:S(2)}, u32[]{:S(2)}) collective-permute-start(bf16[160,640]{1,0:T(8,128)(2,1)S(1)} %shard_map.101), channel_id=1, source_target_pairs={{0,0},{1,8},{2,4},{3,12},{4,5},{5,13},{6,1},{7,9},{8,2},{9,10},{10... | collective-permute-start | bytes 614408 | tf_op jit(solution)/shard_map/ppermute | solution.py:328
  56.4 11.4 %collective-permute-start.13 = (bf16[160,640]{1,0:T(8,128)(2,1)S(1)}, bf16[160,640]{1,0:T(8,128)(2,1)S(1)}, u32[]{:S(2)}, u32[]{:S(2)}) collective-permute-start(bf16[160,640]{1,0:T(8,128)(2,1)S(1)} %shard_map.100), channel_id=1, source_target_pairs={{0,0},{1,8},{2,4},{3,12},{4,5},{5,13},{6,1},{7,9},{8,2},{9,10},{10... | collective-permute-start | bytes 614408 | tf_op jit(solution)/shard_map/ppermute | solution.py:328

commit v11 on v10

--- a/solution.py
+++ b/solution.py
@@ -1,3 +1,5 @@
+import functools
+
 import jax
 import jax.numpy as jnp
 from jax import lax
@@ -138,8 +140,8 @@
 
 def attention_kernel(*refs):
     blocks, sibling = refs[:4], refs[4]
-    outs, key_all, value_all, query_all = refs[5:7], refs[7], refs[8], refs[9]
-    rows = outs[0].shape[0]
+    sent, kept, key_all, value_all, query_all = refs[5:]
+    rows = sent.shape[0]
     half = rows // 2
     for k in range(4):
         here, there = slice(k * half, (k + 1) * half), slice((4 + k) * half, (5 + k) * half)
@@ -147,11 +149,16 @@
         value_all[here, :] = blocks[k][half:rows, :]
         key_all[there, :] = sibling[k * rows : k * rows + half, :]
         value_all[there, :] = sibling[k * rows + half : (k + 1) * rows, :]
+    _, zl = bits()
     x = lax.axis_index("wt")
     for k in range(2):
-        at = pl.ds(pl.multiple_of(flip(x, k) * rows, 16), rows)
-        query_all[at, :] = blocks[k][rows:, :]
-    for h in range(outs[0].shape[1] // HEAD_DIM):
+        for part in range(2):
+            at = rows + flip(x, part == 0) * half
+            to = (part * 2 + flip(zl, k)) * half
+            query_all[pl.ds(pl.multiple_of(to, 16), half), :] = blocks[k][
+                pl.ds(pl.multiple_of(at, 16), half), :
+            ]
+    for h in range(sent.shape[1] // HEAD_DIM):
         columns = slice(h * HEAD_DIM, (h + 1) * HEAD_DIM)
         scores = lax.dot_general(
             query_all[:, columns],
@@ -165,9 +172,9 @@
         result = jnp.dot(
             weights.astype(jnp.bfloat16), value_all[:, columns], preferred_element_type=jnp.float32
         )
-        result = (result / total).astype(outs[0].dtype)
-        for part, out in enumerate(outs):
-            out[:, columns] = result[part * rows : (part + 1) * rows]
+        result = (result / total).astype(sent.dtype)
+        sent[:, columns] = result[:rows]
+        kept[:, columns] = result[rows:]
 
 
 def multiply(shards, weight, weight_c, held):
@@ -191,12 +198,22 @@
     return total
 
 
-def project_kernel(*refs):
+def project_kernel(kept, *refs):
     shards, (weight, weight_c, out0, out1, held) = refs[:4], refs[4:]
     total = multiply(shards, weight, weight_c, held)
-    count = out0.shape[1]
-    out0[...] = total[:, :count].astype(out0.dtype)
-    out1[...] = total[:, count:].astype(out1.dtype)
+    half = out0.shape[0]
+    x = lax.axis_index("wt")
+    for low in range(2):
+        part = total[low * half : (low + 1) * half].astype(out0.dtype)
+        first = flip(x, low) == 1 - kept
+
+        @pl.when(first)
+        def _():
+            out0[...] = part
+
+        @pl.when(jnp.logical_not(first))
+        def _():
+            out1[...] = part
 
 
 def add_kernel(kept, arrived, out):
@@ -211,12 +228,17 @@
 
 
 def final_kernel(owned0, owned1, gate, resting, mixed, fresh):
-    count = owned0.shape[1]
-    for h, owned in enumerate((owned0, owned1)):
-        columns = slice(h * count, (h + 1) * count)
-        delta = owned[...].astype(jnp.float32) * gate[:, columns]
-        fresh[:, columns] = delta
-        mixed[:, columns] = resting[:, columns] + delta
+    half = owned0.shape[0]
+    _, zl = bits()
+    for p, owned in enumerate((owned0, owned1)):
+        rows = pl.ds(pl.multiple_of(flip(zl, p) * half, 16), half)
+        delta = owned[...].astype(jnp.float32) * gate[...]
+        fresh[rows, :] = delta
+        mixed[rows, :] = resting[rows, :] + delta
+
+
+def along(shard, m):
+    return lax.ppermute(shard, "seq", [(z, z ^ m) for z in range(4)])
 
 
 def call(
@@ -268,8 +290,6 @@
         out_space=pl.ANY,
         vmem=PACK_BYTES,
     )
-    late_weight, _ = lax.optimization_barrier((out_weight, packed[0]))
-    weight_c = lax.ppermute(late_weight, "head", swap)
     moved = []
     for k in range(4):
         k1, k0 = k // 2, k % 2
@@ -281,7 +301,8 @@
         moved.append(lax.ppermute(packed[k], ("seq", "head"), pairs))
     (joined,) = call(join_kernel, moved, [((4 * rows, width), bf16)])
     sibling = lax.ppermute(joined, "head", swap)
-    sibling, _ = lax.optimization_barrier((sibling, weight_c))
+    late_weight, _ = lax.optimization_barrier((out_weight, sibling))
+    weight_c = lax.ppermute(late_weight, "head", swap)
     parts = call(
         attention_kernel,
         moved + [sibling],
@@ -296,35 +317,33 @@
 
     flops = 4 * rows * depth * columns
     held = [pltpu.VMEM((4 * rows, width), bf16)]
+    half = rows // 2
     gathers = []
-    for kept in range(2):
-        shards = [parts[1 - kept]]
-        for m in range(1, 4):
-            pairs = [(z, z ^ m) for z in range(4)]
-            shards.append(lax.ppermute(parts[(1 - kept) ^ (m % 2)], "seq", pairs))
-        gathers.append(shards)
-    count = columns // 2
+    for part in parts:
+        near = along(part, 1)
+        two = along(part, 2)
+        gathers.append([part, near, two, along(two, 1)])
     sent, kept = (
         call(
-            project_kernel,
-            shards + [out_weight, weight_c],
-            [((rows, count), dtype)] * 2,
+            functools.partial(project_kernel, i),
+            gathers[i] + [out_weight, weight_c],
+            [((half, columns), dtype)] * 2,
             held,
             flops=effort * flops,
         )
-        for shards, dtype, effort in ((gathers[0], bf16, 1), (gathers[1], jnp.float32, 8))
-    )
-
-    pairs = []
-    for zz in range(4):
-        for xx in range(2):
-            for cc in range(2):
-                to = ((2 * cc + (xx ^ (zz % 2))) * 2 + zz // 2) * 2 + zz % 2
-                pairs.append(((zz * 2 + xx) * 2 + cc, to))
+        for i, dtype, effort in ((0, bf16, 1), (1, jnp.float32, 8))
+    )
+
     owned = []
-    for part, total in zip(sent, kept):
-        arrived = lax.ppermute(part, "wt", swap)
-        (summed,) = call(add_kernel, (total, arrived), [((rows, count), bf16)])
+    for p in range(2):
+        arrived = lax.ppermute(sent[p], "wt", swap)
+        (summed,) = call(add_kernel, (kept[p], arrived), [((half, columns), bf16)])
+        pairs = []
+        for zz in range(4):
+            for xx in range(2):
+                for cc in range(2):
+                    to = ((2 * cc + (p ^ xx)) * 2 + zz // 2) * 2 + zz % 2
+                    pairs.append(((zz * 2 + xx) * 2 + cc, to))
         owned.append(lax.ppermute(summed, ("seq", "wt", "head"), pairs))
     (resting,) = call(
         rest_kernel, (skip_flags, hidden_state, cached_deltas), [((rows, columns), jnp.float32)]
@@ -353,7 +372,7 @@
     def local(*args):
         sizes = tuple(mesh.shape[name] for name in ("seq", "wt", "head"))
         rows, features = args[0].shape
-        if sizes == (4, 2, 2) and rows % 32 == 0 and features % (2 * HEAD_DIM) == 0 and args[3].shape[1] % 256 == 0:
+        if sizes == (4, 2, 2) and rows % 32 == 0 and features % (2 * HEAD_DIM) == 0:
             return local_heads(*args)
         return local_general(*args)
 

time: 69.9 us -> 70.4 us (level)
  the two profiles are of different devices: /device:TPU:2 before, /device:TPU:1 now
where the time goes in v11:
time: 70.4 us; the launch traced here: 70.3 us
  starting transfers between devices  32.4 us (46%)
  waiting for transfers between devices  29.3 us (42%)
  Pallas kernels  7.77 us (11%)
  between operations  0.78 us (1%)
    ppermute x6, waiting for transfers between devices, along(): return lax.ppermute(shard, 'seq', [(z, z ^ m) for z in range(4)])  13.1 us
    ppermute x2, starting transfers between devices, local_heads(): owned.append(lax.ppermute(summed, ('seq', 'wt', 'head'), pairs))  10.9 us
    ppermute x4, starting transfers between devices, local_heads(): moved.append(lax.ppermute(packed[k], ('seq', 'head'), pairs))  9.33 us
    ppermute x4, waiting for transfers between devices, local_heads(): moved.append(lax.ppermute(packed[k], ('seq', 'head'), pairs))  8.25 us
    pallas_call x9, Pallas kernels, call(): pl.pallas_call(kernel, in_specs=[pl.BlockSpec(memory_space=place) for pla...  7.77 us
    ppermute x2, waiting for transfers between devices, local_heads(): owned.append(lax.ppermute(summed, ('seq', 'wt', 'head'), pairs))  6.43 us
    ppermute x6, starting transfers between devices, along(): return lax.ppermute(shard, 'seq', [(z, z ^ m) for z in range(4)])  5.49 us
    ppermute x1, starting transfers between devices, local_heads(): sibling = lax.ppermute(joined, 'head', swap)  4.77 us
  transfers between devices with their start and end apart: 16, of which 9 were waited for; matrix products, arithmetic and copies ran while one was open for 0% of the time, Pallas kernels for 6%

profile of v11, /device:TPU:1, one launch (start us, length us, event | category | flops | bytes accessed | tf_op | source)
XLA Modules:
  0.0 70.3 jit_solution(3583757189161260719)
XLA Ops:
  0.6 0.0 copy-start.1
  0.6 2.1 %shard_map.95 = (bf16[320,384]{1,0:T(8,128)(2,1)}, bf16[320,384]{1,0:T(8,128)(2,1)}, bf16[160,384]{1,0:T(8,128)(2,1)}, bf16[160,384]{1,0:T(8,128)(2,1)}) custom-call(bf16[160,768]{1,0:T(8,128)(2,1)} %queries.1, bf16[160,768]{1,0:T(8,128)(2,1)} %keys.1, bf16[160,768]{1,0:T(8,128)(2,1)} %values.1), custom_call_target="tpu_custom_call" | custom-call | tf_op jit(solution)/shard_map/pallas_call | solution.py:255
  2.8 5.6 %collective-permute-start = (bf16[320,384]{1,0:T(8,128)(2,1)}, bf16[320,384]{1,0:T(8,128)(2,1)S(1)}, u32[]{:S(2)}, u32[]{:S(2)}) collective-permute-start(bf16[320,384]{1,0:T(8,128)(2,1)} %get-tuple-element.13), channel_id=1, source_target_pairs={{0,0},{1,8},{4,4},{5,12},{8,1},{9,9},{12,5},{13,13},{2,2},{3,10},{... | collective-permute-start | bytes 737288 | tf_op jit(solution)/shard_map/ppermute | solution.py:301
  8.4 1.1 %collective-permute-start.1 = (bf16[320,384]{1,0:T(8,128)(2,1)}, bf16[320,384]{1,0:T(8,128)(2,1)S(1)}, u32[]{:S(2)}, u32[]{:S(2)}) collective-permute-start(bf16[320,384]{1,0:T(8,128)(2,1)} %get-tuple-element.14), channel_id=1, source_target_pairs={{0,4},{1,12},{4,0},{5,8},{8,5},{9,13},{12,1},{13,9},{2,6},{3,14},{... | collective-permute-start | bytes 737288 | tf_op jit(solution)/shard_map/ppermute | solution.py:301
  9.5 0.0 collective-permute-start.2
  9.5 2.6 %collective-permute-start.3 = (bf16[160,384]{1,0:T(8,128)(2,1)}, bf16[160,384]{1,0:T(8,128)(2,1)S(1)}, u32[]{:S(2)}, u32[]{:S(2)}) collective-permute-start(bf16[160,384]{1,0:T(8,128)(2,1)} %get-tuple-element.16), channel_id=1, source_target_pairs={{0,5},{1,13},{4,1},{5,9},{8,4},{9,12},{12,0},{13,8},{2,7},{3,15},{... | collective-permute-start | bytes 368648 | tf_op jit(solution)/shard_map/ppermute | solution.py:301
  12.1 6.9 %collective-permute-done.2.refs_2_ = bf16[160,384]{1,0:T(8,128)(2,1)S(1)} collective-permute-done((bf16[160,384]{1,0:T(8,128)(2,1)}, bf16[160,384]{1,0:T(8,128)(2,1)S(1)}, u32[]{:S(2)}, u32[]{:S(2)}) %collective-permute-start.2) | collective-permute-done | bytes 122912 | tf_op jit(solution)/shard_map/ppermute | solution.py:301
  19.1 1.3 %collective-permute-done.3.refs_3_ = bf16[160,384]{1,0:T(8,128)(2,1)S(1)} collective-permute-done((bf16[160,384]{1,0:T(8,128)(2,1)}, bf16[160,384]{1,0:T(8,128)(2,1)S(1)}, u32[]{:S(2)}, u32[]{:S(2)}) %collective-permute-start.3) | collective-permute-done | bytes 122912 | tf_op jit(solution)/shard_map/ppermute | solution.py:301
  20.4 0.0 collective-permute-done.refs_0_
  20.4 0.0 collective-permute-done.1.refs_1_
  20.4 4.8 %collective-permute-start.4 = (bf16[640,384]{1,0:T(8,128)(2,1)S(1)}, bf16[640,384]{1,0:T(8,128)(2,1)S(1)}, u32[]{:S(2)}, u32[]{:S(2)}) collective-permute-start(bf16[640,384]{1,0:T(8,128)(2,1)S(1)} %shard_map.96), channel_id=1, source_target_pairs={{0,1},{1,0},{2,3},{3,2},{4,5},{5,4},{6,7},{7,6},{8,9},{9,8},{10,11... | collective-permute-start | bytes 1474568 | tf_op jit(solution)/shard_map/ppermute | solution.py:303
  25.2 1.5 %collective-permute-done.4.refs_4_ = bf16[640,384]{1,0:T(8,128)(2,1)S(1)} collective-permute-done((bf16[640,384]{1,0:T(8,128)(2,1)S(1)}, bf16[640,384]{1,0:T(8,128)(2,1)S(1)}, u32[]{:S(2)}, u32[]{:S(2)}) %collective-permute-start.4) | collective-permute-done | bytes 491552 | tf_op jit(solution)/shard_map/ppermute | solution.py:303
  26.7 0.0 copy-done.1
  26.7 0.4 collective-permute-start.8
  27.1 1.6 %shard_map.97 = (bf16[160,384]{1,0:T(8,128)(2,1)S(1)}, bf16[160,384]{1,0:T(8,128)(2,1)S(1)}) custom-call(bf16[320,384]{1,0:T(8,128)(2,1)S(1)} %collective-permute-done.refs_0_, bf16[320,384]{1,0:T(8,128)(2,1)S(1)} %collective-permute-done.1.refs_1_, bf16[160,384]{1,0:T(8,128)(2,1)S(1)} %collective-permute-done.2.refs_2_, ...), custom_call_target="tpu_custom_call" | custom-call | flops 314572800 | tf_op jit(solution)/shard_map/pallas_call | solution.py:255
  28.7 2.9 %collective-permute-start.10 = (bf16[160,384]{1,0:T(8,128)(2,1)S(1)}, bf16[160,384]{1,0:T(8,128)(2,1)S(1)}, u32[]{:S(2)}, u32[]{:S(2)}) collective-permute-start(bf16[160,384]{1,0:T(8,128)(2,1)S(1)} %get-tuple-element.20.refs_0_), channel_id=1, source_target_pairs={{0,8},{4,12},{8,0},{12,4},{1,9},{5,13},{9,1},{13,5},{2,10},{6,14},... | collective-permute-start | bytes 368648 | tf_op jit(solution)/shard_map/ppermute | solution.py:241
  31.6 0.1 collective-permute-start.6
  31.6 1.1 %collective-permute-start.9 = (bf16[160,384]{1,0:T(8,128)(2,1)S(1)}, bf16[160,384]{1,0:T(8,128)(2,1)S(1)}, u32[]{:S(2)}, u32[]{:S(2)}) collective-permute-start(bf16[160,384]{1,0:T(8,128)(2,1)S(1)} %get-tuple-element.20.refs_0_), channel_id=1, source_target_pairs={{0,4},{4,0},{8,12},{12,8},{1,5},{5,1},{9,13},{13,9},{2,6},{6,2},{1... | collective-permute-start | bytes 368648 | tf_op jit(solution)/shard_map/ppermute | solution.py:241
  32.7 7.5 %collective-permute-done.10.refs_2_ = bf16[160,384]{1,0:T(8,128)(2,1)S(1)} collective-permute-done((bf16[160,384]{1,0:T(8,128)(2,1)S(1)}, bf16[160,384]{1,0:T(8,128)(2,1)S(1)}, u32[]{:S(2)}, u32[]{:S(2)}) %collective-permute-start.10) | collective-permute-done | bytes 122912 | tf_op jit(solution)/shard_map/ppermute | solution.py:241
  40.2 0.0 collective-permute-start.11
  40.2 1.5 %collective-permute-start.5 = (bf16[160,384]{1,0:T(8,128)(2,1)S(1)}, bf16[160,384]{1,0:T(8,128)(2,1)S(1)}, u32[]{:S(2)}, u32[]{:S(2)}) collective-permute-start(bf16[160,384]{1,0:T(8,128)(2,1)S(1)} %get-tuple-element.17.refs_0_), channel_id=1, source_target_pairs={{0,4},{4,0},{8,12},{12,8},{1,5},{5,1},{9,13},{13,9},{2,6},{6,2},{1... | collective-permute-start | bytes 368648 | tf_op jit(solution)/shard_map/ppermute | solution.py:241
  41.7 1.2 %collective-permute-done.6.refs_2_ = bf16[160,384]{1,0:T(8,128)(2,1)S(1)} collective-permute-done((bf16[160,384]{1,0:T(8,128)(2,1)S(1)}, bf16[160,384]{1,0:T(8,128)(2,1)S(1)}, u32[]{:S(2)}, u32[]{:S(2)}) %collective-permute-start.6) | collective-permute-done | bytes 122912 | tf_op jit(solution)/shard_map/ppermute | solution.py:241
  42.9 0.0 collective-permute-start.7
  42.9 0.0 collective-permute-done.9.refs_1_
  42.9 1.5 %collective-permute-done.11.refs_3_ = bf16[160,384]{1,0:T(8,128)(2,1)S(1)} collective-permute-done((bf16[160,384]{1,0:T(8,128)(2,1)S(1)}, bf16[160,384]{1,0:T(8,128)(2,1)S(1)}, u32[]{:S(2)}, u32[]{:S(2)}) %collective-permute-start.11) | collective-permute-done | bytes 122912 | tf_op jit(solution)/shard_map/ppermute | solution.py:241
  44.4 0.0 collective-permute-done.8.refs_5_
  44.4 0.9 %shard_map.99 = (bf16[80,1280]{1,0:T(8,128)(2,1)S(1)}, bf16[80,1280]{1,0:T(8,128)(2,1)S(1)}) custom-call(bf16[160,384]{1,0:T(8,128)(2,1)S(1)} %get-tuple-element.20.refs_0_, bf16[160,384]{1,0:T(8,128)(2,1)S(1)} %collective-permute-done.9.refs_1_, bf16[160,384]{1,0:T(8,128)(2,1)S(1)} %collective-permute-done.10.refs_2_, ...), custom_call_target="tpu_custom_call" | custom-call | flops 629145600 | tf_op jit(solution)/shard_map/pallas_call | solution.py:255
  45.3 1.3 %collective-permute-start.14 = (bf16[80,1280]{1,0:T(8,128)(2,1)S(1)}, bf16[80,1280]{1,0:T(8,128)(2,1)S(1)}, u32[]{:S(2)}, u32[]{:S(2)}) collective-permute-start(bf16[80,1280]{1,0:T(8,128)(2,1)S(1)} %get-tuple-element.23), channel_id=1, source_target_pairs={{0,2},{2,0},{1,3},{3,1},{4,6},{6,4},{5,7},{7,5},{8,10},{10,8},{9,1... | collective-permute-start | bytes 614408 | tf_op jit(solution)/shard_map/ppermute | solution.py:339
  46.6 0.0 copy-start.4
  46.6 0.0 copy-start.3
  46.6 0.3 collective-permute-start.12
  46.8 0.3 collective-permute-done.5.refs_1_
  47.1 2.6 %collective-permute-done.7.refs_3_ = bf16[160,384]{1,0:T(8,128)(2,1)S(1)} collective-permute-done((bf16[160,384]{1,0:T(8,128)(2,1)S(1)}, bf16[160,384]{1,0:T(8,128)(2,1)S(1)}, u32[]{:S(2)}, u32[]{:S(2)}) %collective-permute-start.7) | collective-permute-done | bytes 122912 | tf_op jit(solution)/shard_map/ppermute | solution.py:241
  49.8 0.9 %shard_map.98 = (f32[80,1280]{1,0:T(8,128)S(1)}, f32[80,1280]{1,0:T(8,128)S(1)}) custom-call(bf16[160,384]{1,0:T(8,128)(2,1)S(1)} %get-tuple-element.17.refs_0_, bf16[160,384]{1,0:T(8,128)(2,1)S(1)} %collective-permute-done.5.refs_1_, bf16[160,384]{1,0:T(8,128)(2,1)S(1)} %collective-permute-done.6.refs_2_, ...), custom_call_target="tpu_custom_call" | custom-call | flops 5033164800 | tf_op jit(solution)/shard_map/pallas_call | solution.py:255
  50.7 0.0 copy-start.2
  50.7 0.0 collective-permute-done.14.arrived
  50.7 0.1 shard_map.101
  50.8 6.7 %collective-permute-start.15 = (bf16[80,1280]{1,0:T(8,128)(2,1)S(1)}, bf16[80,1280]{1,0:T(8,128)(2,1)S(1)}, u32[]{:S(2)}, u32[]{:S(2)}) collective-permute-start(bf16[80,1280]{1,0:T(8,128)(2,1)S(1)} %shard_map.101), channel_id=1, source_target_pairs={{0,4},{1,12},{2,0},{3,8},{4,5},{5,13},{6,1},{7,9},{8,6},{9,14},{10... | collective-permute-start | bytes 614408 | tf_op jit(solution)/shard_map/ppermute | solution.py:347
  57.4 0.0 collective-permute-done.12.arrived
  57.5 4.2 %collective-permute-start.13 = (bf16[80,1280]{1,0:T(8,128)(2,1)S(1)}, bf16[80,1280]{1,0:T(8,128)(2,1)S(1)}, u32[]{:S(2)}, u32[]{:S(2)}) collective-permute-start(bf16[80,1280]{1,0:T(8,128)(2,1)S(1)} %shard_map.100), channel_id=1, source_target_pairs={{0,0},{1,8},{2,4},{3,12},{4,1},{5,9},{6,5},{7,13},{8,2},{9,10},{10... | collective-permute-start | bytes 614408 | tf_op jit(solution)/shard_map/ppermute | solution.py:347
  61.7 0.0 copy-done.4
  61.7 0.0 copy-done.3
  61.7 0.0 copy-done
  61.7 0.0 copy-done.2
  61.7 0.8 %shard_map.102.resting = f32[160,1280]{1,0:T(8,128)S(1)} custom-call(s32[4]{0:T(128)S(1)} %copy-done.3, f32[160,1280]{1,0:T(8,128)S(1)} %copy-done.2, f32[4,160,1280]{2,1,0:T(8,128)S(1)} %copy-done), custom_call_target="tpu_custom_call" | custom-call | tf_op jit(solution)/shard_map/pallas_call | solution.py:255
  62.5 0.0 collective-permute-done.15.owned1
  62.5 6.4 %collective-permute-done.13.owned0 = bf16[80,1280]{1,0:T(8,128)(2,1)S(1)} collective-permute-done((bf16[80,1280]{1,0:T(8,128)(2,1)S(1)}, bf16[80,1280]{1,0:T(8,128)(2,1)S(1)}, u32[]{:S(2)}, u32[]{:S(2)}) %collective-permute-start.13) | collective-permute-done | bytes 204832 | tf_op jit(solution)/shard_map/ppermute | solution.py:347
  68.9 1.3 %shard_map.103 = (f32[160,1280]{1,0:T(8,128)}, f32[160,1280]{1,0:T(8,128)}) custom-call(bf16[80,1280]{1,0:T(8,128)(2,1)S(1)} %collective-permute-done.13.owned0, bf16[80,1280]{1,0:T(8,128)(2,1)S(1)} %collective-permute-done.15.owned1, f32[1,1280]{1,0:T(1,128)S(1)} %broadcast_in_dim.3.gate, f32[160,1280]{1,0:T(8,128)S(1)} %shard_map.102.resting), custom_call_target="tpu_custom_call" | custom-call | tf_op jit(solution)/shard_map/pallas_call | solution.py:255
  (4 shorter events, 0.1 us)
Async XLA Ops:
  0.6 26.1 %copy-start.1 = (bf16[768,1280]{1,0:T(8,128)(2,1)S(1)}, bf16[768,1280]{1,0:T(8,128)(2,1)}, u32[]{:S(2)}) copy-start(bf16[768,1280]{1,0:T(8,128)(2,1)} %refs_4_.3) | copy-start | bytes 5898244
  2.8 17.6 %collective-permute-start = (bf16[320,384]{1,0:T(8,128)(2,1)}, bf16[320,384]{1,0:T(8,128)(2,1)S(1)}, u32[]{:S(2)}, u32[]{:S(2)}) collective-permute-start(bf16[320,384]{1,0:T(8,128)(2,1)} %get-tuple-element.13), channel_id=1, source_target_pairs={{0,0},{1,8},{4,4},{5,12},{8,1},{9,9},{12,5},{13,13},{2,2},{3,10},{... | collective-permute-start | bytes 737288 | tf_op jit(solution)/shard_map/ppermute | solution.py:301
  8.4 12.0 %collective-permute-start.1 = (bf16[320,384]{1,0:T(8,128)(2,1)}, bf16[320,384]{1,0:T(8,128)(2,1)S(1)}, u32[]{:S(2)}, u32[]{:S(2)}) collective-permute-start(bf16[320,384]{1,0:T(8,128)(2,1)} %get-tuple-element.14), channel_id=1, source_target_pairs={{0,4},{1,12},{4,0},{5,8},{8,5},{9,13},{12,1},{13,9},{2,6},{3,14},{... | collective-permute-start | bytes 737288 | tf_op jit(solution)/shard_map/ppermute | solution.py:301
  9.5 9.6 %collective-permute-start.2 = (bf16[160,384]{1,0:T(8,128)(2,1)}, bf16[160,384]{1,0:T(8,128)(2,1)S(1)}, u32[]{:S(2)}, u32[]{:S(2)}) collective-permute-start(bf16[160,384]{1,0:T(8,128)(2,1)} %get-tuple-element.15), channel_id=1, source_target_pairs={{0,1},{1,9},{4,5},{5,13},{8,0},{9,8},{12,4},{13,12},{2,3},{3,11},{... | collective-permute-start | bytes 368648 | tf_op jit(solution)/shard_map/ppermute | solution.py:301
  9.5 10.9 %collective-permute-start.3 = (bf16[160,384]{1,0:T(8,128)(2,1)}, bf16[160,384]{1,0:T(8,128)(2,1)S(1)}, u32[]{:S(2)}, u32[]{:S(2)}) collective-permute-start(bf16[160,384]{1,0:T(8,128)(2,1)} %get-tuple-element.16), channel_id=1, source_target_pairs={{0,5},{1,13},{4,1},{5,9},{8,4},{9,12},{12,0},{13,8},{2,7},{3,15},{... | collective-permute-start | bytes 368648 | tf_op jit(solution)/shard_map/ppermute | solution.py:301
  20.4 6.3 %collective-permute-start.4 = (bf16[640,384]{1,0:T(8,128)(2,1)S(1)}, bf16[640,384]{1,0:T(8,128)(2,1)S(1)}, u32[]{:S(2)}, u32[]{:S(2)}) collective-permute-start(bf16[640,384]{1,0:T(8,128)(2,1)S(1)} %shard_map.96), channel_id=1, source_target_pairs={{0,1},{1,0},{2,3},{3,2},{4,5},{5,4},{6,7},{7,6},{8,9},{9,8},{10,11... | collective-permute-start | bytes 1474568 | tf_op jit(solution)/shard_map/ppermute | solution.py:303
  26.7 17.7 %collective-permute-start.8 = (bf16[768,1280]{1,0:T(8,128)(2,1)S(1)}, bf16[768,1280]{1,0:T(8,128)(2,1)S(1)}, u32[]{:S(2)}, u32[]{:S(2)}) collective-permute-start(bf16[768,1280]{1,0:T(8,128)(2,1)S(1)} %copy-done.1), channel_id=1, source_target_pairs={{0,1},{1,0},{2,3},{3,2},{4,5},{5,4},{6,7},{7,6},{8,9},{9,8},{10,11... | collective-permute-start | bytes 5898248 | tf_op jit(solution)/shard_map/ppermute | solution.py:305
  28.7 11.5 %collective-permute-start.10 = (bf16[160,384]{1,0:T(8,128)(2,1)S(1)}, bf16[160,384]{1,0:T(8,128)(2,1)S(1)}, u32[]{:S(2)}, u32[]{:S(2)}) collective-permute-start(bf16[160,384]{1,0:T(8,128)(2,1)S(1)} %get-tuple-element.20.refs_0_), channel_id=1, source_target_pairs={{0,8},{4,12},{8,0},{12,4},{1,9},{5,13},{9,1},{13,5},{2,10},{6,14},... | collective-permute-start | bytes 368648 | tf_op jit(solution)/shard_map/ppermute | solution.py:241
  31.6 11.3 %collective-permute-start.6 = (bf16[160,384]{1,0:T(8,128)(2,1)S(1)}, bf16[160,384]{1,0:T(8,128)(2,1)S(1)}, u32[]{:S(2)}, u32[]{:S(2)}) collective-permute-start(bf16[160,384]{1,0:T(8,128)(2,1)S(1)} %get-tuple-element.17.refs_0_), channel_id=1, source_target_pairs={{0,8},{4,12},{8,0},{12,4},{1,9},{5,13},{9,1},{13,5},{2,10},{6,14},... | collective-permute-start | bytes 368648 | tf_op jit(solution)/shard_map/ppermute | solution.py:241
  31.6 11.2 %collective-permute-start.9 = (bf16[160,384]{1,0:T(8,128)(2,1)S(1)}, bf16[160,384]{1,0:T(8,128)(2,1)S(1)}, u32[]{:S(2)}, u32[]{:S(2)}) collective-permute-start(bf16[160,384]{1,0:T(8,128)(2,1)S(1)} %get-tuple-element.20.refs_0_), channel_id=1, source_target_pairs={{0,4},{4,0},{8,12},{12,8},{1,5},{5,1},{9,13},{13,9},{2,6},{6,2},{1... | collective-permute-start | bytes 368648 | tf_op jit(solution)/shard_map/ppermute | solution.py:241
  40.2 4.1 %collective-permute-start.11 = (bf16[160,384]{1,0:T(8,128)(2,1)S(1)}, bf16[160,384]{1,0:T(8,128)(2,1)S(1)}, u32[]{:S(2)}, u32[]{:S(2)}) collective-permute-start(bf16[160,384]{1,0:T(8,128)(2,1)S(1)} %collective-permute-done.10.refs_2_), channel_id=1, source_target_pairs={{0,4},{4,0},{8,12},{12,8},{1,5},{5,1},{9,13},{13,9},{2,6},{6,2},{1... | collective-permute-start | bytes 368648 | tf_op jit(solution)/shard_map/ppermute | solution.py:241
  40.2 6.9 %collective-permute-start.5 = (bf16[160,384]{1,0:T(8,128)(2,1)S(1)}, bf16[160,384]{1,0:T(8,128)(2,1)S(1)}, u32[]{:S(2)}, u32[]{:S(2)}) collective-permute-start(bf16[160,384]{1,0:T(8,128)(2,1)S(1)} %get-tuple-element.17.refs_0_), channel_id=1, source_target_pairs={{0,4},{4,0},{8,12},{12,8},{1,5},{5,1},{9,13},{13,9},{2,6},{6,2},{1... | collective-permute-start | bytes 368648 | tf_op jit(solution)/shard_map/ppermute | solution.py:241
  42.9 6.9 %collective-permute-start.7 = (bf16[160,384]{1,0:T(8,128)(2,1)S(1)}, bf16[160,384]{1,0:T(8,128)(2,1)S(1)}, u32[]{:S(2)}, u32[]{:S(2)}) collective-permute-start(bf16[160,384]{1,0:T(8,128)(2,1)S(1)} %collective-permute-done.6.refs_2_), channel_id=1, source_target_pairs={{0,4},{4,0},{8,12},{12,8},{1,5},{5,1},{9,13},{13,9},{2,6},{6,2},{1... | collective-permute-start | bytes 368648 | tf_op jit(solution)/shard_map/ppermute | solution.py:241
  45.3 5.4 %collective-permute-start.14 = (bf16[80,1280]{1,0:T(8,128)(2,1)S(1)}, bf16[80,1280]{1,0:T(8,128)(2,1)S(1)}, u32[]{:S(2)}, u32[]{:S(2)}) collective-permute-start(bf16[80,1280]{1,0:T(8,128)(2,1)S(1)} %get-tuple-element.23), channel_id=1, source_target_pairs={{0,2},{2,0},{1,3},{3,1},{4,6},{6,4},{5,7},{7,5},{8,10},{10,8},{9,1... | collective-permute-start | bytes 614408 | tf_op jit(solution)/shard_map/ppermute | solution.py:339
  46.6 15.1 %copy-start.4 = (f32[1280]{0:T(1024)S(1)}, f32[1280]{0:T(1024)}, u32[]{:S(2)}) copy-start(f32[1280]{0:T(1024)} %param.12) | copy-start | bytes 15364
  46.6 15.2 %copy-start.3 = (s32[4]{0:T(128)S(1)}, s32[4]{0:T(128)}, u32[]{:S(2)}) copy-start(s32[4]{0:T(128)} %flags.1) | copy-start | bytes 52
  46.6 10.9 %collective-permute-start.12 = (bf16[80,1280]{1,0:T(8,128)(2,1)S(1)}, bf16[80,1280]{1,0:T(8,128)(2,1)S(1)}, u32[]{:S(2)}, u32[]{:S(2)}) collective-permute-start(bf16[80,1280]{1,0:T(8,128)(2,1)S(1)} %get-tuple-element.21), channel_id=1, source_target_pairs={{0,2},{2,0},{1,3},{3,1},{4,6},{6,4},{5,7},{7,5},{8,10},{10,8},{9,1... | collective-permute-start | bytes 614408 | tf_op jit(solution)/shard_map/ppermute | solution.py:339
  49.8 12.0 %copy-start = (f32[4,160,1280]{2,1,0:T(8,128)S(1)}, f32[4,160,1280]{2,1,0:T(8,128)}, u32[]{:S(2)}) copy-start(f32[4,160,1280]{2,1,0:T(8,128)} %cached.1) | copy-start | bytes 9830404
  50.7 11.0 %copy-start.2 = (f32[160,1280]{1,0:T(8,128)S(1)}, f32[160,1280]{1,0:T(8,128)}, u32[]{:S(2)}) copy-start(f32[160,1280]{1,0:T(8,128)} %hidden.1) | copy-start | bytes 2457604
  50.8 11.7 %collective-permute-start.15 = (bf16[80,1280]{1,0:T(8,128)(2,1)S(1)}, bf16[80,1280]{1,0:T(8,128)(2,1)S(1)}, u32[]{:S(2)}, u32[]{:S(2)}) collective-permute-start(bf16[80,1280]{1,0:T(8,128)(2,1)S(1)} %shard_map.101), channel_id=1, source_target_pairs={{0,4},{1,12},{2,0},{3,8},{4,5},{5,13},{6,1},{7,9},{8,6},{9,14},{10... | collective-permute-start | bytes 614408 | tf_op jit(solution)/shard_map/ppermute | solution.py:347
  57.5 11.5 %collective-permute-start.13 = (bf16[80,1280]{1,0:T(8,128)(2,1)S(1)}, bf16[80,1280]{1,0:T(8,128)(2,1)S(1)}, u32[]{:S(2)}, u32[]{:S(2)}) collective-permute-start(bf16[80,1280]{1,0:T(8,128)(2,1)S(1)} %shard_map.100), channel_id=1, source_target_pairs={{0,0},{1,8},{2,4},{3,12},{4,1},{5,9},{6,5},{7,13},{8,2},{9,10},{10... | collective-permute-start | bytes 614408 | tf_op jit(solution)/shard_map/ppermute | solution.py:347

commit v12 on v11

--- a/solution.py
+++ b/solution.py
@@ -318,21 +318,23 @@
     flops = 4 * rows * depth * columns
     held = [pltpu.VMEM((4 * rows, width), bf16)]
     half = rows // 2
-    gathers = []
-    for part in parts:
-        near = along(part, 1)
-        two = along(part, 2)
-        gathers.append([part, near, two, along(two, 1)])
-    sent, kept = (
-        call(
+    def projected(i, near, two, far, dtype, effort):
+        return call(
             functools.partial(project_kernel, i),
-            gathers[i] + [out_weight, weight_c],
+            (parts[i], near, two, far, out_weight, weight_c),
             [((half, columns), dtype)] * 2,
             held,
             flops=effort * flops,
         )
-        for i, dtype, effort in ((0, bf16, 1), (1, jnp.float32, 8))
-    )
+
+    near = along(parts[0], 1)
+    two = along(parts[0], 2)
+    late_two, late_part, _ = lax.optimization_barrier((two, parts[1], near))
+    sent = projected(0, near, two, along(late_two, 1), bf16, 1)
+    near = along(late_part, 1)
+    two = along(late_part, 2)
+    late_two, _ = lax.optimization_barrier((two, sent[0]))
+    kept = projected(1, near, two, along(late_two, 1), jnp.float32, 8)
 
     owned = []
     for p in range(2):

time: 70.4 us -> 72.4 us (1.028)
  waiting for transfers between devices: 29.3 us -> 32.4 us
  starting transfers between devices: 32.4 us -> 31.2 us
    ppermute x2, waiting for transfers between devices: 0.01 us -> 2.49 us  [local_heads(): arrived = lax.ppermute(sent[p], 'wt', swap)]
    ppermute x2, starting transfers between devices: 10.9 us -> 9.82 us  [local_heads(): owned.append(lax.ppermute(summed, ('seq', 'wt', 'head'), pairs))]
  transfers between devices with their start and end apart: 16 -> 16, of which waited for: 9 -> 11; matrix products, arithmetic and copies ran while one was open for 0% -> 0% of each run, Pallas kernels for 6% -> 6%
where the time goes in v12:
time: 72.4 us; the launch traced here: 72.2 us
  waiting for transfers between devices  32.4 us (45%)
  starting transfers between devices  31.2 us (43%)
  Pallas kernels  7.77 us (11%)
  between operations  0.77 us (1%)
    ppermute x6, waiting for transfers between devices, along(): return lax.ppermute(shard, 'seq', [(z, z ^ m) for z in range(4)])  13.2 us
    ppermute x2, starting transfers between devices, local_heads(): owned.append(lax.ppermute(summed, ('seq', 'wt', 'head'), pairs))  9.82 us
    ppermute x4, starting transfers between devices, local_heads(): moved.append(lax.ppermute(packed[k], ('seq', 'head'), pairs))  9.33 us
    ppermute x4, waiting for transfers between devices, local_heads(): moved.append(lax.ppermute(packed[k], ('seq', 'head'), pairs))  8.25 us
    pallas_call x9, Pallas kernels, call(): pl.pallas_call(kernel, in_specs=[pl.BlockSpec(memory_space=place) for pla...  7.77 us
    ppermute x2, waiting for transfers between devices, local_heads(): owned.append(lax.ppermute(summed, ('seq', 'wt', 'head'), pairs))  6.97 us
    ppermute x6, starting transfers between devices, along(): return lax.ppermute(shard, 'seq', [(z, z ^ m) for z in range(4)])  5.46 us
    ppermute x1, starting transfers between devices, local_heads(): sibling = lax.ppermute(joined, 'head', swap)  4.77 us
  transfers between devices with their start and end apart: 16, of which 11 were waited for; matrix products, arithmetic and copies ran while one was open for 0% of the time, Pallas kernels for 6%

profile of v12, /device:TPU:1, one launch (start us, length us, event | category | flops | bytes accessed | tf_op | source)
XLA Modules:
  0.0 72.2 jit_solution(14951316815292822333)
XLA Ops:
  0.6 0.0 copy-start.1
  0.6 2.1 %shard_map.95 = (bf16[320,384]{1,0:T(8,128)(2,1)}, bf16[320,384]{1,0:T(8,128)(2,1)}, bf16[160,384]{1,0:T(8,128)(2,1)}, bf16[160,384]{1,0:T(8,128)(2,1)}) custom-call(bf16[160,768]{1,0:T(8,128)(2,1)} %queries.1, bf16[160,768]{1,0:T(8,128)(2,1)} %keys.1, bf16[160,768]{1,0:T(8,128)(2,1)} %values.1), custom_call_target="tpu_custom_call" | custom-call | tf_op jit(solution)/shard_map/pallas_call | solution.py:255
  2.8 5.6 %collective-permute-start = (bf16[320,384]{1,0:T(8,128)(2,1)}, bf16[320,384]{1,0:T(8,128)(2,1)S(1)}, u32[]{:S(2)}, u32[]{:S(2)}) collective-permute-start(bf16[320,384]{1,0:T(8,128)(2,1)} %get-tuple-element.16), channel_id=1, source_target_pairs={{0,0},{1,8},{4,4},{5,12},{8,1},{9,9},{12,5},{13,13},{2,2},{3,10},{... | collective-permute-start | bytes 737288 | tf_op jit(solution)/shard_map/ppermute | solution.py:301
  8.4 1.1 %collective-permute-start.1 = (bf16[320,384]{1,0:T(8,128)(2,1)}, bf16[320,384]{1,0:T(8,128)(2,1)S(1)}, u32[]{:S(2)}, u32[]{:S(2)}) collective-permute-start(bf16[320,384]{1,0:T(8,128)(2,1)} %get-tuple-element.17), channel_id=1, source_target_pairs={{0,4},{1,12},{4,0},{5,8},{8,5},{9,13},{12,1},{13,9},{2,6},{3,14},{... | collective-permute-start | bytes 737288 | tf_op jit(solution)/shard_map/ppermute | solution.py:301
  9.5 0.0 collective-permute-start.2
  9.5 2.6 %collective-permute-start.3 = (bf16[160,384]{1,0:T(8,128)(2,1)}, bf16[160,384]{1,0:T(8,128)(2,1)S(1)}, u32[]{:S(2)}, u32[]{:S(2)}) collective-permute-start(bf16[160,384]{1,0:T(8,128)(2,1)} %get-tuple-element.19), channel_id=1, source_target_pairs={{0,5},{1,13},{4,1},{5,9},{8,4},{9,12},{12,0},{13,8},{2,7},{3,15},{... | collective-permute-start | bytes 368648 | tf_op jit(solution)/shard_map/ppermute | solution.py:301
  12.1 6.9 %collective-permute-done.2.refs_2_ = bf16[160,384]{1,0:T(8,128)(2,1)S(1)} collective-permute-done((bf16[160,384]{1,0:T(8,128)(2,1)}, bf16[160,384]{1,0:T(8,128)(2,1)S(1)}, u32[]{:S(2)}, u32[]{:S(2)}) %collective-permute-start.2) | collective-permute-done | bytes 122912 | tf_op jit(solution)/shard_map/ppermute | solution.py:301
  19.1 1.3 %collective-permute-done.3.refs_3_ = bf16[160,384]{1,0:T(8,128)(2,1)S(1)} collective-permute-done((bf16[160,384]{1,0:T(8,128)(2,1)}, bf16[160,384]{1,0:T(8,128)(2,1)S(1)}, u32[]{:S(2)}, u32[]{:S(2)}) %collective-permute-start.3) | collective-permute-done | bytes 122912 | tf_op jit(solution)/shard_map/ppermute | solution.py:301
  20.4 0.0 collective-permute-done.refs_0_
  20.4 0.0 collective-permute-done.1.refs_1_
  20.4 4.8 %collective-permute-start.4 = (bf16[640,384]{1,0:T(8,128)(2,1)S(1)}, bf16[640,384]{1,0:T(8,128)(2,1)S(1)}, u32[]{:S(2)}, u32[]{:S(2)}) collective-permute-start(bf16[640,384]{1,0:T(8,128)(2,1)S(1)} %shard_map.96), channel_id=1, source_target_pairs={{0,1},{1,0},{2,3},{3,2},{4,5},{5,4},{6,7},{7,6},{8,9},{9,8},{10,11... | collective-permute-start | bytes 1474568 | tf_op jit(solution)/shard_map/ppermute | solution.py:303
  25.2 1.5 %collective-permute-done.4.refs_4_ = bf16[640,384]{1,0:T(8,128)(2,1)S(1)} collective-permute-done((bf16[640,384]{1,0:T(8,128)(2,1)S(1)}, bf16[640,384]{1,0:T(8,128)(2,1)S(1)}, u32[]{:S(2)}, u32[]{:S(2)}) %collective-permute-start.4) | collective-permute-done | bytes 491552 | tf_op jit(solution)/shard_map/ppermute | solution.py:303
  26.7 0.0 copy-done.1
  26.7 0.4 collective-permute-start.10
  27.1 1.6 %shard_map.97 = (bf16[160,384]{1,0:T(8,128)(2,1)S(1)}, bf16[160,384]{1,0:T(8,128)(2,1)S(1)}) custom-call(bf16[320,384]{1,0:T(8,128)(2,1)S(1)} %collective-permute-done.refs_0_, bf16[320,384]{1,0:T(8,128)(2,1)S(1)} %collective-permute-done.1.refs_1_, bf16[160,384]{1,0:T(8,128)(2,1)S(1)} %collective-permute-done.2.refs_2_, ...), custom_call_target="tpu_custom_call" | custom-call | flops 314572800 | tf_op jit(solution)/shard_map/pallas_call | solution.py:255
  28.7 2.9 %collective-permute-start.5 = (bf16[160,384]{1,0:T(8,128)(2,1)S(1)}, bf16[160,384]{1,0:T(8,128)(2,1)S(1)}, u32[]{:S(2)}, u32[]{:S(2)}) collective-permute-start(bf16[160,384]{1,0:T(8,128)(2,1)S(1)} %get-tuple-element.21.refs_0_), channel_id=1, source_target_pairs={{0,8},{4,12},{8,0},{12,4},{1,9},{5,13},{9,1},{13,5},{2,10},{6,14},... | collective-permute-start | bytes 368648 | tf_op jit(solution)/shard_map/ppermute | solution.py:241
  31.6 0.0 collective-permute-start.6
  31.6 6.0 %collective-permute-done.5.refs_2_ = bf16[160,384]{1,0:T(8,128)(2,1)S(1)} collective-permute-done((bf16[160,384]{1,0:T(8,128)(2,1)S(1)}, bf16[160,384]{1,0:T(8,128)(2,1)S(1)}, u32[]{:S(2)}, u32[]{:S(2)}) %collective-permute-start.5) | collective-permute-done | bytes 122912 | tf_op jit(solution)/shard_map/ppermute | solution.py:241
  37.6 0.0 collective-permute-done.6.refs_1_
  37.6 1.2 %collective-permute-start.9 = (bf16[160,384]{1,0:T(8,128)(2,1)S(1)}, bf16[160,384]{1,0:T(8,128)(2,1)S(1)}, u32[]{:S(2)}, u32[]{:S(2)}) collective-permute-start(bf16[160,384]{1,0:T(8,128)(2,1)S(1)} %collective-permute-done.5.refs_2_), channel_id=1, source_target_pairs={{0,4},{4,0},{8,12},{12,8},{1,5},{5,1},{9,13},{13,9},{2,6},{6,2},{1... | collective-permute-start | bytes 368648 | tf_op jit(solution)/shard_map/ppermute | solution.py:241
  38.8 0.9 %collective-permute-start.8 = (bf16[160,384]{1,0:T(8,128)(2,1)S(1)}, bf16[160,384]{1,0:T(8,128)(2,1)S(1)}, u32[]{:S(2)}, u32[]{:S(2)}) collective-permute-start(bf16[160,384]{1,0:T(8,128)(2,1)S(1)} %get-tuple-element.22.refs_0_), channel_id=1, source_target_pairs={{0,8},{4,12},{8,0},{12,4},{1,9},{5,13},{9,1},{13,5},{2,10},{6,14},... | collective-permute-start | bytes 368648 | tf_op jit(solution)/shard_map/ppermute | solution.py:241
  39.7 0.5 collective-permute-start.7
  40.2 1.1 %collective-permute-done.9.refs_3_ = bf16[160,384]{1,0:T(8,128)(2,1)S(1)} collective-permute-done((bf16[160,384]{1,0:T(8,128)(2,1)S(1)}, bf16[160,384]{1,0:T(8,128)(2,1)S(1)}, u32[]{:S(2)}, u32[]{:S(2)}) %collective-permute-start.9) | collective-permute-done | bytes 122912 | tf_op jit(solution)/shard_map/ppermute | solution.py:241
  41.3 0.0 collective-permute-done.10.refs_5_
  41.3 0.9 %shard_map.98 = (bf16[80,1280]{1,0:T(8,128)(2,1)S(1)}, bf16[80,1280]{1,0:T(8,128)(2,1)S(1)}) custom-call(bf16[160,384]{1,0:T(8,128)(2,1)S(1)} %get-tuple-element.21.refs_0_, bf16[160,384]{1,0:T(8,128)(2,1)S(1)} %collective-permute-done.6.refs_1_, bf16[160,384]{1,0:T(8,128)(2,1)S(1)} %collective-permute-done.5.refs_2_, ...), custom_call_target="tpu_custom_call" | custom-call | flops 629145600 | tf_op jit(solution)/shard_map/pallas_call | solution.py:255
  42.2 3.2 %collective-permute-done.8.refs_2_ = bf16[160,384]{1,0:T(8,128)(2,1)S(1)} collective-permute-done((bf16[160,384]{1,0:T(8,128)(2,1)S(1)}, bf16[160,384]{1,0:T(8,128)(2,1)S(1)}, u32[]{:S(2)}, u32[]{:S(2)}) %collective-permute-start.8) | collective-permute-done | bytes 122912 | tf_op jit(solution)/shard_map/ppermute | solution.py:241
  45.4 0.0 collective-permute-start.11
  45.4 1.2 %collective-permute-start.12 = (bf16[80,1280]{1,0:T(8,128)(2,1)S(1)}, bf16[80,1280]{1,0:T(8,128)(2,1)S(1)}, u32[]{:S(2)}, u32[]{:S(2)}) collective-permute-start(bf16[80,1280]{1,0:T(8,128)(2,1)S(1)} %get-tuple-element.25), channel_id=1, source_target_pairs={{0,2},{2,0},{1,3},{3,1},{4,6},{6,4},{5,7},{7,5},{8,10},{10,8},{9,1... | collective-permute-start | bytes 614408 | tf_op jit(solution)/shard_map/ppermute | solution.py:341
  46.6 0.0 copy-start.4
  46.6 0.0 copy-start.3
  46.6 0.3 collective-permute-start.14
  46.9 0.7 %collective-permute-done.7.refs_1_ = bf16[160,384]{1,0:T(8,128)(2,1)S(1)} collective-permute-done((bf16[160,384]{1,0:T(8,128)(2,1)S(1)}, bf16[160,384]{1,0:T(8,128)(2,1)S(1)}, u32[]{:S(2)}, u32[]{:S(2)}) %collective-permute-start.7) | collective-permute-done | bytes 122912 | tf_op jit(solution)/shard_map/ppermute | solution.py:241
  47.6 2.1 %collective-permute-done.11.refs_3_ = bf16[160,384]{1,0:T(8,128)(2,1)S(1)} collective-permute-done((bf16[160,384]{1,0:T(8,128)(2,1)S(1)}, bf16[160,384]{1,0:T(8,128)(2,1)S(1)}, u32[]{:S(2)}, u32[]{:S(2)}) %collective-permute-start.11) | collective-permute-done | bytes 122912 | tf_op jit(solution)/shard_map/ppermute | solution.py:241
  49.8 0.9 %shard_map.99 = (f32[80,1280]{1,0:T(8,128)S(1)}, f32[80,1280]{1,0:T(8,128)S(1)}) custom-call(bf16[160,384]{1,0:T(8,128)(2,1)S(1)} %get-tuple-element.22.refs_0_, bf16[160,384]{1,0:T(8,128)(2,1)S(1)} %collective-permute-done.7.refs_1_, bf16[160,384]{1,0:T(8,128)(2,1)S(1)} %collective-permute-done.8.refs_2_, ...), custom_call_target="tpu_custom_call" | custom-call | flops 5033164800 | tf_op jit(solution)/shard_map/pallas_call | solution.py:255
  50.7 0.0 copy-start.2
  50.7 2.5 %collective-permute-done.14.arrived = bf16[80,1280]{1,0:T(8,128)(2,1)S(1)} collective-permute-done((bf16[80,1280]{1,0:T(8,128)(2,1)S(1)}, bf16[80,1280]{1,0:T(8,128)(2,1)S(1)}, u32[]{:S(2)}, u32[]{:S(2)}) %collective-permute-start.14) | collective-permute-done | bytes 204832 | tf_op jit(solution)/shard_map/ppermute | solution.py:341
  53.2 0.1 shard_map.101
  53.2 6.1 %collective-permute-start.15 = (bf16[80,1280]{1,0:T(8,128)(2,1)S(1)}, bf16[80,1280]{1,0:T(8,128)(2,1)S(1)}, u32[]{:S(2)}, u32[]{:S(2)}) collective-permute-start(bf16[80,1280]{1,0:T(8,128)(2,1)S(1)} %shard_map.101), channel_id=1, source_target_pairs={{0,4},{1,12},{2,0},{3,8},{4,5},{5,13},{6,1},{7,9},{8,6},{9,14},{10... | collective-permute-start | bytes 614408 | tf_op jit(solution)/shard_map/ppermute | solution.py:349
  59.4 0.0 collective-permute-done.12.arrived
  59.4 3.7 %collective-permute-start.13 = (bf16[80,1280]{1,0:T(8,128)(2,1)S(1)}, bf16[80,1280]{1,0:T(8,128)(2,1)S(1)}, u32[]{:S(2)}, u32[]{:S(2)}) collective-permute-start(bf16[80,1280]{1,0:T(8,128)(2,1)S(1)} %shard_map.100), channel_id=1, source_target_pairs={{0,0},{1,8},{2,4},{3,12},{4,1},{5,9},{6,5},{7,13},{8,2},{9,10},{10... | collective-permute-start | bytes 614408 | tf_op jit(solution)/shard_map/ppermute | solution.py:349
  63.1 0.0 copy-done.4
  63.1 0.0 copy-done.3
  63.1 0.0 copy-done
  63.1 0.0 copy-done.2
  63.1 0.8 %shard_map.102.resting = f32[160,1280]{1,0:T(8,128)S(1)} custom-call(s32[4]{0:T(128)S(1)} %copy-done.3, f32[160,1280]{1,0:T(8,128)S(1)} %copy-done.2, f32[4,160,1280]{2,1,0:T(8,128)S(1)} %copy-done), custom_call_target="tpu_custom_call" | custom-call | tf_op jit(solution)/shard_map/pallas_call | solution.py:255
  63.9 2.0 %collective-permute-done.15.owned1 = bf16[80,1280]{1,0:T(8,128)(2,1)S(1)} collective-permute-done((bf16[80,1280]{1,0:T(8,128)(2,1)S(1)}, bf16[80,1280]{1,0:T(8,128)(2,1)S(1)}, u32[]{:S(2)}, u32[]{:S(2)}) %collective-permute-start.15) | collective-permute-done | bytes 204832 | tf_op jit(solution)/shard_map/ppermute | solution.py:349
  65.9 5.0 %collective-permute-done.13.owned0 = bf16[80,1280]{1,0:T(8,128)(2,1)S(1)} collective-permute-done((bf16[80,1280]{1,0:T(8,128)(2,1)S(1)}, bf16[80,1280]{1,0:T(8,128)(2,1)S(1)}, u32[]{:S(2)}, u32[]{:S(2)}) %collective-permute-start.13) | collective-permute-done | bytes 204832 | tf_op jit(solution)/shard_map/ppermute | solution.py:349
  70.9 1.3 %shard_map.103 = (f32[160,1280]{1,0:T(8,128)}, f32[160,1280]{1,0:T(8,128)}) custom-call(bf16[80,1280]{1,0:T(8,128)(2,1)S(1)} %collective-permute-done.13.owned0, bf16[80,1280]{1,0:T(8,128)(2,1)S(1)} %collective-permute-done.15.owned1, f32[1,1280]{1,0:T(1,128)S(1)} %broadcast_in_dim.3.gate, f32[160,1280]{1,0:T(8,128)S(1)} %shard_map.102.resting), custom_call_target="tpu_custom_call" | custom-call | tf_op jit(solution)/shard_map/pallas_call | solution.py:255
  (4 shorter events, 0.1 us)
Async XLA Ops:
  0.6 26.1 %copy-start.1 = (bf16[768,1280]{1,0:T(8,128)(2,1)S(1)}, bf16[768,1280]{1,0:T(8,128)(2,1)}, u32[]{:S(2)}) copy-start(bf16[768,1280]{1,0:T(8,128)(2,1)} %refs_4_.3) | copy-start | bytes 5898244
  2.8 17.6 %collective-permute-start = (bf16[320,384]{1,0:T(8,128)(2,1)}, bf16[320,384]{1,0:T(8,128)(2,1)S(1)}, u32[]{:S(2)}, u32[]{:S(2)}) collective-permute-start(bf16[320,384]{1,0:T(8,128)(2,1)} %get-tuple-element.16), channel_id=1, source_target_pairs={{0,0},{1,8},{4,4},{5,12},{8,1},{9,9},{12,5},{13,13},{2,2},{3,10},{... | collective-permute-start | bytes 737288 | tf_op jit(solution)/shard_map/ppermute | solution.py:301
  8.4 12.0 %collective-permute-start.1 = (bf16[320,384]{1,0:T(8,128)(2,1)}, bf16[320,384]{1,0:T(8,128)(2,1)S(1)}, u32[]{:S(2)}, u32[]{:S(2)}) collective-permute-start(bf16[320,384]{1,0:T(8,128)(2,1)} %get-tuple-element.17), channel_id=1, source_target_pairs={{0,4},{1,12},{4,0},{5,8},{8,5},{9,13},{12,1},{13,9},{2,6},{3,14},{... | collective-permute-start | bytes 737288 | tf_op jit(solution)/shard_map/ppermute | solution.py:301
  9.5 9.6 %collective-permute-start.2 = (bf16[160,384]{1,0:T(8,128)(2,1)}, bf16[160,384]{1,0:T(8,128)(2,1)S(1)}, u32[]{:S(2)}, u32[]{:S(2)}) collective-permute-start(bf16[160,384]{1,0:T(8,128)(2,1)} %get-tuple-element.18), channel_id=1, source_target_pairs={{0,1},{1,9},{4,5},{5,13},{8,0},{9,8},{12,4},{13,12},{2,3},{3,11},{... | collective-permute-start | bytes 368648 | tf_op jit(solution)/shard_map/ppermute | solution.py:301
  9.5 10.9 %collective-permute-start.3 = (bf16[160,384]{1,0:T(8,128)(2,1)}, bf16[160,384]{1,0:T(8,128)(2,1)S(1)}, u32[]{:S(2)}, u32[]{:S(2)}) collective-permute-start(bf16[160,384]{1,0:T(8,128)(2,1)} %get-tuple-element.19), channel_id=1, source_target_pairs={{0,5},{1,13},{4,1},{5,9},{8,4},{9,12},{12,0},{13,8},{2,7},{3,15},{... | collective-permute-start | bytes 368648 | tf_op jit(solution)/shard_map/ppermute | solution.py:301
  20.4 6.3 %collective-permute-start.4 = (bf16[640,384]{1,0:T(8,128)(2,1)S(1)}, bf16[640,384]{1,0:T(8,128)(2,1)S(1)}, u32[]{:S(2)}, u32[]{:S(2)}) collective-permute-start(bf16[640,384]{1,0:T(8,128)(2,1)S(1)} %shard_map.96), channel_id=1, source_target_pairs={{0,1},{1,0},{2,3},{3,2},{4,5},{5,4},{6,7},{7,6},{8,9},{9,8},{10,11... | collective-permute-start | bytes 1474568 | tf_op jit(solution)/shard_map/ppermute | solution.py:303
  26.7 14.6 %collective-permute-start.10 = (bf16[768,1280]{1,0:T(8,128)(2,1)S(1)}, bf16[768,1280]{1,0:T(8,128)(2,1)S(1)}, u32[]{:S(2)}, u32[]{:S(2)}) collective-permute-start(bf16[768,1280]{1,0:T(8,128)(2,1)S(1)} %copy-done.1), channel_id=1, source_target_pairs={{0,1},{1,0},{2,3},{3,2},{4,5},{5,4},{6,7},{7,6},{8,9},{9,8},{10,11... | collective-permute-start | bytes 5898248 | tf_op jit(solution)/shard_map/ppermute | solution.py:305
  28.7 8.9 %collective-permute-start.5 = (bf16[160,384]{1,0:T(8,128)(2,1)S(1)}, bf16[160,384]{1,0:T(8,128)(2,1)S(1)}, u32[]{:S(2)}, u32[]{:S(2)}) collective-permute-start(bf16[160,384]{1,0:T(8,128)(2,1)S(1)} %get-tuple-element.21.refs_0_), channel_id=1, source_target_pairs={{0,8},{4,12},{8,0},{12,4},{1,9},{5,13},{9,1},{13,5},{2,10},{6,14},... | collective-permute-start | bytes 368648 | tf_op jit(solution)/shard_map/ppermute | solution.py:241
  31.6 6.0 %collective-permute-start.6 = (bf16[160,384]{1,0:T(8,128)(2,1)S(1)}, bf16[160,384]{1,0:T(8,128)(2,1)S(1)}, u32[]{:S(2)}, u32[]{:S(2)}) collective-permute-start(bf16[160,384]{1,0:T(8,128)(2,1)S(1)} %get-tuple-element.21.refs_0_), channel_id=1, source_target_pairs={{0,4},{4,0},{8,12},{12,8},{1,5},{5,1},{9,13},{13,9},{2,6},{6,2},{1... | collective-permute-start | bytes 368648 | tf_op jit(solution)/shard_map/ppermute | solution.py:241
  37.6 3.7 %collective-permute-start.9 = (bf16[160,384]{1,0:T(8,128)(2,1)S(1)}, bf16[160,384]{1,0:T(8,128)(2,1)S(1)}, u32[]{:S(2)}, u32[]{:S(2)}) collective-permute-start(bf16[160,384]{1,0:T(8,128)(2,1)S(1)} %collective-permute-done.5.refs_2_), channel_id=1, source_target_pairs={{0,4},{4,0},{8,12},{12,8},{1,5},{5,1},{9,13},{13,9},{2,6},{6,2},{1... | collective-permute-start | bytes 368648 | tf_op jit(solution)/shard_map/ppermute | solution.py:241
  38.8 6.7 %collective-permute-start.8 = (bf16[160,384]{1,0:T(8,128)(2,1)S(1)}, bf16[160,384]{1,0:T(8,128)(2,1)S(1)}, u32[]{:S(2)}, u32[]{:S(2)}) collective-permute-start(bf16[160,384]{1,0:T(8,128)(2,1)S(1)} %get-tuple-element.22.refs_0_), channel_id=1, source_target_pairs={{0,8},{4,12},{8,0},{12,4},{1,9},{5,13},{9,1},{13,5},{2,10},{6,14},... | collective-permute-start | bytes 368648 | tf_op jit(solution)/shard_map/ppermute | solution.py:241
  39.7 8.0 %collective-permute-start.7 = (bf16[160,384]{1,0:T(8,128)(2,1)S(1)}, bf16[160,384]{1,0:T(8,128)(2,1)S(1)}, u32[]{:S(2)}, u32[]{:S(2)}) collective-permute-start(bf16[160,384]{1,0:T(8,128)(2,1)S(1)} %get-tuple-element.22.refs_0_), channel_id=1, source_target_pairs={{0,4},{4,0},{8,12},{12,8},{1,5},{5,1},{9,13},{13,9},{2,6},{6,2},{1... | collective-permute-start | bytes 368648 | tf_op jit(solution)/shard_map/ppermute | solution.py:241
  45.4 4.3 %collective-permute-start.11 = (bf16[160,384]{1,0:T(8,128)(2,1)S(1)}, bf16[160,384]{1,0:T(8,128)(2,1)S(1)}, u32[]{:S(2)}, u32[]{:S(2)}) collective-permute-start(bf16[160,384]{1,0:T(8,128)(2,1)S(1)} %collective-permute-done.8.refs_2_), channel_id=1, source_target_pairs={{0,4},{4,0},{8,12},{12,8},{1,5},{5,1},{9,13},{13,9},{2,6},{6,2},{1... | collective-permute-start | bytes 368648 | tf_op jit(solution)/shard_map/ppermute | solution.py:241
  45.4 13.9 %collective-permute-start.12 = (bf16[80,1280]{1,0:T(8,128)(2,1)S(1)}, bf16[80,1280]{1,0:T(8,128)(2,1)S(1)}, u32[]{:S(2)}, u32[]{:S(2)}) collective-permute-start(bf16[80,1280]{1,0:T(8,128)(2,1)S(1)} %get-tuple-element.25), channel_id=1, source_target_pairs={{0,2},{2,0},{1,3},{3,1},{4,6},{6,4},{5,7},{7,5},{8,10},{10,8},{9,1... | collective-permute-start | bytes 614408 | tf_op jit(solution)/shard_map/ppermute | solution.py:341
  46.6 16.5 %copy-start.4 = (f32[1280]{0:T(1024)S(1)}, f32[1280]{0:T(1024)}, u32[]{:S(2)}) copy-start(f32[1280]{0:T(1024)} %param.12) | copy-start | bytes 15364
  46.6 16.5 %copy-start.3 = (s32[4]{0:T(128)S(1)}, s32[4]{0:T(128)}, u32[]{:S(2)}) copy-start(s32[4]{0:T(128)} %flags.1) | copy-start | bytes 52
  46.6 6.6 %collective-permute-start.14 = (bf16[80,1280]{1,0:T(8,128)(2,1)S(1)}, bf16[80,1280]{1,0:T(8,128)(2,1)S(1)}, u32[]{:S(2)}, u32[]{:S(2)}) collective-permute-start(bf16[80,1280]{1,0:T(8,128)(2,1)S(1)} %get-tuple-element.29), channel_id=1, source_target_pairs={{0,2},{2,0},{1,3},{3,1},{4,6},{6,4},{5,7},{7,5},{8,10},{10,8},{9,1... | collective-permute-start | bytes 614408 | tf_op jit(solution)/shard_map/ppermute | solution.py:341
  49.8 13.4 %copy-start = (f32[4,160,1280]{2,1,0:T(8,128)S(1)}, f32[4,160,1280]{2,1,0:T(8,128)}, u32[]{:S(2)}) copy-start(f32[4,160,1280]{2,1,0:T(8,128)} %cached.1) | copy-start | bytes 9830404
  50.7 12.5 %copy-start.2 = (f32[160,1280]{1,0:T(8,128)S(1)}, f32[160,1280]{1,0:T(8,128)}, u32[]{:S(2)}) copy-start(f32[160,1280]{1,0:T(8,128)} %hidden.1) | copy-start | bytes 2457604
  53.2 12.7 %collective-permute-start.15 = (bf16[80,1280]{1,0:T(8,128)(2,1)S(1)}, bf16[80,1280]{1,0:T(8,128)(2,1)S(1)}, u32[]{:S(2)}, u32[]{:S(2)}) collective-permute-start(bf16[80,1280]{1,0:T(8,128)(2,1)S(1)} %shard_map.101), channel_id=1, source_target_pairs={{0,4},{1,12},{2,0},{3,8},{4,5},{5,13},{6,1},{7,9},{8,6},{9,14},{10... | collective-permute-start | bytes 614408 | tf_op jit(solution)/shard_map/ppermute | solution.py:349
  59.4 11.5 %collective-permute-start.13 = (bf16[80,1280]{1,0:T(8,128)(2,1)S(1)}, bf16[80,1280]{1,0:T(8,128)(2,1)S(1)}, u32[]{:S(2)}, u32[]{:S(2)}) collective-permute-start(bf16[80,1280]{1,0:T(8,128)(2,1)S(1)} %shard_map.100), channel_id=1, source_target_pairs={{0,0},{1,8},{2,4},{3,12},{4,1},{5,9},{6,5},{7,13},{8,2},{9,10},{10... | collective-permute-start | bytes 614408 | tf_op jit(solution)/shard_map/ppermute | solution.py:349

commit v13 on v10

--- a/solution.py
+++ b/solution.py
@@ -1,3 +1,5 @@
+import functools
+
 import jax
 import jax.numpy as jnp
 from jax import lax
@@ -7,7 +9,7 @@
 
 HEAD_DIM = 128
 VMEM_BYTES = 48 * 1024 * 1024
-PACK_BYTES = 59 * 1024 * 1024 + 400 * 1024
+PACK_BYTES = 53 * 1024 * 1024 + 128 * 1024
 LOG2_E = 1.4426950408889634
 
 
@@ -97,35 +99,25 @@
 
 
 def pack_kernel(queries, keys, values, *refs):
-    outs, stages, read_sems, write_sems = refs[:4], refs[4:8], refs[8], refs[9]
+    outs, sems = refs[:4], refs[4]
     rows, width = queries.shape[0], outs[0].shape[1]
     half = rows // 2
     zh, zl = bits()
-    reads = []
-    for k, stage in enumerate(stages):
+    copies = []
+    for k in range(4):
         part = pl.ds(pl.multiple_of(flip(zh, k // 2) * half, 16), half)
         columns = pl.ds(pl.multiple_of(flip(zl, k % 2) * width, 128), width)
         moves = [
-            (keys.at[part, columns], stage.at[pl.ds(0, half), :]),
-            (values.at[part, columns], stage.at[pl.ds(half, half), :]),
+            (keys.at[part, columns], outs[k].at[pl.ds(0, half), :]),
+            (values.at[part, columns], outs[k].at[pl.ds(half, half), :]),
         ]
         if k < 2:
-            moves.append((queries.at[:, columns], stage.at[pl.ds(rows, rows), :]))
-        reads.append(
-            [
-                pltpu.make_async_copy(start, end, read_sems.at[3 * k + i])
-                for i, (start, end) in enumerate(moves)
-            ]
-        )
-        for copy in reads[-1]:
-            copy.start()
-    writes = []
-    for k, stage in enumerate(stages):
-        for copy in reads[k]:
-            copy.wait()
-        writes.append(pltpu.make_async_copy(stage, outs[k], write_sems.at[k]))
-        writes[-1].start()
-    for copy in writes:
+            moves.append((queries.at[:, columns], outs[k].at[pl.ds(rows, rows), :]))
+        for start, end in moves:
+            copies.append(pltpu.make_async_copy(start, end, sems.at[len(copies)]))
+    for copy in copies:
+        copy.start()
+    for copy in copies:
         copy.wait()
 
 
@@ -210,13 +202,18 @@
     out[...] = total
 
 
-def final_kernel(owned0, owned1, gate, resting, mixed, fresh):
-    count = owned0.shape[1]
-    for h, owned in enumerate((owned0, owned1)):
-        columns = slice(h * count, (h + 1) * count)
-        delta = owned[...].astype(jnp.float32) * gate[:, columns]
-        fresh[:, columns] = delta
-        mixed[:, columns] = resting[:, columns] + delta
+def final_kernel(first, owned, gate, resting, *refs):
+    mixed, fresh, mixed_part, fresh_part, sems = refs[-5:]
+    columns = pl.ds(first, owned.shape[1])
+    delta = owned[...].astype(jnp.float32) * gate[:, columns]
+    fresh_part[...] = delta
+    copy_fresh = pltpu.make_async_copy(fresh_part, fresh.at[:, columns], sems.at[0])
+    copy_fresh.start()
+    mixed_part[...] = resting[:, columns] + delta
+    copy_mixed = pltpu.make_async_copy(mixed_part, mixed.at[:, columns], sems.at[1])
+    copy_mixed.start()
+    copy_fresh.wait()
+    copy_mixed.wait()
 
 
 def call(
@@ -261,15 +258,10 @@
         pack_kernel,
         (queries, key_vectors, value_vectors),
         [((2 * rows, width), bf16)] * 2 + [((rows, width), bf16)] * 2,
-        [pltpu.VMEM((2 * rows, width), bf16)] * 2
-        + [pltpu.VMEM((rows, width), bf16)] * 2
-        + [pltpu.SemaphoreType.DMA((12,)), pltpu.SemaphoreType.DMA((4,))],
+        [pltpu.SemaphoreType.DMA((10,))],
         space=pl.ANY,
-        out_space=pl.ANY,
         vmem=PACK_BYTES,
     )
-    late_weight, _ = lax.optimization_barrier((out_weight, packed[0]))
-    weight_c = lax.ppermute(late_weight, "head", swap)
     moved = []
     for k in range(4):
         k1, k0 = k // 2, k % 2
@@ -281,7 +273,8 @@
         moved.append(lax.ppermute(packed[k], ("seq", "head"), pairs))
     (joined,) = call(join_kernel, moved, [((4 * rows, width), bf16)])
     sibling = lax.ppermute(joined, "head", swap)
-    sibling, _ = lax.optimization_barrier((sibling, weight_c))
+    late_weight, _ = lax.optimization_barrier((out_weight, sibling))
+    weight_c = lax.ppermute(late_weight, "head", swap)
     parts = call(
         attention_kernel,
         moved + [sibling],
@@ -329,13 +322,22 @@
     (resting,) = call(
         rest_kernel, (skip_flags, hidden_state, cached_deltas), [((rows, columns), jnp.float32)]
     )
-    return tuple(
-        call(
-            final_kernel,
-            (*owned, gate_values[None, :], resting),
-            [((rows, columns), jnp.float32)] * 2,
-        )
-    )
+    gate = gate_values[None, :]
+    results = ()
+    for h, part in enumerate(owned):
+        results = pl.pallas_call(
+            functools.partial(final_kernel, h * count),
+            in_specs=[pl.BlockSpec(memory_space=pltpu.VMEM)] * 3
+            + [pl.BlockSpec(memory_space=pl.ANY)] * len(results),
+            out_specs=[pl.BlockSpec(memory_space=pl.ANY)] * 2,
+            out_shape=[jax.ShapeDtypeStruct((rows, columns), jnp.float32)] * 2,
+            scratch_shapes=[pltpu.VMEM((rows, count), jnp.float32)] * 2
+            + [pltpu.SemaphoreType.DMA((2,))],
+            input_output_aliases={3 + i: i for i in range(len(results))},
+            compiler_params=pltpu.CompilerParams(vmem_limit_bytes=VMEM_BYTES),
+            cost_estimate=pl.CostEstimate(flops=0, bytes_accessed=0, transcendentals=0),
+        )(part, gate, resting, *results)
+    return tuple(results)
 
 
 def solution(mesh):

time: 69.9 us -> 68.8 us (0.984)
  starting transfers between devices: 24.4 us -> 23.5 us
    pallas_call x9 -> x8, Pallas kernels: 7.69 us -> 5.64 us  [call(): pl.pallas_call(kernel, in_specs=[pl.BlockSpec(memory_space=place) for pla...]
    pallas_call x0 -> x2, Pallas kernels: none -> 1.9 us  [local_heads(): pl.pallas_call(functools.partial(final_kernel, h * count), in_specs=[pl.B...]
    ppermute x6, waiting for transfers between devices: 10.5 us -> 12 us  [local_heads(): shards.append(lax.ppermute(parts[1 - kept ^ m % 2], 'seq', pairs))]
  transfers between devices with their start and end apart: 16 -> 16, of which waited for: 7 -> 6; matrix products, arithmetic and copies ran while one was open for 0% -> 0% of each run, Pallas kernels for 4% -> 8%
where the time goes in v13:
time: 68.8 us; the launch traced here: 68.3 us
  waiting for transfers between devices  36.4 us (53%)
  starting transfers between devices  23.5 us (34%)
  Pallas kernels  7.54 us (11%)
  between operations  0.81 us (1%)
    ppermute x4, waiting for transfers between devices, local_heads(): moved.append(lax.ppermute(packed[k], ('seq', 'head'), pairs))  14.6 us
    ppermute x6, waiting for transfers between devices, local_heads(): shards.append(lax.ppermute(parts[1 - kept ^ m % 2], 'seq', pairs))  12 us
    ppermute x6, starting transfers between devices, local_heads(): shards.append(lax.ppermute(parts[1 - kept ^ m % 2], 'seq', pairs))  8.89 us
    ppermute x2, waiting for transfers between devices, local_heads(): owned.append(lax.ppermute(summed, ('seq', 'wt', 'head'), pairs))  7.96 us
    ppermute x2, starting transfers between devices, local_heads(): owned.append(lax.ppermute(summed, ('seq', 'wt', 'head'), pairs))  6.35 us
    ppermute x4, starting transfers between devices, local_heads(): moved.append(lax.ppermute(packed[k], ('seq', 'head'), pairs))  6.01 us
    pallas_call x8, Pallas kernels, call(): pl.pallas_call(kernel, in_specs=[pl.BlockSpec(memory_space=place) for pla...  5.64 us
    ppermute x2, starting transfers between devices, local_heads(): arrived = lax.ppermute(part, 'wt', swap)  2.09 us
  transfers between devices with their start and end apart: 16, of which 6 were waited for; matrix products, arithmetic and copies ran while one was open for 0% of the time, Pallas kernels for 8%

profile of v13, /device:TPU:2, one launch (start us, length us, event | category | flops | bytes accessed | tf_op | source)
XLA Modules:
  0.0 68.3 jit_solution(3573377645566497085)
XLA Ops:
  0.6 0.0 copy-start.1
  0.6 1.4 %shard_map.95 = (bf16[320,384]{1,0:T(8,128)(2,1)S(1)}, bf16[320,384]{1,0:T(8,128)(2,1)S(1)}, bf16[160,384]{1,0:T(8,128)(2,1)S(1)}, bf16[160,384]{1,0:T(8,128)(2,1)S(1)}) custom-call(bf16[160,768]{1,0:T(8,128)(2,1)} %queries.1, bf16[160,768]{1,0:T(8,128)(2,1)} %keys.1, bf16[160,768]{1,0:T(8,128)(2,1)} %values.1), custom_call_target="tpu_custom_call" | custom-call | tf_op jit(solution)/shard_map/pallas_call | solution.py:230
  2.0 0.7 collective-permute-start
  2.7 1.6 %collective-permute-start.1 = (bf16[320,384]{1,0:T(8,128)(2,1)S(1)}, bf16[320,384]{1,0:T(8,128)(2,1)S(1)}, u32[]{:S(2)}, u32[]{:S(2)}) collective-permute-start(bf16[320,384]{1,0:T(8,128)(2,1)S(1)} %get-tuple-element.16), channel_id=1, source_target_pairs={{0,4},{1,12},{4,0},{5,8},{8,5},{9,13},{12,1},{13,9},{2,6},{3,14},{... | collective-permute-start | bytes 737288 | tf_op jit(solution)/shard_map/ppermute | solution.py:273
  4.3 3.4 %collective-permute-start.2 = (bf16[160,384]{1,0:T(8,128)(2,1)S(1)}, bf16[160,384]{1,0:T(8,128)(2,1)S(1)}, u32[]{:S(2)}, u32[]{:S(2)}) collective-permute-start(bf16[160,384]{1,0:T(8,128)(2,1)S(1)} %get-tuple-element.17), channel_id=1, source_target_pairs={{0,1},{1,9},{4,5},{5,13},{8,0},{9,8},{12,4},{13,12},{2,3},{3,11},{... | collective-permute-start | bytes 368648 | tf_op jit(solution)/shard_map/ppermute | solution.py:273
  7.7 0.3 collective-permute-start.3
  8.0 14.5 %collective-permute-done.2.refs_2_ = bf16[160,384]{1,0:T(8,128)(2,1)S(1)} collective-permute-done((bf16[160,384]{1,0:T(8,128)(2,1)S(1)}, bf16[160,384]{1,0:T(8,128)(2,1)S(1)}, u32[]{:S(2)}, u32[]{:S(2)}) %collective-permute-start.2) | collective-permute-done | bytes 122912 | tf_op jit(solution)/shard_map/ppermute | solution.py:273
  22.6 0.0 collective-permute-done.3.refs_3_
  22.6 0.0 collective-permute-done.refs_0_
  22.6 0.0 collective-permute-done.1.refs_1_
  22.6 0.1 collective-permute-start.4
  22.7 1.9 %collective-permute-done.4.refs_4_ = bf16[640,384]{1,0:T(8,128)(2,1)S(1)} collective-permute-done((bf16[640,384]{1,0:T(8,128)(2,1)S(1)}, bf16[640,384]{1,0:T(8,128)(2,1)S(1)}, u32[]{:S(2)}, u32[]{:S(2)}) %collective-permute-start.4) | collective-permute-done | bytes 491552 | tf_op jit(solution)/shard_map/ppermute | solution.py:275
  24.6 0.0 copy-done.1
  24.6 0.1 collective-permute-start.8
  24.7 1.6 %shard_map.97 = (bf16[160,384]{1,0:T(8,128)(2,1)S(1)}, bf16[160,384]{1,0:T(8,128)(2,1)S(1)}) custom-call(bf16[320,384]{1,0:T(8,128)(2,1)S(1)} %collective-permute-done.refs_0_, bf16[320,384]{1,0:T(8,128)(2,1)S(1)} %collective-permute-done.1.refs_1_, bf16[160,384]{1,0:T(8,128)(2,1)S(1)} %collective-permute-done.2.refs_2_, ...), custom_call_target="tpu_custom_call" | custom-call | flops 314572800 | tf_op jit(solution)/shard_map/pallas_call | solution.py:230
  26.4 3.4 %collective-permute-start.10 = (bf16[160,384]{1,0:T(8,128)(2,1)S(1)}, bf16[160,384]{1,0:T(8,128)(2,1)S(1)}, u32[]{:S(2)}, u32[]{:S(2)}) collective-permute-start(bf16[160,384]{1,0:T(8,128)(2,1)S(1)} %get-tuple-element.20.refs_0_), channel_id=1, source_target_pairs={{0,8},{4,12},{8,0},{12,4},{1,9},{5,13},{9,1},{13,5},{2,10},{6,14},... | collective-permute-start | bytes 368648 | tf_op jit(solution)/shard_map/ppermute | solution.py:297
  29.8 0.9 %collective-permute-start.11 = (bf16[160,384]{1,0:T(8,128)(2,1)S(1)}, bf16[160,384]{1,0:T(8,128)(2,1)S(1)}, u32[]{:S(2)}, u32[]{:S(2)}) collective-permute-start(bf16[160,384]{1,0:T(8,128)(2,1)S(1)} %get-tuple-element.19.refs_0_), channel_id=1, source_target_pairs={{0,12},{4,8},{8,4},{12,0},{1,13},{5,9},{9,5},{13,1},{2,14},{6,10},... | collective-permute-start | bytes 368648 | tf_op jit(solution)/shard_map/ppermute | solution.py:297
  30.7 0.0 collective-permute-start.9
  30.7 2.0 %collective-permute-start.5 = (bf16[160,384]{1,0:T(8,128)(2,1)S(1)}, bf16[160,384]{1,0:T(8,128)(2,1)S(1)}, u32[]{:S(2)}, u32[]{:S(2)}) collective-permute-start(bf16[160,384]{1,0:T(8,128)(2,1)S(1)} %get-tuple-element.20.refs_0_), channel_id=1, source_target_pairs={{0,4},{4,0},{8,12},{12,8},{1,5},{5,1},{9,13},{13,9},{2,6},{6,2},{1... | collective-permute-start | bytes 368648 | tf_op jit(solution)/shard_map/ppermute | solution.py:297
  32.7 6.5 %collective-permute-done.10.refs_2_ = bf16[160,384]{1,0:T(8,128)(2,1)S(1)} collective-permute-done((bf16[160,384]{1,0:T(8,128)(2,1)S(1)}, bf16[160,384]{1,0:T(8,128)(2,1)S(1)}, u32[]{:S(2)}, u32[]{:S(2)}) %collective-permute-start.10) | collective-permute-done | bytes 122912 | tf_op jit(solution)/shard_map/ppermute | solution.py:297
  39.2 0.0 collective-permute-start.6
  39.2 0.0 collective-permute-done.11.refs_3_
  39.2 2.5 %collective-permute-start.7 = (bf16[160,384]{1,0:T(8,128)(2,1)S(1)}, bf16[160,384]{1,0:T(8,128)(2,1)S(1)}, u32[]{:S(2)}, u32[]{:S(2)}) collective-permute-start(bf16[160,384]{1,0:T(8,128)(2,1)S(1)} %get-tuple-element.20.refs_0_), channel_id=1, source_target_pairs={{0,12},{4,8},{8,4},{12,0},{1,13},{5,9},{9,5},{13,1},{2,14},{6,10},... | collective-permute-start | bytes 368648 | tf_op jit(solution)/shard_map/ppermute | solution.py:297
  41.8 0.0 collective-permute-done.9.refs_1_
  41.8 0.0 collective-permute-done.8.refs_5_
  41.8 0.9 %shard_map.99 = (bf16[160,640]{1,0:T(8,128)(2,1)S(1)}, bf16[160,640]{1,0:T(8,128)(2,1)S(1)}) custom-call(bf16[160,384]{1,0:T(8,128)(2,1)S(1)} %get-tuple-element.20.refs_0_, bf16[160,384]{1,0:T(8,128)(2,1)S(1)} %collective-permute-done.9.refs_1_, bf16[160,384]{1,0:T(8,128)(2,1)S(1)} %collective-permute-done.10.refs_2_, ...), custom_call_target="tpu_custom_call" | custom-call | flops 629145600 | tf_op jit(solution)/shard_map/pallas_call | solution.py:230
  42.7 0.6 collective-permute-start.14
  43.3 0.0 copy-start.4
  43.3 1.5 %collective-permute-start.12 = (bf16[160,640]{1,0:T(8,128)(2,1)S(1)}, bf16[160,640]{1,0:T(8,128)(2,1)S(1)}, u32[]{:S(2)}, u32[]{:S(2)}) collective-permute-start(bf16[160,640]{1,0:T(8,128)(2,1)S(1)} %get-tuple-element.23), channel_id=1, source_target_pairs={{0,2},{2,0},{1,3},{3,1},{4,6},{6,4},{5,7},{7,5},{8,10},{10,8},{9,1... | collective-permute-start | bytes 614408 | tf_op jit(solution)/shard_map/ppermute | solution.py:319
  44.8 0.0 collective-permute-done.5.refs_1_
  44.8 5.5 %collective-permute-done.6.refs_2_ = bf16[160,384]{1,0:T(8,128)(2,1)S(1)} collective-permute-done((bf16[160,384]{1,0:T(8,128)(2,1)S(1)}, bf16[160,384]{1,0:T(8,128)(2,1)S(1)}, u32[]{:S(2)}, u32[]{:S(2)}) %collective-permute-start.6) | collective-permute-done | bytes 122912 | tf_op jit(solution)/shard_map/ppermute | solution.py:297
  50.2 0.0 collective-permute-done.7.refs_3_
  50.2 0.9 %shard_map.98 = (f32[160,640]{1,0:T(8,128)S(1)}, f32[160,640]{1,0:T(8,128)S(1)}) custom-call(bf16[160,384]{1,0:T(8,128)(2,1)S(1)} %get-tuple-element.19.refs_0_, bf16[160,384]{1,0:T(8,128)(2,1)S(1)} %collective-permute-done.5.refs_1_, bf16[160,384]{1,0:T(8,128)(2,1)S(1)} %collective-permute-done.6.refs_2_, ...), custom_call_target="tpu_custom_call" | custom-call | flops 5033164800 | tf_op jit(solution)/shard_map/pallas_call | solution.py:230
  51.1 0.0 copy-start.2
  51.1 0.0 collective-permute-done.14.arrived
  51.1 0.1 shard_map.102
  51.2 4.4 %collective-permute-start.15 = (bf16[160,640]{1,0:T(8,128)(2,1)S(1)}, bf16[160,640]{1,0:T(8,128)(2,1)S(1)}, u32[]{:S(2)}, u32[]{:S(2)}) collective-permute-start(bf16[160,640]{1,0:T(8,128)(2,1)S(1)} %shard_map.102), channel_id=1, source_target_pairs={{0,0},{1,8},{2,4},{3,12},{4,5},{5,13},{6,1},{7,9},{8,2},{9,10},{10... | collective-permute-start | bytes 614408 | tf_op jit(solution)/shard_map/ppermute | solution.py:321
  55.6 0.0 collective-permute-done.12.arrived
  55.7 1.9 %collective-permute-start.13 = (bf16[160,640]{1,0:T(8,128)(2,1)S(1)}, bf16[160,640]{1,0:T(8,128)(2,1)S(1)}, u32[]{:S(2)}, u32[]{:S(2)}) collective-permute-start(bf16[160,640]{1,0:T(8,128)(2,1)S(1)} %shard_map.100), channel_id=1, source_target_pairs={{0,0},{1,8},{2,4},{3,12},{4,5},{5,13},{6,1},{7,9},{8,2},{9,10},{10... | collective-permute-start | bytes 614408 | tf_op jit(solution)/shard_map/ppermute | solution.py:321
  57.6 0.0 copy-done.4
  57.6 0.0 copy-done.3
  57.6 0.0 copy-done
  57.7 0.0 copy-done.2
  57.7 0.8 %shard_map.101.resting = f32[160,1280]{1,0:T(8,128)S(1)} custom-call(s32[4]{0:T(128)S(1)} %copy-done.3, f32[160,1280]{1,0:T(8,128)S(1)} %copy-done.2, f32[4,160,1280]{2,1,0:T(8,128)S(1)} %copy-done), custom_call_target="tpu_custom_call" | custom-call | tf_op jit(solution)/shard_map/pallas_call | solution.py:230
  58.4 6.7 %collective-permute-done.15.owned = bf16[160,640]{1,0:T(8,128)(2,1)S(1)} collective-permute-done((bf16[160,640]{1,0:T(8,128)(2,1)S(1)}, bf16[160,640]{1,0:T(8,128)(2,1)S(1)}, u32[]{:S(2)}, u32[]{:S(2)}) %collective-permute-start.15) | collective-permute-done | bytes 204832 | tf_op jit(solution)/shard_map/ppermute | solution.py:321
  65.2 0.9 %shard_map.103 = (f32[160,1280]{1,0:T(8,128)}, f32[160,1280]{1,0:T(8,128)}) custom-call(bf16[160,640]{1,0:T(8,128)(2,1)S(1)} %collective-permute-done.15.owned, f32[1,1280]{1,0:T(1,128)S(1)} %broadcast_in_dim.3.gate, f32[160,1280]{1,0:T(8,128)S(1)} %shard_map.101.resting), custom_call_target="tpu_custom_call" | custom-call | tf_op jit(solution)/shard_map/pallas_call | solution.py:328
  66.1 1.2 %collective-permute-done.13.owned = bf16[160,640]{1,0:T(8,128)(2,1)S(1)} collective-permute-done((bf16[160,640]{1,0:T(8,128)(2,1)S(1)}, bf16[160,640]{1,0:T(8,128)(2,1)S(1)}, u32[]{:S(2)}, u32[]{:S(2)}) %collective-permute-start.13) | collective-permute-done | bytes 204832 | tf_op jit(solution)/shard_map/ppermute | solution.py:321
  67.4 0.9 %shard_map.104 = (f32[160,1280]{1,0:T(8,128)}, f32[160,1280]{1,0:T(8,128)}) custom-call(bf16[160,640]{1,0:T(8,128)(2,1)S(1)} %collective-permute-done.13.owned, f32[1,1280]{1,0:T(1,128)S(1)} %broadcast_in_dim.3.gate, f32[160,1280]{1,0:T(8,128)S(1)} %shard_map.101.resting, ...), custom_call_target="tpu_custom_call", output_to_operand_aliasing={{0}: (3, {}), {1}: (4, {})} | custom-call | tf_op jit(solution)/shard_map/pallas_call | solution.py:328
  (5 shorter events, 0.1 us)
Async XLA Ops:
  0.6 23.9 %copy-start.1 = (bf16[768,1280]{1,0:T(8,128)(2,1)S(1)}, bf16[768,1280]{1,0:T(8,128)(2,1)}, u32[]{:S(2)}) copy-start(bf16[768,1280]{1,0:T(8,128)(2,1)} %refs_4_.3) | copy-start | bytes 5898244
  2.0 20.6 %collective-permute-start = (bf16[320,384]{1,0:T(8,128)(2,1)S(1)}, bf16[320,384]{1,0:T(8,128)(2,1)S(1)}, u32[]{:S(2)}, u32[]{:S(2)}) collective-permute-start(bf16[320,384]{1,0:T(8,128)(2,1)S(1)} %get-tuple-element.15), channel_id=1, source_target_pairs={{0,0},{1,8},{4,4},{5,12},{8,1},{9,9},{12,5},{13,13},{2,2},{3,10},{... | collective-permute-start | bytes 737288 | tf_op jit(solution)/shard_map/ppermute | solution.py:273
  2.7 19.9 %collective-permute-start.1 = (bf16[320,384]{1,0:T(8,128)(2,1)S(1)}, bf16[320,384]{1,0:T(8,128)(2,1)S(1)}, u32[]{:S(2)}, u32[]{:S(2)}) collective-permute-start(bf16[320,384]{1,0:T(8,128)(2,1)S(1)} %get-tuple-element.16), channel_id=1, source_target_pairs={{0,4},{1,12},{4,0},{5,8},{8,5},{9,13},{12,1},{13,9},{2,6},{3,14},{... | collective-permute-start | bytes 737288 | tf_op jit(solution)/shard_map/ppermute | solution.py:273
  4.3 18.2 %collective-permute-start.2 = (bf16[160,384]{1,0:T(8,128)(2,1)S(1)}, bf16[160,384]{1,0:T(8,128)(2,1)S(1)}, u32[]{:S(2)}, u32[]{:S(2)}) collective-permute-start(bf16[160,384]{1,0:T(8,128)(2,1)S(1)} %get-tuple-element.17), channel_id=1, source_target_pairs={{0,1},{1,9},{4,5},{5,13},{8,0},{9,8},{12,4},{13,12},{2,3},{3,11},{... | collective-permute-start | bytes 368648 | tf_op jit(solution)/shard_map/ppermute | solution.py:273
  7.7 14.9 %collective-permute-start.3 = (bf16[160,384]{1,0:T(8,128)(2,1)S(1)}, bf16[160,384]{1,0:T(8,128)(2,1)S(1)}, u32[]{:S(2)}, u32[]{:S(2)}) collective-permute-start(bf16[160,384]{1,0:T(8,128)(2,1)S(1)} %get-tuple-element.18), channel_id=1, source_target_pairs={{0,5},{1,13},{4,1},{5,9},{8,4},{9,12},{12,0},{13,8},{2,7},{3,15},{... | collective-permute-start | bytes 368648 | tf_op jit(solution)/shard_map/ppermute | solution.py:273
  22.6 1.9 %collective-permute-start.4 = (bf16[640,384]{1,0:T(8,128)(2,1)S(1)}, bf16[640,384]{1,0:T(8,128)(2,1)S(1)}, u32[]{:S(2)}, u32[]{:S(2)}) collective-permute-start(bf16[640,384]{1,0:T(8,128)(2,1)S(1)} %shard_map.96), channel_id=1, source_target_pairs={{0,1},{1,0},{2,3},{3,2},{4,5},{5,4},{6,7},{7,6},{8,9},{9,8},{10,11... | collective-permute-start | bytes 1474568 | tf_op jit(solution)/shard_map/ppermute | solution.py:275
  24.6 17.2 %collective-permute-start.8 = (bf16[768,1280]{1,0:T(8,128)(2,1)S(1)}, bf16[768,1280]{1,0:T(8,128)(2,1)S(1)}, u32[]{:S(2)}, u32[]{:S(2)}) collective-permute-start(bf16[768,1280]{1,0:T(8,128)(2,1)S(1)} %copy-done.1), channel_id=1, source_target_pairs={{0,1},{1,0},{2,3},{3,2},{4,5},{5,4},{6,7},{7,6},{8,9},{9,8},{10,11... | collective-permute-start | bytes 5898248 | tf_op jit(solution)/shard_map/ppermute | solution.py:277
  26.4 12.9 %collective-permute-start.10 = (bf16[160,384]{1,0:T(8,128)(2,1)S(1)}, bf16[160,384]{1,0:T(8,128)(2,1)S(1)}, u32[]{:S(2)}, u32[]{:S(2)}) collective-permute-start(bf16[160,384]{1,0:T(8,128)(2,1)S(1)} %get-tuple-element.20.refs_0_), channel_id=1, source_target_pairs={{0,8},{4,12},{8,0},{12,4},{1,9},{5,13},{9,1},{13,5},{2,10},{6,14},... | collective-permute-start | bytes 368648 | tf_op jit(solution)/shard_map/ppermute | solution.py:297
  29.8 9.4 %collective-permute-start.11 = (bf16[160,384]{1,0:T(8,128)(2,1)S(1)}, bf16[160,384]{1,0:T(8,128)(2,1)S(1)}, u32[]{:S(2)}, u32[]{:S(2)}) collective-permute-start(bf16[160,384]{1,0:T(8,128)(2,1)S(1)} %get-tuple-element.19.refs_0_), channel_id=1, source_target_pairs={{0,12},{4,8},{8,4},{12,0},{1,13},{5,9},{9,5},{13,1},{2,14},{6,10},... | collective-permute-start | bytes 368648 | tf_op jit(solution)/shard_map/ppermute | solution.py:297
  30.7 11.1 %collective-permute-start.9 = (bf16[160,384]{1,0:T(8,128)(2,1)S(1)}, bf16[160,384]{1,0:T(8,128)(2,1)S(1)}, u32[]{:S(2)}, u32[]{:S(2)}) collective-permute-start(bf16[160,384]{1,0:T(8,128)(2,1)S(1)} %get-tuple-element.19.refs_0_), channel_id=1, source_target_pairs={{0,4},{4,0},{8,12},{12,8},{1,5},{5,1},{9,13},{13,9},{2,6},{6,2},{1... | collective-permute-start | bytes 368648 | tf_op jit(solution)/shard_map/ppermute | solution.py:297
  30.7 14.1 %collective-permute-start.5 = (bf16[160,384]{1,0:T(8,128)(2,1)S(1)}, bf16[160,384]{1,0:T(8,128)(2,1)S(1)}, u32[]{:S(2)}, u32[]{:S(2)}) collective-permute-start(bf16[160,384]{1,0:T(8,128)(2,1)S(1)} %get-tuple-element.20.refs_0_), channel_id=1, source_target_pairs={{0,4},{4,0},{8,12},{12,8},{1,5},{5,1},{9,13},{13,9},{2,6},{6,2},{1... | collective-permute-start | bytes 368648 | tf_op jit(solution)/shard_map/ppermute | solution.py:297
  39.2 11.0 %collective-permute-start.6 = (bf16[160,384]{1,0:T(8,128)(2,1)S(1)}, bf16[160,384]{1,0:T(8,128)(2,1)S(1)}, u32[]{:S(2)}, u32[]{:S(2)}) collective-permute-start(bf16[160,384]{1,0:T(8,128)(2,1)S(1)} %get-tuple-element.19.refs_0_), channel_id=1, source_target_pairs={{0,8},{4,12},{8,0},{12,4},{1,9},{5,13},{9,1},{13,5},{2,10},{6,14},... | collective-permute-start | bytes 368648 | tf_op jit(solution)/shard_map/ppermute | solution.py:297
  39.2 11.0 %collective-permute-start.7 = (bf16[160,384]{1,0:T(8,128)(2,1)S(1)}, bf16[160,384]{1,0:T(8,128)(2,1)S(1)}, u32[]{:S(2)}, u32[]{:S(2)}) collective-permute-start(bf16[160,384]{1,0:T(8,128)(2,1)S(1)} %get-tuple-element.20.refs_0_), channel_id=1, source_target_pairs={{0,12},{4,8},{8,4},{12,0},{1,13},{5,9},{9,5},{13,1},{2,14},{6,10},... | collective-permute-start | bytes 368648 | tf_op jit(solution)/shard_map/ppermute | solution.py:297
  42.7 8.5 %collective-permute-start.14 = (bf16[160,640]{1,0:T(8,128)(2,1)S(1)}, bf16[160,640]{1,0:T(8,128)(2,1)S(1)}, u32[]{:S(2)}, u32[]{:S(2)}) collective-permute-start(bf16[160,640]{1,0:T(8,128)(2,1)S(1)} %get-tuple-element.25), channel_id=1, source_target_pairs={{0,2},{2,0},{1,3},{3,1},{4,6},{6,4},{5,7},{7,5},{8,10},{10,8},{9,1... | collective-permute-start | bytes 614408 | tf_op jit(solution)/shard_map/ppermute | solution.py:319
  43.3 14.4 %copy-start.4 = (f32[1280]{0:T(1024)S(1)}, f32[1280]{0:T(1024)}, u32[]{:S(2)}) copy-start(f32[1280]{0:T(1024)} %param.12) | copy-start | bytes 15364
  43.3 14.4 %copy-start.3 = (s32[4]{0:T(128)S(1)}, s32[4]{0:T(128)}, u32[]{:S(2)}) copy-start(s32[4]{0:T(128)} %flags.1) | copy-start | bytes 52
  43.3 12.4 %collective-permute-start.12 = (bf16[160,640]{1,0:T(8,128)(2,1)S(1)}, bf16[160,640]{1,0:T(8,128)(2,1)S(1)}, u32[]{:S(2)}, u32[]{:S(2)}) collective-permute-start(bf16[160,640]{1,0:T(8,128)(2,1)S(1)} %get-tuple-element.23), channel_id=1, source_target_pairs={{0,2},{2,0},{1,3},{3,1},{4,6},{6,4},{5,7},{7,5},{8,10},{10,8},{9,1... | collective-permute-start | bytes 614408 | tf_op jit(solution)/shard_map/ppermute | solution.py:319
  50.2 7.4 %copy-start = (f32[4,160,1280]{2,1,0:T(8,128)S(1)}, f32[4,160,1280]{2,1,0:T(8,128)}, u32[]{:S(2)}) copy-start(f32[4,160,1280]{2,1,0:T(8,128)} %cached.1) | copy-start | bytes 9830404
  51.1 6.5 %copy-start.2 = (f32[160,1280]{1,0:T(8,128)S(1)}, f32[160,1280]{1,0:T(8,128)}, u32[]{:S(2)}) copy-start(f32[160,1280]{1,0:T(8,128)} %hidden.1) | copy-start | bytes 2457604
  51.2 14.0 %collective-permute-start.15 = (bf16[160,640]{1,0:T(8,128)(2,1)S(1)}, bf16[160,640]{1,0:T(8,128)(2,1)S(1)}, u32[]{:S(2)}, u32[]{:S(2)}) collective-permute-start(bf16[160,640]{1,0:T(8,128)(2,1)S(1)} %shard_map.102), channel_id=1, source_target_pairs={{0,0},{1,8},{2,4},{3,12},{4,5},{5,13},{6,1},{7,9},{8,2},{9,10},{10... | collective-permute-start | bytes 614408 | tf_op jit(solution)/shard_map/ppermute | solution.py:321
  55.7 11.7 %collective-permute-start.13 = (bf16[160,640]{1,0:T(8,128)(2,1)S(1)}, bf16[160,640]{1,0:T(8,128)(2,1)S(1)}, u32[]{:S(2)}, u32[]{:S(2)}) collective-permute-start(bf16[160,640]{1,0:T(8,128)(2,1)S(1)} %shard_map.100), channel_id=1, source_target_pairs={{0,0},{1,8},{2,4},{3,12},{4,5},{5,13},{6,1},{7,9},{8,2},{9,10},{10... | collective-permute-start | bytes 614408 | tf_op jit(solution)/shard_map/ppermute | solution.py:321

commit v14 on v11

--- a/solution.py
+++ b/solution.py
@@ -9,7 +9,7 @@
 
 HEAD_DIM = 128
 VMEM_BYTES = 48 * 1024 * 1024
-PACK_BYTES = 59 * 1024 * 1024 + 400 * 1024
+PACK_BYTES = 53 * 1024 * 1024 + 128 * 1024
 LOG2_E = 1.4426950408889634
 
 
@@ -99,35 +99,25 @@
 
 
 def pack_kernel(queries, keys, values, *refs):
-    outs, stages, read_sems, write_sems = refs[:4], refs[4:8], refs[8], refs[9]
+    outs, sems = refs[:4], refs[4]
     rows, width = queries.shape[0], outs[0].shape[1]
     half = rows // 2
     zh, zl = bits()
-    reads = []
-    for k, stage in enumerate(stages):
+    copies = []
+    for k in range(4):
         part = pl.ds(pl.multiple_of(flip(zh, k // 2) * half, 16), half)
         columns = pl.ds(pl.multiple_of(flip(zl, k % 2) * width, 128), width)
         moves = [
-            (keys.at[part, columns], stage.at[pl.ds(0, half), :]),
-            (values.at[part, columns], stage.at[pl.ds(half, half), :]),
+            (keys.at[part, columns], outs[k].at[pl.ds(0, half), :]),
+            (values.at[part, columns], outs[k].at[pl.ds(half, half), :]),
         ]
         if k < 2:
-            moves.append((queries.at[:, columns], stage.at[pl.ds(rows, rows), :]))
-        reads.append(
-            [
-                pltpu.make_async_copy(start, end, read_sems.at[3 * k + i])
-                for i, (start, end) in enumerate(moves)
-            ]
-        )
-        for copy in reads[-1]:
-            copy.start()
-    writes = []
-    for k, stage in enumerate(stages):
-        for copy in reads[k]:
-            copy.wait()
-        writes.append(pltpu.make_async_copy(stage, outs[k], write_sems.at[k]))
-        writes[-1].start()
-    for copy in writes:
+            moves.append((queries.at[:, columns], outs[k].at[pl.ds(rows, rows), :]))
+        for start, end in moves:
+            copies.append(pltpu.make_async_copy(start, end, sems.at[len(copies)]))
+    for copy in copies:
+        copy.start()
+    for copy in copies:
         copy.wait()
 
 
@@ -227,14 +217,20 @@
     out[...] = total
 
 
-def final_kernel(owned0, owned1, gate, resting, mixed, fresh):
-    half = owned0.shape[0]
+def final_kernel(piece, owned, gate, resting, *refs):
+    mixed, fresh, mixed_part, fresh_part, sems = refs[-5:]
+    half = owned.shape[0]
     _, zl = bits()
-    for p, owned in enumerate((owned0, owned1)):
-        rows = pl.ds(pl.multiple_of(flip(zl, p) * half, 16), half)
-        delta = owned[...].astype(jnp.float32) * gate[...]
-        fresh[rows, :] = delta
-        mixed[rows, :] = resting[rows, :] + delta
+    rows = pl.ds(pl.multiple_of(flip(zl, piece) * half, 16), half)
+    delta = owned[...].astype(jnp.float32) * gate[...]
+    fresh_part[...] = delta
+    copy_fresh = pltpu.make_async_copy(fresh_part, fresh.at[rows, :], sems.at[0])
+    copy_fresh.start()
+    mixed_part[...] = resting[rows, :] + delta
+    copy_mixed = pltpu.make_async_copy(mixed_part, mixed.at[rows, :], sems.at[1])
+    copy_mixed.start()
+    copy_fresh.wait()
+    copy_mixed.wait()
 
 
 def along(shard, m):
@@ -283,13 +279,12 @@
         pack_kernel,
         (queries, key_vectors, value_vectors),
         [((2 * rows, width), bf16)] * 2 + [((rows, width), bf16)] * 2,
-        [pltpu.VMEM((2 * rows, width), bf16)] * 2
-        + [pltpu.VMEM((rows, width), bf16)] * 2
-        + [pltpu.SemaphoreType.DMA((12,)), pltpu.SemaphoreType.DMA((4,))],
+        [pltpu.SemaphoreType.DMA((10,))],
         space=pl.ANY,
-        out_space=pl.ANY,
         vmem=PACK_BYTES,
     )
+    late_weight, _ = lax.optimization_barrier((out_weight, packed[0]))
+    weight_c = lax.ppermute(late_weight, "head", swap)
     moved = []
     for k in range(4):
         k1, k0 = k // 2, k % 2
@@ -301,8 +296,7 @@
         moved.append(lax.ppermute(packed[k], ("seq", "head"), pairs))
     (joined,) = call(join_kernel, moved, [((4 * rows, width), bf16)])
     sibling = lax.ppermute(joined, "head", swap)
-    late_weight, _ = lax.optimization_barrier((out_weight, sibling))
-    weight_c = lax.ppermute(late_weight, "head", swap)
+    sibling, _ = lax.optimization_barrier((sibling, weight_c))
     parts = call(
         attention_kernel,
         moved + [sibling],
@@ -315,23 +309,17 @@
         flops=4 * (2 * rows) * (4 * rows) * width,
     )
 
+    half = rows // 2
     flops = 4 * rows * depth * columns
-    held = [pltpu.VMEM((4 * rows, width), bf16)]
-    half = rows // 2
-    gathers = []
-    for part in parts:
-        near = along(part, 1)
-        two = along(part, 2)
-        gathers.append([part, near, two, along(two, 1)])
     sent, kept = (
         call(
             functools.partial(project_kernel, i),
-            gathers[i] + [out_weight, weight_c],
+            [part] + [along(part, m) for m in (1, 2, 3)] + [out_weight, weight_c],
             [((half, columns), dtype)] * 2,
-            held,
+            [pltpu.VMEM((4 * rows, width), bf16)],
             flops=effort * flops,
         )
-        for i, dtype, effort in ((0, bf16, 1), (1, jnp.float32, 8))
+        for i, (part, dtype, effort) in enumerate(((parts[0], bf16, 1), (parts[1], jnp.float32, 8)))
     )
 
     owned = []
@@ -348,13 +336,22 @@
     (resting,) = call(
         rest_kernel, (skip_flags, hidden_state, cached_deltas), [((rows, columns), jnp.float32)]
     )
-    return tuple(
-        call(
-            final_kernel,
-            (*owned, gate_values[None, :], resting),
-            [((rows, columns), jnp.float32)] * 2,
-        )
-    )
+    gate = gate_values[None, :]
+    results = ()
+    for p, part in enumerate(owned):
+        results = pl.pallas_call(
+            functools.partial(final_kernel, p),
+            in_specs=[pl.BlockSpec(memory_space=pltpu.VMEM)] * 3
+            + [pl.BlockSpec(memory_space=pl.ANY)] * len(results),
+            out_specs=[pl.BlockSpec(memory_space=pl.ANY)] * 2,
+            out_shape=[jax.ShapeDtypeStruct((rows, columns), jnp.float32)] * 2,
+            scratch_shapes=[pltpu.VMEM((half, columns), jnp.float32)] * 2
+            + [pltpu.SemaphoreType.DMA((2,))],
+            input_output_aliases={3 + i: i for i in range(len(results))},
+            compiler_params=pltpu.CompilerParams(vmem_limit_bytes=VMEM_BYTES),
+            cost_estimate=pl.CostEstimate(flops=0, bytes_accessed=0, transcendentals=0),
+        )(part, gate, resting, *results)
+    return tuple(results)
 
 
 def solution(mesh):

time: 70.4 us -> 68.3 us (0.970)
  the two profiles are of different devices: /device:TPU:1 before, /device:TPU:2 now
where the time goes in v14:
time: 68.3 us; the launch traced here: 68.2 us
  waiting for transfers between devices  36.9 us (54%)
  starting transfers between devices  22.7 us (33%)
  Pallas kernels  7.65 us (11%)
  between operations  0.82 us (1%)
    ppermute x4, waiting for transfers between devices, local_heads(): moved.append(lax.ppermute(packed[k], ('seq', 'head'), pairs))  14.9 us
    ppermute x6, waiting for transfers between devices, along(): return lax.ppermute(shard, 'seq', [(z, z ^ m) for z in range(4)])  10.3 us
    ppermute x2, waiting for transfers between devices, local_heads(): owned.append(lax.ppermute(summed, ('seq', 'wt', 'head'), pairs))  9.89 us
    ppermute x6, starting transfers between devices, along(): return lax.ppermute(shard, 'seq', [(z, z ^ m) for z in range(4)])  9.57 us
    ppermute x4, starting transfers between devices, local_heads(): moved.append(lax.ppermute(packed[k], ('seq', 'head'), pairs))  6.12 us
    pallas_call x8, Pallas kernels, call(): pl.pallas_call(kernel, in_specs=[pl.BlockSpec(memory_space=place) for pla...  5.75 us
    ppermute x2, starting transfers between devices, local_heads(): owned.append(lax.ppermute(summed, ('seq', 'wt', 'head'), pairs))  4.82 us
    ppermute x2, starting transfers between devices, local_heads(): arrived = lax.ppermute(sent[p], 'wt', swap)  2.09 us
  transfers between devices with their start and end apart: 16, of which 7 were waited for; matrix products, arithmetic and copies ran while one was open for 0% of the time, Pallas kernels for 5%

profile of v14, /device:TPU:2, one launch (start us, length us, event | category | flops | bytes accessed | tf_op | source)
XLA Modules:
  0.0 68.2 jit_solution(14654544240566296357)
XLA Ops:
  0.6 0.0 copy-start.1
  0.6 1.4 %shard_map.95 = (bf16[320,384]{1,0:T(8,128)(2,1)S(1)}, bf16[320,384]{1,0:T(8,128)(2,1)S(1)}, bf16[160,384]{1,0:T(8,128)(2,1)S(1)}, bf16[160,384]{1,0:T(8,128)(2,1)S(1)}) custom-call(bf16[160,768]{1,0:T(8,128)(2,1)} %queries.1, bf16[160,768]{1,0:T(8,128)(2,1)} %keys.1, bf16[160,768]{1,0:T(8,128)(2,1)} %values.1), custom_call_target="tpu_custom_call" | custom-call | tf_op jit(solution)/shard_map/pallas_call | solution.py:251
  2.0 0.1 collective-permute-start.5
  2.1 0.7 collective-permute-start
  2.8 1.6 %collective-permute-start.1 = (bf16[320,384]{1,0:T(8,128)(2,1)S(1)}, bf16[320,384]{1,0:T(8,128)(2,1)S(1)}, u32[]{:S(2)}, u32[]{:S(2)}) collective-permute-start(bf16[320,384]{1,0:T(8,128)(2,1)S(1)} %get-tuple-element.17), channel_id=1, source_target_pairs={{0,4},{1,12},{4,0},{5,8},{8,5},{9,13},{12,1},{13,9},{2,6},{3,14},{... | collective-permute-start | bytes 737288 | tf_op jit(solution)/shard_map/ppermute | solution.py:296
  4.4 3.8 %collective-permute-start.2 = (bf16[160,384]{1,0:T(8,128)(2,1)S(1)}, bf16[160,384]{1,0:T(8,128)(2,1)S(1)}, u32[]{:S(2)}, u32[]{:S(2)}) collective-permute-start(bf16[160,384]{1,0:T(8,128)(2,1)S(1)} %get-tuple-element.18), channel_id=1, source_target_pairs={{0,1},{1,9},{4,5},{5,13},{8,0},{9,8},{12,4},{13,12},{2,3},{3,11},{... | collective-permute-start | bytes 368648 | tf_op jit(solution)/shard_map/ppermute | solution.py:296
  8.2 0.0 collective-permute-start.3
  8.2 14.8 %collective-permute-done.2.refs_2_ = bf16[160,384]{1,0:T(8,128)(2,1)S(1)} collective-permute-done((bf16[160,384]{1,0:T(8,128)(2,1)S(1)}, bf16[160,384]{1,0:T(8,128)(2,1)S(1)}, u32[]{:S(2)}, u32[]{:S(2)}) %collective-permute-start.2) | collective-permute-done | bytes 122912 | tf_op jit(solution)/shard_map/ppermute | solution.py:296
  23.1 0.0 collective-permute-done.3.refs_3_
  23.1 0.0 collective-permute-done.refs_0_
  23.1 0.0 collective-permute-done.1.refs_1_
  23.1 0.1 collective-permute-start.4
  23.2 1.9 %collective-permute-done.4.refs_4_ = bf16[640,384]{1,0:T(8,128)(2,1)S(1)} collective-permute-done((bf16[640,384]{1,0:T(8,128)(2,1)S(1)}, bf16[640,384]{1,0:T(8,128)(2,1)S(1)}, u32[]{:S(2)}, u32[]{:S(2)}) %collective-permute-start.4) | collective-permute-done | bytes 491552 | tf_op jit(solution)/shard_map/ppermute | solution.py:298
  25.1 0.0 collective-permute-done.5.refs_5_
  25.1 1.6 %shard_map.97 = (bf16[160,384]{1,0:T(8,128)(2,1)S(1)}, bf16[160,384]{1,0:T(8,128)(2,1)S(1)}) custom-call(bf16[320,384]{1,0:T(8,128)(2,1)S(1)} %collective-permute-done.refs_0_, bf16[320,384]{1,0:T(8,128)(2,1)S(1)} %collective-permute-done.1.refs_1_, bf16[160,384]{1,0:T(8,128)(2,1)S(1)} %collective-permute-done.2.refs_2_, ...), custom_call_target="tpu_custom_call" | custom-call | flops 314572800 | tf_op jit(solution)/shard_map/pallas_call | solution.py:251
  26.7 2.8 %collective-permute-start.10 = (bf16[160,384]{1,0:T(8,128)(2,1)S(1)}, bf16[160,384]{1,0:T(8,128)(2,1)S(1)}, u32[]{:S(2)}, u32[]{:S(2)}) collective-permute-start(bf16[160,384]{1,0:T(8,128)(2,1)S(1)} %get-tuple-element.24.refs_0_), channel_id=1, source_target_pairs={{0,8},{4,12},{8,0},{12,4},{1,9},{5,13},{9,1},{13,5},{2,10},{6,14},... | collective-permute-start | bytes 368648 | tf_op jit(solution)/shard_map/ppermute | solution.py:237
  29.5 1.5 %collective-permute-start.11 = (bf16[160,384]{1,0:T(8,128)(2,1)S(1)}, bf16[160,384]{1,0:T(8,128)(2,1)S(1)}, u32[]{:S(2)}, u32[]{:S(2)}) collective-permute-start(bf16[160,384]{1,0:T(8,128)(2,1)S(1)} %get-tuple-element.24.refs_0_), channel_id=1, source_target_pairs={{0,12},{4,8},{8,4},{12,0},{1,13},{5,9},{9,5},{13,1},{2,14},{6,10},... | collective-permute-start | bytes 368648 | tf_op jit(solution)/shard_map/ppermute | solution.py:237
  31.0 0.0 collective-permute-start.9
  31.0 2.0 %collective-permute-start.6 = (bf16[160,384]{1,0:T(8,128)(2,1)S(1)}, bf16[160,384]{1,0:T(8,128)(2,1)S(1)}, u32[]{:S(2)}, u32[]{:S(2)}) collective-permute-start(bf16[160,384]{1,0:T(8,128)(2,1)S(1)} %get-tuple-element.22.refs_0_), channel_id=1, source_target_pairs={{0,4},{4,0},{8,12},{12,8},{1,5},{5,1},{9,13},{13,9},{2,6},{6,2},{1... | collective-permute-start | bytes 368648 | tf_op jit(solution)/shard_map/ppermute | solution.py:237
  33.0 0.9 %collective-permute-start.7 = (bf16[160,384]{1,0:T(8,128)(2,1)S(1)}, bf16[160,384]{1,0:T(8,128)(2,1)S(1)}, u32[]{:S(2)}, u32[]{:S(2)}) collective-permute-start(bf16[160,384]{1,0:T(8,128)(2,1)S(1)} %get-tuple-element.22.refs_0_), channel_id=1, source_target_pairs={{0,8},{4,12},{8,0},{12,4},{1,9},{5,13},{9,1},{13,5},{2,10},{6,14},... | collective-permute-start | bytes 368648 | tf_op jit(solution)/shard_map/ppermute | solution.py:237
  33.9 5.2 %collective-permute-done.10.refs_2_ = bf16[160,384]{1,0:T(8,128)(2,1)S(1)} collective-permute-done((bf16[160,384]{1,0:T(8,128)(2,1)S(1)}, bf16[160,384]{1,0:T(8,128)(2,1)S(1)}, u32[]{:S(2)}, u32[]{:S(2)}) %collective-permute-start.10) | collective-permute-done | bytes 122912 | tf_op jit(solution)/shard_map/ppermute | solution.py:237
  39.1 2.3 %collective-permute-start.8 = (bf16[160,384]{1,0:T(8,128)(2,1)S(1)}, bf16[160,384]{1,0:T(8,128)(2,1)S(1)}, u32[]{:S(2)}, u32[]{:S(2)}) collective-permute-start(bf16[160,384]{1,0:T(8,128)(2,1)S(1)} %get-tuple-element.22.refs_0_), channel_id=1, source_target_pairs={{0,12},{4,8},{8,4},{12,0},{1,13},{5,9},{9,5},{13,1},{2,14},{6,10},... | collective-permute-start | bytes 368648 | tf_op jit(solution)/shard_map/ppermute | solution.py:237
  41.5 0.0 collective-permute-done.11.refs_3_
  41.5 0.1 collective-permute-done.9.refs_1_
  41.5 0.0 copy-done.1
  41.5 0.9 %shard_map.99 = (bf16[80,1280]{1,0:T(8,128)(2,1)S(1)}, bf16[80,1280]{1,0:T(8,128)(2,1)S(1)}) custom-call(bf16[160,384]{1,0:T(8,128)(2,1)S(1)} %get-tuple-element.24.refs_0_, bf16[160,384]{1,0:T(8,128)(2,1)S(1)} %collective-permute-done.9.refs_1_, bf16[160,384]{1,0:T(8,128)(2,1)S(1)} %collective-permute-done.10.refs_2_, ...), custom_call_target="tpu_custom_call" | custom-call | flops 629145600 | tf_op jit(solution)/shard_map/pallas_call | solution.py:251
  42.5 0.5 collective-permute-start.14
  43.0 0.0 copy-start.4
  43.0 1.6 %collective-permute-start.12 = (bf16[80,1280]{1,0:T(8,128)(2,1)S(1)}, bf16[80,1280]{1,0:T(8,128)(2,1)S(1)}, u32[]{:S(2)}, u32[]{:S(2)}) collective-permute-start(bf16[80,1280]{1,0:T(8,128)(2,1)S(1)} %get-tuple-element.25), channel_id=1, source_target_pairs={{0,2},{2,0},{1,3},{3,1},{4,6},{6,4},{5,7},{7,5},{8,10},{10,8},{9,1... | collective-permute-start | bytes 614408 | tf_op jit(solution)/shard_map/ppermute | solution.py:327
  44.6 0.0 collective-permute-done.6.refs_1_
  44.6 5.1 %collective-permute-done.7.refs_2_ = bf16[160,384]{1,0:T(8,128)(2,1)S(1)} collective-permute-done((bf16[160,384]{1,0:T(8,128)(2,1)S(1)}, bf16[160,384]{1,0:T(8,128)(2,1)S(1)}, u32[]{:S(2)}, u32[]{:S(2)}) %collective-permute-start.7) | collective-permute-done | bytes 122912 | tf_op jit(solution)/shard_map/ppermute | solution.py:237
  49.7 0.0 collective-permute-done.8.refs_3_
  49.7 0.9 %shard_map.98 = (f32[80,1280]{1,0:T(8,128)S(1)}, f32[80,1280]{1,0:T(8,128)S(1)}) custom-call(bf16[160,384]{1,0:T(8,128)(2,1)S(1)} %get-tuple-element.22.refs_0_, bf16[160,384]{1,0:T(8,128)(2,1)S(1)} %collective-permute-done.6.refs_1_, bf16[160,384]{1,0:T(8,128)(2,1)S(1)} %collective-permute-done.7.refs_2_, ...), custom_call_target="tpu_custom_call" | custom-call | flops 5033164800 | tf_op jit(solution)/shard_map/pallas_call | solution.py:251
  50.6 0.0 copy-start.2
  50.6 0.0 collective-permute-done.14.arrived
  50.6 0.1 shard_map.102
  50.7 4.8 %collective-permute-start.15 = (bf16[80,1280]{1,0:T(8,128)(2,1)S(1)}, bf16[80,1280]{1,0:T(8,128)(2,1)S(1)}, u32[]{:S(2)}, u32[]{:S(2)}) collective-permute-start(bf16[80,1280]{1,0:T(8,128)(2,1)S(1)} %shard_map.102), channel_id=1, source_target_pairs={{0,0},{1,8},{2,4},{3,12},{4,1},{5,9},{6,5},{7,13},{8,2},{9,10},{10... | collective-permute-start | bytes 614408 | tf_op jit(solution)/shard_map/ppermute | solution.py:335
  55.4 0.0 collective-permute-done.12.arrived
  55.5 0.1 collective-permute-start.13
  55.6 0.0 copy-done.4
  55.6 0.0 copy-done.3
  55.6 0.0 copy-done
  55.6 0.0 copy-done.2
  55.6 0.8 %shard_map.101.resting = f32[160,1280]{1,0:T(8,128)S(1)} custom-call(s32[4]{0:T(128)S(1)} %copy-done.3, f32[160,1280]{1,0:T(8,128)S(1)} %copy-done.2, f32[4,160,1280]{2,1,0:T(8,128)S(1)} %copy-done), custom_call_target="tpu_custom_call" | custom-call | tf_op jit(solution)/shard_map/pallas_call | solution.py:251
  56.4 8.0 %collective-permute-done.15.owned = bf16[80,1280]{1,0:T(8,128)(2,1)S(1)} collective-permute-done((bf16[80,1280]{1,0:T(8,128)(2,1)S(1)}, bf16[80,1280]{1,0:T(8,128)(2,1)S(1)}, u32[]{:S(2)}, u32[]{:S(2)}) %collective-permute-start.15) | collective-permute-done | bytes 204832 | tf_op jit(solution)/shard_map/ppermute | solution.py:335
  64.4 0.9 %shard_map.103 = (f32[160,1280]{1,0:T(8,128)}, f32[160,1280]{1,0:T(8,128)}) custom-call(bf16[80,1280]{1,0:T(8,128)(2,1)S(1)} %collective-permute-done.15.owned, f32[1,1280]{1,0:T(1,128)S(1)} %broadcast_in_dim.3.gate, f32[160,1280]{1,0:T(8,128)S(1)} %shard_map.101.resting), custom_call_target="tpu_custom_call" | custom-call | tf_op jit(solution)/shard_map/pallas_call | solution.py:342
  65.4 1.9 %collective-permute-done.13.owned = bf16[80,1280]{1,0:T(8,128)(2,1)S(1)} collective-permute-done((bf16[80,1280]{1,0:T(8,128)(2,1)S(1)}, bf16[80,1280]{1,0:T(8,128)(2,1)S(1)}, u32[]{:S(2)}, u32[]{:S(2)}) %collective-permute-start.13) | collective-permute-done | bytes 204832 | tf_op jit(solution)/shard_map/ppermute | solution.py:335
  67.2 0.9 %shard_map.104 = (f32[160,1280]{1,0:T(8,128)}, f32[160,1280]{1,0:T(8,128)}) custom-call(bf16[80,1280]{1,0:T(8,128)(2,1)S(1)} %collective-permute-done.13.owned, f32[1,1280]{1,0:T(1,128)S(1)} %broadcast_in_dim.3.gate, f32[160,1280]{1,0:T(8,128)S(1)} %shard_map.101.resting, ...), custom_call_target="tpu_custom_call", output_to_operand_aliasing={{0}: (3, {}), {1}: (4, {})} | custom-call | tf_op jit(solution)/shard_map/pallas_call | solution.py:342
  (5 shorter events, 0.1 us)
Async XLA Ops:
  0.6 40.9 %copy-start.1 = (bf16[768,1280]{1,0:T(8,128)(2,1)S(1)}, bf16[768,1280]{1,0:T(8,128)(2,1)}, u32[]{:S(2)}) copy-start(bf16[768,1280]{1,0:T(8,128)(2,1)} %refs_4_.3) | copy-start | bytes 5898244
  2.0 23.1 %collective-permute-start.5 = (bf16[768,1280]{1,0:T(8,128)(2,1)}, bf16[768,1280]{1,0:T(8,128)(2,1)S(1)}, u32[]{:S(2)}, u32[]{:S(2)}) collective-permute-start(bf16[768,1280]{1,0:T(8,128)(2,1)} %refs_4_.3), channel_id=1, source_target_pairs={{0,1},{1,0},{2,3},{3,2},{4,5},{5,4},{6,7},{7,6},{8,9},{9,8},{10,11... | collective-permute-start | bytes 5898248 | tf_op jit(solution)/shard_map/ppermute | solution.py:287
  2.1 21.0 %collective-permute-start = (bf16[320,384]{1,0:T(8,128)(2,1)S(1)}, bf16[320,384]{1,0:T(8,128)(2,1)S(1)}, u32[]{:S(2)}, u32[]{:S(2)}) collective-permute-start(bf16[320,384]{1,0:T(8,128)(2,1)S(1)} %get-tuple-element.16), channel_id=1, source_target_pairs={{0,0},{1,8},{4,4},{5,12},{8,1},{9,9},{12,5},{13,13},{2,2},{3,10},{... | collective-permute-start | bytes 737288 | tf_op jit(solution)/shard_map/ppermute | solution.py:296
  2.8 20.3 %collective-permute-start.1 = (bf16[320,384]{1,0:T(8,128)(2,1)S(1)}, bf16[320,384]{1,0:T(8,128)(2,1)S(1)}, u32[]{:S(2)}, u32[]{:S(2)}) collective-permute-start(bf16[320,384]{1,0:T(8,128)(2,1)S(1)} %get-tuple-element.17), channel_id=1, source_target_pairs={{0,4},{1,12},{4,0},{5,8},{8,5},{9,13},{12,1},{13,9},{2,6},{3,14},{... | collective-permute-start | bytes 737288 | tf_op jit(solution)/shard_map/ppermute | solution.py:296
  4.4 18.6 %collective-permute-start.2 = (bf16[160,384]{1,0:T(8,128)(2,1)S(1)}, bf16[160,384]{1,0:T(8,128)(2,1)S(1)}, u32[]{:S(2)}, u32[]{:S(2)}) collective-permute-start(bf16[160,384]{1,0:T(8,128)(2,1)S(1)} %get-tuple-element.18), channel_id=1, source_target_pairs={{0,1},{1,9},{4,5},{5,13},{8,0},{9,8},{12,4},{13,12},{2,3},{3,11},{... | collective-permute-start | bytes 368648 | tf_op jit(solution)/shard_map/ppermute | solution.py:296
  8.2 14.9 %collective-permute-start.3 = (bf16[160,384]{1,0:T(8,128)(2,1)S(1)}, bf16[160,384]{1,0:T(8,128)(2,1)S(1)}, u32[]{:S(2)}, u32[]{:S(2)}) collective-permute-start(bf16[160,384]{1,0:T(8,128)(2,1)S(1)} %get-tuple-element.19), channel_id=1, source_target_pairs={{0,5},{1,13},{4,1},{5,9},{8,4},{9,12},{12,0},{13,8},{2,7},{3,15},{... | collective-permute-start | bytes 368648 | tf_op jit(solution)/shard_map/ppermute | solution.py:296
  23.1 1.9 %collective-permute-start.4 = (bf16[640,384]{1,0:T(8,128)(2,1)S(1)}, bf16[640,384]{1,0:T(8,128)(2,1)S(1)}, u32[]{:S(2)}, u32[]{:S(2)}) collective-permute-start(bf16[640,384]{1,0:T(8,128)(2,1)S(1)} %shard_map.96), channel_id=1, source_target_pairs={{0,1},{1,0},{2,3},{3,2},{4,5},{5,4},{6,7},{7,6},{8,9},{9,8},{10,11... | collective-permute-start | bytes 1474568 | tf_op jit(solution)/shard_map/ppermute | solution.py:298
  26.7 12.4 %collective-permute-start.10 = (bf16[160,384]{1,0:T(8,128)(2,1)S(1)}, bf16[160,384]{1,0:T(8,128)(2,1)S(1)}, u32[]{:S(2)}, u32[]{:S(2)}) collective-permute-start(bf16[160,384]{1,0:T(8,128)(2,1)S(1)} %get-tuple-element.24.refs_0_), channel_id=1, source_target_pairs={{0,8},{4,12},{8,0},{12,4},{1,9},{5,13},{9,1},{13,5},{2,10},{6,14},... | collective-permute-start | bytes 368648 | tf_op jit(solution)/shard_map/ppermute | solution.py:237
  29.5 11.9 %collective-permute-start.11 = (bf16[160,384]{1,0:T(8,128)(2,1)S(1)}, bf16[160,384]{1,0:T(8,128)(2,1)S(1)}, u32[]{:S(2)}, u32[]{:S(2)}) collective-permute-start(bf16[160,384]{1,0:T(8,128)(2,1)S(1)} %get-tuple-element.24.refs_0_), channel_id=1, source_target_pairs={{0,12},{4,8},{8,4},{12,0},{1,13},{5,9},{9,5},{13,1},{2,14},{6,10},... | collective-permute-start | bytes 368648 | tf_op jit(solution)/shard_map/ppermute | solution.py:237
  31.0 10.5 %collective-permute-start.9 = (bf16[160,384]{1,0:T(8,128)(2,1)S(1)}, bf16[160,384]{1,0:T(8,128)(2,1)S(1)}, u32[]{:S(2)}, u32[]{:S(2)}) collective-permute-start(bf16[160,384]{1,0:T(8,128)(2,1)S(1)} %get-tuple-element.24.refs_0_), channel_id=1, source_target_pairs={{0,4},{4,0},{8,12},{12,8},{1,5},{5,1},{9,13},{13,9},{2,6},{6,2},{1... | collective-permute-start | bytes 368648 | tf_op jit(solution)/shard_map/ppermute | solution.py:237
  31.0 13.5 %collective-permute-start.6 = (bf16[160,384]{1,0:T(8,128)(2,1)S(1)}, bf16[160,384]{1,0:T(8,128)(2,1)S(1)}, u32[]{:S(2)}, u32[]{:S(2)}) collective-permute-start(bf16[160,384]{1,0:T(8,128)(2,1)S(1)} %get-tuple-element.22.refs_0_), channel_id=1, source_target_pairs={{0,4},{4,0},{8,12},{12,8},{1,5},{5,1},{9,13},{13,9},{2,6},{6,2},{1... | collective-permute-start | bytes 368648 | tf_op jit(solution)/shard_map/ppermute | solution.py:237
  33.0 16.6 %collective-permute-start.7 = (bf16[160,384]{1,0:T(8,128)(2,1)S(1)}, bf16[160,384]{1,0:T(8,128)(2,1)S(1)}, u32[]{:S(2)}, u32[]{:S(2)}) collective-permute-start(bf16[160,384]{1,0:T(8,128)(2,1)S(1)} %get-tuple-element.22.refs_0_), channel_id=1, source_target_pairs={{0,8},{4,12},{8,0},{12,4},{1,9},{5,13},{9,1},{13,5},{2,10},{6,14},... | collective-permute-start | bytes 368648 | tf_op jit(solution)/shard_map/ppermute | solution.py:237
  39.1 10.5 %collective-permute-start.8 = (bf16[160,384]{1,0:T(8,128)(2,1)S(1)}, bf16[160,384]{1,0:T(8,128)(2,1)S(1)}, u32[]{:S(2)}, u32[]{:S(2)}) collective-permute-start(bf16[160,384]{1,0:T(8,128)(2,1)S(1)} %get-tuple-element.22.refs_0_), channel_id=1, source_target_pairs={{0,12},{4,8},{8,4},{12,0},{1,13},{5,9},{9,5},{13,1},{2,14},{6,10},... | collective-permute-start | bytes 368648 | tf_op jit(solution)/shard_map/ppermute | solution.py:237
  42.5 8.1 %collective-permute-start.14 = (bf16[80,1280]{1,0:T(8,128)(2,1)S(1)}, bf16[80,1280]{1,0:T(8,128)(2,1)S(1)}, u32[]{:S(2)}, u32[]{:S(2)}) collective-permute-start(bf16[80,1280]{1,0:T(8,128)(2,1)S(1)} %get-tuple-element.27), channel_id=1, source_target_pairs={{0,2},{2,0},{1,3},{3,1},{4,6},{6,4},{5,7},{7,5},{8,10},{10,8},{9,1... | collective-permute-start | bytes 614408 | tf_op jit(solution)/shard_map/ppermute | solution.py:327
  43.0 12.6 %copy-start.4 = (f32[1280]{0:T(1024)S(1)}, f32[1280]{0:T(1024)}, u32[]{:S(2)}) copy-start(f32[1280]{0:T(1024)} %param.12) | copy-start | bytes 15364
  43.0 12.6 %copy-start.3 = (s32[4]{0:T(128)S(1)}, s32[4]{0:T(128)}, u32[]{:S(2)}) copy-start(s32[4]{0:T(128)} %flags.1) | copy-start | bytes 52
  43.0 12.4 %collective-permute-start.12 = (bf16[80,1280]{1,0:T(8,128)(2,1)S(1)}, bf16[80,1280]{1,0:T(8,128)(2,1)S(1)}, u32[]{:S(2)}, u32[]{:S(2)}) collective-permute-start(bf16[80,1280]{1,0:T(8,128)(2,1)S(1)} %get-tuple-element.25), channel_id=1, source_target_pairs={{0,2},{2,0},{1,3},{3,1},{4,6},{6,4},{5,7},{7,5},{8,10},{10,8},{9,1... | collective-permute-start | bytes 614408 | tf_op jit(solution)/shard_map/ppermute | solution.py:327
  49.7 6.0 %copy-start = (f32[4,160,1280]{2,1,0:T(8,128)S(1)}, f32[4,160,1280]{2,1,0:T(8,128)}, u32[]{:S(2)}) copy-start(f32[4,160,1280]{2,1,0:T(8,128)} %cached.1) | copy-start | bytes 9830404
  50.6 5.0 %copy-start.2 = (f32[160,1280]{1,0:T(8,128)S(1)}, f32[160,1280]{1,0:T(8,128)}, u32[]{:S(2)}) copy-start(f32[160,1280]{1,0:T(8,128)} %hidden.1) | copy-start | bytes 2457604
  50.7 13.7 %collective-permute-start.15 = (bf16[80,1280]{1,0:T(8,128)(2,1)S(1)}, bf16[80,1280]{1,0:T(8,128)(2,1)S(1)}, u32[]{:S(2)}, u32[]{:S(2)}) collective-permute-start(bf16[80,1280]{1,0:T(8,128)(2,1)S(1)} %shard_map.102), channel_id=1, source_target_pairs={{0,0},{1,8},{2,4},{3,12},{4,1},{5,9},{6,5},{7,13},{8,2},{9,10},{10... | collective-permute-start | bytes 614408 | tf_op jit(solution)/shard_map/ppermute | solution.py:335
  55.5 11.7 %collective-permute-start.13 = (bf16[80,1280]{1,0:T(8,128)(2,1)S(1)}, bf16[80,1280]{1,0:T(8,128)(2,1)S(1)}, u32[]{:S(2)}, u32[]{:S(2)}) collective-permute-start(bf16[80,1280]{1,0:T(8,128)(2,1)S(1)} %shard_map.100), channel_id=1, source_target_pairs={{0,4},{1,12},{2,0},{3,8},{4,5},{5,13},{6,1},{7,9},{8,6},{9,14},{10... | collective-permute-start | bytes 614408 | tf_op jit(solution)/shard_map/ppermute | solution.py:335

commit v15 on v14

--- a/solution.py
+++ b/solution.py
@@ -130,7 +130,7 @@
 
 def attention_kernel(*refs):
     blocks, sibling = refs[:4], refs[4]
-    sent, kept, key_all, value_all, query_all = refs[5:]
+    sent, kept, both, key_all, value_all, query_all = refs[5:]
     rows = sent.shape[0]
     half = rows // 2
     for k in range(4):
@@ -165,14 +165,16 @@
         result = (result / total).astype(sent.dtype)
         sent[:, columns] = result[:rows]
         kept[:, columns] = result[rows:]
-
-
-def multiply(shards, weight, weight_c, held):
+        both[:, columns] = result
+
+
+def multiply(shards, first, weight, weight_c, held):
     rows = shards[0].shape[0]
     zh, zl = bits()
     core = lax.axis_index("head")
     for m, shard in enumerate(shards):
-        held[m * rows : (m + 1) * rows, :] = shard[...]
+        start = first if m == 1 else 0
+        held[m * rows : (m + 1) * rows, :] = shard[start : start + rows, :]
     total = None
     for other, block in enumerate((weight, weight_c)):
         high = 2 * lax.rem(flip(core, other) + zh, 2)
@@ -190,7 +192,7 @@
 
 def project_kernel(kept, *refs):
     shards, (weight, weight_c, out0, out1, held) = refs[:4], refs[4:]
-    total = multiply(shards, weight, weight_c, held)
+    total = multiply(shards, kept * shards[0].shape[0], weight, weight_c, held)
     half = out0.shape[0]
     x = lax.axis_index("wt")
     for low in range(2):
@@ -300,7 +302,7 @@
     parts = call(
         attention_kernel,
         moved + [sibling],
-        [((rows, width), bf16)] * 2,
+        [((rows, width), bf16)] * 2 + [((2 * rows, width), bf16)],
         [
             pltpu.VMEM((4 * rows, width), bf16),
             pltpu.VMEM((4 * rows, width), bf16),
@@ -311,10 +313,11 @@
 
     half = rows // 2
     flops = 4 * rows * depth * columns
+    near = along(parts[2], 1)
     sent, kept = (
         call(
             functools.partial(project_kernel, i),
-            [part] + [along(part, m) for m in (1, 2, 3)] + [out_weight, weight_c],
+            [part, near, along(part, 2), along(part, 3), out_weight, weight_c],
             [((half, columns), dtype)] * 2,
             [pltpu.VMEM((4 * rows, width), bf16)],
             flops=effort * flops,

time: 68.3 us -> 71.3 us (1.044)
  waiting for transfers between devices: 36.9 us -> 42.9 us
  starting transfers between devices: 22.7 us -> 19.5 us
    ppermute x2, waiting for transfers between devices: 0.01 us -> 2.97 us  [local_heads(): arrived = lax.ppermute(sent[p], 'wt', swap)]
    ppermute x6 -> x5, waiting for transfers between devices: 10.3 us -> 13.2 us  [along(): return lax.ppermute(shard, 'seq', [(z, z ^ m) for z in range(4)])]
    ppermute x2, starting transfers between devices: 4.82 us -> 2.5 us  [local_heads(): owned.append(lax.ppermute(summed, ('seq', 'wt', 'head'), pairs))]
    ppermute x6 -> x5, starting transfers between devices: 9.57 us -> 8.69 us  [along(): return lax.ppermute(shard, 'seq', [(z, z ^ m) for z in range(4)])]
  transfers between devices with their start and end apart: 16 -> 15, of which waited for: 7 -> 7; matrix products, arithmetic and copies ran while one was open for 0% -> 0% of each run, Pallas kernels for 5% -> 5%
where the time goes in v15:
time: 71.3 us; the launch traced here: 70.9 us
  waiting for transfers between devices  42.9 us (60%)
  starting transfers between devices  19.5 us (27%)
  Pallas kernels  7.7 us (11%)
  between operations  0.78 us (1%)
    ppermute x4, waiting for transfers between devices, local_heads(): moved.append(lax.ppermute(packed[k], ('seq', 'head'), pairs))  14.9 us
    ppermute x5, waiting for transfers between devices, along(): return lax.ppermute(shard, 'seq', [(z, z ^ m) for z in range(4)])  13.2 us
    ppermute x2, waiting for transfers between devices, local_heads(): owned.append(lax.ppermute(summed, ('seq', 'wt', 'head'), pairs))  9.95 us
    ppermute x5, starting transfers between devices, along(): return lax.ppermute(shard, 'seq', [(z, z ^ m) for z in range(4)])  8.69 us
    ppermute x4, starting transfers between devices, local_heads(): moved.append(lax.ppermute(packed[k], ('seq', 'head'), pairs))  6.12 us
    pallas_call x8, Pallas kernels, call(): pl.pallas_call(kernel, in_specs=[pl.BlockSpec(memory_space=place) for pla...  5.79 us
    ppermute x2, waiting for transfers between devices, local_heads(): arrived = lax.ppermute(sent[p], 'wt', swap)  2.97 us
    ppermute x2, starting transfers between devices, local_heads(): owned.append(lax.ppermute(summed, ('seq', 'wt', 'head'), pairs))  2.5 us
  transfers between devices with their start and end apart: 15, of which 7 were waited for; matrix products, arithmetic and copies ran while one was open for 0% of the time, Pallas kernels for 5%

profile of v15, /device:TPU:2, one launch (start us, length us, event | category | flops | bytes accessed | tf_op | source)
XLA Modules:
  0.0 70.9 jit_solution(3202831429678740570)
XLA Ops:
  0.6 0.0 copy-start.1
  0.6 1.4 %shard_map.95 = (bf16[320,384]{1,0:T(8,128)(2,1)S(1)}, bf16[320,384]{1,0:T(8,128)(2,1)S(1)}, bf16[160,384]{1,0:T(8,128)(2,1)S(1)}, bf16[160,384]{1,0:T(8,128)(2,1)S(1)}) custom-call(bf16[160,768]{1,0:T(8,128)(2,1)} %queries.1, bf16[160,768]{1,0:T(8,128)(2,1)} %keys.1, bf16[160,768]{1,0:T(8,128)(2,1)} %values.1), custom_call_target="tpu_custom_call" | custom-call | tf_op jit(solution)/shard_map/pallas_call | solution.py:253
  2.0 0.1 collective-permute-start.5
  2.1 0.7 collective-permute-start
  2.8 1.6 %collective-permute-start.1 = (bf16[320,384]{1,0:T(8,128)(2,1)S(1)}, bf16[320,384]{1,0:T(8,128)(2,1)S(1)}, u32[]{:S(2)}, u32[]{:S(2)}) collective-permute-start(bf16[320,384]{1,0:T(8,128)(2,1)S(1)} %get-tuple-element.18), channel_id=1, source_target_pairs={{0,4},{1,12},{4,0},{5,8},{8,5},{9,13},{12,1},{13,9},{2,6},{3,14},{... | collective-permute-start | bytes 737288 | tf_op jit(solution)/shard_map/ppermute | solution.py:298
  4.4 3.8 %collective-permute-start.2 = (bf16[160,384]{1,0:T(8,128)(2,1)S(1)}, bf16[160,384]{1,0:T(8,128)(2,1)S(1)}, u32[]{:S(2)}, u32[]{:S(2)}) collective-permute-start(bf16[160,384]{1,0:T(8,128)(2,1)S(1)} %get-tuple-element.19), channel_id=1, source_target_pairs={{0,1},{1,9},{4,5},{5,13},{8,0},{9,8},{12,4},{13,12},{2,3},{3,11},{... | collective-permute-start | bytes 368648 | tf_op jit(solution)/shard_map/ppermute | solution.py:298
  8.2 0.0 collective-permute-start.3
  8.2 14.8 %collective-permute-done.2.refs_2_ = bf16[160,384]{1,0:T(8,128)(2,1)S(1)} collective-permute-done((bf16[160,384]{1,0:T(8,128)(2,1)S(1)}, bf16[160,384]{1,0:T(8,128)(2,1)S(1)}, u32[]{:S(2)}, u32[]{:S(2)}) %collective-permute-start.2) | collective-permute-done | bytes 122912 | tf_op jit(solution)/shard_map/ppermute | solution.py:298
  23.1 0.0 collective-permute-done.3.refs_3_
  23.1 0.0 collective-permute-done.refs_0_
  23.1 0.0 collective-permute-done.1.refs_1_
  23.1 0.1 collective-permute-start.4
  23.2 1.9 %collective-permute-done.4.refs_4_ = bf16[640,384]{1,0:T(8,128)(2,1)S(1)} collective-permute-done((bf16[640,384]{1,0:T(8,128)(2,1)S(1)}, bf16[640,384]{1,0:T(8,128)(2,1)S(1)}, u32[]{:S(2)}, u32[]{:S(2)}) %collective-permute-start.4) | collective-permute-done | bytes 491552 | tf_op jit(solution)/shard_map/ppermute | solution.py:300
  25.1 0.0 collective-permute-done.5.refs_5_
  25.1 1.6 %shard_map.97 = (bf16[160,384]{1,0:T(8,128)(2,1)S(1)}, bf16[160,384]{1,0:T(8,128)(2,1)S(1)}, bf16[320,384]{1,0:T(8,128)(2,1)S(1)}) custom-call(bf16[320,384]{1,0:T(8,128)(2,1)S(1)} %collective-permute-done.refs_0_, bf16[320,384]{1,0:T(8,128)(2,1)S(1)} %collective-permute-done.1.refs_1_, bf16[160,384]{1,0:T(8,128)(2,1)S(1)} %collective-permute-done.2.refs_2_, ...), custom_call_target="tpu_custom_call" | custom-call | flops 314572800 | tf_op jit(solution)/shard_map/pallas_call | solution.py:253
  26.7 1.9 %collective-permute-start.6 = (bf16[320,384]{1,0:T(8,128)(2,1)S(1)}, bf16[320,384]{1,0:T(8,128)(2,1)S(1)}, u32[]{:S(2)}, u32[]{:S(2)}) collective-permute-start(bf16[320,384]{1,0:T(8,128)(2,1)S(1)} %get-tuple-element.24), channel_id=1, source_target_pairs={{0,4},{4,0},{8,12},{12,8},{1,5},{5,1},{9,13},{13,9},{2,6},{6,2},{1... | collective-permute-start | bytes 737288 | tf_op jit(solution)/shard_map/ppermute | solution.py:239
  28.7 2.3 %collective-permute-start.10 = (bf16[160,384]{1,0:T(8,128)(2,1)S(1)}, bf16[160,384]{1,0:T(8,128)(2,1)S(1)}, u32[]{:S(2)}, u32[]{:S(2)}) collective-permute-start(bf16[160,384]{1,0:T(8,128)(2,1)S(1)} %get-tuple-element.26.refs_0_), channel_id=1, source_target_pairs={{0,12},{4,8},{8,4},{12,0},{1,13},{5,9},{9,5},{13,1},{2,14},{6,10},... | collective-permute-start | bytes 368648 | tf_op jit(solution)/shard_map/ppermute | solution.py:239
  31.0 0.0 collective-permute-start.9
  31.0 2.9 %collective-permute-start.7 = (bf16[160,384]{1,0:T(8,128)(2,1)S(1)}, bf16[160,384]{1,0:T(8,128)(2,1)S(1)}, u32[]{:S(2)}, u32[]{:S(2)}) collective-permute-start(bf16[160,384]{1,0:T(8,128)(2,1)S(1)} %get-tuple-element.23.refs_0_), channel_id=1, source_target_pairs={{0,8},{4,12},{8,0},{12,4},{1,9},{5,13},{9,1},{13,5},{2,10},{6,14},... | collective-permute-start | bytes 368648 | tf_op jit(solution)/shard_map/ppermute | solution.py:239
  33.9 1.5 %collective-permute-start.8 = (bf16[160,384]{1,0:T(8,128)(2,1)S(1)}, bf16[160,384]{1,0:T(8,128)(2,1)S(1)}, u32[]{:S(2)}, u32[]{:S(2)}) collective-permute-start(bf16[160,384]{1,0:T(8,128)(2,1)S(1)} %get-tuple-element.23.refs_0_), channel_id=1, source_target_pairs={{0,12},{4,8},{8,4},{12,0},{1,13},{5,9},{9,5},{13,1},{2,14},{6,10},... | collective-permute-start | bytes 368648 | tf_op jit(solution)/shard_map/ppermute | solution.py:239
  35.4 5.1 %collective-permute-done.10.refs_3_ = bf16[160,384]{1,0:T(8,128)(2,1)S(1)} collective-permute-done((bf16[160,384]{1,0:T(8,128)(2,1)S(1)}, bf16[160,384]{1,0:T(8,128)(2,1)S(1)}, u32[]{:S(2)}, u32[]{:S(2)}) %collective-permute-start.10) | collective-permute-done | bytes 122912 | tf_op jit(solution)/shard_map/ppermute | solution.py:239
  40.5 8.2 %collective-permute-done.9.refs_2_ = bf16[160,384]{1,0:T(8,128)(2,1)S(1)} collective-permute-done((bf16[160,384]{1,0:T(8,128)(2,1)S(1)}, bf16[160,384]{1,0:T(8,128)(2,1)S(1)}, u32[]{:S(2)}, u32[]{:S(2)}) %collective-permute-start.9) | collective-permute-done | bytes 122912 | tf_op jit(solution)/shard_map/ppermute | solution.py:239
  48.6 0.0 collective-permute-done.6.refs_1_
  48.6 0.0 copy-done.1
  48.6 0.9 %shard_map.99 = (bf16[80,1280]{1,0:T(8,128)(2,1)S(1)}, bf16[80,1280]{1,0:T(8,128)(2,1)S(1)}) custom-call(bf16[160,384]{1,0:T(8,128)(2,1)S(1)} %get-tuple-element.26.refs_0_, bf16[320,384]{1,0:T(8,128)(2,1)S(1)} %collective-permute-done.6.refs_1_, bf16[160,384]{1,0:T(8,128)(2,1)S(1)} %collective-permute-done.9.refs_2_, ...), custom_call_target="tpu_custom_call" | custom-call | flops 629145600 | tf_op jit(solution)/shard_map/pallas_call | solution.py:253
  49.6 0.6 collective-permute-start.13
  50.2 0.0 copy-start.4
  50.2 0.0 copy-start.3
  50.2 1.5 %collective-permute-start.11 = (bf16[80,1280]{1,0:T(8,128)(2,1)S(1)}, bf16[80,1280]{1,0:T(8,128)(2,1)S(1)}, u32[]{:S(2)}, u32[]{:S(2)}) collective-permute-start(bf16[80,1280]{1,0:T(8,128)(2,1)S(1)} %get-tuple-element.27), channel_id=1, source_target_pairs={{0,2},{2,0},{1,3},{3,1},{4,6},{6,4},{5,7},{7,5},{8,10},{10,8},{9,1... | collective-permute-start | bytes 614408 | tf_op jit(solution)/shard_map/ppermute | solution.py:330
  51.7 0.0 collective-permute-done.7.refs_2_
  51.7 0.0 collective-permute-done.8.refs_3_
  51.7 0.0 copy-start
  51.7 0.9 %shard_map.98 = (f32[80,1280]{1,0:T(8,128)S(1)}, f32[80,1280]{1,0:T(8,128)S(1)}) custom-call(bf16[160,384]{1,0:T(8,128)(2,1)S(1)} %get-tuple-element.23.refs_0_, bf16[320,384]{1,0:T(8,128)(2,1)S(1)} %collective-permute-done.6.refs_1_, bf16[160,384]{1,0:T(8,128)(2,1)S(1)} %collective-permute-done.7.refs_2_, ...), custom_call_target="tpu_custom_call" | custom-call | flops 5033164800 | tf_op jit(solution)/shard_map/pallas_call | solution.py:253
  52.6 0.0 copy-start.2
  52.7 2.7 %collective-permute-done.13.arrived = bf16[80,1280]{1,0:T(8,128)(2,1)S(1)} collective-permute-done((bf16[80,1280]{1,0:T(8,128)(2,1)S(1)}, bf16[80,1280]{1,0:T(8,128)(2,1)S(1)}, u32[]{:S(2)}, u32[]{:S(2)}) %collective-permute-start.13) | collective-permute-done | bytes 204832 | tf_op jit(solution)/shard_map/ppermute | solution.py:330
  55.4 1.9 %collective-permute-start.14 = (bf16[80,1280]{1,0:T(8,128)(2,1)S(1)}, bf16[80,1280]{1,0:T(8,128)(2,1)S(1)}, u32[]{:S(2)}, u32[]{:S(2)}) collective-permute-start(bf16[80,1280]{1,0:T(8,128)(2,1)S(1)} %shard_map.102), channel_id=1, source_target_pairs={{0,0},{1,8},{2,4},{3,12},{4,1},{5,9},{6,5},{7,13},{8,2},{9,10},{10... | collective-permute-start | bytes 614408 | tf_op jit(solution)/shard_map/ppermute | solution.py:338
  57.4 0.2 collective-permute-done.11.arrived
  57.6 0.6 collective-permute-start.12
  58.2 0.0 copy-done.4
  58.2 0.0 copy-done.3
  58.2 0.0 copy-done
  58.2 0.0 copy-done.2
  58.2 0.8 %shard_map.101.resting = f32[160,1280]{1,0:T(8,128)S(1)} custom-call(s32[4]{0:T(128)S(1)} %copy-done.3, f32[160,1280]{1,0:T(8,128)S(1)} %copy-done.2, f32[4,160,1280]{2,1,0:T(8,128)S(1)} %copy-done), custom_call_target="tpu_custom_call" | custom-call | tf_op jit(solution)/shard_map/pallas_call | solution.py:253
  59.0 9.9 %collective-permute-done.14.owned = bf16[80,1280]{1,0:T(8,128)(2,1)S(1)} collective-permute-done((bf16[80,1280]{1,0:T(8,128)(2,1)S(1)}, bf16[80,1280]{1,0:T(8,128)(2,1)S(1)}, u32[]{:S(2)}, u32[]{:S(2)}) %collective-permute-start.14) | collective-permute-done | bytes 204832 | tf_op jit(solution)/shard_map/ppermute | solution.py:338
  69.0 0.9 %shard_map.103 = (f32[160,1280]{1,0:T(8,128)}, f32[160,1280]{1,0:T(8,128)}) custom-call(bf16[80,1280]{1,0:T(8,128)(2,1)S(1)} %collective-permute-done.14.owned, f32[1,1280]{1,0:T(1,128)S(1)} %broadcast_in_dim.3.gate, f32[160,1280]{1,0:T(8,128)S(1)} %shard_map.101.resting), custom_call_target="tpu_custom_call" | custom-call | tf_op jit(solution)/shard_map/pallas_call | solution.py:345
  69.9 0.0 collective-permute-done.12.owned
  69.9 1.0 %shard_map.104 = (f32[160,1280]{1,0:T(8,128)}, f32[160,1280]{1,0:T(8,128)}) custom-call(bf16[80,1280]{1,0:T(8,128)(2,1)S(1)} %collective-permute-done.12.owned, f32[1,1280]{1,0:T(1,128)S(1)} %broadcast_in_dim.3.gate, f32[160,1280]{1,0:T(8,128)S(1)} %shard_map.101.resting, ...), custom_call_target="tpu_custom_call", output_to_operand_aliasing={{0}: (3, {}), {1}: (4, {})} | custom-call | tf_op jit(solution)/shard_map/pallas_call | solution.py:345
  (4 shorter events, 0.1 us)
Async XLA Ops:
  0.6 48.0 %copy-start.1 = (bf16[768,1280]{1,0:T(8,128)(2,1)S(1)}, bf16[768,1280]{1,0:T(8,128)(2,1)}, u32[]{:S(2)}) copy-start(bf16[768,1280]{1,0:T(8,128)(2,1)} %refs_4_.3) | copy-start | bytes 5898244
  2.0 23.1 %collective-permute-start.5 = (bf16[768,1280]{1,0:T(8,128)(2,1)}, bf16[768,1280]{1,0:T(8,128)(2,1)S(1)}, u32[]{:S(2)}, u32[]{:S(2)}) collective-permute-start(bf16[768,1280]{1,0:T(8,128)(2,1)} %refs_4_.3), channel_id=1, source_target_pairs={{0,1},{1,0},{2,3},{3,2},{4,5},{5,4},{6,7},{7,6},{8,9},{9,8},{10,11... | collective-permute-start | bytes 5898248 | tf_op jit(solution)/shard_map/ppermute | solution.py:289
  2.1 21.0 %collective-permute-start = (bf16[320,384]{1,0:T(8,128)(2,1)S(1)}, bf16[320,384]{1,0:T(8,128)(2,1)S(1)}, u32[]{:S(2)}, u32[]{:S(2)}) collective-permute-start(bf16[320,384]{1,0:T(8,128)(2,1)S(1)} %get-tuple-element.17), channel_id=1, source_target_pairs={{0,0},{1,8},{4,4},{5,12},{8,1},{9,9},{12,5},{13,13},{2,2},{3,10},{... | collective-permute-start | bytes 737288 | tf_op jit(solution)/shard_map/ppermute | solution.py:298
  2.8 20.3 %collective-permute-start.1 = (bf16[320,384]{1,0:T(8,128)(2,1)S(1)}, bf16[320,384]{1,0:T(8,128)(2,1)S(1)}, u32[]{:S(2)}, u32[]{:S(2)}) collective-permute-start(bf16[320,384]{1,0:T(8,128)(2,1)S(1)} %get-tuple-element.18), channel_id=1, source_target_pairs={{0,4},{1,12},{4,0},{5,8},{8,5},{9,13},{12,1},{13,9},{2,6},{3,14},{... | collective-permute-start | bytes 737288 | tf_op jit(solution)/shard_map/ppermute | solution.py:298
  4.4 18.6 %collective-permute-start.2 = (bf16[160,384]{1,0:T(8,128)(2,1)S(1)}, bf16[160,384]{1,0:T(8,128)(2,1)S(1)}, u32[]{:S(2)}, u32[]{:S(2)}) collective-permute-start(bf16[160,384]{1,0:T(8,128)(2,1)S(1)} %get-tuple-element.19), channel_id=1, source_target_pairs={{0,1},{1,9},{4,5},{5,13},{8,0},{9,8},{12,4},{13,12},{2,3},{3,11},{... | collective-permute-start | bytes 368648 | tf_op jit(solution)/shard_map/ppermute | solution.py:298
  8.2 14.9 %collective-permute-start.3 = (bf16[160,384]{1,0:T(8,128)(2,1)S(1)}, bf16[160,384]{1,0:T(8,128)(2,1)S(1)}, u32[]{:S(2)}, u32[]{:S(2)}) collective-permute-start(bf16[160,384]{1,0:T(8,128)(2,1)S(1)} %get-tuple-element.20), channel_id=1, source_target_pairs={{0,5},{1,13},{4,1},{5,9},{8,4},{9,12},{12,0},{13,8},{2,7},{3,15},{... | collective-permute-start | bytes 368648 | tf_op jit(solution)/shard_map/ppermute | solution.py:298
  23.1 1.9 %collective-permute-start.4 = (bf16[640,384]{1,0:T(8,128)(2,1)S(1)}, bf16[640,384]{1,0:T(8,128)(2,1)S(1)}, u32[]{:S(2)}, u32[]{:S(2)}) collective-permute-start(bf16[640,384]{1,0:T(8,128)(2,1)S(1)} %shard_map.96), channel_id=1, source_target_pairs={{0,1},{1,0},{2,3},{3,2},{4,5},{5,4},{6,7},{7,6},{8,9},{9,8},{10,11... | collective-permute-start | bytes 1474568 | tf_op jit(solution)/shard_map/ppermute | solution.py:300
  26.7 21.9 %collective-permute-start.6 = (bf16[320,384]{1,0:T(8,128)(2,1)S(1)}, bf16[320,384]{1,0:T(8,128)(2,1)S(1)}, u32[]{:S(2)}, u32[]{:S(2)}) collective-permute-start(bf16[320,384]{1,0:T(8,128)(2,1)S(1)} %get-tuple-element.24), channel_id=1, source_target_pairs={{0,4},{4,0},{8,12},{12,8},{1,5},{5,1},{9,13},{13,9},{2,6},{6,2},{1... | collective-permute-start | bytes 737288 | tf_op jit(solution)/shard_map/ppermute | solution.py:239
  28.7 11.8 %collective-permute-start.10 = (bf16[160,384]{1,0:T(8,128)(2,1)S(1)}, bf16[160,384]{1,0:T(8,128)(2,1)S(1)}, u32[]{:S(2)}, u32[]{:S(2)}) collective-permute-start(bf16[160,384]{1,0:T(8,128)(2,1)S(1)} %get-tuple-element.26.refs_0_), channel_id=1, source_target_pairs={{0,12},{4,8},{8,4},{12,0},{1,13},{5,9},{9,5},{13,1},{2,14},{6,10},... | collective-permute-start | bytes 368648 | tf_op jit(solution)/shard_map/ppermute | solution.py:239
  31.0 17.6 %collective-permute-start.9 = (bf16[160,384]{1,0:T(8,128)(2,1)S(1)}, bf16[160,384]{1,0:T(8,128)(2,1)S(1)}, u32[]{:S(2)}, u32[]{:S(2)}) collective-permute-start(bf16[160,384]{1,0:T(8,128)(2,1)S(1)} %get-tuple-element.26.refs_0_), channel_id=1, source_target_pairs={{0,8},{4,12},{8,0},{12,4},{1,9},{5,13},{9,1},{13,5},{2,10},{6,14},... | collective-permute-start | bytes 368648 | tf_op jit(solution)/shard_map/ppermute | solution.py:239
  31.0 20.7 %collective-permute-start.7 = (bf16[160,384]{1,0:T(8,128)(2,1)S(1)}, bf16[160,384]{1,0:T(8,128)(2,1)S(1)}, u32[]{:S(2)}, u32[]{:S(2)}) collective-permute-start(bf16[160,384]{1,0:T(8,128)(2,1)S(1)} %get-tuple-element.23.refs_0_), channel_id=1, source_target_pairs={{0,8},{4,12},{8,0},{12,4},{1,9},{5,13},{9,1},{13,5},{2,10},{6,14},... | collective-permute-start | bytes 368648 | tf_op jit(solution)/shard_map/ppermute | solution.py:239
  33.9 17.8 %collective-permute-start.8 = (bf16[160,384]{1,0:T(8,128)(2,1)S(1)}, bf16[160,384]{1,0:T(8,128)(2,1)S(1)}, u32[]{:S(2)}, u32[]{:S(2)}) collective-permute-start(bf16[160,384]{1,0:T(8,128)(2,1)S(1)} %get-tuple-element.23.refs_0_), channel_id=1, source_target_pairs={{0,12},{4,8},{8,4},{12,0},{1,13},{5,9},{9,5},{13,1},{2,14},{6,10},... | collective-permute-start | bytes 368648 | tf_op jit(solution)/shard_map/ppermute | solution.py:239
  49.6 5.8 %collective-permute-start.13 = (bf16[80,1280]{1,0:T(8,128)(2,1)S(1)}, bf16[80,1280]{1,0:T(8,128)(2,1)S(1)}, u32[]{:S(2)}, u32[]{:S(2)}) collective-permute-start(bf16[80,1280]{1,0:T(8,128)(2,1)S(1)} %get-tuple-element.29), channel_id=1, source_target_pairs={{0,2},{2,0},{1,3},{3,1},{4,6},{6,4},{5,7},{7,5},{8,10},{10,8},{9,1... | collective-permute-start | bytes 614408 | tf_op jit(solution)/shard_map/ppermute | solution.py:330
  50.2 8.1 %copy-start.4 = (f32[1280]{0:T(1024)S(1)}, f32[1280]{0:T(1024)}, u32[]{:S(2)}) copy-start(f32[1280]{0:T(1024)} %param.12) | copy-start | bytes 15364
  50.2 8.1 %copy-start.3 = (s32[4]{0:T(128)S(1)}, s32[4]{0:T(128)}, u32[]{:S(2)}) copy-start(s32[4]{0:T(128)} %flags.1) | copy-start | bytes 52
  50.2 7.4 %collective-permute-start.11 = (bf16[80,1280]{1,0:T(8,128)(2,1)S(1)}, bf16[80,1280]{1,0:T(8,128)(2,1)S(1)}, u32[]{:S(2)}, u32[]{:S(2)}) collective-permute-start(bf16[80,1280]{1,0:T(8,128)(2,1)S(1)} %get-tuple-element.27), channel_id=1, source_target_pairs={{0,2},{2,0},{1,3},{3,1},{4,6},{6,4},{5,7},{7,5},{8,10},{10,8},{9,1... | collective-permute-start | bytes 614408 | tf_op jit(solution)/shard_map/ppermute | solution.py:330
  51.7 6.5 %copy-start = (f32[4,160,1280]{2,1,0:T(8,128)S(1)}, f32[4,160,1280]{2,1,0:T(8,128)}, u32[]{:S(2)}) copy-start(f32[4,160,1280]{2,1,0:T(8,128)} %cached.1) | copy-start | bytes 9830404
  52.6 5.6 %copy-start.2 = (f32[160,1280]{1,0:T(8,128)S(1)}, f32[160,1280]{1,0:T(8,128)}, u32[]{:S(2)}) copy-start(f32[160,1280]{1,0:T(8,128)} %hidden.1) | copy-start | bytes 2457604
  55.4 13.5 %collective-permute-start.14 = (bf16[80,1280]{1,0:T(8,128)(2,1)S(1)}, bf16[80,1280]{1,0:T(8,128)(2,1)S(1)}, u32[]{:S(2)}, u32[]{:S(2)}) collective-permute-start(bf16[80,1280]{1,0:T(8,128)(2,1)S(1)} %shard_map.102), channel_id=1, source_target_pairs={{0,0},{1,8},{2,4},{3,12},{4,1},{5,9},{6,5},{7,13},{8,2},{9,10},{10... | collective-permute-start | bytes 614408 | tf_op jit(solution)/shard_map/ppermute | solution.py:338
  57.6 12.3 %collective-permute-start.12 = (bf16[80,1280]{1,0:T(8,128)(2,1)S(1)}, bf16[80,1280]{1,0:T(8,128)(2,1)S(1)}, u32[]{:S(2)}, u32[]{:S(2)}) collective-permute-start(bf16[80,1280]{1,0:T(8,128)(2,1)S(1)} %shard_map.100), channel_id=1, source_target_pairs={{0,4},{1,12},{2,0},{3,8},{4,5},{5,13},{6,1},{7,9},{8,6},{9,14},{10... | collective-permute-start | bytes 614408 | tf_op jit(solution)/shard_map/ppermute | solution.py:338

commit v16 on v14

--- a/solution.py
+++ b/solution.py
@@ -105,8 +105,8 @@
     zh, zl = bits()
     copies = []
     for k in range(4):
-        part = pl.ds(pl.multiple_of(flip(zh, k // 2) * half, 16), half)
-        columns = pl.ds(pl.multiple_of(flip(zl, k % 2) * width, 128), width)
+        part = pl.ds(pl.multiple_of(flip(zl, k // 2) * half, 16), half)
+        columns = pl.ds(pl.multiple_of(flip(zh, k % 2) * width, 128), width)
         moves = [
             (keys.at[part, columns], outs[k].at[pl.ds(0, half), :]),
             (values.at[part, columns], outs[k].at[pl.ds(half, half), :]),
@@ -139,12 +139,12 @@
         value_all[here, :] = blocks[k][half:rows, :]
         key_all[there, :] = sibling[k * rows : k * rows + half, :]
         value_all[there, :] = sibling[k * rows + half : (k + 1) * rows, :]
-    _, zl = bits()
+    zh, _ = bits()
     x = lax.axis_index("wt")
     for k in range(2):
         for part in range(2):
             at = rows + flip(x, part == 0) * half
-            to = (part * 2 + flip(zl, k)) * half
+            to = (part * 2 + flip(zh, k)) * half
             query_all[pl.ds(pl.multiple_of(to, 16), half), :] = blocks[k][
                 pl.ds(pl.multiple_of(at, 16), half), :
             ]
@@ -175,11 +175,11 @@
         held[m * rows : (m + 1) * rows, :] = shard[...]
     total = None
     for other, block in enumerate((weight, weight_c)):
-        high = 2 * lax.rem(flip(core, other) + zh, 2)
+        low = lax.rem(flip(core, other) + zl, 2)
         left = jnp.concatenate(
             [
-                held[pl.ds(pl.multiple_of((high + flip(zl, low)) * rows, 16), rows), :]
-                for low in range(2)
+                held[pl.ds(pl.multiple_of((2 * flip(zh, high) + low) * rows, 16), rows), :]
+                for high in range(2)
             ],
             axis=1,
         )
@@ -220,8 +220,8 @@
 def final_kernel(piece, owned, gate, resting, *refs):
     mixed, fresh, mixed_part, fresh_part, sems = refs[-5:]
     half = owned.shape[0]
-    _, zl = bits()
-    rows = pl.ds(pl.multiple_of(flip(zl, piece) * half, 16), half)
+    zh, _ = bits()
+    rows = pl.ds(pl.multiple_of(flip(zh, piece) * half, 16), half)
     delta = owned[...].astype(jnp.float32) * gate[...]
     fresh_part[...] = delta
     copy_fresh = pltpu.make_async_copy(fresh_part, fresh.at[rows, :], sems.at[0])
@@ -291,8 +291,8 @@
         pairs = []
         for zz in range(4):
             for cc in range(2):
-                to_z = 2 * cc + ((zz % 2) ^ k0)
-                pairs.append((zz * 2 + cc, to_z * 2 + ((zz // 2) ^ k1)))
+                to_z = 2 * ((zz // 2) ^ k0) + cc
+                pairs.append((zz * 2 + cc, to_z * 2 + ((zz % 2) ^ k1)))
         moved.append(lax.ppermute(packed[k], ("seq", "head"), pairs))
     (joined,) = call(join_kernel, moved, [((4 * rows, width), bf16)])
     sibling = lax.ppermute(joined, "head", swap)
@@ -330,7 +330,7 @@
         for zz in range(4):
             for xx in range(2):
                 for cc in range(2):
-                    to = ((2 * cc + (p ^ xx)) * 2 + zz // 2) * 2 + zz % 2
+                    to = ((cc + 2 * (p ^ xx)) * 2 + zz // 2) * 2 + zz % 2
                     pairs.append(((zz * 2 + xx) * 2 + cc, to))
         owned.append(lax.ppermute(summed, ("seq", "wt", "head"), pairs))
     (resting,) = call(

time: 68.3 us -> 67.8 us (level)
  waiting for transfers between devices: 36.9 us -> 31.7 us
  starting transfers between devices: 22.7 us -> 27.5 us
    ppermute x4, waiting for transfers between devices: 14.9 us -> 11.5 us  [local_heads(): moved.append(lax.ppermute(packed[k], ('seq', 'head'), pairs))]
    ppermute x1, starting transfers between devices: 0.07 us -> 2.43 us  [local_heads(): sibling = lax.ppermute(joined, 'head', swap)]
    ppermute x6, starting transfers between devices: 9.57 us -> 10.8 us  [along(): return lax.ppermute(shard, 'seq', [(z, z ^ m) for z in range(4)])]
    ppermute x2, starting transfers between devices: 4.82 us -> 5.86 us  [local_heads(): owned.append(lax.ppermute(summed, ('seq', 'wt', 'head'), pairs))]
    ppermute x6, waiting for transfers between devices: 10.3 us -> 9.41 us  [along(): return lax.ppermute(shard, 'seq', [(z, z ^ m) for z in range(4)])]
  transfers between devices with their start and end apart: 16 -> 16, of which waited for: 7 -> 6; matrix products, arithmetic and copies ran while one was open for 0% -> 0% of each run, Pallas kernels for 5% -> 5%
where the time goes in v16:
time: 67.8 us; the launch traced here: 67.7 us
  waiting for transfers between devices  31.7 us (47%)
  starting transfers between devices  27.5 us (41%)
  Pallas kernels  7.63 us (11%)
  between operations  0.82 us (1%)
    ppermute x4, waiting for transfers between devices, local_heads(): moved.append(lax.ppermute(packed[k], ('seq', 'head'), pairs))  11.5 us
    ppermute x6, starting transfers between devices, along(): return lax.ppermute(shard, 'seq', [(z, z ^ m) for z in range(4)])  10.8 us
    ppermute x6, waiting for transfers between devices, along(): return lax.ppermute(shard, 'seq', [(z, z ^ m) for z in range(4)])  9.41 us
    ppermute x2, waiting for transfers between devices, local_heads(): owned.append(lax.ppermute(summed, ('seq', 'wt', 'head'), pairs))  9.24 us
    ppermute x4, starting transfers between devices, local_heads(): moved.append(lax.ppermute(packed[k], ('seq', 'head'), pairs))  6.23 us
    ppermute x2, starting transfers between devices, local_heads(): owned.append(lax.ppermute(summed, ('seq', 'wt', 'head'), pairs))  5.86 us
    pallas_call x8, Pallas kernels, call(): pl.pallas_call(kernel, in_specs=[pl.BlockSpec(memory_space=place) for pla...  5.73 us
    ppermute x1, starting transfers between devices, local_heads(): sibling = lax.ppermute(joined, 'head', swap)  2.43 us
  transfers between devices with their start and end apart: 16, of which 6 were waited for; matrix products, arithmetic and copies ran while one was open for 0% of the time, Pallas kernels for 5%

profile of v16, /device:TPU:2, one launch (start us, length us, event | category | flops | bytes accessed | tf_op | source)
XLA Modules:
  0.0 67.7 jit_solution(10277057876077677251)
XLA Ops:
  0.6 0.0 copy-start.1
  0.6 1.4 %shard_map.95 = (bf16[320,384]{1,0:T(8,128)(2,1)S(1)}, bf16[320,384]{1,0:T(8,128)(2,1)S(1)}, bf16[160,384]{1,0:T(8,128)(2,1)S(1)}, bf16[160,384]{1,0:T(8,128)(2,1)S(1)}) custom-call(bf16[160,768]{1,0:T(8,128)(2,1)} %queries.1, bf16[160,768]{1,0:T(8,128)(2,1)} %keys.1, bf16[160,768]{1,0:T(8,128)(2,1)} %values.1), custom_call_target="tpu_custom_call" | custom-call | tf_op jit(solution)/shard_map/pallas_call | solution.py:251
  2.0 0.1 collective-permute-start.5
  2.1 0.7 collective-permute-start
  2.8 2.7 %collective-permute-start.1 = (bf16[320,384]{1,0:T(8,128)(2,1)S(1)}, bf16[320,384]{1,0:T(8,128)(2,1)S(1)}, u32[]{:S(2)}, u32[]{:S(2)}) collective-permute-start(bf16[320,384]{1,0:T(8,128)(2,1)S(1)} %get-tuple-element.17), channel_id=1, source_target_pairs={{0,8},{1,12},{4,9},{5,13},{8,0},{9,4},{12,1},{13,5},{2,10},{3,14},... | collective-permute-start | bytes 737288 | tf_op jit(solution)/shard_map/ppermute | solution.py:296
  5.4 2.9 %collective-permute-start.2 = (bf16[160,384]{1,0:T(8,128)(2,1)S(1)}, bf16[160,384]{1,0:T(8,128)(2,1)S(1)}, u32[]{:S(2)}, u32[]{:S(2)}) collective-permute-start(bf16[160,384]{1,0:T(8,128)(2,1)S(1)} %get-tuple-element.18), channel_id=1, source_target_pairs={{0,1},{1,5},{4,0},{5,4},{8,9},{9,13},{12,8},{13,12},{2,3},{3,7},{6... | collective-permute-start | bytes 368648 | tf_op jit(solution)/shard_map/ppermute | solution.py:296
  8.3 0.0 collective-permute-start.3
  8.3 4.5 %collective-permute-done.2.refs_2_ = bf16[160,384]{1,0:T(8,128)(2,1)S(1)} collective-permute-done((bf16[160,384]{1,0:T(8,128)(2,1)S(1)}, bf16[160,384]{1,0:T(8,128)(2,1)S(1)}, u32[]{:S(2)}, u32[]{:S(2)}) %collective-permute-start.2) | collective-permute-done | bytes 122912 | tf_op jit(solution)/shard_map/ppermute | solution.py:296
  12.8 7.1 %collective-permute-done.3.refs_3_ = bf16[160,384]{1,0:T(8,128)(2,1)S(1)} collective-permute-done((bf16[160,384]{1,0:T(8,128)(2,1)S(1)}, bf16[160,384]{1,0:T(8,128)(2,1)S(1)}, u32[]{:S(2)}, u32[]{:S(2)}) %collective-permute-start.3) | collective-permute-done | bytes 122912 | tf_op jit(solution)/shard_map/ppermute | solution.py:296
  19.9 0.0 collective-permute-done.refs_0_
  19.9 0.0 collective-permute-done.1.refs_1_
  19.9 2.4 %collective-permute-start.4 = (bf16[640,384]{1,0:T(8,128)(2,1)S(1)}, bf16[640,384]{1,0:T(8,128)(2,1)S(1)}, u32[]{:S(2)}, u32[]{:S(2)}) collective-permute-start(bf16[640,384]{1,0:T(8,128)(2,1)S(1)} %shard_map.96), channel_id=1, source_target_pairs={{0,1},{1,0},{2,3},{3,2},{4,5},{5,4},{6,7},{7,6},{8,9},{9,8},{10,11... | collective-permute-start | bytes 1474568 | tf_op jit(solution)/shard_map/ppermute | solution.py:298
  22.4 1.5 %collective-permute-done.4.refs_4_ = bf16[640,384]{1,0:T(8,128)(2,1)S(1)} collective-permute-done((bf16[640,384]{1,0:T(8,128)(2,1)S(1)}, bf16[640,384]{1,0:T(8,128)(2,1)S(1)}, u32[]{:S(2)}, u32[]{:S(2)}) %collective-permute-start.4) | collective-permute-done | bytes 491552 | tf_op jit(solution)/shard_map/ppermute | solution.py:298
  23.9 0.0 collective-permute-done.5.refs_5_
  23.9 1.6 %shard_map.97 = (bf16[160,384]{1,0:T(8,128)(2,1)S(1)}, bf16[160,384]{1,0:T(8,128)(2,1)S(1)}) custom-call(bf16[320,384]{1,0:T(8,128)(2,1)S(1)} %collective-permute-done.refs_0_, bf16[320,384]{1,0:T(8,128)(2,1)S(1)} %collective-permute-done.1.refs_1_, bf16[160,384]{1,0:T(8,128)(2,1)S(1)} %collective-permute-done.2.refs_2_, ...), custom_call_target="tpu_custom_call" | custom-call | flops 314572800 | tf_op jit(solution)/shard_map/pallas_call | solution.py:251
  25.5 3.5 %collective-permute-start.10 = (bf16[160,384]{1,0:T(8,128)(2,1)S(1)}, bf16[160,384]{1,0:T(8,128)(2,1)S(1)}, u32[]{:S(2)}, u32[]{:S(2)}) collective-permute-start(bf16[160,384]{1,0:T(8,128)(2,1)S(1)} %get-tuple-element.24.refs_0_), channel_id=1, source_target_pairs={{0,8},{4,12},{8,0},{12,4},{1,9},{5,13},{9,1},{13,5},{2,10},{6,14},... | collective-permute-start | bytes 368648 | tf_op jit(solution)/shard_map/ppermute | solution.py:237
  29.0 0.4 collective-permute-start.11
  29.5 0.2 collective-permute-start.9
  29.7 1.8 %collective-permute-start.6 = (bf16[160,384]{1,0:T(8,128)(2,1)S(1)}, bf16[160,384]{1,0:T(8,128)(2,1)S(1)}, u32[]{:S(2)}, u32[]{:S(2)}) collective-permute-start(bf16[160,384]{1,0:T(8,128)(2,1)S(1)} %get-tuple-element.22.refs_0_), channel_id=1, source_target_pairs={{0,4},{4,0},{8,12},{12,8},{1,5},{5,1},{9,13},{13,9},{2,6},{6,2},{1... | collective-permute-start | bytes 368648 | tf_op jit(solution)/shard_map/ppermute | solution.py:237
  31.5 2.0 %collective-permute-start.7 = (bf16[160,384]{1,0:T(8,128)(2,1)S(1)}, bf16[160,384]{1,0:T(8,128)(2,1)S(1)}, u32[]{:S(2)}, u32[]{:S(2)}) collective-permute-start(bf16[160,384]{1,0:T(8,128)(2,1)S(1)} %get-tuple-element.22.refs_0_), channel_id=1, source_target_pairs={{0,8},{4,12},{8,0},{12,4},{1,9},{5,13},{9,1},{13,5},{2,10},{6,14},... | collective-permute-start | bytes 368648 | tf_op jit(solution)/shard_map/ppermute | solution.py:237
  33.4 4.8 %collective-permute-done.10.refs_2_ = bf16[160,384]{1,0:T(8,128)(2,1)S(1)} collective-permute-done((bf16[160,384]{1,0:T(8,128)(2,1)S(1)}, bf16[160,384]{1,0:T(8,128)(2,1)S(1)}, u32[]{:S(2)}, u32[]{:S(2)}) %collective-permute-start.10) | collective-permute-done | bytes 122912 | tf_op jit(solution)/shard_map/ppermute | solution.py:237
  38.2 2.9 %collective-permute-start.8 = (bf16[160,384]{1,0:T(8,128)(2,1)S(1)}, bf16[160,384]{1,0:T(8,128)(2,1)S(1)}, u32[]{:S(2)}, u32[]{:S(2)}) collective-permute-start(bf16[160,384]{1,0:T(8,128)(2,1)S(1)} %get-tuple-element.22.refs_0_), channel_id=1, source_target_pairs={{0,12},{4,8},{8,4},{12,0},{1,13},{5,9},{9,5},{13,1},{2,14},{6,10},... | collective-permute-start | bytes 368648 | tf_op jit(solution)/shard_map/ppermute | solution.py:237
  41.1 0.0 collective-permute-done.11.refs_3_
  41.1 0.0 collective-permute-done.9.refs_1_
  41.1 0.0 copy-done.1
  41.1 0.9 %shard_map.99 = (bf16[80,1280]{1,0:T(8,128)(2,1)S(1)}, bf16[80,1280]{1,0:T(8,128)(2,1)S(1)}) custom-call(bf16[160,384]{1,0:T(8,128)(2,1)S(1)} %get-tuple-element.24.refs_0_, bf16[160,384]{1,0:T(8,128)(2,1)S(1)} %collective-permute-done.9.refs_1_, bf16[160,384]{1,0:T(8,128)(2,1)S(1)} %collective-permute-done.10.refs_2_, ...), custom_call_target="tpu_custom_call" | custom-call | flops 629145600 | tf_op jit(solution)/shard_map/pallas_call | solution.py:251
  42.0 0.6 collective-permute-start.14
  42.6 0.0 copy-start.4
  42.6 1.5 %collective-permute-start.12 = (bf16[80,1280]{1,0:T(8,128)(2,1)S(1)}, bf16[80,1280]{1,0:T(8,128)(2,1)S(1)}, u32[]{:S(2)}, u32[]{:S(2)}) collective-permute-start(bf16[80,1280]{1,0:T(8,128)(2,1)S(1)} %get-tuple-element.25), channel_id=1, source_target_pairs={{0,2},{2,0},{1,3},{3,1},{4,6},{6,4},{5,7},{7,5},{8,10},{10,8},{9,1... | collective-permute-start | bytes 614408 | tf_op jit(solution)/shard_map/ppermute | solution.py:327
  44.1 0.0 collective-permute-done.6.refs_1_
  44.1 4.6 %collective-permute-done.7.refs_2_ = bf16[160,384]{1,0:T(8,128)(2,1)S(1)} collective-permute-done((bf16[160,384]{1,0:T(8,128)(2,1)S(1)}, bf16[160,384]{1,0:T(8,128)(2,1)S(1)}, u32[]{:S(2)}, u32[]{:S(2)}) %collective-permute-start.7) | collective-permute-done | bytes 122912 | tf_op jit(solution)/shard_map/ppermute | solution.py:237
  48.7 0.0 collective-permute-done.8.refs_3_
  48.7 0.9 %shard_map.98 = (f32[80,1280]{1,0:T(8,128)S(1)}, f32[80,1280]{1,0:T(8,128)S(1)}) custom-call(bf16[160,384]{1,0:T(8,128)(2,1)S(1)} %get-tuple-element.22.refs_0_, bf16[160,384]{1,0:T(8,128)(2,1)S(1)} %collective-permute-done.6.refs_1_, bf16[160,384]{1,0:T(8,128)(2,1)S(1)} %collective-permute-done.7.refs_2_, ...), custom_call_target="tpu_custom_call" | custom-call | flops 5033164800 | tf_op jit(solution)/shard_map/pallas_call | solution.py:251
  49.7 0.0 copy-start.2
  49.7 0.0 collective-permute-done.14.arrived
  49.7 0.1 shard_map.102
  49.8 5.8 %collective-permute-start.15 = (bf16[80,1280]{1,0:T(8,128)(2,1)S(1)}, bf16[80,1280]{1,0:T(8,128)(2,1)S(1)}, u32[]{:S(2)}, u32[]{:S(2)}) collective-permute-start(bf16[80,1280]{1,0:T(8,128)(2,1)S(1)} %shard_map.102), channel_id=1, source_target_pairs={{0,0},{1,4},{2,8},{3,12},{4,1},{5,5},{6,9},{7,13},{8,2},{9,6},{10,... | collective-permute-start | bytes 614408 | tf_op jit(solution)/shard_map/ppermute | solution.py:335
  55.6 0.0 collective-permute-done.12.arrived
  55.6 0.1 collective-permute-start.13
  55.7 0.0 copy-done.4
  55.7 0.0 copy-done.3
  55.7 0.0 copy-done
  55.7 0.0 copy-done.2
  55.7 0.8 %shard_map.101.resting = f32[160,1280]{1,0:T(8,128)S(1)} custom-call(s32[4]{0:T(128)S(1)} %copy-done.3, f32[160,1280]{1,0:T(8,128)S(1)} %copy-done.2, f32[4,160,1280]{2,1,0:T(8,128)S(1)} %copy-done), custom_call_target="tpu_custom_call" | custom-call | tf_op jit(solution)/shard_map/pallas_call | solution.py:251
  56.5 9.2 %collective-permute-done.15.owned = bf16[80,1280]{1,0:T(8,128)(2,1)S(1)} collective-permute-done((bf16[80,1280]{1,0:T(8,128)(2,1)S(1)}, bf16[80,1280]{1,0:T(8,128)(2,1)S(1)}, u32[]{:S(2)}, u32[]{:S(2)}) %collective-permute-start.15) | collective-permute-done | bytes 204832 | tf_op jit(solution)/shard_map/ppermute | solution.py:335
  65.7 0.9 %shard_map.103 = (f32[160,1280]{1,0:T(8,128)}, f32[160,1280]{1,0:T(8,128)}) custom-call(bf16[80,1280]{1,0:T(8,128)(2,1)S(1)} %collective-permute-done.15.owned, f32[1,1280]{1,0:T(1,128)S(1)} %broadcast_in_dim.3.gate, f32[160,1280]{1,0:T(8,128)S(1)} %shard_map.101.resting), custom_call_target="tpu_custom_call" | custom-call | tf_op jit(solution)/shard_map/pallas_call | solution.py:342
  66.7 0.0 collective-permute-done.13.owned
  66.7 1.0 %shard_map.104 = (f32[160,1280]{1,0:T(8,128)}, f32[160,1280]{1,0:T(8,128)}) custom-call(bf16[80,1280]{1,0:T(8,128)(2,1)S(1)} %collective-permute-done.13.owned, f32[1,1280]{1,0:T(1,128)S(1)} %broadcast_in_dim.3.gate, f32[160,1280]{1,0:T(8,128)S(1)} %shard_map.101.resting, ...), custom_call_target="tpu_custom_call", output_to_operand_aliasing={{0}: (3, {}), {1}: (4, {})} | custom-call | tf_op jit(solution)/shard_map/pallas_call | solution.py:342
  (5 shorter events, 0.1 us)
Async XLA Ops:
  0.6 40.4 %copy-start.1 = (bf16[768,1280]{1,0:T(8,128)(2,1)S(1)}, bf16[768,1280]{1,0:T(8,128)(2,1)}, u32[]{:S(2)}) copy-start(bf16[768,1280]{1,0:T(8,128)(2,1)} %refs_4_.3) | copy-start | bytes 5898244
  2.0 21.8 %collective-permute-start.5 = (bf16[768,1280]{1,0:T(8,128)(2,1)}, bf16[768,1280]{1,0:T(8,128)(2,1)S(1)}, u32[]{:S(2)}, u32[]{:S(2)}) collective-permute-start(bf16[768,1280]{1,0:T(8,128)(2,1)} %refs_4_.3), channel_id=1, source_target_pairs={{0,1},{1,0},{2,3},{3,2},{4,5},{5,4},{6,7},{7,6},{8,9},{9,8},{10,11... | collective-permute-start | bytes 5898248 | tf_op jit(solution)/shard_map/ppermute | solution.py:287
  2.1 17.8 %collective-permute-start = (bf16[320,384]{1,0:T(8,128)(2,1)S(1)}, bf16[320,384]{1,0:T(8,128)(2,1)S(1)}, u32[]{:S(2)}, u32[]{:S(2)}) collective-permute-start(bf16[320,384]{1,0:T(8,128)(2,1)S(1)} %get-tuple-element.16), channel_id=1, source_target_pairs={{0,0},{1,4},{4,1},{5,5},{8,8},{9,12},{12,9},{13,13},{2,2},{3,6},{6... | collective-permute-start | bytes 737288 | tf_op jit(solution)/shard_map/ppermute | solution.py:296
  2.8 17.1 %collective-permute-start.1 = (bf16[320,384]{1,0:T(8,128)(2,1)S(1)}, bf16[320,384]{1,0:T(8,128)(2,1)S(1)}, u32[]{:S(2)}, u32[]{:S(2)}) collective-permute-start(bf16[320,384]{1,0:T(8,128)(2,1)S(1)} %get-tuple-element.17), channel_id=1, source_target_pairs={{0,8},{1,12},{4,9},{5,13},{8,0},{9,4},{12,1},{13,5},{2,10},{3,14},... | collective-permute-start | bytes 737288 | tf_op jit(solution)/shard_map/ppermute | solution.py:296
  5.4 7.4 %collective-permute-start.2 = (bf16[160,384]{1,0:T(8,128)(2,1)S(1)}, bf16[160,384]{1,0:T(8,128)(2,1)S(1)}, u32[]{:S(2)}, u32[]{:S(2)}) collective-permute-start(bf16[160,384]{1,0:T(8,128)(2,1)S(1)} %get-tuple-element.18), channel_id=1, source_target_pairs={{0,1},{1,5},{4,0},{5,4},{8,9},{9,13},{12,8},{13,12},{2,3},{3,7},{6... | collective-permute-start | bytes 368648 | tf_op jit(solution)/shard_map/ppermute | solution.py:296
  8.3 11.5 %collective-permute-start.3 = (bf16[160,384]{1,0:T(8,128)(2,1)S(1)}, bf16[160,384]{1,0:T(8,128)(2,1)S(1)}, u32[]{:S(2)}, u32[]{:S(2)}) collective-permute-start(bf16[160,384]{1,0:T(8,128)(2,1)S(1)} %get-tuple-element.19), channel_id=1, source_target_pairs={{0,9},{1,13},{4,8},{5,12},{8,1},{9,5},{12,0},{13,4},{2,11},{3,15},... | collective-permute-start | bytes 368648 | tf_op jit(solution)/shard_map/ppermute | solution.py:296
  19.9 3.9 %collective-permute-start.4 = (bf16[640,384]{1,0:T(8,128)(2,1)S(1)}, bf16[640,384]{1,0:T(8,128)(2,1)S(1)}, u32[]{:S(2)}, u32[]{:S(2)}) collective-permute-start(bf16[640,384]{1,0:T(8,128)(2,1)S(1)} %shard_map.96), channel_id=1, source_target_pairs={{0,1},{1,0},{2,3},{3,2},{4,5},{5,4},{6,7},{7,6},{8,9},{9,8},{10,11... | collective-permute-start | bytes 1474568 | tf_op jit(solution)/shard_map/ppermute | solution.py:298
  25.5 12.7 %collective-permute-start.10 = (bf16[160,384]{1,0:T(8,128)(2,1)S(1)}, bf16[160,384]{1,0:T(8,128)(2,1)S(1)}, u32[]{:S(2)}, u32[]{:S(2)}) collective-permute-start(bf16[160,384]{1,0:T(8,128)(2,1)S(1)} %get-tuple-element.24.refs_0_), channel_id=1, source_target_pairs={{0,8},{4,12},{8,0},{12,4},{1,9},{5,13},{9,1},{13,5},{2,10},{6,14},... | collective-permute-start | bytes 368648 | tf_op jit(solution)/shard_map/ppermute | solution.py:237
  29.0 12.1 %collective-permute-start.11 = (bf16[160,384]{1,0:T(8,128)(2,1)S(1)}, bf16[160,384]{1,0:T(8,128)(2,1)S(1)}, u32[]{:S(2)}, u32[]{:S(2)}) collective-permute-start(bf16[160,384]{1,0:T(8,128)(2,1)S(1)} %get-tuple-element.24.refs_0_), channel_id=1, source_target_pairs={{0,12},{4,8},{8,4},{12,0},{1,13},{5,9},{9,5},{13,1},{2,14},{6,10},... | collective-permute-start | bytes 368648 | tf_op jit(solution)/shard_map/ppermute | solution.py:237
  29.5 11.6 %collective-permute-start.9 = (bf16[160,384]{1,0:T(8,128)(2,1)S(1)}, bf16[160,384]{1,0:T(8,128)(2,1)S(1)}, u32[]{:S(2)}, u32[]{:S(2)}) collective-permute-start(bf16[160,384]{1,0:T(8,128)(2,1)S(1)} %get-tuple-element.24.refs_0_), channel_id=1, source_target_pairs={{0,4},{4,0},{8,12},{12,8},{1,5},{5,1},{9,13},{13,9},{2,6},{6,2},{1... | collective-permute-start | bytes 368648 | tf_op jit(solution)/shard_map/ppermute | solution.py:237
  29.7 14.4 %collective-permute-start.6 = (bf16[160,384]{1,0:T(8,128)(2,1)S(1)}, bf16[160,384]{1,0:T(8,128)(2,1)S(1)}, u32[]{:S(2)}, u32[]{:S(2)}) collective-permute-start(bf16[160,384]{1,0:T(8,128)(2,1)S(1)} %get-tuple-element.22.refs_0_), channel_id=1, source_target_pairs={{0,4},{4,0},{8,12},{12,8},{1,5},{5,1},{9,13},{13,9},{2,6},{6,2},{1... | collective-permute-start | bytes 368648 | tf_op jit(solution)/shard_map/ppermute | solution.py:237
  31.5 17.2 %collective-permute-start.7 = (bf16[160,384]{1,0:T(8,128)(2,1)S(1)}, bf16[160,384]{1,0:T(8,128)(2,1)S(1)}, u32[]{:S(2)}, u32[]{:S(2)}) collective-permute-start(bf16[160,384]{1,0:T(8,128)(2,1)S(1)} %get-tuple-element.22.refs_0_), channel_id=1, source_target_pairs={{0,8},{4,12},{8,0},{12,4},{1,9},{5,13},{9,1},{13,5},{2,10},{6,14},... | collective-permute-start | bytes 368648 | tf_op jit(solution)/shard_map/ppermute | solution.py:237
  38.2 10.5 %collective-permute-start.8 = (bf16[160,384]{1,0:T(8,128)(2,1)S(1)}, bf16[160,384]{1,0:T(8,128)(2,1)S(1)}, u32[]{:S(2)}, u32[]{:S(2)}) collective-permute-start(bf16[160,384]{1,0:T(8,128)(2,1)S(1)} %get-tuple-element.22.refs_0_), channel_id=1, source_target_pairs={{0,12},{4,8},{8,4},{12,0},{1,13},{5,9},{9,5},{13,1},{2,14},{6,10},... | collective-permute-start | bytes 368648 | tf_op jit(solution)/shard_map/ppermute | solution.py:237
  42.0 7.7 %collective-permute-start.14 = (bf16[80,1280]{1,0:T(8,128)(2,1)S(1)}, bf16[80,1280]{1,0:T(8,128)(2,1)S(1)}, u32[]{:S(2)}, u32[]{:S(2)}) collective-permute-start(bf16[80,1280]{1,0:T(8,128)(2,1)S(1)} %get-tuple-element.27), channel_id=1, source_target_pairs={{0,2},{2,0},{1,3},{3,1},{4,6},{6,4},{5,7},{7,5},{8,10},{10,8},{9,1... | collective-permute-start | bytes 614408 | tf_op jit(solution)/shard_map/ppermute | solution.py:327
  42.6 13.1 %copy-start.4 = (f32[1280]{0:T(1024)S(1)}, f32[1280]{0:T(1024)}, u32[]{:S(2)}) copy-start(f32[1280]{0:T(1024)} %param.12) | copy-start | bytes 15364
  42.6 13.1 %copy-start.3 = (s32[4]{0:T(128)S(1)}, s32[4]{0:T(128)}, u32[]{:S(2)}) copy-start(s32[4]{0:T(128)} %flags.1) | copy-start | bytes 52
  42.6 13.0 %collective-permute-start.12 = (bf16[80,1280]{1,0:T(8,128)(2,1)S(1)}, bf16[80,1280]{1,0:T(8,128)(2,1)S(1)}, u32[]{:S(2)}, u32[]{:S(2)}) collective-permute-start(bf16[80,1280]{1,0:T(8,128)(2,1)S(1)} %get-tuple-element.25), channel_id=1, source_target_pairs={{0,2},{2,0},{1,3},{3,1},{4,6},{6,4},{5,7},{7,5},{8,10},{10,8},{9,1... | collective-permute-start | bytes 614408 | tf_op jit(solution)/shard_map/ppermute | solution.py:327
  48.7 7.0 %copy-start = (f32[4,160,1280]{2,1,0:T(8,128)S(1)}, f32[4,160,1280]{2,1,0:T(8,128)}, u32[]{:S(2)}) copy-start(f32[4,160,1280]{2,1,0:T(8,128)} %cached.1) | copy-start | bytes 9830404
  49.7 6.1 %copy-start.2 = (f32[160,1280]{1,0:T(8,128)S(1)}, f32[160,1280]{1,0:T(8,128)}, u32[]{:S(2)}) copy-start(f32[160,1280]{1,0:T(8,128)} %hidden.1) | copy-start | bytes 2457604
  49.8 16.0 %collective-permute-start.15 = (bf16[80,1280]{1,0:T(8,128)(2,1)S(1)}, bf16[80,1280]{1,0:T(8,128)(2,1)S(1)}, u32[]{:S(2)}, u32[]{:S(2)}) collective-permute-start(bf16[80,1280]{1,0:T(8,128)(2,1)S(1)} %shard_map.102), channel_id=1, source_target_pairs={{0,0},{1,4},{2,8},{3,12},{4,1},{5,5},{6,9},{7,13},{8,2},{9,6},{10,... | collective-permute-start | bytes 614408 | tf_op jit(solution)/shard_map/ppermute | solution.py:335
  55.6 11.1 %collective-permute-start.13 = (bf16[80,1280]{1,0:T(8,128)(2,1)S(1)}, bf16[80,1280]{1,0:T(8,128)(2,1)S(1)}, u32[]{:S(2)}, u32[]{:S(2)}) collective-permute-start(bf16[80,1280]{1,0:T(8,128)(2,1)S(1)} %shard_map.100), channel_id=1, source_target_pairs={{0,8},{1,12},{2,0},{3,4},{4,9},{5,13},{6,1},{7,5},{8,10},{9,14},{1... | collective-permute-start | bytes 614408 | tf_op jit(solution)/shard_map/ppermute | solution.py:335

commit v17 on v16

--- a/solution.py
+++ b/solution.py
@@ -192,10 +192,10 @@
     shards, (weight, weight_c, out0, out1, held) = refs[:4], refs[4:]
     total = multiply(shards, weight, weight_c, held)
     half = out0.shape[0]
-    x = lax.axis_index("wt")
-    for low in range(2):
-        part = total[low * half : (low + 1) * half].astype(out0.dtype)
-        first = flip(x, low) == 1 - kept
+    side = lax.rem(lax.axis_index("wt") + lax.axis_index("head"), 2)
+    for high in range(2):
+        part = total[high * half : (high + 1) * half].astype(out0.dtype)
+        first = flip(side, high) == 1 - kept
 
         @pl.when(first)
         def _():
@@ -220,8 +220,8 @@
 def final_kernel(piece, owned, gate, resting, *refs):
     mixed, fresh, mixed_part, fresh_part, sems = refs[-5:]
     half = owned.shape[0]
-    zh, _ = bits()
-    rows = pl.ds(pl.multiple_of(flip(zh, piece) * half, 16), half)
+    zh, zl = bits()
+    rows = pl.ds(pl.multiple_of(flip(lax.rem(zh + zl, 2), piece) * half, 16), half)
     delta = owned[...].astype(jnp.float32) * gate[...]
     fresh_part[...] = delta
     copy_fresh = pltpu.make_async_copy(fresh_part, fresh.at[rows, :], sems.at[0])
@@ -330,7 +330,7 @@
         for zz in range(4):
             for xx in range(2):
                 for cc in range(2):
-                    to = ((cc + 2 * (p ^ xx)) * 2 + zz // 2) * 2 + zz % 2
+                    to = ((cc + 2 * (p ^ xx ^ cc)) * 2 + zz // 2) * 2 + zz % 2
                     pairs.append(((zz * 2 + xx) * 2 + cc, to))
         owned.append(lax.ppermute(summed, ("seq", "wt", "head"), pairs))
     (resting,) = call(

time: 67.8 us -> 69.4 us (1.024)
  the two profiles are of different devices: /device:TPU:2 before, /device:TPU:1 now
where the time goes in v17:
time: 69.4 us; the launch traced here: 69.2 us
  waiting for transfers between devices  34.8 us (50%)
  starting transfers between devices  25.9 us (37%)
  Pallas kernels  7.63 us (11%)
  between operations  0.81 us (1%)
    ppermute x4, waiting for transfers between devices, local_heads(): moved.append(lax.ppermute(packed[k], ('seq', 'head'), pairs))  12.2 us
    ppermute x6, waiting for transfers between devices, along(): return lax.ppermute(shard, 'seq', [(z, z ^ m) for z in range(4)])  12.1 us
    ppermute x2, waiting for transfers between devices, local_heads(): owned.append(lax.ppermute(summed, ('seq', 'wt', 'head'), pairs))  8.63 us
    ppermute x6, starting transfers between devices, along(): return lax.ppermute(shard, 'seq', [(z, z ^ m) for z in range(4)])  8.54 us
    ppermute x4, starting transfers between devices, local_heads(): moved.append(lax.ppermute(packed[k], ('seq', 'head'), pairs))  8.28 us
    ppermute x2, starting transfers between devices, local_heads(): owned.append(lax.ppermute(summed, ('seq', 'wt', 'head'), pairs))  7.4 us
    pallas_call x8, Pallas kernels, call(): pl.pallas_call(kernel, in_specs=[pl.BlockSpec(memory_space=place) for pla...  5.73 us
    pallas_call x2, Pallas kernels, local_heads(): pl.pallas_call(functools.partial(final_kernel, p), in_specs=[pl.BlockSpec...  1.9 us
  transfers between devices with their start and end apart: 16, of which 7 were waited for; matrix products, arithmetic and copies ran while one was open for 0% of the time, Pallas kernels for 5%

profile of v17, /device:TPU:1, one launch (start us, length us, event | category | flops | bytes accessed | tf_op | source)
XLA Modules:
  0.0 69.2 jit_solution(13364570830248971645)
XLA Ops:
  0.6 0.0 copy-start.1
  0.6 1.4 %shard_map.95 = (bf16[320,384]{1,0:T(8,128)(2,1)S(1)}, bf16[320,384]{1,0:T(8,128)(2,1)S(1)}, bf16[160,384]{1,0:T(8,128)(2,1)S(1)}, bf16[160,384]{1,0:T(8,128)(2,1)S(1)}) custom-call(bf16[160,768]{1,0:T(8,128)(2,1)} %queries.1, bf16[160,768]{1,0:T(8,128)(2,1)} %keys.1, bf16[160,768]{1,0:T(8,128)(2,1)} %values.1), custom_call_target="tpu_custom_call" | custom-call | tf_op jit(solution)/shard_map/pallas_call | solution.py:251
  2.0 0.1 collective-permute-start.5
  2.1 4.6 %collective-permute-start = (bf16[320,384]{1,0:T(8,128)(2,1)S(1)}, bf16[320,384]{1,0:T(8,128)(2,1)S(1)}, u32[]{:S(2)}, u32[]{:S(2)}) collective-permute-start(bf16[320,384]{1,0:T(8,128)(2,1)S(1)} %get-tuple-element.16), channel_id=1, source_target_pairs={{0,0},{1,4},{4,1},{5,5},{8,8},{9,12},{12,9},{13,13},{2,2},{3,6},{6... | collective-permute-start | bytes 737288 | tf_op jit(solution)/shard_map/ppermute | solution.py:296
  6.7 2.6 %collective-permute-start.1 = (bf16[320,384]{1,0:T(8,128)(2,1)S(1)}, bf16[320,384]{1,0:T(8,128)(2,1)S(1)}, u32[]{:S(2)}, u32[]{:S(2)}) collective-permute-start(bf16[320,384]{1,0:T(8,128)(2,1)S(1)} %get-tuple-element.17), channel_id=1, source_target_pairs={{0,8},{1,12},{4,9},{5,13},{8,0},{9,4},{12,1},{13,5},{2,10},{3,14},... | collective-permute-start | bytes 737288 | tf_op jit(solution)/shard_map/ppermute | solution.py:296
  9.3 0.0 collective-permute-start.2
  9.3 1.1 %collective-permute-start.3 = (bf16[160,384]{1,0:T(8,128)(2,1)S(1)}, bf16[160,384]{1,0:T(8,128)(2,1)S(1)}, u32[]{:S(2)}, u32[]{:S(2)}) collective-permute-start(bf16[160,384]{1,0:T(8,128)(2,1)S(1)} %get-tuple-element.19), channel_id=1, source_target_pairs={{0,9},{1,13},{4,8},{5,12},{8,1},{9,5},{12,0},{13,4},{2,11},{3,15},... | collective-permute-start | bytes 368648 | tf_op jit(solution)/shard_map/ppermute | solution.py:296
  10.4 7.3 %collective-permute-done.2.refs_2_ = bf16[160,384]{1,0:T(8,128)(2,1)S(1)} collective-permute-done((bf16[160,384]{1,0:T(8,128)(2,1)S(1)}, bf16[160,384]{1,0:T(8,128)(2,1)S(1)}, u32[]{:S(2)}, u32[]{:S(2)}) %collective-permute-start.2) | collective-permute-done | bytes 122912 | tf_op jit(solution)/shard_map/ppermute | solution.py:296
  17.7 4.9 %collective-permute-done.3.refs_3_ = bf16[160,384]{1,0:T(8,128)(2,1)S(1)} collective-permute-done((bf16[160,384]{1,0:T(8,128)(2,1)S(1)}, bf16[160,384]{1,0:T(8,128)(2,1)S(1)}, u32[]{:S(2)}, u32[]{:S(2)}) %collective-permute-start.3) | collective-permute-done | bytes 122912 | tf_op jit(solution)/shard_map/ppermute | solution.py:296
  22.6 0.0 collective-permute-done.refs_0_
  22.6 0.0 collective-permute-done.1.refs_1_
  22.6 0.1 collective-permute-start.4
  22.7 1.9 %collective-permute-done.4.refs_4_ = bf16[640,384]{1,0:T(8,128)(2,1)S(1)} collective-permute-done((bf16[640,384]{1,0:T(8,128)(2,1)S(1)}, bf16[640,384]{1,0:T(8,128)(2,1)S(1)}, u32[]{:S(2)}, u32[]{:S(2)}) %collective-permute-start.4) | collective-permute-done | bytes 491552 | tf_op jit(solution)/shard_map/ppermute | solution.py:298
  24.6 0.0 collective-permute-done.5.refs_5_
  24.6 1.6 %shard_map.97 = (bf16[160,384]{1,0:T(8,128)(2,1)S(1)}, bf16[160,384]{1,0:T(8,128)(2,1)S(1)}) custom-call(bf16[320,384]{1,0:T(8,128)(2,1)S(1)} %collective-permute-done.refs_0_, bf16[320,384]{1,0:T(8,128)(2,1)S(1)} %collective-permute-done.1.refs_1_, bf16[160,384]{1,0:T(8,128)(2,1)S(1)} %collective-permute-done.2.refs_2_, ...), custom_call_target="tpu_custom_call" | custom-call | flops 314572800 | tf_op jit(solution)/shard_map/pallas_call | solution.py:251
  26.2 3.7 %collective-permute-start.10 = (bf16[160,384]{1,0:T(8,128)(2,1)S(1)}, bf16[160,384]{1,0:T(8,128)(2,1)S(1)}, u32[]{:S(2)}, u32[]{:S(2)}) collective-permute-start(bf16[160,384]{1,0:T(8,128)(2,1)S(1)} %get-tuple-element.24.refs_0_), channel_id=1, source_target_pairs={{0,8},{4,12},{8,0},{12,4},{1,9},{5,13},{9,1},{13,5},{2,10},{6,14},... | collective-permute-start | bytes 368648 | tf_op jit(solution)/shard_map/ppermute | solution.py:237
  29.9 0.2 collective-permute-start.11
  30.0 0.2 collective-permute-start.9
  30.2 1.3 %collective-permute-start.6 = (bf16[160,384]{1,0:T(8,128)(2,1)S(1)}, bf16[160,384]{1,0:T(8,128)(2,1)S(1)}, u32[]{:S(2)}, u32[]{:S(2)}) collective-permute-start(bf16[160,384]{1,0:T(8,128)(2,1)S(1)} %get-tuple-element.22.refs_0_), channel_id=1, source_target_pairs={{0,4},{4,0},{8,12},{12,8},{1,5},{5,1},{9,13},{13,9},{2,6},{6,2},{1... | collective-permute-start | bytes 368648 | tf_op jit(solution)/shard_map/ppermute | solution.py:237
  31.5 2.0 %collective-permute-start.7 = (bf16[160,384]{1,0:T(8,128)(2,1)S(1)}, bf16[160,384]{1,0:T(8,128)(2,1)S(1)}, u32[]{:S(2)}, u32[]{:S(2)}) collective-permute-start(bf16[160,384]{1,0:T(8,128)(2,1)S(1)} %get-tuple-element.22.refs_0_), channel_id=1, source_target_pairs={{0,8},{4,12},{8,0},{12,4},{1,9},{5,13},{9,1},{13,5},{2,10},{6,14},... | collective-permute-start | bytes 368648 | tf_op jit(solution)/shard_map/ppermute | solution.py:237
  33.4 5.4 %collective-permute-done.10.refs_2_ = bf16[160,384]{1,0:T(8,128)(2,1)S(1)} collective-permute-done((bf16[160,384]{1,0:T(8,128)(2,1)S(1)}, bf16[160,384]{1,0:T(8,128)(2,1)S(1)}, u32[]{:S(2)}, u32[]{:S(2)}) %collective-permute-start.10) | collective-permute-done | bytes 122912 | tf_op jit(solution)/shard_map/ppermute | solution.py:237
  38.8 1.3 %collective-permute-start.8 = (bf16[160,384]{1,0:T(8,128)(2,1)S(1)}, bf16[160,384]{1,0:T(8,128)(2,1)S(1)}, u32[]{:S(2)}, u32[]{:S(2)}) collective-permute-start(bf16[160,384]{1,0:T(8,128)(2,1)S(1)} %get-tuple-element.22.refs_0_), channel_id=1, source_target_pairs={{0,12},{4,8},{8,4},{12,0},{1,13},{5,9},{9,5},{13,1},{2,14},{6,10},... | collective-permute-start | bytes 368648 | tf_op jit(solution)/shard_map/ppermute | solution.py:237
  40.1 0.0 collective-permute-done.11.refs_3_
  40.1 0.0 collective-permute-done.9.refs_1_
  40.1 0.0 copy-done.1
  40.1 0.9 %shard_map.99 = (bf16[80,1280]{1,0:T(8,128)(2,1)S(1)}, bf16[80,1280]{1,0:T(8,128)(2,1)S(1)}) custom-call(bf16[160,384]{1,0:T(8,128)(2,1)S(1)} %get-tuple-element.24.refs_0_, bf16[160,384]{1,0:T(8,128)(2,1)S(1)} %collective-permute-done.9.refs_1_, bf16[160,384]{1,0:T(8,128)(2,1)S(1)} %collective-permute-done.10.refs_2_, ...), custom_call_target="tpu_custom_call" | custom-call | flops 629145600 | tf_op jit(solution)/shard_map/pallas_call | solution.py:251
  41.0 1.3 %collective-permute-start.14 = (bf16[80,1280]{1,0:T(8,128)(2,1)S(1)}, bf16[80,1280]{1,0:T(8,128)(2,1)S(1)}, u32[]{:S(2)}, u32[]{:S(2)}) collective-permute-start(bf16[80,1280]{1,0:T(8,128)(2,1)S(1)} %get-tuple-element.27), channel_id=1, source_target_pairs={{0,2},{2,0},{1,3},{3,1},{4,6},{6,4},{5,7},{7,5},{8,10},{10,8},{9,1... | collective-permute-start | bytes 614408 | tf_op jit(solution)/shard_map/ppermute | solution.py:327
  42.3 0.0 copy-start.4
  42.3 0.3 collective-permute-start.12
  42.6 0.0 collective-permute-done.6.refs_1_
  42.6 6.8 %collective-permute-done.7.refs_2_ = bf16[160,384]{1,0:T(8,128)(2,1)S(1)} collective-permute-done((bf16[160,384]{1,0:T(8,128)(2,1)S(1)}, bf16[160,384]{1,0:T(8,128)(2,1)S(1)}, u32[]{:S(2)}, u32[]{:S(2)}) %collective-permute-start.7) | collective-permute-done | bytes 122912 | tf_op jit(solution)/shard_map/ppermute | solution.py:237
  49.3 0.0 collective-permute-done.8.refs_3_
  49.3 0.9 %shard_map.98 = (f32[80,1280]{1,0:T(8,128)S(1)}, f32[80,1280]{1,0:T(8,128)S(1)}) custom-call(bf16[160,384]{1,0:T(8,128)(2,1)S(1)} %get-tuple-element.22.refs_0_, bf16[160,384]{1,0:T(8,128)(2,1)S(1)} %collective-permute-done.6.refs_1_, bf16[160,384]{1,0:T(8,128)(2,1)S(1)} %collective-permute-done.7.refs_2_, ...), custom_call_target="tpu_custom_call" | custom-call | flops 5033164800 | tf_op jit(solution)/shard_map/pallas_call | solution.py:251
  50.3 0.0 copy-start.2
  50.3 0.0 collective-permute-done.14.arrived
  50.3 0.1 shard_map.102
  50.4 5.4 %collective-permute-start.15 = (bf16[80,1280]{1,0:T(8,128)(2,1)S(1)}, bf16[80,1280]{1,0:T(8,128)(2,1)S(1)}, u32[]{:S(2)}, u32[]{:S(2)}) collective-permute-start(bf16[80,1280]{1,0:T(8,128)(2,1)S(1)} %shard_map.102), channel_id=1, source_target_pairs={{0,0},{1,12},{2,8},{3,4},{4,1},{5,13},{6,9},{7,5},{8,2},{9,14},{10... | collective-permute-start | bytes 614408 | tf_op jit(solution)/shard_map/ppermute | solution.py:335
  55.8 0.0 collective-permute-done.12.arrived
  55.8 2.0 %collective-permute-start.13 = (bf16[80,1280]{1,0:T(8,128)(2,1)S(1)}, bf16[80,1280]{1,0:T(8,128)(2,1)S(1)}, u32[]{:S(2)}, u32[]{:S(2)}) collective-permute-start(bf16[80,1280]{1,0:T(8,128)(2,1)S(1)} %shard_map.100), channel_id=1, source_target_pairs={{0,8},{1,4},{2,0},{3,12},{4,9},{5,5},{6,1},{7,13},{8,10},{9,6},{10... | collective-permute-start | bytes 614408 | tf_op jit(solution)/shard_map/ppermute | solution.py:335
  57.8 0.0 copy-done.4
  57.8 0.0 copy-done.3
  57.9 0.0 copy-done
  57.9 0.0 copy-done.2
  57.9 0.8 %shard_map.101.resting = f32[160,1280]{1,0:T(8,128)S(1)} custom-call(s32[4]{0:T(128)S(1)} %copy-done.3, f32[160,1280]{1,0:T(8,128)S(1)} %copy-done.2, f32[4,160,1280]{2,1,0:T(8,128)S(1)} %copy-done), custom_call_target="tpu_custom_call" | custom-call | tf_op jit(solution)/shard_map/pallas_call | solution.py:251
  58.6 4.3 %collective-permute-done.15.owned = bf16[80,1280]{1,0:T(8,128)(2,1)S(1)} collective-permute-done((bf16[80,1280]{1,0:T(8,128)(2,1)S(1)}, bf16[80,1280]{1,0:T(8,128)(2,1)S(1)}, u32[]{:S(2)}, u32[]{:S(2)}) %collective-permute-start.15) | collective-permute-done | bytes 204832 | tf_op jit(solution)/shard_map/ppermute | solution.py:335
  62.9 0.9 %shard_map.103 = (f32[160,1280]{1,0:T(8,128)}, f32[160,1280]{1,0:T(8,128)}) custom-call(bf16[80,1280]{1,0:T(8,128)(2,1)S(1)} %collective-permute-done.15.owned, f32[1,1280]{1,0:T(1,128)S(1)} %broadcast_in_dim.3.gate, f32[160,1280]{1,0:T(8,128)S(1)} %shard_map.101.resting), custom_call_target="tpu_custom_call" | custom-call | tf_op jit(solution)/shard_map/pallas_call | solution.py:342
  63.9 4.3 %collective-permute-done.13.owned = bf16[80,1280]{1,0:T(8,128)(2,1)S(1)} collective-permute-done((bf16[80,1280]{1,0:T(8,128)(2,1)S(1)}, bf16[80,1280]{1,0:T(8,128)(2,1)S(1)}, u32[]{:S(2)}, u32[]{:S(2)}) %collective-permute-start.13) | collective-permute-done | bytes 204832 | tf_op jit(solution)/shard_map/ppermute | solution.py:335
  68.2 0.9 %shard_map.104 = (f32[160,1280]{1,0:T(8,128)}, f32[160,1280]{1,0:T(8,128)}) custom-call(bf16[80,1280]{1,0:T(8,128)(2,1)S(1)} %collective-permute-done.13.owned, f32[1,1280]{1,0:T(1,128)S(1)} %broadcast_in_dim.3.gate, f32[160,1280]{1,0:T(8,128)S(1)} %shard_map.101.resting, ...), custom_call_target="tpu_custom_call", output_to_operand_aliasing={{0}: (3, {}), {1}: (4, {})} | custom-call | tf_op jit(solution)/shard_map/pallas_call | solution.py:342
  (5 shorter events, 0.1 us)
Async XLA Ops:
  0.6 39.5 %copy-start.1 = (bf16[768,1280]{1,0:T(8,128)(2,1)S(1)}, bf16[768,1280]{1,0:T(8,128)(2,1)}, u32[]{:S(2)}) copy-start(bf16[768,1280]{1,0:T(8,128)(2,1)} %refs_4_.3) | copy-start | bytes 5898244
  2.0 22.5 %collective-permute-start.5 = (bf16[768,1280]{1,0:T(8,128)(2,1)}, bf16[768,1280]{1,0:T(8,128)(2,1)S(1)}, u32[]{:S(2)}, u32[]{:S(2)}) collective-permute-start(bf16[768,1280]{1,0:T(8,128)(2,1)} %refs_4_.3), channel_id=1, source_target_pairs={{0,1},{1,0},{2,3},{3,2},{4,5},{5,4},{6,7},{7,6},{8,9},{9,8},{10,11... | collective-permute-start | bytes 5898248 | tf_op jit(solution)/shard_map/ppermute | solution.py:287
  2.1 20.4 %collective-permute-start = (bf16[320,384]{1,0:T(8,128)(2,1)S(1)}, bf16[320,384]{1,0:T(8,128)(2,1)S(1)}, u32[]{:S(2)}, u32[]{:S(2)}) collective-permute-start(bf16[320,384]{1,0:T(8,128)(2,1)S(1)} %get-tuple-element.16), channel_id=1, source_target_pairs={{0,0},{1,4},{4,1},{5,5},{8,8},{9,12},{12,9},{13,13},{2,2},{3,6},{6... | collective-permute-start | bytes 737288 | tf_op jit(solution)/shard_map/ppermute | solution.py:296
  6.7 15.9 %collective-permute-start.1 = (bf16[320,384]{1,0:T(8,128)(2,1)S(1)}, bf16[320,384]{1,0:T(8,128)(2,1)S(1)}, u32[]{:S(2)}, u32[]{:S(2)}) collective-permute-start(bf16[320,384]{1,0:T(8,128)(2,1)S(1)} %get-tuple-element.17), channel_id=1, source_target_pairs={{0,8},{1,12},{4,9},{5,13},{8,0},{9,4},{12,1},{13,5},{2,10},{3,14},... | collective-permute-start | bytes 737288 | tf_op jit(solution)/shard_map/ppermute | solution.py:296
  9.3 8.4 %collective-permute-start.2 = (bf16[160,384]{1,0:T(8,128)(2,1)S(1)}, bf16[160,384]{1,0:T(8,128)(2,1)S(1)}, u32[]{:S(2)}, u32[]{:S(2)}) collective-permute-start(bf16[160,384]{1,0:T(8,128)(2,1)S(1)} %get-tuple-element.18), channel_id=1, source_target_pairs={{0,1},{1,5},{4,0},{5,4},{8,9},{9,13},{12,8},{13,12},{2,3},{3,7},{6... | collective-permute-start | bytes 368648 | tf_op jit(solution)/shard_map/ppermute | solution.py:296
  9.3 13.2 %collective-permute-start.3 = (bf16[160,384]{1,0:T(8,128)(2,1)S(1)}, bf16[160,384]{1,0:T(8,128)(2,1)S(1)}, u32[]{:S(2)}, u32[]{:S(2)}) collective-permute-start(bf16[160,384]{1,0:T(8,128)(2,1)S(1)} %get-tuple-element.19), channel_id=1, source_target_pairs={{0,9},{1,13},{4,8},{5,12},{8,1},{9,5},{12,0},{13,4},{2,11},{3,15},... | collective-permute-start | bytes 368648 | tf_op jit(solution)/shard_map/ppermute | solution.py:296
  22.6 1.9 %collective-permute-start.4 = (bf16[640,384]{1,0:T(8,128)(2,1)S(1)}, bf16[640,384]{1,0:T(8,128)(2,1)S(1)}, u32[]{:S(2)}, u32[]{:S(2)}) collective-permute-start(bf16[640,384]{1,0:T(8,128)(2,1)S(1)} %shard_map.96), channel_id=1, source_target_pairs={{0,1},{1,0},{2,3},{3,2},{4,5},{5,4},{6,7},{7,6},{8,9},{9,8},{10,11... | collective-permute-start | bytes 1474568 | tf_op jit(solution)/shard_map/ppermute | solution.py:298
  26.2 12.6 %collective-permute-start.10 = (bf16[160,384]{1,0:T(8,128)(2,1)S(1)}, bf16[160,384]{1,0:T(8,128)(2,1)S(1)}, u32[]{:S(2)}, u32[]{:S(2)}) collective-permute-start(bf16[160,384]{1,0:T(8,128)(2,1)S(1)} %get-tuple-element.24.refs_0_), channel_id=1, source_target_pairs={{0,8},{4,12},{8,0},{12,4},{1,9},{5,13},{9,1},{13,5},{2,10},{6,14},... | collective-permute-start | bytes 368648 | tf_op jit(solution)/shard_map/ppermute | solution.py:237
  29.9 10.2 %collective-permute-start.11 = (bf16[160,384]{1,0:T(8,128)(2,1)S(1)}, bf16[160,384]{1,0:T(8,128)(2,1)S(1)}, u32[]{:S(2)}, u32[]{:S(2)}) collective-permute-start(bf16[160,384]{1,0:T(8,128)(2,1)S(1)} %get-tuple-element.24.refs_0_), channel_id=1, source_target_pairs={{0,12},{4,8},{8,4},{12,0},{1,13},{5,9},{9,5},{13,1},{2,14},{6,10},... | collective-permute-start | bytes 368648 | tf_op jit(solution)/shard_map/ppermute | solution.py:237
  30.0 10.1 %collective-permute-start.9 = (bf16[160,384]{1,0:T(8,128)(2,1)S(1)}, bf16[160,384]{1,0:T(8,128)(2,1)S(1)}, u32[]{:S(2)}, u32[]{:S(2)}) collective-permute-start(bf16[160,384]{1,0:T(8,128)(2,1)S(1)} %get-tuple-element.24.refs_0_), channel_id=1, source_target_pairs={{0,4},{4,0},{8,12},{12,8},{1,5},{5,1},{9,13},{13,9},{2,6},{6,2},{1... | collective-permute-start | bytes 368648 | tf_op jit(solution)/shard_map/ppermute | solution.py:237
  30.2 12.3 %collective-permute-start.6 = (bf16[160,384]{1,0:T(8,128)(2,1)S(1)}, bf16[160,384]{1,0:T(8,128)(2,1)S(1)}, u32[]{:S(2)}, u32[]{:S(2)}) collective-permute-start(bf16[160,384]{1,0:T(8,128)(2,1)S(1)} %get-tuple-element.22.refs_0_), channel_id=1, source_target_pairs={{0,4},{4,0},{8,12},{12,8},{1,5},{5,1},{9,13},{13,9},{2,6},{6,2},{1... | collective-permute-start | bytes 368648 | tf_op jit(solution)/shard_map/ppermute | solution.py:237
  31.5 17.8 %collective-permute-start.7 = (bf16[160,384]{1,0:T(8,128)(2,1)S(1)}, bf16[160,384]{1,0:T(8,128)(2,1)S(1)}, u32[]{:S(2)}, u32[]{:S(2)}) collective-permute-start(bf16[160,384]{1,0:T(8,128)(2,1)S(1)} %get-tuple-element.22.refs_0_), channel_id=1, source_target_pairs={{0,8},{4,12},{8,0},{12,4},{1,9},{5,13},{9,1},{13,5},{2,10},{6,14},... | collective-permute-start | bytes 368648 | tf_op jit(solution)/shard_map/ppermute | solution.py:237
  38.8 10.5 %collective-permute-start.8 = (bf16[160,384]{1,0:T(8,128)(2,1)S(1)}, bf16[160,384]{1,0:T(8,128)(2,1)S(1)}, u32[]{:S(2)}, u32[]{:S(2)}) collective-permute-start(bf16[160,384]{1,0:T(8,128)(2,1)S(1)} %get-tuple-element.22.refs_0_), channel_id=1, source_target_pairs={{0,12},{4,8},{8,4},{12,0},{1,13},{5,9},{9,5},{13,1},{2,14},{6,10},... | collective-permute-start | bytes 368648 | tf_op jit(solution)/shard_map/ppermute | solution.py:237
  41.0 9.3 %collective-permute-start.14 = (bf16[80,1280]{1,0:T(8,128)(2,1)S(1)}, bf16[80,1280]{1,0:T(8,128)(2,1)S(1)}, u32[]{:S(2)}, u32[]{:S(2)}) collective-permute-start(bf16[80,1280]{1,0:T(8,128)(2,1)S(1)} %get-tuple-element.27), channel_id=1, source_target_pairs={{0,2},{2,0},{1,3},{3,1},{4,6},{6,4},{5,7},{7,5},{8,10},{10,8},{9,1... | collective-permute-start | bytes 614408 | tf_op jit(solution)/shard_map/ppermute | solution.py:327
  42.3 15.5 %copy-start.4 = (f32[1280]{0:T(1024)S(1)}, f32[1280]{0:T(1024)}, u32[]{:S(2)}) copy-start(f32[1280]{0:T(1024)} %param.12) | copy-start | bytes 15364
  42.3 15.6 %copy-start.3 = (s32[4]{0:T(128)S(1)}, s32[4]{0:T(128)}, u32[]{:S(2)}) copy-start(s32[4]{0:T(128)} %flags.1) | copy-start | bytes 52
  42.3 13.5 %collective-permute-start.12 = (bf16[80,1280]{1,0:T(8,128)(2,1)S(1)}, bf16[80,1280]{1,0:T(8,128)(2,1)S(1)}, u32[]{:S(2)}, u32[]{:S(2)}) collective-permute-start(bf16[80,1280]{1,0:T(8,128)(2,1)S(1)} %get-tuple-element.25), channel_id=1, source_target_pairs={{0,2},{2,0},{1,3},{3,1},{4,6},{6,4},{5,7},{7,5},{8,10},{10,8},{9,1... | collective-permute-start | bytes 614408 | tf_op jit(solution)/shard_map/ppermute | solution.py:327
  49.3 8.5 %copy-start = (f32[4,160,1280]{2,1,0:T(8,128)S(1)}, f32[4,160,1280]{2,1,0:T(8,128)}, u32[]{:S(2)}) copy-start(f32[4,160,1280]{2,1,0:T(8,128)} %cached.1) | copy-start | bytes 9830404
  50.3 7.6 %copy-start.2 = (f32[160,1280]{1,0:T(8,128)S(1)}, f32[160,1280]{1,0:T(8,128)}, u32[]{:S(2)}) copy-start(f32[160,1280]{1,0:T(8,128)} %hidden.1) | copy-start | bytes 2457604
  50.4 12.6 %collective-permute-start.15 = (bf16[80,1280]{1,0:T(8,128)(2,1)S(1)}, bf16[80,1280]{1,0:T(8,128)(2,1)S(1)}, u32[]{:S(2)}, u32[]{:S(2)}) collective-permute-start(bf16[80,1280]{1,0:T(8,128)(2,1)S(1)} %shard_map.102), channel_id=1, source_target_pairs={{0,0},{1,12},{2,8},{3,4},{4,1},{5,13},{6,9},{7,5},{8,2},{9,14},{10... | collective-permute-start | bytes 614408 | tf_op jit(solution)/shard_map/ppermute | solution.py:335
  55.8 12.4 %collective-permute-start.13 = (bf16[80,1280]{1,0:T(8,128)(2,1)S(1)}, bf16[80,1280]{1,0:T(8,128)(2,1)S(1)}, u32[]{:S(2)}, u32[]{:S(2)}) collective-permute-start(bf16[80,1280]{1,0:T(8,128)(2,1)S(1)} %shard_map.100), channel_id=1, source_target_pairs={{0,8},{1,4},{2,0},{3,12},{4,9},{5,5},{6,1},{7,13},{8,10},{9,6},{10... | collective-permute-start | bytes 614408 | tf_op jit(solution)/shard_map/ppermute | solution.py:335

commit v18 on v16

--- a/solution.py
+++ b/solution.py
@@ -11,6 +11,7 @@
 VMEM_BYTES = 48 * 1024 * 1024
 PACK_BYTES = 53 * 1024 * 1024 + 128 * 1024
 LOG2_E = 1.4426950408889634
+ORDERS = ((2, 3, 1), (1, 2, 3))
 
 
 def attend(state_in, key_rows, value_rows, query_heads, score_scale):
@@ -128,17 +129,24 @@
         joined[k * rows : (k + 1) * rows, :] = block[:rows, :]
 
 
-def attention_kernel(*refs):
-    blocks, sibling = refs[:4], refs[4]
-    sent, kept, key_all, value_all, query_all = refs[5:]
-    rows = sent.shape[0]
-    half = rows // 2
+def exp_scaled(scores):
+    return jnp.exp2(scores * (LOG2_E * HEAD_DIM ** (-0.5)))
+
+
+def dot_keys(queries, keys):
+    return lax.dot_general(
+        queries, keys, (((1,), (1,)), ((), ())), preferred_element_type=jnp.float32
+    )
+
+
+def near_attention_kernel(*refs):
+    blocks, (query_all, weighted, peaks, totals, key_all, value_all) = refs[:4], refs[4:]
+    half = query_all.shape[0] // 4
+    rows = 2 * half
     for k in range(4):
-        here, there = slice(k * half, (k + 1) * half), slice((4 + k) * half, (5 + k) * half)
+        here = slice(k * half, (k + 1) * half)
         key_all[here, :] = blocks[k][:half, :]
         value_all[here, :] = blocks[k][half:rows, :]
-        key_all[there, :] = sibling[k * rows : k * rows + half, :]
-        value_all[there, :] = sibling[k * rows + half : (k + 1) * rows, :]
     zh, _ = bits()
     x = lax.axis_index("wt")
     for k in range(2):
@@ -148,18 +156,36 @@
             query_all[pl.ds(pl.multiple_of(to, 16), half), :] = blocks[k][
                 pl.ds(pl.multiple_of(at, 16), half), :
             ]
+    for h in range(query_all.shape[1] // HEAD_DIM):
+        columns = slice(h * HEAD_DIM, (h + 1) * HEAD_DIM)
+        scores = dot_keys(query_all[:, columns], key_all[:, columns])
+        peak = jnp.max(scores, axis=1, keepdims=True)
+        weights = exp_scaled(scores - peak)
+        weighted[:, columns] = jnp.dot(
+            weights.astype(jnp.bfloat16), value_all[:, columns], preferred_element_type=jnp.float32
+        )
+        shape = (scores.shape[0], HEAD_DIM)
+        peaks[:, columns] = jnp.broadcast_to(peak, shape)
+        totals[:, columns] = jnp.broadcast_to(jnp.sum(weights, axis=1, keepdims=True), shape)
+
+
+def attention_kernel(query_all, weighted, peaks, totals, sibling, *refs):
+    sent, kept, key_all, value_all = refs
+    rows = sent.shape[0]
+    half = rows // 2
+    for k in range(4):
+        there = slice(k * half, (k + 1) * half)
+        key_all[there, :] = sibling[k * rows : k * rows + half, :]
+        value_all[there, :] = sibling[k * rows + half : (k + 1) * rows, :]
     for h in range(sent.shape[1] // HEAD_DIM):
         columns = slice(h * HEAD_DIM, (h + 1) * HEAD_DIM)
-        scores = lax.dot_general(
-            query_all[:, columns],
-            key_all[:, columns],
-            (((1,), (1,)), ((), ())),
-            preferred_element_type=jnp.float32,
-        )
-        peak = jnp.max(scores, axis=1, keepdims=True)
-        weights = jnp.exp2((scores - peak) * (LOG2_E * HEAD_DIM ** (-0.5)))
-        total = jnp.sum(weights, axis=1, keepdims=True)
-        result = jnp.dot(
+        scores = dot_keys(query_all[:, columns], key_all[:, columns])
+        first_peak = peaks[:, columns]
+        peak = jnp.maximum(first_peak, jnp.max(scores, axis=1, keepdims=True))
+        rescale = exp_scaled(first_peak - peak)
+        weights = exp_scaled(scores - peak[:, :1])
+        total = totals[:, columns] * rescale + jnp.sum(weights, axis=1, keepdims=True)
+        result = weighted[:, columns] * rescale + jnp.dot(
             weights.astype(jnp.bfloat16), value_all[:, columns], preferred_element_type=jnp.float32
         )
         result = (result / total).astype(sent.dtype)
@@ -167,11 +193,11 @@
         kept[:, columns] = result[rows:]
 
 
-def multiply(shards, weight, weight_c, held):
+def multiply(shards, order, weight, weight_c, held):
     rows = shards[0].shape[0]
     zh, zl = bits()
     core = lax.axis_index("head")
-    for m, shard in enumerate(shards):
+    for m, shard in zip((0,) + order, shards):
         held[m * rows : (m + 1) * rows, :] = shard[...]
     total = None
     for other, block in enumerate((weight, weight_c)):
@@ -190,7 +216,7 @@
 
 def project_kernel(kept, *refs):
     shards, (weight, weight_c, out0, out1, held) = refs[:4], refs[4:]
-    total = multiply(shards, weight, weight_c, held)
+    total = multiply(shards, ORDERS[kept], weight, weight_c, held)
     half = out0.shape[0]
     x = lax.axis_index("wt")
     for low in range(2):
@@ -217,20 +243,26 @@
     out[...] = total
 
 
-def final_kernel(piece, owned, gate, resting, *refs):
-    mixed, fresh, mixed_part, fresh_part, sems = refs[-5:]
-    half = owned.shape[0]
+def final_kernel(owned0, owned1, gate, resting, mixed, fresh, mixed_part, fresh_part, sems):
+    half, count = owned0.shape[0], owned0.shape[1] // 2
     zh, _ = bits()
-    rows = pl.ds(pl.multiple_of(flip(zh, piece) * half, 16), half)
-    delta = owned[...].astype(jnp.float32) * gate[...]
-    fresh_part[...] = delta
-    copy_fresh = pltpu.make_async_copy(fresh_part, fresh.at[rows, :], sems.at[0])
-    copy_fresh.start()
-    mixed_part[...] = resting[rows, :] + delta
-    copy_mixed = pltpu.make_async_copy(mixed_part, mixed.at[rows, :], sems.at[1])
-    copy_mixed.start()
-    copy_fresh.wait()
-    copy_mixed.wait()
+    copies = []
+    for p, owned in enumerate((owned0, owned1)):
+        rows = pl.ds(pl.multiple_of(flip(zh, p) * half, 16), half)
+        for h in range(2):
+            columns = slice(h * count, (h + 1) * count)
+            delta = owned[:, columns].astype(jnp.float32) * gate[:, columns]
+            fresh_part[rows, columns] = delta
+            mixed_part[rows, columns] = resting[rows, columns] + delta
+            for part, out in ((fresh_part, fresh), (mixed_part, mixed)):
+                copies.append(
+                    pltpu.make_async_copy(
+                        part.at[rows, columns], out.at[rows, columns], sems.at[len(copies)]
+                    )
+                )
+                copies[-1].start()
+    for copy in copies:
+        copy.wait()
 
 
 def along(shard, m):
@@ -297,16 +329,21 @@
     (joined,) = call(join_kernel, moved, [((4 * rows, width), bf16)])
     sibling = lax.ppermute(joined, "head", swap)
     sibling, _ = lax.optimization_barrier((sibling, weight_c))
+    flops = 4 * (2 * rows) * (2 * rows) * width
+    half_keys = [pltpu.VMEM((2 * rows, width), bf16)] * 2
+    near = call(
+        near_attention_kernel,
+        moved,
+        [((2 * rows, width), bf16)] + [((2 * rows, width), jnp.float32)] * 3,
+        half_keys,
+        flops=flops,
+    )
     parts = call(
         attention_kernel,
-        moved + [sibling],
+        list(near) + [sibling],
         [((rows, width), bf16)] * 2,
-        [
-            pltpu.VMEM((4 * rows, width), bf16),
-            pltpu.VMEM((4 * rows, width), bf16),
-            pltpu.VMEM((2 * rows, width), bf16),
-        ],
-        flops=4 * (2 * rows) * (4 * rows) * width,
+        half_keys,
+        flops=flops,
     )
 
     half = rows // 2
@@ -314,7 +351,7 @@
     sent, kept = (
         call(
             functools.partial(project_kernel, i),
-            [part] + [along(part, m) for m in (1, 2, 3)] + [out_weight, weight_c],
+            [part] + [along(part, m) for m in ORDERS[i]] + [out_weight, weight_c],
             [((half, columns), dtype)] * 2,
             [pltpu.VMEM((4 * rows, width), bf16)],
             flops=effort * flops,
@@ -336,22 +373,15 @@
     (resting,) = call(
         rest_kernel, (skip_flags, hidden_state, cached_deltas), [((rows, columns), jnp.float32)]
     )
-    gate = gate_values[None, :]
-    results = ()
-    for p, part in enumerate(owned):
-        results = pl.pallas_call(
-            functools.partial(final_kernel, p),
-            in_specs=[pl.BlockSpec(memory_space=pltpu.VMEM)] * 3
-            + [pl.BlockSpec(memory_space=pl.ANY)] * len(results),
-            out_specs=[pl.BlockSpec(memory_space=pl.ANY)] * 2,
-            out_shape=[jax.ShapeDtypeStruct((rows, columns), jnp.float32)] * 2,
-            scratch_shapes=[pltpu.VMEM((half, columns), jnp.float32)] * 2
-            + [pltpu.SemaphoreType.DMA((2,))],
-            input_output_aliases={3 + i: i for i in range(len(results))},
-            compiler_params=pltpu.CompilerParams(vmem_limit_bytes=VMEM_BYTES),
-            cost_estimate=pl.CostEstimate(flops=0, bytes_accessed=0, transcendentals=0),
-        )(part, gate, resting, *results)
-    return tuple(results)
+    return tuple(
+        call(
+            final_kernel,
+            (*owned, gate_values[None, :], resting),
+            [((rows, columns), jnp.float32)] * 2,
+            [pltpu.VMEM((rows, columns), jnp.float32)] * 2 + [pltpu.SemaphoreType.DMA((8,))],
+            out_space=pl.ANY,
+        )
+    )
 
 
 def solution(mesh):
@@ -369,7 +399,7 @@
     def local(*args):
         sizes = tuple(mesh.shape[name] for name in ("seq", "wt", "head"))
         rows, features = args[0].shape
-        if sizes == (4, 2, 2) and rows % 32 == 0 and features % (2 * HEAD_DIM) == 0:
+        if sizes == (4, 2, 2) and rows % 32 == 0 and features % (2 * HEAD_DIM) == 0 and args[3].shape[1] % 256 == 0:
             return local_heads(*args)
         return local_general(*args)
 

time: 67.8 us -> 67.7 us (level)
    pallas_call x8 -> x10, Pallas kernels: 5.73 us -> 7.96 us  [call(): pl.pallas_call(kernel, in_specs=[pl.BlockSpec(memory_space=place) for pla...]
    pallas_call x2 -> x0, Pallas kernels: 1.9 us -> none  [local_heads(): pl.pallas_call(functools.partial(final_kernel, p), in_specs=[pl.BlockSpec...]
    ppermute x1, waiting for transfers between devices: 1.49 us -> 0.37 us  [local_heads(): sibling = lax.ppermute(joined, 'head', swap)]
  transfers between devices with their start and end apart: 16 -> 16, of which waited for: 6 -> 7; matrix products, arithmetic and copies ran while one was open for 0% -> 0% of each run, Pallas kernels for 5% -> 6%
where the time goes in v18:
time: 67.7 us; the launch traced here: 67.4 us
  waiting for transfers between devices  31.2 us (46%)
  starting transfers between devices  27.5 us (41%)
  Pallas kernels  7.96 us (12%)
  between operations  0.81 us (1%)
    ppermute x4, waiting for transfers between devices, local_heads(): moved.append(lax.ppermute(packed[k], ('seq', 'head'), pairs))  11.5 us
    ppermute x6, starting transfers between devices, along(): return lax.ppermute(shard, 'seq', [(z, z ^ m) for z in range(4)])  10.8 us
    ppermute x2, waiting for transfers between devices, local_heads(): owned.append(lax.ppermute(summed, ('seq', 'wt', 'head'), pairs))  9.83 us
    ppermute x6, waiting for transfers between devices, along(): return lax.ppermute(shard, 'seq', [(z, z ^ m) for z in range(4)])  9.42 us
    pallas_call x10, Pallas kernels, call(): pl.pallas_call(kernel, in_specs=[pl.BlockSpec(memory_space=place) for pla...  7.96 us
    ppermute x4, starting transfers between devices, local_heads(): moved.append(lax.ppermute(packed[k], ('seq', 'head'), pairs))  6.23 us
    ppermute x2, starting transfers between devices, local_heads(): owned.append(lax.ppermute(summed, ('seq', 'wt', 'head'), pairs))  5.87 us
    ppermute x1, starting transfers between devices, local_heads(): sibling = lax.ppermute(joined, 'head', swap)  2.43 us
  transfers between devices with their start and end apart: 16, of which 7 were waited for; matrix products, arithmetic and copies ran while one was open for 0% of the time, Pallas kernels for 6%

profile of v18, /device:TPU:2, one launch (start us, length us, event | category | flops | bytes accessed | tf_op | source)
XLA Modules:
  0.0 67.4 jit_solution(7317795336056163727)
XLA Ops:
  0.6 1.2 %shard_map.95 = (bf16[320,384]{1,0:T(8,128)(2,1)S(1)}, bf16[320,384]{1,0:T(8,128)(2,1)S(1)}, bf16[160,384]{1,0:T(8,128)(2,1)S(1)}, bf16[160,384]{1,0:T(8,128)(2,1)S(1)}) custom-call(bf16[160,768]{1,0:T(8,128)(2,1)} %queries.1, bf16[160,768]{1,0:T(8,128)(2,1)} %keys.1, bf16[160,768]{1,0:T(8,128)(2,1)} %values.1), custom_call_target="tpu_custom_call" | custom-call | tf_op jit(solution)/shard_map/pallas_call | solution.py:283
  1.9 0.1 collective-permute-start.5
  2.0 0.7 %collective-permute-start = (bf16[320,384]{1,0:T(8,128)(2,1)S(1)}, bf16[320,384]{1,0:T(8,128)(2,1)S(1)}, u32[]{:S(2)}, u32[]{:S(2)}) collective-permute-start(bf16[320,384]{1,0:T(8,128)(2,1)S(1)} %get-tuple-element.18), channel_id=1, source_target_pairs={{0,0},{1,4},{4,1},{5,5},{8,8},{9,12},{12,9},{13,13},{2,2},{3,6},{6... | collective-permute-start | bytes 737288 | tf_op jit(solution)/shard_map/ppermute | solution.py:328
  2.6 2.7 %collective-permute-start.1 = (bf16[320,384]{1,0:T(8,128)(2,1)S(1)}, bf16[320,384]{1,0:T(8,128)(2,1)S(1)}, u32[]{:S(2)}, u32[]{:S(2)}) collective-permute-start(bf16[320,384]{1,0:T(8,128)(2,1)S(1)} %get-tuple-element.19), channel_id=1, source_target_pairs={{0,8},{1,12},{4,9},{5,13},{8,0},{9,4},{12,1},{13,5},{2,10},{3,14},... | collective-permute-start | bytes 737288 | tf_op jit(solution)/shard_map/ppermute | solution.py:328
  5.3 2.9 %collective-permute-start.2 = (bf16[160,384]{1,0:T(8,128)(2,1)S(1)}, bf16[160,384]{1,0:T(8,128)(2,1)S(1)}, u32[]{:S(2)}, u32[]{:S(2)}) collective-permute-start(bf16[160,384]{1,0:T(8,128)(2,1)S(1)} %get-tuple-element.20), channel_id=1, source_target_pairs={{0,1},{1,5},{4,0},{5,4},{8,9},{9,13},{12,8},{13,12},{2,3},{3,7},{6... | collective-permute-start | bytes 368648 | tf_op jit(solution)/shard_map/ppermute | solution.py:328
  8.2 0.0 copy-start.1
  8.2 0.0 collective-permute-start.3
  8.2 4.5 %collective-permute-done.2.refs_2_ = bf16[160,384]{1,0:T(8,128)(2,1)S(1)} collective-permute-done((bf16[160,384]{1,0:T(8,128)(2,1)S(1)}, bf16[160,384]{1,0:T(8,128)(2,1)S(1)}, u32[]{:S(2)}, u32[]{:S(2)}) %collective-permute-start.2) | collective-permute-done | bytes 122912 | tf_op jit(solution)/shard_map/ppermute | solution.py:328
  12.7 7.1 %collective-permute-done.3.refs_3_ = bf16[160,384]{1,0:T(8,128)(2,1)S(1)} collective-permute-done((bf16[160,384]{1,0:T(8,128)(2,1)S(1)}, bf16[160,384]{1,0:T(8,128)(2,1)S(1)}, u32[]{:S(2)}, u32[]{:S(2)}) %collective-permute-start.3) | collective-permute-done | bytes 122912 | tf_op jit(solution)/shard_map/ppermute | solution.py:328
  19.7 0.0 collective-permute-done.refs_0_
  19.7 0.0 collective-permute-done.1.refs_1_
  19.8 2.4 %collective-permute-start.4 = (bf16[640,384]{1,0:T(8,128)(2,1)S(1)}, bf16[640,384]{1,0:T(8,128)(2,1)S(1)}, u32[]{:S(2)}, u32[]{:S(2)}) collective-permute-start(bf16[640,384]{1,0:T(8,128)(2,1)S(1)} %shard_map.97), channel_id=1, source_target_pairs={{0,1},{1,0},{2,3},{3,2},{4,5},{5,4},{6,7},{7,6},{8,9},{9,8},{10,11... | collective-permute-start | bytes 1474568 | tf_op jit(solution)/shard_map/ppermute | solution.py:330
  22.2 1.1 %shard_map.96 = (bf16[320,384]{1,0:T(8,128)(2,1)S(1)}, f32[320,384]{1,0:T(8,128)S(1)}, f32[320,384]{1,0:T(8,128)S(1)}, f32[320,384]{1,0:T(8,128)S(1)}) custom-call(bf16[320,384]{1,0:T(8,128)(2,1)S(1)} %collective-permute-done.refs_0_, bf16[320,384]{1,0:T(8,128)(2,1)S(1)} %collective-permute-done.1.refs_1_, ...), custom_call_target="tpu_custom_call" | custom-call | flops 157286400 | tf_op jit(solution)/shard_map/pallas_call | solution.py:283
  23.3 0.4 collective-permute-done.4.sibling
  23.7 0.0 collective-permute-done.5.refs_5_
  23.7 1.6 %shard_map.98 = (bf16[160,384]{1,0:T(8,128)(2,1)S(1)}, bf16[160,384]{1,0:T(8,128)(2,1)S(1)}) custom-call(bf16[320,384]{1,0:T(8,128)(2,1)S(1)} %get-tuple-element.22.query_all, f32[320,384]{1,0:T(8,128)S(1)} %get-tuple-element.23.weighted, f32[320,384]{1,0:T(8,128)S(1)} %get-tuple-element.24.peaks, f32[320,384]{1,0:T(8,128)S(1)} %get-tuple-element.25.totals, ...), custom_call_target="tpu_custom_call" | custom-call | flops 157286400 | tf_op jit(solution)/shard_map/pallas_call | solution.py:283
  25.3 3.5 %collective-permute-start.9 = (bf16[160,384]{1,0:T(8,128)(2,1)S(1)}, bf16[160,384]{1,0:T(8,128)(2,1)S(1)}, u32[]{:S(2)}, u32[]{:S(2)}) collective-permute-start(bf16[160,384]{1,0:T(8,128)(2,1)S(1)} %get-tuple-element.30.refs_0_), channel_id=1, source_target_pairs={{0,8},{4,12},{8,0},{12,4},{1,9},{5,13},{9,1},{13,5},{2,10},{6,14},... | collective-permute-start | bytes 368648 | tf_op jit(solution)/shard_map/ppermute | solution.py:269
  28.8 0.4 collective-permute-start.10
  29.3 0.2 collective-permute-start.11
  29.4 1.8 %collective-permute-start.6 = (bf16[160,384]{1,0:T(8,128)(2,1)S(1)}, bf16[160,384]{1,0:T(8,128)(2,1)S(1)}, u32[]{:S(2)}, u32[]{:S(2)}) collective-permute-start(bf16[160,384]{1,0:T(8,128)(2,1)S(1)} %get-tuple-element.28.refs_0_), channel_id=1, source_target_pairs={{0,4},{4,0},{8,12},{12,8},{1,5},{5,1},{9,13},{13,9},{2,6},{6,2},{1... | collective-permute-start | bytes 368648 | tf_op jit(solution)/shard_map/ppermute | solution.py:269
  31.3 2.0 %collective-permute-start.7 = (bf16[160,384]{1,0:T(8,128)(2,1)S(1)}, bf16[160,384]{1,0:T(8,128)(2,1)S(1)}, u32[]{:S(2)}, u32[]{:S(2)}) collective-permute-start(bf16[160,384]{1,0:T(8,128)(2,1)S(1)} %get-tuple-element.28.refs_0_), channel_id=1, source_target_pairs={{0,8},{4,12},{8,0},{12,4},{1,9},{5,13},{9,1},{13,5},{2,10},{6,14},... | collective-permute-start | bytes 368648 | tf_op jit(solution)/shard_map/ppermute | solution.py:269
  33.2 4.8 %collective-permute-done.9.refs_1_ = bf16[160,384]{1,0:T(8,128)(2,1)S(1)} collective-permute-done((bf16[160,384]{1,0:T(8,128)(2,1)S(1)}, bf16[160,384]{1,0:T(8,128)(2,1)S(1)}, u32[]{:S(2)}, u32[]{:S(2)}) %collective-permute-start.9) | collective-permute-done | bytes 122912 | tf_op jit(solution)/shard_map/ppermute | solution.py:269
  38.0 2.9 %collective-permute-start.8 = (bf16[160,384]{1,0:T(8,128)(2,1)S(1)}, bf16[160,384]{1,0:T(8,128)(2,1)S(1)}, u32[]{:S(2)}, u32[]{:S(2)}) collective-permute-start(bf16[160,384]{1,0:T(8,128)(2,1)S(1)} %get-tuple-element.28.refs_0_), channel_id=1, source_target_pairs={{0,12},{4,8},{8,4},{12,0},{1,13},{5,9},{9,5},{13,1},{2,14},{6,10},... | collective-permute-start | bytes 368648 | tf_op jit(solution)/shard_map/ppermute | solution.py:269
  40.9 0.0 collective-permute-done.10.refs_2_
  40.9 0.0 collective-permute-done.11.refs_3_
  40.9 0.0 copy-done.1
  40.9 0.9 %shard_map.100 = (bf16[80,1280]{1,0:T(8,128)(2,1)S(1)}, bf16[80,1280]{1,0:T(8,128)(2,1)S(1)}) custom-call(bf16[160,384]{1,0:T(8,128)(2,1)S(1)} %get-tuple-element.30.refs_0_, bf16[160,384]{1,0:T(8,128)(2,1)S(1)} %collective-permute-done.9.refs_1_, bf16[160,384]{1,0:T(8,128)(2,1)S(1)} %collective-permute-done.10.refs_2_, ...), custom_call_target="tpu_custom_call" | custom-call | flops 629145600 | tf_op jit(solution)/shard_map/pallas_call | solution.py:283
  41.8 0.6 collective-permute-start.12
  42.4 0.0 copy-start.4
  42.4 1.5 %collective-permute-start.14 = (bf16[80,1280]{1,0:T(8,128)(2,1)S(1)}, bf16[80,1280]{1,0:T(8,128)(2,1)S(1)}, u32[]{:S(2)}, u32[]{:S(2)}) collective-permute-start(bf16[80,1280]{1,0:T(8,128)(2,1)S(1)} %get-tuple-element.33), channel_id=1, source_target_pairs={{0,2},{2,0},{1,3},{3,1},{4,6},{6,4},{5,7},{7,5},{8,10},{10,8},{9,1... | collective-permute-start | bytes 614408 | tf_op jit(solution)/shard_map/ppermute | solution.py:364
  43.9 0.0 collective-permute-done.6.refs_1_
  43.9 4.6 %collective-permute-done.7.refs_2_ = bf16[160,384]{1,0:T(8,128)(2,1)S(1)} collective-permute-done((bf16[160,384]{1,0:T(8,128)(2,1)S(1)}, bf16[160,384]{1,0:T(8,128)(2,1)S(1)}, u32[]{:S(2)}, u32[]{:S(2)}) %collective-permute-start.7) | collective-permute-done | bytes 122912 | tf_op jit(solution)/shard_map/ppermute | solution.py:269
  48.5 0.0 collective-permute-done.8.refs_3_
  48.5 0.9 %shard_map.99 = (f32[80,1280]{1,0:T(8,128)S(1)}, f32[80,1280]{1,0:T(8,128)S(1)}) custom-call(bf16[160,384]{1,0:T(8,128)(2,1)S(1)} %get-tuple-element.28.refs_0_, bf16[160,384]{1,0:T(8,128)(2,1)S(1)} %collective-permute-done.6.refs_1_, bf16[160,384]{1,0:T(8,128)(2,1)S(1)} %collective-permute-done.7.refs_2_, ...), custom_call_target="tpu_custom_call" | custom-call | flops 5033164800 | tf_op jit(solution)/shard_map/pallas_call | solution.py:283
  49.5 0.0 copy-start.2
  49.5 0.0 collective-permute-done.12.arrived
  49.5 0.1 shard_map.101
  49.5 5.8 %collective-permute-start.13 = (bf16[80,1280]{1,0:T(8,128)(2,1)S(1)}, bf16[80,1280]{1,0:T(8,128)(2,1)S(1)}, u32[]{:S(2)}, u32[]{:S(2)}) collective-permute-start(bf16[80,1280]{1,0:T(8,128)(2,1)S(1)} %shard_map.101), channel_id=1, source_target_pairs={{0,0},{1,4},{2,8},{3,12},{4,1},{5,5},{6,9},{7,13},{8,2},{9,6},{10,... | collective-permute-start | bytes 614408 | tf_op jit(solution)/shard_map/ppermute | solution.py:372
  55.4 0.0 collective-permute-done.14.arrived
  55.4 0.1 collective-permute-start.15
  55.5 0.0 copy-done.4
  55.5 0.0 copy-done.3
  55.5 0.0 copy-done
  55.5 0.0 copy-done.2
  55.5 0.8 %shard_map.103.resting = f32[160,1280]{1,0:T(8,128)S(1)} custom-call(s32[4]{0:T(128)S(1)} %copy-done.3, f32[160,1280]{1,0:T(8,128)S(1)} %copy-done.2, f32[4,160,1280]{2,1,0:T(8,128)S(1)} %copy-done), custom_call_target="tpu_custom_call" | custom-call | tf_op jit(solution)/shard_map/pallas_call | solution.py:283
  56.3 9.2 %collective-permute-done.13.owned0 = bf16[80,1280]{1,0:T(8,128)(2,1)S(1)} collective-permute-done((bf16[80,1280]{1,0:T(8,128)(2,1)S(1)}, bf16[80,1280]{1,0:T(8,128)(2,1)S(1)}, u32[]{:S(2)}, u32[]{:S(2)}) %collective-permute-start.13) | collective-permute-done | bytes 204832 | tf_op jit(solution)/shard_map/ppermute | solution.py:372
  65.6 0.6 collective-permute-done.15.owned1
  66.1 1.3 %shard_map.104 = (f32[160,1280]{1,0:T(8,128)}, f32[160,1280]{1,0:T(8,128)}) custom-call(bf16[80,1280]{1,0:T(8,128)(2,1)S(1)} %collective-permute-done.13.owned0, bf16[80,1280]{1,0:T(8,128)(2,1)S(1)} %collective-permute-done.15.owned1, f32[1,1280]{1,0:T(1,128)S(1)} %broadcast_in_dim.3.gate, f32[160,1280]{1,0:T(8,128)S(1)} %shard_map.103.resting), custom_call_target="tpu_custom_call" | custom-call | tf_op jit(solution)/shard_map/pallas_call | solution.py:283
  (5 shorter events, 0.1 us)
Async XLA Ops:
  1.9 21.8 %collective-permute-start.5 = (bf16[768,1280]{1,0:T(8,128)(2,1)}, bf16[768,1280]{1,0:T(8,128)(2,1)S(1)}, u32[]{:S(2)}, u32[]{:S(2)}) collective-permute-start(bf16[768,1280]{1,0:T(8,128)(2,1)} %refs_4_.3), channel_id=1, source_target_pairs={{0,1},{1,0},{2,3},{3,2},{4,5},{5,4},{6,7},{7,6},{8,9},{9,8},{10,11... | collective-permute-start | bytes 5898248 | tf_op jit(solution)/shard_map/ppermute | solution.py:319
  2.0 17.8 %collective-permute-start = (bf16[320,384]{1,0:T(8,128)(2,1)S(1)}, bf16[320,384]{1,0:T(8,128)(2,1)S(1)}, u32[]{:S(2)}, u32[]{:S(2)}) collective-permute-start(bf16[320,384]{1,0:T(8,128)(2,1)S(1)} %get-tuple-element.18), channel_id=1, source_target_pairs={{0,0},{1,4},{4,1},{5,5},{8,8},{9,12},{12,9},{13,13},{2,2},{3,6},{6... | collective-permute-start | bytes 737288 | tf_op jit(solution)/shard_map/ppermute | solution.py:328
  2.6 17.1 %collective-permute-start.1 = (bf16[320,384]{1,0:T(8,128)(2,1)S(1)}, bf16[320,384]{1,0:T(8,128)(2,1)S(1)}, u32[]{:S(2)}, u32[]{:S(2)}) collective-permute-start(bf16[320,384]{1,0:T(8,128)(2,1)S(1)} %get-tuple-element.19), channel_id=1, source_target_pairs={{0,8},{1,12},{4,9},{5,13},{8,0},{9,4},{12,1},{13,5},{2,10},{3,14},... | collective-permute-start | bytes 737288 | tf_op jit(solution)/shard_map/ppermute | solution.py:328
  5.3 7.4 %collective-permute-start.2 = (bf16[160,384]{1,0:T(8,128)(2,1)S(1)}, bf16[160,384]{1,0:T(8,128)(2,1)S(1)}, u32[]{:S(2)}, u32[]{:S(2)}) collective-permute-start(bf16[160,384]{1,0:T(8,128)(2,1)S(1)} %get-tuple-element.20), channel_id=1, source_target_pairs={{0,1},{1,5},{4,0},{5,4},{8,9},{9,13},{12,8},{13,12},{2,3},{3,7},{6... | collective-permute-start | bytes 368648 | tf_op jit(solution)/shard_map/ppermute | solution.py:328
  8.2 32.7 %copy-start.1 = (bf16[768,1280]{1,0:T(8,128)(2,1)S(1)}, bf16[768,1280]{1,0:T(8,128)(2,1)}, u32[]{:S(2)}) copy-start(bf16[768,1280]{1,0:T(8,128)(2,1)} %refs_4_.3) | copy-start | bytes 5898244
  8.2 11.5 %collective-permute-start.3 = (bf16[160,384]{1,0:T(8,128)(2,1)S(1)}, bf16[160,384]{1,0:T(8,128)(2,1)S(1)}, u32[]{:S(2)}, u32[]{:S(2)}) collective-permute-start(bf16[160,384]{1,0:T(8,128)(2,1)S(1)} %get-tuple-element.21), channel_id=1, source_target_pairs={{0,9},{1,13},{4,8},{5,12},{8,1},{9,5},{12,0},{13,4},{2,11},{3,15},... | collective-permute-start | bytes 368648 | tf_op jit(solution)/shard_map/ppermute | solution.py:328
  19.8 3.9 %collective-permute-start.4 = (bf16[640,384]{1,0:T(8,128)(2,1)S(1)}, bf16[640,384]{1,0:T(8,128)(2,1)S(1)}, u32[]{:S(2)}, u32[]{:S(2)}) collective-permute-start(bf16[640,384]{1,0:T(8,128)(2,1)S(1)} %shard_map.97), channel_id=1, source_target_pairs={{0,1},{1,0},{2,3},{3,2},{4,5},{5,4},{6,7},{7,6},{8,9},{9,8},{10,11... | collective-permute-start | bytes 1474568 | tf_op jit(solution)/shard_map/ppermute | solution.py:330
  25.3 12.7 %collective-permute-start.9 = (bf16[160,384]{1,0:T(8,128)(2,1)S(1)}, bf16[160,384]{1,0:T(8,128)(2,1)S(1)}, u32[]{:S(2)}, u32[]{:S(2)}) collective-permute-start(bf16[160,384]{1,0:T(8,128)(2,1)S(1)} %get-tuple-element.30.refs_0_), channel_id=1, source_target_pairs={{0,8},{4,12},{8,0},{12,4},{1,9},{5,13},{9,1},{13,5},{2,10},{6,14},... | collective-permute-start | bytes 368648 | tf_op jit(solution)/shard_map/ppermute | solution.py:269
  28.8 12.1 %collective-permute-start.10 = (bf16[160,384]{1,0:T(8,128)(2,1)S(1)}, bf16[160,384]{1,0:T(8,128)(2,1)S(1)}, u32[]{:S(2)}, u32[]{:S(2)}) collective-permute-start(bf16[160,384]{1,0:T(8,128)(2,1)S(1)} %get-tuple-element.30.refs_0_), channel_id=1, source_target_pairs={{0,12},{4,8},{8,4},{12,0},{1,13},{5,9},{9,5},{13,1},{2,14},{6,10},... | collective-permute-start | bytes 368648 | tf_op jit(solution)/shard_map/ppermute | solution.py:269
  29.3 11.6 %collective-permute-start.11 = (bf16[160,384]{1,0:T(8,128)(2,1)S(1)}, bf16[160,384]{1,0:T(8,128)(2,1)S(1)}, u32[]{:S(2)}, u32[]{:S(2)}) collective-permute-start(bf16[160,384]{1,0:T(8,128)(2,1)S(1)} %get-tuple-element.30.refs_0_), channel_id=1, source_target_pairs={{0,4},{4,0},{8,12},{12,8},{1,5},{5,1},{9,13},{13,9},{2,6},{6,2},{1... | collective-permute-start | bytes 368648 | tf_op jit(solution)/shard_map/ppermute | solution.py:269
  29.4 14.4 %collective-permute-start.6 = (bf16[160,384]{1,0:T(8,128)(2,1)S(1)}, bf16[160,384]{1,0:T(8,128)(2,1)S(1)}, u32[]{:S(2)}, u32[]{:S(2)}) collective-permute-start(bf16[160,384]{1,0:T(8,128)(2,1)S(1)} %get-tuple-element.28.refs_0_), channel_id=1, source_target_pairs={{0,4},{4,0},{8,12},{12,8},{1,5},{5,1},{9,13},{13,9},{2,6},{6,2},{1... | collective-permute-start | bytes 368648 | tf_op jit(solution)/shard_map/ppermute | solution.py:269
  31.3 17.3 %collective-permute-start.7 = (bf16[160,384]{1,0:T(8,128)(2,1)S(1)}, bf16[160,384]{1,0:T(8,128)(2,1)S(1)}, u32[]{:S(2)}, u32[]{:S(2)}) collective-permute-start(bf16[160,384]{1,0:T(8,128)(2,1)S(1)} %get-tuple-element.28.refs_0_), channel_id=1, source_target_pairs={{0,8},{4,12},{8,0},{12,4},{1,9},{5,13},{9,1},{13,5},{2,10},{6,14},... | collective-permute-start | bytes 368648 | tf_op jit(solution)/shard_map/ppermute | solution.py:269
  38.0 10.5 %collective-permute-start.8 = (bf16[160,384]{1,0:T(8,128)(2,1)S(1)}, bf16[160,384]{1,0:T(8,128)(2,1)S(1)}, u32[]{:S(2)}, u32[]{:S(2)}) collective-permute-start(bf16[160,384]{1,0:T(8,128)(2,1)S(1)} %get-tuple-element.28.refs_0_), channel_id=1, source_target_pairs={{0,12},{4,8},{8,4},{12,0},{1,13},{5,9},{9,5},{13,1},{2,14},{6,10},... | collective-permute-start | bytes 368648 | tf_op jit(solution)/shard_map/ppermute | solution.py:269
  41.8 7.7 %collective-permute-start.12 = (bf16[80,1280]{1,0:T(8,128)(2,1)S(1)}, bf16[80,1280]{1,0:T(8,128)(2,1)S(1)}, u32[]{:S(2)}, u32[]{:S(2)}) collective-permute-start(bf16[80,1280]{1,0:T(8,128)(2,1)S(1)} %get-tuple-element.31), channel_id=1, source_target_pairs={{0,2},{2,0},{1,3},{3,1},{4,6},{6,4},{5,7},{7,5},{8,10},{10,8},{9,1... | collective-permute-start | bytes 614408 | tf_op jit(solution)/shard_map/ppermute | solution.py:364
  42.4 13.1 %copy-start.4 = (f32[1280]{0:T(1024)S(1)}, f32[1280]{0:T(1024)}, u32[]{:S(2)}) copy-start(f32[1280]{0:T(1024)} %param.12) | copy-start | bytes 15364
  42.4 13.1 %copy-start.3 = (s32[4]{0:T(128)S(1)}, s32[4]{0:T(128)}, u32[]{:S(2)}) copy-start(s32[4]{0:T(128)} %flags.1) | copy-start | bytes 52
  42.4 13.0 %collective-permute-start.14 = (bf16[80,1280]{1,0:T(8,128)(2,1)S(1)}, bf16[80,1280]{1,0:T(8,128)(2,1)S(1)}, u32[]{:S(2)}, u32[]{:S(2)}) collective-permute-start(bf16[80,1280]{1,0:T(8,128)(2,1)S(1)} %get-tuple-element.33), channel_id=1, source_target_pairs={{0,2},{2,0},{1,3},{3,1},{4,6},{6,4},{5,7},{7,5},{8,10},{10,8},{9,1... | collective-permute-start | bytes 614408 | tf_op jit(solution)/shard_map/ppermute | solution.py:364
  48.5 7.0 %copy-start = (f32[4,160,1280]{2,1,0:T(8,128)S(1)}, f32[4,160,1280]{2,1,0:T(8,128)}, u32[]{:S(2)}) copy-start(f32[4,160,1280]{2,1,0:T(8,128)} %cached.1) | copy-start | bytes 9830404
  49.5 6.1 %copy-start.2 = (f32[160,1280]{1,0:T(8,128)S(1)}, f32[160,1280]{1,0:T(8,128)}, u32[]{:S(2)}) copy-start(f32[160,1280]{1,0:T(8,128)} %hidden.1) | copy-start | bytes 2457604
  49.5 16.0 %collective-permute-start.13 = (bf16[80,1280]{1,0:T(8,128)(2,1)S(1)}, bf16[80,1280]{1,0:T(8,128)(2,1)S(1)}, u32[]{:S(2)}, u32[]{:S(2)}) collective-permute-start(bf16[80,1280]{1,0:T(8,128)(2,1)S(1)} %shard_map.101), channel_id=1, source_target_pairs={{0,0},{1,4},{2,8},{3,12},{4,1},{5,5},{6,9},{7,13},{8,2},{9,6},{10,... | collective-permute-start | bytes 614408 | tf_op jit(solution)/shard_map/ppermute | solution.py:372
  55.4 10.7 %collective-permute-start.15 = (bf16[80,1280]{1,0:T(8,128)(2,1)S(1)}, bf16[80,1280]{1,0:T(8,128)(2,1)S(1)}, u32[]{:S(2)}, u32[]{:S(2)}) collective-permute-start(bf16[80,1280]{1,0:T(8,128)(2,1)S(1)} %shard_map.102), channel_id=1, source_target_pairs={{0,8},{1,12},{2,0},{3,4},{4,9},{5,13},{6,1},{7,5},{8,10},{9,14},{1... | collective-permute-start | bytes 614408 | tf_op jit(solution)/shard_map/ppermute | solution.py:372

commit v19 on v16

--- a/solution.py
+++ b/solution.py
@@ -130,7 +130,7 @@
 
 def attention_kernel(*refs):
     blocks, sibling = refs[:4], refs[4]
-    sent, kept, key_all, value_all, query_all = refs[5:]
+    sent, kept0, kept1, key_all, value_all, query_all = refs[5:]
     rows = sent.shape[0]
     half = rows // 2
     for k in range(4):
@@ -142,9 +142,9 @@
     zh, _ = bits()
     x = lax.axis_index("wt")
     for k in range(2):
-        for part in range(2):
-            at = rows + flip(x, part == 0) * half
-            to = (part * 2 + flip(zh, k)) * half
+        high = flip(zh, k)
+        for at, to in ((1 - x, high), (x, 2 + lax.rem(high + x, 2))):
+            at, to = rows + at * half, to * half
             query_all[pl.ds(pl.multiple_of(to, 16), half), :] = blocks[k][
                 pl.ds(pl.multiple_of(at, 16), half), :
             ]
@@ -164,7 +164,8 @@
         )
         result = (result / total).astype(sent.dtype)
         sent[:, columns] = result[:rows]
-        kept[:, columns] = result[rows:]
+        kept0[:, columns] = result[rows : rows + half]
+        kept1[:, columns] = result[rows + half :]
 
 
 def multiply(shards, weight, weight_c, held):
@@ -188,22 +189,26 @@
     return total
 
 
-def project_kernel(kept, *refs):
+def sent_kernel(*refs):
     shards, (weight, weight_c, out0, out1, held) = refs[:4], refs[4:]
     total = multiply(shards, weight, weight_c, held)
     half = out0.shape[0]
     x = lax.axis_index("wt")
-    for low in range(2):
-        part = total[low * half : (low + 1) * half].astype(out0.dtype)
-        first = flip(x, low) == 1 - kept
-
-        @pl.when(first)
+    for high in range(2):
+        part = total[high * half : (high + 1) * half].astype(out0.dtype)
+
+        @pl.when(x != high)
         def _():
             out0[...] = part
 
-        @pl.when(jnp.logical_not(first))
+        @pl.when(x == high)
         def _():
             out1[...] = part
+
+
+def kept_kernel(*refs):
+    shards, (weight, weight_c, out, held) = refs[:4], refs[4:]
+    out[...] = multiply(shards, weight, weight_c, held)
 
 
 def add_kernel(kept, arrived, out):
@@ -300,7 +305,7 @@
     parts = call(
         attention_kernel,
         moved + [sibling],
-        [((rows, width), bf16)] * 2,
+        [((rows, width), bf16)] + [((rows // 2, width), bf16)] * 2,
         [
             pltpu.VMEM((4 * rows, width), bf16),
             pltpu.VMEM((4 * rows, width), bf16),
@@ -311,21 +316,29 @@
 
     half = rows // 2
     flops = 4 * rows * depth * columns
-    sent, kept = (
-        call(
-            functools.partial(project_kernel, i),
-            [part] + [along(part, m) for m in (1, 2, 3)] + [out_weight, weight_c],
-            [((half, columns), dtype)] * 2,
-            [pltpu.VMEM((4 * rows, width), bf16)],
-            flops=effort * flops,
-        )
-        for i, (part, dtype, effort) in enumerate(((parts[0], bf16, 1), (parts[1], jnp.float32, 8)))
-    )
+    weights = [out_weight, weight_c]
+    shards = [[part] + [along(part, m) for m in (1, 2, 3)] for part in parts[:2]]
+    sent = call(
+        sent_kernel,
+        shards[0] + weights,
+        [((half, columns), bf16)] * 2,
+        [pltpu.VMEM((4 * rows, width), bf16)],
+        flops=flops,
+    )
+    part, _ = lax.optimization_barrier((parts[2], sent[0]))
+    shards.append([part] + [along(part, m) for m in (1, 2, 3)])
 
     owned = []
     for p in range(2):
         arrived = lax.ppermute(sent[p], "wt", swap)
-        (summed,) = call(add_kernel, (kept[p], arrived), [((half, columns), bf16)])
+        (kept,) = call(
+            kept_kernel,
+            shards[1 + p] + weights,
+            [((half, columns), jnp.float32)],
+            [pltpu.VMEM((4 * half, width), bf16)],
+            flops=flops,
+        )
+        (summed,) = call(add_kernel, (kept, arrived), [((half, columns), bf16)])
         pairs = []
         for zz in range(4):
             for xx in range(2):

time: 67.8 us -> 71.7 us (1.058)
  waiting for transfers between devices: 31.7 us -> 34.5 us
  Pallas kernels: 7.63 us -> 8.38 us
    ppermute x6 -> x9, waiting for transfers between devices: 9.41 us -> 14.1 us  [along(): return lax.ppermute(shard, 'seq', [(z, z ^ m) for z in range(4)])]
    ppermute x6 -> x9, starting transfers between devices: 10.8 us -> 13.3 us  [along(): return lax.ppermute(shard, 'seq', [(z, z ^ m) for z in range(4)])]
    ppermute x2, starting transfers between devices: 5.86 us -> 3.9 us  [local_heads(): owned.append(lax.ppermute(summed, ('seq', 'wt', 'head'), pairs))]
    ppermute x2, waiting for transfers between devices: 9.24 us -> 7.56 us  [local_heads(): owned.append(lax.ppermute(summed, ('seq', 'wt', 'head'), pairs))]
    pallas_call x8 -> x9, Pallas kernels: 5.73 us -> 6.48 us  [call(): pl.pallas_call(kernel, in_specs=[pl.BlockSpec(memory_space=place) for pla...]
  transfers between devices with their start and end apart: 16 -> 19, of which waited for: 6 -> 10; matrix products, arithmetic and copies ran while one was open for 0% -> 0% of each run, Pallas kernels for 5% -> 5%
where the time goes in v19:
time: 71.7 us; the launch traced here: 71.5 us
  waiting for transfers between devices  34.5 us (48%)
  starting transfers between devices  27.8 us (39%)
  Pallas kernels  8.38 us (12%)
  between operations  0.82 us (1%)
    ppermute x9, waiting for transfers between devices, along(): return lax.ppermute(shard, 'seq', [(z, z ^ m) for z in range(4)])  14.1 us
    ppermute x9, starting transfers between devices, along(): return lax.ppermute(shard, 'seq', [(z, z ^ m) for z in range(4)])  13.3 us
    ppermute x4, waiting for transfers between devices, local_heads(): moved.append(lax.ppermute(packed[k], ('seq', 'head'), pairs))  11.4 us
    ppermute x2, waiting for transfers between devices, local_heads(): owned.append(lax.ppermute(summed, ('seq', 'wt', 'head'), pairs))  7.56 us
    pallas_call x9, Pallas kernels, call(): pl.pallas_call(kernel, in_specs=[pl.BlockSpec(memory_space=place) for pla...  6.48 us
    ppermute x4, starting transfers between devices, local_heads(): moved.append(lax.ppermute(packed[k], ('seq', 'head'), pairs))  6.24 us
    ppermute x2, starting transfers between devices, local_heads(): owned.append(lax.ppermute(summed, ('seq', 'wt', 'head'), pairs))  3.9 us
    ppermute x1, starting transfers between devices, local_heads(): sibling = lax.ppermute(joined, 'head', swap)  2.14 us
  transfers between devices with their start and end apart: 19, of which 10 were waited for; matrix products, arithmetic and copies ran while one was open for 0% of the time, Pallas kernels for 5%

profile of v19, /device:TPU:2, one launch (start us, length us, event | category | flops | bytes accessed | tf_op | source)
XLA Modules:
  0.0 71.5 jit_solution(9559910278768154318)
XLA Ops:
  0.6 0.0 copy-start
  0.6 1.4 %shard_map.95 = (bf16[320,384]{1,0:T(8,128)(2,1)S(1)}, bf16[320,384]{1,0:T(8,128)(2,1)S(1)}, bf16[160,384]{1,0:T(8,128)(2,1)S(1)}, bf16[160,384]{1,0:T(8,128)(2,1)S(1)}) custom-call(bf16[160,768]{1,0:T(8,128)(2,1)} %queries.1, bf16[160,768]{1,0:T(8,128)(2,1)} %keys.1, bf16[160,768]{1,0:T(8,128)(2,1)} %values.1), custom_call_target="tpu_custom_call" | custom-call | tf_op jit(solution)/shard_map/pallas_call | solution.py:256
  2.0 0.1 collective-permute-start.5
  2.1 2.7 %collective-permute-start.1 = (bf16[320,384]{1,0:T(8,128)(2,1)S(1)}, bf16[320,384]{1,0:T(8,128)(2,1)S(1)}, u32[]{:S(2)}, u32[]{:S(2)}) collective-permute-start(bf16[320,384]{1,0:T(8,128)(2,1)S(1)} %get-tuple-element.17), channel_id=1, source_target_pairs={{0,8},{1,12},{4,9},{5,13},{8,0},{9,4},{12,1},{13,5},{2,10},{3,14},... | collective-permute-start | bytes 737288 | tf_op jit(solution)/shard_map/ppermute | solution.py:301
  4.8 0.7 collective-permute-start
  5.4 2.4 %collective-permute-start.2 = (bf16[160,384]{1,0:T(8,128)(2,1)S(1)}, bf16[160,384]{1,0:T(8,128)(2,1)S(1)}, u32[]{:S(2)}, u32[]{:S(2)}) collective-permute-start(bf16[160,384]{1,0:T(8,128)(2,1)S(1)} %get-tuple-element.18), channel_id=1, source_target_pairs={{0,1},{1,5},{4,0},{5,4},{8,9},{9,13},{12,8},{13,12},{2,3},{3,7},{6... | collective-permute-start | bytes 368648 | tf_op jit(solution)/shard_map/ppermute | solution.py:301
  7.9 0.5 collective-permute-start.3
  8.4 10.8 %collective-permute-done.2.refs_2_ = bf16[160,384]{1,0:T(8,128)(2,1)S(1)} collective-permute-done((bf16[160,384]{1,0:T(8,128)(2,1)S(1)}, bf16[160,384]{1,0:T(8,128)(2,1)S(1)}, u32[]{:S(2)}, u32[]{:S(2)}) %collective-permute-start.2) | collective-permute-done | bytes 122912 | tf_op jit(solution)/shard_map/ppermute | solution.py:301
  19.2 0.0 collective-permute-done.3.refs_3_
  19.2 0.6 collective-permute-done.1.refs_1_
  19.7 0.0 collective-permute-done.refs_0_
  19.8 2.1 %collective-permute-start.4 = (bf16[640,384]{1,0:T(8,128)(2,1)S(1)}, bf16[640,384]{1,0:T(8,128)(2,1)S(1)}, u32[]{:S(2)}, u32[]{:S(2)}) collective-permute-start(bf16[640,384]{1,0:T(8,128)(2,1)S(1)} %shard_map.96), channel_id=1, source_target_pairs={{0,1},{1,0},{2,3},{3,2},{4,5},{5,4},{6,7},{7,6},{8,9},{9,8},{10,11... | collective-permute-start | bytes 1474568 | tf_op jit(solution)/shard_map/ppermute | solution.py:303
  21.9 1.5 %collective-permute-done.4.refs_4_ = bf16[640,384]{1,0:T(8,128)(2,1)S(1)} collective-permute-done((bf16[640,384]{1,0:T(8,128)(2,1)S(1)}, bf16[640,384]{1,0:T(8,128)(2,1)S(1)}, u32[]{:S(2)}, u32[]{:S(2)}) %collective-permute-start.4) | collective-permute-done | bytes 491552 | tf_op jit(solution)/shard_map/ppermute | solution.py:303
  23.4 0.0 collective-permute-done.5.refs_5_
  23.4 1.6 %shard_map.97 = (bf16[160,384]{1,0:T(8,128)(2,1)S(1)}, bf16[80,384]{1,0:T(8,128)(2,1)S(1)}, bf16[80,384]{1,0:T(8,128)(2,1)S(1)}) custom-call(bf16[320,384]{1,0:T(8,128)(2,1)S(1)} %collective-permute-done.refs_0_, bf16[320,384]{1,0:T(8,128)(2,1)S(1)} %collective-permute-done.1.refs_1_, bf16[160,384]{1,0:T(8,128)(2,1)S(1)} %collective-permute-done.2.refs_2_, ...), custom_call_target="tpu_custom_call" | custom-call | flops 314572800 | tf_op jit(solution)/shard_map/pallas_call | solution.py:256
  25.0 3.7 %collective-permute-start.8 = (bf16[160,384]{1,0:T(8,128)(2,1)S(1)}, bf16[160,384]{1,0:T(8,128)(2,1)S(1)}, u32[]{:S(2)}, u32[]{:S(2)}) collective-permute-start(bf16[160,384]{1,0:T(8,128)(2,1)S(1)} %get-tuple-element.23.refs_0_), channel_id=1, source_target_pairs={{0,12},{4,8},{8,4},{12,0},{1,13},{5,9},{9,5},{13,1},{2,14},{6,10},... | collective-permute-start | bytes 368648 | tf_op jit(solution)/shard_map/ppermute | solution.py:242
  28.7 0.0 collective-permute-start.7
  28.7 0.8 %collective-permute-start.6 = (bf16[160,384]{1,0:T(8,128)(2,1)S(1)}, bf16[160,384]{1,0:T(8,128)(2,1)S(1)}, u32[]{:S(2)}, u32[]{:S(2)}) collective-permute-start(bf16[160,384]{1,0:T(8,128)(2,1)S(1)} %get-tuple-element.23.refs_0_), channel_id=1, source_target_pairs={{0,4},{4,0},{8,12},{12,8},{1,5},{5,1},{9,13},{13,9},{2,6},{6,2},{1... | collective-permute-start | bytes 368648 | tf_op jit(solution)/shard_map/ppermute | solution.py:242
  29.5 3.6 %collective-permute-done.8.refs_3_ = bf16[160,384]{1,0:T(8,128)(2,1)S(1)} collective-permute-done((bf16[160,384]{1,0:T(8,128)(2,1)S(1)}, bf16[160,384]{1,0:T(8,128)(2,1)S(1)}, u32[]{:S(2)}, u32[]{:S(2)}) %collective-permute-start.8) | collective-permute-done | bytes 122912 | tf_op jit(solution)/shard_map/ppermute | solution.py:242
  33.2 5.9 %collective-permute-done.7.refs_2_ = bf16[160,384]{1,0:T(8,128)(2,1)S(1)} collective-permute-done((bf16[160,384]{1,0:T(8,128)(2,1)S(1)}, bf16[160,384]{1,0:T(8,128)(2,1)S(1)}, u32[]{:S(2)}, u32[]{:S(2)}) %collective-permute-start.7) | collective-permute-done | bytes 122912 | tf_op jit(solution)/shard_map/ppermute | solution.py:242
  39.0 0.0 collective-permute-done.6.refs_1_
  39.0 0.9 %shard_map.98 = (bf16[80,1280]{1,0:T(8,128)(2,1)S(1)}, bf16[80,1280]{1,0:T(8,128)(2,1)S(1)}) custom-call(bf16[160,384]{1,0:T(8,128)(2,1)S(1)} %get-tuple-element.23.refs_0_, bf16[160,384]{1,0:T(8,128)(2,1)S(1)} %collective-permute-done.6.refs_1_, bf16[160,384]{1,0:T(8,128)(2,1)S(1)} %collective-permute-done.7.refs_2_, ...), custom_call_target="tpu_custom_call" | custom-call | flops 629145600 | tf_op jit(solution)/shard_map/pallas_call | solution.py:256
  39.9 0.6 collective-permute-start.17
  40.5 1.5 %collective-permute-start.12 = (bf16[80,1280]{1,0:T(8,128)(2,1)S(1)}, bf16[80,1280]{1,0:T(8,128)(2,1)S(1)}, u32[]{:S(2)}, u32[]{:S(2)}) collective-permute-start(bf16[80,1280]{1,0:T(8,128)(2,1)S(1)} %get-tuple-element.26), channel_id=1, source_target_pairs={{0,2},{2,0},{1,3},{3,1},{4,6},{6,4},{5,7},{7,5},{8,10},{10,8},{9,1... | collective-permute-start | bytes 614408 | tf_op jit(solution)/shard_map/ppermute | solution.py:333
  42.0 2.7 %collective-permute-start.16 = (bf16[80,384]{1,0:T(8,128)(2,1)S(1)}, bf16[80,384]{1,0:T(8,128)(2,1)S(1)}, u32[]{:S(2)}, u32[]{:S(2)}) collective-permute-start(bf16[80,384]{1,0:T(8,128)(2,1)S(1)} %get-tuple-element.27.refs_0_), channel_id=1, source_target_pairs={{0,12},{4,8},{8,4},{12,0},{1,13},{5,9},{9,5},{13,1},{2,14},{6,10},... | collective-permute-start | bytes 184328 | tf_op jit(solution)/shard_map/ppermute | solution.py:242
  44.7 0.0 collective-permute-start.15
  44.7 1.7 %collective-permute-start.14 = (bf16[80,384]{1,0:T(8,128)(2,1)S(1)}, bf16[80,384]{1,0:T(8,128)(2,1)S(1)}, u32[]{:S(2)}, u32[]{:S(2)}) collective-permute-start(bf16[80,384]{1,0:T(8,128)(2,1)S(1)} %get-tuple-element.27.refs_0_), channel_id=1, source_target_pairs={{0,4},{4,0},{8,12},{12,8},{1,5},{5,1},{9,13},{13,9},{2,6},{6,2},{1... | collective-permute-start | bytes 184328 | tf_op jit(solution)/shard_map/ppermute | solution.py:242
  46.4 1.9 %collective-permute-done.16.refs_3_ = bf16[80,384]{1,0:T(8,128)(2,1)S(1)} collective-permute-done((bf16[80,384]{1,0:T(8,128)(2,1)S(1)}, bf16[80,384]{1,0:T(8,128)(2,1)S(1)}, u32[]{:S(2)}, u32[]{:S(2)}) %collective-permute-start.16) | collective-permute-done | bytes 61472 | tf_op jit(solution)/shard_map/ppermute | solution.py:242
  48.3 2.5 %collective-permute-start.11 = (bf16[80,384]{1,0:T(8,128)(2,1)S(1)}, bf16[80,384]{1,0:T(8,128)(2,1)S(1)}, u32[]{:S(2)}, u32[]{:S(2)}) collective-permute-start(bf16[80,384]{1,0:T(8,128)(2,1)S(1)} %get-tuple-element.25.refs_0_), channel_id=1, source_target_pairs={{0,12},{4,8},{8,4},{12,0},{1,13},{5,9},{9,5},{13,1},{2,14},{6,10},... | collective-permute-start | bytes 184328 | tf_op jit(solution)/shard_map/ppermute | solution.py:242
  50.8 0.2 collective-permute-done.15.refs_2_
  51.0 0.0 collective-permute-start.10
  51.0 0.0 collective-permute-done.14.refs_1_
  51.0 2.0 %collective-permute-start.9 = (bf16[80,384]{1,0:T(8,128)(2,1)S(1)}, bf16[80,384]{1,0:T(8,128)(2,1)S(1)}, u32[]{:S(2)}, u32[]{:S(2)}) collective-permute-start(bf16[80,384]{1,0:T(8,128)(2,1)S(1)} %get-tuple-element.25.refs_0_), channel_id=1, source_target_pairs={{0,4},{4,0},{8,12},{12,8},{1,5},{5,1},{9,13},{13,9},{2,6},{6,2},{1... | collective-permute-start | bytes 184328 | tf_op jit(solution)/shard_map/ppermute | solution.py:242
  53.0 0.8 %shard_map.102.kept = f32[80,1280]{1,0:T(8,128)S(1)} custom-call(bf16[80,384]{1,0:T(8,128)(2,1)S(1)} %get-tuple-element.27.refs_0_, bf16[80,384]{1,0:T(8,128)(2,1)S(1)} %collective-permute-done.14.refs_1_, bf16[80,384]{1,0:T(8,128)(2,1)S(1)} %collective-permute-done.15.refs_2_, bf16[80,384]{1,0:T(8,128)(2,1)S(1)} %collective-permute-done.16.refs_3_, ...), custom_call_target="tpu_custom_call" | custom-call | flops 629145600 | tf_op jit(solution)/shard_map/pallas_call | solution.py:256
  53.8 0.0 copy-start.3
  53.8 0.9 %collective-permute-done.11.refs_3_ = bf16[80,384]{1,0:T(8,128)(2,1)S(1)} collective-permute-done((bf16[80,384]{1,0:T(8,128)(2,1)S(1)}, bf16[80,384]{1,0:T(8,128)(2,1)S(1)}, u32[]{:S(2)}, u32[]{:S(2)}) %collective-permute-start.11) | collective-permute-done | bytes 61472 | tf_op jit(solution)/shard_map/ppermute | solution.py:242
  54.8 1.5 %collective-permute-done.10.refs_2_ = bf16[80,384]{1,0:T(8,128)(2,1)S(1)} collective-permute-done((bf16[80,384]{1,0:T(8,128)(2,1)S(1)}, bf16[80,384]{1,0:T(8,128)(2,1)S(1)}, u32[]{:S(2)}, u32[]{:S(2)}) %collective-permute-start.10) | collective-permute-done | bytes 61472 | tf_op jit(solution)/shard_map/ppermute | solution.py:242
  56.3 0.0 collective-permute-done.9.refs_1_
  56.3 0.8 %shard_map.99.kept = f32[80,1280]{1,0:T(8,128)S(1)} custom-call(bf16[80,384]{1,0:T(8,128)(2,1)S(1)} %get-tuple-element.25.refs_0_, bf16[80,384]{1,0:T(8,128)(2,1)S(1)} %collective-permute-done.9.refs_1_, bf16[80,384]{1,0:T(8,128)(2,1)S(1)} %collective-permute-done.10.refs_2_, bf16[80,384]{1,0:T(8,128)(2,1)S(1)} %collective-permute-done.11.refs_3_, ...), custom_call_target="tpu_custom_call" | custom-call | flops 629145600 | tf_op jit(solution)/shard_map/pallas_call | solution.py:256
  57.2 0.0 collective-permute-done.17.arrived
  57.2 3.8 %collective-permute-start.18 = (bf16[80,1280]{1,0:T(8,128)(2,1)S(1)}, bf16[80,1280]{1,0:T(8,128)(2,1)S(1)}, u32[]{:S(2)}, u32[]{:S(2)}) collective-permute-start(bf16[80,1280]{1,0:T(8,128)(2,1)S(1)} %shard_map.103), channel_id=1, source_target_pairs={{0,0},{1,4},{2,8},{3,12},{4,1},{5,5},{6,9},{7,13},{8,2},{9,6},{10,... | collective-permute-start | bytes 614408 | tf_op jit(solution)/shard_map/ppermute | solution.py:348
  61.1 0.0 collective-permute-done.12.arrived
  61.1 0.1 collective-permute-start.13
  61.2 0.8 %shard_map.101.resting = f32[160,1280]{1,0:T(8,128)S(1)} custom-call(s32[4]{0:T(128)S(1)} %copy-done.3, f32[160,1280]{1,0:T(8,128)S(1)} %copy-done.2, f32[4,160,1280]{2,1,0:T(8,128)S(1)} %copy-done.1), custom_call_target="tpu_custom_call" | custom-call | tf_op jit(solution)/shard_map/pallas_call | solution.py:256
  62.0 7.6 %collective-permute-done.18.owned = bf16[80,1280]{1,0:T(8,128)(2,1)S(1)} collective-permute-done((bf16[80,1280]{1,0:T(8,128)(2,1)S(1)}, bf16[80,1280]{1,0:T(8,128)(2,1)S(1)}, u32[]{:S(2)}, u32[]{:S(2)}) %collective-permute-start.18) | collective-permute-done | bytes 204832 | tf_op jit(solution)/shard_map/ppermute | solution.py:348
  69.6 0.9 %shard_map.104 = (f32[160,1280]{1,0:T(8,128)}, f32[160,1280]{1,0:T(8,128)}) custom-call(bf16[80,1280]{1,0:T(8,128)(2,1)S(1)} %collective-permute-done.18.owned, f32[1,1280]{1,0:T(1,128)S(1)} %broadcast_in_dim.3.gate, f32[160,1280]{1,0:T(8,128)S(1)} %shard_map.101.resting), custom_call_target="tpu_custom_call" | custom-call | tf_op jit(solution)/shard_map/pallas_call | solution.py:355
  70.6 0.0 collective-permute-done.13.owned
  70.6 1.0 %shard_map.105 = (f32[160,1280]{1,0:T(8,128)}, f32[160,1280]{1,0:T(8,128)}) custom-call(bf16[80,1280]{1,0:T(8,128)(2,1)S(1)} %collective-permute-done.13.owned, f32[1,1280]{1,0:T(1,128)S(1)} %broadcast_in_dim.3.gate, f32[160,1280]{1,0:T(8,128)S(1)} %shard_map.101.resting, ...), custom_call_target="tpu_custom_call", output_to_operand_aliasing={{0}: (3, {}), {1}: (4, {})} | custom-call | tf_op jit(solution)/shard_map/pallas_call | solution.py:355
  (12 shorter events, 0.1 us)
Async XLA Ops:
  0.6 38.4 %copy-start = (bf16[768,1280]{1,0:T(8,128)(2,1)S(1)}, bf16[768,1280]{1,0:T(8,128)(2,1)}, u32[]{:S(2)}) copy-start(bf16[768,1280]{1,0:T(8,128)(2,1)} %refs_4_.5) | copy-start | bytes 5898244
  2.0 21.4 %collective-permute-start.5 = (bf16[768,1280]{1,0:T(8,128)(2,1)}, bf16[768,1280]{1,0:T(8,128)(2,1)S(1)}, u32[]{:S(2)}, u32[]{:S(2)}) collective-permute-start(bf16[768,1280]{1,0:T(8,128)(2,1)} %refs_4_.5), channel_id=1, source_target_pairs={{0,1},{1,0},{2,3},{3,2},{4,5},{5,4},{6,7},{7,6},{8,9},{9,8},{10,11... | collective-permute-start | bytes 5898248 | tf_op jit(solution)/shard_map/ppermute | solution.py:292
  2.1 17.6 %collective-permute-start.1 = (bf16[320,384]{1,0:T(8,128)(2,1)S(1)}, bf16[320,384]{1,0:T(8,128)(2,1)S(1)}, u32[]{:S(2)}, u32[]{:S(2)}) collective-permute-start(bf16[320,384]{1,0:T(8,128)(2,1)S(1)} %get-tuple-element.17), channel_id=1, source_target_pairs={{0,8},{1,12},{4,9},{5,13},{8,0},{9,4},{12,1},{13,5},{2,10},{3,14},... | collective-permute-start | bytes 737288 | tf_op jit(solution)/shard_map/ppermute | solution.py:301
  4.8 15.0 %collective-permute-start = (bf16[320,384]{1,0:T(8,128)(2,1)S(1)}, bf16[320,384]{1,0:T(8,128)(2,1)S(1)}, u32[]{:S(2)}, u32[]{:S(2)}) collective-permute-start(bf16[320,384]{1,0:T(8,128)(2,1)S(1)} %get-tuple-element.16), channel_id=1, source_target_pairs={{0,0},{1,4},{4,1},{5,5},{8,8},{9,12},{12,9},{13,13},{2,2},{3,6},{6... | collective-permute-start | bytes 737288 | tf_op jit(solution)/shard_map/ppermute | solution.py:301
  5.4 13.7 %collective-permute-start.2 = (bf16[160,384]{1,0:T(8,128)(2,1)S(1)}, bf16[160,384]{1,0:T(8,128)(2,1)S(1)}, u32[]{:S(2)}, u32[]{:S(2)}) collective-permute-start(bf16[160,384]{1,0:T(8,128)(2,1)S(1)} %get-tuple-element.18), channel_id=1, source_target_pairs={{0,1},{1,5},{4,0},{5,4},{8,9},{9,13},{12,8},{13,12},{2,3},{3,7},{6... | collective-permute-start | bytes 368648 | tf_op jit(solution)/shard_map/ppermute | solution.py:301
  7.9 11.3 %collective-permute-start.3 = (bf16[160,384]{1,0:T(8,128)(2,1)S(1)}, bf16[160,384]{1,0:T(8,128)(2,1)S(1)}, u32[]{:S(2)}, u32[]{:S(2)}) collective-permute-start(bf16[160,384]{1,0:T(8,128)(2,1)S(1)} %get-tuple-element.19), channel_id=1, source_target_pairs={{0,9},{1,13},{4,8},{5,12},{8,1},{9,5},{12,0},{13,4},{2,11},{3,15},... | collective-permute-start | bytes 368648 | tf_op jit(solution)/shard_map/ppermute | solution.py:301
  19.8 3.6 %collective-permute-start.4 = (bf16[640,384]{1,0:T(8,128)(2,1)S(1)}, bf16[640,384]{1,0:T(8,128)(2,1)S(1)}, u32[]{:S(2)}, u32[]{:S(2)}) collective-permute-start(bf16[640,384]{1,0:T(8,128)(2,1)S(1)} %shard_map.96), channel_id=1, source_target_pairs={{0,1},{1,0},{2,3},{3,2},{4,5},{5,4},{6,7},{7,6},{8,9},{9,8},{10,11... | collective-permute-start | bytes 1474568 | tf_op jit(solution)/shard_map/ppermute | solution.py:303
  25.0 8.1 %collective-permute-start.8 = (bf16[160,384]{1,0:T(8,128)(2,1)S(1)}, bf16[160,384]{1,0:T(8,128)(2,1)S(1)}, u32[]{:S(2)}, u32[]{:S(2)}) collective-permute-start(bf16[160,384]{1,0:T(8,128)(2,1)S(1)} %get-tuple-element.23.refs_0_), channel_id=1, source_target_pairs={{0,12},{4,8},{8,4},{12,0},{1,13},{5,9},{9,5},{13,1},{2,14},{6,10},... | collective-permute-start | bytes 368648 | tf_op jit(solution)/shard_map/ppermute | solution.py:242
  28.7 10.3 %collective-permute-start.7 = (bf16[160,384]{1,0:T(8,128)(2,1)S(1)}, bf16[160,384]{1,0:T(8,128)(2,1)S(1)}, u32[]{:S(2)}, u32[]{:S(2)}) collective-permute-start(bf16[160,384]{1,0:T(8,128)(2,1)S(1)} %get-tuple-element.23.refs_0_), channel_id=1, source_target_pairs={{0,8},{4,12},{8,0},{12,4},{1,9},{5,13},{9,1},{13,5},{2,10},{6,14},... | collective-permute-start | bytes 368648 | tf_op jit(solution)/shard_map/ppermute | solution.py:242
  28.7 10.3 %collective-permute-start.6 = (bf16[160,384]{1,0:T(8,128)(2,1)S(1)}, bf16[160,384]{1,0:T(8,128)(2,1)S(1)}, u32[]{:S(2)}, u32[]{:S(2)}) collective-permute-start(bf16[160,384]{1,0:T(8,128)(2,1)S(1)} %get-tuple-element.23.refs_0_), channel_id=1, source_target_pairs={{0,4},{4,0},{8,12},{12,8},{1,5},{5,1},{9,13},{13,9},{2,6},{6,2},{1... | collective-permute-start | bytes 368648 | tf_op jit(solution)/shard_map/ppermute | solution.py:242
  39.9 17.2 %collective-permute-start.17 = (bf16[80,1280]{1,0:T(8,128)(2,1)S(1)}, bf16[80,1280]{1,0:T(8,128)(2,1)S(1)}, u32[]{:S(2)}, u32[]{:S(2)}) collective-permute-start(bf16[80,1280]{1,0:T(8,128)(2,1)S(1)} %get-tuple-element.24), channel_id=1, source_target_pairs={{0,2},{2,0},{1,3},{3,1},{4,6},{6,4},{5,7},{7,5},{8,10},{10,8},{9,1... | collective-permute-start | bytes 614408 | tf_op jit(solution)/shard_map/ppermute | solution.py:333
  40.5 20.5 %collective-permute-start.12 = (bf16[80,1280]{1,0:T(8,128)(2,1)S(1)}, bf16[80,1280]{1,0:T(8,128)(2,1)S(1)}, u32[]{:S(2)}, u32[]{:S(2)}) collective-permute-start(bf16[80,1280]{1,0:T(8,128)(2,1)S(1)} %get-tuple-element.26), channel_id=1, source_target_pairs={{0,2},{2,0},{1,3},{3,1},{4,6},{6,4},{5,7},{7,5},{8,10},{10,8},{9,1... | collective-permute-start | bytes 614408 | tf_op jit(solution)/shard_map/ppermute | solution.py:333
  42.0 6.3 %collective-permute-start.16 = (bf16[80,384]{1,0:T(8,128)(2,1)S(1)}, bf16[80,384]{1,0:T(8,128)(2,1)S(1)}, u32[]{:S(2)}, u32[]{:S(2)}) collective-permute-start(bf16[80,384]{1,0:T(8,128)(2,1)S(1)} %get-tuple-element.27.refs_0_), channel_id=1, source_target_pairs={{0,12},{4,8},{8,4},{12,0},{1,13},{5,9},{9,5},{13,1},{2,14},{6,10},... | collective-permute-start | bytes 184328 | tf_op jit(solution)/shard_map/ppermute | solution.py:242
  44.7 6.3 %collective-permute-start.15 = (bf16[80,384]{1,0:T(8,128)(2,1)S(1)}, bf16[80,384]{1,0:T(8,128)(2,1)S(1)}, u32[]{:S(2)}, u32[]{:S(2)}) collective-permute-start(bf16[80,384]{1,0:T(8,128)(2,1)S(1)} %get-tuple-element.27.refs_0_), channel_id=1, source_target_pairs={{0,8},{4,12},{8,0},{12,4},{1,9},{5,13},{9,1},{13,5},{2,10},{6,14},... | collective-permute-start | bytes 184328 | tf_op jit(solution)/shard_map/ppermute | solution.py:242
  44.7 6.3 %collective-permute-start.14 = (bf16[80,384]{1,0:T(8,128)(2,1)S(1)}, bf16[80,384]{1,0:T(8,128)(2,1)S(1)}, u32[]{:S(2)}, u32[]{:S(2)}) collective-permute-start(bf16[80,384]{1,0:T(8,128)(2,1)S(1)} %get-tuple-element.27.refs_0_), channel_id=1, source_target_pairs={{0,4},{4,0},{8,12},{12,8},{1,5},{5,1},{9,13},{13,9},{2,6},{6,2},{1... | collective-permute-start | bytes 184328 | tf_op jit(solution)/shard_map/ppermute | solution.py:242
  48.3 6.5 %collective-permute-start.11 = (bf16[80,384]{1,0:T(8,128)(2,1)S(1)}, bf16[80,384]{1,0:T(8,128)(2,1)S(1)}, u32[]{:S(2)}, u32[]{:S(2)}) collective-permute-start(bf16[80,384]{1,0:T(8,128)(2,1)S(1)} %get-tuple-element.25.refs_0_), channel_id=1, source_target_pairs={{0,12},{4,8},{8,4},{12,0},{1,13},{5,9},{9,5},{13,1},{2,14},{6,10},... | collective-permute-start | bytes 184328 | tf_op jit(solution)/shard_map/ppermute | solution.py:242
  51.0 5.3 %collective-permute-start.10 = (bf16[80,384]{1,0:T(8,128)(2,1)S(1)}, bf16[80,384]{1,0:T(8,128)(2,1)S(1)}, u32[]{:S(2)}, u32[]{:S(2)}) collective-permute-start(bf16[80,384]{1,0:T(8,128)(2,1)S(1)} %get-tuple-element.25.refs_0_), channel_id=1, source_target_pairs={{0,8},{4,12},{8,0},{12,4},{1,9},{5,13},{9,1},{13,5},{2,10},{6,14},... | collective-permute-start | bytes 184328 | tf_op jit(solution)/shard_map/ppermute | solution.py:242
  51.0 5.3 %collective-permute-start.9 = (bf16[80,384]{1,0:T(8,128)(2,1)S(1)}, bf16[80,384]{1,0:T(8,128)(2,1)S(1)}, u32[]{:S(2)}, u32[]{:S(2)}) collective-permute-start(bf16[80,384]{1,0:T(8,128)(2,1)S(1)} %get-tuple-element.25.refs_0_), channel_id=1, source_target_pairs={{0,4},{4,0},{8,12},{12,8},{1,5},{5,1},{9,13},{13,9},{2,6},{6,2},{1... | collective-permute-start | bytes 184328 | tf_op jit(solution)/shard_map/ppermute | solution.py:242
  53.8 7.4 %copy-start.4 = (f32[1280]{0:T(1024)S(1)}, f32[1280]{0:T(1024)}, u32[]{:S(2)}) copy-start(f32[1280]{0:T(1024)} %param.12) | copy-start | bytes 15364
  53.8 7.4 %copy-start.3 = (s32[4]{0:T(128)S(1)}, s32[4]{0:T(128)}, u32[]{:S(2)}) copy-start(s32[4]{0:T(128)} %flags.1) | copy-start | bytes 52
  56.3 4.9 %copy-start.1 = (f32[4,160,1280]{2,1,0:T(8,128)S(1)}, f32[4,160,1280]{2,1,0:T(8,128)}, u32[]{:S(2)}) copy-start(f32[4,160,1280]{2,1,0:T(8,128)} %cached.1) | copy-start | bytes 9830404
  57.1 4.1 %copy-start.2 = (f32[160,1280]{1,0:T(8,128)S(1)}, f32[160,1280]{1,0:T(8,128)}, u32[]{:S(2)}) copy-start(f32[160,1280]{1,0:T(8,128)} %hidden.1) | copy-start | bytes 2457604
  57.2 12.4 %collective-permute-start.18 = (bf16[80,1280]{1,0:T(8,128)(2,1)S(1)}, bf16[80,1280]{1,0:T(8,128)(2,1)S(1)}, u32[]{:S(2)}, u32[]{:S(2)}) collective-permute-start(bf16[80,1280]{1,0:T(8,128)(2,1)S(1)} %shard_map.103), channel_id=1, source_target_pairs={{0,0},{1,4},{2,8},{3,12},{4,1},{5,5},{6,9},{7,13},{8,2},{9,6},{10,... | collective-permute-start | bytes 614408 | tf_op jit(solution)/shard_map/ppermute | solution.py:348
  61.1 9.4 %collective-permute-start.13 = (bf16[80,1280]{1,0:T(8,128)(2,1)S(1)}, bf16[80,1280]{1,0:T(8,128)(2,1)S(1)}, u32[]{:S(2)}, u32[]{:S(2)}) collective-permute-start(bf16[80,1280]{1,0:T(8,128)(2,1)S(1)} %shard_map.100), channel_id=1, source_target_pairs={{0,8},{1,12},{2,0},{3,4},{4,9},{5,13},{6,1},{7,5},{8,10},{9,14},{1... | collective-permute-start | bytes 614408 | tf_op jit(solution)/shard_map/ppermute | solution.py:348

commit v20 on v16

--- a/solution.py
+++ b/solution.py
@@ -106,7 +106,7 @@
     copies = []
     for k in range(4):
         part = pl.ds(pl.multiple_of(flip(zl, k // 2) * half, 16), half)
-        columns = pl.ds(pl.multiple_of(flip(zh, k % 2) * width, 128), width)
+        columns = pl.ds(pl.multiple_of(flip(zh, 1 - k % 2) * width, 128), width)
         moves = [
             (keys.at[part, columns], outs[k].at[pl.ds(0, half), :]),
             (values.at[part, columns], outs[k].at[pl.ds(half, half), :]),
@@ -144,7 +144,7 @@
     for k in range(2):
         for part in range(2):
             at = rows + flip(x, part == 0) * half
-            to = (part * 2 + flip(zh, k)) * half
+            to = (part * 2 + flip(zh, 1 - k)) * half
             query_all[pl.ds(pl.multiple_of(to, 16), half), :] = blocks[k][
                 pl.ds(pl.multiple_of(at, 16), half), :
             ]
@@ -287,7 +287,7 @@
     weight_c = lax.ppermute(late_weight, "head", swap)
     moved = []
     for k in range(4):
-        k1, k0 = k // 2, k % 2
+        k1, k0 = k // 2, 1 - k % 2
         pairs = []
         for zz in range(4):
             for cc in range(2):

time: 67.8 us -> 66.8 us (0.985)
    ppermute x2, waiting for transfers between devices: 9.24 us -> 8.54 us  [local_heads(): owned.append(lax.ppermute(summed, ('seq', 'wt', 'head'), pairs))]
  transfers between devices with their start and end apart: 16 -> 16, of which waited for: 6 -> 8; matrix products, arithmetic and copies ran while one was open for 0% -> 0% of each run, Pallas kernels for 5% -> 6%
where the time goes in v20:
time: 66.8 us; the launch traced here: 66.7 us
  waiting for transfers between devices  31.2 us (47%)
  starting transfers between devices  27 us (40%)
  Pallas kernels  7.63 us (11%)
  between operations  0.8 us (1%)
    ppermute x4, waiting for transfers between devices, local_heads(): moved.append(lax.ppermute(packed[k], ('seq', 'head'), pairs))  11.4 us
    ppermute x6, starting transfers between devices, along(): return lax.ppermute(shard, 'seq', [(z, z ^ m) for z in range(4)])  10.3 us
    ppermute x6, waiting for transfers between devices, along(): return lax.ppermute(shard, 'seq', [(z, z ^ m) for z in range(4)])  9.63 us
    ppermute x2, waiting for transfers between devices, local_heads(): owned.append(lax.ppermute(summed, ('seq', 'wt', 'head'), pairs))  8.54 us
    ppermute x2, starting transfers between devices, local_heads(): owned.append(lax.ppermute(summed, ('seq', 'wt', 'head'), pairs))  6.23 us
    ppermute x4, starting transfers between devices, local_heads(): moved.append(lax.ppermute(packed[k], ('seq', 'head'), pairs))  6.17 us
    pallas_call x8, Pallas kernels, call(): pl.pallas_call(kernel, in_specs=[pl.BlockSpec(memory_space=place) for pla...  5.73 us
    ppermute x1, starting transfers between devices, local_heads(): sibling = lax.ppermute(joined, 'head', swap)  2.15 us
  transfers between devices with their start and end apart: 16, of which 8 were waited for; matrix products, arithmetic and copies ran while one was open for 0% of the time, Pallas kernels for 6%

profile of v20, /device:TPU:2, one launch (start us, length us, event | category | flops | bytes accessed | tf_op | source)
XLA Modules:
  0.0 66.7 jit_solution(15168498676815667612)
XLA Ops:
  0.6 0.0 copy-start.1
  0.6 1.4 %shard_map.95 = (bf16[320,384]{1,0:T(8,128)(2,1)S(1)}, bf16[320,384]{1,0:T(8,128)(2,1)S(1)}, bf16[160,384]{1,0:T(8,128)(2,1)S(1)}, bf16[160,384]{1,0:T(8,128)(2,1)S(1)}) custom-call(bf16[160,768]{1,0:T(8,128)(2,1)} %queries.1, bf16[160,768]{1,0:T(8,128)(2,1)} %keys.1, bf16[160,768]{1,0:T(8,128)(2,1)} %values.1), custom_call_target="tpu_custom_call" | custom-call | tf_op jit(solution)/shard_map/pallas_call | solution.py:251
  2.0 0.1 collective-permute-start.5
  2.1 2.7 %collective-permute-start = (bf16[320,384]{1,0:T(8,128)(2,1)S(1)}, bf16[320,384]{1,0:T(8,128)(2,1)S(1)}, u32[]{:S(2)}, u32[]{:S(2)}) collective-permute-start(bf16[320,384]{1,0:T(8,128)(2,1)S(1)} %get-tuple-element.16), channel_id=1, source_target_pairs={{0,8},{1,12},{4,9},{5,13},{8,0},{9,4},{12,1},{13,5},{2,10},{3,14},... | collective-permute-start | bytes 737288 | tf_op jit(solution)/shard_map/ppermute | solution.py:296
  4.8 0.7 collective-permute-start.1
  5.4 2.8 %collective-permute-start.2 = (bf16[160,384]{1,0:T(8,128)(2,1)S(1)}, bf16[160,384]{1,0:T(8,128)(2,1)S(1)}, u32[]{:S(2)}, u32[]{:S(2)}) collective-permute-start(bf16[160,384]{1,0:T(8,128)(2,1)S(1)} %get-tuple-element.18), channel_id=1, source_target_pairs={{0,9},{1,13},{4,8},{5,12},{8,1},{9,5},{12,0},{13,4},{2,11},{3,15},... | collective-permute-start | bytes 368648 | tf_op jit(solution)/shard_map/ppermute | solution.py:296
  8.3 0.0 collective-permute-start.3
  8.3 9.6 %collective-permute-done.2.refs_2_ = bf16[160,384]{1,0:T(8,128)(2,1)S(1)} collective-permute-done((bf16[160,384]{1,0:T(8,128)(2,1)S(1)}, bf16[160,384]{1,0:T(8,128)(2,1)S(1)}, u32[]{:S(2)}, u32[]{:S(2)}) %collective-permute-start.2) | collective-permute-done | bytes 122912 | tf_op jit(solution)/shard_map/ppermute | solution.py:296
  17.8 1.4 %collective-permute-done.3.refs_3_ = bf16[160,384]{1,0:T(8,128)(2,1)S(1)} collective-permute-done((bf16[160,384]{1,0:T(8,128)(2,1)S(1)}, bf16[160,384]{1,0:T(8,128)(2,1)S(1)}, u32[]{:S(2)}, u32[]{:S(2)}) %collective-permute-start.3) | collective-permute-done | bytes 122912 | tf_op jit(solution)/shard_map/ppermute | solution.py:296
  19.2 0.5 collective-permute-done.refs_0_
  19.7 0.0 collective-permute-done.1.refs_1_
  19.8 2.1 %collective-permute-start.4 = (bf16[640,384]{1,0:T(8,128)(2,1)S(1)}, bf16[640,384]{1,0:T(8,128)(2,1)S(1)}, u32[]{:S(2)}, u32[]{:S(2)}) collective-permute-start(bf16[640,384]{1,0:T(8,128)(2,1)S(1)} %shard_map.96), channel_id=1, source_target_pairs={{0,1},{1,0},{2,3},{3,2},{4,5},{5,4},{6,7},{7,6},{8,9},{9,8},{10,11... | collective-permute-start | bytes 1474568 | tf_op jit(solution)/shard_map/ppermute | solution.py:298
  21.9 1.5 %collective-permute-done.4.refs_4_ = bf16[640,384]{1,0:T(8,128)(2,1)S(1)} collective-permute-done((bf16[640,384]{1,0:T(8,128)(2,1)S(1)}, bf16[640,384]{1,0:T(8,128)(2,1)S(1)}, u32[]{:S(2)}, u32[]{:S(2)}) %collective-permute-start.4) | collective-permute-done | bytes 491552 | tf_op jit(solution)/shard_map/ppermute | solution.py:298
  23.4 0.0 collective-permute-done.5.refs_5_
  23.4 1.6 %shard_map.97 = (bf16[160,384]{1,0:T(8,128)(2,1)S(1)}, bf16[160,384]{1,0:T(8,128)(2,1)S(1)}) custom-call(bf16[320,384]{1,0:T(8,128)(2,1)S(1)} %collective-permute-done.refs_0_, bf16[320,384]{1,0:T(8,128)(2,1)S(1)} %collective-permute-done.1.refs_1_, bf16[160,384]{1,0:T(8,128)(2,1)S(1)} %collective-permute-done.2.refs_2_, ...), custom_call_target="tpu_custom_call" | custom-call | flops 314572800 | tf_op jit(solution)/shard_map/pallas_call | solution.py:251
  25.0 2.4 %collective-permute-start.10 = (bf16[160,384]{1,0:T(8,128)(2,1)S(1)}, bf16[160,384]{1,0:T(8,128)(2,1)S(1)}, u32[]{:S(2)}, u32[]{:S(2)}) collective-permute-start(bf16[160,384]{1,0:T(8,128)(2,1)S(1)} %get-tuple-element.24.refs_0_), channel_id=1, source_target_pairs={{0,8},{4,12},{8,0},{12,4},{1,9},{5,13},{9,1},{13,5},{2,10},{6,14},... | collective-permute-start | bytes 368648 | tf_op jit(solution)/shard_map/ppermute | solution.py:237
  27.5 1.3 %collective-permute-start.11 = (bf16[160,384]{1,0:T(8,128)(2,1)S(1)}, bf16[160,384]{1,0:T(8,128)(2,1)S(1)}, u32[]{:S(2)}, u32[]{:S(2)}) collective-permute-start(bf16[160,384]{1,0:T(8,128)(2,1)S(1)} %get-tuple-element.24.refs_0_), channel_id=1, source_target_pairs={{0,12},{4,8},{8,4},{12,0},{1,13},{5,9},{9,5},{13,1},{2,14},{6,10},... | collective-permute-start | bytes 368648 | tf_op jit(solution)/shard_map/ppermute | solution.py:237
  28.8 0.5 collective-permute-start.9
  29.3 1.5 %collective-permute-start.6 = (bf16[160,384]{1,0:T(8,128)(2,1)S(1)}, bf16[160,384]{1,0:T(8,128)(2,1)S(1)}, u32[]{:S(2)}, u32[]{:S(2)}) collective-permute-start(bf16[160,384]{1,0:T(8,128)(2,1)S(1)} %get-tuple-element.22.refs_0_), channel_id=1, source_target_pairs={{0,4},{4,0},{8,12},{12,8},{1,5},{5,1},{9,13},{13,9},{2,6},{6,2},{1... | collective-permute-start | bytes 368648 | tf_op jit(solution)/shard_map/ppermute | solution.py:237
  30.9 1.9 %collective-permute-start.7 = (bf16[160,384]{1,0:T(8,128)(2,1)S(1)}, bf16[160,384]{1,0:T(8,128)(2,1)S(1)}, u32[]{:S(2)}, u32[]{:S(2)}) collective-permute-start(bf16[160,384]{1,0:T(8,128)(2,1)S(1)} %get-tuple-element.22.refs_0_), channel_id=1, source_target_pairs={{0,8},{4,12},{8,0},{12,4},{1,9},{5,13},{9,1},{13,5},{2,10},{6,14},... | collective-permute-start | bytes 368648 | tf_op jit(solution)/shard_map/ppermute | solution.py:237
  32.8 4.7 %collective-permute-done.10.refs_2_ = bf16[160,384]{1,0:T(8,128)(2,1)S(1)} collective-permute-done((bf16[160,384]{1,0:T(8,128)(2,1)S(1)}, bf16[160,384]{1,0:T(8,128)(2,1)S(1)}, u32[]{:S(2)}, u32[]{:S(2)}) %collective-permute-start.10) | collective-permute-done | bytes 122912 | tf_op jit(solution)/shard_map/ppermute | solution.py:237
  37.5 2.6 %collective-permute-start.8 = (bf16[160,384]{1,0:T(8,128)(2,1)S(1)}, bf16[160,384]{1,0:T(8,128)(2,1)S(1)}, u32[]{:S(2)}, u32[]{:S(2)}) collective-permute-start(bf16[160,384]{1,0:T(8,128)(2,1)S(1)} %get-tuple-element.22.refs_0_), channel_id=1, source_target_pairs={{0,12},{4,8},{8,4},{12,0},{1,13},{5,9},{9,5},{13,1},{2,14},{6,10},... | collective-permute-start | bytes 368648 | tf_op jit(solution)/shard_map/ppermute | solution.py:237
  40.0 0.0 collective-permute-done.11.refs_3_
  40.0 0.0 collective-permute-done.9.refs_1_
  40.1 0.0 copy-done.1
  40.1 0.9 %shard_map.99 = (bf16[80,1280]{1,0:T(8,128)(2,1)S(1)}, bf16[80,1280]{1,0:T(8,128)(2,1)S(1)}) custom-call(bf16[160,384]{1,0:T(8,128)(2,1)S(1)} %get-tuple-element.24.refs_0_, bf16[160,384]{1,0:T(8,128)(2,1)S(1)} %collective-permute-done.9.refs_1_, bf16[160,384]{1,0:T(8,128)(2,1)S(1)} %collective-permute-done.10.refs_2_, ...), custom_call_target="tpu_custom_call" | custom-call | flops 629145600 | tf_op jit(solution)/shard_map/pallas_call | solution.py:251
  41.0 0.6 collective-permute-start.14
  41.6 0.0 copy-start.4
  41.6 1.5 %collective-permute-start.12 = (bf16[80,1280]{1,0:T(8,128)(2,1)S(1)}, bf16[80,1280]{1,0:T(8,128)(2,1)S(1)}, u32[]{:S(2)}, u32[]{:S(2)}) collective-permute-start(bf16[80,1280]{1,0:T(8,128)(2,1)S(1)} %get-tuple-element.25), channel_id=1, source_target_pairs={{0,2},{2,0},{1,3},{3,1},{4,6},{6,4},{5,7},{7,5},{8,10},{10,8},{9,1... | collective-permute-start | bytes 614408 | tf_op jit(solution)/shard_map/ppermute | solution.py:327
  43.1 0.0 collective-permute-done.6.refs_1_
  43.1 4.9 %collective-permute-done.7.refs_2_ = bf16[160,384]{1,0:T(8,128)(2,1)S(1)} collective-permute-done((bf16[160,384]{1,0:T(8,128)(2,1)S(1)}, bf16[160,384]{1,0:T(8,128)(2,1)S(1)}, u32[]{:S(2)}, u32[]{:S(2)}) %collective-permute-start.7) | collective-permute-done | bytes 122912 | tf_op jit(solution)/shard_map/ppermute | solution.py:237
  48.0 0.0 collective-permute-done.8.refs_3_
  48.0 0.9 %shard_map.98 = (f32[80,1280]{1,0:T(8,128)S(1)}, f32[80,1280]{1,0:T(8,128)S(1)}) custom-call(bf16[160,384]{1,0:T(8,128)(2,1)S(1)} %get-tuple-element.22.refs_0_, bf16[160,384]{1,0:T(8,128)(2,1)S(1)} %collective-permute-done.6.refs_1_, bf16[160,384]{1,0:T(8,128)(2,1)S(1)} %collective-permute-done.7.refs_2_, ...), custom_call_target="tpu_custom_call" | custom-call | flops 5033164800 | tf_op jit(solution)/shard_map/pallas_call | solution.py:251
  49.0 0.0 copy-start.2
  49.0 0.1 collective-permute-done.14.arrived
  49.0 0.1 shard_map.102
  49.1 6.2 %collective-permute-start.15 = (bf16[80,1280]{1,0:T(8,128)(2,1)S(1)}, bf16[80,1280]{1,0:T(8,128)(2,1)S(1)}, u32[]{:S(2)}, u32[]{:S(2)}) collective-permute-start(bf16[80,1280]{1,0:T(8,128)(2,1)S(1)} %shard_map.102), channel_id=1, source_target_pairs={{0,0},{1,4},{2,8},{3,12},{4,1},{5,5},{6,9},{7,13},{8,2},{9,6},{10,... | collective-permute-start | bytes 614408 | tf_op jit(solution)/shard_map/ppermute | solution.py:335
  55.3 0.0 collective-permute-done.12.arrived
  55.3 0.1 collective-permute-start.13
  55.4 0.0 copy-done.4
  55.4 0.0 copy-done.3
  55.4 0.0 copy-done
  55.4 0.0 copy-done.2
  55.4 0.8 %shard_map.101.resting = f32[160,1280]{1,0:T(8,128)S(1)} custom-call(s32[4]{0:T(128)S(1)} %copy-done.3, f32[160,1280]{1,0:T(8,128)S(1)} %copy-done.2, f32[4,160,1280]{2,1,0:T(8,128)S(1)} %copy-done), custom_call_target="tpu_custom_call" | custom-call | tf_op jit(solution)/shard_map/pallas_call | solution.py:251
  56.2 8.5 %collective-permute-done.15.owned = bf16[80,1280]{1,0:T(8,128)(2,1)S(1)} collective-permute-done((bf16[80,1280]{1,0:T(8,128)(2,1)S(1)}, bf16[80,1280]{1,0:T(8,128)(2,1)S(1)}, u32[]{:S(2)}, u32[]{:S(2)}) %collective-permute-start.15) | collective-permute-done | bytes 204832 | tf_op jit(solution)/shard_map/ppermute | solution.py:335
  64.7 0.9 %shard_map.103 = (f32[160,1280]{1,0:T(8,128)}, f32[160,1280]{1,0:T(8,128)}) custom-call(bf16[80,1280]{1,0:T(8,128)(2,1)S(1)} %collective-permute-done.15.owned, f32[1,1280]{1,0:T(1,128)S(1)} %broadcast_in_dim.3.gate, f32[160,1280]{1,0:T(8,128)S(1)} %shard_map.101.resting), custom_call_target="tpu_custom_call" | custom-call | tf_op jit(solution)/shard_map/pallas_call | solution.py:342
  65.7 0.0 collective-permute-done.13.owned
  65.7 1.0 %shard_map.104 = (f32[160,1280]{1,0:T(8,128)}, f32[160,1280]{1,0:T(8,128)}) custom-call(bf16[80,1280]{1,0:T(8,128)(2,1)S(1)} %collective-permute-done.13.owned, f32[1,1280]{1,0:T(1,128)S(1)} %broadcast_in_dim.3.gate, f32[160,1280]{1,0:T(8,128)S(1)} %shard_map.101.resting, ...), custom_call_target="tpu_custom_call", output_to_operand_aliasing={{0}: (3, {}), {1}: (4, {})} | custom-call | tf_op jit(solution)/shard_map/pallas_call | solution.py:342
  (5 shorter events, 0.1 us)
Async XLA Ops:
  0.6 39.4 %copy-start.1 = (bf16[768,1280]{1,0:T(8,128)(2,1)S(1)}, bf16[768,1280]{1,0:T(8,128)(2,1)}, u32[]{:S(2)}) copy-start(bf16[768,1280]{1,0:T(8,128)(2,1)} %refs_4_.3) | copy-start | bytes 5898244
  2.0 21.4 %collective-permute-start.5 = (bf16[768,1280]{1,0:T(8,128)(2,1)}, bf16[768,1280]{1,0:T(8,128)(2,1)S(1)}, u32[]{:S(2)}, u32[]{:S(2)}) collective-permute-start(bf16[768,1280]{1,0:T(8,128)(2,1)} %refs_4_.3), channel_id=1, source_target_pairs={{0,1},{1,0},{2,3},{3,2},{4,5},{5,4},{6,7},{7,6},{8,9},{9,8},{10,11... | collective-permute-start | bytes 5898248 | tf_op jit(solution)/shard_map/ppermute | solution.py:287
  2.1 17.6 %collective-permute-start = (bf16[320,384]{1,0:T(8,128)(2,1)S(1)}, bf16[320,384]{1,0:T(8,128)(2,1)S(1)}, u32[]{:S(2)}, u32[]{:S(2)}) collective-permute-start(bf16[320,384]{1,0:T(8,128)(2,1)S(1)} %get-tuple-element.16), channel_id=1, source_target_pairs={{0,8},{1,12},{4,9},{5,13},{8,0},{9,4},{12,1},{13,5},{2,10},{3,14},... | collective-permute-start | bytes 737288 | tf_op jit(solution)/shard_map/ppermute | solution.py:296
  4.8 15.0 %collective-permute-start.1 = (bf16[320,384]{1,0:T(8,128)(2,1)S(1)}, bf16[320,384]{1,0:T(8,128)(2,1)S(1)}, u32[]{:S(2)}, u32[]{:S(2)}) collective-permute-start(bf16[320,384]{1,0:T(8,128)(2,1)S(1)} %get-tuple-element.17), channel_id=1, source_target_pairs={{0,0},{1,4},{4,1},{5,5},{8,8},{9,12},{12,9},{13,13},{2,2},{3,6},{6... | collective-permute-start | bytes 737288 | tf_op jit(solution)/shard_map/ppermute | solution.py:296
  5.4 12.4 %collective-permute-start.2 = (bf16[160,384]{1,0:T(8,128)(2,1)S(1)}, bf16[160,384]{1,0:T(8,128)(2,1)S(1)}, u32[]{:S(2)}, u32[]{:S(2)}) collective-permute-start(bf16[160,384]{1,0:T(8,128)(2,1)S(1)} %get-tuple-element.18), channel_id=1, source_target_pairs={{0,9},{1,13},{4,8},{5,12},{8,1},{9,5},{12,0},{13,4},{2,11},{3,15},... | collective-permute-start | bytes 368648 | tf_op jit(solution)/shard_map/ppermute | solution.py:296
  8.3 10.9 %collective-permute-start.3 = (bf16[160,384]{1,0:T(8,128)(2,1)S(1)}, bf16[160,384]{1,0:T(8,128)(2,1)S(1)}, u32[]{:S(2)}, u32[]{:S(2)}) collective-permute-start(bf16[160,384]{1,0:T(8,128)(2,1)S(1)} %get-tuple-element.19), channel_id=1, source_target_pairs={{0,1},{1,5},{4,0},{5,4},{8,9},{9,13},{12,8},{13,12},{2,3},{3,7},{6... | collective-permute-start | bytes 368648 | tf_op jit(solution)/shard_map/ppermute | solution.py:296
  19.8 3.6 %collective-permute-start.4 = (bf16[640,384]{1,0:T(8,128)(2,1)S(1)}, bf16[640,384]{1,0:T(8,128)(2,1)S(1)}, u32[]{:S(2)}, u32[]{:S(2)}) collective-permute-start(bf16[640,384]{1,0:T(8,128)(2,1)S(1)} %shard_map.96), channel_id=1, source_target_pairs={{0,1},{1,0},{2,3},{3,2},{4,5},{5,4},{6,7},{7,6},{8,9},{9,8},{10,11... | collective-permute-start | bytes 1474568 | tf_op jit(solution)/shard_map/ppermute | solution.py:298
  25.0 12.4 %collective-permute-start.10 = (bf16[160,384]{1,0:T(8,128)(2,1)S(1)}, bf16[160,384]{1,0:T(8,128)(2,1)S(1)}, u32[]{:S(2)}, u32[]{:S(2)}) collective-permute-start(bf16[160,384]{1,0:T(8,128)(2,1)S(1)} %get-tuple-element.24.refs_0_), channel_id=1, source_target_pairs={{0,8},{4,12},{8,0},{12,4},{1,9},{5,13},{9,1},{13,5},{2,10},{6,14},... | collective-permute-start | bytes 368648 | tf_op jit(solution)/shard_map/ppermute | solution.py:237
  27.5 12.6 %collective-permute-start.11 = (bf16[160,384]{1,0:T(8,128)(2,1)S(1)}, bf16[160,384]{1,0:T(8,128)(2,1)S(1)}, u32[]{:S(2)}, u32[]{:S(2)}) collective-permute-start(bf16[160,384]{1,0:T(8,128)(2,1)S(1)} %get-tuple-element.24.refs_0_), channel_id=1, source_target_pairs={{0,12},{4,8},{8,4},{12,0},{1,13},{5,9},{9,5},{13,1},{2,14},{6,10},... | collective-permute-start | bytes 368648 | tf_op jit(solution)/shard_map/ppermute | solution.py:237
  28.8 11.2 %collective-permute-start.9 = (bf16[160,384]{1,0:T(8,128)(2,1)S(1)}, bf16[160,384]{1,0:T(8,128)(2,1)S(1)}, u32[]{:S(2)}, u32[]{:S(2)}) collective-permute-start(bf16[160,384]{1,0:T(8,128)(2,1)S(1)} %get-tuple-element.24.refs_0_), channel_id=1, source_target_pairs={{0,4},{4,0},{8,12},{12,8},{1,5},{5,1},{9,13},{13,9},{2,6},{6,2},{1... | collective-permute-start | bytes 368648 | tf_op jit(solution)/shard_map/ppermute | solution.py:237
  29.3 13.8 %collective-permute-start.6 = (bf16[160,384]{1,0:T(8,128)(2,1)S(1)}, bf16[160,384]{1,0:T(8,128)(2,1)S(1)}, u32[]{:S(2)}, u32[]{:S(2)}) collective-permute-start(bf16[160,384]{1,0:T(8,128)(2,1)S(1)} %get-tuple-element.22.refs_0_), channel_id=1, source_target_pairs={{0,4},{4,0},{8,12},{12,8},{1,5},{5,1},{9,13},{13,9},{2,6},{6,2},{1... | collective-permute-start | bytes 368648 | tf_op jit(solution)/shard_map/ppermute | solution.py:237
  30.9 17.2 %collective-permute-start.7 = (bf16[160,384]{1,0:T(8,128)(2,1)S(1)}, bf16[160,384]{1,0:T(8,128)(2,1)S(1)}, u32[]{:S(2)}, u32[]{:S(2)}) collective-permute-start(bf16[160,384]{1,0:T(8,128)(2,1)S(1)} %get-tuple-element.22.refs_0_), channel_id=1, source_target_pairs={{0,8},{4,12},{8,0},{12,4},{1,9},{5,13},{9,1},{13,5},{2,10},{6,14},... | collective-permute-start | bytes 368648 | tf_op jit(solution)/shard_map/ppermute | solution.py:237
  37.5 10.5 %collective-permute-start.8 = (bf16[160,384]{1,0:T(8,128)(2,1)S(1)}, bf16[160,384]{1,0:T(8,128)(2,1)S(1)}, u32[]{:S(2)}, u32[]{:S(2)}) collective-permute-start(bf16[160,384]{1,0:T(8,128)(2,1)S(1)} %get-tuple-element.22.refs_0_), channel_id=1, source_target_pairs={{0,12},{4,8},{8,4},{12,0},{1,13},{5,9},{9,5},{13,1},{2,14},{6,10},... | collective-permute-start | bytes 368648 | tf_op jit(solution)/shard_map/ppermute | solution.py:237
  41.0 8.1 %collective-permute-start.14 = (bf16[80,1280]{1,0:T(8,128)(2,1)S(1)}, bf16[80,1280]{1,0:T(8,128)(2,1)S(1)}, u32[]{:S(2)}, u32[]{:S(2)}) collective-permute-start(bf16[80,1280]{1,0:T(8,128)(2,1)S(1)} %get-tuple-element.27), channel_id=1, source_target_pairs={{0,2},{2,0},{1,3},{3,1},{4,6},{6,4},{5,7},{7,5},{8,10},{10,8},{9,1... | collective-permute-start | bytes 614408 | tf_op jit(solution)/shard_map/ppermute | solution.py:327
  41.6 13.8 %copy-start.4 = (f32[1280]{0:T(1024)S(1)}, f32[1280]{0:T(1024)}, u32[]{:S(2)}) copy-start(f32[1280]{0:T(1024)} %param.12) | copy-start | bytes 15364
  41.6 13.8 %copy-start.3 = (s32[4]{0:T(128)S(1)}, s32[4]{0:T(128)}, u32[]{:S(2)}) copy-start(s32[4]{0:T(128)} %flags.1) | copy-start | bytes 52
  41.6 13.7 %collective-permute-start.12 = (bf16[80,1280]{1,0:T(8,128)(2,1)S(1)}, bf16[80,1280]{1,0:T(8,128)(2,1)S(1)}, u32[]{:S(2)}, u32[]{:S(2)}) collective-permute-start(bf16[80,1280]{1,0:T(8,128)(2,1)S(1)} %get-tuple-element.25), channel_id=1, source_target_pairs={{0,2},{2,0},{1,3},{3,1},{4,6},{6,4},{5,7},{7,5},{8,10},{10,8},{9,1... | collective-permute-start | bytes 614408 | tf_op jit(solution)/shard_map/ppermute | solution.py:327
  48.0 7.4 %copy-start = (f32[4,160,1280]{2,1,0:T(8,128)S(1)}, f32[4,160,1280]{2,1,0:T(8,128)}, u32[]{:S(2)}) copy-start(f32[4,160,1280]{2,1,0:T(8,128)} %cached.1) | copy-start | bytes 9830404
  49.0 6.5 %copy-start.2 = (f32[160,1280]{1,0:T(8,128)S(1)}, f32[160,1280]{1,0:T(8,128)}, u32[]{:S(2)}) copy-start(f32[160,1280]{1,0:T(8,128)} %hidden.1) | copy-start | bytes 2457604
  49.1 15.7 %collective-permute-start.15 = (bf16[80,1280]{1,0:T(8,128)(2,1)S(1)}, bf16[80,1280]{1,0:T(8,128)(2,1)S(1)}, u32[]{:S(2)}, u32[]{:S(2)}) collective-permute-start(bf16[80,1280]{1,0:T(8,128)(2,1)S(1)} %shard_map.102), channel_id=1, source_target_pairs={{0,0},{1,4},{2,8},{3,12},{4,1},{5,5},{6,9},{7,13},{8,2},{9,6},{10,... | collective-permute-start | bytes 614408 | tf_op jit(solution)/shard_map/ppermute | solution.py:335
  55.3 10.4 %collective-permute-start.13 = (bf16[80,1280]{1,0:T(8,128)(2,1)S(1)}, bf16[80,1280]{1,0:T(8,128)(2,1)S(1)}, u32[]{:S(2)}, u32[]{:S(2)}) collective-permute-start(bf16[80,1280]{1,0:T(8,128)(2,1)S(1)} %shard_map.100), channel_id=1, source_target_pairs={{0,8},{1,12},{2,0},{3,4},{4,9},{5,13},{6,1},{7,5},{8,10},{9,14},{1... | collective-permute-start | bytes 614408 | tf_op jit(solution)/shard_map/ppermute | solution.py:335

commit v21 on v20

--- a/solution.py
+++ b/solution.py
@@ -285,6 +285,8 @@
     )
     late_weight, _ = lax.optimization_barrier((out_weight, packed[0]))
     weight_c = lax.ppermute(late_weight, "head", swap)
+    packed = list(packed)
+    packed[1], packed[3], _ = lax.optimization_barrier((packed[1], packed[3], weight_c))
     moved = []
     for k in range(4):
         k1, k0 = k // 2, 1 - k % 2

time: 66.8 us -> 66.8 us (level)
  waiting for transfers between devices: 31.2 us -> 28.8 us
  starting transfers between devices: 27 us -> 29.3 us
    ppermute x4, waiting for transfers between devices: 11.4 us -> 7.62 us  [local_heads(): moved.append(lax.ppermute(packed[k], ('seq', 'head'), pairs))]
    ppermute x4, starting transfers between devices: 6.17 us -> 8.5 us  [local_heads(): moved.append(lax.ppermute(packed[k], ('seq', 'head'), pairs))]
    ppermute x1, waiting for transfers between devices: 0.01 us -> 1.51 us  [local_heads(): weight_c = lax.ppermute(late_weight, 'head', swap)]
  transfers between devices with their start and end apart: 16 -> 16, of which waited for: 8 -> 8; matrix products, arithmetic and copies ran while one was open for 0% -> 0% of each run, Pallas kernels for 6% -> 5%
where the time goes in v21:
time: 66.8 us; the launch traced here: 66.7 us
  starting transfers between devices  29.3 us (44%)
  waiting for transfers between devices  28.8 us (43%)
  Pallas kernels  7.62 us (11%)
  between operations  0.8 us (1%)
    ppermute x6, starting transfers between devices, along(): return lax.ppermute(shard, 'seq', [(z, z ^ m) for z in range(4)])  10.3 us
    ppermute x6, waiting for transfers between devices, along(): return lax.ppermute(shard, 'seq', [(z, z ^ m) for z in range(4)])  9.61 us
    ppermute x2, waiting for transfers between devices, local_heads(): owned.append(lax.ppermute(summed, ('seq', 'wt', 'head'), pairs))  8.54 us
    ppermute x4, starting transfers between devices, local_heads(): moved.append(lax.ppermute(packed[k], ('seq', 'head'), pairs))  8.5 us
    ppermute x4, waiting for transfers between devices, local_heads(): moved.append(lax.ppermute(packed[k], ('seq', 'head'), pairs))  7.62 us
    ppermute x2, starting transfers between devices, local_heads(): owned.append(lax.ppermute(summed, ('seq', 'wt', 'head'), pairs))  6.23 us
    pallas_call x8, Pallas kernels, call(): pl.pallas_call(kernel, in_specs=[pl.BlockSpec(memory_space=place) for pla...  5.72 us
    ppermute x1, starting transfers between devices, local_heads(): sibling = lax.ppermute(joined, 'head', swap)  2.13 us
  transfers between devices with their start and end apart: 16, of which 8 were waited for; matrix products, arithmetic and copies ran while one was open for 0% of the time, Pallas kernels for 5%

profile of v21, /device:TPU:2, one launch (start us, length us, event | category | flops | bytes accessed | tf_op | source)
XLA Modules:
  0.0 66.7 jit_solution(245593756919570866)
XLA Ops:
  0.6 0.0 copy-start.1
  0.6 1.4 %shard_map.95 = (bf16[320,384]{1,0:T(8,128)(2,1)S(1)}, bf16[320,384]{1,0:T(8,128)(2,1)S(1)}, bf16[160,384]{1,0:T(8,128)(2,1)S(1)}, bf16[160,384]{1,0:T(8,128)(2,1)S(1)}) custom-call(bf16[160,768]{1,0:T(8,128)(2,1)} %queries.1, bf16[160,768]{1,0:T(8,128)(2,1)} %keys.1, bf16[160,768]{1,0:T(8,128)(2,1)} %values.1), custom_call_target="tpu_custom_call" | custom-call | tf_op jit(solution)/shard_map/pallas_call | solution.py:251
  2.0 0.1 collective-permute-start.1
  2.1 2.7 %collective-permute-start = (bf16[320,384]{1,0:T(8,128)(2,1)S(1)}, bf16[320,384]{1,0:T(8,128)(2,1)S(1)}, u32[]{:S(2)}, u32[]{:S(2)}) collective-permute-start(bf16[320,384]{1,0:T(8,128)(2,1)S(1)} %get-tuple-element.18), channel_id=1, source_target_pairs={{0,8},{1,12},{4,9},{5,13},{8,0},{9,4},{12,1},{13,5},{2,10},{3,14},... | collective-permute-start | bytes 737288 | tf_op jit(solution)/shard_map/ppermute | solution.py:298
  4.8 1.5 %collective-permute-done.1.refs_5_ = bf16[768,1280]{1,0:T(8,128)(2,1)S(1)} collective-permute-done((bf16[768,1280]{1,0:T(8,128)(2,1)}, bf16[768,1280]{1,0:T(8,128)(2,1)S(1)}, u32[]{:S(2)}, u32[]{:S(2)}) %collective-permute-start.1) | collective-permute-done | bytes 1966112 | tf_op jit(solution)/shard_map/ppermute | solution.py:287
  6.3 0.7 collective-permute-start.2
  6.9 5.2 %collective-permute-start.3 = (bf16[160,384]{1,0:T(8,128)(2,1)S(1)}, bf16[160,384]{1,0:T(8,128)(2,1)S(1)}, u32[]{:S(2)}, u32[]{:S(2)}) collective-permute-start(bf16[160,384]{1,0:T(8,128)(2,1)S(1)} %get-tuple-element.23), channel_id=1, source_target_pairs={{0,9},{1,13},{4,8},{5,12},{8,1},{9,5},{12,0},{13,4},{2,11},{3,15},... | collective-permute-start | bytes 368648 | tf_op jit(solution)/shard_map/ppermute | solution.py:298
  12.1 0.0 collective-permute-start.4
  12.1 6.6 %collective-permute-done.3.refs_2_ = bf16[160,384]{1,0:T(8,128)(2,1)S(1)} collective-permute-done((bf16[160,384]{1,0:T(8,128)(2,1)S(1)}, bf16[160,384]{1,0:T(8,128)(2,1)S(1)}, u32[]{:S(2)}, u32[]{:S(2)}) %collective-permute-start.3) | collective-permute-done | bytes 122912 | tf_op jit(solution)/shard_map/ppermute | solution.py:298
  18.8 1.0 %collective-permute-done.refs_0_ = bf16[320,384]{1,0:T(8,128)(2,1)S(1)} collective-permute-done((bf16[320,384]{1,0:T(8,128)(2,1)S(1)}, bf16[320,384]{1,0:T(8,128)(2,1)S(1)}, u32[]{:S(2)}, u32[]{:S(2)}) %collective-permute-start) | collective-permute-done | bytes 245792 | tf_op jit(solution)/shard_map/ppermute | solution.py:298
  19.7 0.0 collective-permute-done.4.refs_3_
  19.7 0.0 collective-permute-done.2.refs_1_
  19.8 2.1 %collective-permute-start.5 = (bf16[640,384]{1,0:T(8,128)(2,1)S(1)}, bf16[640,384]{1,0:T(8,128)(2,1)S(1)}, u32[]{:S(2)}, u32[]{:S(2)}) collective-permute-start(bf16[640,384]{1,0:T(8,128)(2,1)S(1)} %shard_map.96), channel_id=1, source_target_pairs={{0,1},{1,0},{2,3},{3,2},{4,5},{5,4},{6,7},{7,6},{8,9},{9,8},{10,11... | collective-permute-start | bytes 1474568 | tf_op jit(solution)/shard_map/ppermute | solution.py:300
  21.9 1.5 %collective-permute-done.5.refs_4_ = bf16[640,384]{1,0:T(8,128)(2,1)S(1)} collective-permute-done((bf16[640,384]{1,0:T(8,128)(2,1)S(1)}, bf16[640,384]{1,0:T(8,128)(2,1)S(1)}, u32[]{:S(2)}, u32[]{:S(2)}) %collective-permute-start.5) | collective-permute-done | bytes 491552 | tf_op jit(solution)/shard_map/ppermute | solution.py:300
  23.4 1.6 %shard_map.97 = (bf16[160,384]{1,0:T(8,128)(2,1)S(1)}, bf16[160,384]{1,0:T(8,128)(2,1)S(1)}) custom-call(bf16[320,384]{1,0:T(8,128)(2,1)S(1)} %collective-permute-done.refs_0_, bf16[320,384]{1,0:T(8,128)(2,1)S(1)} %collective-permute-done.2.refs_1_, bf16[160,384]{1,0:T(8,128)(2,1)S(1)} %collective-permute-done.3.refs_2_, ...), custom_call_target="tpu_custom_call" | custom-call | flops 314572800 | tf_op jit(solution)/shard_map/pallas_call | solution.py:251
  25.0 2.4 %collective-permute-start.10 = (bf16[160,384]{1,0:T(8,128)(2,1)S(1)}, bf16[160,384]{1,0:T(8,128)(2,1)S(1)}, u32[]{:S(2)}, u32[]{:S(2)}) collective-permute-start(bf16[160,384]{1,0:T(8,128)(2,1)S(1)} %get-tuple-element.28.refs_0_), channel_id=1, source_target_pairs={{0,8},{4,12},{8,0},{12,4},{1,9},{5,13},{9,1},{13,5},{2,10},{6,14},... | collective-permute-start | bytes 368648 | tf_op jit(solution)/shard_map/ppermute | solution.py:237
  27.5 1.3 %collective-permute-start.11 = (bf16[160,384]{1,0:T(8,128)(2,1)S(1)}, bf16[160,384]{1,0:T(8,128)(2,1)S(1)}, u32[]{:S(2)}, u32[]{:S(2)}) collective-permute-start(bf16[160,384]{1,0:T(8,128)(2,1)S(1)} %get-tuple-element.28.refs_0_), channel_id=1, source_target_pairs={{0,12},{4,8},{8,4},{12,0},{1,13},{5,9},{9,5},{13,1},{2,14},{6,10},... | collective-permute-start | bytes 368648 | tf_op jit(solution)/shard_map/ppermute | solution.py:237
  28.8 0.5 collective-permute-start.9
  29.3 1.5 %collective-permute-start.6 = (bf16[160,384]{1,0:T(8,128)(2,1)S(1)}, bf16[160,384]{1,0:T(8,128)(2,1)S(1)}, u32[]{:S(2)}, u32[]{:S(2)}) collective-permute-start(bf16[160,384]{1,0:T(8,128)(2,1)S(1)} %get-tuple-element.26.refs_0_), channel_id=1, source_target_pairs={{0,4},{4,0},{8,12},{12,8},{1,5},{5,1},{9,13},{13,9},{2,6},{6,2},{1... | collective-permute-start | bytes 368648 | tf_op jit(solution)/shard_map/ppermute | solution.py:237
  30.8 1.9 %collective-permute-start.7 = (bf16[160,384]{1,0:T(8,128)(2,1)S(1)}, bf16[160,384]{1,0:T(8,128)(2,1)S(1)}, u32[]{:S(2)}, u32[]{:S(2)}) collective-permute-start(bf16[160,384]{1,0:T(8,128)(2,1)S(1)} %get-tuple-element.26.refs_0_), channel_id=1, source_target_pairs={{0,8},{4,12},{8,0},{12,4},{1,9},{5,13},{9,1},{13,5},{2,10},{6,14},... | collective-permute-start | bytes 368648 | tf_op jit(solution)/shard_map/ppermute | solution.py:237
  32.8 4.7 %collective-permute-done.10.refs_2_ = bf16[160,384]{1,0:T(8,128)(2,1)S(1)} collective-permute-done((bf16[160,384]{1,0:T(8,128)(2,1)S(1)}, bf16[160,384]{1,0:T(8,128)(2,1)S(1)}, u32[]{:S(2)}, u32[]{:S(2)}) %collective-permute-start.10) | collective-permute-done | bytes 122912 | tf_op jit(solution)/shard_map/ppermute | solution.py:237
  37.5 2.6 %collective-permute-start.8 = (bf16[160,384]{1,0:T(8,128)(2,1)S(1)}, bf16[160,384]{1,0:T(8,128)(2,1)S(1)}, u32[]{:S(2)}, u32[]{:S(2)}) collective-permute-start(bf16[160,384]{1,0:T(8,128)(2,1)S(1)} %get-tuple-element.26.refs_0_), channel_id=1, source_target_pairs={{0,12},{4,8},{8,4},{12,0},{1,13},{5,9},{9,5},{13,1},{2,14},{6,10},... | collective-permute-start | bytes 368648 | tf_op jit(solution)/shard_map/ppermute | solution.py:237
  40.0 0.0 collective-permute-done.11.refs_3_
  40.0 0.0 collective-permute-done.9.refs_1_
  40.0 0.0 copy-done.1
  40.1 0.9 %shard_map.99 = (bf16[80,1280]{1,0:T(8,128)(2,1)S(1)}, bf16[80,1280]{1,0:T(8,128)(2,1)S(1)}) custom-call(bf16[160,384]{1,0:T(8,128)(2,1)S(1)} %get-tuple-element.28.refs_0_, bf16[160,384]{1,0:T(8,128)(2,1)S(1)} %collective-permute-done.9.refs_1_, bf16[160,384]{1,0:T(8,128)(2,1)S(1)} %collective-permute-done.10.refs_2_, ...), custom_call_target="tpu_custom_call" | custom-call | flops 629145600 | tf_op jit(solution)/shard_map/pallas_call | solution.py:251
  41.0 0.6 collective-permute-start.14
  41.6 0.0 copy-start.4
  41.6 1.5 %collective-permute-start.12 = (bf16[80,1280]{1,0:T(8,128)(2,1)S(1)}, bf16[80,1280]{1,0:T(8,128)(2,1)S(1)}, u32[]{:S(2)}, u32[]{:S(2)}) collective-permute-start(bf16[80,1280]{1,0:T(8,128)(2,1)S(1)} %get-tuple-element.29), channel_id=1, source_target_pairs={{0,2},{2,0},{1,3},{3,1},{4,6},{6,4},{5,7},{7,5},{8,10},{10,8},{9,1... | collective-permute-start | bytes 614408 | tf_op jit(solution)/shard_map/ppermute | solution.py:329
  43.1 0.0 collective-permute-done.6.refs_1_
  43.1 4.9 %collective-permute-done.7.refs_2_ = bf16[160,384]{1,0:T(8,128)(2,1)S(1)} collective-permute-done((bf16[160,384]{1,0:T(8,128)(2,1)S(1)}, bf16[160,384]{1,0:T(8,128)(2,1)S(1)}, u32[]{:S(2)}, u32[]{:S(2)}) %collective-permute-start.7) | collective-permute-done | bytes 122912 | tf_op jit(solution)/shard_map/ppermute | solution.py:237
  48.0 0.0 collective-permute-done.8.refs_3_
  48.0 0.9 %shard_map.98 = (f32[80,1280]{1,0:T(8,128)S(1)}, f32[80,1280]{1,0:T(8,128)S(1)}) custom-call(bf16[160,384]{1,0:T(8,128)(2,1)S(1)} %get-tuple-element.26.refs_0_, bf16[160,384]{1,0:T(8,128)(2,1)S(1)} %collective-permute-done.6.refs_1_, bf16[160,384]{1,0:T(8,128)(2,1)S(1)} %collective-permute-done.7.refs_2_, ...), custom_call_target="tpu_custom_call" | custom-call | flops 5033164800 | tf_op jit(solution)/shard_map/pallas_call | solution.py:251
  48.9 0.0 copy-start.2
  49.0 0.1 collective-permute-done.14.arrived
  49.0 0.1 shard_map.102
  49.1 6.2 %collective-permute-start.15 = (bf16[80,1280]{1,0:T(8,128)(2,1)S(1)}, bf16[80,1280]{1,0:T(8,128)(2,1)S(1)}, u32[]{:S(2)}, u32[]{:S(2)}) collective-permute-start(bf16[80,1280]{1,0:T(8,128)(2,1)S(1)} %shard_map.102), channel_id=1, source_target_pairs={{0,0},{1,4},{2,8},{3,12},{4,1},{5,5},{6,9},{7,13},{8,2},{9,6},{10,... | collective-permute-start | bytes 614408 | tf_op jit(solution)/shard_map/ppermute | solution.py:337
  55.3 0.0 collective-permute-done.12.arrived
  55.3 0.1 collective-permute-start.13
  55.4 0.0 copy-done.4
  55.4 0.0 copy-done.3
  55.4 0.0 copy-done
  55.4 0.0 copy-done.2
  55.4 0.8 %shard_map.101.resting = f32[160,1280]{1,0:T(8,128)S(1)} custom-call(s32[4]{0:T(128)S(1)} %copy-done.3, f32[160,1280]{1,0:T(8,128)S(1)} %copy-done.2, f32[4,160,1280]{2,1,0:T(8,128)S(1)} %copy-done), custom_call_target="tpu_custom_call" | custom-call | tf_op jit(solution)/shard_map/pallas_call | solution.py:251
  56.2 8.5 %collective-permute-done.15.owned = bf16[80,1280]{1,0:T(8,128)(2,1)S(1)} collective-permute-done((bf16[80,1280]{1,0:T(8,128)(2,1)S(1)}, bf16[80,1280]{1,0:T(8,128)(2,1)S(1)}, u32[]{:S(2)}, u32[]{:S(2)}) %collective-permute-start.15) | collective-permute-done | bytes 204832 | tf_op jit(solution)/shard_map/ppermute | solution.py:337
  64.7 0.9 %shard_map.103 = (f32[160,1280]{1,0:T(8,128)}, f32[160,1280]{1,0:T(8,128)}) custom-call(bf16[80,1280]{1,0:T(8,128)(2,1)S(1)} %collective-permute-done.15.owned, f32[1,1280]{1,0:T(1,128)S(1)} %broadcast_in_dim.3.gate, f32[160,1280]{1,0:T(8,128)S(1)} %shard_map.101.resting), custom_call_target="tpu_custom_call" | custom-call | tf_op jit(solution)/shard_map/pallas_call | solution.py:344
  65.7 0.0 collective-permute-done.13.owned
  65.7 1.0 %shard_map.104 = (f32[160,1280]{1,0:T(8,128)}, f32[160,1280]{1,0:T(8,128)}) custom-call(bf16[80,1280]{1,0:T(8,128)(2,1)S(1)} %collective-permute-done.13.owned, f32[1,1280]{1,0:T(1,128)S(1)} %broadcast_in_dim.3.gate, f32[160,1280]{1,0:T(8,128)S(1)} %shard_map.101.resting, ...), custom_call_target="tpu_custom_call", output_to_operand_aliasing={{0}: (3, {}), {1}: (4, {})} | custom-call | tf_op jit(solution)/shard_map/pallas_call | solution.py:344
  (5 shorter events, 0.1 us)
Async XLA Ops:
  0.6 39.4 %copy-start.1 = (bf16[768,1280]{1,0:T(8,128)(2,1)S(1)}, bf16[768,1280]{1,0:T(8,128)(2,1)}, u32[]{:S(2)}) copy-start(bf16[768,1280]{1,0:T(8,128)(2,1)} %refs_4_.3) | copy-start | bytes 5898244
  2.0 4.2 %collective-permute-start.1 = (bf16[768,1280]{1,0:T(8,128)(2,1)}, bf16[768,1280]{1,0:T(8,128)(2,1)S(1)}, u32[]{:S(2)}, u32[]{:S(2)}) collective-permute-start(bf16[768,1280]{1,0:T(8,128)(2,1)} %refs_4_.3), channel_id=1, source_target_pairs={{0,1},{1,0},{2,3},{3,2},{4,5},{5,4},{6,7},{7,6},{8,9},{9,8},{10,11... | collective-permute-start | bytes 5898248 | tf_op jit(solution)/shard_map/ppermute | solution.py:287
  2.1 17.6 %collective-permute-start = (bf16[320,384]{1,0:T(8,128)(2,1)S(1)}, bf16[320,384]{1,0:T(8,128)(2,1)S(1)}, u32[]{:S(2)}, u32[]{:S(2)}) collective-permute-start(bf16[320,384]{1,0:T(8,128)(2,1)S(1)} %get-tuple-element.18), channel_id=1, source_target_pairs={{0,8},{1,12},{4,9},{5,13},{8,0},{9,4},{12,1},{13,5},{2,10},{3,14},... | collective-permute-start | bytes 737288 | tf_op jit(solution)/shard_map/ppermute | solution.py:298
  6.3 13.5 %collective-permute-start.2 = (bf16[320,384]{1,0:T(8,128)(2,1)S(1)}, bf16[320,384]{1,0:T(8,128)(2,1)S(1)}, u32[]{:S(2)}, u32[]{:S(2)}) collective-permute-start(bf16[320,384]{1,0:T(8,128)(2,1)S(1)} %get-tuple-element.22), channel_id=1, source_target_pairs={{0,0},{1,4},{4,1},{5,5},{8,8},{9,12},{12,9},{13,13},{2,2},{3,6},{6... | collective-permute-start | bytes 737288 | tf_op jit(solution)/shard_map/ppermute | solution.py:298
  6.9 11.8 %collective-permute-start.3 = (bf16[160,384]{1,0:T(8,128)(2,1)S(1)}, bf16[160,384]{1,0:T(8,128)(2,1)S(1)}, u32[]{:S(2)}, u32[]{:S(2)}) collective-permute-start(bf16[160,384]{1,0:T(8,128)(2,1)S(1)} %get-tuple-element.23), channel_id=1, source_target_pairs={{0,9},{1,13},{4,8},{5,12},{8,1},{9,5},{12,0},{13,4},{2,11},{3,15},... | collective-permute-start | bytes 368648 | tf_op jit(solution)/shard_map/ppermute | solution.py:298
  12.1 7.6 %collective-permute-start.4 = (bf16[160,384]{1,0:T(8,128)(2,1)S(1)}, bf16[160,384]{1,0:T(8,128)(2,1)S(1)}, u32[]{:S(2)}, u32[]{:S(2)}) collective-permute-start(bf16[160,384]{1,0:T(8,128)(2,1)S(1)} %get-tuple-element.24), channel_id=1, source_target_pairs={{0,1},{1,5},{4,0},{5,4},{8,9},{9,13},{12,8},{13,12},{2,3},{3,7},{6... | collective-permute-start | bytes 368648 | tf_op jit(solution)/shard_map/ppermute | solution.py:298
  19.8 3.6 %collective-permute-start.5 = (bf16[640,384]{1,0:T(8,128)(2,1)S(1)}, bf16[640,384]{1,0:T(8,128)(2,1)S(1)}, u32[]{:S(2)}, u32[]{:S(2)}) collective-permute-start(bf16[640,384]{1,0:T(8,128)(2,1)S(1)} %shard_map.96), channel_id=1, source_target_pairs={{0,1},{1,0},{2,3},{3,2},{4,5},{5,4},{6,7},{7,6},{8,9},{9,8},{10,11... | collective-permute-start | bytes 1474568 | tf_op jit(solution)/shard_map/ppermute | solution.py:300
  25.0 12.4 %collective-permute-start.10 = (bf16[160,384]{1,0:T(8,128)(2,1)S(1)}, bf16[160,384]{1,0:T(8,128)(2,1)S(1)}, u32[]{:S(2)}, u32[]{:S(2)}) collective-permute-start(bf16[160,384]{1,0:T(8,128)(2,1)S(1)} %get-tuple-element.28.refs_0_), channel_id=1, source_target_pairs={{0,8},{4,12},{8,0},{12,4},{1,9},{5,13},{9,1},{13,5},{2,10},{6,14},... | collective-permute-start | bytes 368648 | tf_op jit(solution)/shard_map/ppermute | solution.py:237
  27.5 12.6 %collective-permute-start.11 = (bf16[160,384]{1,0:T(8,128)(2,1)S(1)}, bf16[160,384]{1,0:T(8,128)(2,1)S(1)}, u32[]{:S(2)}, u32[]{:S(2)}) collective-permute-start(bf16[160,384]{1,0:T(8,128)(2,1)S(1)} %get-tuple-element.28.refs_0_), channel_id=1, source_target_pairs={{0,12},{4,8},{8,4},{12,0},{1,13},{5,9},{9,5},{13,1},{2,14},{6,10},... | collective-permute-start | bytes 368648 | tf_op jit(solution)/shard_map/ppermute | solution.py:237
  28.8 11.2 %collective-permute-start.9 = (bf16[160,384]{1,0:T(8,128)(2,1)S(1)}, bf16[160,384]{1,0:T(8,128)(2,1)S(1)}, u32[]{:S(2)}, u32[]{:S(2)}) collective-permute-start(bf16[160,384]{1,0:T(8,128)(2,1)S(1)} %get-tuple-element.28.refs_0_), channel_id=1, source_target_pairs={{0,4},{4,0},{8,12},{12,8},{1,5},{5,1},{9,13},{13,9},{2,6},{6,2},{1... | collective-permute-start | bytes 368648 | tf_op jit(solution)/shard_map/ppermute | solution.py:237
  29.3 13.8 %collective-permute-start.6 = (bf16[160,384]{1,0:T(8,128)(2,1)S(1)}, bf16[160,384]{1,0:T(8,128)(2,1)S(1)}, u32[]{:S(2)}, u32[]{:S(2)}) collective-permute-start(bf16[160,384]{1,0:T(8,128)(2,1)S(1)} %get-tuple-element.26.refs_0_), channel_id=1, source_target_pairs={{0,4},{4,0},{8,12},{12,8},{1,5},{5,1},{9,13},{13,9},{2,6},{6,2},{1... | collective-permute-start | bytes 368648 | tf_op jit(solution)/shard_map/ppermute | solution.py:237
  30.8 17.2 %collective-permute-start.7 = (bf16[160,384]{1,0:T(8,128)(2,1)S(1)}, bf16[160,384]{1,0:T(8,128)(2,1)S(1)}, u32[]{:S(2)}, u32[]{:S(2)}) collective-permute-start(bf16[160,384]{1,0:T(8,128)(2,1)S(1)} %get-tuple-element.26.refs_0_), channel_id=1, source_target_pairs={{0,8},{4,12},{8,0},{12,4},{1,9},{5,13},{9,1},{13,5},{2,10},{6,14},... | collective-permute-start | bytes 368648 | tf_op jit(solution)/shard_map/ppermute | solution.py:237
  37.5 10.5 %collective-permute-start.8 = (bf16[160,384]{1,0:T(8,128)(2,1)S(1)}, bf16[160,384]{1,0:T(8,128)(2,1)S(1)}, u32[]{:S(2)}, u32[]{:S(2)}) collective-permute-start(bf16[160,384]{1,0:T(8,128)(2,1)S(1)} %get-tuple-element.26.refs_0_), channel_id=1, source_target_pairs={{0,12},{4,8},{8,4},{12,0},{1,13},{5,9},{9,5},{13,1},{2,14},{6,10},... | collective-permute-start | bytes 368648 | tf_op jit(solution)/shard_map/ppermute | solution.py:237
  41.0 8.1 %collective-permute-start.14 = (bf16[80,1280]{1,0:T(8,128)(2,1)S(1)}, bf16[80,1280]{1,0:T(8,128)(2,1)S(1)}, u32[]{:S(2)}, u32[]{:S(2)}) collective-permute-start(bf16[80,1280]{1,0:T(8,128)(2,1)S(1)} %get-tuple-element.31), channel_id=1, source_target_pairs={{0,2},{2,0},{1,3},{3,1},{4,6},{6,4},{5,7},{7,5},{8,10},{10,8},{9,1... | collective-permute-start | bytes 614408 | tf_op jit(solution)/shard_map/ppermute | solution.py:329
  41.6 13.8 %copy-start.4 = (f32[1280]{0:T(1024)S(1)}, f32[1280]{0:T(1024)}, u32[]{:S(2)}) copy-start(f32[1280]{0:T(1024)} %param.12) | copy-start | bytes 15364
  41.6 13.8 %copy-start.3 = (s32[4]{0:T(128)S(1)}, s32[4]{0:T(128)}, u32[]{:S(2)}) copy-start(s32[4]{0:T(128)} %flags.1) | copy-start | bytes 52
  41.6 13.7 %collective-permute-start.12 = (bf16[80,1280]{1,0:T(8,128)(2,1)S(1)}, bf16[80,1280]{1,0:T(8,128)(2,1)S(1)}, u32[]{:S(2)}, u32[]{:S(2)}) collective-permute-start(bf16[80,1280]{1,0:T(8,128)(2,1)S(1)} %get-tuple-element.29), channel_id=1, source_target_pairs={{0,2},{2,0},{1,3},{3,1},{4,6},{6,4},{5,7},{7,5},{8,10},{10,8},{9,1... | collective-permute-start | bytes 614408 | tf_op jit(solution)/shard_map/ppermute | solution.py:329
  48.0 7.4 %copy-start = (f32[4,160,1280]{2,1,0:T(8,128)S(1)}, f32[4,160,1280]{2,1,0:T(8,128)}, u32[]{:S(2)}) copy-start(f32[4,160,1280]{2,1,0:T(8,128)} %cached.1) | copy-start | bytes 9830404
  48.9 6.5 %copy-start.2 = (f32[160,1280]{1,0:T(8,128)S(1)}, f32[160,1280]{1,0:T(8,128)}, u32[]{:S(2)}) copy-start(f32[160,1280]{1,0:T(8,128)} %hidden.1) | copy-start | bytes 2457604
  49.1 15.7 %collective-permute-start.15 = (bf16[80,1280]{1,0:T(8,128)(2,1)S(1)}, bf16[80,1280]{1,0:T(8,128)(2,1)S(1)}, u32[]{:S(2)}, u32[]{:S(2)}) collective-permute-start(bf16[80,1280]{1,0:T(8,128)(2,1)S(1)} %shard_map.102), channel_id=1, source_target_pairs={{0,0},{1,4},{2,8},{3,12},{4,1},{5,5},{6,9},{7,13},{8,2},{9,6},{10,... | collective-permute-start | bytes 614408 | tf_op jit(solution)/shard_map/ppermute | solution.py:337
  55.3 10.4 %collective-permute-start.13 = (bf16[80,1280]{1,0:T(8,128)(2,1)S(1)}, bf16[80,1280]{1,0:T(8,128)(2,1)S(1)}, u32[]{:S(2)}, u32[]{:S(2)}) collective-permute-start(bf16[80,1280]{1,0:T(8,128)(2,1)S(1)} %shard_map.100), channel_id=1, source_target_pairs={{0,8},{1,12},{2,0},{3,4},{4,9},{5,13},{6,1},{7,5},{8,10},{9,14},{1... | collective-permute-start | bytes 614408 | tf_op jit(solution)/shard_map/ppermute | solution.py:337

commit v22 on v20

--- a/solution.py
+++ b/solution.py
@@ -192,10 +192,11 @@
     shards, (weight, weight_c, out0, out1, held) = refs[:4], refs[4:]
     total = multiply(shards, weight, weight_c, held)
     half = out0.shape[0]
-    x = lax.axis_index("wt")
-    for low in range(2):
-        part = total[low * half : (low + 1) * half].astype(out0.dtype)
-        first = flip(x, low) == 1 - kept
+    _, zl = bits()
+    side = lax.rem(lax.axis_index("wt") + zl, 2)
+    for high in range(2):
+        part = total[high * half : (high + 1) * half].astype(out0.dtype)
+        first = flip(side, high) == 1 - kept
 
         @pl.when(first)
         def _():
@@ -221,7 +222,8 @@
     mixed, fresh, mixed_part, fresh_part, sems = refs[-5:]
     half = owned.shape[0]
     zh, _ = bits()
-    rows = pl.ds(pl.multiple_of(flip(zh, piece) * half, 16), half)
+    side = lax.rem(zh + lax.axis_index("head"), 2)
+    rows = pl.ds(pl.multiple_of(flip(side, piece) * half, 16), half)
     delta = owned[...].astype(jnp.float32) * gate[...]
     fresh_part[...] = delta
     copy_fresh = pltpu.make_async_copy(fresh_part, fresh.at[rows, :], sems.at[0])
@@ -330,7 +332,7 @@
         for zz in range(4):
             for xx in range(2):
                 for cc in range(2):
-                    to = ((cc + 2 * (p ^ xx)) * 2 + zz // 2) * 2 + zz % 2
+                    to = ((cc + 2 * (p ^ xx ^ (zz % 2))) * 2 + zz // 2) * 2 + zz % 2
                     pairs.append(((zz * 2 + xx) * 2 + cc, to))
         owned.append(lax.ppermute(summed, ("seq", "wt", "head"), pairs))
     (resting,) = call(

time: 66.8 us -> 66.6 us (level)
  the two profiles are of different devices: /device:TPU:2 before, /device:TPU:14 now
where the time goes in v22:
time: 66.6 us; the launch traced here: 66.5 us
  waiting for transfers between devices  33.4 us (50%)
  starting transfers between devices  24.6 us (37%)
  Pallas kernels  7.62 us (11%)
  between operations  0.83 us (1%)
    ppermute x6, waiting for transfers between devices, along(): return lax.ppermute(shard, 'seq', [(z, z ^ m) for z in range(4)])  13.4 us
    ppermute x4, waiting for transfers between devices, local_heads(): moved.append(lax.ppermute(packed[k], ('seq', 'head'), pairs))  11.6 us
    ppermute x6, starting transfers between devices, along(): return lax.ppermute(shard, 'seq', [(z, z ^ m) for z in range(4)])  8.65 us
    ppermute x2, waiting for transfers between devices, local_heads(): owned.append(lax.ppermute(summed, ('seq', 'wt', 'head'), pairs))  6.98 us
    ppermute x4, starting transfers between devices, local_heads(): moved.append(lax.ppermute(packed[k], ('seq', 'head'), pairs))  6.61 us
    ppermute x2, starting transfers between devices, local_heads(): owned.append(lax.ppermute(summed, ('seq', 'wt', 'head'), pairs))  6.59 us
    pallas_call x8, Pallas kernels, call(): pl.pallas_call(kernel, in_specs=[pl.BlockSpec(memory_space=place) for pla...  5.72 us
    ppermute x2, starting transfers between devices, local_heads(): arrived = lax.ppermute(sent[p], 'wt', swap)  2.09 us
  transfers between devices with their start and end apart: 16, of which 7 were waited for; matrix products, arithmetic and copies ran while one was open for 0% of the time, Pallas kernels for 6%

profile of v22, /device:TPU:14, one launch (start us, length us, event | category | flops | bytes accessed | tf_op | source)
XLA Modules:
  0.0 66.5 jit_solution(11730918906826020561)
XLA Ops:
  0.6 0.0 copy-start.1
  0.6 1.4 %shard_map.95 = (bf16[320,384]{1,0:T(8,128)(2,1)S(1)}, bf16[320,384]{1,0:T(8,128)(2,1)S(1)}, bf16[160,384]{1,0:T(8,128)(2,1)S(1)}, bf16[160,384]{1,0:T(8,128)(2,1)S(1)}) custom-call(bf16[160,768]{1,0:T(8,128)(2,1)} %queries.1, bf16[160,768]{1,0:T(8,128)(2,1)} %keys.1, bf16[160,768]{1,0:T(8,128)(2,1)} %values.1), custom_call_target="tpu_custom_call" | custom-call | tf_op jit(solution)/shard_map/pallas_call | solution.py:253
  2.0 0.1 collective-permute-start.5
  2.1 1.7 %collective-permute-start = (bf16[320,384]{1,0:T(8,128)(2,1)S(1)}, bf16[320,384]{1,0:T(8,128)(2,1)S(1)}, u32[]{:S(2)}, u32[]{:S(2)}) collective-permute-start(bf16[320,384]{1,0:T(8,128)(2,1)S(1)} %get-tuple-element.16), channel_id=1, source_target_pairs={{0,8},{1,12},{4,9},{5,13},{8,0},{9,4},{12,1},{13,5},{2,10},{3,14},... | collective-permute-start | bytes 737288 | tf_op jit(solution)/shard_map/ppermute | solution.py:298
  3.8 4.1 %collective-permute-start.1 = (bf16[320,384]{1,0:T(8,128)(2,1)S(1)}, bf16[320,384]{1,0:T(8,128)(2,1)S(1)}, u32[]{:S(2)}, u32[]{:S(2)}) collective-permute-start(bf16[320,384]{1,0:T(8,128)(2,1)S(1)} %get-tuple-element.17), channel_id=1, source_target_pairs={{0,0},{1,4},{4,1},{5,5},{8,8},{9,12},{12,9},{13,13},{2,2},{3,6},{6... | collective-permute-start | bytes 737288 | tf_op jit(solution)/shard_map/ppermute | solution.py:298
  7.8 0.1 collective-permute-start.2
  7.9 0.8 %collective-permute-start.3 = (bf16[160,384]{1,0:T(8,128)(2,1)S(1)}, bf16[160,384]{1,0:T(8,128)(2,1)S(1)}, u32[]{:S(2)}, u32[]{:S(2)}) collective-permute-start(bf16[160,384]{1,0:T(8,128)(2,1)S(1)} %get-tuple-element.19), channel_id=1, source_target_pairs={{0,1},{1,5},{4,0},{5,4},{8,9},{9,13},{12,8},{13,12},{2,3},{3,7},{6... | collective-permute-start | bytes 368648 | tf_op jit(solution)/shard_map/ppermute | solution.py:298
  8.7 11.6 %collective-permute-done.2.refs_2_ = bf16[160,384]{1,0:T(8,128)(2,1)S(1)} collective-permute-done((bf16[160,384]{1,0:T(8,128)(2,1)S(1)}, bf16[160,384]{1,0:T(8,128)(2,1)S(1)}, u32[]{:S(2)}, u32[]{:S(2)}) %collective-permute-start.2) | collective-permute-done | bytes 122912 | tf_op jit(solution)/shard_map/ppermute | solution.py:298
  20.3 0.0 collective-permute-done.3.refs_3_
  20.3 0.0 collective-permute-done.refs_0_
  20.3 0.0 collective-permute-done.1.refs_1_
  20.4 0.5 collective-permute-start.4
  20.9 1.5 %collective-permute-done.4.refs_4_ = bf16[640,384]{1,0:T(8,128)(2,1)S(1)} collective-permute-done((bf16[640,384]{1,0:T(8,128)(2,1)S(1)}, bf16[640,384]{1,0:T(8,128)(2,1)S(1)}, u32[]{:S(2)}, u32[]{:S(2)}) %collective-permute-start.4) | collective-permute-done | bytes 491552 | tf_op jit(solution)/shard_map/ppermute | solution.py:300
  22.4 0.0 collective-permute-done.5.refs_5_
  22.4 1.6 %shard_map.97 = (bf16[160,384]{1,0:T(8,128)(2,1)S(1)}, bf16[160,384]{1,0:T(8,128)(2,1)S(1)}) custom-call(bf16[320,384]{1,0:T(8,128)(2,1)S(1)} %collective-permute-done.refs_0_, bf16[320,384]{1,0:T(8,128)(2,1)S(1)} %collective-permute-done.1.refs_1_, bf16[160,384]{1,0:T(8,128)(2,1)S(1)} %collective-permute-done.2.refs_2_, ...), custom_call_target="tpu_custom_call" | custom-call | flops 314572800 | tf_op jit(solution)/shard_map/pallas_call | solution.py:253
  24.0 3.7 %collective-permute-start.10 = (bf16[160,384]{1,0:T(8,128)(2,1)S(1)}, bf16[160,384]{1,0:T(8,128)(2,1)S(1)}, u32[]{:S(2)}, u32[]{:S(2)}) collective-permute-start(bf16[160,384]{1,0:T(8,128)(2,1)S(1)} %get-tuple-element.24.refs_0_), channel_id=1, source_target_pairs={{0,8},{4,12},{8,0},{12,4},{1,9},{5,13},{9,1},{13,5},{2,10},{6,14},... | collective-permute-start | bytes 368648 | tf_op jit(solution)/shard_map/ppermute | solution.py:239
  27.7 0.0 collective-permute-start.11
  27.7 1.5 %collective-permute-start.9 = (bf16[160,384]{1,0:T(8,128)(2,1)S(1)}, bf16[160,384]{1,0:T(8,128)(2,1)S(1)}, u32[]{:S(2)}, u32[]{:S(2)}) collective-permute-start(bf16[160,384]{1,0:T(8,128)(2,1)S(1)} %get-tuple-element.24.refs_0_), channel_id=1, source_target_pairs={{0,4},{4,0},{8,12},{12,8},{1,5},{5,1},{9,13},{13,9},{2,6},{6,2},{1... | collective-permute-start | bytes 368648 | tf_op jit(solution)/shard_map/ppermute | solution.py:239
  29.3 0.5 collective-permute-start.6
  29.8 2.6 %collective-permute-start.7 = (bf16[160,384]{1,0:T(8,128)(2,1)S(1)}, bf16[160,384]{1,0:T(8,128)(2,1)S(1)}, u32[]{:S(2)}, u32[]{:S(2)}) collective-permute-start(bf16[160,384]{1,0:T(8,128)(2,1)S(1)} %get-tuple-element.22.refs_0_), channel_id=1, source_target_pairs={{0,8},{4,12},{8,0},{12,4},{1,9},{5,13},{9,1},{13,5},{2,10},{6,14},... | collective-permute-start | bytes 368648 | tf_op jit(solution)/shard_map/ppermute | solution.py:239
  32.3 3.3 %collective-permute-done.10.refs_2_ = bf16[160,384]{1,0:T(8,128)(2,1)S(1)} collective-permute-done((bf16[160,384]{1,0:T(8,128)(2,1)S(1)}, bf16[160,384]{1,0:T(8,128)(2,1)S(1)}, u32[]{:S(2)}, u32[]{:S(2)}) %collective-permute-start.10) | collective-permute-done | bytes 122912 | tf_op jit(solution)/shard_map/ppermute | solution.py:239
  35.7 0.4 collective-permute-start.8
  36.0 3.4 %collective-permute-done.11.refs_3_ = bf16[160,384]{1,0:T(8,128)(2,1)S(1)} collective-permute-done((bf16[160,384]{1,0:T(8,128)(2,1)S(1)}, bf16[160,384]{1,0:T(8,128)(2,1)S(1)}, u32[]{:S(2)}, u32[]{:S(2)}) %collective-permute-start.11) | collective-permute-done | bytes 122912 | tf_op jit(solution)/shard_map/ppermute | solution.py:239
  39.4 0.0 collective-permute-done.9.refs_1_
  39.4 0.0 copy-done.1
  39.4 0.9 %shard_map.99 = (bf16[80,1280]{1,0:T(8,128)(2,1)S(1)}, bf16[80,1280]{1,0:T(8,128)(2,1)S(1)}) custom-call(bf16[160,384]{1,0:T(8,128)(2,1)S(1)} %get-tuple-element.24.refs_0_, bf16[160,384]{1,0:T(8,128)(2,1)S(1)} %collective-permute-done.9.refs_1_, bf16[160,384]{1,0:T(8,128)(2,1)S(1)} %collective-permute-done.10.refs_2_, ...), custom_call_target="tpu_custom_call" | custom-call | flops 629145600 | tf_op jit(solution)/shard_map/pallas_call | solution.py:253
  40.3 0.6 collective-permute-start.14
  40.9 0.0 copy-start.4
  40.9 1.5 %collective-permute-start.12 = (bf16[80,1280]{1,0:T(8,128)(2,1)S(1)}, bf16[80,1280]{1,0:T(8,128)(2,1)S(1)}, u32[]{:S(2)}, u32[]{:S(2)}) collective-permute-start(bf16[80,1280]{1,0:T(8,128)(2,1)S(1)} %get-tuple-element.25), channel_id=1, source_target_pairs={{0,2},{2,0},{1,3},{3,1},{4,6},{6,4},{5,7},{7,5},{8,10},{10,8},{9,1... | collective-permute-start | bytes 614408 | tf_op jit(solution)/shard_map/ppermute | solution.py:329
  42.4 0.0 collective-permute-done.6.refs_1_
  42.4 3.8 %collective-permute-done.7.refs_2_ = bf16[160,384]{1,0:T(8,128)(2,1)S(1)} collective-permute-done((bf16[160,384]{1,0:T(8,128)(2,1)S(1)}, bf16[160,384]{1,0:T(8,128)(2,1)S(1)}, u32[]{:S(2)}, u32[]{:S(2)}) %collective-permute-start.7) | collective-permute-done | bytes 122912 | tf_op jit(solution)/shard_map/ppermute | solution.py:239
  46.2 2.9 %collective-permute-done.8.refs_3_ = bf16[160,384]{1,0:T(8,128)(2,1)S(1)} collective-permute-done((bf16[160,384]{1,0:T(8,128)(2,1)S(1)}, bf16[160,384]{1,0:T(8,128)(2,1)S(1)}, u32[]{:S(2)}, u32[]{:S(2)}) %collective-permute-start.8) | collective-permute-done | bytes 122912 | tf_op jit(solution)/shard_map/ppermute | solution.py:239
  49.1 0.9 %shard_map.98 = (f32[80,1280]{1,0:T(8,128)S(1)}, f32[80,1280]{1,0:T(8,128)S(1)}) custom-call(bf16[160,384]{1,0:T(8,128)(2,1)S(1)} %get-tuple-element.22.refs_0_, bf16[160,384]{1,0:T(8,128)(2,1)S(1)} %collective-permute-done.6.refs_1_, bf16[160,384]{1,0:T(8,128)(2,1)S(1)} %collective-permute-done.7.refs_2_, ...), custom_call_target="tpu_custom_call" | custom-call | flops 5033164800 | tf_op jit(solution)/shard_map/pallas_call | solution.py:253
  50.0 0.0 copy-start.2
  50.0 0.0 collective-permute-done.14.arrived
  50.0 0.1 shard_map.102
  50.1 2.1 %collective-permute-start.15 = (bf16[80,1280]{1,0:T(8,128)(2,1)S(1)}, bf16[80,1280]{1,0:T(8,128)(2,1)S(1)}, u32[]{:S(2)}, u32[]{:S(2)}) collective-permute-start(bf16[80,1280]{1,0:T(8,128)(2,1)S(1)} %shard_map.102), channel_id=1, source_target_pairs={{0,0},{1,4},{2,8},{3,12},{4,9},{5,13},{6,1},{7,5},{8,2},{9,6},{10,... | collective-permute-start | bytes 614408 | tf_op jit(solution)/shard_map/ppermute | solution.py:337
  52.1 0.0 collective-permute-done.12.arrived
  52.2 4.5 %collective-permute-start.13 = (bf16[80,1280]{1,0:T(8,128)(2,1)S(1)}, bf16[80,1280]{1,0:T(8,128)(2,1)S(1)}, u32[]{:S(2)}, u32[]{:S(2)}) collective-permute-start(bf16[80,1280]{1,0:T(8,128)(2,1)S(1)} %shard_map.100), channel_id=1, source_target_pairs={{0,8},{1,12},{2,0},{3,4},{4,1},{5,5},{6,9},{7,13},{8,10},{9,14},{1... | collective-permute-start | bytes 614408 | tf_op jit(solution)/shard_map/ppermute | solution.py:337
  56.7 0.0 copy-done.4
  56.8 0.0 copy-done.3
  56.8 0.0 copy-done
  56.8 0.0 copy-done.2
  56.8 0.8 %shard_map.101.resting = f32[160,1280]{1,0:T(8,128)S(1)} custom-call(s32[4]{0:T(128)S(1)} %copy-done.3, f32[160,1280]{1,0:T(8,128)S(1)} %copy-done.2, f32[4,160,1280]{2,1,0:T(8,128)S(1)} %copy-done), custom_call_target="tpu_custom_call" | custom-call | tf_op jit(solution)/shard_map/pallas_call | solution.py:253
  57.6 7.0 %collective-permute-done.15.owned = bf16[80,1280]{1,0:T(8,128)(2,1)S(1)} collective-permute-done((bf16[80,1280]{1,0:T(8,128)(2,1)S(1)}, bf16[80,1280]{1,0:T(8,128)(2,1)S(1)}, u32[]{:S(2)}, u32[]{:S(2)}) %collective-permute-start.15) | collective-permute-done | bytes 204832 | tf_op jit(solution)/shard_map/ppermute | solution.py:337
  64.5 0.9 %shard_map.103 = (f32[160,1280]{1,0:T(8,128)}, f32[160,1280]{1,0:T(8,128)}) custom-call(bf16[80,1280]{1,0:T(8,128)(2,1)S(1)} %collective-permute-done.15.owned, f32[1,1280]{1,0:T(1,128)S(1)} %broadcast_in_dim.3.gate, f32[160,1280]{1,0:T(8,128)S(1)} %shard_map.101.resting), custom_call_target="tpu_custom_call" | custom-call | tf_op jit(solution)/shard_map/pallas_call | solution.py:344
  65.5 0.0 collective-permute-done.13.owned
  65.5 1.0 %shard_map.104 = (f32[160,1280]{1,0:T(8,128)}, f32[160,1280]{1,0:T(8,128)}) custom-call(bf16[80,1280]{1,0:T(8,128)(2,1)S(1)} %collective-permute-done.13.owned, f32[1,1280]{1,0:T(1,128)S(1)} %broadcast_in_dim.3.gate, f32[160,1280]{1,0:T(8,128)S(1)} %shard_map.101.resting, ...), custom_call_target="tpu_custom_call", output_to_operand_aliasing={{0}: (3, {}), {1}: (4, {})} | custom-call | tf_op jit(solution)/shard_map/pallas_call | solution.py:344
  (5 shorter events, 0.1 us)
Async XLA Ops:
  0.6 38.8 %copy-start.1 = (bf16[768,1280]{1,0:T(8,128)(2,1)S(1)}, bf16[768,1280]{1,0:T(8,128)(2,1)}, u32[]{:S(2)}) copy-start(bf16[768,1280]{1,0:T(8,128)(2,1)} %refs_4_.3) | copy-start | bytes 5898244
  2.0 20.4 %collective-permute-start.5 = (bf16[768,1280]{1,0:T(8,128)(2,1)}, bf16[768,1280]{1,0:T(8,128)(2,1)S(1)}, u32[]{:S(2)}, u32[]{:S(2)}) collective-permute-start(bf16[768,1280]{1,0:T(8,128)(2,1)} %refs_4_.3), channel_id=1, source_target_pairs={{0,1},{1,0},{2,3},{3,2},{4,5},{5,4},{6,7},{7,6},{8,9},{9,8},{10,11... | collective-permute-start | bytes 5898248 | tf_op jit(solution)/shard_map/ppermute | solution.py:289
  2.1 18.2 %collective-permute-start = (bf16[320,384]{1,0:T(8,128)(2,1)S(1)}, bf16[320,384]{1,0:T(8,128)(2,1)S(1)}, u32[]{:S(2)}, u32[]{:S(2)}) collective-permute-start(bf16[320,384]{1,0:T(8,128)(2,1)S(1)} %get-tuple-element.16), channel_id=1, source_target_pairs={{0,8},{1,12},{4,9},{5,13},{8,0},{9,4},{12,1},{13,5},{2,10},{3,14},... | collective-permute-start | bytes 737288 | tf_op jit(solution)/shard_map/ppermute | solution.py:298
  3.8 16.5 %collective-permute-start.1 = (bf16[320,384]{1,0:T(8,128)(2,1)S(1)}, bf16[320,384]{1,0:T(8,128)(2,1)S(1)}, u32[]{:S(2)}, u32[]{:S(2)}) collective-permute-start(bf16[320,384]{1,0:T(8,128)(2,1)S(1)} %get-tuple-element.17), channel_id=1, source_target_pairs={{0,0},{1,4},{4,1},{5,5},{8,8},{9,12},{12,9},{13,13},{2,2},{3,6},{6... | collective-permute-start | bytes 737288 | tf_op jit(solution)/shard_map/ppermute | solution.py:298
  7.8 12.5 %collective-permute-start.2 = (bf16[160,384]{1,0:T(8,128)(2,1)S(1)}, bf16[160,384]{1,0:T(8,128)(2,1)S(1)}, u32[]{:S(2)}, u32[]{:S(2)}) collective-permute-start(bf16[160,384]{1,0:T(8,128)(2,1)S(1)} %get-tuple-element.18), channel_id=1, source_target_pairs={{0,9},{1,13},{4,8},{5,12},{8,1},{9,5},{12,0},{13,4},{2,11},{3,15},... | collective-permute-start | bytes 368648 | tf_op jit(solution)/shard_map/ppermute | solution.py:298
  7.9 12.4 %collective-permute-start.3 = (bf16[160,384]{1,0:T(8,128)(2,1)S(1)}, bf16[160,384]{1,0:T(8,128)(2,1)S(1)}, u32[]{:S(2)}, u32[]{:S(2)}) collective-permute-start(bf16[160,384]{1,0:T(8,128)(2,1)S(1)} %get-tuple-element.19), channel_id=1, source_target_pairs={{0,1},{1,5},{4,0},{5,4},{8,9},{9,13},{12,8},{13,12},{2,3},{3,7},{6... | collective-permute-start | bytes 368648 | tf_op jit(solution)/shard_map/ppermute | solution.py:298
  20.4 2.0 %collective-permute-start.4 = (bf16[640,384]{1,0:T(8,128)(2,1)S(1)}, bf16[640,384]{1,0:T(8,128)(2,1)S(1)}, u32[]{:S(2)}, u32[]{:S(2)}) collective-permute-start(bf16[640,384]{1,0:T(8,128)(2,1)S(1)} %shard_map.96), channel_id=1, source_target_pairs={{0,1},{1,0},{2,3},{3,2},{4,5},{5,4},{6,7},{7,6},{8,9},{9,8},{10,11... | collective-permute-start | bytes 1474568 | tf_op jit(solution)/shard_map/ppermute | solution.py:300
  24.0 11.6 %collective-permute-start.10 = (bf16[160,384]{1,0:T(8,128)(2,1)S(1)}, bf16[160,384]{1,0:T(8,128)(2,1)S(1)}, u32[]{:S(2)}, u32[]{:S(2)}) collective-permute-start(bf16[160,384]{1,0:T(8,128)(2,1)S(1)} %get-tuple-element.24.refs_0_), channel_id=1, source_target_pairs={{0,8},{4,12},{8,0},{12,4},{1,9},{5,13},{9,1},{13,5},{2,10},{6,14},... | collective-permute-start | bytes 368648 | tf_op jit(solution)/shard_map/ppermute | solution.py:239
  27.7 11.6 %collective-permute-start.11 = (bf16[160,384]{1,0:T(8,128)(2,1)S(1)}, bf16[160,384]{1,0:T(8,128)(2,1)S(1)}, u32[]{:S(2)}, u32[]{:S(2)}) collective-permute-start(bf16[160,384]{1,0:T(8,128)(2,1)S(1)} %get-tuple-element.24.refs_0_), channel_id=1, source_target_pairs={{0,12},{4,8},{8,4},{12,0},{1,13},{5,9},{9,5},{13,1},{2,14},{6,10},... | collective-permute-start | bytes 368648 | tf_op jit(solution)/shard_map/ppermute | solution.py:239
  27.7 11.6 %collective-permute-start.9 = (bf16[160,384]{1,0:T(8,128)(2,1)S(1)}, bf16[160,384]{1,0:T(8,128)(2,1)S(1)}, u32[]{:S(2)}, u32[]{:S(2)}) collective-permute-start(bf16[160,384]{1,0:T(8,128)(2,1)S(1)} %get-tuple-element.24.refs_0_), channel_id=1, source_target_pairs={{0,4},{4,0},{8,12},{12,8},{1,5},{5,1},{9,13},{13,9},{2,6},{6,2},{1... | collective-permute-start | bytes 368648 | tf_op jit(solution)/shard_map/ppermute | solution.py:239
  29.3 13.1 %collective-permute-start.6 = (bf16[160,384]{1,0:T(8,128)(2,1)S(1)}, bf16[160,384]{1,0:T(8,128)(2,1)S(1)}, u32[]{:S(2)}, u32[]{:S(2)}) collective-permute-start(bf16[160,384]{1,0:T(8,128)(2,1)S(1)} %get-tuple-element.22.refs_0_), channel_id=1, source_target_pairs={{0,4},{4,0},{8,12},{12,8},{1,5},{5,1},{9,13},{13,9},{2,6},{6,2},{1... | collective-permute-start | bytes 368648 | tf_op jit(solution)/shard_map/ppermute | solution.py:239
  29.8 16.4 %collective-permute-start.7 = (bf16[160,384]{1,0:T(8,128)(2,1)S(1)}, bf16[160,384]{1,0:T(8,128)(2,1)S(1)}, u32[]{:S(2)}, u32[]{:S(2)}) collective-permute-start(bf16[160,384]{1,0:T(8,128)(2,1)S(1)} %get-tuple-element.22.refs_0_), channel_id=1, source_target_pairs={{0,8},{4,12},{8,0},{12,4},{1,9},{5,13},{9,1},{13,5},{2,10},{6,14},... | collective-permute-start | bytes 368648 | tf_op jit(solution)/shard_map/ppermute | solution.py:239
  35.7 13.4 %collective-permute-start.8 = (bf16[160,384]{1,0:T(8,128)(2,1)S(1)}, bf16[160,384]{1,0:T(8,128)(2,1)S(1)}, u32[]{:S(2)}, u32[]{:S(2)}) collective-permute-start(bf16[160,384]{1,0:T(8,128)(2,1)S(1)} %get-tuple-element.22.refs_0_), channel_id=1, source_target_pairs={{0,12},{4,8},{8,4},{12,0},{1,13},{5,9},{9,5},{13,1},{2,14},{6,10},... | collective-permute-start | bytes 368648 | tf_op jit(solution)/shard_map/ppermute | solution.py:239
  40.3 9.7 %collective-permute-start.14 = (bf16[80,1280]{1,0:T(8,128)(2,1)S(1)}, bf16[80,1280]{1,0:T(8,128)(2,1)S(1)}, u32[]{:S(2)}, u32[]{:S(2)}) collective-permute-start(bf16[80,1280]{1,0:T(8,128)(2,1)S(1)} %get-tuple-element.27), channel_id=1, source_target_pairs={{0,2},{2,0},{1,3},{3,1},{4,6},{6,4},{5,7},{7,5},{8,10},{10,8},{9,1... | collective-permute-start | bytes 614408 | tf_op jit(solution)/shard_map/ppermute | solution.py:329
  40.9 15.8 %copy-start.4 = (f32[1280]{0:T(1024)S(1)}, f32[1280]{0:T(1024)}, u32[]{:S(2)}) copy-start(f32[1280]{0:T(1024)} %param.12) | copy-start | bytes 15364
  40.9 15.9 %copy-start.3 = (s32[4]{0:T(128)S(1)}, s32[4]{0:T(128)}, u32[]{:S(2)}) copy-start(s32[4]{0:T(128)} %flags.1) | copy-start | bytes 52
  40.9 11.2 %collective-permute-start.12 = (bf16[80,1280]{1,0:T(8,128)(2,1)S(1)}, bf16[80,1280]{1,0:T(8,128)(2,1)S(1)}, u32[]{:S(2)}, u32[]{:S(2)}) collective-permute-start(bf16[80,1280]{1,0:T(8,128)(2,1)S(1)} %get-tuple-element.25), channel_id=1, source_target_pairs={{0,2},{2,0},{1,3},{3,1},{4,6},{6,4},{5,7},{7,5},{8,10},{10,8},{9,1... | collective-permute-start | bytes 614408 | tf_op jit(solution)/shard_map/ppermute | solution.py:329
  49.1 7.7 %copy-start = (f32[4,160,1280]{2,1,0:T(8,128)S(1)}, f32[4,160,1280]{2,1,0:T(8,128)}, u32[]{:S(2)}) copy-start(f32[4,160,1280]{2,1,0:T(8,128)} %cached.1) | copy-start | bytes 9830404
  50.0 6.8 %copy-start.2 = (f32[160,1280]{1,0:T(8,128)S(1)}, f32[160,1280]{1,0:T(8,128)}, u32[]{:S(2)}) copy-start(f32[160,1280]{1,0:T(8,128)} %hidden.1) | copy-start | bytes 2457604
  50.1 14.5 %collective-permute-start.15 = (bf16[80,1280]{1,0:T(8,128)(2,1)S(1)}, bf16[80,1280]{1,0:T(8,128)(2,1)S(1)}, u32[]{:S(2)}, u32[]{:S(2)}) collective-permute-start(bf16[80,1280]{1,0:T(8,128)(2,1)S(1)} %shard_map.102), channel_id=1, source_target_pairs={{0,0},{1,4},{2,8},{3,12},{4,9},{5,13},{6,1},{7,5},{8,2},{9,6},{10,... | collective-permute-start | bytes 614408 | tf_op jit(solution)/shard_map/ppermute | solution.py:337
  52.2 13.3 %collective-permute-start.13 = (bf16[80,1280]{1,0:T(8,128)(2,1)S(1)}, bf16[80,1280]{1,0:T(8,128)(2,1)S(1)}, u32[]{:S(2)}, u32[]{:S(2)}) collective-permute-start(bf16[80,1280]{1,0:T(8,128)(2,1)S(1)} %shard_map.100), channel_id=1, source_target_pairs={{0,8},{1,12},{2,0},{3,4},{4,1},{5,5},{6,9},{7,13},{8,10},{9,14},{1... | collective-permute-start | bytes 614408 | tf_op jit(solution)/shard_map/ppermute | solution.py:337

commit v23 on v22

--- a/solution.py
+++ b/solution.py
@@ -148,21 +148,30 @@
             query_all[pl.ds(pl.multiple_of(to, 16), half), :] = blocks[k][
                 pl.ds(pl.multiple_of(at, 16), half), :
             ]
-    for h in range(sent.shape[1] // HEAD_DIM):
-        columns = slice(h * HEAD_DIM, (h + 1) * HEAD_DIM)
-        scores = lax.dot_general(
+    heads = [
+        slice(h * HEAD_DIM, (h + 1) * HEAD_DIM) for h in range(sent.shape[1] // HEAD_DIM)
+    ]
+    scores = [
+        lax.dot_general(
             query_all[:, columns],
             key_all[:, columns],
             (((1,), (1,)), ((), ())),
             preferred_element_type=jnp.float32,
         )
-        peak = jnp.max(scores, axis=1, keepdims=True)
-        weights = jnp.exp2((scores - peak) * (LOG2_E * HEAD_DIM ** (-0.5)))
-        total = jnp.sum(weights, axis=1, keepdims=True)
-        result = jnp.dot(
-            weights.astype(jnp.bfloat16), value_all[:, columns], preferred_element_type=jnp.float32
-        )
-        result = (result / total).astype(sent.dtype)
+        for columns in heads
+    ]
+    weights = [
+        jnp.exp2((score - jnp.max(score, axis=1, keepdims=True)) * (LOG2_E * HEAD_DIM ** (-0.5)))
+        for score in scores
+    ]
+    results = [
+        jnp.dot(
+            weight.astype(jnp.bfloat16), value_all[:, columns], preferred_element_type=jnp.float32
+        )
+        for weight, columns in zip(weights, heads)
+    ]
+    for weight, result, columns in zip(weights, results, heads):
+        result = (result / jnp.sum(weight, axis=1, keepdims=True)).astype(sent.dtype)
         sent[:, columns] = result[:rows]
         kept[:, columns] = result[rows:]
 

time: 66.6 us -> 66.3 us (level)
  no operation moved by 1% of the time
where the time goes in v23:
time: 66.3 us; the launch traced here: 66.1 us
  waiting for transfers between devices  33.4 us (50%)
  starting transfers between devices  24.6 us (37%)
  Pallas kernels  7.23 us (11%)
  between operations  0.83 us (1%)
    ppermute x6, waiting for transfers between devices, along(): return lax.ppermute(shard, 'seq', [(z, z ^ m) for z in range(4)])  13.4 us
    ppermute x4, waiting for transfers between devices, local_heads(): moved.append(lax.ppermute(packed[k], ('seq', 'head'), pairs))  11.6 us
    ppermute x6, starting transfers between devices, along(): return lax.ppermute(shard, 'seq', [(z, z ^ m) for z in range(4)])  8.65 us
    ppermute x2, waiting for transfers between devices, local_heads(): owned.append(lax.ppermute(summed, ('seq', 'wt', 'head'), pairs))  6.99 us
    ppermute x4, starting transfers between devices, local_heads(): moved.append(lax.ppermute(packed[k], ('seq', 'head'), pairs))  6.61 us
    ppermute x2, starting transfers between devices, local_heads(): owned.append(lax.ppermute(summed, ('seq', 'wt', 'head'), pairs))  6.59 us
    pallas_call x8, Pallas kernels, call(): pl.pallas_call(kernel, in_specs=[pl.BlockSpec(memory_space=place) for pla...  5.33 us
    ppermute x2, starting transfers between devices, local_heads(): arrived = lax.ppermute(sent[p], 'wt', swap)  2.09 us
  transfers between devices with their start and end apart: 16, of which 7 were waited for; matrix products, arithmetic and copies ran while one was open for 0% of the time, Pallas kernels for 6%

profile of v23, /device:TPU:14, one launch (start us, length us, event | category | flops | bytes accessed | tf_op | source)
XLA Modules:
  0.0 66.1 jit_solution(15730541484001113646)
XLA Ops:
  0.6 0.0 copy-start.1
  0.6 1.4 %shard_map.95 = (bf16[320,384]{1,0:T(8,128)(2,1)S(1)}, bf16[320,384]{1,0:T(8,128)(2,1)S(1)}, bf16[160,384]{1,0:T(8,128)(2,1)S(1)}, bf16[160,384]{1,0:T(8,128)(2,1)S(1)}) custom-call(bf16[160,768]{1,0:T(8,128)(2,1)} %queries.1, bf16[160,768]{1,0:T(8,128)(2,1)} %keys.1, bf16[160,768]{1,0:T(8,128)(2,1)} %values.1), custom_call_target="tpu_custom_call" | custom-call | tf_op jit(solution)/shard_map/pallas_call | solution.py:262
  2.0 0.1 collective-permute-start.5
  2.1 1.7 %collective-permute-start = (bf16[320,384]{1,0:T(8,128)(2,1)S(1)}, bf16[320,384]{1,0:T(8,128)(2,1)S(1)}, u32[]{:S(2)}, u32[]{:S(2)}) collective-permute-start(bf16[320,384]{1,0:T(8,128)(2,1)S(1)} %get-tuple-element.16), channel_id=1, source_target_pairs={{0,8},{1,12},{4,9},{5,13},{8,0},{9,4},{12,1},{13,5},{2,10},{3,14},... | collective-permute-start | bytes 737288 | tf_op jit(solution)/shard_map/ppermute | solution.py:307
  3.8 4.1 %collective-permute-start.1 = (bf16[320,384]{1,0:T(8,128)(2,1)S(1)}, bf16[320,384]{1,0:T(8,128)(2,1)S(1)}, u32[]{:S(2)}, u32[]{:S(2)}) collective-permute-start(bf16[320,384]{1,0:T(8,128)(2,1)S(1)} %get-tuple-element.17), channel_id=1, source_target_pairs={{0,0},{1,4},{4,1},{5,5},{8,8},{9,12},{12,9},{13,13},{2,2},{3,6},{6... | collective-permute-start | bytes 737288 | tf_op jit(solution)/shard_map/ppermute | solution.py:307
  7.8 0.1 collective-permute-start.2
  7.9 0.8 %collective-permute-start.3 = (bf16[160,384]{1,0:T(8,128)(2,1)S(1)}, bf16[160,384]{1,0:T(8,128)(2,1)S(1)}, u32[]{:S(2)}, u32[]{:S(2)}) collective-permute-start(bf16[160,384]{1,0:T(8,128)(2,1)S(1)} %get-tuple-element.19), channel_id=1, source_target_pairs={{0,1},{1,5},{4,0},{5,4},{8,9},{9,13},{12,8},{13,12},{2,3},{3,7},{6... | collective-permute-start | bytes 368648 | tf_op jit(solution)/shard_map/ppermute | solution.py:307
  8.7 11.6 %collective-permute-done.2.refs_2_ = bf16[160,384]{1,0:T(8,128)(2,1)S(1)} collective-permute-done((bf16[160,384]{1,0:T(8,128)(2,1)S(1)}, bf16[160,384]{1,0:T(8,128)(2,1)S(1)}, u32[]{:S(2)}, u32[]{:S(2)}) %collective-permute-start.2) | collective-permute-done | bytes 122912 | tf_op jit(solution)/shard_map/ppermute | solution.py:307
  20.3 0.0 collective-permute-done.3.refs_3_
  20.3 0.0 collective-permute-done.refs_0_
  20.3 0.0 collective-permute-done.1.refs_1_
  20.4 0.5 collective-permute-start.4
  20.9 1.5 %collective-permute-done.4.refs_4_ = bf16[640,384]{1,0:T(8,128)(2,1)S(1)} collective-permute-done((bf16[640,384]{1,0:T(8,128)(2,1)S(1)}, bf16[640,384]{1,0:T(8,128)(2,1)S(1)}, u32[]{:S(2)}, u32[]{:S(2)}) %collective-permute-start.4) | collective-permute-done | bytes 491552 | tf_op jit(solution)/shard_map/ppermute | solution.py:309
  22.4 0.0 collective-permute-done.5.refs_5_
  22.4 1.2 %shard_map.97 = (bf16[160,384]{1,0:T(8,128)(2,1)S(1)}, bf16[160,384]{1,0:T(8,128)(2,1)S(1)}) custom-call(bf16[320,384]{1,0:T(8,128)(2,1)S(1)} %collective-permute-done.refs_0_, bf16[320,384]{1,0:T(8,128)(2,1)S(1)} %collective-permute-done.1.refs_1_, bf16[160,384]{1,0:T(8,128)(2,1)S(1)} %collective-permute-done.2.refs_2_, ...), custom_call_target="tpu_custom_call" | custom-call | flops 314572800 | tf_op jit(solution)/shard_map/pallas_call | solution.py:262
  23.6 3.7 %collective-permute-start.10 = (bf16[160,384]{1,0:T(8,128)(2,1)S(1)}, bf16[160,384]{1,0:T(8,128)(2,1)S(1)}, u32[]{:S(2)}, u32[]{:S(2)}) collective-permute-start(bf16[160,384]{1,0:T(8,128)(2,1)S(1)} %get-tuple-element.24.refs_0_), channel_id=1, source_target_pairs={{0,8},{4,12},{8,0},{12,4},{1,9},{5,13},{9,1},{13,5},{2,10},{6,14},... | collective-permute-start | bytes 368648 | tf_op jit(solution)/shard_map/ppermute | solution.py:248
  27.3 0.0 collective-permute-start.11
  27.3 1.5 %collective-permute-start.9 = (bf16[160,384]{1,0:T(8,128)(2,1)S(1)}, bf16[160,384]{1,0:T(8,128)(2,1)S(1)}, u32[]{:S(2)}, u32[]{:S(2)}) collective-permute-start(bf16[160,384]{1,0:T(8,128)(2,1)S(1)} %get-tuple-element.24.refs_0_), channel_id=1, source_target_pairs={{0,4},{4,0},{8,12},{12,8},{1,5},{5,1},{9,13},{13,9},{2,6},{6,2},{1... | collective-permute-start | bytes 368648 | tf_op jit(solution)/shard_map/ppermute | solution.py:248
  28.9 0.5 collective-permute-start.6
  29.4 2.6 %collective-permute-start.7 = (bf16[160,384]{1,0:T(8,128)(2,1)S(1)}, bf16[160,384]{1,0:T(8,128)(2,1)S(1)}, u32[]{:S(2)}, u32[]{:S(2)}) collective-permute-start(bf16[160,384]{1,0:T(8,128)(2,1)S(1)} %get-tuple-element.22.refs_0_), channel_id=1, source_target_pairs={{0,8},{4,12},{8,0},{12,4},{1,9},{5,13},{9,1},{13,5},{2,10},{6,14},... | collective-permute-start | bytes 368648 | tf_op jit(solution)/shard_map/ppermute | solution.py:248
  31.9 3.3 %collective-permute-done.10.refs_2_ = bf16[160,384]{1,0:T(8,128)(2,1)S(1)} collective-permute-done((bf16[160,384]{1,0:T(8,128)(2,1)S(1)}, bf16[160,384]{1,0:T(8,128)(2,1)S(1)}, u32[]{:S(2)}, u32[]{:S(2)}) %collective-permute-start.10) | collective-permute-done | bytes 122912 | tf_op jit(solution)/shard_map/ppermute | solution.py:248
  35.2 0.4 collective-permute-start.8
  35.6 3.3 %collective-permute-done.11.refs_3_ = bf16[160,384]{1,0:T(8,128)(2,1)S(1)} collective-permute-done((bf16[160,384]{1,0:T(8,128)(2,1)S(1)}, bf16[160,384]{1,0:T(8,128)(2,1)S(1)}, u32[]{:S(2)}, u32[]{:S(2)}) %collective-permute-start.11) | collective-permute-done | bytes 122912 | tf_op jit(solution)/shard_map/ppermute | solution.py:248
  38.9 0.0 collective-permute-done.9.refs_1_
  39.0 0.0 copy-done.1
  39.0 0.9 %shard_map.99 = (bf16[80,1280]{1,0:T(8,128)(2,1)S(1)}, bf16[80,1280]{1,0:T(8,128)(2,1)S(1)}) custom-call(bf16[160,384]{1,0:T(8,128)(2,1)S(1)} %get-tuple-element.24.refs_0_, bf16[160,384]{1,0:T(8,128)(2,1)S(1)} %collective-permute-done.9.refs_1_, bf16[160,384]{1,0:T(8,128)(2,1)S(1)} %collective-permute-done.10.refs_2_, ...), custom_call_target="tpu_custom_call" | custom-call | flops 629145600 | tf_op jit(solution)/shard_map/pallas_call | solution.py:262
  39.9 0.7 collective-permute-start.14
  40.5 0.0 copy-start.3
  40.5 1.4 %collective-permute-start.12 = (bf16[80,1280]{1,0:T(8,128)(2,1)S(1)}, bf16[80,1280]{1,0:T(8,128)(2,1)S(1)}, u32[]{:S(2)}, u32[]{:S(2)}) collective-permute-start(bf16[80,1280]{1,0:T(8,128)(2,1)S(1)} %get-tuple-element.25), channel_id=1, source_target_pairs={{0,2},{2,0},{1,3},{3,1},{4,6},{6,4},{5,7},{7,5},{8,10},{10,8},{9,1... | collective-permute-start | bytes 614408 | tf_op jit(solution)/shard_map/ppermute | solution.py:338
  42.0 0.0 collective-permute-done.6.refs_1_
  42.0 3.8 %collective-permute-done.7.refs_2_ = bf16[160,384]{1,0:T(8,128)(2,1)S(1)} collective-permute-done((bf16[160,384]{1,0:T(8,128)(2,1)S(1)}, bf16[160,384]{1,0:T(8,128)(2,1)S(1)}, u32[]{:S(2)}, u32[]{:S(2)}) %collective-permute-start.7) | collective-permute-done | bytes 122912 | tf_op jit(solution)/shard_map/ppermute | solution.py:248
  45.8 2.9 %collective-permute-done.8.refs_3_ = bf16[160,384]{1,0:T(8,128)(2,1)S(1)} collective-permute-done((bf16[160,384]{1,0:T(8,128)(2,1)S(1)}, bf16[160,384]{1,0:T(8,128)(2,1)S(1)}, u32[]{:S(2)}, u32[]{:S(2)}) %collective-permute-start.8) | collective-permute-done | bytes 122912 | tf_op jit(solution)/shard_map/ppermute | solution.py:248
  48.7 0.9 %shard_map.98 = (f32[80,1280]{1,0:T(8,128)S(1)}, f32[80,1280]{1,0:T(8,128)S(1)}) custom-call(bf16[160,384]{1,0:T(8,128)(2,1)S(1)} %get-tuple-element.22.refs_0_, bf16[160,384]{1,0:T(8,128)(2,1)S(1)} %collective-permute-done.6.refs_1_, bf16[160,384]{1,0:T(8,128)(2,1)S(1)} %collective-permute-done.7.refs_2_, ...), custom_call_target="tpu_custom_call" | custom-call | flops 5033164800 | tf_op jit(solution)/shard_map/pallas_call | solution.py:262
  49.6 0.0 copy-start.2
  49.6 0.0 collective-permute-done.14.arrived
  49.6 0.1 shard_map.102
  49.7 2.1 %collective-permute-start.15 = (bf16[80,1280]{1,0:T(8,128)(2,1)S(1)}, bf16[80,1280]{1,0:T(8,128)(2,1)S(1)}, u32[]{:S(2)}, u32[]{:S(2)}) collective-permute-start(bf16[80,1280]{1,0:T(8,128)(2,1)S(1)} %shard_map.102), channel_id=1, source_target_pairs={{0,0},{1,4},{2,8},{3,12},{4,9},{5,13},{6,1},{7,5},{8,2},{9,6},{10,... | collective-permute-start | bytes 614408 | tf_op jit(solution)/shard_map/ppermute | solution.py:346
  51.7 0.0 collective-permute-done.12.arrived
  51.8 4.5 %collective-permute-start.13 = (bf16[80,1280]{1,0:T(8,128)(2,1)S(1)}, bf16[80,1280]{1,0:T(8,128)(2,1)S(1)}, u32[]{:S(2)}, u32[]{:S(2)}) collective-permute-start(bf16[80,1280]{1,0:T(8,128)(2,1)S(1)} %shard_map.100), channel_id=1, source_target_pairs={{0,8},{1,12},{2,0},{3,4},{4,1},{5,5},{6,9},{7,13},{8,10},{9,14},{1... | collective-permute-start | bytes 614408 | tf_op jit(solution)/shard_map/ppermute | solution.py:346
  56.3 0.0 copy-done.4
  56.4 0.0 copy-done.3
  56.4 0.0 copy-done
  56.4 0.0 copy-done.2
  56.4 0.8 %shard_map.101.resting = f32[160,1280]{1,0:T(8,128)S(1)} custom-call(s32[4]{0:T(128)S(1)} %copy-done.3, f32[160,1280]{1,0:T(8,128)S(1)} %copy-done.2, f32[4,160,1280]{2,1,0:T(8,128)S(1)} %copy-done), custom_call_target="tpu_custom_call" | custom-call | tf_op jit(solution)/shard_map/pallas_call | solution.py:262
  57.2 7.0 %collective-permute-done.15.owned = bf16[80,1280]{1,0:T(8,128)(2,1)S(1)} collective-permute-done((bf16[80,1280]{1,0:T(8,128)(2,1)S(1)}, bf16[80,1280]{1,0:T(8,128)(2,1)S(1)}, u32[]{:S(2)}, u32[]{:S(2)}) %collective-permute-start.15) | collective-permute-done | bytes 204832 | tf_op jit(solution)/shard_map/ppermute | solution.py:346
  64.2 0.9 %shard_map.103 = (f32[160,1280]{1,0:T(8,128)}, f32[160,1280]{1,0:T(8,128)}) custom-call(bf16[80,1280]{1,0:T(8,128)(2,1)S(1)} %collective-permute-done.15.owned, f32[1,1280]{1,0:T(1,128)S(1)} %broadcast_in_dim.3.gate, f32[160,1280]{1,0:T(8,128)S(1)} %shard_map.101.resting), custom_call_target="tpu_custom_call" | custom-call | tf_op jit(solution)/shard_map/pallas_call | solution.py:353
  65.1 0.0 collective-permute-done.13.owned
  65.1 1.0 %shard_map.104 = (f32[160,1280]{1,0:T(8,128)}, f32[160,1280]{1,0:T(8,128)}) custom-call(bf16[80,1280]{1,0:T(8,128)(2,1)S(1)} %collective-permute-done.13.owned, f32[1,1280]{1,0:T(1,128)S(1)} %broadcast_in_dim.3.gate, f32[160,1280]{1,0:T(8,128)S(1)} %shard_map.101.resting, ...), custom_call_target="tpu_custom_call", output_to_operand_aliasing={{0}: (3, {}), {1}: (4, {})} | custom-call | tf_op jit(solution)/shard_map/pallas_call | solution.py:353
  (5 shorter events, 0.1 us)
Async XLA Ops:
  0.6 38.3 %copy-start.1 = (bf16[768,1280]{1,0:T(8,128)(2,1)S(1)}, bf16[768,1280]{1,0:T(8,128)(2,1)}, u32[]{:S(2)}) copy-start(bf16[768,1280]{1,0:T(8,128)(2,1)} %refs_4_.3) | copy-start | bytes 5898244
  2.0 20.4 %collective-permute-start.5 = (bf16[768,1280]{1,0:T(8,128)(2,1)}, bf16[768,1280]{1,0:T(8,128)(2,1)S(1)}, u32[]{:S(2)}, u32[]{:S(2)}) collective-permute-start(bf16[768,1280]{1,0:T(8,128)(2,1)} %refs_4_.3), channel_id=1, source_target_pairs={{0,1},{1,0},{2,3},{3,2},{4,5},{5,4},{6,7},{7,6},{8,9},{9,8},{10,11... | collective-permute-start | bytes 5898248 | tf_op jit(solution)/shard_map/ppermute | solution.py:298
  2.1 18.2 %collective-permute-start = (bf16[320,384]{1,0:T(8,128)(2,1)S(1)}, bf16[320,384]{1,0:T(8,128)(2,1)S(1)}, u32[]{:S(2)}, u32[]{:S(2)}) collective-permute-start(bf16[320,384]{1,0:T(8,128)(2,1)S(1)} %get-tuple-element.16), channel_id=1, source_target_pairs={{0,8},{1,12},{4,9},{5,13},{8,0},{9,4},{12,1},{13,5},{2,10},{3,14},... | collective-permute-start | bytes 737288 | tf_op jit(solution)/shard_map/ppermute | solution.py:307
  3.8 16.5 %collective-permute-start.1 = (bf16[320,384]{1,0:T(8,128)(2,1)S(1)}, bf16[320,384]{1,0:T(8,128)(2,1)S(1)}, u32[]{:S(2)}, u32[]{:S(2)}) collective-permute-start(bf16[320,384]{1,0:T(8,128)(2,1)S(1)} %get-tuple-element.17), channel_id=1, source_target_pairs={{0,0},{1,4},{4,1},{5,5},{8,8},{9,12},{12,9},{13,13},{2,2},{3,6},{6... | collective-permute-start | bytes 737288 | tf_op jit(solution)/shard_map/ppermute | solution.py:307
  7.8 12.5 %collective-permute-start.2 = (bf16[160,384]{1,0:T(8,128)(2,1)S(1)}, bf16[160,384]{1,0:T(8,128)(2,1)S(1)}, u32[]{:S(2)}, u32[]{:S(2)}) collective-permute-start(bf16[160,384]{1,0:T(8,128)(2,1)S(1)} %get-tuple-element.18), channel_id=1, source_target_pairs={{0,9},{1,13},{4,8},{5,12},{8,1},{9,5},{12,0},{13,4},{2,11},{3,15},... | collective-permute-start | bytes 368648 | tf_op jit(solution)/shard_map/ppermute | solution.py:307
  7.9 12.4 %collective-permute-start.3 = (bf16[160,384]{1,0:T(8,128)(2,1)S(1)}, bf16[160,384]{1,0:T(8,128)(2,1)S(1)}, u32[]{:S(2)}, u32[]{:S(2)}) collective-permute-start(bf16[160,384]{1,0:T(8,128)(2,1)S(1)} %get-tuple-element.19), channel_id=1, source_target_pairs={{0,1},{1,5},{4,0},{5,4},{8,9},{9,13},{12,8},{13,12},{2,3},{3,7},{6... | collective-permute-start | bytes 368648 | tf_op jit(solution)/shard_map/ppermute | solution.py:307
  20.4 2.0 %collective-permute-start.4 = (bf16[640,384]{1,0:T(8,128)(2,1)S(1)}, bf16[640,384]{1,0:T(8,128)(2,1)S(1)}, u32[]{:S(2)}, u32[]{:S(2)}) collective-permute-start(bf16[640,384]{1,0:T(8,128)(2,1)S(1)} %shard_map.96), channel_id=1, source_target_pairs={{0,1},{1,0},{2,3},{3,2},{4,5},{5,4},{6,7},{7,6},{8,9},{9,8},{10,11... | collective-permute-start | bytes 1474568 | tf_op jit(solution)/shard_map/ppermute | solution.py:309
  23.6 11.6 %collective-permute-start.10 = (bf16[160,384]{1,0:T(8,128)(2,1)S(1)}, bf16[160,384]{1,0:T(8,128)(2,1)S(1)}, u32[]{:S(2)}, u32[]{:S(2)}) collective-permute-start(bf16[160,384]{1,0:T(8,128)(2,1)S(1)} %get-tuple-element.24.refs_0_), channel_id=1, source_target_pairs={{0,8},{4,12},{8,0},{12,4},{1,9},{5,13},{9,1},{13,5},{2,10},{6,14},... | collective-permute-start | bytes 368648 | tf_op jit(solution)/shard_map/ppermute | solution.py:248
  27.3 11.6 %collective-permute-start.11 = (bf16[160,384]{1,0:T(8,128)(2,1)S(1)}, bf16[160,384]{1,0:T(8,128)(2,1)S(1)}, u32[]{:S(2)}, u32[]{:S(2)}) collective-permute-start(bf16[160,384]{1,0:T(8,128)(2,1)S(1)} %get-tuple-element.24.refs_0_), channel_id=1, source_target_pairs={{0,12},{4,8},{8,4},{12,0},{1,13},{5,9},{9,5},{13,1},{2,14},{6,10},... | collective-permute-start | bytes 368648 | tf_op jit(solution)/shard_map/ppermute | solution.py:248
  27.3 11.6 %collective-permute-start.9 = (bf16[160,384]{1,0:T(8,128)(2,1)S(1)}, bf16[160,384]{1,0:T(8,128)(2,1)S(1)}, u32[]{:S(2)}, u32[]{:S(2)}) collective-permute-start(bf16[160,384]{1,0:T(8,128)(2,1)S(1)} %get-tuple-element.24.refs_0_), channel_id=1, source_target_pairs={{0,4},{4,0},{8,12},{12,8},{1,5},{5,1},{9,13},{13,9},{2,6},{6,2},{1... | collective-permute-start | bytes 368648 | tf_op jit(solution)/shard_map/ppermute | solution.py:248
  28.9 13.1 %collective-permute-start.6 = (bf16[160,384]{1,0:T(8,128)(2,1)S(1)}, bf16[160,384]{1,0:T(8,128)(2,1)S(1)}, u32[]{:S(2)}, u32[]{:S(2)}) collective-permute-start(bf16[160,384]{1,0:T(8,128)(2,1)S(1)} %get-tuple-element.22.refs_0_), channel_id=1, source_target_pairs={{0,4},{4,0},{8,12},{12,8},{1,5},{5,1},{9,13},{13,9},{2,6},{6,2},{1... | collective-permute-start | bytes 368648 | tf_op jit(solution)/shard_map/ppermute | solution.py:248
  29.4 16.4 %collective-permute-start.7 = (bf16[160,384]{1,0:T(8,128)(2,1)S(1)}, bf16[160,384]{1,0:T(8,128)(2,1)S(1)}, u32[]{:S(2)}, u32[]{:S(2)}) collective-permute-start(bf16[160,384]{1,0:T(8,128)(2,1)S(1)} %get-tuple-element.22.refs_0_), channel_id=1, source_target_pairs={{0,8},{4,12},{8,0},{12,4},{1,9},{5,13},{9,1},{13,5},{2,10},{6,14},... | collective-permute-start | bytes 368648 | tf_op jit(solution)/shard_map/ppermute | solution.py:248
  35.2 13.4 %collective-permute-start.8 = (bf16[160,384]{1,0:T(8,128)(2,1)S(1)}, bf16[160,384]{1,0:T(8,128)(2,1)S(1)}, u32[]{:S(2)}, u32[]{:S(2)}) collective-permute-start(bf16[160,384]{1,0:T(8,128)(2,1)S(1)} %get-tuple-element.22.refs_0_), channel_id=1, source_target_pairs={{0,12},{4,8},{8,4},{12,0},{1,13},{5,9},{9,5},{13,1},{2,14},{6,10},... | collective-permute-start | bytes 368648 | tf_op jit(solution)/shard_map/ppermute | solution.py:248
  39.9 9.8 %collective-permute-start.14 = (bf16[80,1280]{1,0:T(8,128)(2,1)S(1)}, bf16[80,1280]{1,0:T(8,128)(2,1)S(1)}, u32[]{:S(2)}, u32[]{:S(2)}) collective-permute-start(bf16[80,1280]{1,0:T(8,128)(2,1)S(1)} %get-tuple-element.27), channel_id=1, source_target_pairs={{0,2},{2,0},{1,3},{3,1},{4,6},{6,4},{5,7},{7,5},{8,10},{10,8},{9,1... | collective-permute-start | bytes 614408 | tf_op jit(solution)/shard_map/ppermute | solution.py:338
  40.5 15.8 %copy-start.4 = (f32[1280]{0:T(1024)S(1)}, f32[1280]{0:T(1024)}, u32[]{:S(2)}) copy-start(f32[1280]{0:T(1024)} %param.12) | copy-start | bytes 15364
  40.5 15.8 %copy-start.3 = (s32[4]{0:T(128)S(1)}, s32[4]{0:T(128)}, u32[]{:S(2)}) copy-start(s32[4]{0:T(128)} %flags.1) | copy-start | bytes 52
  40.5 11.2 %collective-permute-start.12 = (bf16[80,1280]{1,0:T(8,128)(2,1)S(1)}, bf16[80,1280]{1,0:T(8,128)(2,1)S(1)}, u32[]{:S(2)}, u32[]{:S(2)}) collective-permute-start(bf16[80,1280]{1,0:T(8,128)(2,1)S(1)} %get-tuple-element.25), channel_id=1, source_target_pairs={{0,2},{2,0},{1,3},{3,1},{4,6},{6,4},{5,7},{7,5},{8,10},{10,8},{9,1... | collective-permute-start | bytes 614408 | tf_op jit(solution)/shard_map/ppermute | solution.py:338
  48.7 7.7 %copy-start = (f32[4,160,1280]{2,1,0:T(8,128)S(1)}, f32[4,160,1280]{2,1,0:T(8,128)}, u32[]{:S(2)}) copy-start(f32[4,160,1280]{2,1,0:T(8,128)} %cached.1) | copy-start | bytes 9830404
  49.6 6.8 %copy-start.2 = (f32[160,1280]{1,0:T(8,128)S(1)}, f32[160,1280]{1,0:T(8,128)}, u32[]{:S(2)}) copy-start(f32[160,1280]{1,0:T(8,128)} %hidden.1) | copy-start | bytes 2457604
  49.7 14.5 %collective-permute-start.15 = (bf16[80,1280]{1,0:T(8,128)(2,1)S(1)}, bf16[80,1280]{1,0:T(8,128)(2,1)S(1)}, u32[]{:S(2)}, u32[]{:S(2)}) collective-permute-start(bf16[80,1280]{1,0:T(8,128)(2,1)S(1)} %shard_map.102), channel_id=1, source_target_pairs={{0,0},{1,4},{2,8},{3,12},{4,9},{5,13},{6,1},{7,5},{8,2},{9,6},{10,... | collective-permute-start | bytes 614408 | tf_op jit(solution)/shard_map/ppermute | solution.py:346
  51.8 13.3 %collective-permute-start.13 = (bf16[80,1280]{1,0:T(8,128)(2,1)S(1)}, bf16[80,1280]{1,0:T(8,128)(2,1)S(1)}, u32[]{:S(2)}, u32[]{:S(2)}) collective-permute-start(bf16[80,1280]{1,0:T(8,128)(2,1)S(1)} %shard_map.100), channel_id=1, source_target_pairs={{0,8},{1,12},{2,0},{3,4},{4,1},{5,5},{6,9},{7,13},{8,10},{9,14},{1... | collective-permute-start | bytes 614408 | tf_op jit(solution)/shard_map/ppermute | solution.py:346

commit v24 on v23

--- a/solution.py
+++ b/solution.py
@@ -198,13 +198,17 @@
 
 
 def project_kernel(kept, *refs):
-    shards, (weight, weight_c, out0, out1, held) = refs[:4], refs[4:]
+    shards, (weight, weight_c), outs, held = refs[:4], refs[4:6], refs[6:-1], refs[-1]
     total = multiply(shards, weight, weight_c, held)
-    half = out0.shape[0]
+    half = total.shape[0] // 2
+    if len(outs) == 1:
+        out0, out1 = outs[0].at[:half, :], outs[0].at[half:, :]
+    else:
+        out0, out1 = outs
     _, zl = bits()
     side = lax.rem(lax.axis_index("wt") + zl, 2)
     for high in range(2):
-        part = total[high * half : (high + 1) * half].astype(out0.dtype)
+        part = total[high * half : (high + 1) * half].astype(outs[0].dtype)
         first = flip(side, high) == 1 - kept
 
         @pl.when(first)
@@ -216,8 +220,9 @@
             out1[...] = part
 
 
-def add_kernel(kept, arrived, out):
-    out[...] = (kept[...] + arrived[...].astype(jnp.float32)).astype(out.dtype)
+def add_kernel(piece, kept, arrived, out):
+    rows = slice(piece * kept.shape[0], (piece + 1) * kept.shape[0])
+    out[...] = (kept[...] + arrived[rows, :].astype(jnp.float32)).astype(out.dtype)
 
 
 def rest_kernel(flags, hidden, cached, out):
@@ -326,17 +331,24 @@
         call(
             functools.partial(project_kernel, i),
             [part] + [along(part, m) for m in (1, 2, 3)] + [out_weight, weight_c],
-            [((half, columns), dtype)] * 2,
+            shapes,
             [pltpu.VMEM((4 * rows, width), bf16)],
             flops=effort * flops,
         )
-        for i, (part, dtype, effort) in enumerate(((parts[0], bf16, 1), (parts[1], jnp.float32, 8)))
+        for i, (part, shapes, effort) in enumerate(
+            (
+                (parts[0], [((rows, columns), bf16)], 1),
+                (parts[1], [((half, columns), jnp.float32)] * 2, 8),
+            )
+        )
     )
 
     owned = []
+    arrived = lax.ppermute(sent[0], "wt", swap)
     for p in range(2):
-        arrived = lax.ppermute(sent[p], "wt", swap)
-        (summed,) = call(add_kernel, (kept[p], arrived), [((half, columns), bf16)])
+        (summed,) = call(
+            functools.partial(add_kernel, p), (kept[p], arrived), [((half, columns), bf16)]
+        )
         pairs = []
         for zz in range(4):
             for xx in range(2):

time: 66.3 us -> 68.2 us (1.029)
  the two profiles are of different devices: /device:TPU:14 before, /device:TPU:2 now
where the time goes in v24:
time: 68.2 us; the launch traced here: 68 us
  waiting for transfers between devices  34 us (50%)
  starting transfers between devices  25.8 us (38%)
  Pallas kernels  7.26 us (11%)
  between operations  0.81 us (1%)
    ppermute x4, waiting for transfers between devices, local_heads(): moved.append(lax.ppermute(packed[k], ('seq', 'head'), pairs))  11.4 us
    ppermute x6, waiting for transfers between devices, along(): return lax.ppermute(shard, 'seq', [(z, z ^ m) for z in range(4)])  11.1 us
    ppermute x6, starting transfers between devices, along(): return lax.ppermute(shard, 'seq', [(z, z ^ m) for z in range(4)])  10.3 us
    ppermute x2, waiting for transfers between devices, local_heads(): owned.append(lax.ppermute(summed, ('seq', 'wt', 'head'), pairs))  6.86 us
    ppermute x2, starting transfers between devices, local_heads(): owned.append(lax.ppermute(summed, ('seq', 'wt', 'head'), pairs))  6.53 us
    ppermute x4, starting transfers between devices, local_heads(): moved.append(lax.ppermute(packed[k], ('seq', 'head'), pairs))  6.17 us
    pallas_call x8, Pallas kernels, call(): pl.pallas_call(kernel, in_specs=[pl.BlockSpec(memory_space=place) for pla...  5.36 us
    ppermute x1, waiting for transfers between devices, local_heads(): arrived = lax.ppermute(sent[0], 'wt', swap)  3.09 us
  transfers between devices with their start and end apart: 15, of which 9 were waited for; matrix products, arithmetic and copies ran while one was open for 0% of the time, Pallas kernels for 5%

profile of v24, /device:TPU:2, one launch (start us, length us, event | category | flops | bytes accessed | tf_op | source)
XLA Modules:
  0.0 68.0 jit_solution(3281366336185861562)
XLA Ops:
  0.6 0.0 copy-start.1
  0.6 1.4 %shard_map.95 = (bf16[320,384]{1,0:T(8,128)(2,1)S(1)}, bf16[320,384]{1,0:T(8,128)(2,1)S(1)}, bf16[160,384]{1,0:T(8,128)(2,1)S(1)}, bf16[160,384]{1,0:T(8,128)(2,1)S(1)}) custom-call(bf16[160,768]{1,0:T(8,128)(2,1)} %queries.1, bf16[160,768]{1,0:T(8,128)(2,1)} %keys.1, bf16[160,768]{1,0:T(8,128)(2,1)} %values.1), custom_call_target="tpu_custom_call" | custom-call | tf_op jit(solution)/shard_map/pallas_call | solution.py:267
  2.0 0.1 collective-permute-start.5
  2.1 2.7 %collective-permute-start = (bf16[320,384]{1,0:T(8,128)(2,1)S(1)}, bf16[320,384]{1,0:T(8,128)(2,1)S(1)}, u32[]{:S(2)}, u32[]{:S(2)}) collective-permute-start(bf16[320,384]{1,0:T(8,128)(2,1)S(1)} %get-tuple-element.14), channel_id=1, source_target_pairs={{0,8},{1,12},{4,9},{5,13},{8,0},{9,4},{12,1},{13,5},{2,10},{3,14},... | collective-permute-start | bytes 737288 | tf_op jit(solution)/shard_map/ppermute | solution.py:312
  4.8 0.7 collective-permute-start.1
  5.4 2.8 %collective-permute-start.2 = (bf16[160,384]{1,0:T(8,128)(2,1)S(1)}, bf16[160,384]{1,0:T(8,128)(2,1)S(1)}, u32[]{:S(2)}, u32[]{:S(2)}) collective-permute-start(bf16[160,384]{1,0:T(8,128)(2,1)S(1)} %get-tuple-element.16), channel_id=1, source_target_pairs={{0,9},{1,13},{4,8},{5,12},{8,1},{9,5},{12,0},{13,4},{2,11},{3,15},... | collective-permute-start | bytes 368648 | tf_op jit(solution)/shard_map/ppermute | solution.py:312
  8.3 0.0 collective-permute-start.3
  8.3 9.6 %collective-permute-done.2.refs_2_ = bf16[160,384]{1,0:T(8,128)(2,1)S(1)} collective-permute-done((bf16[160,384]{1,0:T(8,128)(2,1)S(1)}, bf16[160,384]{1,0:T(8,128)(2,1)S(1)}, u32[]{:S(2)}, u32[]{:S(2)}) %collective-permute-start.2) | collective-permute-done | bytes 122912 | tf_op jit(solution)/shard_map/ppermute | solution.py:312
  17.8 1.4 %collective-permute-done.3.refs_3_ = bf16[160,384]{1,0:T(8,128)(2,1)S(1)} collective-permute-done((bf16[160,384]{1,0:T(8,128)(2,1)S(1)}, bf16[160,384]{1,0:T(8,128)(2,1)S(1)}, u32[]{:S(2)}, u32[]{:S(2)}) %collective-permute-start.3) | collective-permute-done | bytes 122912 | tf_op jit(solution)/shard_map/ppermute | solution.py:312
  19.2 0.5 collective-permute-done.refs_0_
  19.7 0.0 collective-permute-done.1.refs_1_
  19.8 2.1 %collective-permute-start.4 = (bf16[640,384]{1,0:T(8,128)(2,1)S(1)}, bf16[640,384]{1,0:T(8,128)(2,1)S(1)}, u32[]{:S(2)}, u32[]{:S(2)}) collective-permute-start(bf16[640,384]{1,0:T(8,128)(2,1)S(1)} %shard_map.96), channel_id=1, source_target_pairs={{0,1},{1,0},{2,3},{3,2},{4,5},{5,4},{6,7},{7,6},{8,9},{9,8},{10,11... | collective-permute-start | bytes 1474568 | tf_op jit(solution)/shard_map/ppermute | solution.py:314
  21.9 1.5 %collective-permute-done.4.refs_4_ = bf16[640,384]{1,0:T(8,128)(2,1)S(1)} collective-permute-done((bf16[640,384]{1,0:T(8,128)(2,1)S(1)}, bf16[640,384]{1,0:T(8,128)(2,1)S(1)}, u32[]{:S(2)}, u32[]{:S(2)}) %collective-permute-start.4) | collective-permute-done | bytes 491552 | tf_op jit(solution)/shard_map/ppermute | solution.py:314
  23.4 0.0 collective-permute-done.5.refs_5_
  23.4 1.2 %shard_map.97 = (bf16[160,384]{1,0:T(8,128)(2,1)S(1)}, bf16[160,384]{1,0:T(8,128)(2,1)S(1)}) custom-call(bf16[320,384]{1,0:T(8,128)(2,1)S(1)} %collective-permute-done.refs_0_, bf16[320,384]{1,0:T(8,128)(2,1)S(1)} %collective-permute-done.1.refs_1_, bf16[160,384]{1,0:T(8,128)(2,1)S(1)} %collective-permute-done.2.refs_2_, ...), custom_call_target="tpu_custom_call" | custom-call | flops 314572800 | tf_op jit(solution)/shard_map/pallas_call | solution.py:267
  24.6 2.4 %collective-permute-start.10 = (bf16[160,384]{1,0:T(8,128)(2,1)S(1)}, bf16[160,384]{1,0:T(8,128)(2,1)S(1)}, u32[]{:S(2)}, u32[]{:S(2)}) collective-permute-start(bf16[160,384]{1,0:T(8,128)(2,1)S(1)} %get-tuple-element.22.refs_0_), channel_id=1, source_target_pairs={{0,8},{4,12},{8,0},{12,4},{1,9},{5,13},{9,1},{13,5},{2,10},{6,14},... | collective-permute-start | bytes 368648 | tf_op jit(solution)/shard_map/ppermute | solution.py:253
  27.1 1.3 %collective-permute-start.11 = (bf16[160,384]{1,0:T(8,128)(2,1)S(1)}, bf16[160,384]{1,0:T(8,128)(2,1)S(1)}, u32[]{:S(2)}, u32[]{:S(2)}) collective-permute-start(bf16[160,384]{1,0:T(8,128)(2,1)S(1)} %get-tuple-element.22.refs_0_), channel_id=1, source_target_pairs={{0,12},{4,8},{8,4},{12,0},{1,13},{5,9},{9,5},{13,1},{2,14},{6,10},... | collective-permute-start | bytes 368648 | tf_op jit(solution)/shard_map/ppermute | solution.py:253
  28.4 0.5 collective-permute-start.9
  28.9 1.5 %collective-permute-start.6 = (bf16[160,384]{1,0:T(8,128)(2,1)S(1)}, bf16[160,384]{1,0:T(8,128)(2,1)S(1)}, u32[]{:S(2)}, u32[]{:S(2)}) collective-permute-start(bf16[160,384]{1,0:T(8,128)(2,1)S(1)} %get-tuple-element.20.refs_0_), channel_id=1, source_target_pairs={{0,4},{4,0},{8,12},{12,8},{1,5},{5,1},{9,13},{13,9},{2,6},{6,2},{1... | collective-permute-start | bytes 368648 | tf_op jit(solution)/shard_map/ppermute | solution.py:253
  30.5 1.9 %collective-permute-start.7 = (bf16[160,384]{1,0:T(8,128)(2,1)S(1)}, bf16[160,384]{1,0:T(8,128)(2,1)S(1)}, u32[]{:S(2)}, u32[]{:S(2)}) collective-permute-start(bf16[160,384]{1,0:T(8,128)(2,1)S(1)} %get-tuple-element.20.refs_0_), channel_id=1, source_target_pairs={{0,8},{4,12},{8,0},{12,4},{1,9},{5,13},{9,1},{13,5},{2,10},{6,14},... | collective-permute-start | bytes 368648 | tf_op jit(solution)/shard_map/ppermute | solution.py:253
  32.4 4.7 %collective-permute-done.10.refs_2_ = bf16[160,384]{1,0:T(8,128)(2,1)S(1)} collective-permute-done((bf16[160,384]{1,0:T(8,128)(2,1)S(1)}, bf16[160,384]{1,0:T(8,128)(2,1)S(1)}, u32[]{:S(2)}, u32[]{:S(2)}) %collective-permute-start.10) | collective-permute-done | bytes 122912 | tf_op jit(solution)/shard_map/ppermute | solution.py:253
  37.1 2.6 %collective-permute-start.8 = (bf16[160,384]{1,0:T(8,128)(2,1)S(1)}, bf16[160,384]{1,0:T(8,128)(2,1)S(1)}, u32[]{:S(2)}, u32[]{:S(2)}) collective-permute-start(bf16[160,384]{1,0:T(8,128)(2,1)S(1)} %get-tuple-element.20.refs_0_), channel_id=1, source_target_pairs={{0,12},{4,8},{8,4},{12,0},{1,13},{5,9},{9,5},{13,1},{2,14},{6,10},... | collective-permute-start | bytes 368648 | tf_op jit(solution)/shard_map/ppermute | solution.py:253
  39.6 0.0 collective-permute-done.11.refs_3_
  39.7 0.0 collective-permute-done.9.refs_1_
  39.7 0.0 copy-done.1
  39.7 0.9 %shard_map.99 = bf16[160,1280]{1,0:T(8,128)(2,1)S(1)} custom-call(bf16[160,384]{1,0:T(8,128)(2,1)S(1)} %get-tuple-element.22.refs_0_, bf16[160,384]{1,0:T(8,128)(2,1)S(1)} %collective-permute-done.9.refs_1_, bf16[160,384]{1,0:T(8,128)(2,1)S(1)} %collective-permute-done.10.refs_2_, bf16[160,384]{1,0:T(8,128)(2,1)S(1)} %collective-permute-done.11.refs_3_, ...), custom_call_target="tpu_custom_call" | custom-call | flops 629145600 | tf_op jit(solution)/shard_map/pallas_call | solution.py:267
  40.6 0.6 collective-permute-start.12
  41.2 0.2 collective-permute-done.6.refs_1_
  41.4 6.2 %collective-permute-done.7.refs_2_ = bf16[160,384]{1,0:T(8,128)(2,1)S(1)} collective-permute-done((bf16[160,384]{1,0:T(8,128)(2,1)S(1)}, bf16[160,384]{1,0:T(8,128)(2,1)S(1)}, u32[]{:S(2)}, u32[]{:S(2)}) %collective-permute-start.7) | collective-permute-done | bytes 122912 | tf_op jit(solution)/shard_map/ppermute | solution.py:253
  47.6 0.0 collective-permute-done.8.refs_3_
  47.6 0.0 copy-start
  47.6 0.9 %shard_map.98 = (f32[80,1280]{1,0:T(8,128)S(1)}, f32[80,1280]{1,0:T(8,128)S(1)}) custom-call(bf16[160,384]{1,0:T(8,128)(2,1)S(1)} %get-tuple-element.20.refs_0_, bf16[160,384]{1,0:T(8,128)(2,1)S(1)} %collective-permute-done.6.refs_1_, bf16[160,384]{1,0:T(8,128)(2,1)S(1)} %collective-permute-done.7.refs_2_, ...), custom_call_target="tpu_custom_call" | custom-call | flops 5033164800 | tf_op jit(solution)/shard_map/pallas_call | solution.py:267
  48.6 0.0 copy-start.4
  48.6 0.0 copy-start.2
  48.6 0.0 copy-start.3
  48.6 3.1 %collective-permute-done.12.arrived = bf16[160,1280]{1,0:T(8,128)(2,1)S(1)} collective-permute-done((bf16[160,1280]{1,0:T(8,128)(2,1)S(1)}, bf16[160,1280]{1,0:T(8,128)(2,1)S(1)}, u32[]{:S(2)}, u32[]{:S(2)}) %collective-permute-start.12) | collective-permute-done | bytes 409632 | tf_op jit(solution)/shard_map/ppermute | solution.py:347
  51.7 4.6 %collective-permute-start.14 = (bf16[80,1280]{1,0:T(8,128)(2,1)S(1)}, bf16[80,1280]{1,0:T(8,128)(2,1)S(1)}, u32[]{:S(2)}, u32[]{:S(2)}) collective-permute-start(bf16[80,1280]{1,0:T(8,128)(2,1)S(1)} %shard_map.102), channel_id=1, source_target_pairs={{0,0},{1,4},{2,8},{3,12},{4,9},{5,13},{6,1},{7,5},{8,2},{9,6},{10,... | collective-permute-start | bytes 614408 | tf_op jit(solution)/shard_map/ppermute | solution.py:358
  56.3 0.1 shard_map.100
  56.4 1.9 %collective-permute-start.13 = (bf16[80,1280]{1,0:T(8,128)(2,1)S(1)}, bf16[80,1280]{1,0:T(8,128)(2,1)S(1)}, u32[]{:S(2)}, u32[]{:S(2)}) collective-permute-start(bf16[80,1280]{1,0:T(8,128)(2,1)S(1)} %shard_map.100), channel_id=1, source_target_pairs={{0,8},{1,12},{2,0},{3,4},{4,1},{5,5},{6,9},{7,13},{8,10},{9,14},{1... | collective-permute-start | bytes 614408 | tf_op jit(solution)/shard_map/ppermute | solution.py:358
  58.3 0.0 copy-done.4
  58.4 0.0 copy-done
  58.4 0.0 copy-done.2
  58.4 0.0 copy-done.3
  58.4 0.8 %shard_map.101.resting = f32[160,1280]{1,0:T(8,128)S(1)} custom-call(s32[4]{0:T(128)S(1)} %copy-done.3, f32[160,1280]{1,0:T(8,128)S(1)} %copy-done.2, f32[4,160,1280]{2,1,0:T(8,128)S(1)} %copy-done), custom_call_target="tpu_custom_call" | custom-call | tf_op jit(solution)/shard_map/pallas_call | solution.py:267
  59.2 6.9 %collective-permute-done.14.owned = bf16[80,1280]{1,0:T(8,128)(2,1)S(1)} collective-permute-done((bf16[80,1280]{1,0:T(8,128)(2,1)S(1)}, bf16[80,1280]{1,0:T(8,128)(2,1)S(1)}, u32[]{:S(2)}, u32[]{:S(2)}) %collective-permute-start.14) | collective-permute-done | bytes 204832 | tf_op jit(solution)/shard_map/ppermute | solution.py:358
  66.0 0.9 %shard_map.103 = (f32[160,1280]{1,0:T(8,128)}, f32[160,1280]{1,0:T(8,128)}) custom-call(bf16[80,1280]{1,0:T(8,128)(2,1)S(1)} %collective-permute-done.14.owned, f32[1,1280]{1,0:T(1,128)S(1)} %broadcast_in_dim.3.gate, f32[160,1280]{1,0:T(8,128)S(1)} %shard_map.101.resting), custom_call_target="tpu_custom_call" | custom-call | tf_op jit(solution)/shard_map/pallas_call | solution.py:365
  67.0 0.0 collective-permute-done.13.owned
  67.0 1.0 %shard_map.104 = (f32[160,1280]{1,0:T(8,128)}, f32[160,1280]{1,0:T(8,128)}) custom-call(bf16[80,1280]{1,0:T(8,128)(2,1)S(1)} %collective-permute-done.13.owned, f32[1,1280]{1,0:T(1,128)S(1)} %broadcast_in_dim.3.gate, f32[160,1280]{1,0:T(8,128)S(1)} %shard_map.101.resting, ...), custom_call_target="tpu_custom_call", output_to_operand_aliasing={{0}: (3, {}), {1}: (4, {})} | custom-call | tf_op jit(solution)/shard_map/pallas_call | solution.py:365
  (3 shorter events, 0.1 us)
Async XLA Ops:
  0.6 39.0 %copy-start.1 = (bf16[768,1280]{1,0:T(8,128)(2,1)S(1)}, bf16[768,1280]{1,0:T(8,128)(2,1)}, u32[]{:S(2)}) copy-start(bf16[768,1280]{1,0:T(8,128)(2,1)} %refs_4_.3) | copy-start | bytes 5898244
  2.0 21.4 %collective-permute-start.5 = (bf16[768,1280]{1,0:T(8,128)(2,1)}, bf16[768,1280]{1,0:T(8,128)(2,1)S(1)}, u32[]{:S(2)}, u32[]{:S(2)}) collective-permute-start(bf16[768,1280]{1,0:T(8,128)(2,1)} %refs_4_.3), channel_id=1, source_target_pairs={{0,1},{1,0},{2,3},{3,2},{4,5},{5,4},{6,7},{7,6},{8,9},{9,8},{10,11... | collective-permute-start | bytes 5898248 | tf_op jit(solution)/shard_map/ppermute | solution.py:303
  2.1 17.6 %collective-permute-start = (bf16[320,384]{1,0:T(8,128)(2,1)S(1)}, bf16[320,384]{1,0:T(8,128)(2,1)S(1)}, u32[]{:S(2)}, u32[]{:S(2)}) collective-permute-start(bf16[320,384]{1,0:T(8,128)(2,1)S(1)} %get-tuple-element.14), channel_id=1, source_target_pairs={{0,8},{1,12},{4,9},{5,13},{8,0},{9,4},{12,1},{13,5},{2,10},{3,14},... | collective-permute-start | bytes 737288 | tf_op jit(solution)/shard_map/ppermute | solution.py:312
  4.8 15.0 %collective-permute-start.1 = (bf16[320,384]{1,0:T(8,128)(2,1)S(1)}, bf16[320,384]{1,0:T(8,128)(2,1)S(1)}, u32[]{:S(2)}, u32[]{:S(2)}) collective-permute-start(bf16[320,384]{1,0:T(8,128)(2,1)S(1)} %get-tuple-element.15), channel_id=1, source_target_pairs={{0,0},{1,4},{4,1},{5,5},{8,8},{9,12},{12,9},{13,13},{2,2},{3,6},{6... | collective-permute-start | bytes 737288 | tf_op jit(solution)/shard_map/ppermute | solution.py:312
  5.4 12.4 %collective-permute-start.2 = (bf16[160,384]{1,0:T(8,128)(2,1)S(1)}, bf16[160,384]{1,0:T(8,128)(2,1)S(1)}, u32[]{:S(2)}, u32[]{:S(2)}) collective-permute-start(bf16[160,384]{1,0:T(8,128)(2,1)S(1)} %get-tuple-element.16), channel_id=1, source_target_pairs={{0,9},{1,13},{4,8},{5,12},{8,1},{9,5},{12,0},{13,4},{2,11},{3,15},... | collective-permute-start | bytes 368648 | tf_op jit(solution)/shard_map/ppermute | solution.py:312
  8.3 10.9 %collective-permute-start.3 = (bf16[160,384]{1,0:T(8,128)(2,1)S(1)}, bf16[160,384]{1,0:T(8,128)(2,1)S(1)}, u32[]{:S(2)}, u32[]{:S(2)}) collective-permute-start(bf16[160,384]{1,0:T(8,128)(2,1)S(1)} %get-tuple-element.17), channel_id=1, source_target_pairs={{0,1},{1,5},{4,0},{5,4},{8,9},{9,13},{12,8},{13,12},{2,3},{3,7},{6... | collective-permute-start | bytes 368648 | tf_op jit(solution)/shard_map/ppermute | solution.py:312
  19.8 3.6 %collective-permute-start.4 = (bf16[640,384]{1,0:T(8,128)(2,1)S(1)}, bf16[640,384]{1,0:T(8,128)(2,1)S(1)}, u32[]{:S(2)}, u32[]{:S(2)}) collective-permute-start(bf16[640,384]{1,0:T(8,128)(2,1)S(1)} %shard_map.96), channel_id=1, source_target_pairs={{0,1},{1,0},{2,3},{3,2},{4,5},{5,4},{6,7},{7,6},{8,9},{9,8},{10,11... | collective-permute-start | bytes 1474568 | tf_op jit(solution)/shard_map/ppermute | solution.py:314
  24.6 12.4 %collective-permute-start.10 = (bf16[160,384]{1,0:T(8,128)(2,1)S(1)}, bf16[160,384]{1,0:T(8,128)(2,1)S(1)}, u32[]{:S(2)}, u32[]{:S(2)}) collective-permute-start(bf16[160,384]{1,0:T(8,128)(2,1)S(1)} %get-tuple-element.22.refs_0_), channel_id=1, source_target_pairs={{0,8},{4,12},{8,0},{12,4},{1,9},{5,13},{9,1},{13,5},{2,10},{6,14},... | collective-permute-start | bytes 368648 | tf_op jit(solution)/shard_map/ppermute | solution.py:253
  27.1 12.6 %collective-permute-start.11 = (bf16[160,384]{1,0:T(8,128)(2,1)S(1)}, bf16[160,384]{1,0:T(8,128)(2,1)S(1)}, u32[]{:S(2)}, u32[]{:S(2)}) collective-permute-start(bf16[160,384]{1,0:T(8,128)(2,1)S(1)} %get-tuple-element.22.refs_0_), channel_id=1, source_target_pairs={{0,12},{4,8},{8,4},{12,0},{1,13},{5,9},{9,5},{13,1},{2,14},{6,10},... | collective-permute-start | bytes 368648 | tf_op jit(solution)/shard_map/ppermute | solution.py:253
  28.4 11.2 %collective-permute-start.9 = (bf16[160,384]{1,0:T(8,128)(2,1)S(1)}, bf16[160,384]{1,0:T(8,128)(2,1)S(1)}, u32[]{:S(2)}, u32[]{:S(2)}) collective-permute-start(bf16[160,384]{1,0:T(8,128)(2,1)S(1)} %get-tuple-element.22.refs_0_), channel_id=1, source_target_pairs={{0,4},{4,0},{8,12},{12,8},{1,5},{5,1},{9,13},{13,9},{2,6},{6,2},{1... | collective-permute-start | bytes 368648 | tf_op jit(solution)/shard_map/ppermute | solution.py:253
  28.9 12.5 %collective-permute-start.6 = (bf16[160,384]{1,0:T(8,128)(2,1)S(1)}, bf16[160,384]{1,0:T(8,128)(2,1)S(1)}, u32[]{:S(2)}, u32[]{:S(2)}) collective-permute-start(bf16[160,384]{1,0:T(8,128)(2,1)S(1)} %get-tuple-element.20.refs_0_), channel_id=1, source_target_pairs={{0,4},{4,0},{8,12},{12,8},{1,5},{5,1},{9,13},{13,9},{2,6},{6,2},{1... | collective-permute-start | bytes 368648 | tf_op jit(solution)/shard_map/ppermute | solution.py:253
  30.5 17.2 %collective-permute-start.7 = (bf16[160,384]{1,0:T(8,128)(2,1)S(1)}, bf16[160,384]{1,0:T(8,128)(2,1)S(1)}, u32[]{:S(2)}, u32[]{:S(2)}) collective-permute-start(bf16[160,384]{1,0:T(8,128)(2,1)S(1)} %get-tuple-element.20.refs_0_), channel_id=1, source_target_pairs={{0,8},{4,12},{8,0},{12,4},{1,9},{5,13},{9,1},{13,5},{2,10},{6,14},... | collective-permute-start | bytes 368648 | tf_op jit(solution)/shard_map/ppermute | solution.py:253
  37.1 10.5 %collective-permute-start.8 = (bf16[160,384]{1,0:T(8,128)(2,1)S(1)}, bf16[160,384]{1,0:T(8,128)(2,1)S(1)}, u32[]{:S(2)}, u32[]{:S(2)}) collective-permute-start(bf16[160,384]{1,0:T(8,128)(2,1)S(1)} %get-tuple-element.20.refs_0_), channel_id=1, source_target_pairs={{0,12},{4,8},{8,4},{12,0},{1,13},{5,9},{9,5},{13,1},{2,14},{6,10},... | collective-permute-start | bytes 368648 | tf_op jit(solution)/shard_map/ppermute | solution.py:253
  40.6 11.1 %collective-permute-start.12 = (bf16[160,1280]{1,0:T(8,128)(2,1)S(1)}, bf16[160,1280]{1,0:T(8,128)(2,1)S(1)}, u32[]{:S(2)}, u32[]{:S(2)}) collective-permute-start(bf16[160,1280]{1,0:T(8,128)(2,1)S(1)} %shard_map.99), channel_id=1, source_target_pairs={{0,2},{2,0},{1,3},{3,1},{4,6},{6,4},{5,7},{7,5},{8,10},{10,8},{9,1... | collective-permute-start | bytes 1228808 | tf_op jit(solution)/shard_map/ppermute | solution.py:347
  47.6 10.7 %copy-start = (f32[4,160,1280]{2,1,0:T(8,128)S(1)}, f32[4,160,1280]{2,1,0:T(8,128)}, u32[]{:S(2)}) copy-start(f32[4,160,1280]{2,1,0:T(8,128)} %cached.1) | copy-start | bytes 9830404
  48.6 9.8 %copy-start.4 = (f32[1280]{0:T(1024)S(1)}, f32[1280]{0:T(1024)}, u32[]{:S(2)}) copy-start(f32[1280]{0:T(1024)} %param.12) | copy-start | bytes 15364
  48.6 9.8 %copy-start.2 = (f32[160,1280]{1,0:T(8,128)S(1)}, f32[160,1280]{1,0:T(8,128)}, u32[]{:S(2)}) copy-start(f32[160,1280]{1,0:T(8,128)} %hidden.1) | copy-start | bytes 2457604
  48.6 9.8 %copy-start.3 = (s32[4]{0:T(128)S(1)}, s32[4]{0:T(128)}, u32[]{:S(2)}) copy-start(s32[4]{0:T(128)} %flags.1) | copy-start | bytes 52
  51.7 14.3 %collective-permute-start.14 = (bf16[80,1280]{1,0:T(8,128)(2,1)S(1)}, bf16[80,1280]{1,0:T(8,128)(2,1)S(1)}, u32[]{:S(2)}, u32[]{:S(2)}) collective-permute-start(bf16[80,1280]{1,0:T(8,128)(2,1)S(1)} %shard_map.102), channel_id=1, source_target_pairs={{0,0},{1,4},{2,8},{3,12},{4,9},{5,13},{6,1},{7,5},{8,2},{9,6},{10,... | collective-permute-start | bytes 614408 | tf_op jit(solution)/shard_map/ppermute | solution.py:358
  56.4 10.6 %collective-permute-start.13 = (bf16[80,1280]{1,0:T(8,128)(2,1)S(1)}, bf16[80,1280]{1,0:T(8,128)(2,1)S(1)}, u32[]{:S(2)}, u32[]{:S(2)}) collective-permute-start(bf16[80,1280]{1,0:T(8,128)(2,1)S(1)} %shard_map.100), channel_id=1, source_target_pairs={{0,8},{1,12},{2,0},{3,4},{4,1},{5,5},{6,9},{7,13},{8,10},{9,14},{1... | collective-permute-start | bytes 614408 | tf_op jit(solution)/shard_map/ppermute | solution.py:358
